TPU v7x, 128 devices: a whole 4x4x4 slice. The times are simulated.
128 devices in a mesh: group: 8 (over x_hi, y), tp: 16 (over x_lo, z, core).
Axes of the slice: x: 4 (x_hi: 2, x_lo: 2; x = x_hi * 2 + x_lo), y: 4, z: 4, core: 2. Of those that a mesh axis runs over, the one named last changes fastest.
Arguments:
- master: float32 [8192, 32768], P(None, ('group', 'tp')), may hold values from -0.5524272 to 0.5524272
- activations: bfloat16 [2048, 8192], P('group', 'tp'), may hold values from -6 to 6
- owner: int32 [8], replicated, may hold values from 0 to 7, each once
Outputs:
- hidden: bfloat16 [2048, 32768], P('group', 'tp')
Inputs may be any that keep to these rules, and one draw needn't show every extreme that they name: `owner`: every section owns exactly one span.
All inputs are finite; a program needn't handle non-finite values.
Results may differ from a plain program's by a relative error of at most 0.022.
Values may be sent and summed in bfloat16 or wider, within the bound.
No kernel may reach another device: no remote copies, remote signals or barrier semaphores. Data moves between devices by JAX's collectives and lax.ppermute only.
A program may use at most 320 MiB of HBM per device.

v0:
```python
import jax
import jax.numpy as jnp
from jax import lax
from jax.sharding import PartitionSpec as P

BLOCK = 128


def quantize(master, block):
    rows, cols = master.shape
    tiles = master.reshape(rows // block, block, cols // block, block)
    amax = jnp.max(jnp.abs(tiles), axis=(1, 3))
    scales = ((amax + 1e-06) / 448.0).astype(jnp.bfloat16)
    coded = (tiles / scales.astype(jnp.float32)[:, None, :, None]).astype(jnp.bfloat16)
    return (coded.reshape(rows, cols), scales)


def scaled_product(acts, coded, scales, block):
    count = acts.shape[0]
    cols = coded.shape[1]

    def step(index, total):
        start = index * block
        left = lax.dynamic_slice_in_dim(acts, start, block, 1)
        right = lax.dynamic_slice_in_dim(coded, start, block, 0)
        scale_row = lax.dynamic_slice_in_dim(scales, index, 1, 0)[0].astype(jnp.float32)
        product = jnp.dot(left, right, preferred_element_type=jnp.float32)
        return total + product.reshape(count, cols // block, block) * scale_row[None, :, None]

    start_total = jnp.zeros((count, cols // block, block), jnp.float32)
    total = lax.fori_loop(0, coded.shape[0] // block, step, start_total)
    return total.reshape(count, cols)


def shards(master, activations, owner):
    coded, scales = quantize(master, BLOCK)
    sections = lax.axis_size("group")
    coded_rows, scale_rows = (
        lax.all_to_all(coded, "tp", split_axis=0, concat_axis=1, tiled=True),
        lax.all_to_all(scales, "tp", split_axis=0, concat_axis=1, tiled=True),
    )
    row_count = coded_rows.shape[0]
    width = coded_rows.shape[1]
    every_code, every_scale = (
        lax.all_gather(coded_rows, "group", axis=1, tiled=True),
        lax.all_gather(scale_rows, "group", axis=1, tiled=True),
    )
    every_code = jnp.take(every_code.reshape(row_count, sections, width), owner, axis=1).reshape(
        row_count, sections * width
    )
    every_scale = jnp.take(
        every_scale.reshape(row_count // BLOCK, sections, width // BLOCK), owner, axis=1
    ).reshape(row_count // BLOCK, sections * width // BLOCK)
    partial_value = scaled_product(activations, every_code, every_scale, BLOCK)
    return lax.psum_scatter(
        partial_value.astype(jnp.bfloat16), "tp", scatter_dimension=1, tiled=True
    )


def solution(mesh):
    in_specs = (P(None, ("group", "tp")), P("group", "tp"), P())
    out_specs = P("group", "tp")
    return jax.shard_map(shards, mesh=mesh, in_specs=in_specs, out_specs=out_specs, check_vma=False)
```

profile of v0, /device:TPU:3, one launch (start us, length us, event | category | flops | bytes accessed | tf_op | source)
XLA Modules:
  0.0 1063.9 jit_solution(4622837478446141298)
XLA Ops:
  6.5 0.0 all-gather.3.cloned.1.call-start
  6.5 7.3 abs.6
  13.9 10.8 %abs.7 = f32[64,128,2,128]{3,2,1,0:T(2,128)} reshape(f32[8192,256]{1,0:T(8,128)} %abs.6) | data formatting | bytes 16777216 | tf_op jit(solution)/shard_map/abs | solution.py:12
  24.6 5.7 reduce_max.9
  30.3 0.1 copy.35
  30.4 0.1 copy.36
  30.5 5.5 div.19
  36.0 7.0 fusion.4
  42.9 0.0 copy-start
  42.9 55.5 %all_to_all.35 = bf16[16,512,256]{2,1,0:T(8,128)(2,1)} all-to-all(bf16[16,512,256]{2,1,0:T(8,128)(2,1)S(1)} %bitcast.55), channel_id=1, replica_groups=mesh['group'=8,'tp'=16] {'tp'}, dimensions={0} | all-to-all | bytes 8388608 | tf_op jit(solution)/shard_map/all_to_all | solution.py:39
  98.4 6.4 copy.37
  104.8 0.0 all-gather.3.cloned.1.call-update
  104.9 0.1 convert_element_type.45
  105.0 0.6 copy.42
  105.6 5.1 all-to-all-start.1
  110.7 0.0 reduce-scatter.2.cloned.1.call-start
  110.7 0.0 copy-done
  110.8 0.1 broadcast_bitcast_fusion
  110.9 0.1 broadcast_in_dim.43
  110.9 0.1 broadcast_in_dim.44
  111.1 3.9 all-to-all-done.1
  115.0 0.1 copy.43
  115.1 19.1 %all-gather = bf16[8,32,4]{1,2,0:T(4,128)(2,1)S(1)} all-gather(bf16[1,32,4]{1,2,0:T(4,128)(2,1)S(1)} %bitcast.63), channel_id=1, replica_groups=mesh['group'=8,'tp'=16] {'group'}, dimensions={0}, use_global_device_ids=true | all-gather | bytes 2304 | tf_op jit(solution)/shard_map/all_gather | solution.py:46
  134.2 0.1 reshape.97
  134.3 0.1 reshape.58
  134.4 0.6 gather_fusion
  135.0 0.1 gather.15
  135.1 302.7 %all-gather.3.cloned.1.call-done = bf16[512,32768]{0,1:T(8,128)(2,1)} async-done(((bf16[512,4096]{0,1:T(8,128)(2,1)}), bf16[512,32768]{0,1:T(8,128)(2,1)}) %all-gather.3.cloned.1.call-update) | async-done | bytes 33554448 | tf_op jit(solution)/shard_map/all_gather | solution.py:45
  437.7 8.6 mini-gather-slice.5
  446.3 16.0 %fusion.5 = (bf16[512,8,1408]{0,2,1:T(8,128)(2,1)}, bf16[512,8,1408]{0,2,1:T(8,128)(2,1)}) fusion(bf16[512,8,4096]{0,2,1:T(8,128)(2,1)} %bitcast.53), kind=kLoop, calls=%fused_computation.22 | loop fusion | bytes 46137344 | tf_op jit(solution)/shard_map/jit(_take)/gather | solution.py:48
  462.3 15.1 %copy.49 = bf16[512,8,1408]{2,0,1:T(8,128)(2,1)} copy(bf16[512,8,1408]{0,2,1:T(8,128)(2,1)} %get-tuple-element.143) | data formatting | bytes 23068672
  477.4 10.4 gather_fusion.1
  487.8 15.1 %copy.51 = bf16[512,8,1280]{2,0,1:T(8,128)(2,1)} copy(bf16[512,8,1280]{0,2,1:T(8,128)(2,1)} %mini-gather-slice.5) | data formatting | bytes 20971520
  502.9 9.6 gather_fusion.3
  512.4 15.1 %copy.50 = bf16[512,8,1408]{2,0,1:T(8,128)(2,1)} copy(bf16[512,8,1408]{0,2,1:T(8,128)(2,1)} %get-tuple-element.144) | data formatting | bytes 23068672
  527.5 10.4 gather_fusion.2
  537.9 22.7 %pad_maximum_fusion = bf16[512,8,4096]{2,0,1:T(8,128)(2,1)} fusion(bf16[512,8,1280]{2,0,1:T(8,128)(2,1)} %bitcast.51, bf16[512,8,1408]{2,0,1:T(8,128)(2,1)} %bitcast.50, bf16[512,8,1408]{2,0,1:T(8,128)(2,1)} %bitcast.49), kind=kLoop, calls=%fused_computation.11 | loop fusion | flops 100663296 | bytes 67108864
  560.6 41.6 %copy.41 = bf16[512,8,4096]{0,2,1:T(8,128)(2,1)} copy(bf16[512,8,4096]{2,0,1:T(8,128)(2,1)} %pad_maximum_fusion) | data formatting | bytes 67108864
  602.2 22.9 %bitcast_select_fusion = bf16[512,32768]{0,1:T(8,128)(2,1)} fusion(bf16[512,8,4096]{0,2,1:T(8,128)(2,1)} %copy.41, pred[32768]{0:T(1024)(128)(4,1)S(1)} %bitcast.58), kind=kLoop, calls=%fused_computation.12 | loop fusion | flops 16777216 | bytes 67141632 | tf_op jit(solution)/shard_map/jit(_take)/select_n | solution.py:48
  625.1 311.5 %while.14 = (s32[]{:T(128)}, f32[256,256,128]{2,1,0:T(8,128)}, bf16[256,512]{1,0:T(8,128)(2,1)}, bf16[512,32768]{0,1:T(8,128)(2,1)}, bf16[4,256]{1,0:T(4,128)(2,...) while((s32[]{:T(128)}, f32[256,256,128]{2,1,0:T(8,128)}, bf16[256,512]{1,0:T(8,128)(2,1)}, ...), condition=%wide.region_2.3_spmd.clone, body=%wide.region_1.2_spmd.clone.sunk | while | flops 2172649728 | bytes 209784464 | solution.py:31
  625.1 19.0 %convolution_bitcast_fusion.2 = f32[32,8,256,128]{3,1,2,0:T(8,128)} fusion(bf16[512,32768]{0,1:T(8,128)(2,1)} %get-tuple-element.197, s32[]{:T(128)S(6)} %select_n.40, bf16[256,512]{1,0:T(8,128)(2,1)} %get-tuple-element.196), kind=kOutput, calls=%fused_computation.6.clone.1 | convolution fusion | flops 2147483648 | bytes 42009600 | tf_op jit(solution)/shard_map/while/body/eval_jaxpr/dot_general | solution.py:27
  644.1 27.5 %copy.60 = f32[32,8,256,128]{3,2,1,0:T(8,128)} copy(f32[32,8,256,128]{3,1,2,0:T(8,128)} %convolution_bitcast_fusion.2) | data formatting | bytes 67108864 | tf_op jit(solution)/shard_map/while
  671.7 25.3 %fusion.11 = f32[256,256,128]{2,1,0:T(8,128)} fusion(f32[32,8,256,128]{3,2,1,0:T(8,128)} %copy.60, f32[256,256,128]{2,1,0:T(8,128)} %get-tuple-element.186, f32[256]{0:T(256)S(1)} %bitcast.59, pred[]{:T(512)S(6)} %compare.3), kind=kLoop, calls=%fused_computation.5.clone.1 | loop fusion | flops 25165824 | bytes 100664320 | tf_op jit(solution)/shard_map/while/body/eval_jaxpr/add | solution.py:28
  696.9 19.0 %convolution_bitcast_fusion.2 = f32[32,8,256,128]{3,1,2,0:T(8,128)} fusion(bf16[512,32768]{0,1:T(8,128)(2,1)} %get-tuple-element.197, s32[]{:T(128)S(6)} %select_n.40, bf16[256,512]{1,0:T(8,128)(2,1)} %get-tuple-element.196), kind=kOutput, calls=%fused_computation.6.clone.1 | convolution fusion | flops 2147483648 | bytes 42009600 | tf_op jit(solution)/shard_map/while/body/eval_jaxpr/dot_general | solution.py:27
  715.9 27.5 %copy.60 = f32[32,8,256,128]{3,2,1,0:T(8,128)} copy(f32[32,8,256,128]{3,1,2,0:T(8,128)} %convolution_bitcast_fusion.2) | data formatting | bytes 67108864 | tf_op jit(solution)/shard_map/while
  743.5 33.3 %fusion.11 = f32[256,256,128]{2,1,0:T(8,128)} fusion(f32[32,8,256,128]{3,2,1,0:T(8,128)} %copy.60, f32[256,256,128]{2,1,0:T(8,128)} %get-tuple-element.186, f32[256]{0:T(256)S(1)} %bitcast.59, pred[]{:T(512)S(6)} %compare.3), kind=kLoop, calls=%fused_computation.5.clone.1 | loop fusion | flops 25165824 | bytes 100664320 | tf_op jit(solution)/shard_map/while/body/eval_jaxpr/add | solution.py:28
  776.8 19.0 %convolution_bitcast_fusion.2 = f32[32,8,256,128]{3,1,2,0:T(8,128)} fusion(bf16[512,32768]{0,1:T(8,128)(2,1)} %get-tuple-element.197, s32[]{:T(128)S(6)} %select_n.40, bf16[256,512]{1,0:T(8,128)(2,1)} %get-tuple-element.196), kind=kOutput, calls=%fused_computation.6.clone.1 | convolution fusion | flops 2147483648 | bytes 42009600 | tf_op jit(solution)/shard_map/while/body/eval_jaxpr/dot_general | solution.py:27
  795.8 27.5 %copy.60 = f32[32,8,256,128]{3,2,1,0:T(8,128)} copy(f32[32,8,256,128]{3,1,2,0:T(8,128)} %convolution_bitcast_fusion.2) | data formatting | bytes 67108864 | tf_op jit(solution)/shard_map/while
  823.3 33.3 %fusion.11 = f32[256,256,128]{2,1,0:T(8,128)} fusion(f32[32,8,256,128]{3,2,1,0:T(8,128)} %copy.60, f32[256,256,128]{2,1,0:T(8,128)} %get-tuple-element.186, f32[256]{0:T(256)S(1)} %bitcast.59, pred[]{:T(512)S(6)} %compare.3), kind=kLoop, calls=%fused_computation.5.clone.1 | loop fusion | flops 25165824 | bytes 100664320 | tf_op jit(solution)/shard_map/while/body/eval_jaxpr/add | solution.py:28
  856.6 19.1 %convolution_bitcast_fusion.2 = f32[32,8,256,128]{3,1,2,0:T(8,128)} fusion(bf16[512,32768]{0,1:T(8,128)(2,1)} %get-tuple-element.197, s32[]{:T(128)S(6)} %select_n.40, bf16[256,512]{1,0:T(8,128)(2,1)} %get-tuple-element.196), kind=kOutput, calls=%fused_computation.6.clone.1 | convolution fusion | flops 2147483648 | bytes 42009600 | tf_op jit(solution)/shard_map/while/body/eval_jaxpr/dot_general | solution.py:27
  875.7 27.5 %copy.60 = f32[32,8,256,128]{3,2,1,0:T(8,128)} copy(f32[32,8,256,128]{3,1,2,0:T(8,128)} %convolution_bitcast_fusion.2) | data formatting | bytes 67108864 | tf_op jit(solution)/shard_map/while
  903.3 33.3 %fusion.11 = f32[256,256,128]{2,1,0:T(8,128)} fusion(f32[32,8,256,128]{3,2,1,0:T(8,128)} %copy.60, f32[256,256,128]{2,1,0:T(8,128)} %get-tuple-element.186, f32[256]{0:T(256)S(1)} %bitcast.59, pred[]{:T(512)S(6)} %compare.3), kind=kLoop, calls=%fused_computation.5.clone.1 | loop fusion | flops 25165824 | bytes 100664320 | tf_op jit(solution)/shard_map/while/body/eval_jaxpr/add | solution.py:28
  936.5 12.1 %convert_element_type.46 = bf16[256,256,128]{2,1,0:T(8,128)(2,1)S(1)} convert(f32[256,256,128]{2,1,0:T(8,128)} %get-tuple-element.99) | non-fusion elementwise | flops 8388608 | bytes 50331648 | tf_op jit(solution)/shard_map/convert_element_type | solution.py:56
  948.7 12.1 %copy.58 = bf16[32,8,256,128]{3,1,2,0:T(8,128)(2,1)} copy(bf16[32,8,256,128]{3,2,1,0:T(8,128)(2,1)S(1)} %bitcast.47) | data formatting | bytes 33554432
  960.8 0.0 reduce-scatter.2.cloned.1.call-update
  960.8 96.2 %reduce-scatter.2.cloned.1.call-done = bf16[256,2048]{1,0:T(8,128)(2,1)} async-done(((bf16[256,32768]{1,0:T(8,128)(2,1)}), bf16[256,2048]{1,0:T(8,128)(2,1)}) %reduce-scatter.2.cloned.1.call-update) | async-done | bytes 1048592 | tf_op jit(solution)/shard_map/reduce_scatter | solution.py:55
  (14 shorter events, 0.1 us)
Async XLA Ops:
  6.5 431.2 %all-gather.3.cloned.1.call-start = ((), (), s32[]{:S(2)}) async-start(), calls=%async_computation.3 | async-start | bytes 37748736 | tf_op jit(solution)/shard_map/all_gather | solution.py:45
  42.9 67.8 %copy-start = (s32[8]{0:T(128)S(1)}, s32[8]{0:T(128)}, u32[]{:S(2)}) copy-start(s32[8]{0:T(128)} %param.7) | copy-start | bytes 100
  105.6 9.4 all-to-all-start.1
  110.7 946.4 %reduce-scatter.2.cloned.1.call-start = ((), (), s32[]{:S(2)}) async-start(), calls=%async_computation.4 | async-start | bytes 17825792 | tf_op jit(solution)/shard_map/reduce_scatter | solution.py:55
Sparse Core Ops, SparseCore 0:
  105.0 332.7 all-gather.2
  961.0 96.0 reduce-scatter.1
where the time goes:
time: 1070 us; the launch traced here: 1060 us
  waiting for transfers between devices  403 us (38%)
  local copies, waits for them, and re-layouts  289 us (27%)
  other arithmetic  203 us (19%)
  matrix products  76.2 us (7%)
  blocking collectives  74.6 us (7%)
  between operations  13.5 us (1%)
    all_gather x1, waiting for transfers between devices, shards(): lax.all_gather(coded_rows, 'group', axis=1, tiled=True)  303 us
    add x4, other arithmetic, step(): total + product.reshape(count, cols // block, block) * scale_row[None, :,...  125 us
    while x4, local copies, waits for them, and re-layouts  110 us
    unnamed x11, local copies, waits for them, and re-layouts  99.3 us
    reduce_scatter x1, waiting for transfers between devices, shards(): lax.psum_scatter(partial_value.astype(jnp.bfloat16), 'tp', scatter_dimens...  96.2 us
    dot_general x4, matrix products, step(): product = jnp.dot(left, right, preferred_element_type=jnp.float32)  76.2 us
    all_to_all x1, blocking collectives, shards(): lax.all_to_all(coded, 'tp', split_axis=0, concat_axis=1, tiled=True)  55.5 us
    gather x5, local copies, waits for them, and re-layouts, shards(): jnp.take(every_code.reshape(row_count, sections, width), owner, axis=1)  54.9 us
  transfers between devices with their start and end apart: 3, of which 3 were waited for; matrix products, arithmetic and copies ran while one was open for 0% of the time, Pallas kernels for 0%

commit v1 on v0

v1 whole, which is shorter than its diff:
```python
import functools

import jax
import jax.numpy as jnp
from jax import lax
from jax.experimental import pallas as pl
from jax.experimental.pallas import tpu as pltpu
from jax.sharding import PartitionSpec as P

BLOCK = 128
AXES = ("group", "tp")
N_DEV = 128
PARTS = {"z": (0, 96), "y": (96, 80), "x": (176, 80)}
ORDER = {"z": "xyz", "y": "zxy", "x": "yzx"}
SLOTS = 4


def coords(i):
    xh, y, xl, z, core = i // 64, i // 16 % 4, i // 8 % 2, i // 2 % 4, i % 2
    return xh * 2 + xl, y, z, core


def linear(x, y, z, core):
    return (x // 2) * 64 + (y % 4) * 16 + (x % 2) * 8 + (z % 4) * 2 + core


def permute(value, move):
    return lax.ppermute(value, AXES, [(i, move(*coords(i))) for i in range(N_DEV)])


def along(axis, sign):
    def move(x, y, z, core):
        step = sign if core == 0 else -sign
        x, y, z = (x + step) % 4 if axis == "x" else x, y + step if axis == "y" else y, z + step if axis == "z" else z
        return linear(x, y, z, core)

    return move


def offset(slot, core):
    return (0, 1 if core else 3, 3 if core else 1, 2)[slot]


def ring(block, axis):
    first = permute(block, along(axis, 1))
    second = permute(block, along(axis, -1))
    relayed = permute(first, along(axis, 1))
    return [block, first, second, relayed]


def gather(block, order):
    for axis in order[:2]:
        block = jnp.concatenate(ring(block, axis), axis=0)
    return ring(block, order[2])


def refit_kernel(table, master, out):
    for r in range(master.shape[0] // BLOCK):
        for c in range(master.shape[1] // BLOCK):
            at = (pl.ds(r * BLOCK, BLOCK), pl.ds(c * BLOCK, BLOCK))
            tile = master[at]
            amax = jnp.max(jnp.abs(tile), axis=(0, 1), keepdims=True)
            scale = ((amax + 1e-6) / 448.0).astype(jnp.bfloat16).astype(jnp.float32)
            coded = (tile * (1.0 / scale)).astype(jnp.bfloat16)
            out[at] = (coded.astype(jnp.float32) * scale).astype(jnp.bfloat16)


def refit(master, chunks, share):
    cols = master.shape[1]
    return pl.pallas_call(
        refit_kernel,
        grid_spec=pltpu.PrefetchScalarGridSpec(
            num_scalar_prefetch=1,
            grid=(8,),
            in_specs=[pl.BlockSpec((share, cols), lambda i, t: (t[i], 0))],
            out_specs=pl.BlockSpec((share, cols), lambda i, t: (i, 0)),
        ),
        out_shape=jax.ShapeDtypeStruct((8 * share, cols), jnp.bfloat16),
        cost_estimate=pl.CostEstimate(flops=8 * share * cols * 6, bytes_accessed=8 * share * cols * 6, transcendentals=0),
    )(chunks, master)


def product_kernel(where, mine, theirs, *refs):
    blocks, (out_mine, out_theirs, held, sems) = refs[:12], refs[12:]
    z_part, y_part, x_part = blocks[0:4], blocks[4:8], blocks[8:12]
    core, swap = where[0], where[1]

    def source_slot(xh, xl):
        if xl == 0:
            return 2 + 1 if xh else 0
        return jnp.where(swap == xh, 1, 2)

    def copies(n, go):
        xl, zs = n // 4, n % 4
        buf = n % 2
        sem = sems.at[buf]
        z0, zn = PARTS["z"]
        y0, yn = PARTS["y"]
        x0, xn = PARTS["x"]
        for xh in range(2):
            sx = source_slot(xh, xl)
            for ys in range(4):
                go(z_part[zs].at[ys * 4 + sx], held.at[buf, xh, ys, pl.ds(z0, zn)], sem)
                go(y_part[ys].at[sx * 4 + zs], held.at[buf, xh, ys, pl.ds(y0, yn)], sem)
            dst = held.at[buf, xh, :, pl.ds(x0, xn)]
            if xl == 0:
                go(x_part[sx].at[pl.ds(zs * 4, 4)], dst, sem)
            else:

                @pl.when(swap == xh)
                def _():
                    go(x_part[1].at[pl.ds(zs * 4, 4)], dst, sem)

                @pl.when(swap != xh)
                def _():
                    go(x_part[2].at[pl.ds(zs * 4, 4)], dst, sem)

    def start(src, dst, sem):
        pltpu.make_async_copy(src, dst, sem).start()

    copies(0, start)
    total_refs = (out_mine, out_theirs)
    for n in range(8):
        buf = n % 2
        pltpu.make_async_copy(held.at[buf], held.at[buf], sems.at[buf]).wait()
        if n < 7:
            copies(n + 1, start)
        rows = pl.ds(n * 512, 512)

        def body(g, _):
            xh, ys = g // 4, g % 4
            dy = jnp.where(ys == 0, 0, jnp.where(ys == 3, 2, jnp.where((ys == 1) == (core == 1), 1, 3)))
            acts = held[buf, xh, ys]
            for weight, total in ((mine, out_mine), (theirs, out_theirs)):
                product = jnp.dot(acts, weight[rows, :], preferred_element_type=jnp.float32)
                if n == 0:
                    total[xh, dy] = product
                else:
                    total[xh, dy] += product
            return 0

        lax.fori_loop(0, 8, body, 0)


def product(where, mine, theirs, blocks):
    out = jax.ShapeDtypeStruct((2, 4, 256, 256), jnp.float32)
    vmem = pl.BlockSpec(memory_space=pltpu.VMEM)
    return pl.pallas_call(
        product_kernel,
        in_specs=[pl.BlockSpec(memory_space=pltpu.SMEM), vmem, vmem] + [pl.BlockSpec(memory_space=pl.ANY)] * 12,
        out_specs=[vmem, vmem],
        out_shape=[out, out],
        scratch_shapes=[pltpu.VMEM((2, 2, 4, 256, 512), jnp.bfloat16), pltpu.SemaphoreType.DMA((2,))],
        compiler_params=pltpu.CompilerParams(vmem_limit_bytes=48 * 1024 * 1024),
        cost_estimate=pl.CostEstimate(flops=2 * 2048 * 4096 * 512, bytes_accessed=30 * 1024 * 1024, transcendentals=0),
    )(where, mine, theirs, *blocks)


def shards(master, activations, owner):
    group, tp = lax.axis_index("group"), lax.axis_index("tp")
    xh, y = group // 4, group % 4
    xl, z, core = tp // 8, tp // 2 % 4, tp % 2
    share = activations.shape[1]

    def chunks(c):
        table = []
        for n in range(8):
            zs = n % 4
            dz = jnp.where(c == 1, offset(zs, 1), offset(zs, 0))
            table.append((xl ^ (n // 4)) * 8 + (z + dz) % 4 * 2 + c)
        return jnp.stack(table).astype(jnp.int32)

    sent = refit(master, chunks(1 - core), share)
    mine = refit(master, chunks(core), share)
    theirs = permute(sent, lambda x, y, z, c: linear(x, y, z, 1 - c))

    blocks = []
    for axis in "zyx":
        at, count = PARTS[axis]
        blocks += gather(activations[None, at : at + count], ORDER[axis])

    where = jnp.stack([core, (xl == core).astype(jnp.int32)]).astype(jnp.int32)
    kept, passed = product(where, mine, theirs, blocks)
    passed = permute(passed.astype(jnp.bfloat16), lambda x, y, z, c: linear(x, y, z, 1 - c))
    total = (kept + passed.astype(jnp.float32)).astype(jnp.bfloat16)

    parts = []
    for eh in range(2):
        for dy in range(4):
            part = total[eh, dy]
            if eh or dy:
                part = permute(part, lambda x, y, z, c: linear((x + 2 * eh) % 4, y + dy, z, c))
            parts.append(part)
    parts = jnp.stack(parts)

    out = {}
    for dz in range(4):
        for cross in range(2):

            def move(x, y, z, c):
                return linear(x ^ (c ^ cross), y, z + dz, x % 2)

            dest = (xl ^ core ^ cross) * 4 + (z + dz) % 4
            section = owner[dest]
            index = ((section // 4) ^ xh) * 4 + (y - section % 4) % 4
            value = lax.dynamic_index_in_dim(parts, index, 0, keepdims=False)
            out[dz, cross] = permute(value, move)
    stacked = jnp.stack([out[dz, cross] for dz in range(4) for cross in range(2)])
    columns = []
    for zs in range(4):
        for c in range(2):
            cross = (xl ^ core) ^ c
            columns.append(lax.dynamic_index_in_dim(stacked, (z - zs) % 4 * 2 + cross, 0, keepdims=False))
    return jnp.concatenate(columns, axis=1)


def solution(mesh):
    in_specs = (P(None, ("group", "tp")), P("group", "tp"), P())
    out_specs = P("group", "tp")
    return jax.shard_map(shards, mesh=mesh, in_specs=in_specs, out_specs=out_specs, check_vma=False)
```

time: 1070 us -> 235 us (0.22)
  the two profiles are of different devices: /device:TPU:3 before, /device:TPU:0 now
where the time goes in v1:
time: 235 us; the launch traced here: 234 us
  waiting for transfers between devices  94.4 us (40%)
  starting transfers between devices  54.4 us (23%)
  Pallas kernels  45.2 us (19%)
  between operations  20.9 us (9%)
  local copies, waits for them, and re-layouts  16 us (7%)
  other arithmetic  3.54 us (2%)
    ppermute x44, waiting for transfers between devices, permute(): lax.ppermute(value, AXES, [(i, move(*coords(i))) for i in range(N_DEV)])  94.4 us
    ppermute x44, starting transfers between devices, permute(): lax.ppermute(value, AXES, [(i, move(*coords(i))) for i in range(N_DEV)])  54.4 us
    pallas_call x1, Pallas kernels, product(): pl.pallas_call(product_kernel, in_specs=[pl.BlockSpec(memory_space=pltpu....  30.2 us
    pallas_call x2, Pallas kernels, refit(): pl.pallas_call(refit_kernel, grid_spec=pltpu.PrefetchScalarGridSpec(num_s...  15 us
    unnamed x52, local copies, waits for them, and re-layouts  9.74 us
  transfers between devices with their start and end apart: 44, of which 20 were waited for; matrix products, arithmetic and copies ran while one was open for 5% of the time, Pallas kernels for 6%

profile of v1, /device:TPU:0, one launch (start us, length us, event | category | flops | bytes accessed | tf_op | source)
XLA Modules:
  0.0 234.4 jit_solution(12025064659809456758)
XLA Ops:
  0.0 0.9 slice_bitcast_fusion.8
  0.9 1.6 collective-permute-start.1
  2.5 1.7 collective-permute-start.2
  4.1 0.9 slice_bitcast_fusion.9
  5.1 2.1 collective-permute-start.10
  7.1 2.2 collective-permute-start.11
  9.3 1.6 collective-permute-start.19
  10.9 0.9 constant_dynamic-update-slice_fusion.20
  11.9 1.5 constant_dynamic-update-slice_fusion.6
  13.4 0.6 stack.138.table
  14.0 7.5 %shard_map.38 = bf16[4096,256]{1,0:T(8,128)(2,1)} custom-call(s32[8]{0:T(128)} %stack.138.table, f32[8192,256]{1,0:T(8,128)} %master.3), custom_call_target="tpu_custom_call" | custom-call | flops 6291456 | bytes 6291456 | tf_op jit(solution)/shard_map/pallas_call | solution.py:70
  21.5 1.7 collective-permute-start.20
  23.4 2.5 %collective-permute-done.20 = bf16[1,80,512]{2,1,0:T(8,128)(2,1)S(1)} collective-permute-done((bf16[1,80,512]{2,1,0:T(8,128)(2,1)S(1)}, bf16[1,80,512]{2,1,0:T(8,128)(2,1)S(1)}, u32[]{:S(2)}, u32[]{:S(2)}) %collective-permute-start.20) | collective-permute-done | bytes 81952 | tf_op jit(solution)/shard_map/ppermute | solution.py:28
  26.0 1.6 collective-permute-start.21
  27.9 0.6 constant_dynamic-update-slice_fusion.5
  28.6 0.7 constant_dynamic-update-slice_fusion.4
  29.2 4.2 %collective-permute-done.3 = bf16[1,96,512]{2,1,0:T(8,128)(2,1)S(1)} collective-permute-done((bf16[1,96,512]{2,1,0:T(8,128)(2,1)S(1)}, bf16[1,96,512]{2,1,0:T(8,128)(2,1)S(1)}, u32[]{:S(2)}, u32[]{:S(2)}) %collective-permute-start.3) | collective-permute-done | bytes 98336 | tf_op jit(solution)/shard_map/ppermute | solution.py:28
  33.5 1.4 collective-permute-start.4
  35.0 3.2 %collective-permute-start.14 = (bf16[4,80,512]{2,1,0:T(8,128)(2,1)S(1)}, bf16[4,80,512]{2,1,0:T(8,128)(2,1)S(1)}, u32[]{:S(2)}, u32[]{:S(2)}) collective-permute-start(bf16[4,80,512]{2,1,0:T(8,128)(2,1)S(1)} %pad_maximum_fusion.1), channel_id=1, source_target_pairs={{0,72},{1,9},{2,74},{3,11},{4,76},{5,13},{6,78},{7,15},{8,0},{9,65... | collective-permute-start | bytes 983048 | tf_op jit(solution)/shard_map/ppermute | solution.py:28
  38.3 2.0 collective-permute-start.5
  40.3 6.1 %collective-permute-done.4 = bf16[4,96,512]{2,1,0:T(8,128)(2,1)S(1)} collective-permute-done((bf16[4,96,512]{2,1,0:T(8,128)(2,1)S(1)}, bf16[4,96,512]{2,1,0:T(8,128)(2,1)S(1)}, u32[]{:S(2)}, u32[]{:S(2)}) %collective-permute-start.4) | collective-permute-done | bytes 393248 | tf_op jit(solution)/shard_map/ppermute | solution.py:28
  46.5 0.6 constant_dynamic-update-slice_fusion.3
  47.3 0.8 constant_dynamic-update-slice_fusion.2
  48.1 1.4 collective-permute-done.5
  49.5 1.8 collective-permute-start.23
  51.3 0.8 constant_dynamic-update-slice_fusion.1
  52.1 3.3 %collective-permute-done.6 = bf16[4,96,512]{2,1,0:T(8,128)(2,1)S(1)} collective-permute-done((bf16[4,96,512]{2,1,0:T(8,128)(2,1)S(1)}, bf16[4,96,512]{2,1,0:T(8,128)(2,1)S(1)}, u32[]{:S(2)}, u32[]{:S(2)}) %collective-permute-start.6) | collective-permute-done | bytes 393248 | tf_op jit(solution)/shard_map/ppermute | solution.py:28
  55.4 0.8 constant_dynamic-update-slice_fusion.refs_0_
  56.2 1.2 collective-permute-done.22
  57.6 1.8 collective-permute-done.23
  59.5 4.3 %collective-permute-done.15 = bf16[4,80,512]{2,1,0:T(8,128)(2,1)S(1)} collective-permute-done((bf16[4,80,512]{2,1,0:T(8,128)(2,1)S(1)}, bf16[4,80,512]{2,1,0:T(8,128)(2,1)S(1)}, u32[]{:S(2)}, u32[]{:S(2)}) %collective-permute-start.15) | collective-permute-done | bytes 327712 | tf_op jit(solution)/shard_map/ppermute | solution.py:28
  63.8 3.2 %collective-permute-start.17 = (bf16[16,80,512]{2,1,0:T(8,128)(2,1)S(1)}, bf16[16,80,512]{2,1,0:T(8,128)(2,1)S(1)}, u32[]{:S(2)}, u32[]{:S(2)}) collective-permute-start(bf16[16,80,512]{2,1,0:T(8,128)(2,1)S(1)} %constant_dynamic-update-slice_fusion.7.refs_4_), channel_id=1, source_target_pairs={{0,48},{1,17},{2,50},{3,19},{4,52},{5,21},{6,54},{7,23},{8,56},{9,... | collective-permute-start | bytes 3932168 | tf_op jit(solution)/shard_map/ppermute | solution.py:28
  67.1 16.4 %collective-permute-done.24 = bf16[4,80,512]{2,1,0:T(8,128)(2,1)S(1)} collective-permute-done((bf16[4,80,512]{2,1,0:T(8,128)(2,1)S(1)}, bf16[4,80,512]{2,1,0:T(8,128)(2,1)S(1)}, u32[]{:S(2)}, u32[]{:S(2)}) %collective-permute-start.24) | collective-permute-done | bytes 327712 | tf_op jit(solution)/shard_map/ppermute | solution.py:28
  83.5 0.7 constant_dynamic-update-slice_fusion.14.refs_8_
  84.3 2.0 collective-permute-start.9
  86.3 2.8 %collective-permute-done.16.refs_5_ = bf16[16,80,512]{2,1,0:T(8,128)(2,1)S(1)} collective-permute-done((bf16[16,80,512]{2,1,0:T(8,128)(2,1)S(1)}, bf16[16,80,512]{2,1,0:T(8,128)(2,1)S(1)}, u32[]{:S(2)}, u32[]{:S(2)}) %collective-permute-start.16) | collective-permute-done | bytes 1310752 | tf_op jit(solution)/shard_map/ppermute | solution.py:28
  89.1 3.3 %collective-permute-start.26 = (bf16[16,80,512]{2,1,0:T(8,128)(2,1)}, bf16[16,80,512]{2,1,0:T(8,128)(2,1)}, u32[]{:S(2)}, u32[]{:S(2)}) collective-permute-start(bf16[16,80,512]{2,1,0:T(8,128)(2,1)} %constant_dynamic-update-slice_fusion.14.refs_8_), channel_id=1, source_target_pairs={{0,72},{1,9},{2,74},{3,11},{4,76},{5,13},{6,78},{7,15},{8,0},{9,65... | collective-permute-start | bytes 3932168 | tf_op jit(solution)/shard_map/ppermute | solution.py:28
  92.5 1.1 copy-done
  93.6 19.4 %collective-permute-done.25.refs_9_ = bf16[16,80,512]{2,1,0:T(8,128)(2,1)} collective-permute-done((bf16[16,80,512]{2,1,0:T(8,128)(2,1)}, bf16[16,80,512]{2,1,0:T(8,128)(2,1)}, u32[]{:S(2)}, u32[]{:S(2)}) %collective-permute-start.25) | collective-permute-done | bytes 1310752 | tf_op jit(solution)/shard_map/ppermute | solution.py:28
  113.5 0.7 stack.129.table
  114.1 7.5 %shard_map.37.mine = bf16[4096,256]{1,0:T(8,128)(2,1)} custom-call(s32[8]{0:T(128)} %stack.129.table, f32[8192,256]{1,0:T(8,128)} %master.3), custom_call_target="tpu_custom_call" | custom-call | flops 6291456 | bytes 6291456 | tf_op jit(solution)/shard_map/pallas_call | solution.py:70
  121.7 10.4 %collective-permute-done.27.refs_11_ = bf16[16,80,512]{2,1,0:T(8,128)(2,1)} collective-permute-done((bf16[16,80,512]{2,1,0:T(8,128)(2,1)}, bf16[16,80,512]{2,1,0:T(8,128)(2,1)}, u32[]{:S(2)}, u32[]{:S(2)}) %collective-permute-start.27) | collective-permute-done | bytes 1310752 | tf_op jit(solution)/shard_map/ppermute | solution.py:28
  132.1 1.3 copy-done.1
  133.4 30.2 %shard_map.39 = (f32[2,4,256,256]{3,2,1,0:T(8,128)}, f32[2,4,256,256]{3,2,1,0:T(8,128)}) custom-call(s32[2]{0:T(128)S(1)} %pad_add_fusion.where, bf16[4096,256]{1,0:T(8,128)(2,1)} %shard_map.37.mine, bf16[4096,256]{1,0:T(8,128)(2,1)} %copy-done.6, bf16[16,96,512]{2,1,0:T(8,128)(2,1)} %constant_dynamic-update-slice_fusion.refs_0_, ...), custom_call_target="tpu_custom_call" | custom-call | flops 8589934592 | bytes 31457280 | tf_op jit(solution)/shard_map/pallas_call | solution.py:148
  163.6 1.9 convert_element_type.10
  165.7 0.7 fusion.1
  186.7 1.5 add_convert_fusion
  188.2 1.6 collective-permute-start.29
  189.8 3.0 %collective-permute-start.30 = (bf16[256,256]{1,0:T(8,128)(2,1)S(1)}, bf16[256,256]{1,0:T(8,128)(2,1)S(1)}, u32[]{:S(2)}, u32[]{:S(2)}) collective-permute-start(bf16[256,256]{1,0:T(8,128)(2,1)S(1)} %get-tuple-element.22), channel_id=1, source_target_pairs={{0,32},{1,33},{2,34},{3,35},{4,36},{5,37},{6,38},{7,39},{8,40},{9,... | collective-permute-start | bytes 393224 | tf_op jit(solution)/shard_map/ppermute | solution.py:28
  192.8 0.6 collective-permute-start.32
  193.4 4.4 %collective-permute-start.33 = (bf16[256,256]{1,0:T(8,128)(2,1)S(1)}, bf16[256,256]{1,0:T(8,128)(2,1)S(1)}, u32[]{:S(2)}, u32[]{:S(2)}) collective-permute-start(bf16[256,256]{1,0:T(8,128)(2,1)S(1)} %get-tuple-element.19), channel_id=1, source_target_pairs={{0,80},{1,81},{2,82},{3,83},{4,84},{5,85},{6,86},{7,87},{8,88},{9,... | collective-permute-start | bytes 393224 | tf_op jit(solution)/shard_map/ppermute | solution.py:28
  198.3 1.3 collective-permute-done.30
  199.6 3.1 %collective-permute-start.35 = (bf16[256,256]{1,0:T(8,128)(2,1)S(1)}, bf16[256,256]{1,0:T(8,128)(2,1)S(1)}, u32[]{:S(2)}, u32[]{:S(2)}) collective-permute-start(bf16[256,256]{1,0:T(8,128)(2,1)S(1)} %get-tuple-element.17), channel_id=1, source_target_pairs={{0,112},{1,113},{2,114},{3,115},{4,116},{5,117},{6,118},{7,119},{8... | collective-permute-start | bytes 393224 | tf_op jit(solution)/shard_map/ppermute | solution.py:28
  202.8 4.8 %collective-permute-done.34 = bf16[256,256]{1,0:T(8,128)(2,1)S(1)} collective-permute-done((bf16[256,256]{1,0:T(8,128)(2,1)S(1)}, bf16[256,256]{1,0:T(8,128)(2,1)S(1)}, u32[]{:S(2)}, u32[]{:S(2)}) %collective-permute-start.34) | collective-permute-done | bytes 131104 | tf_op jit(solution)/shard_map/ppermute | solution.py:28
  207.6 1.5 collective-permute-done.35
  209.2 0.7 collective-permute-start.36
  210.0 2.4 %collective-permute-start.37 = (bf16[256,256]{1,0:T(8,128)(2,1)S(1)}, bf16[256,256]{1,0:T(8,128)(2,1)S(1)}, u32[]{:S(2)}, u32[]{:S(2)}) collective-permute-start(bf16[256,256]{1,0:T(8,128)(2,1)S(1)} %get-tuple-element.15), channel_id=1, source_target_pairs={{0,8},{1,0},{2,10},{3,2},{4,12},{5,4},{6,14},{7,6},{8,1},{9,9},{10... | collective-permute-start | bytes 393224 | tf_op jit(solution)/shard_map/ppermute | solution.py:28
  212.8 3.6 %collective-permute-start.40 = (bf16[256,256]{1,0:T(8,128)(2,1)S(1)}, bf16[256,256]{1,0:T(8,128)(2,1)S(1)}, u32[]{:S(2)}, u32[]{:S(2)}) collective-permute-start(bf16[256,256]{1,0:T(8,128)(2,1)S(1)} %get-tuple-element.12), channel_id=1, source_target_pairs={{0,4},{1,12},{2,6},{3,14},{4,0},{5,8},{6,2},{7,10},{8,13},{9,5},{1... | collective-permute-start | bytes 393224 | tf_op jit(solution)/shard_map/ppermute | solution.py:28
  216.3 2.7 %collective-permute-start.41 = (bf16[256,256]{1,0:T(8,128)(2,1)S(1)}, bf16[256,256]{1,0:T(8,128)(2,1)S(1)}, u32[]{:S(2)}, u32[]{:S(2)}) collective-permute-start(bf16[256,256]{1,0:T(8,128)(2,1)S(1)} %get-tuple-element.11), channel_id=1, source_target_pairs={{0,12},{1,4},{2,14},{3,6},{4,8},{5,0},{6,10},{7,2},{8,5},{9,13},{1... | collective-permute-start | bytes 393224 | tf_op jit(solution)/shard_map/ppermute | solution.py:28
  219.0 0.7 collective-permute-start.42
  219.7 8.5 %collective-permute-done.38 = bf16[256,256]{1,0:T(8,128)(2,1)S(1)} collective-permute-done((bf16[256,256]{1,0:T(8,128)(2,1)S(1)}, bf16[256,256]{1,0:T(8,128)(2,1)S(1)}, u32[]{:S(2)}, u32[]{:S(2)}) %collective-permute-start.38) | collective-permute-done | bytes 131104 | tf_op jit(solution)/shard_map/ppermute | solution.py:28
  228.9 3.7 %collective-permute-done.43 = bf16[256,256]{1,0:T(8,128)(2,1)S(1)} collective-permute-done((bf16[256,256]{1,0:T(8,128)(2,1)S(1)}, bf16[256,256]{1,0:T(8,128)(2,1)S(1)}, u32[]{:S(2)}, u32[]{:S(2)}) %collective-permute-start.43) | collective-permute-done | bytes 131104 | tf_op jit(solution)/shard_map/ppermute | solution.py:28
  232.8 1.0 copy-done.4
  233.8 0.7 bitcast_dynamic-update-slice_fusion
  (98 shorter events, 4.0 us)
Async XLA Ops:
  0.9 26.7 %collective-permute-start.1 = (bf16[1,96,512]{2,1,0:T(8,128)(2,1)S(1)}, bf16[1,96,512]{2,1,0:T(8,128)(2,1)S(1)}, u32[]{:S(2)}, u32[]{:S(2)}) collective-permute-start(bf16[1,96,512]{2,1,0:T(8,128)(2,1)S(1)} %slice_bitcast_fusion.8), channel_id=1, source_target_pairs={{0,8},{1,73},{2,10},{3,75},{4,12},{5,77},{6,14},{7,79},{8,64},{9,1... | collective-permute-start | bytes 294920 | tf_op jit(solution)/shard_map/ppermute | solution.py:28
  2.5 26.1 %collective-permute-start.2 = (bf16[1,96,512]{2,1,0:T(8,128)(2,1)S(1)}, bf16[1,96,512]{2,1,0:T(8,128)(2,1)S(1)}, u32[]{:S(2)}, u32[]{:S(2)}) collective-permute-start(bf16[1,96,512]{2,1,0:T(8,128)(2,1)S(1)} %slice_bitcast_fusion.8), channel_id=1, source_target_pairs={{0,72},{1,9},{2,74},{3,11},{4,76},{5,13},{6,78},{7,15},{8,0},{9,65... | collective-permute-start | bytes 294920 | tf_op jit(solution)/shard_map/ppermute | solution.py:28
  5.1 16.5 %collective-permute-start.10 = (bf16[1,80,512]{2,1,0:T(8,128)(2,1)S(1)}, bf16[1,80,512]{2,1,0:T(8,128)(2,1)S(1)}, u32[]{:S(2)}, u32[]{:S(2)}) collective-permute-start(bf16[1,80,512]{2,1,0:T(8,128)(2,1)S(1)} %get-tuple-element.25), channel_id=1, source_target_pairs={{0,2},{1,7},{2,4},{3,1},{4,6},{5,3},{6,0},{7,5},{8,10},{9,15},{10,... | collective-permute-start | bytes 245768 | tf_op jit(solution)/shard_map/ppermute | solution.py:28
  7.1 16.1 %collective-permute-start.11 = (bf16[1,80,512]{2,1,0:T(8,128)(2,1)S(1)}, bf16[1,80,512]{2,1,0:T(8,128)(2,1)S(1)}, u32[]{:S(2)}, u32[]{:S(2)}) collective-permute-start(bf16[1,80,512]{2,1,0:T(8,128)(2,1)S(1)} %get-tuple-element.25), channel_id=1, source_target_pairs={{0,6},{1,3},{2,0},{3,5},{4,2},{5,7},{6,4},{7,1},{8,14},{9,11},{10,... | collective-permute-start | bytes 245768 | tf_op jit(solution)/shard_map/ppermute | solution.py:28
  9.3 14.0 %collective-permute-start.19 = (bf16[1,80,512]{2,1,0:T(8,128)(2,1)S(1)}, bf16[1,80,512]{2,1,0:T(8,128)(2,1)S(1)}, u32[]{:S(2)}, u32[]{:S(2)}) collective-permute-start(bf16[1,80,512]{2,1,0:T(8,128)(2,1)S(1)} %get-tuple-element.24), channel_id=1, source_target_pairs={{0,16},{1,49},{2,18},{3,51},{4,20},{5,53},{6,22},{7,55},{8,24},{9,... | collective-permute-start | bytes 245768 | tf_op jit(solution)/shard_map/ppermute | solution.py:28
  21.5 4.4 %collective-permute-start.20 = (bf16[1,80,512]{2,1,0:T(8,128)(2,1)S(1)}, bf16[1,80,512]{2,1,0:T(8,128)(2,1)S(1)}, u32[]{:S(2)}, u32[]{:S(2)}) collective-permute-start(bf16[1,80,512]{2,1,0:T(8,128)(2,1)S(1)} %get-tuple-element.24), channel_id=1, source_target_pairs={{0,48},{1,17},{2,50},{3,19},{4,52},{5,21},{6,54},{7,23},{8,56},{9,... | collective-permute-start | bytes 245768 | tf_op jit(solution)/shard_map/ppermute | solution.py:28
  23.2 61.0 %collective-permute-start = (bf16[4096,256]{1,0:T(8,128)(2,1)}, bf16[4096,256]{1,0:T(8,128)(2,1)S(1)}, u32[]{:S(2)}, u32[]{:S(2)}) collective-permute-start(bf16[4096,256]{1,0:T(8,128)(2,1)} %shard_map.38), channel_id=1, source_target_pairs={{0,1},{1,0},{2,3},{3,2},{4,5},{5,4},{6,7},{7,6},{8,9},{9,8},{10,11... | collective-permute-start | bytes 6291464 | tf_op jit(solution)/shard_map/ppermute | solution.py:28
  23.3 11.5 %collective-permute-start.12 = (bf16[1,80,512]{2,1,0:T(8,128)(2,1)S(1)}, bf16[1,80,512]{2,1,0:T(8,128)(2,1)S(1)}, u32[]{:S(2)}, u32[]{:S(2)}) collective-permute-start(bf16[1,80,512]{2,1,0:T(8,128)(2,1)S(1)} %collective-permute-done.10), channel_id=1, source_target_pairs={{0,2},{1,7},{2,4},{3,1},{4,6},{5,3},{6,0},{7,5},{8,10},{9,15},{10,... | collective-permute-start | bytes 245768 | tf_op jit(solution)/shard_map/ppermute | solution.py:28
  26.0 12.3 %collective-permute-start.21 = (bf16[1,80,512]{2,1,0:T(8,128)(2,1)S(1)}, bf16[1,80,512]{2,1,0:T(8,128)(2,1)S(1)}, u32[]{:S(2)}, u32[]{:S(2)}) collective-permute-start(bf16[1,80,512]{2,1,0:T(8,128)(2,1)S(1)} %collective-permute-done.19), channel_id=1, source_target_pairs={{0,16},{1,49},{2,18},{3,51},{4,20},{5,53},{6,22},{7,55},{8,24},{9,... | collective-permute-start | bytes 245768 | tf_op jit(solution)/shard_map/ppermute | solution.py:28
  27.6 5.9 %collective-permute-start.3 = (bf16[1,96,512]{2,1,0:T(8,128)(2,1)S(1)}, bf16[1,96,512]{2,1,0:T(8,128)(2,1)S(1)}, u32[]{:S(2)}, u32[]{:S(2)}) collective-permute-start(bf16[1,96,512]{2,1,0:T(8,128)(2,1)S(1)} %collective-permute-done.1), channel_id=1, source_target_pairs={{0,8},{1,73},{2,10},{3,75},{4,12},{5,77},{6,14},{7,79},{8,64},{9,1... | collective-permute-start | bytes 294920 | tf_op jit(solution)/shard_map/ppermute | solution.py:28
  33.5 12.9 %collective-permute-start.4 = (bf16[4,96,512]{2,1,0:T(8,128)(2,1)S(1)}, bf16[4,96,512]{2,1,0:T(8,128)(2,1)S(1)}, u32[]{:S(2)}, u32[]{:S(2)}) collective-permute-start(bf16[4,96,512]{2,1,0:T(8,128)(2,1)S(1)} %pad_maximum_fusion), channel_id=1, source_target_pairs={{0,16},{1,49},{2,18},{3,51},{4,20},{5,53},{6,22},{7,55},{8,24},{9,... | collective-permute-start | bytes 1179656 | tf_op jit(solution)/shard_map/ppermute | solution.py:28
  34.9 12.2 %collective-permute-start.13 = (bf16[4,80,512]{2,1,0:T(8,128)(2,1)S(1)}, bf16[4,80,512]{2,1,0:T(8,128)(2,1)S(1)}, u32[]{:S(2)}, u32[]{:S(2)}) collective-permute-start(bf16[4,80,512]{2,1,0:T(8,128)(2,1)S(1)} %pad_maximum_fusion.1), channel_id=1, source_target_pairs={{0,8},{1,73},{2,10},{3,75},{4,12},{5,77},{6,14},{7,79},{8,64},{9,1... | collective-permute-start | bytes 983048 | tf_op jit(solution)/shard_map/ppermute | solution.py:28
  35.0 22.5 %collective-permute-start.14 = (bf16[4,80,512]{2,1,0:T(8,128)(2,1)S(1)}, bf16[4,80,512]{2,1,0:T(8,128)(2,1)S(1)}, u32[]{:S(2)}, u32[]{:S(2)}) collective-permute-start(bf16[4,80,512]{2,1,0:T(8,128)(2,1)S(1)} %pad_maximum_fusion.1), channel_id=1, source_target_pairs={{0,72},{1,9},{2,74},{3,11},{4,76},{5,13},{6,78},{7,15},{8,0},{9,65... | collective-permute-start | bytes 983048 | tf_op jit(solution)/shard_map/ppermute | solution.py:28
  38.3 11.2 %collective-permute-start.5 = (bf16[4,96,512]{2,1,0:T(8,128)(2,1)S(1)}, bf16[4,96,512]{2,1,0:T(8,128)(2,1)S(1)}, u32[]{:S(2)}, u32[]{:S(2)}) collective-permute-start(bf16[4,96,512]{2,1,0:T(8,128)(2,1)S(1)} %pad_maximum_fusion), channel_id=1, source_target_pairs={{0,48},{1,17},{2,50},{3,19},{4,52},{5,21},{6,54},{7,23},{8,56},{9,... | collective-permute-start | bytes 1179656 | tf_op jit(solution)/shard_map/ppermute | solution.py:28
  46.4 9.0 %collective-permute-start.6 = (bf16[4,96,512]{2,1,0:T(8,128)(2,1)S(1)}, bf16[4,96,512]{2,1,0:T(8,128)(2,1)S(1)}, u32[]{:S(2)}, u32[]{:S(2)}) collective-permute-start(bf16[4,96,512]{2,1,0:T(8,128)(2,1)S(1)} %collective-permute-done.4), channel_id=1, source_target_pairs={{0,16},{1,49},{2,18},{3,51},{4,20},{5,53},{6,22},{7,55},{8,24},{9,... | collective-permute-start | bytes 1179656 | tf_op jit(solution)/shard_map/ppermute | solution.py:28
  47.1 10.3 %collective-permute-start.22 = (bf16[4,80,512]{2,1,0:T(8,128)(2,1)S(1)}, bf16[4,80,512]{2,1,0:T(8,128)(2,1)S(1)}, u32[]{:S(2)}, u32[]{:S(2)}) collective-permute-start(bf16[4,80,512]{2,1,0:T(8,128)(2,1)S(1)} %pad_maximum_fusion.2), channel_id=1, source_target_pairs={{0,2},{1,7},{2,4},{3,1},{4,6},{5,3},{6,0},{7,5},{8,10},{9,15},{10,... | collective-permute-start | bytes 983048 | tf_op jit(solution)/shard_map/ppermute | solution.py:28
  49.5 9.9 %collective-permute-start.23 = (bf16[4,80,512]{2,1,0:T(8,128)(2,1)S(1)}, bf16[4,80,512]{2,1,0:T(8,128)(2,1)S(1)}, u32[]{:S(2)}, u32[]{:S(2)}) collective-permute-start(bf16[4,80,512]{2,1,0:T(8,128)(2,1)S(1)} %pad_maximum_fusion.2), channel_id=1, source_target_pairs={{0,6},{1,3},{2,0},{3,5},{4,2},{5,7},{6,4},{7,1},{8,14},{9,11},{10,... | collective-permute-start | bytes 983048 | tf_op jit(solution)/shard_map/ppermute | solution.py:28
  55.4 8.3 %collective-permute-start.15 = (bf16[4,80,512]{2,1,0:T(8,128)(2,1)S(1)}, bf16[4,80,512]{2,1,0:T(8,128)(2,1)S(1)}, u32[]{:S(2)}, u32[]{:S(2)}) collective-permute-start(bf16[4,80,512]{2,1,0:T(8,128)(2,1)S(1)} %collective-permute-done.13), channel_id=1, source_target_pairs={{0,8},{1,73},{2,10},{3,75},{4,12},{5,77},{6,14},{7,79},{8,64},{9,1... | collective-permute-start | bytes 983048 | tf_op jit(solution)/shard_map/ppermute | solution.py:28
  57.4 26.9 %collective-permute-start.7 = (bf16[16,96,512]{2,1,0:T(8,128)(2,1)}, bf16[16,96,512]{2,1,0:T(8,128)(2,1)}, u32[]{:S(2)}, u32[]{:S(2)}) collective-permute-start(bf16[16,96,512]{2,1,0:T(8,128)(2,1)} %constant_dynamic-update-slice_fusion.refs_0_), channel_id=1, source_target_pairs={{0,2},{1,7},{2,4},{3,1},{4,6},{5,3},{6,0},{7,5},{8,10},{9,15},{10,... | collective-permute-start | bytes 4718600 | tf_op jit(solution)/shard_map/ppermute | solution.py:28
  57.5 26.0 %collective-permute-start.24 = (bf16[4,80,512]{2,1,0:T(8,128)(2,1)S(1)}, bf16[4,80,512]{2,1,0:T(8,128)(2,1)S(1)}, u32[]{:S(2)}, u32[]{:S(2)}) collective-permute-start(bf16[4,80,512]{2,1,0:T(8,128)(2,1)S(1)} %collective-permute-done.22), channel_id=1, source_target_pairs={{0,2},{1,7},{2,4},{3,1},{4,6},{5,3},{6,0},{7,5},{8,10},{9,15},{10,... | collective-permute-start | bytes 983048 | tf_op jit(solution)/shard_map/ppermute | solution.py:28
  59.4 4.3 %copy-start.5 = (bf16[16,80,512]{2,1,0:T(8,128)(2,1)}, bf16[16,80,512]{2,1,0:T(8,128)(2,1)S(1)}, u32[]{:S(2)}) copy-start(bf16[16,80,512]{2,1,0:T(8,128)(2,1)S(1)} %constant_dynamic-update-slice_fusion.15) | copy-start | bytes 3932164
  63.8 25.4 %collective-permute-start.16 = (bf16[16,80,512]{2,1,0:T(8,128)(2,1)S(1)}, bf16[16,80,512]{2,1,0:T(8,128)(2,1)S(1)}, u32[]{:S(2)}, u32[]{:S(2)}) collective-permute-start(bf16[16,80,512]{2,1,0:T(8,128)(2,1)S(1)} %constant_dynamic-update-slice_fusion.7.refs_4_), channel_id=1, source_target_pairs={{0,16},{1,49},{2,18},{3,51},{4,20},{5,53},{6,22},{7,55},{8,24},{9,... | collective-permute-start | bytes 3932168 | tf_op jit(solution)/shard_map/ppermute | solution.py:28
  63.8 28.6 %collective-permute-start.17 = (bf16[16,80,512]{2,1,0:T(8,128)(2,1)S(1)}, bf16[16,80,512]{2,1,0:T(8,128)(2,1)S(1)}, u32[]{:S(2)}, u32[]{:S(2)}) collective-permute-start(bf16[16,80,512]{2,1,0:T(8,128)(2,1)S(1)} %constant_dynamic-update-slice_fusion.7.refs_4_), channel_id=1, source_target_pairs={{0,48},{1,17},{2,50},{3,19},{4,52},{5,21},{6,54},{7,23},{8,56},{9,... | collective-permute-start | bytes 3932168 | tf_op jit(solution)/shard_map/ppermute | solution.py:28
  84.2 28.7 %collective-permute-start.25 = (bf16[16,80,512]{2,1,0:T(8,128)(2,1)}, bf16[16,80,512]{2,1,0:T(8,128)(2,1)}, u32[]{:S(2)}, u32[]{:S(2)}) collective-permute-start(bf16[16,80,512]{2,1,0:T(8,128)(2,1)} %constant_dynamic-update-slice_fusion.14.refs_8_), channel_id=1, source_target_pairs={{0,8},{1,73},{2,10},{3,75},{4,12},{5,77},{6,14},{7,79},{8,64},{9,1... | collective-permute-start | bytes 3932168 | tf_op jit(solution)/shard_map/ppermute | solution.py:28
  84.2 8.2 %copy-start.6 = (bf16[4096,256]{1,0:T(8,128)(2,1)}, bf16[4096,256]{1,0:T(8,128)(2,1)S(1)}, u32[]{:S(2)}) copy-start(bf16[4096,256]{1,0:T(8,128)(2,1)S(1)} %collective-permute-done.theirs) | copy-start | bytes 6291460
  84.2 37.5 %collective-permute-start.8 = (bf16[16,96,512]{2,1,0:T(8,128)(2,1)}, bf16[16,96,512]{2,1,0:T(8,128)(2,1)}, u32[]{:S(2)}, u32[]{:S(2)}) collective-permute-start(bf16[16,96,512]{2,1,0:T(8,128)(2,1)} %constant_dynamic-update-slice_fusion.refs_0_), channel_id=1, source_target_pairs={{0,6},{1,3},{2,0},{3,5},{4,2},{5,7},{6,4},{7,1},{8,14},{9,11},{10,... | collective-permute-start | bytes 4718600 | tf_op jit(solution)/shard_map/ppermute | solution.py:28
  84.3 47.8 %collective-permute-start.9 = (bf16[16,96,512]{2,1,0:T(8,128)(2,1)}, bf16[16,96,512]{2,1,0:T(8,128)(2,1)}, u32[]{:S(2)}, u32[]{:S(2)}) collective-permute-start(bf16[16,96,512]{2,1,0:T(8,128)(2,1)} %collective-permute-done.7.refs_1_), channel_id=1, source_target_pairs={{0,2},{1,7},{2,4},{3,1},{4,6},{5,3},{6,0},{7,5},{8,10},{9,15},{10,... | collective-permute-start | bytes 4718600 | tf_op jit(solution)/shard_map/ppermute | solution.py:28
  89.1 32.6 %collective-permute-start.26 = (bf16[16,80,512]{2,1,0:T(8,128)(2,1)}, bf16[16,80,512]{2,1,0:T(8,128)(2,1)}, u32[]{:S(2)}, u32[]{:S(2)}) collective-permute-start(bf16[16,80,512]{2,1,0:T(8,128)(2,1)} %constant_dynamic-update-slice_fusion.14.refs_8_), channel_id=1, source_target_pairs={{0,72},{1,9},{2,74},{3,11},{4,76},{5,13},{6,78},{7,15},{8,0},{9,65... | collective-permute-start | bytes 3932168 | tf_op jit(solution)/shard_map/ppermute | solution.py:28
  92.5 1.1 copy-start
  93.5 28.2 %collective-permute-start.18 = (bf16[16,80,512]{2,1,0:T(8,128)(2,1)S(1)}, bf16[16,80,512]{2,1,0:T(8,128)(2,1)}, u32[]{:S(2)}, u32[]{:S(2)}) collective-permute-start(bf16[16,80,512]{2,1,0:T(8,128)(2,1)S(1)} %collective-permute-done.16.refs_5_), channel_id=1, source_target_pairs={{0,16},{1,49},{2,18},{3,51},{4,20},{5,53},{6,22},{7,55},{8,24},{9,... | collective-permute-start | bytes 3932168 | tf_op jit(solution)/shard_map/ppermute | solution.py:28
  113.0 19.1 %collective-permute-start.27 = (bf16[16,80,512]{2,1,0:T(8,128)(2,1)}, bf16[16,80,512]{2,1,0:T(8,128)(2,1)}, u32[]{:S(2)}, u32[]{:S(2)}) collective-permute-start(bf16[16,80,512]{2,1,0:T(8,128)(2,1)} %collective-permute-done.25.refs_9_), channel_id=1, source_target_pairs={{0,8},{1,73},{2,10},{3,75},{4,12},{5,77},{6,14},{7,79},{8,64},{9,1... | collective-permute-start | bytes 3932168 | tf_op jit(solution)/shard_map/ppermute | solution.py:28
  132.1 1.3 copy-start.1
  163.6 2.1 copy-start.3
  163.6 23.0 %copy-start.2 = (f32[2,4,256,256]{3,2,1,0:T(8,128)S(1)}, f32[2,4,256,256]{3,2,1,0:T(8,128)}, u32[]{:S(2)}) copy-start(f32[2,4,256,256]{3,2,1,0:T(8,128)} %get-tuple-element.7) | copy-start | bytes 6291460
  165.5 21.2 %collective-permute-start.28 = (bf16[2,4,256,256]{3,2,1,0:T(8,128)(2,1)S(1)}, bf16[2,4,256,256]{3,2,1,0:T(8,128)(2,1)}, u32[]{:S(2)}, u32[]{:S(2)}) collective-permute-start(bf16[2,4,256,256]{3,2,1,0:T(8,128)(2,1)S(1)} %convert_element_type.10), channel_id=1, source_target_pairs={{0,1},{1,0},{2,3},{3,2},{4,5},{5,4},{6,7},{7,6},{8,9},{9,8},{10,11... | collective-permute-start | bytes 3145736 | tf_op jit(solution)/shard_map/ppermute | solution.py:28
  188.2 9.6 %collective-permute-start.29 = (bf16[256,256]{1,0:T(8,128)(2,1)S(1)}, bf16[256,256]{1,0:T(8,128)(2,1)S(1)}, u32[]{:S(2)}, u32[]{:S(2)}) collective-permute-start(bf16[256,256]{1,0:T(8,128)(2,1)S(1)} %get-tuple-element.23), channel_id=1, source_target_pairs={{0,16},{1,17},{2,18},{3,19},{4,20},{5,21},{6,22},{7,23},{8,24},{9,... | collective-permute-start | bytes 393224 | tf_op jit(solution)/shard_map/ppermute | solution.py:28
  189.8 9.8 %collective-permute-start.30 = (bf16[256,256]{1,0:T(8,128)(2,1)S(1)}, bf16[256,256]{1,0:T(8,128)(2,1)S(1)}, u32[]{:S(2)}, u32[]{:S(2)}) collective-permute-start(bf16[256,256]{1,0:T(8,128)(2,1)S(1)} %get-tuple-element.22), channel_id=1, source_target_pairs={{0,32},{1,33},{2,34},{3,35},{4,36},{5,37},{6,38},{7,39},{8,40},{9,... | collective-permute-start | bytes 393224 | tf_op jit(solution)/shard_map/ppermute | solution.py:28
  192.8 9.9 %collective-permute-start.31 = (bf16[256,256]{1,0:T(8,128)(2,1)S(1)}, bf16[256,256]{1,0:T(8,128)(2,1)S(1)}, u32[]{:S(2)}, u32[]{:S(2)}) collective-permute-start(bf16[256,256]{1,0:T(8,128)(2,1)S(1)} %get-tuple-element.21), channel_id=1, source_target_pairs={{0,48},{1,49},{2,50},{3,51},{4,52},{5,53},{6,54},{7,55},{8,56},{9,... | collective-permute-start | bytes 393224 | tf_op jit(solution)/shard_map/ppermute | solution.py:28
  192.8 9.9 %collective-permute-start.32 = (bf16[256,256]{1,0:T(8,128)(2,1)S(1)}, bf16[256,256]{1,0:T(8,128)(2,1)S(1)}, u32[]{:S(2)}, u32[]{:S(2)}) collective-permute-start(bf16[256,256]{1,0:T(8,128)(2,1)S(1)} %get-tuple-element.20), channel_id=1, source_target_pairs={{0,64},{1,65},{2,66},{3,67},{4,68},{5,69},{6,70},{7,71},{8,72},{9,... | collective-permute-start | bytes 393224 | tf_op jit(solution)/shard_map/ppermute | solution.py:28
  193.4 9.4 %collective-permute-start.33 = (bf16[256,256]{1,0:T(8,128)(2,1)S(1)}, bf16[256,256]{1,0:T(8,128)(2,1)S(1)}, u32[]{:S(2)}, u32[]{:S(2)}) collective-permute-start(bf16[256,256]{1,0:T(8,128)(2,1)S(1)} %get-tuple-element.19), channel_id=1, source_target_pairs={{0,80},{1,81},{2,82},{3,83},{4,84},{5,85},{6,86},{7,87},{8,88},{9,... | collective-permute-start | bytes 393224 | tf_op jit(solution)/shard_map/ppermute | solution.py:28
  197.8 9.8 %collective-permute-start.34 = (bf16[256,256]{1,0:T(8,128)(2,1)S(1)}, bf16[256,256]{1,0:T(8,128)(2,1)S(1)}, u32[]{:S(2)}, u32[]{:S(2)}) collective-permute-start(bf16[256,256]{1,0:T(8,128)(2,1)S(1)} %get-tuple-element.18), channel_id=1, source_target_pairs={{0,96},{1,97},{2,98},{3,99},{4,100},{5,101},{6,102},{7,103},{8,104... | collective-permute-start | bytes 393224 | tf_op jit(solution)/shard_map/ppermute | solution.py:28
  199.6 9.5 %collective-permute-start.35 = (bf16[256,256]{1,0:T(8,128)(2,1)S(1)}, bf16[256,256]{1,0:T(8,128)(2,1)S(1)}, u32[]{:S(2)}, u32[]{:S(2)}) collective-permute-start(bf16[256,256]{1,0:T(8,128)(2,1)S(1)} %get-tuple-element.17), channel_id=1, source_target_pairs={{0,112},{1,113},{2,114},{3,115},{4,116},{5,117},{6,118},{7,119},{8... | collective-permute-start | bytes 393224 | tf_op jit(solution)/shard_map/ppermute | solution.py:28
  209.2 7.1 %collective-permute-start.36 = (bf16[256,256]{1,0:T(8,128)(2,1)S(1)}, bf16[256,256]{1,0:T(8,128)(2,1)S(1)}, u32[]{:S(2)}, u32[]{:S(2)}) collective-permute-start(bf16[256,256]{1,0:T(8,128)(2,1)S(1)} %get-tuple-element.16), channel_id=1, source_target_pairs={{0,0},{1,8},{2,2},{3,10},{4,4},{5,12},{6,6},{7,14},{8,9},{9,1},{10... | collective-permute-start | bytes 393224 | tf_op jit(solution)/shard_map/ppermute | solution.py:28
  210.0 9.0 %collective-permute-start.37 = (bf16[256,256]{1,0:T(8,128)(2,1)S(1)}, bf16[256,256]{1,0:T(8,128)(2,1)S(1)}, u32[]{:S(2)}, u32[]{:S(2)}) collective-permute-start(bf16[256,256]{1,0:T(8,128)(2,1)S(1)} %get-tuple-element.15), channel_id=1, source_target_pairs={{0,8},{1,0},{2,10},{3,2},{4,12},{5,4},{6,14},{7,6},{8,1},{9,9},{10... | collective-permute-start | bytes 393224 | tf_op jit(solution)/shard_map/ppermute | solution.py:28
  212.4 15.8 %collective-permute-start.38 = (bf16[256,256]{1,0:T(8,128)(2,1)S(1)}, bf16[256,256]{1,0:T(8,128)(2,1)S(1)}, u32[]{:S(2)}, u32[]{:S(2)}) collective-permute-start(bf16[256,256]{1,0:T(8,128)(2,1)S(1)} %get-tuple-element.14), channel_id=1, source_target_pairs={{0,2},{1,10},{2,4},{3,12},{4,6},{5,14},{6,0},{7,8},{8,11},{9,3},{1... | collective-permute-start | bytes 393224 | tf_op jit(solution)/shard_map/ppermute | solution.py:28
  212.5 16.0 %collective-permute-start.39 = (bf16[256,256]{1,0:T(8,128)(2,1)S(1)}, bf16[256,256]{1,0:T(8,128)(2,1)S(1)}, u32[]{:S(2)}, u32[]{:S(2)}) collective-permute-start(bf16[256,256]{1,0:T(8,128)(2,1)S(1)} %get-tuple-element.13), channel_id=1, source_target_pairs={{0,10},{1,2},{2,12},{3,4},{4,14},{5,6},{6,8},{7,0},{8,3},{9,11},{1... | collective-permute-start | bytes 393224 | tf_op jit(solution)/shard_map/ppermute | solution.py:28
  212.8 15.7 %collective-permute-start.40 = (bf16[256,256]{1,0:T(8,128)(2,1)S(1)}, bf16[256,256]{1,0:T(8,128)(2,1)S(1)}, u32[]{:S(2)}, u32[]{:S(2)}) collective-permute-start(bf16[256,256]{1,0:T(8,128)(2,1)S(1)} %get-tuple-element.12), channel_id=1, source_target_pairs={{0,4},{1,12},{2,6},{3,14},{4,0},{5,8},{6,2},{7,10},{8,13},{9,5},{1... | collective-permute-start | bytes 393224 | tf_op jit(solution)/shard_map/ppermute | solution.py:28
  216.3 12.2 %collective-permute-start.41 = (bf16[256,256]{1,0:T(8,128)(2,1)S(1)}, bf16[256,256]{1,0:T(8,128)(2,1)S(1)}, u32[]{:S(2)}, u32[]{:S(2)}) collective-permute-start(bf16[256,256]{1,0:T(8,128)(2,1)S(1)} %get-tuple-element.11), channel_id=1, source_target_pairs={{0,12},{1,4},{2,14},{3,6},{4,8},{5,0},{6,10},{7,2},{8,5},{9,13},{1... | collective-permute-start | bytes 393224 | tf_op jit(solution)/shard_map/ppermute | solution.py:28
  219.0 9.9 %collective-permute-start.42 = (bf16[256,256]{1,0:T(8,128)(2,1)S(1)}, bf16[256,256]{1,0:T(8,128)(2,1)S(1)}, u32[]{:S(2)}, u32[]{:S(2)}) collective-permute-start(bf16[256,256]{1,0:T(8,128)(2,1)S(1)} %get-tuple-element.10), channel_id=1, source_target_pairs={{0,6},{1,14},{2,0},{3,8},{4,2},{5,10},{6,4},{7,12},{8,15},{9,7},{1... | collective-permute-start | bytes 393224 | tf_op jit(solution)/shard_map/ppermute | solution.py:28
  228.2 4.4 %collective-permute-start.43 = (bf16[256,256]{1,0:T(8,128)(2,1)S(1)}, bf16[256,256]{1,0:T(8,128)(2,1)S(1)}, u32[]{:S(2)}, u32[]{:S(2)}) collective-permute-start(bf16[256,256]{1,0:T(8,128)(2,1)S(1)} %get-tuple-element.9), channel_id=1, source_target_pairs={{0,14},{1,6},{2,8},{3,0},{4,10},{5,2},{6,12},{7,4},{8,7},{9,15},{1... | collective-permute-start | bytes 393224 | tf_op jit(solution)/shard_map/ppermute | solution.py:28
  232.8 1.0 copy-start.4

commit v2 on v0

v2 whole, which is shorter than its diff:
```python
import functools

import jax
import jax.numpy as jnp
import numpy as np
from jax import lax
from jax.experimental import pallas as pl
from jax.experimental.pallas import tpu as pltpu
from jax.sharding import PartitionSpec as P

BLOCK = 128
AXES = ("group", "tp")
N_DEV = 128
SHARE = 512
COLS = 256
PARTS = {"z": (0, 96), "y": (96, 80), "x": (176, 80)}
ORDER = {"z": "xyz", "y": "zxy", "x": "yzx"}
MIB = 1024 * 1024


def coords(i):
    return i // 64 * 2 + i // 8 % 2, i // 16 % 4, i // 2 % 4, i % 2


def linear(x, y, z, core):
    x, y, z = x % 4, y % 4, z % 4
    return x // 2 * 64 + y * 16 + x % 2 * 8 + z * 2 + core


def permute(value, move):
    return lax.ppermute(value, AXES, [(i, move(*coords(i))) for i in range(N_DEV)])


def offset(slot, at, core):
    step = -1 if (at + core) % 2 else 1
    return (0, step, -step, 2)[slot] % 4


def exchange(value, axis, which):
    def move(x, y, z, core):
        at = {"x": x, "y": y, "z": z}
        at[axis] += offset(which, at[axis], core)
        return linear(at["x"], at["y"], at["z"], core)

    return permute(value, move)


def gather(block, order):
    for axis in order[:2]:
        for which in (1, 2):
            block = jnp.concatenate([block, exchange(block, axis, which)], axis=0)
    axis = order[2]
    first = exchange(block, axis, 1)
    second = exchange(block, axis, 2)
    relayed = exchange(first, axis, 2)
    return [v.reshape(4, 4, *v.shape[1:]) for v in (block, first, second, relayed)]


MINE, THEIRS, CORE, SLOT_OFFSET, XH, Y, DEST, SOURCE, WIDTH = 0, 8, 16, 17, 21, 22, 23, 31, 39


def device_row(i):
    x, y, z, core = coords(i)
    xh, xl = x // 2, x % 2

    def chunks(c):
        return [(xl ^ n // 4) * 8 + (z + offset(n % 4, z, c)) % 4 * 2 + c for n in range(8)]

    dest, source = [], []
    for dz in range(4):
        for cross in range(2):
            dest.append((xl ^ core ^ cross) * 4 + (z + dz) % 4)
    for zs in range(4):
        for c in range(2):
            source.append((z - zs) % 4 * 2 + (xl ^ core ^ c))
    row = chunks(core) + chunks(1 - core) + [core] + [offset(s, y, core) for s in range(4)] + [xh, y] + dest + source
    assert len(row) == WIDTH
    return row


def refit_kernel(table, master, out):
    for r in range(master.shape[0] // BLOCK):
        for c in range(master.shape[1] // BLOCK):
            at = (pl.ds(r * BLOCK, BLOCK), pl.ds(c * BLOCK, BLOCK))
            tile = master[at]
            amax = jnp.max(jnp.max(jnp.abs(tile), axis=0, keepdims=True), axis=1, keepdims=True)
            scale = ((amax + 1e-6) / 448.0).astype(jnp.bfloat16).astype(jnp.float32)
            coded = (tile * (1.0 / scale)).astype(jnp.bfloat16)
            out[at] = (coded.astype(jnp.float32) * scale).astype(jnp.bfloat16)


def refit(table, master, first):
    size = 8 * SHARE * COLS
    return pl.pallas_call(
        refit_kernel,
        grid_spec=pltpu.PrefetchScalarGridSpec(
            num_scalar_prefetch=1,
            grid=(8,),
            in_specs=[pl.BlockSpec((SHARE, COLS), lambda i, t: (t[first + i], 0))],
            out_specs=pl.BlockSpec((SHARE, COLS), lambda i, t: (i, 0)),
        ),
        out_shape=jax.ShapeDtypeStruct((8 * SHARE, COLS), jnp.bfloat16),
        cost_estimate=pl.CostEstimate(flops=size * 6, bytes_accessed=size * 6, transcendentals=0),
    )(table, master)


def rows_of(axis):
    at, count = PARTS[axis]
    return pl.ds(at, count)


def product_kernel(slots, n_weights, first, table, *refs):
    refs = list(refs)

    def take(count):
        got = refs[:count]
        del refs[:count]
        return got

    n = len(slots)
    weights = take(n_weights)
    z_part, y_part, x_part = take(n), take(n), take(n)
    before = [None] * n_weights if first else take(n_weights)
    outs = take(n_weights)
    z_held, y_held, x_held, sems = refs
    core = table[CORE]
    halves = ((0, 0), (core, 1), (1 - core, 1), (1, 0))
    zn, yn, xn = (PARTS[a][1] for a in "zyx")

    for i in range(n):
        for sx, (eh, el) in enumerate(halves):
            pltpu.make_async_copy(
                z_part[i].at[:, sx], z_held.at[i, pl.ds(eh * 4, 4), :, pl.ds(el * SHARE, SHARE)], sems.at[i, 0]
            ).start()
            for zs in range(4):
                pltpu.make_async_copy(
                    y_part[i].at[sx, zs], y_held.at[i, eh, :, pl.ds((el * 4 + zs) * SHARE, SHARE)], sems.at[i, 1]
                ).start()
        for zs in range(4):
            pltpu.make_async_copy(
                x_part[i].at[zs], x_held.at[i, :, :, pl.ds(zs * SHARE, SHARE)], sems.at[i, 2]
            ).start()

    def dot(a, b):
        return jnp.dot(a, b, preferred_element_type=jnp.float32)

    def ready(held, i, which):
        pltpu.make_async_copy(held.at[i], held.at[i], sems.at[i, which]).wait()

    z_rows, y_rows, x_rows = rows_of("z"), rows_of("y"), rows_of("x")
    for i, slot in enumerate(slots):
        ready(z_held, i, 0)
        for weight, out, old in zip(weights, outs, before):
            for eh in range(2):
                acts = z_held[i, pl.ds(eh * 4, 4)].reshape(4 * zn, 2 * SHARE)
                got = dot(acts[:, :SHARE], weight[pl.ds(slot * SHARE, SHARE), :])
                got += dot(acts[:, SHARE:], weight[pl.ds((4 + slot) * SHARE, SHARE), :])
                got = got.reshape(4, zn, COLS)
                if first:
                    if i == 0:
                        out[eh, :, z_rows, :] = got
                    else:
                        out[eh, :, z_rows, :] += got
                else:
                    for ys in range(4):
                        value = old[eh, ys, z_rows, :] + got[ys]
                        out[eh, table[SLOT_OFFSET + ys], z_rows, :] = value.astype(out.dtype)
        ready(y_held, i, 1)
        acts = y_held[i].reshape(2 * yn, 8 * SHARE)
        for weight, out, old in zip(weights, outs, before):
            got = dot(acts, weight[...]).reshape(2, yn, COLS)
            if first:
                out[:, slot, y_rows, :] = got
            else:
                for eh in range(2):
                    for ys in range(4):
                        value = got[eh] if ys == slot else old[eh, ys, y_rows, :]
                        out[eh, table[SLOT_OFFSET + ys], y_rows, :] = value.astype(out.dtype)
        ready(x_held, i, 2)
        acts = x_held[i].reshape(4 * xn, 4 * SHARE)
        eh, el = halves[slot]
        for weight, out, old in zip(weights, outs, before):
            got = dot(acts, weight[pl.ds(el * 4 * SHARE, 4 * SHARE), :]).reshape(4, xn, COLS)
            if first:
                if slot == 0:
                    out[0, :, x_rows, :] = got
                    out[1, :, x_rows, :] = jnp.zeros_like(got)
                else:
                    out[eh, :, x_rows, :] += got
            else:
                for ys in range(4):
                    to = table[SLOT_OFFSET + ys]
                    out[0, to, x_rows, :] = old[0, ys, x_rows, :].astype(out.dtype)
                    out[1, to, x_rows, :] = (old[1, ys, x_rows, :] + got[ys]).astype(out.dtype)


def product(table, weights, blocks, slots, before, types):
    first = before is None
    vmem = pl.BlockSpec(memory_space=pltpu.VMEM)
    n, n_weights = len(slots), len(weights)
    zn, yn, xn = (PARTS[a][1] for a in "zyx")
    parts = [blocks[axis][s] for axis in "zyx" for s in slots]
    share = n * n_weights
    before = [] if first else before
    return pl.pallas_call(
        functools.partial(product_kernel, slots, n_weights, first),
        in_specs=[pl.BlockSpec(memory_space=pltpu.SMEM)]
        + [vmem] * n_weights
        + [pl.BlockSpec(memory_space=pl.ANY)] * (3 * n)
        + [vmem] * len(before),
        out_specs=[vmem] * n_weights,
        out_shape=[jax.ShapeDtypeStruct((2, 4, 256, COLS), t) for t in types],
        scratch_shapes=[
            pltpu.VMEM((n, 8, zn, 2 * SHARE), jnp.bfloat16),
            pltpu.VMEM((n, 2, yn, 8 * SHARE), jnp.bfloat16),
            pltpu.VMEM((n, 4, xn, 4 * SHARE), jnp.bfloat16),
            pltpu.SemaphoreType.DMA((n, 3)),
        ],
        compiler_params=pltpu.CompilerParams(vmem_limit_bytes=40 * MIB),
        cost_estimate=pl.CostEstimate(
            flops=share * 2 * 512 * 4096 * COLS, bytes_accessed=n * 4 * MIB + n_weights * 6 * MIB, transcendentals=0
        ),
    )(table, *weights, *parts, *before)


def spread_kernel(table, owner, parts, out):
    for k in range(8):
        section = owner[table[DEST + k]]
        half = jnp.where(section >= 4, 1, 0)
        far = jnp.where(half == table[XH], 0, 4)
        out[k] = parts[far + ((table[Y] + 8 - section) & 3)]


def arrange_kernel(table, parts, out):
    for k in range(8):
        out[:, k * COLS : (k + 1) * COLS] = parts[table[SOURCE + k]]


def small_call(kernel, scalars, parts, shape):
    smem, vmem = pl.BlockSpec(memory_space=pltpu.SMEM), pl.BlockSpec(memory_space=pltpu.VMEM)
    return pl.pallas_call(
        kernel,
        in_specs=[smem] * len(scalars) + [vmem],
        out_specs=vmem,
        out_shape=jax.ShapeDtypeStruct(shape, jnp.bfloat16),
        cost_estimate=pl.CostEstimate(flops=0, bytes_accessed=2 * MIB, transcendentals=0),
    )(*scalars, parts)


def shards(master, activations, owner):
    rows = jnp.asarray(np.array([device_row(i) for i in range(N_DEV)], np.int32))
    me = lax.axis_index("group") * 16 + lax.axis_index("tp")
    table = lax.dynamic_index_in_dim(rows, me, 0, keepdims=False)

    sent = refit(table, master, THEIRS)
    mine = refit(table, master, MINE)
    theirs = permute(sent, lambda x, y, z, c: linear(x, y, z, 1 - c))

    blocks = {}
    for axis in "zyx":
        at, count = PARTS[axis]
        blocks[axis] = gather(activations[None, at : at + count], ORDER[axis])

    f32, bf16 = jnp.float32, jnp.bfloat16
    kept, passed = product(table, [mine, theirs], blocks, (0, 1, 2), None, [f32, f32])
    (passed,) = product(table, [theirs], blocks, (3,), [passed], [bf16])
    passed = permute(passed, lambda x, y, z, c: linear(x, y, z, 1 - c))
    (kept,) = product(table, [mine], blocks, (3,), [kept], [f32])
    total = (kept + passed.astype(f32)).astype(bf16)

    parts = []
    for eh in range(2):
        for dy in range(4):
            part = total[eh, dy]
            if eh or dy:
                part = permute(part, lambda x, y, z, c: linear(x + 2 * eh, y + dy, z, c))
            parts.append(part)

    picked = small_call(spread_kernel, [table, owner], jnp.stack(parts), (8, 256, COLS))
    out = []
    for dz in range(4):
        for cross in range(2):
            move = lambda x, y, z, c: linear(x ^ (c ^ cross), y, z + dz, x % 2)
            out.append(permute(picked[dz * 2 + cross], move))
    return small_call(arrange_kernel, [table], jnp.stack(out), (256, 8 * COLS))


def solution(mesh):
    in_specs = (P(None, ("group", "tp")), P("group", "tp"), P())
    out_specs = P("group", "tp")
    return jax.shard_map(shards, mesh=mesh, in_specs=in_specs, out_specs=out_specs, check_vma=False)
```

time: 1070 us -> 193 us (0.18)
  the two profiles are of different devices: /device:TPU:3 before, /device:TPU:4 now
where the time goes in v2:
time: 193 us; the launch traced here: 192 us
  starting transfers between devices  69.4 us (36%)
  waiting for transfers between devices  62.3 us (32%)
  Pallas kernels  40 us (21%)
  local copies, waits for them, and re-layouts  19.3 us (10%)
    ppermute x38, starting transfers between devices, permute(): lax.ppermute(value, AXES, [(i, move(*coords(i))) for i in range(N_DEV)])  69.4 us
    ppermute x38, waiting for transfers between devices, permute(): lax.ppermute(value, AXES, [(i, move(*coords(i))) for i in range(N_DEV)])  62.3 us
    pallas_call x3, Pallas kernels, product(): pl.pallas_call(functools.partial(product_kernel, slots, n_weights, first)...  20.4 us
    pallas_call x2, Pallas kernels, refit(): pl.pallas_call(refit_kernel, grid_spec=pltpu.PrefetchScalarGridSpec(num_s...  15 us
    unnamed x51, local copies, waits for them, and re-layouts  13 us
    pallas_call x2, Pallas kernels, small_call(): pl.pallas_call(kernel, in_specs=[smem] * len(scalars) + [vmem], out_specs...  4.65 us
  transfers between devices with their start and end apart: 38, of which 14 were waited for; matrix products, arithmetic and copies ran while one was open for 5% of the time, Pallas kernels for 17%

profile of v2, /device:TPU:4, one launch (start us, length us, event | category | flops | bytes accessed | tf_op | source)
XLA Modules:
  0.0 192.0 jit_solution(6009816696590560190)
XLA Ops:
  0.0 0.9 slice_bitcast_fusion.17
  0.9 2.0 %collective-permute-start.6 = (bf16[1,80,512]{2,1,0:T(8,128)(2,1)S(1)}, bf16[1,80,512]{2,1,0:T(8,128)(2,1)S(1)}, u32[]{:S(2)}, u32[]{:S(2)}) collective-permute-start(bf16[1,80,512]{2,1,0:T(8,128)(2,1)S(1)} %get-tuple-element.25), channel_id=1, source_target_pairs={{0,2},{1,7},{2,0},{3,5},{4,6},{5,3},{6,4},{7,1},{8,10},{9,15},{10,... | collective-permute-start | bytes 245768 | tf_op jit(solution)/shard_map/ppermute | solution.py:31
  2.9 1.6 collective-permute-start.12
  4.5 0.9 slice_bitcast_fusion.16
  5.4 1.2 collective-permute-start
  6.6 1.2 dynamic-slice_bitcast_fusion.table
  7.8 7.6 %shard_map.47 = bf16[4096,256]{1,0:T(8,128)(2,1)} custom-call(s32[39]{0:T(128)} %dynamic-slice_bitcast_fusion.table, f32[8192,256]{1,0:T(8,128)} %master.3), custom_call_target="tpu_custom_call" | custom-call | flops 6291456 | bytes 6291456 | tf_op jit(solution)/shard_map/pallas_call | solution.py:94
  15.4 1.9 collective-permute-start.18
  17.3 0.6 constant_dynamic-update-slice_fusion.14
  17.9 0.7 collective-permute-start.7
  18.7 1.3 collective-permute-start.1
  20.0 1.1 collective-permute-start.13
  21.1 3.5 %collective-permute-done.7 = bf16[2,80,512]{2,1,0:T(8,128)(2,1)S(1)} collective-permute-done((bf16[2,80,512]{2,1,0:T(8,128)(2,1)S(1)}, bf16[2,80,512]{2,1,0:T(8,128)(2,1)S(1)}, u32[]{:S(2)}, u32[]{:S(2)}) %collective-permute-start.7) | collective-permute-done | bytes 163872 | tf_op jit(solution)/shard_map/ppermute | solution.py:31
  24.6 1.2 collective-permute-start.8
  26.1 0.7 constant_dynamic-update-slice_fusion.4
  26.9 4.9 %collective-permute-done.8 = bf16[4,80,512]{2,1,0:T(8,128)(2,1)S(1)} collective-permute-done((bf16[4,80,512]{2,1,0:T(8,128)(2,1)S(1)}, bf16[4,80,512]{2,1,0:T(8,128)(2,1)S(1)}, u32[]{:S(2)}, u32[]{:S(2)}) %collective-permute-start.8) | collective-permute-done | bytes 327712 | tf_op jit(solution)/shard_map/ppermute | solution.py:31
  31.9 1.5 collective-permute-start.9
  33.8 1.6 collective-permute-start.3
  36.1 0.7 constant_dynamic-update-slice_fusion.2
  36.8 1.5 collective-permute-start.15
  38.3 0.8 constant_dynamic-update-slice_fusion.1
  39.1 3.4 %collective-permute-done.9 = bf16[8,80,512]{2,1,0:T(8,128)(2,1)S(1)} collective-permute-done((bf16[8,80,512]{2,1,0:T(8,128)(2,1)S(1)}, bf16[8,80,512]{2,1,0:T(8,128)(2,1)S(1)}, u32[]{:S(2)}, u32[]{:S(2)}) %collective-permute-start.9) | collective-permute-done | bytes 655392 | tf_op jit(solution)/shard_map/ppermute | solution.py:31
  42.8 8.4 %collective-permute-done.3 = bf16[8,96,512]{2,1,0:T(8,128)(2,1)S(1)} collective-permute-done((bf16[8,96,512]{2,1,0:T(8,128)(2,1)S(1)}, bf16[8,96,512]{2,1,0:T(8,128)(2,1)S(1)}, u32[]{:S(2)}, u32[]{:S(2)}) %collective-permute-start.3) | collective-permute-done | bytes 786464 | tf_op jit(solution)/shard_map/ppermute | solution.py:31
  51.3 1.0 constant_dynamic-update-slice_fusion
  52.3 2.2 %collective-permute-start.4 = (bf16[16,96,512]{2,1,0:T(8,128)(2,1)}, bf16[16,96,512]{2,1,0:T(8,128)(2,1)}, u32[]{:S(2)}, u32[]{:S(2)}) collective-permute-start(bf16[16,96,512]{2,1,0:T(8,128)(2,1)} %constant_dynamic-update-slice_fusion), channel_id=1, source_target_pairs={{0,2},{1,7},{2,0},{3,5},{4,6},{5,3},{6,4},{7,1},{8,10},{9,15},{10,... | collective-permute-start | bytes 4718600 | tf_op jit(solution)/shard_map/ppermute | solution.py:31
  55.1 0.7 constant_dynamic-update-slice_fusion.12
  55.8 0.8 constant_dynamic-update-slice_fusion.11
  56.5 0.9 constant_dynamic-update-slice_fusion.10
  57.4 3.4 %collective-permute-start.16 = (bf16[16,80,512]{2,1,0:T(8,128)(2,1)}, bf16[16,80,512]{2,1,0:T(8,128)(2,1)}, u32[]{:S(2)}, u32[]{:S(2)}) collective-permute-start(bf16[16,80,512]{2,1,0:T(8,128)(2,1)} %constant_dynamic-update-slice_fusion.10), channel_id=1, source_target_pairs={{0,8},{1,73},{2,10},{3,75},{4,12},{5,77},{6,14},{7,79},{8,0},{9,65... | collective-permute-start | bytes 3932168 | tf_op jit(solution)/shard_map/ppermute | solution.py:31
  60.8 3.7 %collective-permute-start.20 = (bf16[16,80,512]{2,1,0:T(8,128)(2,1)S(1)}, bf16[16,80,512]{2,1,0:T(8,128)(2,1)S(1)}, u32[]{:S(2)}, u32[]{:S(2)}) collective-permute-start(bf16[16,80,512]{2,1,0:T(8,128)(2,1)S(1)} %constant_dynamic-update-slice_fusion.5), channel_id=1, source_target_pairs={{0,48},{1,17},{2,50},{3,19},{4,52},{5,21},{6,54},{7,23},{8,56},{9,... | collective-permute-start | bytes 3932168 | tf_op jit(solution)/shard_map/ppermute | solution.py:31
  64.5 3.4 %collective-permute-done.10 = bf16[16,80,512]{2,1,0:T(8,128)(2,1)} collective-permute-done((bf16[16,80,512]{2,1,0:T(8,128)(2,1)S(1)}, bf16[16,80,512]{2,1,0:T(8,128)(2,1)}, u32[]{:S(2)}, u32[]{:S(2)}) %collective-permute-start.10) | collective-permute-done | bytes 1310752 | tf_op jit(solution)/shard_map/ppermute | solution.py:31
  67.9 2.5 %collective-permute-start.21 = (bf16[16,80,512]{2,1,0:T(8,128)(2,1)}, bf16[16,80,512]{2,1,0:T(8,128)(2,1)}, u32[]{:S(2)}, u32[]{:S(2)}) collective-permute-start(bf16[16,80,512]{2,1,0:T(8,128)(2,1)} %constant_dynamic-update-slice_fusion.10), channel_id=1, source_target_pairs={{0,72},{1,9},{2,74},{3,11},{4,76},{5,13},{6,78},{7,15},{8,64},{9,1... | collective-permute-start | bytes 3932168 | tf_op jit(solution)/shard_map/ppermute | solution.py:31
  70.3 19.8 %collective-permute-done.4 = bf16[16,96,512]{2,1,0:T(8,128)(2,1)} collective-permute-done((bf16[16,96,512]{2,1,0:T(8,128)(2,1)}, bf16[16,96,512]{2,1,0:T(8,128)(2,1)}, u32[]{:S(2)}, u32[]{:S(2)}) %collective-permute-start.4) | collective-permute-done | bytes 1572896 | tf_op jit(solution)/shard_map/ppermute | solution.py:31
  90.1 1.7 collective-permute-start.5
  91.8 2.5 %collective-permute-start.11 = (bf16[16,80,512]{2,1,0:T(8,128)(2,1)}, bf16[16,80,512]{2,1,0:T(8,128)(2,1)S(1)}, u32[]{:S(2)}, u32[]{:S(2)}) collective-permute-start(bf16[16,80,512]{2,1,0:T(8,128)(2,1)} %collective-permute-done.10), channel_id=1, source_target_pairs={{0,48},{1,17},{2,50},{3,19},{4,52},{5,21},{6,54},{7,23},{8,56},{9,... | collective-permute-start | bytes 3932168 | tf_op jit(solution)/shard_map/ppermute | solution.py:31
  94.3 1.1 copy-done.8
  95.4 2.0 %collective-permute-start.17 = (bf16[16,80,512]{2,1,0:T(8,128)(2,1)}, bf16[16,80,512]{2,1,0:T(8,128)(2,1)}, u32[]{:S(2)}, u32[]{:S(2)}) collective-permute-start(bf16[16,80,512]{2,1,0:T(8,128)(2,1)} %collective-permute-done.16), channel_id=1, source_target_pairs={{0,72},{1,9},{2,74},{3,11},{4,76},{5,13},{6,78},{7,15},{8,64},{9,1... | collective-permute-start | bytes 3932168 | tf_op jit(solution)/shard_map/ppermute | solution.py:31
  97.4 7.4 %shard_map.46.refs_0_ = bf16[4096,256]{1,0:T(8,128)(2,1)} custom-call(s32[39]{0:T(128)} %dynamic-slice_bitcast_fusion.table, f32[8192,256]{1,0:T(8,128)} %master.3), custom_call_target="tpu_custom_call" | custom-call | flops 6291456 | bytes 6291456 | tf_op jit(solution)/shard_map/pallas_call | solution.py:94
  104.9 1.3 copy-done.7
  106.2 1.3 copy-done.9
  107.5 13.9 %shard_map.48 = (f32[2,4,256,256]{3,2,1,0:T(8,128)}, f32[2,4,256,256]{3,2,1,0:T(8,128)}) custom-call(s32[39]{0:T(128)S(1)} %copy-done.5, bf16[4096,256]{1,0:T(8,128)(2,1)} %shard_map.46.refs_0_, bf16[4096,256]{1,0:T(8,128)(2,1)} %copy-done.1, bf16[4,4,96,512]{3,2,1,0:T(8,128)(2,1)} %bitcast.7.refs_2_, bf16[4,4,96,512]{3,2,1,0:T(8,128)(2,1)} %bitcast.8.refs_3_, ...), custom_call_target="tpu_custom_call" | custom-call | flops 6442450944 | bytes 25165824 | tf_op jit(solution)/shard_map/pallas_call | solution.py:205
  121.4 1.6 copy-done.3
  123.0 3.3 %shard_map.50 = bf16[2,4,256,256]{3,2,1,0:T(8,128)(2,1)S(1)} custom-call(s32[39]{0:T(128)S(1)} %copy-done.5, bf16[4096,256]{1,0:T(8,128)(2,1)S(1)} %copy-done.2, bf16[4,4,96,512]{3,2,1,0:T(8,128)(2,1)S(1)} %bitcast.90, bf16[4,4,80,512]{3,2,1,0:T(8,128)(2,1)S(1)} %bitcast.92, bf16[4,4,80,512]{3,2,1,0:T(8,128)(2,1)} %bitcast.6.refs_3_, ...), custom_call_target="tpu_custom_call" | custom-call | flops 1073741824 | bytes 10485760 | tf_op jit(solution)/shard_map/pallas_call | solution.py:205
  126.5 3.1 %shard_map.49 = f32[2,4,256,256]{3,2,1,0:T(8,128)S(1)} custom-call(s32[39]{0:T(128)S(1)} %copy-done.5, bf16[4096,256]{1,0:T(8,128)(2,1)S(1)} %copy-done, bf16[4,4,96,512]{3,2,1,0:T(8,128)(2,1)S(1)} %bitcast.91, bf16[4,4,80,512]{3,2,1,0:T(8,128)(2,1)S(1)} %bitcast.93, bf16[4,4,80,512]{3,2,1,0:T(8,128)(2,1)} %bitcast.6.refs_3_, f32[2,4,256,256]{3,2,1,0:T(8,128)S(1)} %copy-done.4), custom_call_target="tpu_custom_call" | custom-call | flops 1073741824 | bytes 10485760 | tf_op jit(solution)/shard_map/pallas_call | solution.py:205
  130.0 4.7 %collective-permute-start.24 = (bf16[256,256]{1,0:T(8,128)(2,1)S(1)}, bf16[256,256]{1,0:T(8,128)(2,1)S(1)}, u32[]{:S(2)}, u32[]{:S(2)}) collective-permute-start(bf16[256,256]{1,0:T(8,128)(2,1)S(1)} %get-tuple-element.22), channel_id=1, source_target_pairs={{0,32},{1,33},{2,34},{3,35},{4,36},{5,37},{6,38},{7,39},{8,40},{9,... | collective-permute-start | bytes 393224 | tf_op jit(solution)/shard_map/ppermute | solution.py:31
  134.7 7.5 %collective-permute-start.26 = (bf16[256,256]{1,0:T(8,128)(2,1)S(1)}, bf16[256,256]{1,0:T(8,128)(2,1)S(1)}, u32[]{:S(2)}, u32[]{:S(2)}) collective-permute-start(bf16[256,256]{1,0:T(8,128)(2,1)S(1)} %get-tuple-element.20), channel_id=1, source_target_pairs={{0,64},{1,65},{2,66},{3,67},{4,68},{5,69},{6,70},{7,71},{8,72},{9,... | collective-permute-start | bytes 393224 | tf_op jit(solution)/shard_map/ppermute | solution.py:31
  142.2 1.5 collective-permute-start.27
  143.7 3.0 %collective-permute-start.28 = (bf16[256,256]{1,0:T(8,128)(2,1)S(1)}, bf16[256,256]{1,0:T(8,128)(2,1)S(1)}, u32[]{:S(2)}, u32[]{:S(2)}) collective-permute-start(bf16[256,256]{1,0:T(8,128)(2,1)S(1)} %get-tuple-element.18), channel_id=1, source_target_pairs={{0,96},{1,97},{2,98},{3,99},{4,100},{5,101},{6,102},{7,103},{8,104... | collective-permute-start | bytes 393224 | tf_op jit(solution)/shard_map/ppermute | solution.py:31
  146.8 3.0 %collective-permute-start.29 = (bf16[256,256]{1,0:T(8,128)(2,1)S(1)}, bf16[256,256]{1,0:T(8,128)(2,1)S(1)}, u32[]{:S(2)}, u32[]{:S(2)}) collective-permute-start(bf16[256,256]{1,0:T(8,128)(2,1)S(1)} %get-tuple-element.17), channel_id=1, source_target_pairs={{0,112},{1,113},{2,114},{3,115},{4,116},{5,117},{6,118},{7,119},{8... | collective-permute-start | bytes 393224 | tf_op jit(solution)/shard_map/ppermute | solution.py:31
  149.8 3.3 %collective-permute-done.27 = bf16[256,256]{1,0:T(8,128)(2,1)S(1)} collective-permute-done((bf16[256,256]{1,0:T(8,128)(2,1)S(1)}, bf16[256,256]{1,0:T(8,128)(2,1)S(1)}, u32[]{:S(2)}, u32[]{:S(2)}) %collective-permute-start.27) | collective-permute-done | bytes 131104 | tf_op jit(solution)/shard_map/ppermute | solution.py:31
  153.8 1.6 collective-permute-done.29
  155.4 1.0 copy-done.11
  156.4 2.3 %shard_map.51 = bf16[8,256,256]{2,1,0:T(8,128)(2,1)} custom-call(s32[39]{0:T(128)} %dynamic-slice_bitcast_fusion.table, s32[8]{0:T(128)} %owner.1, bf16[8,256,256]{2,1,0:T(8,128)(2,1)} %copy-done.11), custom_call_target="tpu_custom_call" | custom-call | bytes 2097152 | tf_op jit(solution)/shard_map/pallas_call | solution.py:241
  158.7 1.4 slice_bitcast_fusion
  160.1 0.7 collective-permute-start.30
  160.7 7.6 %collective-permute-start.31 = (bf16[256,256]{1,0:T(8,128)(2,1)S(1)}, bf16[256,256]{1,0:T(8,128)(2,1)S(1)}, u32[]{:S(2)}, u32[]{:S(2)}) collective-permute-start(bf16[256,256]{1,0:T(8,128)(2,1)S(1)} %get-tuple-element.15), channel_id=1, source_target_pairs={{0,8},{1,0},{2,10},{3,2},{4,12},{5,4},{6,14},{7,6},{8,1},{9,9},{10... | collective-permute-start | bytes 393224 | tf_op jit(solution)/shard_map/ppermute | solution.py:31
  168.4 0.6 collective-permute-start.33
  169.1 2.1 %collective-permute-start.34 = (bf16[256,256]{1,0:T(8,128)(2,1)S(1)}, bf16[256,256]{1,0:T(8,128)(2,1)S(1)}, u32[]{:S(2)}, u32[]{:S(2)}) collective-permute-start(bf16[256,256]{1,0:T(8,128)(2,1)S(1)} %get-tuple-element.12), channel_id=1, source_target_pairs={{0,4},{1,12},{2,6},{3,14},{4,0},{5,8},{6,2},{7,10},{8,13},{9,5},{1... | collective-permute-start | bytes 393224 | tf_op jit(solution)/shard_map/ppermute | solution.py:31
  171.2 3.7 %collective-permute-start.35 = (bf16[256,256]{1,0:T(8,128)(2,1)S(1)}, bf16[256,256]{1,0:T(8,128)(2,1)S(1)}, u32[]{:S(2)}, u32[]{:S(2)}) collective-permute-start(bf16[256,256]{1,0:T(8,128)(2,1)S(1)} %get-tuple-element.11), channel_id=1, source_target_pairs={{0,12},{1,4},{2,14},{3,6},{4,8},{5,0},{6,10},{7,2},{8,5},{9,13},{1... | collective-permute-start | bytes 393224 | tf_op jit(solution)/shard_map/ppermute | solution.py:31
  175.0 0.7 collective-permute-start.36
  175.6 8.6 %collective-permute-done.32 = bf16[256,256]{1,0:T(8,128)(2,1)S(1)} collective-permute-done((bf16[256,256]{1,0:T(8,128)(2,1)S(1)}, bf16[256,256]{1,0:T(8,128)(2,1)S(1)}, u32[]{:S(2)}, u32[]{:S(2)}) %collective-permute-start.32) | collective-permute-done | bytes 131104 | tf_op jit(solution)/shard_map/ppermute | solution.py:31
  184.6 4.0 %collective-permute-done.37 = bf16[256,256]{1,0:T(8,128)(2,1)S(1)} collective-permute-done((bf16[256,256]{1,0:T(8,128)(2,1)S(1)}, bf16[256,256]{1,0:T(8,128)(2,1)S(1)}, u32[]{:S(2)}, u32[]{:S(2)}) %collective-permute-start.37) | collective-permute-done | bytes 131104 | tf_op jit(solution)/shard_map/ppermute | solution.py:31
  188.7 1.0 copy-done.10
  189.7 2.3 %shard_map.52 = bf16[256,2048]{1,0:T(8,128)(2,1)} custom-call(s32[39]{0:T(128)} %dynamic-slice_bitcast_fusion.table, bf16[8,256,256]{2,1,0:T(8,128)(2,1)} %copy-done.10), custom_call_target="tpu_custom_call" | custom-call | bytes 2097152 | tf_op jit(solution)/shard_map/pallas_call | solution.py:241
  (90 shorter events, 4.3 us)
Async XLA Ops:
  0.9 17.0 %collective-permute-start.6 = (bf16[1,80,512]{2,1,0:T(8,128)(2,1)S(1)}, bf16[1,80,512]{2,1,0:T(8,128)(2,1)S(1)}, u32[]{:S(2)}, u32[]{:S(2)}) collective-permute-start(bf16[1,80,512]{2,1,0:T(8,128)(2,1)S(1)} %get-tuple-element.25), channel_id=1, source_target_pairs={{0,2},{1,7},{2,0},{3,5},{4,6},{5,3},{6,4},{7,1},{8,10},{9,15},{10,... | collective-permute-start | bytes 245768 | tf_op jit(solution)/shard_map/ppermute | solution.py:31
  2.9 17.1 %collective-permute-start.12 = (bf16[1,80,512]{2,1,0:T(8,128)(2,1)S(1)}, bf16[1,80,512]{2,1,0:T(8,128)(2,1)S(1)}, u32[]{:S(2)}, u32[]{:S(2)}) collective-permute-start(bf16[1,80,512]{2,1,0:T(8,128)(2,1)S(1)} %get-tuple-element.24), channel_id=1, source_target_pairs={{0,16},{1,49},{2,18},{3,51},{4,20},{5,53},{6,22},{7,55},{8,24},{9,... | collective-permute-start | bytes 245768 | tf_op jit(solution)/shard_map/ppermute | solution.py:31
  5.4 13.3 %collective-permute-start = (bf16[1,96,512]{2,1,0:T(8,128)(2,1)S(1)}, bf16[1,96,512]{2,1,0:T(8,128)(2,1)S(1)}, u32[]{:S(2)}, u32[]{:S(2)}) collective-permute-start(bf16[1,96,512]{2,1,0:T(8,128)(2,1)S(1)} %slice_bitcast_fusion.16), channel_id=1, source_target_pairs={{0,8},{1,73},{2,10},{3,75},{4,12},{5,77},{6,14},{7,79},{8,0},{9,65... | collective-permute-start | bytes 294920 | tf_op jit(solution)/shard_map/ppermute | solution.py:31
  7.8 9.5 %copy-start.12 = (bf16[256,512]{1,0:T(8,128)(2,1)S(1)}, bf16[256,512]{1,0:T(8,128)(2,1)}, u32[]{:S(2)}) copy-start(bf16[256,512]{1,0:T(8,128)(2,1)} %param.5) | copy-start | bytes 786436
  15.4 49.1 %collective-permute-start.18 = (bf16[4096,256]{1,0:T(8,128)(2,1)}, bf16[4096,256]{1,0:T(8,128)(2,1)S(1)}, u32[]{:S(2)}, u32[]{:S(2)}) collective-permute-start(bf16[4096,256]{1,0:T(8,128)(2,1)} %shard_map.47), channel_id=1, source_target_pairs={{0,1},{1,0},{2,3},{3,2},{4,5},{5,4},{6,7},{7,6},{8,9},{9,8},{10,11... | collective-permute-start | bytes 6291464 | tf_op jit(solution)/shard_map/ppermute | solution.py:31
  17.9 6.6 %collective-permute-start.7 = (bf16[2,80,512]{2,1,0:T(8,128)(2,1)S(1)}, bf16[2,80,512]{2,1,0:T(8,128)(2,1)S(1)}, u32[]{:S(2)}, u32[]{:S(2)}) collective-permute-start(bf16[2,80,512]{2,1,0:T(8,128)(2,1)S(1)} %pad_maximum_fusion.7), channel_id=1, source_target_pairs={{0,6},{1,3},{2,4},{3,1},{4,2},{5,7},{6,0},{7,5},{8,14},{9,11},{10,... | collective-permute-start | bytes 491528 | tf_op jit(solution)/shard_map/ppermute | solution.py:31
  18.7 7.1 %collective-permute-start.1 = (bf16[2,96,512]{2,1,0:T(8,128)(2,1)S(1)}, bf16[2,96,512]{2,1,0:T(8,128)(2,1)S(1)}, u32[]{:S(2)}, u32[]{:S(2)}) collective-permute-start(bf16[2,96,512]{2,1,0:T(8,128)(2,1)S(1)} %pad_maximum_fusion.6), channel_id=1, source_target_pairs={{0,72},{1,9},{2,74},{3,11},{4,76},{5,13},{6,78},{7,15},{8,64},{9,1... | collective-permute-start | bytes 589832 | tf_op jit(solution)/shard_map/ppermute | solution.py:31
  20.0 6.7 %collective-permute-start.13 = (bf16[2,80,512]{2,1,0:T(8,128)(2,1)S(1)}, bf16[2,80,512]{2,1,0:T(8,128)(2,1)S(1)}, u32[]{:S(2)}, u32[]{:S(2)}) collective-permute-start(bf16[2,80,512]{2,1,0:T(8,128)(2,1)S(1)} %pad_maximum_fusion.8), channel_id=1, source_target_pairs={{0,48},{1,17},{2,50},{3,19},{4,52},{5,21},{6,54},{7,23},{8,56},{9,... | collective-permute-start | bytes 491528 | tf_op jit(solution)/shard_map/ppermute | solution.py:31
  24.6 7.2 %collective-permute-start.8 = (bf16[4,80,512]{2,1,0:T(8,128)(2,1)S(1)}, bf16[4,80,512]{2,1,0:T(8,128)(2,1)S(1)}, u32[]{:S(2)}, u32[]{:S(2)}) collective-permute-start(bf16[4,80,512]{2,1,0:T(8,128)(2,1)S(1)} %pad_maximum_fusion.4), channel_id=1, source_target_pairs={{0,8},{1,73},{2,10},{3,75},{4,12},{5,77},{6,14},{7,79},{8,0},{9,65... | collective-permute-start | bytes 983048 | tf_op jit(solution)/shard_map/ppermute | solution.py:31
  25.9 7.9 %collective-permute-start.2 = (bf16[4,96,512]{2,1,0:T(8,128)(2,1)S(1)}, bf16[4,96,512]{2,1,0:T(8,128)(2,1)S(1)}, u32[]{:S(2)}, u32[]{:S(2)}) collective-permute-start(bf16[4,96,512]{2,1,0:T(8,128)(2,1)S(1)} %pad_maximum_fusion.3), channel_id=1, source_target_pairs={{0,16},{1,49},{2,18},{3,51},{4,20},{5,53},{6,22},{7,55},{8,24},{9,... | collective-permute-start | bytes 1179656 | tf_op jit(solution)/shard_map/ppermute | solution.py:31
  26.8 9.9 %collective-permute-start.14 = (bf16[4,80,512]{2,1,0:T(8,128)(2,1)S(1)}, bf16[4,80,512]{2,1,0:T(8,128)(2,1)S(1)}, u32[]{:S(2)}, u32[]{:S(2)}) collective-permute-start(bf16[4,80,512]{2,1,0:T(8,128)(2,1)S(1)} %pad_maximum_fusion.5), channel_id=1, source_target_pairs={{0,2},{1,7},{2,0},{3,5},{4,6},{5,3},{6,4},{7,1},{8,10},{9,15},{10,... | collective-permute-start | bytes 983048 | tf_op jit(solution)/shard_map/ppermute | solution.py:31
  31.9 10.7 %collective-permute-start.9 = (bf16[8,80,512]{2,1,0:T(8,128)(2,1)S(1)}, bf16[8,80,512]{2,1,0:T(8,128)(2,1)S(1)}, u32[]{:S(2)}, u32[]{:S(2)}) collective-permute-start(bf16[8,80,512]{2,1,0:T(8,128)(2,1)S(1)} %pad_maximum_fusion.1), channel_id=1, source_target_pairs={{0,72},{1,9},{2,74},{3,11},{4,76},{5,13},{6,78},{7,15},{8,64},{9,1... | collective-permute-start | bytes 1966088 | tf_op jit(solution)/shard_map/ppermute | solution.py:31
  33.8 17.5 %collective-permute-start.3 = (bf16[8,96,512]{2,1,0:T(8,128)(2,1)S(1)}, bf16[8,96,512]{2,1,0:T(8,128)(2,1)S(1)}, u32[]{:S(2)}, u32[]{:S(2)}) collective-permute-start(bf16[8,96,512]{2,1,0:T(8,128)(2,1)S(1)} %pad_maximum_fusion), channel_id=1, source_target_pairs={{0,48},{1,17},{2,50},{3,19},{4,52},{5,21},{6,54},{7,23},{8,56},{9,... | collective-permute-start | bytes 2359304 | tf_op jit(solution)/shard_map/ppermute | solution.py:31
  36.8 19.7 %collective-permute-start.15 = (bf16[8,80,512]{2,1,0:T(8,128)(2,1)S(1)}, bf16[8,80,512]{2,1,0:T(8,128)(2,1)S(1)}, u32[]{:S(2)}, u32[]{:S(2)}) collective-permute-start(bf16[8,80,512]{2,1,0:T(8,128)(2,1)S(1)} %pad_maximum_fusion.2), channel_id=1, source_target_pairs={{0,6},{1,3},{2,4},{3,1},{4,2},{5,7},{6,0},{7,5},{8,14},{9,11},{10,... | collective-permute-start | bytes 1966088 | tf_op jit(solution)/shard_map/ppermute | solution.py:31
  42.6 18.1 %copy-start.6 = (bf16[16,80,512]{2,1,0:T(8,128)(2,1)}, bf16[16,80,512]{2,1,0:T(8,128)(2,1)S(1)}, u32[]{:S(2)}) copy-start(bf16[16,80,512]{2,1,0:T(8,128)(2,1)S(1)} %constant_dynamic-update-slice_fusion.5) | copy-start | bytes 3932164
  42.6 25.2 %collective-permute-start.10 = (bf16[16,80,512]{2,1,0:T(8,128)(2,1)S(1)}, bf16[16,80,512]{2,1,0:T(8,128)(2,1)}, u32[]{:S(2)}, u32[]{:S(2)}) collective-permute-start(bf16[16,80,512]{2,1,0:T(8,128)(2,1)S(1)} %constant_dynamic-update-slice_fusion.5), channel_id=1, source_target_pairs={{0,16},{1,49},{2,18},{3,51},{4,20},{5,53},{6,22},{7,55},{8,24},{9,... | collective-permute-start | bytes 3932168 | tf_op jit(solution)/shard_map/ppermute | solution.py:31
  52.3 37.8 %collective-permute-start.4 = (bf16[16,96,512]{2,1,0:T(8,128)(2,1)}, bf16[16,96,512]{2,1,0:T(8,128)(2,1)}, u32[]{:S(2)}, u32[]{:S(2)}) collective-permute-start(bf16[16,96,512]{2,1,0:T(8,128)(2,1)} %constant_dynamic-update-slice_fusion), channel_id=1, source_target_pairs={{0,2},{1,7},{2,0},{3,5},{4,6},{5,3},{6,4},{7,1},{8,10},{9,15},{10,... | collective-permute-start | bytes 4718600 | tf_op jit(solution)/shard_map/ppermute | solution.py:31
  57.4 47.4 %copy-start.5 = (s32[39]{0:T(128)S(1)}, s32[39]{0:T(128)}, u32[]{:S(2)}) copy-start(s32[39]{0:T(128)} %dynamic-slice_bitcast_fusion.table) | copy-start | bytes 472
  57.4 34.4 %collective-permute-start.16 = (bf16[16,80,512]{2,1,0:T(8,128)(2,1)}, bf16[16,80,512]{2,1,0:T(8,128)(2,1)}, u32[]{:S(2)}, u32[]{:S(2)}) collective-permute-start(bf16[16,80,512]{2,1,0:T(8,128)(2,1)} %constant_dynamic-update-slice_fusion.10), channel_id=1, source_target_pairs={{0,8},{1,73},{2,10},{3,75},{4,12},{5,77},{6,14},{7,79},{8,0},{9,65... | collective-permute-start | bytes 3932168 | tf_op jit(solution)/shard_map/ppermute | solution.py:31
  60.8 33.6 %collective-permute-start.20 = (bf16[16,80,512]{2,1,0:T(8,128)(2,1)S(1)}, bf16[16,80,512]{2,1,0:T(8,128)(2,1)S(1)}, u32[]{:S(2)}, u32[]{:S(2)}) collective-permute-start(bf16[16,80,512]{2,1,0:T(8,128)(2,1)S(1)} %constant_dynamic-update-slice_fusion.5), channel_id=1, source_target_pairs={{0,48},{1,17},{2,50},{3,19},{4,52},{5,21},{6,54},{7,23},{8,56},{9,... | collective-permute-start | bytes 3932168 | tf_op jit(solution)/shard_map/ppermute | solution.py:31
  64.5 27.3 %copy-start.1 = (bf16[4096,256]{1,0:T(8,128)(2,1)}, bf16[4096,256]{1,0:T(8,128)(2,1)S(1)}, u32[]{:S(2)}) copy-start(bf16[4096,256]{1,0:T(8,128)(2,1)S(1)} %collective-permute-done.18.refs_1_.refs_0_) | copy-start | bytes 6291460
  64.5 40.4 %collective-permute-start.19 = (bf16[16,96,512]{2,1,0:T(8,128)(2,1)}, bf16[16,96,512]{2,1,0:T(8,128)(2,1)}, u32[]{:S(2)}, u32[]{:S(2)}) collective-permute-start(bf16[16,96,512]{2,1,0:T(8,128)(2,1)} %constant_dynamic-update-slice_fusion), channel_id=1, source_target_pairs={{0,6},{1,3},{2,4},{3,1},{4,2},{5,7},{6,0},{7,5},{8,14},{9,11},{10,... | collective-permute-start | bytes 4718600 | tf_op jit(solution)/shard_map/ppermute | solution.py:31
  67.9 37.0 %collective-permute-start.21 = (bf16[16,80,512]{2,1,0:T(8,128)(2,1)}, bf16[16,80,512]{2,1,0:T(8,128)(2,1)}, u32[]{:S(2)}, u32[]{:S(2)}) collective-permute-start(bf16[16,80,512]{2,1,0:T(8,128)(2,1)} %constant_dynamic-update-slice_fusion.10), channel_id=1, source_target_pairs={{0,72},{1,9},{2,74},{3,11},{4,76},{5,13},{6,78},{7,15},{8,64},{9,1... | collective-permute-start | bytes 3932168 | tf_op jit(solution)/shard_map/ppermute | solution.py:31
  90.1 31.3 %collective-permute-start.5 = (bf16[16,96,512]{2,1,0:T(8,128)(2,1)}, bf16[16,96,512]{2,1,0:T(8,128)(2,1)S(1)}, u32[]{:S(2)}, u32[]{:S(2)}) collective-permute-start(bf16[16,96,512]{2,1,0:T(8,128)(2,1)} %collective-permute-done.4), channel_id=1, source_target_pairs={{0,6},{1,3},{2,4},{3,1},{4,2},{5,7},{6,0},{7,5},{8,14},{9,11},{10,... | collective-permute-start | bytes 4718600 | tf_op jit(solution)/shard_map/ppermute | solution.py:31
  91.8 29.6 %collective-permute-start.11 = (bf16[16,80,512]{2,1,0:T(8,128)(2,1)}, bf16[16,80,512]{2,1,0:T(8,128)(2,1)S(1)}, u32[]{:S(2)}, u32[]{:S(2)}) collective-permute-start(bf16[16,80,512]{2,1,0:T(8,128)(2,1)} %collective-permute-done.10), channel_id=1, source_target_pairs={{0,48},{1,17},{2,50},{3,19},{4,52},{5,21},{6,54},{7,23},{8,56},{9,... | collective-permute-start | bytes 3932168 | tf_op jit(solution)/shard_map/ppermute | solution.py:31
  94.3 1.1 copy-start.8
  95.4 26.0 %collective-permute-start.17 = (bf16[16,80,512]{2,1,0:T(8,128)(2,1)}, bf16[16,80,512]{2,1,0:T(8,128)(2,1)}, u32[]{:S(2)}, u32[]{:S(2)}) collective-permute-start(bf16[16,80,512]{2,1,0:T(8,128)(2,1)} %collective-permute-done.16), channel_id=1, source_target_pairs={{0,72},{1,9},{2,74},{3,11},{4,76},{5,13},{6,78},{7,15},{8,64},{9,1... | collective-permute-start | bytes 3932168 | tf_op jit(solution)/shard_map/ppermute | solution.py:31
  104.8 1.3 copy-start.7
  106.2 1.3 copy-start.9
  107.5 13.9 %copy-start.2 = (bf16[4096,256]{1,0:T(8,128)(2,1)S(1)}, bf16[4096,256]{1,0:T(8,128)(2,1)}, u32[]{:S(2)}) copy-start(bf16[4096,256]{1,0:T(8,128)(2,1)} %copy-done.1) | copy-start | bytes 6291460
  121.4 1.6 copy-start.3
  123.0 3.5 %copy-start = (bf16[4096,256]{1,0:T(8,128)(2,1)S(1)}, bf16[4096,256]{1,0:T(8,128)(2,1)}, u32[]{:S(2)}) copy-start(bf16[4096,256]{1,0:T(8,128)(2,1)} %shard_map.46.refs_0_) | copy-start | bytes 6291460
  123.0 3.5 %copy-start.4 = (f32[2,4,256,256]{3,2,1,0:T(8,128)S(1)}, f32[2,4,256,256]{3,2,1,0:T(8,128)}, u32[]{:S(2)}) copy-start(f32[2,4,256,256]{3,2,1,0:T(8,128)} %get-tuple-element.7.refs_4_) | copy-start | bytes 6291460
  126.4 3.3 %collective-permute-start.22 = (bf16[2,4,256,256]{3,2,1,0:T(8,128)(2,1)S(1)}, bf16[2,4,256,256]{3,2,1,0:T(8,128)(2,1)S(1)}, u32[]{:S(2)}, u32[]{:S(2)}) collective-permute-start(bf16[2,4,256,256]{3,2,1,0:T(8,128)(2,1)S(1)} %shard_map.50), channel_id=1, source_target_pairs={{0,1},{1,0},{2,3},{3,2},{4,5},{5,4},{6,7},{7,6},{8,9},{9,8},{10,11... | collective-permute-start | bytes 3145736 | tf_op jit(solution)/shard_map/ppermute | solution.py:31
  130.0 13.7 %collective-permute-start.23 = (bf16[256,256]{1,0:T(8,128)(2,1)S(1)}, bf16[256,256]{1,0:T(8,128)(2,1)S(1)}, u32[]{:S(2)}, u32[]{:S(2)}) collective-permute-start(bf16[256,256]{1,0:T(8,128)(2,1)S(1)} %get-tuple-element.23), channel_id=1, source_target_pairs={{0,16},{1,17},{2,18},{3,19},{4,20},{5,21},{6,22},{7,23},{8,24},{9,... | collective-permute-start | bytes 393224 | tf_op jit(solution)/shard_map/ppermute | solution.py:31
  130.0 16.7 %collective-permute-start.24 = (bf16[256,256]{1,0:T(8,128)(2,1)S(1)}, bf16[256,256]{1,0:T(8,128)(2,1)S(1)}, u32[]{:S(2)}, u32[]{:S(2)}) collective-permute-start(bf16[256,256]{1,0:T(8,128)(2,1)S(1)} %get-tuple-element.22), channel_id=1, source_target_pairs={{0,32},{1,33},{2,34},{3,35},{4,36},{5,37},{6,38},{7,39},{8,40},{9,... | collective-permute-start | bytes 393224 | tf_op jit(solution)/shard_map/ppermute | solution.py:31
  134.7 15.0 %collective-permute-start.25 = (bf16[256,256]{1,0:T(8,128)(2,1)S(1)}, bf16[256,256]{1,0:T(8,128)(2,1)S(1)}, u32[]{:S(2)}, u32[]{:S(2)}) collective-permute-start(bf16[256,256]{1,0:T(8,128)(2,1)S(1)} %get-tuple-element.21), channel_id=1, source_target_pairs={{0,48},{1,49},{2,50},{3,51},{4,52},{5,53},{6,54},{7,55},{8,56},{9,... | collective-permute-start | bytes 393224 | tf_op jit(solution)/shard_map/ppermute | solution.py:31
  134.7 15.1 %collective-permute-start.26 = (bf16[256,256]{1,0:T(8,128)(2,1)S(1)}, bf16[256,256]{1,0:T(8,128)(2,1)S(1)}, u32[]{:S(2)}, u32[]{:S(2)}) collective-permute-start(bf16[256,256]{1,0:T(8,128)(2,1)S(1)} %get-tuple-element.20), channel_id=1, source_target_pairs={{0,64},{1,65},{2,66},{3,67},{4,68},{5,69},{6,70},{7,71},{8,72},{9,... | collective-permute-start | bytes 393224 | tf_op jit(solution)/shard_map/ppermute | solution.py:31
  142.2 10.9 %collective-permute-start.27 = (bf16[256,256]{1,0:T(8,128)(2,1)S(1)}, bf16[256,256]{1,0:T(8,128)(2,1)S(1)}, u32[]{:S(2)}, u32[]{:S(2)}) collective-permute-start(bf16[256,256]{1,0:T(8,128)(2,1)S(1)} %get-tuple-element.19), channel_id=1, source_target_pairs={{0,80},{1,81},{2,82},{3,83},{4,84},{5,85},{6,86},{7,87},{8,88},{9,... | collective-permute-start | bytes 393224 | tf_op jit(solution)/shard_map/ppermute | solution.py:31
  143.7 10.1 %collective-permute-start.28 = (bf16[256,256]{1,0:T(8,128)(2,1)S(1)}, bf16[256,256]{1,0:T(8,128)(2,1)S(1)}, u32[]{:S(2)}, u32[]{:S(2)}) collective-permute-start(bf16[256,256]{1,0:T(8,128)(2,1)S(1)} %get-tuple-element.18), channel_id=1, source_target_pairs={{0,96},{1,97},{2,98},{3,99},{4,100},{5,101},{6,102},{7,103},{8,104... | collective-permute-start | bytes 393224 | tf_op jit(solution)/shard_map/ppermute | solution.py:31
  146.8 8.6 %collective-permute-start.29 = (bf16[256,256]{1,0:T(8,128)(2,1)S(1)}, bf16[256,256]{1,0:T(8,128)(2,1)S(1)}, u32[]{:S(2)}, u32[]{:S(2)}) collective-permute-start(bf16[256,256]{1,0:T(8,128)(2,1)S(1)} %get-tuple-element.17), channel_id=1, source_target_pairs={{0,112},{1,113},{2,114},{3,115},{4,116},{5,117},{6,118},{7,119},{8... | collective-permute-start | bytes 393224 | tf_op jit(solution)/shard_map/ppermute | solution.py:31
  155.4 1.0 copy-start.11
  160.1 11.1 %collective-permute-start.30 = (bf16[256,256]{1,0:T(8,128)(2,1)S(1)}, bf16[256,256]{1,0:T(8,128)(2,1)S(1)}, u32[]{:S(2)}, u32[]{:S(2)}) collective-permute-start(bf16[256,256]{1,0:T(8,128)(2,1)S(1)} %get-tuple-element.16), channel_id=1, source_target_pairs={{0,0},{1,8},{2,2},{3,10},{4,4},{5,12},{6,6},{7,14},{8,9},{9,1},{10... | collective-permute-start | bytes 393224 | tf_op jit(solution)/shard_map/ppermute | solution.py:31
  160.7 14.2 %collective-permute-start.31 = (bf16[256,256]{1,0:T(8,128)(2,1)S(1)}, bf16[256,256]{1,0:T(8,128)(2,1)S(1)}, u32[]{:S(2)}, u32[]{:S(2)}) collective-permute-start(bf16[256,256]{1,0:T(8,128)(2,1)S(1)} %get-tuple-element.15), channel_id=1, source_target_pairs={{0,8},{1,0},{2,10},{3,2},{4,12},{5,4},{6,14},{7,6},{8,1},{9,9},{10... | collective-permute-start | bytes 393224 | tf_op jit(solution)/shard_map/ppermute | solution.py:31
  168.3 15.9 %collective-permute-start.32 = (bf16[256,256]{1,0:T(8,128)(2,1)S(1)}, bf16[256,256]{1,0:T(8,128)(2,1)S(1)}, u32[]{:S(2)}, u32[]{:S(2)}) collective-permute-start(bf16[256,256]{1,0:T(8,128)(2,1)S(1)} %get-tuple-element.14), channel_id=1, source_target_pairs={{0,2},{1,10},{2,4},{3,12},{4,6},{5,14},{6,0},{7,8},{8,11},{9,3},{1... | collective-permute-start | bytes 393224 | tf_op jit(solution)/shard_map/ppermute | solution.py:31
  168.4 16.0 %collective-permute-start.33 = (bf16[256,256]{1,0:T(8,128)(2,1)S(1)}, bf16[256,256]{1,0:T(8,128)(2,1)S(1)}, u32[]{:S(2)}, u32[]{:S(2)}) collective-permute-start(bf16[256,256]{1,0:T(8,128)(2,1)S(1)} %get-tuple-element.13), channel_id=1, source_target_pairs={{0,10},{1,2},{2,12},{3,4},{4,14},{5,6},{6,8},{7,0},{8,3},{9,11},{1... | collective-permute-start | bytes 393224 | tf_op jit(solution)/shard_map/ppermute | solution.py:31
  169.1 15.4 %collective-permute-start.34 = (bf16[256,256]{1,0:T(8,128)(2,1)S(1)}, bf16[256,256]{1,0:T(8,128)(2,1)S(1)}, u32[]{:S(2)}, u32[]{:S(2)}) collective-permute-start(bf16[256,256]{1,0:T(8,128)(2,1)S(1)} %get-tuple-element.12), channel_id=1, source_target_pairs={{0,4},{1,12},{2,6},{3,14},{4,0},{5,8},{6,2},{7,10},{8,13},{9,5},{1... | collective-permute-start | bytes 393224 | tf_op jit(solution)/shard_map/ppermute | solution.py:31
  171.2 13.2 %collective-permute-start.35 = (bf16[256,256]{1,0:T(8,128)(2,1)S(1)}, bf16[256,256]{1,0:T(8,128)(2,1)S(1)}, u32[]{:S(2)}, u32[]{:S(2)}) collective-permute-start(bf16[256,256]{1,0:T(8,128)(2,1)S(1)} %get-tuple-element.11), channel_id=1, source_target_pairs={{0,12},{1,4},{2,14},{3,6},{4,8},{5,0},{6,10},{7,2},{8,5},{9,13},{1... | collective-permute-start | bytes 393224 | tf_op jit(solution)/shard_map/ppermute | solution.py:31
  175.0 9.7 %collective-permute-start.36 = (bf16[256,256]{1,0:T(8,128)(2,1)S(1)}, bf16[256,256]{1,0:T(8,128)(2,1)S(1)}, u32[]{:S(2)}, u32[]{:S(2)}) collective-permute-start(bf16[256,256]{1,0:T(8,128)(2,1)S(1)} %get-tuple-element.10), channel_id=1, source_target_pairs={{0,6},{1,14},{2,0},{3,8},{4,2},{5,10},{6,4},{7,12},{8,15},{9,7},{1... | collective-permute-start | bytes 393224 | tf_op jit(solution)/shard_map/ppermute | solution.py:31
  184.3 4.4 %collective-permute-start.37 = (bf16[256,256]{1,0:T(8,128)(2,1)S(1)}, bf16[256,256]{1,0:T(8,128)(2,1)S(1)}, u32[]{:S(2)}, u32[]{:S(2)}) collective-permute-start(bf16[256,256]{1,0:T(8,128)(2,1)S(1)} %get-tuple-element.9), channel_id=1, source_target_pairs={{0,14},{1,6},{2,8},{3,0},{4,10},{5,2},{6,12},{7,4},{8,7},{9,15},{1... | collective-permute-start | bytes 393224 | tf_op jit(solution)/shard_map/ppermute | solution.py:31
  188.7 1.0 copy-start.10

commit v3 on v0

v3 whole, which is shorter than its diff:
```python
import functools

import jax
import jax.numpy as jnp
import numpy as np
from jax import lax
from jax.experimental import pallas as pl
from jax.experimental.pallas import tpu as pltpu
from jax.sharding import PartitionSpec as P

BLOCK = 128
AXES = ("group", "tp")
N_DEV = 128
SHARE = 512
COLS = 256
PARTS = {"z": (0, 96), "y": (96, 80), "x": (176, 80)}
ORDER = {"z": "xyz", "y": "zxy", "x": "yzx"}
MIB = 1024 * 1024


def coords(i):
    return i // 64 * 2 + i // 8 % 2, i // 16 % 4, i // 2 % 4, i % 2


def linear(x, y, z, core):
    x, y, z = x % 4, y % 4, z % 4
    return x // 2 * 64 + y * 16 + x % 2 * 8 + z * 2 + core


def permute(value, move):
    return lax.ppermute(value, AXES, [(i, move(*coords(i))) for i in range(N_DEV)])


def offset(slot, at, core):
    step = -1 if (at + core) % 2 else 1
    return (0, step, -step, 2)[slot] % 4


def exchange(value, axis, which):
    def move(x, y, z, core):
        at = {"x": x, "y": y, "z": z}
        at[axis] += offset(which, at[axis], core)
        return linear(at["x"], at["y"], at["z"], core)

    return permute(value, move)


def gather_plane(block, order):
    for axis in order[:2]:
        for which in (1, 2):
            block = jnp.concatenate([block, exchange(block, axis, which)], axis=0)
    return block


def gather_last(block, axis):
    first = exchange(block, axis, 1)
    second = exchange(block, axis, 2)
    relayed = exchange(first, axis, 2)
    return [v.reshape(4, 4, *v.shape[1:]) for v in (block, first, second, relayed)]


MINE, THEIRS, CORE, SLOT_OFFSET, XH, Y, Z, DEST, WIDTH = 0, 8, 16, 17, 21, 22, 23, 24, 28


def device_row(i):
    x, y, z, core = coords(i)
    xh, xl = x // 2, x % 2

    def chunks(c):
        return [(xl ^ n // 4) * 8 + (z + offset(n % 4, z, c)) % 4 * 2 + c for n in range(8)]

    dest = [(xl ^ core) * 4 + (z + dz) % 4 for dz in range(4)]
    row = chunks(core) + chunks(1 - core) + [core] + [offset(s, y, core) for s in range(4)] + [xh, y, z] + dest
    assert len(row) == WIDTH
    return row


def refit_kernel(table, master, out):
    for r in range(master.shape[0] // BLOCK):
        for c in range(master.shape[1] // BLOCK):
            at = (pl.ds(r * BLOCK, BLOCK), pl.ds(c * BLOCK, BLOCK))
            tile = master[at]
            amax = jnp.max(jnp.max(jnp.abs(tile), axis=0, keepdims=True), axis=1, keepdims=True)
            scale = ((amax + 1e-6) / 448.0).astype(jnp.bfloat16).astype(jnp.float32)
            coded = (tile * (1.0 / scale)).astype(jnp.bfloat16)
            out[at] = (coded.astype(jnp.float32) * scale).astype(jnp.bfloat16)


def refit(table, master, first):
    size = 8 * SHARE * COLS
    return pl.pallas_call(
        refit_kernel,
        grid_spec=pltpu.PrefetchScalarGridSpec(
            num_scalar_prefetch=1,
            grid=(8,),
            in_specs=[pl.BlockSpec((SHARE, COLS), lambda i, t: (t[first + i], 0))],
            out_specs=pl.BlockSpec((SHARE, COLS), lambda i, t: (i, 0)),
        ),
        out_shape=jax.ShapeDtypeStruct((8 * SHARE, COLS), jnp.bfloat16),
        cost_estimate=pl.CostEstimate(flops=size * 6, bytes_accessed=size * 6, transcendentals=0),
    )(table, master)


def rows_of(axis):
    at, count = PARTS[axis]
    return pl.ds(at, count)


def dot(a, b):
    return jnp.dot(a, b, preferred_element_type=jnp.float32)


def halves(core):
    return ((0, 0), (core, 1), (1 - core, 1), (1, 0))


def column_slices(core):
    return [pl.ds(pl.multiple_of(c * COLS, COLS), COLS) for c in (core, 1 - core)]


def early_kernel(table, mine, theirs, z0, z1, y0, y1, x0, x1, out, z_held, y_held, x_held, sems):
    core = table[CORE]
    zn, yn, xn = (PARTS[a][1] for a in "zyx")
    for i, (z_part, y_part, x_part) in enumerate(((z0, y0, x0), (z1, y1, x1))):
        for sx, (eh, el) in enumerate(halves(core)):
            cols = pl.ds(el * SHARE, SHARE)
            pltpu.make_async_copy(z_part.at[:, sx], z_held.at[i, pl.ds(eh * 4, 4), :, cols], sems.at[i, 0]).start()
            for zs in range(4):
                cols = pl.ds((el * 4 + zs) * SHARE, SHARE)
                pltpu.make_async_copy(y_part.at[sx, zs], y_held.at[i, eh, :, cols], sems.at[i, 1]).start()
        for zs in range(4):
            cols = pl.ds(zs * SHARE, SHARE)
            pltpu.make_async_copy(x_part.at[zs], x_held.at[i, :, :, cols], sems.at[i, 2]).start()

    z_rows, y_rows, x_rows = rows_of("z"), rows_of("y"), rows_of("x")
    weights = list(zip((mine, theirs), column_slices(core)))
    for i in range(2):
        for which, held in enumerate((z_held, y_held, x_held)):
            pltpu.make_async_copy(held.at[i], held.at[i], sems.at[i, which]).wait()
        for weight, cols in weights:
            for eh in range(2):
                acts = z_held[i, pl.ds(eh * 4, 4)].reshape(4 * zn, 2 * SHARE)
                got = dot(acts[:, :SHARE], weight[pl.ds(i * SHARE, SHARE), :])
                got += dot(acts[:, SHARE:], weight[pl.ds((4 + i) * SHARE, SHARE), :])
                got = got.reshape(4, zn, COLS)
                if i == 0:
                    out[eh, :, z_rows, cols] = got
                else:
                    out[eh, :, z_rows, cols] += got
            acts = y_held[i].reshape(2 * yn, 8 * SHARE)
            out[:, i, y_rows, cols] = dot(acts, weight[...]).reshape(2, yn, COLS)
            eh, el = halves(core)[i]
            acts = x_held[i].reshape(4 * xn, 4 * SHARE)
            got = dot(acts, weight[pl.ds(el * 4 * SHARE, 4 * SHARE), :]).reshape(4, xn, COLS)
            if i == 0:
                out[0, :, x_rows, cols] = got
                out[1, :, x_rows, cols] = jnp.zeros_like(got)
            else:
                out[eh, :, x_rows, cols] += got


def late_kernel(keep, table, mine, theirs, z2, z3, y2, y3, x2, x3, early, out, z_held, y_held, x_held, total, sems):
    core = table[CORE]
    half = core if keep else 1 - core
    near = jnp.where(half == 0, 0, 3)
    sources = ((near, 0), (1 if keep else 2, 1))
    zn, yn, xn = (PARTS[a][1] for a in "zyx")
    pltpu.make_async_copy(early.at[half], total, sems.at[3]).start()
    for i, (z_part, y_part, x_part) in enumerate(((z2, y2, x2), (z3, y3, x3))):
        for sx, el in sources:
            cols = pl.ds(el * SHARE, SHARE)
            pltpu.make_async_copy(z_part.at[:, sx], z_held.at[i, :, :, cols], sems.at[0]).start()
            for zs in range(4):
                cols = pl.ds((el * 4 + zs) * SHARE, SHARE)
                pltpu.make_async_copy(y_part.at[sx, zs], y_held.at[i, :, cols], sems.at[1]).start()
        for zs in range(4):
            cols = pl.ds(zs * SHARE, SHARE)
            pltpu.make_async_copy(x_part.at[zs], x_held.at[i, :, :, cols], sems.at[2]).start()
    for which, held in enumerate((z_held, y_held, x_held, total)):
        pltpu.make_async_copy(held, held, sems.at[which]).wait()

    z_rows, y_rows, x_rows = rows_of("z"), rows_of("y"), rows_of("x")
    for weight, cols in zip((mine, theirs), column_slices(core)):
        got = None
        for i in range(2):
            acts = z_held[i].reshape(4 * zn, 2 * SHARE)
            term = dot(acts[:, :SHARE], weight[pl.ds((2 + i) * SHARE, SHARE), :])
            term += dot(acts[:, SHARE:], weight[pl.ds((6 + i) * SHARE, SHARE), :])
            got = term if got is None else got + term
        total[:, z_rows, cols] += got.reshape(4, zn, COLS)
        acts = y_held[...].reshape(2 * yn, 8 * SHARE)
        total[2:4, y_rows, cols] = dot(acts, weight[...]).reshape(2, yn, COLS)

        def add(i, el):
            acts = x_held[i].reshape(4 * xn, 4 * SHARE)
            total[:, x_rows, cols] += dot(acts, weight[pl.ds(el * 4 * SHARE, 4 * SHARE), :]).reshape(4, xn, COLS)

        if not keep:
            add(0, 1)

        @pl.when(half == 1)
        def _():
            add(1, 0)

    for ys in range(4):
        out[table[SLOT_OFFSET + ys]] = total[ys].astype(out.dtype)


def product(kernel, table, weights, blocks, slots, held, out, more=()):
    vmem, anywhere = pl.BlockSpec(memory_space=pltpu.VMEM), pl.BlockSpec(memory_space=pl.ANY)
    parts = [blocks[axis][s] for axis in "zyx" for s in slots] + list(more)
    work = 2 * out.shape[0] * (2 if out.ndim == 4 else 1)
    return pl.pallas_call(
        kernel,
        in_specs=[pl.BlockSpec(memory_space=pltpu.SMEM)] + [vmem] * 2 + [anywhere] * len(parts),
        out_specs=vmem,
        out_shape=out,
        scratch_shapes=held,
        compiler_params=pltpu.CompilerParams(vmem_limit_bytes=32 * MIB),
        cost_estimate=pl.CostEstimate(
            flops=work * 512 * 4096 * 256, bytes_accessed=(6 + work) * MIB, transcendentals=0
        ),
    )(table, *weights, *parts)


def spread_kernel(table, owner, own, other, out):
    for k in range(4):
        section = owner[table[DEST + k]]
        half = jnp.where(section >= 4, 1, 0)
        far = jnp.where(half == table[XH], 0, 1)
        at = (table[Y] + 8 - section) & 3

        @pl.when(far == table[CORE])
        def _():
            out[k] = own[at]

        @pl.when(far != table[CORE])
        def _():
            out[k] = other[at]


def arrange_kernel(table, parts, out):
    for k in range(4):
        out[:, k * 2 * COLS : (k + 1) * 2 * COLS] = parts[(table[Z] + 4 - k) & 3]


def small_call(kernel, scalars, parts, shape):
    smem, vmem = pl.BlockSpec(memory_space=pltpu.SMEM), pl.BlockSpec(memory_space=pltpu.VMEM)
    return pl.pallas_call(
        kernel,
        in_specs=[smem] * len(scalars) + [vmem] * len(parts),
        out_specs=vmem,
        out_shape=jax.ShapeDtypeStruct(shape, jnp.bfloat16),
        cost_estimate=pl.CostEstimate(flops=0, bytes_accessed=2 * MIB, transcendentals=0),
    )(*scalars, *parts)


def other_core(x, y, z, core):
    return linear(x, y, z, 1 - core)


def shards(master, activations, owner):
    f32, bf16 = jnp.float32, jnp.bfloat16
    rows = jnp.asarray(np.array([device_row(i) for i in range(N_DEV)], np.int32))
    me = lax.axis_index("group") * 16 + lax.axis_index("tp")
    table = lax.dynamic_index_in_dim(rows, me, 0, keepdims=False)

    planes = {}
    for axis in "zyx":
        at, count = PARTS[axis]
        planes[axis] = gather_plane(activations[None, at : at + count], ORDER[axis])
    late_table, *held = lax.optimization_barrier((table, *planes.values()))
    blocks = {axis: gather_last(v, axis) for axis, v in zip("zyx", held)}

    theirs = permute(refit(late_table, master, THEIRS), other_core)
    mine = refit(late_table, master, MINE)
    weights = [mine, theirs]

    zn, yn, xn = (PARTS[a][1] for a in "zyx")
    early = product(
        early_kernel,
        table,
        weights,
        blocks,
        (0, 1),
        [
            pltpu.VMEM((2, 8, zn, 2 * SHARE), bf16),
            pltpu.VMEM((2, 2, yn, 8 * SHARE), bf16),
            pltpu.VMEM((2, 4, xn, 4 * SHARE), bf16),
            pltpu.SemaphoreType.DMA((2, 3)),
        ],
        jax.ShapeDtypeStruct((2, 4, 256, 2 * COLS), f32),
    )
    late = [
        pltpu.VMEM((2, 4, zn, 2 * SHARE), bf16),
        pltpu.VMEM((2, yn, 8 * SHARE), bf16),
        pltpu.VMEM((2, 4, xn, 4 * SHARE), bf16),
        pltpu.VMEM((4, 256, 2 * COLS), f32),
        pltpu.SemaphoreType.DMA((4,)),
    ]
    passed, kept = (
        product(
            functools.partial(late_kernel, keep),
            table,
            weights,
            blocks,
            (2, 3),
            late,
            jax.ShapeDtypeStruct((4, 256, 2 * COLS), f32 if keep else bf16),
            (early,),
        )
        for keep in (False, True)
    )
    total = (kept + permute(passed, other_core).astype(f32)).astype(bf16)

    got = {}
    for dy in (2, 1, 3, 0):
        got[dy] = permute(total[dy], lambda x, y, z, c: linear(x + 2 * c, y + dy, z, c))
    own = jnp.stack([got[dy] for dy in range(4)])
    other = permute(own, other_core)

    picked = small_call(spread_kernel, [table, owner], [own, other], (4, 256, 2 * COLS))
    got = {}
    for dz in (2, 1, 3, 0):
        got[dz] = permute(picked[dz], lambda x, y, z, c: linear(x ^ c, y, z + dz, x % 2))
    return small_call(arrange_kernel, [table], [jnp.stack([got[dz] for dz in range(4)])], (256, 8 * COLS))


def solution(mesh):
    in_specs = (P(None, ("group", "tp")), P("group", "tp"), P())
    out_specs = P("group", "tp")
    return jax.shard_map(shards, mesh=mesh, in_specs=in_specs, out_specs=out_specs, check_vma=False)
```

time: 1070 us -> 194 us (0.18)
  waiting for transfers between devices: 403 us -> 74.1 us
  local copies, waits for them, and re-layouts: 289 us -> 18.1 us
  other arithmetic: 203 us -> 1.98 us
  matrix products: 76.2 us -> 0 us
  blocking collectives: 74.6 us -> 0 us
  starting transfers between devices: 5.15 us -> 58.4 us
  Pallas kernels: 0 us -> 38.7 us
  between operations: 13.5 us -> 0.28 us
    all_gather x1 -> x0, waiting for transfers between devices: 303 us -> none  [shards(): lax.all_gather(coded_rows, 'group', axis=1, tiled=True)]
    add x4 -> x0, other arithmetic: 125 us -> none  [step(): total + product.reshape(count, cols // block, block) * scale_row[None, :,...]
    while x4 -> x0, local copies, waits for them, and re-layouts: 110 us -> none
    reduce_scatter x1 -> x0, waiting for transfers between devices: 96.2 us -> none  [shards(): lax.psum_scatter(partial_value.astype(jnp.bfloat16), 'tp', scatter_dimens...]
    unnamed x11 -> x23, local copies, waits for them, and re-layouts: 99.3 us -> 11.8 us
    dot_general x4 -> x0, matrix products: 76.2 us -> none  [step(): product = jnp.dot(left, right, preferred_element_type=jnp.float32)]
    ppermute x0 -> x32, waiting for transfers between devices: none -> 74.1 us  [permute(): lax.ppermute(value, AXES, [(i, move(*coords(i))) for i in range(N_DEV)])]
    ppermute x0 -> x32, starting transfers between devices: none -> 58.4 us  [permute(): lax.ppermute(value, AXES, [(i, move(*coords(i))) for i in range(N_DEV)])]
  transfers between devices with their start and end apart: 3 -> 32, of which waited for: 3 -> 15; matrix products, arithmetic and copies ran while one was open for 0% -> 6% of each run, Pallas kernels for 0% -> 11%
where the time goes in v3:
time: 194 us; the launch traced here: 192 us
  waiting for transfers between devices  74.1 us (38%)
  starting transfers between devices  58.4 us (30%)
  Pallas kernels  38.7 us (20%)
  local copies, waits for them, and re-layouts  18.1 us (9%)
  other arithmetic  1.98 us (1%)
    ppermute x32, waiting for transfers between devices, permute(): lax.ppermute(value, AXES, [(i, move(*coords(i))) for i in range(N_DEV)])  74.1 us
    ppermute x32, starting transfers between devices, permute(): lax.ppermute(value, AXES, [(i, move(*coords(i))) for i in range(N_DEV)])  58.4 us
    pallas_call x3, Pallas kernels, product(): pl.pallas_call(kernel, in_specs=[pl.BlockSpec(memory_space=pltpu.SMEM)] +...  19 us
    pallas_call x2, Pallas kernels, refit(): pl.pallas_call(refit_kernel, grid_spec=pltpu.PrefetchScalarGridSpec(num_s...  14.8 us
    unnamed x23, local copies, waits for them, and re-layouts  11.8 us
    pallas_call x2, Pallas kernels, small_call(): pl.pallas_call(kernel, in_specs=[smem] * len(scalars) + [vmem] * len(part...  4.95 us
  transfers between devices with their start and end apart: 32, of which 15 were waited for; matrix products, arithmetic and copies ran while one was open for 6% of the time, Pallas kernels for 11%

profile of v3, /device:TPU:3, one launch (start us, length us, event | category | flops | bytes accessed | tf_op | source)
XLA Modules:
  0.0 191.7 jit_solution(5292415376701622727)
XLA Ops:
  0.0 0.9 slice_bitcast_fusion.9
  0.9 2.8 %collective-permute-start.8 = (bf16[1,80,512]{2,1,0:T(8,128)(2,1)S(1)}, bf16[1,80,512]{2,1,0:T(8,128)(2,1)S(1)}, u32[]{:S(2)}, u32[]{:S(2)}) collective-permute-start(bf16[1,80,512]{2,1,0:T(8,128)(2,1)S(1)} %get-tuple-element.21), channel_id=1, source_target_pairs={{0,16},{1,49},{2,18},{3,51},{4,20},{5,53},{6,22},{7,55},{8,24},{9,... | collective-permute-start | bytes 245768 | tf_op jit(solution)/shard_map/ppermute | solution.py:31
  3.8 3.8 %collective-permute-start.4 = (bf16[1,80,512]{2,1,0:T(8,128)(2,1)S(1)}, bf16[1,80,512]{2,1,0:T(8,128)(2,1)S(1)}, u32[]{:S(2)}, u32[]{:S(2)}) collective-permute-start(bf16[1,80,512]{2,1,0:T(8,128)(2,1)S(1)} %get-tuple-element.22), channel_id=1, source_target_pairs={{0,2},{1,7},{2,0},{3,5},{4,6},{5,3},{6,4},{7,1},{8,10},{9,15},{10,... | collective-permute-start | bytes 245768 | tf_op jit(solution)/shard_map/ppermute | solution.py:31
  7.5 0.9 slice_bitcast_fusion.8
  8.4 1.2 collective-permute-start
  9.6 1.6 constant_dynamic-update-slice_fusion.14
  11.2 0.9 constant_dynamic-update-slice_fusion.4
  12.1 1.3 dynamic-slice_bitcast_fusion.table
  13.6 0.6 constant_dynamic-update-slice_fusion.13
  14.3 0.6 constant_dynamic-update-slice_fusion.8
  14.9 1.6 collective-permute-start.1
  16.5 1.4 collective-permute-done.9
  18.1 0.3 collective-permute-start.6
  18.5 1.1 collective-permute-done.1
  19.6 0.7 collective-permute-start.2
  20.3 0.7 constant_dynamic-update-slice_fusion.12
  21.0 4.2 %collective-permute-done.10 = bf16[4,80,512]{2,1,0:T(8,128)(2,1)S(1)} collective-permute-done((bf16[4,80,512]{2,1,0:T(8,128)(2,1)S(1)}, bf16[4,80,512]{2,1,0:T(8,128)(2,1)S(1)}, u32[]{:S(2)}, u32[]{:S(2)}) %collective-permute-start.10) | collective-permute-done | bytes 327712 | tf_op jit(solution)/shard_map/ppermute | solution.py:31
  25.7 2.1 %collective-permute-start.7 = (bf16[8,80,512]{2,1,0:T(8,128)(2,1)S(1)}, bf16[8,80,512]{2,1,0:T(8,128)(2,1)S(1)}, u32[]{:S(2)}, u32[]{:S(2)}) collective-permute-start(bf16[8,80,512]{2,1,0:T(8,128)(2,1)S(1)} %pad_maximum_fusion.3), channel_id=1, source_target_pairs={{0,72},{1,9},{2,74},{3,11},{4,76},{5,13},{6,78},{7,15},{8,64},{9,1... | collective-permute-start | bytes 1966088 | tf_op jit(solution)/shard_map/ppermute | solution.py:31
  27.8 0.7 collective-permute-start.3
  28.5 0.7 constant_dynamic-update-slice_fusion.7
  29.2 0.7 constant_dynamic-update-slice_fusion.11
  30.0 0.7 constant_dynamic-update-slice_fusion.6
  30.8 4.3 %collective-permute-done.11 = bf16[8,80,512]{2,1,0:T(8,128)(2,1)S(1)} collective-permute-done((bf16[8,80,512]{2,1,0:T(8,128)(2,1)S(1)}, bf16[8,80,512]{2,1,0:T(8,128)(2,1)S(1)}, u32[]{:S(2)}, u32[]{:S(2)}) %collective-permute-start.11) | collective-permute-done | bytes 655392 | tf_op jit(solution)/shard_map/ppermute | solution.py:31
  35.1 0.9 constant_dynamic-update-slice_fusion.10
  36.0 0.9 constant_dynamic-update-slice_fusion.5
  36.9 3.1 %collective-permute-done.3 = bf16[8,96,512]{2,1,0:T(8,128)(2,1)S(1)} collective-permute-done((bf16[8,96,512]{2,1,0:T(8,128)(2,1)S(1)}, bf16[8,96,512]{2,1,0:T(8,128)(2,1)S(1)}, u32[]{:S(2)}, u32[]{:S(2)}) %collective-permute-start.3) | collective-permute-done | bytes 786464 | tf_op jit(solution)/shard_map/ppermute | solution.py:31
  40.1 1.2 copy-done.1
  41.2 7.4 %shard_map.47 = bf16[4096,256]{1,0:T(8,128)(2,1)} custom-call(s32[28]{0:T(128)} %dynamic-slice_bitcast_fusion.table, f32[8192,256]{1,0:T(8,128)} %master.3), custom_call_target="tpu_custom_call" | custom-call | flops 6291456 | bytes 6291456 | tf_op jit(solution)/shard_map/pallas_call | solution.py:91
  48.7 6.2 %collective-permute-start.12 = (bf16[4096,256]{1,0:T(8,128)(2,1)}, bf16[4096,256]{1,0:T(8,128)(2,1)S(1)}, u32[]{:S(2)}, u32[]{:S(2)}) collective-permute-start(bf16[4096,256]{1,0:T(8,128)(2,1)} %shard_map.47), channel_id=1, source_target_pairs={{0,1},{1,0},{2,3},{3,2},{4,5},{5,4},{6,7},{7,6},{8,9},{9,8},{10,11... | collective-permute-start | bytes 6291464 | tf_op jit(solution)/shard_map/ppermute | solution.py:31
  54.9 2.0 %collective-permute-start.17 = (bf16[16,80,512]{2,1,0:T(8,128)(2,1)}, bf16[16,80,512]{2,1,0:T(8,128)(2,1)}, u32[]{:S(2)}, u32[]{:S(2)}) collective-permute-start(bf16[16,80,512]{2,1,0:T(8,128)(2,1)} %constant_dynamic-update-slice_fusion.5), channel_id=1, source_target_pairs={{0,16},{1,49},{2,18},{3,51},{4,20},{5,53},{6,22},{7,55},{8,24},{9,... | collective-permute-start | bytes 3932168 | tf_op jit(solution)/shard_map/ppermute | solution.py:31
  56.9 2.4 %collective-permute-start.20 = (bf16[16,80,512]{2,1,0:T(8,128)(2,1)}, bf16[16,80,512]{2,1,0:T(8,128)(2,1)}, u32[]{:S(2)}, u32[]{:S(2)}) collective-permute-start(bf16[16,80,512]{2,1,0:T(8,128)(2,1)} %constant_dynamic-update-slice_fusion.10), channel_id=1, source_target_pairs={{0,8},{1,73},{2,10},{3,75},{4,12},{5,77},{6,14},{7,79},{8,0},{9,65... | collective-permute-start | bytes 3932168 | tf_op jit(solution)/shard_map/ppermute | solution.py:31
  59.3 23.5 %collective-permute-done.17 = bf16[16,80,512]{2,1,0:T(8,128)(2,1)} collective-permute-done((bf16[16,80,512]{2,1,0:T(8,128)(2,1)}, bf16[16,80,512]{2,1,0:T(8,128)(2,1)}, u32[]{:S(2)}, u32[]{:S(2)}) %collective-permute-start.17) | collective-permute-done | bytes 1310752 | tf_op jit(solution)/shard_map/ppermute | solution.py:31
  82.8 1.1 collective-permute-start.13
  83.9 0.4 collective-permute-start.15
  84.3 5.3 %collective-permute-start.19 = (bf16[16,80,512]{2,1,0:T(8,128)(2,1)}, bf16[16,80,512]{2,1,0:T(8,128)(2,1)}, u32[]{:S(2)}, u32[]{:S(2)}) collective-permute-start(bf16[16,80,512]{2,1,0:T(8,128)(2,1)} %constant_dynamic-update-slice_fusion.10), channel_id=1, source_target_pairs={{0,72},{1,9},{2,74},{3,11},{4,76},{5,13},{6,78},{7,15},{8,64},{9,1... | collective-permute-start | bytes 3932168 | tf_op jit(solution)/shard_map/ppermute | solution.py:31
  89.7 0.4 collective-permute-start.21
  90.0 7.4 %shard_map.46.mine = bf16[4096,256]{1,0:T(8,128)(2,1)} custom-call(s32[28]{0:T(128)} %dynamic-slice_bitcast_fusion.table, f32[8192,256]{1,0:T(8,128)} %master.3), custom_call_target="tpu_custom_call" | custom-call | flops 6291456 | bytes 6291456 | tf_op jit(solution)/shard_map/pallas_call | solution.py:91
  97.5 1.6 copy-done
  99.1 1.4 copy-done.2
  100.5 7.2 %shard_map.48.early = f32[2,4,256,512]{3,2,1,0:T(8,128)S(1)} custom-call(s32[28]{0:T(128)S(1)} %copy-done.3, bf16[4096,256]{1,0:T(8,128)(2,1)S(1)} %copy-done, bf16[4096,256]{1,0:T(8,128)(2,1)S(1)} %collective-permute-done.12.theirs, bf16[4,4,96,512]{3,2,1,0:T(8,128)(2,1)S(1)} %bitcast.52, bf16[4,4,96,512]{3,2,1,0:T(8,128)(2,1)} %bitcast.11.z1, ...), custom_call_target="tpu_custom_call" | custom-call | flops 4294967296 | bytes 14680064 | tf_op jit(solution)/shard_map/pallas_call | solution.py:213
  107.7 11.6 %collective-permute-done.21 = bf16[16,80,512]{2,1,0:T(8,128)(2,1)} collective-permute-done((bf16[16,80,512]{2,1,0:T(8,128)(2,1)}, bf16[16,80,512]{2,1,0:T(8,128)(2,1)}, u32[]{:S(2)}, u32[]{:S(2)}) %collective-permute-start.21) | collective-permute-done | bytes 1310752 | tf_op jit(solution)/shard_map/ppermute | solution.py:31
  119.3 0.3 collective-permute-done.15
  119.6 5.7 %shard_map.50 = bf16[4,256,512]{2,1,0:T(8,128)(2,1)S(1)} custom-call(s32[28]{0:T(128)S(1)} %copy-done.3, bf16[4096,256]{1,0:T(8,128)(2,1)S(1)} %copy-done, bf16[4096,256]{1,0:T(8,128)(2,1)S(1)} %collective-permute-done.12.theirs, bf16[4,4,96,512]{3,2,1,0:T(8,128)(2,1)} %bitcast.4.z2, bf16[4,4,96,512]{3,2,1,0:T(8,128)(2,1)} %bitcast.5.z3, ...), custom_call_target="tpu_custom_call" | custom-call | flops 4294967296 | bytes 14680064 | tf_op jit(solution)/shard_map/pallas_call | solution.py:213
  125.3 5.8 %collective-permute-start.22 = (bf16[4,256,512]{2,1,0:T(8,128)(2,1)S(1)}, bf16[4,256,512]{2,1,0:T(8,128)(2,1)S(1)}, u32[]{:S(2)}, u32[]{:S(2)}) collective-permute-start(bf16[4,256,512]{2,1,0:T(8,128)(2,1)S(1)} %shard_map.50), channel_id=1, source_target_pairs={{0,1},{1,0},{2,3},{3,2},{4,5},{5,4},{6,7},{7,6},{8,9},{9,8},{10,11... | collective-permute-start | bytes 3145736 | tf_op jit(solution)/shard_map/ppermute | solution.py:31
  131.1 6.1 %shard_map.49 = f32[4,256,512]{2,1,0:T(8,128)S(1)} custom-call(s32[28]{0:T(128)S(1)} %copy-done.3, bf16[4096,256]{1,0:T(8,128)(2,1)S(1)} %copy-done, bf16[4096,256]{1,0:T(8,128)(2,1)S(1)} %collective-permute-done.12.theirs, bf16[4,4,96,512]{3,2,1,0:T(8,128)(2,1)} %bitcast.4.z2, bf16[4,4,96,512]{3,2,1,0:T(8,128)(2,1)} %bitcast.5.z3, ...), custom_call_target="tpu_custom_call" | custom-call | flops 4294967296 | bytes 14680064 | tf_op jit(solution)/shard_map/pallas_call | solution.py:213
  137.2 0.3 add_convert_fusion
  137.6 9.4 %collective-permute-start.23 = (bf16[256,512]{1,0:T(8,128)(2,1)S(1)}, bf16[256,512]{1,0:T(8,128)(2,1)S(1)}, u32[]{:S(2)}, u32[]{:S(2)}) collective-permute-start(bf16[256,512]{1,0:T(8,128)(2,1)S(1)} %get-tuple-element.17), channel_id=1, source_target_pairs={{0,0},{1,65},{2,2},{3,67},{4,4},{5,69},{6,6},{7,71},{8,8},{9,73},{... | collective-permute-start | bytes 786440 | tf_op jit(solution)/shard_map/ppermute | solution.py:31
  147.1 5.4 %collective-permute-start.25 = (bf16[256,512]{1,0:T(8,128)(2,1)S(1)}, bf16[256,512]{1,0:T(8,128)(2,1)S(1)}, u32[]{:S(2)}, u32[]{:S(2)}) collective-permute-start(bf16[256,512]{1,0:T(8,128)(2,1)S(1)} %get-tuple-element.19), channel_id=1, source_target_pairs={{0,32},{1,97},{2,34},{3,99},{4,36},{5,101},{6,38},{7,103},{8,40},{... | collective-permute-start | bytes 786440 | tf_op jit(solution)/shard_map/ppermute | solution.py:31
  152.5 0.4 collective-permute-start.26
  152.9 3.0 %collective-permute-done.24 = bf16[256,512]{1,0:T(8,128)(2,1)S(1)} collective-permute-done((bf16[256,512]{1,0:T(8,128)(2,1)S(1)}, bf16[256,512]{1,0:T(8,128)(2,1)S(1)}, u32[]{:S(2)}, u32[]{:S(2)}) %collective-permute-start.24) | collective-permute-done | bytes 262176 | tf_op jit(solution)/shard_map/ppermute | solution.py:31
  155.9 3.2 %collective-permute-done.25 = bf16[256,512]{1,0:T(8,128)(2,1)S(1)} collective-permute-done((bf16[256,512]{1,0:T(8,128)(2,1)S(1)}, bf16[256,512]{1,0:T(8,128)(2,1)S(1)}, u32[]{:S(2)}, u32[]{:S(2)}) %collective-permute-start.25) | collective-permute-done | bytes 262176 | tf_op jit(solution)/shard_map/ppermute | solution.py:31
  159.1 1.1 collective-permute-done.26
  160.4 2.6 %collective-permute-done.27.other = bf16[4,256,512]{2,1,0:T(8,128)(2,1)S(1)} collective-permute-done((bf16[4,256,512]{2,1,0:T(8,128)(2,1)S(1)}, bf16[4,256,512]{2,1,0:T(8,128)(2,1)S(1)}, u32[]{:S(2)}, u32[]{:S(2)}) %collective-permute-start.27) | collective-permute-done | bytes 1048608 | tf_op jit(solution)/shard_map/ppermute | solution.py:31
  163.0 1.0 copy-done.5
  164.0 2.7 %shard_map.51 = bf16[4,256,512]{2,1,0:T(8,128)(2,1)} custom-call(s32[28]{0:T(128)} %dynamic-slice_bitcast_fusion.table, s32[8]{0:T(128)} %owner.1, bf16[4,256,512]{2,1,0:T(8,128)(2,1)} %copy-done.4, bf16[4,256,512]{2,1,0:T(8,128)(2,1)} %copy-done.5), custom_call_target="tpu_custom_call" | custom-call | bytes 2097152 | tf_op jit(solution)/shard_map/pallas_call | solution.py:249
  166.7 1.3 slice_bitcast_fusion.3
  167.9 1.9 %collective-permute-start.28 = (bf16[256,512]{1,0:T(8,128)(2,1)S(1)}, bf16[256,512]{1,0:T(8,128)(2,1)S(1)}, u32[]{:S(2)}, u32[]{:S(2)}) collective-permute-start(bf16[256,512]{1,0:T(8,128)(2,1)S(1)} %get-tuple-element.13), channel_id=1, source_target_pairs={{0,0},{1,8},{2,2},{3,10},{4,4},{5,12},{6,6},{7,14},{8,9},{9,1},{10... | collective-permute-start | bytes 786440 | tf_op jit(solution)/shard_map/ppermute | solution.py:31
  169.9 0.3 collective-permute-start.29
  170.1 2.0 %collective-permute-start.30 = (bf16[256,512]{1,0:T(8,128)(2,1)S(1)}, bf16[256,512]{1,0:T(8,128)(2,1)S(1)}, u32[]{:S(2)}, u32[]{:S(2)}) collective-permute-start(bf16[256,512]{1,0:T(8,128)(2,1)S(1)} %get-tuple-element.15), channel_id=1, source_target_pairs={{0,4},{1,12},{2,6},{3,14},{4,0},{5,8},{6,2},{7,10},{8,13},{9,5},{1... | collective-permute-start | bytes 786440 | tf_op jit(solution)/shard_map/ppermute | solution.py:31
  172.1 1.8 collective-permute-start.31
  173.9 11.5 %collective-permute-done.29 = bf16[256,512]{1,0:T(8,128)(2,1)S(1)} collective-permute-done((bf16[256,512]{1,0:T(8,128)(2,1)S(1)}, bf16[256,512]{1,0:T(8,128)(2,1)S(1)}, u32[]{:S(2)}, u32[]{:S(2)}) %collective-permute-start.29) | collective-permute-done | bytes 262176 | tf_op jit(solution)/shard_map/ppermute | solution.py:31
  185.4 2.9 %collective-permute-done.31 = bf16[256,512]{1,0:T(8,128)(2,1)S(1)} collective-permute-done((bf16[256,512]{1,0:T(8,128)(2,1)S(1)}, bf16[256,512]{1,0:T(8,128)(2,1)S(1)}, u32[]{:S(2)}, u32[]{:S(2)}) %collective-permute-start.31) | collective-permute-done | bytes 262176 | tf_op jit(solution)/shard_map/ppermute | solution.py:31
  188.3 1.1 pad_maximum_fusion.1.parts
  189.4 2.3 %shard_map.52 = bf16[256,2048]{1,0:T(8,128)(2,1)} custom-call(s32[28]{0:T(128)} %dynamic-slice_bitcast_fusion.table, bf16[4,256,512]{2,1,0:T(8,128)(2,1)} %pad_maximum_fusion.1.parts), custom_call_target="tpu_custom_call" | custom-call | bytes 2097152 | tf_op jit(solution)/shard_map/pallas_call | solution.py:249
  (50 shorter events, 1.5 us)
Async XLA Ops:
  0.9 12.5 %collective-permute-start.8 = (bf16[1,80,512]{2,1,0:T(8,128)(2,1)S(1)}, bf16[1,80,512]{2,1,0:T(8,128)(2,1)S(1)}, u32[]{:S(2)}, u32[]{:S(2)}) collective-permute-start(bf16[1,80,512]{2,1,0:T(8,128)(2,1)S(1)} %get-tuple-element.21), channel_id=1, source_target_pairs={{0,16},{1,49},{2,18},{3,51},{4,20},{5,53},{6,22},{7,55},{8,24},{9,... | collective-permute-start | bytes 245768 | tf_op jit(solution)/shard_map/ppermute | solution.py:31
  3.8 9.8 %collective-permute-start.4 = (bf16[1,80,512]{2,1,0:T(8,128)(2,1)S(1)}, bf16[1,80,512]{2,1,0:T(8,128)(2,1)S(1)}, u32[]{:S(2)}, u32[]{:S(2)}) collective-permute-start(bf16[1,80,512]{2,1,0:T(8,128)(2,1)S(1)} %get-tuple-element.22), channel_id=1, source_target_pairs={{0,2},{1,7},{2,0},{3,5},{4,6},{5,3},{6,4},{7,1},{8,10},{9,15},{10,... | collective-permute-start | bytes 245768 | tf_op jit(solution)/shard_map/ppermute | solution.py:31
  8.4 6.5 %collective-permute-start = (bf16[1,96,512]{2,1,0:T(8,128)(2,1)S(1)}, bf16[1,96,512]{2,1,0:T(8,128)(2,1)S(1)}, u32[]{:S(2)}, u32[]{:S(2)}) collective-permute-start(bf16[1,96,512]{2,1,0:T(8,128)(2,1)S(1)} %slice_bitcast_fusion.8), channel_id=1, source_target_pairs={{0,8},{1,73},{2,10},{3,75},{4,12},{5,77},{6,14},{7,79},{8,0},{9,65... | collective-permute-start | bytes 294920 | tf_op jit(solution)/shard_map/ppermute | solution.py:31
  13.4 4.5 %collective-permute-start.9 = (bf16[2,80,512]{2,1,0:T(8,128)(2,1)S(1)}, bf16[2,80,512]{2,1,0:T(8,128)(2,1)S(1)}, u32[]{:S(2)}, u32[]{:S(2)}) collective-permute-start(bf16[2,80,512]{2,1,0:T(8,128)(2,1)S(1)} %pad_maximum_fusion.10), channel_id=1, source_target_pairs={{0,48},{1,17},{2,50},{3,19},{4,52},{5,21},{6,54},{7,23},{8,56},{9,... | collective-permute-start | bytes 491528 | tf_op jit(solution)/shard_map/ppermute | solution.py:31
  13.5 4.5 %collective-permute-start.5 = (bf16[2,80,512]{2,1,0:T(8,128)(2,1)S(1)}, bf16[2,80,512]{2,1,0:T(8,128)(2,1)S(1)}, u32[]{:S(2)}, u32[]{:S(2)}) collective-permute-start(bf16[2,80,512]{2,1,0:T(8,128)(2,1)S(1)} %pad_maximum_fusion.9), channel_id=1, source_target_pairs={{0,6},{1,3},{2,4},{3,1},{4,2},{5,7},{6,0},{7,5},{8,14},{9,11},{10,... | collective-permute-start | bytes 491528 | tf_op jit(solution)/shard_map/ppermute | solution.py:31
  14.9 4.7 %collective-permute-start.1 = (bf16[2,96,512]{2,1,0:T(8,128)(2,1)S(1)}, bf16[2,96,512]{2,1,0:T(8,128)(2,1)S(1)}, u32[]{:S(2)}, u32[]{:S(2)}) collective-permute-start(bf16[2,96,512]{2,1,0:T(8,128)(2,1)S(1)} %pad_maximum_fusion.8), channel_id=1, source_target_pairs={{0,72},{1,9},{2,74},{3,11},{4,76},{5,13},{6,78},{7,15},{8,64},{9,1... | collective-permute-start | bytes 589832 | tf_op jit(solution)/shard_map/ppermute | solution.py:31
  18.0 7.2 %collective-permute-start.10 = (bf16[4,80,512]{2,1,0:T(8,128)(2,1)S(1)}, bf16[4,80,512]{2,1,0:T(8,128)(2,1)S(1)}, u32[]{:S(2)}, u32[]{:S(2)}) collective-permute-start(bf16[4,80,512]{2,1,0:T(8,128)(2,1)S(1)} %pad_maximum_fusion.7), channel_id=1, source_target_pairs={{0,2},{1,7},{2,0},{3,5},{4,6},{5,3},{6,4},{7,1},{8,10},{9,15},{10,... | collective-permute-start | bytes 983048 | tf_op jit(solution)/shard_map/ppermute | solution.py:31
  18.1 7.4 %collective-permute-start.6 = (bf16[4,80,512]{2,1,0:T(8,128)(2,1)S(1)}, bf16[4,80,512]{2,1,0:T(8,128)(2,1)S(1)}, u32[]{:S(2)}, u32[]{:S(2)}) collective-permute-start(bf16[4,80,512]{2,1,0:T(8,128)(2,1)S(1)} %pad_maximum_fusion.6), channel_id=1, source_target_pairs={{0,8},{1,73},{2,10},{3,75},{4,12},{5,77},{6,14},{7,79},{8,0},{9,65... | collective-permute-start | bytes 983048 | tf_op jit(solution)/shard_map/ppermute | solution.py:31
  19.6 8.1 %collective-permute-start.2 = (bf16[4,96,512]{2,1,0:T(8,128)(2,1)S(1)}, bf16[4,96,512]{2,1,0:T(8,128)(2,1)S(1)}, u32[]{:S(2)}, u32[]{:S(2)}) collective-permute-start(bf16[4,96,512]{2,1,0:T(8,128)(2,1)S(1)} %pad_maximum_fusion.5), channel_id=1, source_target_pairs={{0,16},{1,49},{2,18},{3,51},{4,20},{5,53},{6,22},{7,55},{8,24},{9,... | collective-permute-start | bytes 1179656 | tf_op jit(solution)/shard_map/ppermute | solution.py:31
  25.3 9.8 %collective-permute-start.11 = (bf16[8,80,512]{2,1,0:T(8,128)(2,1)S(1)}, bf16[8,80,512]{2,1,0:T(8,128)(2,1)S(1)}, u32[]{:S(2)}, u32[]{:S(2)}) collective-permute-start(bf16[8,80,512]{2,1,0:T(8,128)(2,1)S(1)} %pad_maximum_fusion.4), channel_id=1, source_target_pairs={{0,6},{1,3},{2,4},{3,1},{4,2},{5,7},{6,0},{7,5},{8,14},{9,11},{10,... | collective-permute-start | bytes 1966088 | tf_op jit(solution)/shard_map/ppermute | solution.py:31
  25.7 10.3 %collective-permute-start.7 = (bf16[8,80,512]{2,1,0:T(8,128)(2,1)S(1)}, bf16[8,80,512]{2,1,0:T(8,128)(2,1)S(1)}, u32[]{:S(2)}, u32[]{:S(2)}) collective-permute-start(bf16[8,80,512]{2,1,0:T(8,128)(2,1)S(1)} %pad_maximum_fusion.3), channel_id=1, source_target_pairs={{0,72},{1,9},{2,74},{3,11},{4,76},{5,13},{6,78},{7,15},{8,64},{9,1... | collective-permute-start | bytes 1966088 | tf_op jit(solution)/shard_map/ppermute | solution.py:31
  27.8 12.2 %collective-permute-start.3 = (bf16[8,96,512]{2,1,0:T(8,128)(2,1)S(1)}, bf16[8,96,512]{2,1,0:T(8,128)(2,1)S(1)}, u32[]{:S(2)}, u32[]{:S(2)}) collective-permute-start(bf16[8,96,512]{2,1,0:T(8,128)(2,1)S(1)} %pad_maximum_fusion.2), channel_id=1, source_target_pairs={{0,48},{1,17},{2,50},{3,19},{4,52},{5,21},{6,54},{7,23},{8,56},{9,... | collective-permute-start | bytes 2359304 | tf_op jit(solution)/shard_map/ppermute | solution.py:31
  40.1 1.2 copy-start.1
  48.7 48.8 %copy-start.3 = (s32[28]{0:T(128)S(1)}, s32[28]{0:T(128)}, u32[]{:S(2)}) copy-start(s32[28]{0:T(128)} %dynamic-slice_bitcast_fusion.table) | copy-start | bytes 340
  48.7 41.0 %collective-permute-start.12 = (bf16[4096,256]{1,0:T(8,128)(2,1)}, bf16[4096,256]{1,0:T(8,128)(2,1)S(1)}, u32[]{:S(2)}, u32[]{:S(2)}) collective-permute-start(bf16[4096,256]{1,0:T(8,128)(2,1)} %shard_map.47), channel_id=1, source_target_pairs={{0,1},{1,0},{2,3},{3,2},{4,5},{5,4},{6,7},{7,6},{8,9},{9,8},{10,11... | collective-permute-start | bytes 6291464 | tf_op jit(solution)/shard_map/ppermute | solution.py:31
  54.9 29.0 %collective-permute-start.14 = (bf16[16,96,512]{2,1,0:T(8,128)(2,1)}, bf16[16,96,512]{2,1,0:T(8,128)(2,1)}, u32[]{:S(2)}, u32[]{:S(2)}) collective-permute-start(bf16[16,96,512]{2,1,0:T(8,128)(2,1)} %copy-done.1), channel_id=1, source_target_pairs={{0,2},{1,7},{2,0},{3,5},{4,6},{5,3},{6,4},{7,1},{8,10},{9,15},{10,... | collective-permute-start | bytes 4718600 | tf_op jit(solution)/shard_map/ppermute | solution.py:31
  54.9 27.9 %collective-permute-start.17 = (bf16[16,80,512]{2,1,0:T(8,128)(2,1)}, bf16[16,80,512]{2,1,0:T(8,128)(2,1)}, u32[]{:S(2)}, u32[]{:S(2)}) collective-permute-start(bf16[16,80,512]{2,1,0:T(8,128)(2,1)} %constant_dynamic-update-slice_fusion.5), channel_id=1, source_target_pairs={{0,16},{1,49},{2,18},{3,51},{4,20},{5,53},{6,22},{7,55},{8,24},{9,... | collective-permute-start | bytes 3932168 | tf_op jit(solution)/shard_map/ppermute | solution.py:31
  56.9 27.4 %collective-permute-start.20 = (bf16[16,80,512]{2,1,0:T(8,128)(2,1)}, bf16[16,80,512]{2,1,0:T(8,128)(2,1)}, u32[]{:S(2)}, u32[]{:S(2)}) collective-permute-start(bf16[16,80,512]{2,1,0:T(8,128)(2,1)} %constant_dynamic-update-slice_fusion.10), channel_id=1, source_target_pairs={{0,8},{1,73},{2,10},{3,75},{4,12},{5,77},{6,14},{7,79},{8,0},{9,65... | collective-permute-start | bytes 3932168 | tf_op jit(solution)/shard_map/ppermute | solution.py:31
  59.3 30.4 %collective-permute-start.16 = (bf16[16,80,512]{2,1,0:T(8,128)(2,1)}, bf16[16,80,512]{2,1,0:T(8,128)(2,1)S(1)}, u32[]{:S(2)}, u32[]{:S(2)}) collective-permute-start(bf16[16,80,512]{2,1,0:T(8,128)(2,1)} %constant_dynamic-update-slice_fusion.5), channel_id=1, source_target_pairs={{0,48},{1,17},{2,50},{3,19},{4,52},{5,21},{6,54},{7,23},{8,56},{9,... | collective-permute-start | bytes 3932168 | tf_op jit(solution)/shard_map/ppermute | solution.py:31
  82.8 24.8 %collective-permute-start.13 = (bf16[16,96,512]{2,1,0:T(8,128)(2,1)}, bf16[16,96,512]{2,1,0:T(8,128)(2,1)}, u32[]{:S(2)}, u32[]{:S(2)}) collective-permute-start(bf16[16,96,512]{2,1,0:T(8,128)(2,1)} %copy-done.1), channel_id=1, source_target_pairs={{0,6},{1,3},{2,4},{3,1},{4,2},{5,7},{6,0},{7,5},{8,14},{9,11},{10,... | collective-permute-start | bytes 4718600 | tf_op jit(solution)/shard_map/ppermute | solution.py:31
  83.9 35.7 %collective-permute-start.15 = (bf16[16,96,512]{2,1,0:T(8,128)(2,1)}, bf16[16,96,512]{2,1,0:T(8,128)(2,1)}, u32[]{:S(2)}, u32[]{:S(2)}) collective-permute-start(bf16[16,96,512]{2,1,0:T(8,128)(2,1)} %collective-permute-done.14), channel_id=1, source_target_pairs={{0,6},{1,3},{2,4},{3,1},{4,2},{5,7},{6,0},{7,5},{8,14},{9,11},{10,... | collective-permute-start | bytes 4718600 | tf_op jit(solution)/shard_map/ppermute | solution.py:31
  84.3 23.3 %collective-permute-start.19 = (bf16[16,80,512]{2,1,0:T(8,128)(2,1)}, bf16[16,80,512]{2,1,0:T(8,128)(2,1)}, u32[]{:S(2)}, u32[]{:S(2)}) collective-permute-start(bf16[16,80,512]{2,1,0:T(8,128)(2,1)} %constant_dynamic-update-slice_fusion.10), channel_id=1, source_target_pairs={{0,72},{1,9},{2,74},{3,11},{4,76},{5,13},{6,78},{7,15},{8,64},{9,1... | collective-permute-start | bytes 3932168 | tf_op jit(solution)/shard_map/ppermute | solution.py:31
  89.6 18.0 %collective-permute-start.18 = (bf16[16,80,512]{2,1,0:T(8,128)(2,1)}, bf16[16,80,512]{2,1,0:T(8,128)(2,1)}, u32[]{:S(2)}, u32[]{:S(2)}) collective-permute-start(bf16[16,80,512]{2,1,0:T(8,128)(2,1)} %collective-permute-done.17), channel_id=1, source_target_pairs={{0,48},{1,17},{2,50},{3,19},{4,52},{5,21},{6,54},{7,23},{8,56},{9,... | collective-permute-start | bytes 3932168 | tf_op jit(solution)/shard_map/ppermute | solution.py:31
  89.7 29.6 %collective-permute-start.21 = (bf16[16,80,512]{2,1,0:T(8,128)(2,1)}, bf16[16,80,512]{2,1,0:T(8,128)(2,1)}, u32[]{:S(2)}, u32[]{:S(2)}) collective-permute-start(bf16[16,80,512]{2,1,0:T(8,128)(2,1)} %collective-permute-done.20), channel_id=1, source_target_pairs={{0,72},{1,9},{2,74},{3,11},{4,76},{5,13},{6,78},{7,15},{8,64},{9,1... | collective-permute-start | bytes 3932168 | tf_op jit(solution)/shard_map/ppermute | solution.py:31
  97.5 1.6 copy-start
  99.0 1.4 copy-start.2
  125.3 11.9 %collective-permute-start.22 = (bf16[4,256,512]{2,1,0:T(8,128)(2,1)S(1)}, bf16[4,256,512]{2,1,0:T(8,128)(2,1)S(1)}, u32[]{:S(2)}, u32[]{:S(2)}) collective-permute-start(bf16[4,256,512]{2,1,0:T(8,128)(2,1)S(1)} %shard_map.50), channel_id=1, source_target_pairs={{0,1},{1,0},{2,3},{3,2},{4,5},{5,4},{6,7},{7,6},{8,9},{9,8},{10,11... | collective-permute-start | bytes 3145736 | tf_op jit(solution)/shard_map/ppermute | solution.py:31
  137.6 15.3 %collective-permute-start.23 = (bf16[256,512]{1,0:T(8,128)(2,1)S(1)}, bf16[256,512]{1,0:T(8,128)(2,1)S(1)}, u32[]{:S(2)}, u32[]{:S(2)}) collective-permute-start(bf16[256,512]{1,0:T(8,128)(2,1)S(1)} %get-tuple-element.17), channel_id=1, source_target_pairs={{0,0},{1,65},{2,2},{3,67},{4,4},{5,69},{6,6},{7,71},{8,8},{9,73},{... | collective-permute-start | bytes 786440 | tf_op jit(solution)/shard_map/ppermute | solution.py:31
  147.0 8.9 %collective-permute-start.24 = (bf16[256,512]{1,0:T(8,128)(2,1)S(1)}, bf16[256,512]{1,0:T(8,128)(2,1)S(1)}, u32[]{:S(2)}, u32[]{:S(2)}) collective-permute-start(bf16[256,512]{1,0:T(8,128)(2,1)S(1)} %get-tuple-element.20), channel_id=1, source_target_pairs={{0,16},{1,81},{2,18},{3,83},{4,20},{5,85},{6,22},{7,87},{8,24},{9,... | collective-permute-start | bytes 786440 | tf_op jit(solution)/shard_map/ppermute | solution.py:31
  147.1 12.0 %collective-permute-start.25 = (bf16[256,512]{1,0:T(8,128)(2,1)S(1)}, bf16[256,512]{1,0:T(8,128)(2,1)S(1)}, u32[]{:S(2)}, u32[]{:S(2)}) collective-permute-start(bf16[256,512]{1,0:T(8,128)(2,1)S(1)} %get-tuple-element.19), channel_id=1, source_target_pairs={{0,32},{1,97},{2,34},{3,99},{4,36},{5,101},{6,38},{7,103},{8,40},{... | collective-permute-start | bytes 786440 | tf_op jit(solution)/shard_map/ppermute | solution.py:31
  152.5 7.6 %collective-permute-start.26 = (bf16[256,512]{1,0:T(8,128)(2,1)S(1)}, bf16[256,512]{1,0:T(8,128)(2,1)S(1)}, u32[]{:S(2)}, u32[]{:S(2)}) collective-permute-start(bf16[256,512]{1,0:T(8,128)(2,1)S(1)} %get-tuple-element.18), channel_id=1, source_target_pairs={{0,48},{1,113},{2,50},{3,115},{4,52},{5,117},{6,54},{7,119},{8,56}... | collective-permute-start | bytes 786440 | tf_op jit(solution)/shard_map/ppermute | solution.py:31
  160.3 2.8 %copy-start.4 = (bf16[4,256,512]{2,1,0:T(8,128)(2,1)}, bf16[4,256,512]{2,1,0:T(8,128)(2,1)S(1)}, u32[]{:S(2)}) copy-start(bf16[4,256,512]{2,1,0:T(8,128)(2,1)S(1)} %pad_maximum_fusion.own) | copy-start | bytes 3145732
  160.3 2.7 %collective-permute-start.27 = (bf16[4,256,512]{2,1,0:T(8,128)(2,1)S(1)}, bf16[4,256,512]{2,1,0:T(8,128)(2,1)S(1)}, u32[]{:S(2)}, u32[]{:S(2)}) collective-permute-start(bf16[4,256,512]{2,1,0:T(8,128)(2,1)S(1)} %pad_maximum_fusion.own), channel_id=1, source_target_pairs={{0,1},{1,0},{2,3},{3,2},{4,5},{5,4},{6,7},{7,6},{8,9},{9,8},{10,11... | collective-permute-start | bytes 3145736 | tf_op jit(solution)/shard_map/ppermute | solution.py:31
  163.0 1.0 copy-start.5
  167.9 6.0 %collective-permute-start.28 = (bf16[256,512]{1,0:T(8,128)(2,1)S(1)}, bf16[256,512]{1,0:T(8,128)(2,1)S(1)}, u32[]{:S(2)}, u32[]{:S(2)}) collective-permute-start(bf16[256,512]{1,0:T(8,128)(2,1)S(1)} %get-tuple-element.13), channel_id=1, source_target_pairs={{0,0},{1,8},{2,2},{3,10},{4,4},{5,12},{6,6},{7,14},{8,9},{9,1},{10... | collective-permute-start | bytes 786440 | tf_op jit(solution)/shard_map/ppermute | solution.py:31
  169.9 15.5 %collective-permute-start.29 = (bf16[256,512]{1,0:T(8,128)(2,1)S(1)}, bf16[256,512]{1,0:T(8,128)(2,1)S(1)}, u32[]{:S(2)}, u32[]{:S(2)}) collective-permute-start(bf16[256,512]{1,0:T(8,128)(2,1)S(1)} %get-tuple-element.16), channel_id=1, source_target_pairs={{0,2},{1,10},{2,4},{3,12},{4,6},{5,14},{6,0},{7,8},{8,11},{9,3},{1... | collective-permute-start | bytes 786440 | tf_op jit(solution)/shard_map/ppermute | solution.py:31
  170.1 15.3 %collective-permute-start.30 = (bf16[256,512]{1,0:T(8,128)(2,1)S(1)}, bf16[256,512]{1,0:T(8,128)(2,1)S(1)}, u32[]{:S(2)}, u32[]{:S(2)}) collective-permute-start(bf16[256,512]{1,0:T(8,128)(2,1)S(1)} %get-tuple-element.15), channel_id=1, source_target_pairs={{0,4},{1,12},{2,6},{3,14},{4,0},{5,8},{6,2},{7,10},{8,13},{9,5},{1... | collective-permute-start | bytes 786440 | tf_op jit(solution)/shard_map/ppermute | solution.py:31
  172.1 16.1 %collective-permute-start.31 = (bf16[256,512]{1,0:T(8,128)(2,1)S(1)}, bf16[256,512]{1,0:T(8,128)(2,1)S(1)}, u32[]{:S(2)}, u32[]{:S(2)}) collective-permute-start(bf16[256,512]{1,0:T(8,128)(2,1)S(1)} %get-tuple-element.14), channel_id=1, source_target_pairs={{0,6},{1,14},{2,0},{3,8},{4,2},{5,10},{6,4},{7,12},{8,15},{9,7},{1... | collective-permute-start | bytes 786440 | tf_op jit(solution)/shard_map/ppermute | solution.py:31

commit v4 on v3

--- a/solution.py
+++ b/solution.py
@@ -45,11 +45,15 @@
     return permute(value, move)
 
 
-def gather_plane(block, order):
-    for axis in order[:2]:
+def gather_planes(blocks):
+    for level in range(2):
         for which in (1, 2):
-            block = jnp.concatenate([block, exchange(block, axis, which)], axis=0)
-    return block
+            blocks = {
+                part: jnp.concatenate([block, exchange(block, ORDER[part][level], which)], axis=0)
+                for part, block in blocks.items()
+            }
+            blocks = lax.optimization_barrier(blocks)
+    return blocks
 
 
 def gather_last(block, axis):
@@ -76,14 +80,17 @@
 
 
 def refit_kernel(table, master, out):
-    for r in range(master.shape[0] // BLOCK):
-        for c in range(master.shape[1] // BLOCK):
-            at = (pl.ds(r * BLOCK, BLOCK), pl.ds(c * BLOCK, BLOCK))
-            tile = master[at]
-            amax = jnp.max(jnp.max(jnp.abs(tile), axis=0, keepdims=True), axis=1, keepdims=True)
-            scale = ((amax + 1e-6) / 448.0).astype(jnp.bfloat16).astype(jnp.float32)
-            coded = (tile * (1.0 / scale)).astype(jnp.bfloat16)
-            out[at] = (coded.astype(jnp.float32) * scale).astype(jnp.bfloat16)
+    tiles = master.shape[0] // BLOCK
+    amax = jnp.max(jnp.abs(master[...]).reshape(tiles, BLOCK, COLS), axis=1)
+    for c in range(COLS // BLOCK):
+        cols = slice(c * BLOCK, (c + 1) * BLOCK)
+        top = jnp.max(amax[:, cols], axis=1, keepdims=True)
+        scales = ((top + 1e-6) / 448.0).astype(jnp.bfloat16).astype(jnp.float32)
+        inverses = 1.0 / scales
+        for r in range(tiles):
+            at = (slice(r * BLOCK, (r + 1) * BLOCK), cols)
+            coded = (master[at] * inverses[r : r + 1]).astype(jnp.bfloat16)
+            out[at] = (coded.astype(jnp.float32) * scales[r : r + 1]).astype(jnp.bfloat16)
 
 
 def refit(table, master, first):
@@ -97,6 +104,7 @@
             out_specs=pl.BlockSpec((SHARE, COLS), lambda i, t: (i, 0)),
         ),
         out_shape=jax.ShapeDtypeStruct((8 * SHARE, COLS), jnp.bfloat16),
+        compiler_params=pltpu.CompilerParams(vmem_limit_bytes=60 * MIB),
         cost_estimate=pl.CostEstimate(flops=size * 6, bytes_accessed=size * 6, transcendentals=0),
     )(table, master)
 
@@ -165,22 +173,30 @@
     near = jnp.where(half == 0, 0, 3)
     sources = ((near, 0), (1 if keep else 2, 1))
     zn, yn, xn = (PARTS[a][1] for a in "zyx")
-    pltpu.make_async_copy(early.at[half], total, sems.at[3]).start()
-    for i, (z_part, y_part, x_part) in enumerate(((z2, y2, x2), (z3, y3, x3))):
+
+    def start(src, dst, which):
+        pltpu.make_async_copy(src, dst, sems.at[which]).start()
+
+    def ready(held, which):
+        pltpu.make_async_copy(held, held, sems.at[which]).wait()
+
+    for i, part in enumerate((z2, z3)):
         for sx, el in sources:
-            cols = pl.ds(el * SHARE, SHARE)
-            pltpu.make_async_copy(z_part.at[:, sx], z_held.at[i, :, :, cols], sems.at[0]).start()
+            start(part.at[:, sx], z_held.at[i, :, :, pl.ds(el * SHARE, SHARE)], 0)
+    start(early.at[half], total, 1)
+    for i, part in enumerate((y2, y3)):
+        for sx, el in sources:
             for zs in range(4):
-                cols = pl.ds((el * 4 + zs) * SHARE, SHARE)
-                pltpu.make_async_copy(y_part.at[sx, zs], y_held.at[i, :, cols], sems.at[1]).start()
+                start(part.at[sx, zs], y_held.at[i, :, pl.ds((el * 4 + zs) * SHARE, SHARE)], 2)
+    for i, part in enumerate((x2, x3)):
         for zs in range(4):
-            cols = pl.ds(zs * SHARE, SHARE)
-            pltpu.make_async_copy(x_part.at[zs], x_held.at[i, :, :, cols], sems.at[2]).start()
-    for which, held in enumerate((z_held, y_held, x_held, total)):
-        pltpu.make_async_copy(held, held, sems.at[which]).wait()
+            start(part.at[zs], x_held.at[i, :, :, pl.ds(zs * SHARE, SHARE)], 3)
 
     z_rows, y_rows, x_rows = rows_of("z"), rows_of("y"), rows_of("x")
-    for weight, cols in zip((mine, theirs), column_slices(core)):
+    weights = list(zip((mine, theirs), column_slices(core)))
+    ready(z_held, 0)
+    ready(total, 1)
+    for weight, cols in weights:
         got = None
         for i in range(2):
             acts = z_held[i].reshape(4 * zn, 2 * SHARE)
@@ -188,8 +204,12 @@
             term += dot(acts[:, SHARE:], weight[pl.ds((6 + i) * SHARE, SHARE), :])
             got = term if got is None else got + term
         total[:, z_rows, cols] += got.reshape(4, zn, COLS)
+    ready(y_held, 2)
+    for weight, cols in weights:
         acts = y_held[...].reshape(2 * yn, 8 * SHARE)
         total[2:4, y_rows, cols] = dot(acts, weight[...]).reshape(2, yn, COLS)
+    ready(x_held, 3)
+    for weight, cols in weights:
 
         def add(i, el):
             acts = x_held[i].reshape(4 * xn, 4 * SHARE)
@@ -223,8 +243,9 @@
     )(table, *weights, *parts)
 
 
-def spread_kernel(table, owner, own, other, out):
-    for k in range(4):
+def spread_kernel(table, owner, own, other, *refs):
+    outs, sems = refs[:4], refs[4]
+    for k, out in enumerate(outs):
         section = owner[table[DEST + k]]
         half = jnp.where(section >= 4, 1, 0)
         far = jnp.where(half == table[XH], 0, 1)
@@ -232,25 +253,35 @@
 
         @pl.when(far == table[CORE])
         def _():
-            out[k] = own[at]
+            pltpu.make_async_copy(own.at[at], out, sems.at[k]).start()
 
         @pl.when(far != table[CORE])
         def _():
-            out[k] = other[at]
-
-
-def arrange_kernel(table, parts, out):
-    for k in range(4):
-        out[:, k * 2 * COLS : (k + 1) * 2 * COLS] = parts[(table[Z] + 4 - k) & 3]
-
-
-def small_call(kernel, scalars, parts, shape):
-    smem, vmem = pl.BlockSpec(memory_space=pltpu.SMEM), pl.BlockSpec(memory_space=pltpu.VMEM)
+            pltpu.make_async_copy(other.at[at], out, sems.at[k]).start()
+
+    for k, out in enumerate(outs):
+        pltpu.make_async_copy(out, out, sems.at[k]).wait()
+
+
+def arrange_kernel(table, *refs):
+    parts, out, sems = refs[:4], refs[4], refs[5]
+    copies = []
+    for dz, part in enumerate(parts):
+        at = pl.multiple_of(((table[Z] + 4 - dz) & 3) * (2 * COLS), 2 * COLS)
+        copies.append(pltpu.make_async_copy(part, out.at[:, pl.ds(at, 2 * COLS)], sems.at[dz]))
+        copies[-1].start()
+    for copy in copies:
+        copy.wait()
+
+
+def small_call(kernel, scalars, parts, shapes):
+    smem, anywhere = pl.BlockSpec(memory_space=pltpu.SMEM), pl.BlockSpec(memory_space=pl.ANY)
     return pl.pallas_call(
         kernel,
-        in_specs=[smem] * len(scalars) + [vmem] * len(parts),
-        out_specs=vmem,
-        out_shape=jax.ShapeDtypeStruct(shape, jnp.bfloat16),
+        in_specs=[smem] * len(scalars) + [anywhere] * len(parts),
+        out_specs=[anywhere] * len(shapes),
+        out_shape=[jax.ShapeDtypeStruct(shape, jnp.bfloat16) for shape in shapes],
+        scratch_shapes=[pltpu.SemaphoreType.DMA((4,))],
         cost_estimate=pl.CostEstimate(flops=0, bytes_accessed=2 * MIB, transcendentals=0),
     )(*scalars, *parts)
 
@@ -265,15 +296,11 @@
     me = lax.axis_index("group") * 16 + lax.axis_index("tp")
     table = lax.dynamic_index_in_dim(rows, me, 0, keepdims=False)
 
-    planes = {}
-    for axis in "zyx":
-        at, count = PARTS[axis]
-        planes[axis] = gather_plane(activations[None, at : at + count], ORDER[axis])
-    late_table, *held = lax.optimization_barrier((table, *planes.values()))
-    blocks = {axis: gather_last(v, axis) for axis, v in zip("zyx", held)}
-
-    theirs = permute(refit(late_table, master, THEIRS), other_core)
-    mine = refit(late_table, master, MINE)
+    planes = gather_planes({part: activations[None, at : at + n] for part, (at, n) in PARTS.items()})
+    blocks = {axis: gather_last(planes[axis], axis) for axis in "zyx"}
+
+    theirs = permute(refit(table, master, THEIRS), other_core)
+    mine = refit(table, master, MINE)
     weights = [mine, theirs]
 
     zn, yn, xn = (PARTS[a][1] for a in "zyx")
@@ -319,11 +346,11 @@
     own = jnp.stack([got[dy] for dy in range(4)])
     other = permute(own, other_core)
 
-    picked = small_call(spread_kernel, [table, owner], [own, other], (4, 256, 2 * COLS))
+    picked = small_call(spread_kernel, [table, owner], [own, other], [(256, 2 * COLS)] * 4)
     got = {}
     for dz in (2, 1, 3, 0):
         got[dz] = permute(picked[dz], lambda x, y, z, c: linear(x ^ c, y, z + dz, x % 2))
-    return small_call(arrange_kernel, [table], [jnp.stack([got[dz] for dz in range(4)])], (256, 8 * COLS))
+    return small_call(arrange_kernel, [table], [got[dz] for dz in range(4)], [(256, 8 * COLS)])[0]
 
 
 def solution(mesh):

time: 194 us -> 246 us (1.27)
  Pallas kernels: 38.7 us -> 99.3 us
  local copies, waits for them, and re-layouts: 18.1 us -> 8.88 us
  starting transfers between devices: 58.4 us -> 50 us
  other arithmetic: 1.98 us -> 7.16 us
  waiting for transfers between devices: 74.1 us -> 77.7 us
    pallas_call x2, Pallas kernels: 4.95 us -> 67.1 us  [small_call(): pl.pallas_call(kernel, in_specs=[smem] * len(scalars) + [anywhere] * len(...]
    ppermute x32, starting transfers between devices: 58.4 us -> 50 us  [permute(): lax.ppermute(value, AXES, [(i, move(*coords(i))) for i in range(N_DEV)])]
    concatenate x9 -> x12, other arithmetic: 0.38 us -> 6.68 us  [gather_planes(): jnp.concatenate([block, exchange(block, ORDER[part][level], which)], axis=0)]
    unnamed x23 -> x28, local copies, waits for them, and re-layouts: 11.8 us -> 5.72 us
    ppermute x32, waiting for transfers between devices: 74.1 us -> 77.7 us  [permute(): lax.ppermute(value, AXES, [(i, move(*coords(i))) for i in range(N_DEV)])]
  transfers between devices with their start and end apart: 32 -> 32, of which waited for: 15 -> 16; matrix products, arithmetic and copies ran while one was open for 6% -> 4% of each run, Pallas kernels for 11% -> 11%
where the time goes in v4:
time: 246 us; the launch traced here: 244 us
  Pallas kernels  99.3 us (40%)
  waiting for transfers between devices  77.7 us (32%)
  starting transfers between devices  50 us (20%)
  local copies, waits for them, and re-layouts  8.88 us (4%)
  other arithmetic  7.16 us (3%)
    ppermute x32, waiting for transfers between devices, permute(): lax.ppermute(value, AXES, [(i, move(*coords(i))) for i in range(N_DEV)])  77.7 us
    pallas_call x2, Pallas kernels, small_call(): pl.pallas_call(kernel, in_specs=[smem] * len(scalars) + [anywhere] * len(...  67.1 us
    ppermute x32, starting transfers between devices, permute(): lax.ppermute(value, AXES, [(i, move(*coords(i))) for i in range(N_DEV)])  50 us
    pallas_call x3, Pallas kernels, product(): pl.pallas_call(kernel, in_specs=[pl.BlockSpec(memory_space=pltpu.SMEM)] +...  17.3 us
    pallas_call x2, Pallas kernels, refit(): pl.pallas_call(refit_kernel, grid_spec=pltpu.PrefetchScalarGridSpec(num_s...  14.9 us
    concatenate x12, other arithmetic, gather_planes(): jnp.concatenate([block, exchange(block, ORDER[part][level], which)], axis=0)  6.68 us
    unnamed x28, local copies, waits for them, and re-layouts  5.72 us
  transfers between devices with their start and end apart: 32, of which 16 were waited for; matrix products, arithmetic and copies ran while one was open for 4% of the time, Pallas kernels for 11%

profile of v4, /device:TPU:3, one launch (start us, length us, event | category | flops | bytes accessed | tf_op | source)
XLA Modules:
  0.0 243.6 jit_solution(10263540939560010043)
XLA Ops:
  0.0 0.9 slice_bitcast_fusion.5
  0.9 2.8 %collective-permute-start.1 = (bf16[1,80,512]{2,1,0:T(8,128)(2,1)S(1)}, bf16[1,80,512]{2,1,0:T(8,128)(2,1)S(1)}, u32[]{:S(2)}, u32[]{:S(2)}) collective-permute-start(bf16[1,80,512]{2,1,0:T(8,128)(2,1)S(1)} %get-tuple-element.42), channel_id=1, source_target_pairs={{0,16},{1,49},{2,18},{3,51},{4,20},{5,53},{6,22},{7,55},{8,24},{9,... | collective-permute-start | bytes 245768 | tf_op jit(solution)/shard_map/ppermute | solution.py:31
  3.8 3.8 %collective-permute-start.2 = (bf16[1,80,512]{2,1,0:T(8,128)(2,1)S(1)}, bf16[1,80,512]{2,1,0:T(8,128)(2,1)S(1)}, u32[]{:S(2)}, u32[]{:S(2)}) collective-permute-start(bf16[1,80,512]{2,1,0:T(8,128)(2,1)S(1)} %get-tuple-element.41), channel_id=1, source_target_pairs={{0,2},{1,7},{2,0},{3,5},{4,6},{5,3},{6,4},{7,1},{8,10},{9,15},{10,... | collective-permute-start | bytes 245768 | tf_op jit(solution)/shard_map/ppermute | solution.py:31
  7.5 0.9 slice_bitcast_fusion.4
  8.4 1.2 collective-permute-start.3
  9.7 2.2 collective-permute-done.3
  11.9 0.1 collective-permute-start.4
  12.0 0.1 collective-permute-start.5
  12.1 1.5 collective-permute-start.6
  13.6 2.8 %collective-permute-done.4 = bf16[2,80,512]{2,1,0:T(8,128)(2,1)S(1)} collective-permute-done((bf16[2,80,512]{2,1,0:T(8,128)(2,1)S(1)}, bf16[2,80,512]{2,1,0:T(8,128)(2,1)S(1)}, u32[]{:S(2)}, u32[]{:S(2)}) %collective-permute-start.4) | collective-permute-done | bytes 163872 | tf_op jit(solution)/shard_map/ppermute | solution.py:31
  16.6 0.4 collective-permute-done.6
  17.0 2.0 collective-permute-start.8
  19.0 0.4 collective-permute-start.9
  19.4 4.6 %collective-permute-done.8 = bf16[4,80,512]{2,1,0:T(8,128)(2,1)S(1)} collective-permute-done((bf16[4,80,512]{2,1,0:T(8,128)(2,1)S(1)}, bf16[4,80,512]{2,1,0:T(8,128)(2,1)S(1)}, u32[]{:S(2)}, u32[]{:S(2)}) %collective-permute-start.8) | collective-permute-done | bytes 327712 | tf_op jit(solution)/shard_map/ppermute | solution.py:31
  24.1 2.1 collective-permute-done.7
  26.1 0.9 pad_maximum_fusion.5
  27.0 0.1 pad_maximum_fusion.4
  27.1 2.1 collective-permute-start.11
  29.2 0.9 collective-permute-start.10
  30.1 0.6 collective-permute-start.12
  30.8 1.3 dynamic-slice_bitcast_fusion.table
  32.0 7.5 %shard_map.47 = bf16[4096,256]{1,0:T(8,128)(2,1)} custom-call(s32[28]{0:T(128)} %dynamic-slice_bitcast_fusion.table, f32[8192,256]{1,0:T(8,128)} %master.3), custom_call_target="tpu_custom_call" | custom-call | flops 6291456 | bytes 6291456 | tf_op jit(solution)/shard_map/pallas_call | solution.py:98
  39.5 5.3 %collective-permute-start = (bf16[4096,256]{1,0:T(8,128)(2,1)}, bf16[4096,256]{1,0:T(8,128)(2,1)S(1)}, u32[]{:S(2)}, u32[]{:S(2)}) collective-permute-start(bf16[4096,256]{1,0:T(8,128)(2,1)} %shard_map.47), channel_id=1, source_target_pairs={{0,1},{1,0},{2,3},{3,2},{4,5},{5,4},{6,7},{7,6},{8,9},{9,8},{10,11... | collective-permute-start | bytes 6291464 | tf_op jit(solution)/shard_map/ppermute | solution.py:31
  44.8 1.2 pad_maximum_fusion.2
  46.1 3.0 %pad_maximum_fusion.1 = bf16[16,80,512]{2,1,0:T(8,128)(2,1)} fusion(bf16[8,80,512]{2,1,0:T(8,128)(2,1)} %collective-permute-done.10, bf16[8,80,512]{2,1,0:T(8,128)(2,1)} %pad_maximum_fusion.5), kind=kLoop, calls=%fused_computation.2 | loop fusion | flops 655360 | bytes 2621440 | tf_op jit(solution)/shard_map/concatenate | solution.py:52
  49.1 1.3 pad_maximum_fusion
  50.4 3.0 %collective-permute-start.14 = (bf16[16,96,512]{2,1,0:T(8,128)(2,1)S(1)}, bf16[16,96,512]{2,1,0:T(8,128)(2,1)}, u32[]{:S(2)}, u32[]{:S(2)}) collective-permute-start(bf16[16,96,512]{2,1,0:T(8,128)(2,1)S(1)} %pad_maximum_fusion), channel_id=1, source_target_pairs={{0,2},{1,7},{2,0},{3,5},{4,6},{5,3},{6,4},{7,1},{8,10},{9,15},{10,... | collective-permute-start | bytes 4718600 | tf_op jit(solution)/shard_map/ppermute | solution.py:31
  53.4 1.8 collective-permute-start.17
  55.2 0.1 collective-permute-start.13
  55.3 29.2 %collective-permute-done.14 = bf16[16,96,512]{2,1,0:T(8,128)(2,1)} collective-permute-done((bf16[16,96,512]{2,1,0:T(8,128)(2,1)S(1)}, bf16[16,96,512]{2,1,0:T(8,128)(2,1)}, u32[]{:S(2)}, u32[]{:S(2)}) %collective-permute-start.14) | collective-permute-done | bytes 1572896 | tf_op jit(solution)/shard_map/ppermute | solution.py:31
  84.5 0.2 collective-permute-start.15
  84.7 0.4 collective-permute-done.17
  85.1 1.1 copy-done.3
  86.2 1.5 collective-permute-start.21
  87.6 7.5 %shard_map.46.mine = bf16[4096,256]{1,0:T(8,128)(2,1)} custom-call(s32[28]{0:T(128)} %dynamic-slice_bitcast_fusion.table, f32[8192,256]{1,0:T(8,128)} %master.3), custom_call_target="tpu_custom_call" | custom-call | flops 6291456 | bytes 6291456 | tf_op jit(solution)/shard_map/pallas_call | solution.py:98
  95.1 1.6 copy-done
  96.7 1.3 copy-done.2
  98.0 6.9 %shard_map.48.early = f32[2,4,256,512]{3,2,1,0:T(8,128)S(1)} custom-call(s32[28]{0:T(128)S(1)} %copy-done.5, bf16[4096,256]{1,0:T(8,128)(2,1)S(1)} %copy-done, bf16[4096,256]{1,0:T(8,128)(2,1)S(1)} %collective-permute-done.theirs, bf16[4,4,96,512]{3,2,1,0:T(8,128)(2,1)S(1)} %bitcast.32, bf16[4,4,96,512]{3,2,1,0:T(8,128)(2,1)} %bitcast.11.z1, ...), custom_call_target="tpu_custom_call" | custom-call | flops 4294967296 | bytes 14680064 | tf_op jit(solution)/shard_map/pallas_call | solution.py:233
  105.0 11.2 %collective-permute-done.21 = bf16[16,80,512]{2,1,0:T(8,128)(2,1)} collective-permute-done((bf16[16,80,512]{2,1,0:T(8,128)(2,1)}, bf16[16,80,512]{2,1,0:T(8,128)(2,1)}, u32[]{:S(2)}, u32[]{:S(2)}) %collective-permute-start.21) | collective-permute-done | bytes 1310752 | tf_op jit(solution)/shard_map/ppermute | solution.py:31
  116.2 5.6 %shard_map.50 = bf16[4,256,512]{2,1,0:T(8,128)(2,1)S(1)} custom-call(s32[28]{0:T(128)S(1)} %copy-done.5, bf16[4096,256]{1,0:T(8,128)(2,1)S(1)} %copy-done, bf16[4096,256]{1,0:T(8,128)(2,1)S(1)} %collective-permute-done.theirs, bf16[4,4,96,512]{3,2,1,0:T(8,128)(2,1)} %bitcast.4.z2, bf16[4,4,96,512]{3,2,1,0:T(8,128)(2,1)} %bitcast.5.z3, ...), custom_call_target="tpu_custom_call" | custom-call | flops 4294967296 | bytes 14680064 | tf_op jit(solution)/shard_map/pallas_call | solution.py:233
  121.8 6.3 %collective-permute-start.22 = (bf16[4,256,512]{2,1,0:T(8,128)(2,1)S(1)}, bf16[4,256,512]{2,1,0:T(8,128)(2,1)S(1)}, u32[]{:S(2)}, u32[]{:S(2)}) collective-permute-start(bf16[4,256,512]{2,1,0:T(8,128)(2,1)S(1)} %shard_map.50), channel_id=1, source_target_pairs={{0,1},{1,0},{2,3},{3,2},{4,5},{5,4},{6,7},{7,6},{8,9},{9,8},{10,11... | collective-permute-start | bytes 3145736 | tf_op jit(solution)/shard_map/ppermute | solution.py:31
  128.1 4.8 %shard_map.49 = f32[4,256,512]{2,1,0:T(8,128)S(1)} custom-call(s32[28]{0:T(128)S(1)} %copy-done.5, bf16[4096,256]{1,0:T(8,128)(2,1)S(1)} %copy-done, bf16[4096,256]{1,0:T(8,128)(2,1)S(1)} %collective-permute-done.theirs, bf16[4,4,96,512]{3,2,1,0:T(8,128)(2,1)} %bitcast.4.z2, bf16[4,4,96,512]{3,2,1,0:T(8,128)(2,1)} %bitcast.5.z3, ...), custom_call_target="tpu_custom_call" | custom-call | flops 4294967296 | bytes 14680064 | tf_op jit(solution)/shard_map/pallas_call | solution.py:233
  132.9 0.3 add_convert_fusion
  133.3 0.1 slice_bitcast_fusion.3
  133.4 1.9 collective-permute-start.23
  135.3 0.1 collective-permute-start.24
  135.4 6.4 %collective-permute-start.25 = (bf16[256,512]{1,0:T(8,128)(2,1)S(1)}, bf16[256,512]{1,0:T(8,128)(2,1)S(1)}, u32[]{:S(2)}, u32[]{:S(2)}) collective-permute-start(bf16[256,512]{1,0:T(8,128)(2,1)S(1)} %get-tuple-element.39), channel_id=1, source_target_pairs={{0,32},{1,97},{2,34},{3,99},{4,36},{5,101},{6,38},{7,103},{8,40},{... | collective-permute-start | bytes 786440 | tf_op jit(solution)/shard_map/ppermute | solution.py:31
  141.7 0.5 collective-permute-done.23
  142.3 6.8 %collective-permute-done.24 = bf16[256,512]{1,0:T(8,128)(2,1)S(1)} collective-permute-done((bf16[256,512]{1,0:T(8,128)(2,1)S(1)}, bf16[256,512]{1,0:T(8,128)(2,1)S(1)}, u32[]{:S(2)}, u32[]{:S(2)}) %collective-permute-start.24) | collective-permute-done | bytes 262176 | tf_op jit(solution)/shard_map/ppermute | solution.py:31
  149.1 1.0 collective-permute-done.25
  150.1 0.4 collective-permute-done.26
  150.5 0.1 pad_maximum_fusion.3.own
  150.7 1.8 collective-permute-start.27
  152.5 2.3 collective-permute-done.27.other
  154.8 1.0 copy-done.9
  155.8 33.6 %shard_map.51 = (bf16[256,512]{1,0:T(8,128)(2,1)}, bf16[256,512]{1,0:T(8,128)(2,1)}, bf16[256,512]{1,0:T(8,128)(2,1)}, bf16[256,512]{1,0:T(8,128)(2,1)}) custom-call(s32[28]{0:T(128)} %dynamic-slice_bitcast_fusion.table, s32[8]{0:T(128)} %owner.1, bf16[4,256,512]{2,1,0:T(8,128)(2,1)} %copy-done.6, bf16[4,256,512]{2,1,0:T(8,128)(2,1)} %copy-done.9), custom_call_target="tpu_custom_call" | custom-call | bytes 2097152 | tf_op jit(solution)/shard_map/pallas_call | solution.py:279
  189.4 1.9 collective-permute-start.28
  191.3 1.0 collective-permute-start.29
  192.3 1.3 collective-permute-start.30
  193.6 1.8 collective-permute-start.31
  195.4 11.7 %collective-permute-done.29.refs_1_ = bf16[256,512]{1,0:T(8,128)(2,1)S(1)} collective-permute-done((bf16[256,512]{1,0:T(8,128)(2,1)}, bf16[256,512]{1,0:T(8,128)(2,1)S(1)}, u32[]{:S(2)}, u32[]{:S(2)}) %collective-permute-start.29) | collective-permute-done | bytes 262176 | tf_op jit(solution)/shard_map/ppermute | solution.py:31
  207.1 2.0 collective-permute-done.31.refs_3_
  209.1 0.7 copy-done.13
  209.8 33.6 %shard_map.52 = bf16[256,2048]{1,0:T(8,128)(2,1)} custom-call(s32[28]{0:T(128)} %dynamic-slice_bitcast_fusion.table, bf16[256,512]{1,0:T(8,128)(2,1)} %copy-done.10, bf16[256,512]{1,0:T(8,128)(2,1)} %copy-done.11, bf16[256,512]{1,0:T(8,128)(2,1)} %copy-done.12, bf16[256,512]{1,0:T(8,128)(2,1)} %copy-done.13), custom_call_target="tpu_custom_call" | custom-call | bytes 2097152 | tf_op jit(solution)/shard_map/pallas_call | solution.py:279
  (53 shorter events, 0.4 us)
Async XLA Ops:
  0.9 8.7 %collective-permute-start.1 = (bf16[1,80,512]{2,1,0:T(8,128)(2,1)S(1)}, bf16[1,80,512]{2,1,0:T(8,128)(2,1)S(1)}, u32[]{:S(2)}, u32[]{:S(2)}) collective-permute-start(bf16[1,80,512]{2,1,0:T(8,128)(2,1)S(1)} %get-tuple-element.42), channel_id=1, source_target_pairs={{0,16},{1,49},{2,18},{3,51},{4,20},{5,53},{6,22},{7,55},{8,24},{9,... | collective-permute-start | bytes 245768 | tf_op jit(solution)/shard_map/ppermute | solution.py:31
  3.8 5.9 %collective-permute-start.2 = (bf16[1,80,512]{2,1,0:T(8,128)(2,1)S(1)}, bf16[1,80,512]{2,1,0:T(8,128)(2,1)S(1)}, u32[]{:S(2)}, u32[]{:S(2)}) collective-permute-start(bf16[1,80,512]{2,1,0:T(8,128)(2,1)S(1)} %get-tuple-element.41), channel_id=1, source_target_pairs={{0,2},{1,7},{2,0},{3,5},{4,6},{5,3},{6,4},{7,1},{8,10},{9,15},{10,... | collective-permute-start | bytes 245768 | tf_op jit(solution)/shard_map/ppermute | solution.py:31
  8.4 3.5 %collective-permute-start.3 = (bf16[1,96,512]{2,1,0:T(8,128)(2,1)S(1)}, bf16[1,96,512]{2,1,0:T(8,128)(2,1)S(1)}, u32[]{:S(2)}, u32[]{:S(2)}) collective-permute-start(bf16[1,96,512]{2,1,0:T(8,128)(2,1)S(1)} %slice_bitcast_fusion.4), channel_id=1, source_target_pairs={{0,8},{1,73},{2,10},{3,75},{4,12},{5,77},{6,14},{7,79},{8,0},{9,65... | collective-permute-start | bytes 294920 | tf_op jit(solution)/shard_map/ppermute | solution.py:31
  11.9 4.5 %collective-permute-start.4 = (bf16[2,80,512]{2,1,0:T(8,128)(2,1)S(1)}, bf16[2,80,512]{2,1,0:T(8,128)(2,1)S(1)}, u32[]{:S(2)}, u32[]{:S(2)}) collective-permute-start(bf16[2,80,512]{2,1,0:T(8,128)(2,1)S(1)} %pad_maximum_fusion.11), channel_id=1, source_target_pairs={{0,48},{1,17},{2,50},{3,19},{4,52},{5,21},{6,54},{7,23},{8,56},{9,... | collective-permute-start | bytes 491528 | tf_op jit(solution)/shard_map/ppermute | solution.py:31
  12.0 4.5 %collective-permute-start.5 = (bf16[2,80,512]{2,1,0:T(8,128)(2,1)S(1)}, bf16[2,80,512]{2,1,0:T(8,128)(2,1)S(1)}, u32[]{:S(2)}, u32[]{:S(2)}) collective-permute-start(bf16[2,80,512]{2,1,0:T(8,128)(2,1)S(1)} %pad_maximum_fusion.12), channel_id=1, source_target_pairs={{0,6},{1,3},{2,4},{3,1},{4,2},{5,7},{6,0},{7,5},{8,14},{9,11},{10,... | collective-permute-start | bytes 491528 | tf_op jit(solution)/shard_map/ppermute | solution.py:31
  12.1 4.9 %collective-permute-start.6 = (bf16[2,96,512]{2,1,0:T(8,128)(2,1)S(1)}, bf16[2,96,512]{2,1,0:T(8,128)(2,1)S(1)}, u32[]{:S(2)}, u32[]{:S(2)}) collective-permute-start(bf16[2,96,512]{2,1,0:T(8,128)(2,1)S(1)} %pad_maximum_fusion.10), channel_id=1, source_target_pairs={{0,72},{1,9},{2,74},{3,11},{4,76},{5,13},{6,78},{7,15},{8,64},{9,1... | collective-permute-start | bytes 589832 | tf_op jit(solution)/shard_map/ppermute | solution.py:31
  17.0 7.0 %collective-permute-start.8 = (bf16[4,80,512]{2,1,0:T(8,128)(2,1)S(1)}, bf16[4,80,512]{2,1,0:T(8,128)(2,1)S(1)}, u32[]{:S(2)}, u32[]{:S(2)}) collective-permute-start(bf16[4,80,512]{2,1,0:T(8,128)(2,1)S(1)} %pad_maximum_fusion.9), channel_id=1, source_target_pairs={{0,8},{1,73},{2,10},{3,75},{4,12},{5,77},{6,14},{7,79},{8,0},{9,65... | collective-permute-start | bytes 983048 | tf_op jit(solution)/shard_map/ppermute | solution.py:31
  19.0 7.1 %collective-permute-start.7 = (bf16[4,80,512]{2,1,0:T(8,128)(2,1)S(1)}, bf16[4,80,512]{2,1,0:T(8,128)(2,1)S(1)}, u32[]{:S(2)}, u32[]{:S(2)}) collective-permute-start(bf16[4,80,512]{2,1,0:T(8,128)(2,1)S(1)} %pad_maximum_fusion.8), channel_id=1, source_target_pairs={{0,2},{1,7},{2,0},{3,5},{4,6},{5,3},{6,4},{7,1},{8,10},{9,15},{10,... | collective-permute-start | bytes 983048 | tf_op jit(solution)/shard_map/ppermute | solution.py:31
  19.0 8.0 %collective-permute-start.9 = (bf16[4,96,512]{2,1,0:T(8,128)(2,1)S(1)}, bf16[4,96,512]{2,1,0:T(8,128)(2,1)S(1)}, u32[]{:S(2)}, u32[]{:S(2)}) collective-permute-start(bf16[4,96,512]{2,1,0:T(8,128)(2,1)S(1)} %pad_maximum_fusion.7), channel_id=1, source_target_pairs={{0,16},{1,49},{2,18},{3,51},{4,20},{5,53},{6,22},{7,55},{8,24},{9,... | collective-permute-start | bytes 1179656 | tf_op jit(solution)/shard_map/ppermute | solution.py:31
  27.1 12.4 %copy-start.7 = (bf16[8,96,512]{2,1,0:T(8,128)(2,1)}, bf16[8,96,512]{2,1,0:T(8,128)(2,1)S(1)}, u32[]{:S(2)}) copy-start(bf16[8,96,512]{2,1,0:T(8,128)(2,1)S(1)} %pad_maximum_fusion.4) | copy-start | bytes 2359300
  27.1 17.7 %collective-permute-start.11 = (bf16[8,80,512]{2,1,0:T(8,128)(2,1)S(1)}, bf16[8,80,512]{2,1,0:T(8,128)(2,1)}, u32[]{:S(2)}, u32[]{:S(2)}) collective-permute-start(bf16[8,80,512]{2,1,0:T(8,128)(2,1)S(1)} %pad_maximum_fusion.6), channel_id=1, source_target_pairs={{0,72},{1,9},{2,74},{3,11},{4,76},{5,13},{6,78},{7,15},{8,64},{9,1... | collective-permute-start | bytes 1966088 | tf_op jit(solution)/shard_map/ppermute | solution.py:31
  29.2 16.8 %collective-permute-start.10 = (bf16[8,80,512]{2,1,0:T(8,128)(2,1)}, bf16[8,80,512]{2,1,0:T(8,128)(2,1)}, u32[]{:S(2)}, u32[]{:S(2)}) collective-permute-start(bf16[8,80,512]{2,1,0:T(8,128)(2,1)} %pad_maximum_fusion.5), channel_id=1, source_target_pairs={{0,6},{1,3},{2,4},{3,1},{4,2},{5,7},{6,0},{7,5},{8,14},{9,11},{10,... | collective-permute-start | bytes 1966088 | tf_op jit(solution)/shard_map/ppermute | solution.py:31
  30.1 19.0 %collective-permute-start.12 = (bf16[8,96,512]{2,1,0:T(8,128)(2,1)S(1)}, bf16[8,96,512]{2,1,0:T(8,128)(2,1)}, u32[]{:S(2)}, u32[]{:S(2)}) collective-permute-start(bf16[8,96,512]{2,1,0:T(8,128)(2,1)S(1)} %pad_maximum_fusion.4), channel_id=1, source_target_pairs={{0,48},{1,17},{2,50},{3,19},{4,52},{5,21},{6,54},{7,23},{8,56},{9,... | collective-permute-start | bytes 2359304 | tf_op jit(solution)/shard_map/ppermute | solution.py:31
  39.5 15.7 %collective-permute-start = (bf16[4096,256]{1,0:T(8,128)(2,1)}, bf16[4096,256]{1,0:T(8,128)(2,1)S(1)}, u32[]{:S(2)}, u32[]{:S(2)}) collective-permute-start(bf16[4096,256]{1,0:T(8,128)(2,1)} %shard_map.47), channel_id=1, source_target_pairs={{0,1},{1,0},{2,3},{3,2},{4,5},{5,4},{6,7},{7,6},{8,9},{9,8},{10,11... | collective-permute-start | bytes 6291464 | tf_op jit(solution)/shard_map/ppermute | solution.py:31
  46.0 9.2 %copy-start.1 = (bf16[16,80,512]{2,1,0:T(8,128)(2,1)}, bf16[16,80,512]{2,1,0:T(8,128)(2,1)S(1)}, u32[]{:S(2)}) copy-start(bf16[16,80,512]{2,1,0:T(8,128)(2,1)S(1)} %pad_maximum_fusion.2) | copy-start | bytes 3932164
  46.0 3.1 %copy-start.8 = (bf16[8,96,512]{2,1,0:T(8,128)(2,1)S(1)}, bf16[8,96,512]{2,1,0:T(8,128)(2,1)}, u32[]{:S(2)}) copy-start(bf16[8,96,512]{2,1,0:T(8,128)(2,1)} %copy-done.7) | copy-start | bytes 2359300
  50.4 44.7 %copy-start.5 = (s32[28]{0:T(128)S(1)}, s32[28]{0:T(128)}, u32[]{:S(2)}) copy-start(s32[28]{0:T(128)} %dynamic-slice_bitcast_fusion.table) | copy-start | bytes 340
  50.4 34.1 %collective-permute-start.14 = (bf16[16,96,512]{2,1,0:T(8,128)(2,1)S(1)}, bf16[16,96,512]{2,1,0:T(8,128)(2,1)}, u32[]{:S(2)}, u32[]{:S(2)}) collective-permute-start(bf16[16,96,512]{2,1,0:T(8,128)(2,1)S(1)} %pad_maximum_fusion), channel_id=1, source_target_pairs={{0,2},{1,7},{2,0},{3,5},{4,6},{5,3},{6,4},{7,1},{8,10},{9,15},{10,... | collective-permute-start | bytes 4718600 | tf_op jit(solution)/shard_map/ppermute | solution.py:31
  53.4 31.7 %collective-permute-start.17 = (bf16[16,80,512]{2,1,0:T(8,128)(2,1)S(1)}, bf16[16,80,512]{2,1,0:T(8,128)(2,1)}, u32[]{:S(2)}, u32[]{:S(2)}) collective-permute-start(bf16[16,80,512]{2,1,0:T(8,128)(2,1)S(1)} %pad_maximum_fusion.2), channel_id=1, source_target_pairs={{0,16},{1,49},{2,18},{3,51},{4,20},{5,53},{6,22},{7,55},{8,24},{9,... | collective-permute-start | bytes 3932168 | tf_op jit(solution)/shard_map/ppermute | solution.py:31
  55.2 29.9 %collective-permute-start.20 = (bf16[16,80,512]{2,1,0:T(8,128)(2,1)}, bf16[16,80,512]{2,1,0:T(8,128)(2,1)}, u32[]{:S(2)}, u32[]{:S(2)}) collective-permute-start(bf16[16,80,512]{2,1,0:T(8,128)(2,1)} %pad_maximum_fusion.1), channel_id=1, source_target_pairs={{0,8},{1,73},{2,10},{3,75},{4,12},{5,77},{6,14},{7,79},{8,0},{9,65... | collective-permute-start | bytes 3932168 | tf_op jit(solution)/shard_map/ppermute | solution.py:31
  55.2 29.9 %collective-permute-start.16 = (bf16[16,80,512]{2,1,0:T(8,128)(2,1)S(1)}, bf16[16,80,512]{2,1,0:T(8,128)(2,1)S(1)}, u32[]{:S(2)}, u32[]{:S(2)}) collective-permute-start(bf16[16,80,512]{2,1,0:T(8,128)(2,1)S(1)} %pad_maximum_fusion.2), channel_id=1, source_target_pairs={{0,48},{1,17},{2,50},{3,19},{4,52},{5,21},{6,54},{7,23},{8,56},{9,... | collective-permute-start | bytes 3932168 | tf_op jit(solution)/shard_map/ppermute | solution.py:31
  55.2 49.7 %collective-permute-start.13 = (bf16[16,96,512]{2,1,0:T(8,128)(2,1)S(1)}, bf16[16,96,512]{2,1,0:T(8,128)(2,1)}, u32[]{:S(2)}, u32[]{:S(2)}) collective-permute-start(bf16[16,96,512]{2,1,0:T(8,128)(2,1)S(1)} %pad_maximum_fusion), channel_id=1, source_target_pairs={{0,6},{1,3},{2,4},{3,1},{4,2},{5,7},{6,0},{7,5},{8,14},{9,11},{10,... | collective-permute-start | bytes 4718600 | tf_op jit(solution)/shard_map/ppermute | solution.py:31
  84.5 31.7 %collective-permute-start.15 = (bf16[16,96,512]{2,1,0:T(8,128)(2,1)}, bf16[16,96,512]{2,1,0:T(8,128)(2,1)}, u32[]{:S(2)}, u32[]{:S(2)}) collective-permute-start(bf16[16,96,512]{2,1,0:T(8,128)(2,1)} %collective-permute-done.14), channel_id=1, source_target_pairs={{0,6},{1,3},{2,4},{3,1},{4,2},{5,7},{6,0},{7,5},{8,14},{9,11},{10,... | collective-permute-start | bytes 4718600 | tf_op jit(solution)/shard_map/ppermute | solution.py:31
  85.1 19.8 %collective-permute-start.19 = (bf16[16,80,512]{2,1,0:T(8,128)(2,1)}, bf16[16,80,512]{2,1,0:T(8,128)(2,1)}, u32[]{:S(2)}, u32[]{:S(2)}) collective-permute-start(bf16[16,80,512]{2,1,0:T(8,128)(2,1)} %pad_maximum_fusion.1), channel_id=1, source_target_pairs={{0,72},{1,9},{2,74},{3,11},{4,76},{5,13},{6,78},{7,15},{8,64},{9,1... | collective-permute-start | bytes 3932168 | tf_op jit(solution)/shard_map/ppermute | solution.py:31
  85.1 19.9 %collective-permute-start.18 = (bf16[16,80,512]{2,1,0:T(8,128)(2,1)}, bf16[16,80,512]{2,1,0:T(8,128)(2,1)}, u32[]{:S(2)}, u32[]{:S(2)}) collective-permute-start(bf16[16,80,512]{2,1,0:T(8,128)(2,1)} %collective-permute-done.17), channel_id=1, source_target_pairs={{0,48},{1,17},{2,50},{3,19},{4,52},{5,21},{6,54},{7,23},{8,56},{9,... | collective-permute-start | bytes 3932168 | tf_op jit(solution)/shard_map/ppermute | solution.py:31
  85.1 1.1 copy-start.3
  86.2 30.0 %collective-permute-start.21 = (bf16[16,80,512]{2,1,0:T(8,128)(2,1)}, bf16[16,80,512]{2,1,0:T(8,128)(2,1)}, u32[]{:S(2)}, u32[]{:S(2)}) collective-permute-start(bf16[16,80,512]{2,1,0:T(8,128)(2,1)} %collective-permute-done.20), channel_id=1, source_target_pairs={{0,72},{1,9},{2,74},{3,11},{4,76},{5,13},{6,78},{7,15},{8,64},{9,1... | collective-permute-start | bytes 3932168 | tf_op jit(solution)/shard_map/ppermute | solution.py:31
  95.1 1.6 copy-start
  96.7 1.3 copy-start.2
  98.0 18.2 %copy-start.4 = (bf16[16,80,512]{2,1,0:T(8,128)(2,1)S(1)}, bf16[16,80,512]{2,1,0:T(8,128)(2,1)}, u32[]{:S(2)}) copy-start(bf16[16,80,512]{2,1,0:T(8,128)(2,1)} %copy-done.3) | copy-start | bytes 3932164
  121.8 11.1 %collective-permute-start.22 = (bf16[4,256,512]{2,1,0:T(8,128)(2,1)S(1)}, bf16[4,256,512]{2,1,0:T(8,128)(2,1)S(1)}, u32[]{:S(2)}, u32[]{:S(2)}) collective-permute-start(bf16[4,256,512]{2,1,0:T(8,128)(2,1)S(1)} %shard_map.50), channel_id=1, source_target_pairs={{0,1},{1,0},{2,3},{3,2},{4,5},{5,4},{6,7},{7,6},{8,9},{9,8},{10,11... | collective-permute-start | bytes 3145736 | tf_op jit(solution)/shard_map/ppermute | solution.py:31
  133.4 8.9 %collective-permute-start.23 = (bf16[256,512]{1,0:T(8,128)(2,1)S(1)}, bf16[256,512]{1,0:T(8,128)(2,1)S(1)}, u32[]{:S(2)}, u32[]{:S(2)}) collective-permute-start(bf16[256,512]{1,0:T(8,128)(2,1)S(1)} %get-tuple-element.37), channel_id=1, source_target_pairs={{0,0},{1,65},{2,2},{3,67},{4,4},{5,69},{6,6},{7,71},{8,8},{9,73},{... | collective-permute-start | bytes 786440 | tf_op jit(solution)/shard_map/ppermute | solution.py:31
  135.3 13.8 %collective-permute-start.24 = (bf16[256,512]{1,0:T(8,128)(2,1)S(1)}, bf16[256,512]{1,0:T(8,128)(2,1)S(1)}, u32[]{:S(2)}, u32[]{:S(2)}) collective-permute-start(bf16[256,512]{1,0:T(8,128)(2,1)S(1)} %get-tuple-element.40), channel_id=1, source_target_pairs={{0,16},{1,81},{2,18},{3,83},{4,20},{5,85},{6,22},{7,87},{8,24},{9,... | collective-permute-start | bytes 786440 | tf_op jit(solution)/shard_map/ppermute | solution.py:31
  135.4 14.7 %collective-permute-start.25 = (bf16[256,512]{1,0:T(8,128)(2,1)S(1)}, bf16[256,512]{1,0:T(8,128)(2,1)S(1)}, u32[]{:S(2)}, u32[]{:S(2)}) collective-permute-start(bf16[256,512]{1,0:T(8,128)(2,1)S(1)} %get-tuple-element.39), channel_id=1, source_target_pairs={{0,32},{1,97},{2,34},{3,99},{4,36},{5,101},{6,38},{7,103},{8,40},{... | collective-permute-start | bytes 786440 | tf_op jit(solution)/shard_map/ppermute | solution.py:31
  141.7 8.8 %collective-permute-start.26 = (bf16[256,512]{1,0:T(8,128)(2,1)S(1)}, bf16[256,512]{1,0:T(8,128)(2,1)S(1)}, u32[]{:S(2)}, u32[]{:S(2)}) collective-permute-start(bf16[256,512]{1,0:T(8,128)(2,1)S(1)} %get-tuple-element.38), channel_id=1, source_target_pairs={{0,48},{1,113},{2,50},{3,115},{4,52},{5,117},{6,54},{7,119},{8,56}... | collective-permute-start | bytes 786440 | tf_op jit(solution)/shard_map/ppermute | solution.py:31
  150.7 4.1 %copy-start.6 = (bf16[4,256,512]{2,1,0:T(8,128)(2,1)}, bf16[4,256,512]{2,1,0:T(8,128)(2,1)S(1)}, u32[]{:S(2)}) copy-start(bf16[4,256,512]{2,1,0:T(8,128)(2,1)S(1)} %pad_maximum_fusion.3.own) | copy-start | bytes 3145732
  150.7 4.1 %collective-permute-start.27 = (bf16[4,256,512]{2,1,0:T(8,128)(2,1)S(1)}, bf16[4,256,512]{2,1,0:T(8,128)(2,1)S(1)}, u32[]{:S(2)}, u32[]{:S(2)}) collective-permute-start(bf16[4,256,512]{2,1,0:T(8,128)(2,1)S(1)} %pad_maximum_fusion.3.own), channel_id=1, source_target_pairs={{0,1},{1,0},{2,3},{3,2},{4,5},{5,4},{6,7},{7,6},{8,9},{9,8},{10,11... | collective-permute-start | bytes 3145736 | tf_op jit(solution)/shard_map/ppermute | solution.py:31
  154.8 1.0 copy-start.9
  189.4 6.0 %collective-permute-start.28 = (bf16[256,512]{1,0:T(8,128)(2,1)}, bf16[256,512]{1,0:T(8,128)(2,1)S(1)}, u32[]{:S(2)}, u32[]{:S(2)}) collective-permute-start(bf16[256,512]{1,0:T(8,128)(2,1)} %get-tuple-element.33), channel_id=1, source_target_pairs={{0,0},{1,8},{2,2},{3,10},{4,4},{5,12},{6,6},{7,14},{8,9},{9,1},{10... | collective-permute-start | bytes 786440 | tf_op jit(solution)/shard_map/ppermute | solution.py:31
  191.3 15.7 %collective-permute-start.29 = (bf16[256,512]{1,0:T(8,128)(2,1)}, bf16[256,512]{1,0:T(8,128)(2,1)S(1)}, u32[]{:S(2)}, u32[]{:S(2)}) collective-permute-start(bf16[256,512]{1,0:T(8,128)(2,1)} %get-tuple-element.34), channel_id=1, source_target_pairs={{0,2},{1,10},{2,4},{3,12},{4,6},{5,14},{6,0},{7,8},{8,11},{9,3},{1... | collective-permute-start | bytes 786440 | tf_op jit(solution)/shard_map/ppermute | solution.py:31
  192.3 14.8 %collective-permute-start.30 = (bf16[256,512]{1,0:T(8,128)(2,1)}, bf16[256,512]{1,0:T(8,128)(2,1)S(1)}, u32[]{:S(2)}, u32[]{:S(2)}) collective-permute-start(bf16[256,512]{1,0:T(8,128)(2,1)} %get-tuple-element.35), channel_id=1, source_target_pairs={{0,4},{1,12},{2,6},{3,14},{4,0},{5,8},{6,2},{7,10},{8,13},{9,5},{1... | collective-permute-start | bytes 786440 | tf_op jit(solution)/shard_map/ppermute | solution.py:31
  193.6 15.5 %collective-permute-start.31 = (bf16[256,512]{1,0:T(8,128)(2,1)}, bf16[256,512]{1,0:T(8,128)(2,1)S(1)}, u32[]{:S(2)}, u32[]{:S(2)}) collective-permute-start(bf16[256,512]{1,0:T(8,128)(2,1)} %get-tuple-element.36), channel_id=1, source_target_pairs={{0,6},{1,14},{2,0},{3,8},{4,2},{5,10},{6,4},{7,12},{8,15},{9,7},{1... | collective-permute-start | bytes 786440 | tf_op jit(solution)/shard_map/ppermute | solution.py:31
  195.4 13.7 %copy-start.10 = (bf16[256,512]{1,0:T(8,128)(2,1)}, bf16[256,512]{1,0:T(8,128)(2,1)S(1)}, u32[]{:S(2)}) copy-start(bf16[256,512]{1,0:T(8,128)(2,1)S(1)} %collective-permute-done.28.refs_0_) | copy-start | bytes 786436
  207.1 2.1 copy-start.11
  207.1 2.1 copy-start.12
  209.1 0.7 copy-start.13

commit v5 on v4

--- a/solution.py
+++ b/solution.py
@@ -58,6 +58,8 @@
 
 def gather_last(block, axis):
     first = exchange(block, axis, 1)
+    if axis == "z":
+        first, block = lax.optimization_barrier((first, block))
     second = exchange(block, axis, 2)
     relayed = exchange(first, axis, 2)
     return [v.reshape(4, 4, *v.shape[1:]) for v in (block, first, second, relayed)]
@@ -79,32 +81,37 @@
     return row
 
 
-def refit_kernel(table, master, out):
-    tiles = master.shape[0] // BLOCK
-    amax = jnp.max(jnp.abs(master[...]).reshape(tiles, BLOCK, COLS), axis=1)
-    for c in range(COLS // BLOCK):
-        cols = slice(c * BLOCK, (c + 1) * BLOCK)
-        top = jnp.max(amax[:, cols], axis=1, keepdims=True)
-        scales = ((top + 1e-6) / 448.0).astype(jnp.bfloat16).astype(jnp.float32)
-        inverses = 1.0 / scales
-        for r in range(tiles):
-            at = (slice(r * BLOCK, (r + 1) * BLOCK), cols)
-            coded = (master[at] * inverses[r : r + 1]).astype(jnp.bfloat16)
-            out[at] = (coded.astype(jnp.float32) * scales[r : r + 1]).astype(jnp.bfloat16)
+def refit_kernel(first, table, master, out, held, sems):
+    copies = []
+    for n in range(8):
+        at = pl.multiple_of(table[first + n] * SHARE, SHARE)
+        copies.append(pltpu.make_async_copy(master.at[pl.ds(at, SHARE)], held.at[n], sems.at[n]))
+        copies[-1].start()
+    tiles = SHARE // BLOCK
+    for n in range(8):
+        copies[n].wait()
+        amax = jnp.max(jnp.abs(held[n]).reshape(tiles, BLOCK, COLS), axis=1)
+        for c in range(COLS // BLOCK):
+            cols = slice(c * BLOCK, (c + 1) * BLOCK)
+            top = jnp.max(amax[:, cols], axis=1, keepdims=True)
+            scales = ((top + 1e-6) / 448.0).astype(jnp.bfloat16).astype(jnp.float32)
+            inverses = 1.0 / scales
+            for r in range(tiles):
+                tile = held[n, r * BLOCK : (r + 1) * BLOCK, cols]
+                coded = (tile * inverses[r : r + 1]).astype(jnp.bfloat16)
+                value = (coded.astype(jnp.float32) * scales[r : r + 1]).astype(jnp.bfloat16)
+                out[n * SHARE + r * BLOCK : n * SHARE + (r + 1) * BLOCK, cols] = value
 
 
 def refit(table, master, first):
     size = 8 * SHARE * COLS
     return pl.pallas_call(
-        refit_kernel,
-        grid_spec=pltpu.PrefetchScalarGridSpec(
-            num_scalar_prefetch=1,
-            grid=(8,),
-            in_specs=[pl.BlockSpec((SHARE, COLS), lambda i, t: (t[first + i], 0))],
-            out_specs=pl.BlockSpec((SHARE, COLS), lambda i, t: (i, 0)),
-        ),
+        functools.partial(refit_kernel, first),
+        in_specs=[pl.BlockSpec(memory_space=pltpu.SMEM), pl.BlockSpec(memory_space=pltpu.HBM)],
+        out_specs=pl.BlockSpec(memory_space=pltpu.VMEM),
         out_shape=jax.ShapeDtypeStruct((8 * SHARE, COLS), jnp.bfloat16),
-        compiler_params=pltpu.CompilerParams(vmem_limit_bytes=60 * MIB),
+        scratch_shapes=[pltpu.VMEM((8, SHARE, COLS), jnp.float32), pltpu.SemaphoreType.DMA((8,))],
+        compiler_params=pltpu.CompilerParams(vmem_limit_bytes=48 * MIB),
         cost_estimate=pl.CostEstimate(flops=size * 6, bytes_accessed=size * 6, transcendentals=0),
     )(table, master)
 
@@ -243,8 +250,7 @@
     )(table, *weights, *parts)
 
 
-def spread_kernel(table, owner, own, other, *refs):
-    outs, sems = refs[:4], refs[4]
+def spread_kernel(table, owner, own, other, *outs):
     for k, out in enumerate(outs):
         section = owner[table[DEST + k]]
         half = jnp.where(section >= 4, 1, 0)
@@ -253,14 +259,11 @@
 
         @pl.when(far == table[CORE])
         def _():
-            pltpu.make_async_copy(own.at[at], out, sems.at[k]).start()
+            out[...] = own[at]
 
         @pl.when(far != table[CORE])
         def _():
-            pltpu.make_async_copy(other.at[at], out, sems.at[k]).start()
-
-    for k, out in enumerate(outs):
-        pltpu.make_async_copy(out, out, sems.at[k]).wait()
+            out[...] = other[at]
 
 
 def arrange_kernel(table, *refs):
@@ -274,14 +277,15 @@
         copy.wait()
 
 
-def small_call(kernel, scalars, parts, shapes):
-    smem, anywhere = pl.BlockSpec(memory_space=pltpu.SMEM), pl.BlockSpec(memory_space=pl.ANY)
+def small_call(kernel, scalars, parts, shapes, out_space, scratch=()):
+    smem, vmem = pl.BlockSpec(memory_space=pltpu.SMEM), pl.BlockSpec(memory_space=pltpu.VMEM)
     return pl.pallas_call(
         kernel,
-        in_specs=[smem] * len(scalars) + [anywhere] * len(parts),
-        out_specs=[anywhere] * len(shapes),
+        in_specs=[smem] * len(scalars) + [vmem] * len(parts),
+        out_specs=[pl.BlockSpec(memory_space=out_space)] * len(shapes),
         out_shape=[jax.ShapeDtypeStruct(shape, jnp.bfloat16) for shape in shapes],
-        scratch_shapes=[pltpu.SemaphoreType.DMA((4,))],
+        scratch_shapes=scratch,
+        compiler_params=pltpu.CompilerParams(vmem_limit_bytes=16 * MIB),
         cost_estimate=pl.CostEstimate(flops=0, bytes_accessed=2 * MIB, transcendentals=0),
     )(*scalars, *parts)
 
@@ -346,11 +350,12 @@
     own = jnp.stack([got[dy] for dy in range(4)])
     other = permute(own, other_core)
 
-    picked = small_call(spread_kernel, [table, owner], [own, other], [(256, 2 * COLS)] * 4)
+    picked = small_call(spread_kernel, [table, owner], [own, other], [(256, 2 * COLS)] * 4, pltpu.VMEM)
     got = {}
     for dz in (2, 1, 3, 0):
         got[dz] = permute(picked[dz], lambda x, y, z, c: linear(x ^ c, y, z + dz, x % 2))
-    return small_call(arrange_kernel, [table], [got[dz] for dz in range(4)], [(256, 8 * COLS)])[0]
+    got = [got[dz] for dz in range(4)]
+    return small_call(arrange_kernel, [table], got, [(256, 8 * COLS)], pltpu.HBM, [pltpu.SemaphoreType.DMA((4,))])[0]
 
 
 def solution(mesh):

time: 246 us -> 168 us (0.68)
  Pallas kernels: 99.3 us -> 23.4 us
  starting transfers between devices: 50 us -> 58.5 us
  local copies, waits for them, and re-layouts: 8.88 us -> 2.62 us
    pallas_call x4, Pallas kernels: 82.1 us -> 8.79 us  [the longest x2 6.55 us: refit(): pl.pallas_call(functools.partial(refit_kernel, first), in_specs=[pl.Block...]
    ppermute x32, starting transfers between devices: 50 us -> 58.5 us  [permute(): lax.ppermute(value, AXES, [(i, move(*coords(i))) for i in range(N_DEV)])]
    unnamed x28 -> x10, local copies, waits for them, and re-layouts: 5.72 us -> 0.02 us
    pallas_call x3, Pallas kernels: 17.3 us -> 14.6 us  [product(): pl.pallas_call(kernel, in_specs=[pl.BlockSpec(memory_space=pltpu.SMEM)] +...]
  transfers between devices with their start and end apart: 32 -> 32, of which waited for: 16 -> 19; matrix products, arithmetic and copies ran while one was open for 4% -> 3% of each run, Pallas kernels for 11% -> 10%
where the time goes in v5:
time: 168 us; the launch traced here: 167 us
  waiting for transfers between devices  76.6 us (46%)
  starting transfers between devices  58.5 us (35%)
  Pallas kernels  23.4 us (14%)
  other arithmetic  5.7 us (3%)
  local copies, waits for them, and re-layouts  2.62 us (2%)
    ppermute x32, waiting for transfers between devices, permute(): lax.ppermute(value, AXES, [(i, move(*coords(i))) for i in range(N_DEV)])  76.6 us
    ppermute x32, starting transfers between devices, permute(): lax.ppermute(value, AXES, [(i, move(*coords(i))) for i in range(N_DEV)])  58.5 us
    pallas_call x3, Pallas kernels, product(): pl.pallas_call(kernel, in_specs=[pl.BlockSpec(memory_space=pltpu.SMEM)] +...  14.6 us
    pallas_call x2, Pallas kernels, refit(): pl.pallas_call(functools.partial(refit_kernel, first), in_specs=[pl.Block...  6.55 us
    concatenate x12, other arithmetic, gather_planes(): jnp.concatenate([block, exchange(block, ORDER[part][level], which)], axis=0)  5.2 us
  transfers between devices with their start and end apart: 32, of which 19 were waited for; matrix products, arithmetic and copies ran while one was open for 3% of the time, Pallas kernels for 10%

profile of v5, /device:TPU:3, one launch (start us, length us, event | category | flops | bytes accessed | tf_op | source)
XLA Modules:
  0.0 167.2 jit_solution(6463681064777655283)
XLA Ops:
  0.0 0.9 slice_bitcast_fusion.5
  0.9 2.8 %collective-permute-start.1 = (bf16[1,80,512]{2,1,0:T(8,128)(2,1)S(1)}, bf16[1,80,512]{2,1,0:T(8,128)(2,1)S(1)}, u32[]{:S(2)}, u32[]{:S(2)}) collective-permute-start(bf16[1,80,512]{2,1,0:T(8,128)(2,1)S(1)} %get-tuple-element.46), channel_id=1, source_target_pairs={{0,16},{1,49},{2,18},{3,51},{4,20},{5,53},{6,22},{7,55},{8,24},{9,... | collective-permute-start | bytes 245768 | tf_op jit(solution)/shard_map/ppermute | solution.py:31
  3.8 3.8 %collective-permute-start.2 = (bf16[1,80,512]{2,1,0:T(8,128)(2,1)S(1)}, bf16[1,80,512]{2,1,0:T(8,128)(2,1)S(1)}, u32[]{:S(2)}, u32[]{:S(2)}) collective-permute-start(bf16[1,80,512]{2,1,0:T(8,128)(2,1)S(1)} %get-tuple-element.45), channel_id=1, source_target_pairs={{0,2},{1,7},{2,0},{3,5},{4,6},{5,3},{6,4},{7,1},{8,10},{9,15},{10,... | collective-permute-start | bytes 245768 | tf_op jit(solution)/shard_map/ppermute | solution.py:31
  7.5 0.9 slice_bitcast_fusion.4
  8.4 1.2 collective-permute-start.3
  9.7 2.2 %collective-permute-done.3 = bf16[1,96,512]{2,1,0:T(8,128)(2,1)S(1)} collective-permute-done((bf16[1,96,512]{2,1,0:T(8,128)(2,1)S(1)}, bf16[1,96,512]{2,1,0:T(8,128)(2,1)S(1)}, u32[]{:S(2)}, u32[]{:S(2)}) %collective-permute-start.3) | collective-permute-done | bytes 98336 | tf_op jit(solution)/shard_map/ppermute | solution.py:31
  11.9 0.1 collective-permute-start.4
  12.0 0.1 collective-permute-start.5
  12.1 1.5 collective-permute-start.6
  13.6 2.8 %collective-permute-done.4 = bf16[2,80,512]{2,1,0:T(8,128)(2,1)S(1)} collective-permute-done((bf16[2,80,512]{2,1,0:T(8,128)(2,1)S(1)}, bf16[2,80,512]{2,1,0:T(8,128)(2,1)S(1)}, u32[]{:S(2)}, u32[]{:S(2)}) %collective-permute-start.4) | collective-permute-done | bytes 163872 | tf_op jit(solution)/shard_map/ppermute | solution.py:31
  16.5 0.1 collective-permute-done.5
  16.6 0.4 collective-permute-done.6
  17.0 2.0 %collective-permute-start.8 = (bf16[4,80,512]{2,1,0:T(8,128)(2,1)S(1)}, bf16[4,80,512]{2,1,0:T(8,128)(2,1)S(1)}, u32[]{:S(2)}, u32[]{:S(2)}) collective-permute-start(bf16[4,80,512]{2,1,0:T(8,128)(2,1)S(1)} %pad_maximum_fusion.9), channel_id=1, source_target_pairs={{0,8},{1,73},{2,10},{3,75},{4,12},{5,77},{6,14},{7,79},{8,0},{9,65... | collective-permute-start | bytes 983048 | tf_op jit(solution)/shard_map/ppermute | solution.py:31
  19.0 0.4 collective-permute-start.9
  19.4 4.6 %collective-permute-done.8 = bf16[4,80,512]{2,1,0:T(8,128)(2,1)S(1)} collective-permute-done((bf16[4,80,512]{2,1,0:T(8,128)(2,1)S(1)}, bf16[4,80,512]{2,1,0:T(8,128)(2,1)S(1)}, u32[]{:S(2)}, u32[]{:S(2)}) %collective-permute-start.8) | collective-permute-done | bytes 327712 | tf_op jit(solution)/shard_map/ppermute | solution.py:31
  24.0 0.1 pad_maximum_fusion.6
  24.1 2.1 %collective-permute-done.7 = bf16[4,80,512]{2,1,0:T(8,128)(2,1)S(1)} collective-permute-done((bf16[4,80,512]{2,1,0:T(8,128)(2,1)S(1)}, bf16[4,80,512]{2,1,0:T(8,128)(2,1)S(1)}, u32[]{:S(2)}, u32[]{:S(2)}) %collective-permute-start.7) | collective-permute-done | bytes 327712 | tf_op jit(solution)/shard_map/ppermute | solution.py:31
  26.1 0.1 pad_maximum_fusion.5
  26.2 0.7 collective-permute-done.9
  26.9 0.9 pad_maximum_fusion.4
  27.8 2.1 %collective-permute-start.11 = (bf16[8,80,512]{2,1,0:T(8,128)(2,1)S(1)}, bf16[8,80,512]{2,1,0:T(8,128)(2,1)}, u32[]{:S(2)}, u32[]{:S(2)}) collective-permute-start(bf16[8,80,512]{2,1,0:T(8,128)(2,1)S(1)} %pad_maximum_fusion.6), channel_id=1, source_target_pairs={{0,72},{1,9},{2,74},{3,11},{4,76},{5,13},{6,78},{7,15},{8,64},{9,1... | collective-permute-start | bytes 1966088 | tf_op jit(solution)/shard_map/ppermute | solution.py:31
  29.9 1.0 collective-permute-start.10
  30.9 0.5 collective-permute-start.12
  31.4 0.7 dynamic-slice_bitcast_fusion.table
  32.1 3.3 %shard_map.47 = bf16[4096,256]{1,0:T(8,128)(2,1)S(1)} custom-call(s32[28]{0:T(128)S(1)} %dynamic-slice_bitcast_fusion.table, f32[8192,256]{1,0:T(8,128)} %master.3), custom_call_target="tpu_custom_call" | custom-call | flops 6291456 | bytes 6291456 | tf_op jit(solution)/shard_map/pallas_call | solution.py:108
  35.4 5.3 %collective-permute-start = (bf16[4096,256]{1,0:T(8,128)(2,1)S(1)}, bf16[4096,256]{1,0:T(8,128)(2,1)S(1)}, u32[]{:S(2)}, u32[]{:S(2)}) collective-permute-start(bf16[4096,256]{1,0:T(8,128)(2,1)S(1)} %shard_map.47), channel_id=1, source_target_pairs={{0,1},{1,0},{2,3},{3,2},{4,5},{5,4},{6,7},{7,6},{8,9},{9,8},{10,11... | collective-permute-start | bytes 6291464 | tf_op jit(solution)/shard_map/ppermute | solution.py:31
  40.7 1.3 pad_maximum_fusion.2
  42.0 1.2 pad_maximum_fusion.1
  43.2 1.5 pad_maximum_fusion
  44.7 2.4 %collective-permute-start.13 = (bf16[16,96,512]{2,1,0:T(8,128)(2,1)S(1)}, bf16[16,96,512]{2,1,0:T(8,128)(2,1)}, u32[]{:S(2)}, u32[]{:S(2)}) collective-permute-start(bf16[16,96,512]{2,1,0:T(8,128)(2,1)S(1)} %pad_maximum_fusion), channel_id=1, source_target_pairs={{0,2},{1,7},{2,0},{3,5},{4,6},{5,3},{6,4},{7,1},{8,10},{9,15},{10,... | collective-permute-start | bytes 4718600 | tf_op jit(solution)/shard_map/ppermute | solution.py:31
  47.1 1.9 %collective-permute-start.17 = (bf16[16,80,512]{2,1,0:T(8,128)(2,1)S(1)}, bf16[16,80,512]{2,1,0:T(8,128)(2,1)}, u32[]{:S(2)}, u32[]{:S(2)}) collective-permute-start(bf16[16,80,512]{2,1,0:T(8,128)(2,1)S(1)} %pad_maximum_fusion.2), channel_id=1, source_target_pairs={{0,16},{1,49},{2,18},{3,51},{4,20},{5,53},{6,22},{7,55},{8,24},{9,... | collective-permute-start | bytes 3932168 | tf_op jit(solution)/shard_map/ppermute | solution.py:31
  49.0 16.5 %collective-permute-done.13 = bf16[16,96,512]{2,1,0:T(8,128)(2,1)} collective-permute-done((bf16[16,96,512]{2,1,0:T(8,128)(2,1)S(1)}, bf16[16,96,512]{2,1,0:T(8,128)(2,1)}, u32[]{:S(2)}, u32[]{:S(2)}) %collective-permute-start.13) | collective-permute-done | bytes 1572896 | tf_op jit(solution)/shard_map/ppermute | solution.py:31
  65.6 1.5 collective-permute-start.15
  67.0 6.7 %collective-permute-done.17 = bf16[16,80,512]{2,1,0:T(8,128)(2,1)} collective-permute-done((bf16[16,80,512]{2,1,0:T(8,128)(2,1)S(1)}, bf16[16,80,512]{2,1,0:T(8,128)(2,1)}, u32[]{:S(2)}, u32[]{:S(2)}) %collective-permute-start.17) | collective-permute-done | bytes 1310752 | tf_op jit(solution)/shard_map/ppermute | solution.py:31
  73.7 3.5 %collective-permute-done.16 = bf16[16,80,512]{2,1,0:T(8,128)(2,1)S(1)} collective-permute-done((bf16[16,80,512]{2,1,0:T(8,128)(2,1)S(1)}, bf16[16,80,512]{2,1,0:T(8,128)(2,1)S(1)}, u32[]{:S(2)}, u32[]{:S(2)}) %collective-permute-start.16) | collective-permute-done | bytes 1310752 | tf_op jit(solution)/shard_map/ppermute | solution.py:31
  77.2 1.1 collective-permute-start.21
  78.3 3.3 %shard_map.46.mine = bf16[4096,256]{1,0:T(8,128)(2,1)S(1)} custom-call(s32[28]{0:T(128)S(1)} %dynamic-slice_bitcast_fusion.table, f32[8192,256]{1,0:T(8,128)} %master.3), custom_call_target="tpu_custom_call" | custom-call | flops 6291456 | bytes 6291456 | tf_op jit(solution)/shard_map/pallas_call | solution.py:108
  81.6 6.0 %shard_map.48.early = f32[2,4,256,512]{3,2,1,0:T(8,128)S(1)} custom-call(s32[28]{0:T(128)S(1)} %dynamic-slice_bitcast_fusion.table, bf16[4096,256]{1,0:T(8,128)(2,1)S(1)} %shard_map.46.mine, bf16[4096,256]{1,0:T(8,128)(2,1)S(1)} %collective-permute-done.theirs, bf16[4,4,96,512]{3,2,1,0:T(8,128)(2,1)S(1)} %bitcast.32, bf16[4,4,96,512]{3,2,1,0:T(8,128)(2,1)} %bitcast.11.z1, ...), custom_call_target="tpu_custom_call" | custom-call | flops 4294967296 | bytes 14680064 | tf_op jit(solution)/shard_map/pallas_call | solution.py:240
  87.6 3.0 %collective-permute-done.19 = bf16[16,80,512]{2,1,0:T(8,128)(2,1)} collective-permute-done((bf16[16,80,512]{2,1,0:T(8,128)(2,1)S(1)}, bf16[16,80,512]{2,1,0:T(8,128)(2,1)}, u32[]{:S(2)}, u32[]{:S(2)}) %collective-permute-start.19) | collective-permute-done | bytes 1310752 | tf_op jit(solution)/shard_map/ppermute | solution.py:31
  90.6 3.4 %collective-permute-done.18 = bf16[16,80,512]{2,1,0:T(8,128)(2,1)} collective-permute-done((bf16[16,80,512]{2,1,0:T(8,128)(2,1)}, bf16[16,80,512]{2,1,0:T(8,128)(2,1)}, u32[]{:S(2)}, u32[]{:S(2)}) %collective-permute-start.18) | collective-permute-done | bytes 1310752 | tf_op jit(solution)/shard_map/ppermute | solution.py:31
  94.0 10.6 %collective-permute-done.21 = bf16[16,80,512]{2,1,0:T(8,128)(2,1)} collective-permute-done((bf16[16,80,512]{2,1,0:T(8,128)(2,1)}, bf16[16,80,512]{2,1,0:T(8,128)(2,1)}, u32[]{:S(2)}, u32[]{:S(2)}) %collective-permute-start.21) | collective-permute-done | bytes 1310752 | tf_op jit(solution)/shard_map/ppermute | solution.py:31
  104.6 4.6 %shard_map.50 = bf16[4,256,512]{2,1,0:T(8,128)(2,1)S(1)} custom-call(s32[28]{0:T(128)S(1)} %dynamic-slice_bitcast_fusion.table, bf16[4096,256]{1,0:T(8,128)(2,1)S(1)} %shard_map.46.mine, bf16[4096,256]{1,0:T(8,128)(2,1)S(1)} %collective-permute-done.theirs, bf16[4,4,96,512]{3,2,1,0:T(8,128)(2,1)S(1)} %bitcast.33, bf16[4,4,96,512]{3,2,1,0:T(8,128)(2,1)S(1)} %bitcast.35, ...), custom_call_target="tpu_custom_call" | custom-call | flops 4294967296 | bytes 14680064 | tf_op jit(solution)/shard_map/pallas_call | solution.py:240
  109.3 11.3 %collective-permute-start.22 = (bf16[4,256,512]{2,1,0:T(8,128)(2,1)S(1)}, bf16[4,256,512]{2,1,0:T(8,128)(2,1)S(1)}, u32[]{:S(2)}, u32[]{:S(2)}) collective-permute-start(bf16[4,256,512]{2,1,0:T(8,128)(2,1)S(1)} %shard_map.50), channel_id=1, source_target_pairs={{0,1},{1,0},{2,3},{3,2},{4,5},{5,4},{6,7},{7,6},{8,9},{9,8},{10,11... | collective-permute-start | bytes 3145736 | tf_op jit(solution)/shard_map/ppermute | solution.py:31
  120.6 4.0 %shard_map.49 = f32[4,256,512]{2,1,0:T(8,128)S(1)} custom-call(s32[28]{0:T(128)S(1)} %dynamic-slice_bitcast_fusion.table, bf16[4096,256]{1,0:T(8,128)(2,1)S(1)} %shard_map.46.mine, bf16[4096,256]{1,0:T(8,128)(2,1)S(1)} %collective-permute-done.theirs, bf16[4,4,96,512]{3,2,1,0:T(8,128)(2,1)S(1)} %bitcast.34, bf16[4,4,96,512]{3,2,1,0:T(8,128)(2,1)S(1)} %bitcast.36, ...), custom_call_target="tpu_custom_call" | custom-call | flops 4294967296 | bytes 14680064 | tf_op jit(solution)/shard_map/pallas_call | solution.py:240
  124.6 0.4 add_convert_fusion
  125.0 0.1 slice_bitcast_fusion.3
  125.1 3.8 %collective-permute-start.23 = (bf16[256,512]{1,0:T(8,128)(2,1)S(1)}, bf16[256,512]{1,0:T(8,128)(2,1)S(1)}, u32[]{:S(2)}, u32[]{:S(2)}) collective-permute-start(bf16[256,512]{1,0:T(8,128)(2,1)S(1)} %get-tuple-element.41), channel_id=1, source_target_pairs={{0,0},{1,65},{2,2},{3,67},{4,4},{5,69},{6,6},{7,71},{8,8},{9,73},{... | collective-permute-start | bytes 786440 | tf_op jit(solution)/shard_map/ppermute | solution.py:31
  128.9 0.8 collective-permute-start.24
  129.7 4.5 %collective-permute-start.25 = (bf16[256,512]{1,0:T(8,128)(2,1)S(1)}, bf16[256,512]{1,0:T(8,128)(2,1)S(1)}, u32[]{:S(2)}, u32[]{:S(2)}) collective-permute-start(bf16[256,512]{1,0:T(8,128)(2,1)S(1)} %get-tuple-element.43), channel_id=1, source_target_pairs={{0,32},{1,97},{2,34},{3,99},{4,36},{5,101},{6,38},{7,103},{8,40},{... | collective-permute-start | bytes 786440 | tf_op jit(solution)/shard_map/ppermute | solution.py:31
  134.2 0.1 collective-permute-start.26
  134.3 3.8 %collective-permute-done.24 = bf16[256,512]{1,0:T(8,128)(2,1)S(1)} collective-permute-done((bf16[256,512]{1,0:T(8,128)(2,1)S(1)}, bf16[256,512]{1,0:T(8,128)(2,1)S(1)}, u32[]{:S(2)}, u32[]{:S(2)}) %collective-permute-start.24) | collective-permute-done | bytes 262176 | tf_op jit(solution)/shard_map/ppermute | solution.py:31
  138.1 2.7 %collective-permute-done.25 = bf16[256,512]{1,0:T(8,128)(2,1)S(1)} collective-permute-done((bf16[256,512]{1,0:T(8,128)(2,1)S(1)}, bf16[256,512]{1,0:T(8,128)(2,1)S(1)}, u32[]{:S(2)}, u32[]{:S(2)}) %collective-permute-start.25) | collective-permute-done | bytes 262176 | tf_op jit(solution)/shard_map/ppermute | solution.py:31
  140.9 1.3 collective-permute-done.26
  142.2 0.1 pad_maximum_fusion.3.own
  142.3 0.1 collective-permute-start.27
  142.4 2.6 %collective-permute-done.27.other = bf16[4,256,512]{2,1,0:T(8,128)(2,1)S(1)} collective-permute-done((bf16[4,256,512]{2,1,0:T(8,128)(2,1)S(1)}, bf16[4,256,512]{2,1,0:T(8,128)(2,1)S(1)}, u32[]{:S(2)}, u32[]{:S(2)}) %collective-permute-start.27) | collective-permute-done | bytes 1048608 | tf_op jit(solution)/shard_map/ppermute | solution.py:31
  145.1 0.7 shard_map.51
  145.8 3.6 %collective-permute-start.28 = (bf16[256,512]{1,0:T(8,128)(2,1)S(1)}, bf16[256,512]{1,0:T(8,128)(2,1)S(1)}, u32[]{:S(2)}, u32[]{:S(2)}) collective-permute-start(bf16[256,512]{1,0:T(8,128)(2,1)S(1)} %get-tuple-element.37), channel_id=1, source_target_pairs={{0,0},{1,8},{2,2},{3,10},{4,4},{5,12},{6,6},{7,14},{8,9},{9,1},{10... | collective-permute-start | bytes 786440 | tf_op jit(solution)/shard_map/ppermute | solution.py:31
  149.4 0.9 collective-permute-start.29
  150.3 2.3 %collective-permute-start.30 = (bf16[256,512]{1,0:T(8,128)(2,1)S(1)}, bf16[256,512]{1,0:T(8,128)(2,1)S(1)}, u32[]{:S(2)}, u32[]{:S(2)}) collective-permute-start(bf16[256,512]{1,0:T(8,128)(2,1)S(1)} %get-tuple-element.39), channel_id=1, source_target_pairs={{0,4},{1,12},{2,6},{3,14},{4,0},{5,8},{6,2},{7,10},{8,13},{9,5},{1... | collective-permute-start | bytes 786440 | tf_op jit(solution)/shard_map/ppermute | solution.py:31
  152.5 3.3 %collective-permute-start.31 = (bf16[256,512]{1,0:T(8,128)(2,1)S(1)}, bf16[256,512]{1,0:T(8,128)(2,1)S(1)}, u32[]{:S(2)}, u32[]{:S(2)}) collective-permute-start(bf16[256,512]{1,0:T(8,128)(2,1)S(1)} %get-tuple-element.40), channel_id=1, source_target_pairs={{0,6},{1,14},{2,0},{3,8},{4,2},{5,10},{6,4},{7,12},{8,15},{9,7},{1... | collective-permute-start | bytes 786440 | tf_op jit(solution)/shard_map/ppermute | solution.py:31
  155.8 6.4 %collective-permute-done.29.refs_1_ = bf16[256,512]{1,0:T(8,128)(2,1)S(1)} collective-permute-done((bf16[256,512]{1,0:T(8,128)(2,1)S(1)}, bf16[256,512]{1,0:T(8,128)(2,1)S(1)}, u32[]{:S(2)}, u32[]{:S(2)}) %collective-permute-start.29) | collective-permute-done | bytes 262176 | tf_op jit(solution)/shard_map/ppermute | solution.py:31
  162.2 3.2 %collective-permute-done.30.refs_2_ = bf16[256,512]{1,0:T(8,128)(2,1)S(1)} collective-permute-done((bf16[256,512]{1,0:T(8,128)(2,1)S(1)}, bf16[256,512]{1,0:T(8,128)(2,1)S(1)}, u32[]{:S(2)}, u32[]{:S(2)}) %collective-permute-start.30) | collective-permute-done | bytes 262176 | tf_op jit(solution)/shard_map/ppermute | solution.py:31
  165.5 1.5 shard_map.52
  (35 shorter events, 0.3 us)
Async XLA Ops:
  0.9 8.7 %collective-permute-start.1 = (bf16[1,80,512]{2,1,0:T(8,128)(2,1)S(1)}, bf16[1,80,512]{2,1,0:T(8,128)(2,1)S(1)}, u32[]{:S(2)}, u32[]{:S(2)}) collective-permute-start(bf16[1,80,512]{2,1,0:T(8,128)(2,1)S(1)} %get-tuple-element.46), channel_id=1, source_target_pairs={{0,16},{1,49},{2,18},{3,51},{4,20},{5,53},{6,22},{7,55},{8,24},{9,... | collective-permute-start | bytes 245768 | tf_op jit(solution)/shard_map/ppermute | solution.py:31
  3.8 5.9 %collective-permute-start.2 = (bf16[1,80,512]{2,1,0:T(8,128)(2,1)S(1)}, bf16[1,80,512]{2,1,0:T(8,128)(2,1)S(1)}, u32[]{:S(2)}, u32[]{:S(2)}) collective-permute-start(bf16[1,80,512]{2,1,0:T(8,128)(2,1)S(1)} %get-tuple-element.45), channel_id=1, source_target_pairs={{0,2},{1,7},{2,0},{3,5},{4,6},{5,3},{6,4},{7,1},{8,10},{9,15},{10,... | collective-permute-start | bytes 245768 | tf_op jit(solution)/shard_map/ppermute | solution.py:31
  8.4 3.5 %collective-permute-start.3 = (bf16[1,96,512]{2,1,0:T(8,128)(2,1)S(1)}, bf16[1,96,512]{2,1,0:T(8,128)(2,1)S(1)}, u32[]{:S(2)}, u32[]{:S(2)}) collective-permute-start(bf16[1,96,512]{2,1,0:T(8,128)(2,1)S(1)} %slice_bitcast_fusion.4), channel_id=1, source_target_pairs={{0,8},{1,73},{2,10},{3,75},{4,12},{5,77},{6,14},{7,79},{8,0},{9,65... | collective-permute-start | bytes 294920 | tf_op jit(solution)/shard_map/ppermute | solution.py:31
  11.9 4.5 %collective-permute-start.4 = (bf16[2,80,512]{2,1,0:T(8,128)(2,1)S(1)}, bf16[2,80,512]{2,1,0:T(8,128)(2,1)S(1)}, u32[]{:S(2)}, u32[]{:S(2)}) collective-permute-start(bf16[2,80,512]{2,1,0:T(8,128)(2,1)S(1)} %pad_maximum_fusion.11), channel_id=1, source_target_pairs={{0,48},{1,17},{2,50},{3,19},{4,52},{5,21},{6,54},{7,23},{8,56},{9,... | collective-permute-start | bytes 491528 | tf_op jit(solution)/shard_map/ppermute | solution.py:31
  12.0 4.5 %collective-permute-start.5 = (bf16[2,80,512]{2,1,0:T(8,128)(2,1)S(1)}, bf16[2,80,512]{2,1,0:T(8,128)(2,1)S(1)}, u32[]{:S(2)}, u32[]{:S(2)}) collective-permute-start(bf16[2,80,512]{2,1,0:T(8,128)(2,1)S(1)} %pad_maximum_fusion.12), channel_id=1, source_target_pairs={{0,6},{1,3},{2,4},{3,1},{4,2},{5,7},{6,0},{7,5},{8,14},{9,11},{10,... | collective-permute-start | bytes 491528 | tf_op jit(solution)/shard_map/ppermute | solution.py:31
  12.1 4.9 %collective-permute-start.6 = (bf16[2,96,512]{2,1,0:T(8,128)(2,1)S(1)}, bf16[2,96,512]{2,1,0:T(8,128)(2,1)S(1)}, u32[]{:S(2)}, u32[]{:S(2)}) collective-permute-start(bf16[2,96,512]{2,1,0:T(8,128)(2,1)S(1)} %pad_maximum_fusion.10), channel_id=1, source_target_pairs={{0,72},{1,9},{2,74},{3,11},{4,76},{5,13},{6,78},{7,15},{8,64},{9,1... | collective-permute-start | bytes 589832 | tf_op jit(solution)/shard_map/ppermute | solution.py:31
  17.0 7.0 %collective-permute-start.8 = (bf16[4,80,512]{2,1,0:T(8,128)(2,1)S(1)}, bf16[4,80,512]{2,1,0:T(8,128)(2,1)S(1)}, u32[]{:S(2)}, u32[]{:S(2)}) collective-permute-start(bf16[4,80,512]{2,1,0:T(8,128)(2,1)S(1)} %pad_maximum_fusion.9), channel_id=1, source_target_pairs={{0,8},{1,73},{2,10},{3,75},{4,12},{5,77},{6,14},{7,79},{8,0},{9,65... | collective-permute-start | bytes 983048 | tf_op jit(solution)/shard_map/ppermute | solution.py:31
  19.0 7.1 %collective-permute-start.7 = (bf16[4,80,512]{2,1,0:T(8,128)(2,1)S(1)}, bf16[4,80,512]{2,1,0:T(8,128)(2,1)S(1)}, u32[]{:S(2)}, u32[]{:S(2)}) collective-permute-start(bf16[4,80,512]{2,1,0:T(8,128)(2,1)S(1)} %pad_maximum_fusion.8), channel_id=1, source_target_pairs={{0,2},{1,7},{2,0},{3,5},{4,6},{5,3},{6,4},{7,1},{8,10},{9,15},{10,... | collective-permute-start | bytes 983048 | tf_op jit(solution)/shard_map/ppermute | solution.py:31
  19.0 7.8 %collective-permute-start.9 = (bf16[4,96,512]{2,1,0:T(8,128)(2,1)S(1)}, bf16[4,96,512]{2,1,0:T(8,128)(2,1)S(1)}, u32[]{:S(2)}, u32[]{:S(2)}) collective-permute-start(bf16[4,96,512]{2,1,0:T(8,128)(2,1)S(1)} %pad_maximum_fusion.7), channel_id=1, source_target_pairs={{0,16},{1,49},{2,18},{3,51},{4,20},{5,53},{6,22},{7,55},{8,24},{9,... | collective-permute-start | bytes 1179656 | tf_op jit(solution)/shard_map/ppermute | solution.py:31
  26.2 9.2 %copy-start.3 = (bf16[8,80,512]{2,1,0:T(8,128)(2,1)}, bf16[8,80,512]{2,1,0:T(8,128)(2,1)S(1)}, u32[]{:S(2)}) copy-start(bf16[8,80,512]{2,1,0:T(8,128)(2,1)S(1)} %pad_maximum_fusion.5) | copy-start | bytes 1966084
  27.8 12.9 %collective-permute-start.11 = (bf16[8,80,512]{2,1,0:T(8,128)(2,1)S(1)}, bf16[8,80,512]{2,1,0:T(8,128)(2,1)}, u32[]{:S(2)}, u32[]{:S(2)}) collective-permute-start(bf16[8,80,512]{2,1,0:T(8,128)(2,1)S(1)} %pad_maximum_fusion.6), channel_id=1, source_target_pairs={{0,72},{1,9},{2,74},{3,11},{4,76},{5,13},{6,78},{7,15},{8,64},{9,1... | collective-permute-start | bytes 1966088 | tf_op jit(solution)/shard_map/ppermute | solution.py:31
  29.9 12.1 %collective-permute-start.10 = (bf16[8,80,512]{2,1,0:T(8,128)(2,1)S(1)}, bf16[8,80,512]{2,1,0:T(8,128)(2,1)}, u32[]{:S(2)}, u32[]{:S(2)}) collective-permute-start(bf16[8,80,512]{2,1,0:T(8,128)(2,1)S(1)} %pad_maximum_fusion.5), channel_id=1, source_target_pairs={{0,6},{1,3},{2,4},{3,1},{4,2},{5,7},{6,0},{7,5},{8,14},{9,11},{10,... | collective-permute-start | bytes 1966088 | tf_op jit(solution)/shard_map/ppermute | solution.py:31
  30.9 12.3 %collective-permute-start.12 = (bf16[8,96,512]{2,1,0:T(8,128)(2,1)}, bf16[8,96,512]{2,1,0:T(8,128)(2,1)}, u32[]{:S(2)}, u32[]{:S(2)}) collective-permute-start(bf16[8,96,512]{2,1,0:T(8,128)(2,1)} %pad_maximum_fusion.4), channel_id=1, source_target_pairs={{0,48},{1,17},{2,50},{3,19},{4,52},{5,21},{6,54},{7,23},{8,56},{9,... | collective-permute-start | bytes 2359304 | tf_op jit(solution)/shard_map/ppermute | solution.py:31
  35.4 30.2 %collective-permute-start = (bf16[4096,256]{1,0:T(8,128)(2,1)S(1)}, bf16[4096,256]{1,0:T(8,128)(2,1)S(1)}, u32[]{:S(2)}, u32[]{:S(2)}) collective-permute-start(bf16[4096,256]{1,0:T(8,128)(2,1)S(1)} %shard_map.47), channel_id=1, source_target_pairs={{0,1},{1,0},{2,3},{3,2},{4,5},{5,4},{6,7},{7,6},{8,9},{9,8},{10,11... | collective-permute-start | bytes 6291464 | tf_op jit(solution)/shard_map/ppermute | solution.py:31
  40.7 1.3 copy-start.4
  44.7 20.9 %collective-permute-start.13 = (bf16[16,96,512]{2,1,0:T(8,128)(2,1)S(1)}, bf16[16,96,512]{2,1,0:T(8,128)(2,1)}, u32[]{:S(2)}, u32[]{:S(2)}) collective-permute-start(bf16[16,96,512]{2,1,0:T(8,128)(2,1)S(1)} %pad_maximum_fusion), channel_id=1, source_target_pairs={{0,2},{1,7},{2,0},{3,5},{4,6},{5,3},{6,4},{7,1},{8,10},{9,15},{10,... | collective-permute-start | bytes 4718600 | tf_op jit(solution)/shard_map/ppermute | solution.py:31
  47.1 26.6 %collective-permute-start.17 = (bf16[16,80,512]{2,1,0:T(8,128)(2,1)S(1)}, bf16[16,80,512]{2,1,0:T(8,128)(2,1)}, u32[]{:S(2)}, u32[]{:S(2)}) collective-permute-start(bf16[16,80,512]{2,1,0:T(8,128)(2,1)S(1)} %pad_maximum_fusion.2), channel_id=1, source_target_pairs={{0,16},{1,49},{2,18},{3,51},{4,20},{5,53},{6,22},{7,55},{8,24},{9,... | collective-permute-start | bytes 3932168 | tf_op jit(solution)/shard_map/ppermute | solution.py:31
  49.0 24.7 %collective-permute-start.20 = (bf16[16,80,512]{2,1,0:T(8,128)(2,1)S(1)}, bf16[16,80,512]{2,1,0:T(8,128)(2,1)}, u32[]{:S(2)}, u32[]{:S(2)}) collective-permute-start(bf16[16,80,512]{2,1,0:T(8,128)(2,1)S(1)} %pad_maximum_fusion.1), channel_id=1, source_target_pairs={{0,8},{1,73},{2,10},{3,75},{4,12},{5,77},{6,14},{7,79},{8,0},{9,65... | collective-permute-start | bytes 3932168 | tf_op jit(solution)/shard_map/ppermute | solution.py:31
  49.0 28.1 %collective-permute-start.16 = (bf16[16,80,512]{2,1,0:T(8,128)(2,1)S(1)}, bf16[16,80,512]{2,1,0:T(8,128)(2,1)S(1)}, u32[]{:S(2)}, u32[]{:S(2)}) collective-permute-start(bf16[16,80,512]{2,1,0:T(8,128)(2,1)S(1)} %pad_maximum_fusion.2), channel_id=1, source_target_pairs={{0,48},{1,17},{2,50},{3,19},{4,52},{5,21},{6,54},{7,23},{8,56},{9,... | collective-permute-start | bytes 3932168 | tf_op jit(solution)/shard_map/ppermute | solution.py:31
  65.6 39.0 %collective-permute-start.14 = (bf16[16,96,512]{2,1,0:T(8,128)(2,1)S(1)}, bf16[16,96,512]{2,1,0:T(8,128)(2,1)S(1)}, u32[]{:S(2)}, u32[]{:S(2)}) collective-permute-start(bf16[16,96,512]{2,1,0:T(8,128)(2,1)S(1)} %pad_maximum_fusion), channel_id=1, source_target_pairs={{0,6},{1,3},{2,4},{3,1},{4,2},{5,7},{6,0},{7,5},{8,14},{9,11},{10,... | collective-permute-start | bytes 4718600 | tf_op jit(solution)/shard_map/ppermute | solution.py:31
  65.6 39.0 %collective-permute-start.15 = (bf16[16,96,512]{2,1,0:T(8,128)(2,1)}, bf16[16,96,512]{2,1,0:T(8,128)(2,1)S(1)}, u32[]{:S(2)}, u32[]{:S(2)}) collective-permute-start(bf16[16,96,512]{2,1,0:T(8,128)(2,1)} %collective-permute-done.13), channel_id=1, source_target_pairs={{0,6},{1,3},{2,4},{3,1},{4,2},{5,7},{6,0},{7,5},{8,14},{9,11},{10,... | collective-permute-start | bytes 4718600 | tf_op jit(solution)/shard_map/ppermute | solution.py:31
  73.7 16.9 %collective-permute-start.19 = (bf16[16,80,512]{2,1,0:T(8,128)(2,1)S(1)}, bf16[16,80,512]{2,1,0:T(8,128)(2,1)}, u32[]{:S(2)}, u32[]{:S(2)}) collective-permute-start(bf16[16,80,512]{2,1,0:T(8,128)(2,1)S(1)} %pad_maximum_fusion.1), channel_id=1, source_target_pairs={{0,72},{1,9},{2,74},{3,11},{4,76},{5,13},{6,78},{7,15},{8,64},{9,1... | collective-permute-start | bytes 3932168 | tf_op jit(solution)/shard_map/ppermute | solution.py:31
  73.7 20.3 %collective-permute-start.18 = (bf16[16,80,512]{2,1,0:T(8,128)(2,1)}, bf16[16,80,512]{2,1,0:T(8,128)(2,1)}, u32[]{:S(2)}, u32[]{:S(2)}) collective-permute-start(bf16[16,80,512]{2,1,0:T(8,128)(2,1)} %collective-permute-done.17), channel_id=1, source_target_pairs={{0,48},{1,17},{2,50},{3,19},{4,52},{5,21},{6,54},{7,23},{8,56},{9,... | collective-permute-start | bytes 3932168 | tf_op jit(solution)/shard_map/ppermute | solution.py:31
  77.2 4.4 %copy-start = (bf16[16,80,512]{2,1,0:T(8,128)(2,1)}, bf16[16,80,512]{2,1,0:T(8,128)(2,1)S(1)}, u32[]{:S(2)}) copy-start(bf16[16,80,512]{2,1,0:T(8,128)(2,1)S(1)} %collective-permute-done.16) | copy-start | bytes 3932164
  77.2 27.4 %collective-permute-start.21 = (bf16[16,80,512]{2,1,0:T(8,128)(2,1)}, bf16[16,80,512]{2,1,0:T(8,128)(2,1)}, u32[]{:S(2)}, u32[]{:S(2)}) collective-permute-start(bf16[16,80,512]{2,1,0:T(8,128)(2,1)} %collective-permute-done.20), channel_id=1, source_target_pairs={{0,72},{1,9},{2,74},{3,11},{4,76},{5,13},{6,78},{7,15},{8,64},{9,1... | collective-permute-start | bytes 3932168 | tf_op jit(solution)/shard_map/ppermute | solution.py:31
  81.6 23.0 %copy-start.1 = (bf16[16,80,512]{2,1,0:T(8,128)(2,1)S(1)}, bf16[16,80,512]{2,1,0:T(8,128)(2,1)}, u32[]{:S(2)}) copy-start(bf16[16,80,512]{2,1,0:T(8,128)(2,1)} %copy-done) | copy-start | bytes 3932164
  109.3 15.3 %collective-permute-start.22 = (bf16[4,256,512]{2,1,0:T(8,128)(2,1)S(1)}, bf16[4,256,512]{2,1,0:T(8,128)(2,1)S(1)}, u32[]{:S(2)}, u32[]{:S(2)}) collective-permute-start(bf16[4,256,512]{2,1,0:T(8,128)(2,1)S(1)} %shard_map.50), channel_id=1, source_target_pairs={{0,1},{1,0},{2,3},{3,2},{4,5},{5,4},{6,7},{7,6},{8,9},{9,8},{10,11... | collective-permute-start | bytes 3145736 | tf_op jit(solution)/shard_map/ppermute | solution.py:31
  125.1 20.0 %copy-start.2 = (s32[8]{0:T(128)S(1)}, s32[8]{0:T(128)}, u32[]{:S(2)}) copy-start(s32[8]{0:T(128)} %owner.1) | copy-start | bytes 100
  125.1 9.2 %collective-permute-start.23 = (bf16[256,512]{1,0:T(8,128)(2,1)S(1)}, bf16[256,512]{1,0:T(8,128)(2,1)S(1)}, u32[]{:S(2)}, u32[]{:S(2)}) collective-permute-start(bf16[256,512]{1,0:T(8,128)(2,1)S(1)} %get-tuple-element.41), channel_id=1, source_target_pairs={{0,0},{1,65},{2,2},{3,67},{4,4},{5,69},{6,6},{7,71},{8,8},{9,73},{... | collective-permute-start | bytes 786440 | tf_op jit(solution)/shard_map/ppermute | solution.py:31
  128.9 9.2 %collective-permute-start.24 = (bf16[256,512]{1,0:T(8,128)(2,1)S(1)}, bf16[256,512]{1,0:T(8,128)(2,1)S(1)}, u32[]{:S(2)}, u32[]{:S(2)}) collective-permute-start(bf16[256,512]{1,0:T(8,128)(2,1)S(1)} %get-tuple-element.44), channel_id=1, source_target_pairs={{0,16},{1,81},{2,18},{3,83},{4,20},{5,85},{6,22},{7,87},{8,24},{9,... | collective-permute-start | bytes 786440 | tf_op jit(solution)/shard_map/ppermute | solution.py:31
  129.7 11.2 %collective-permute-start.25 = (bf16[256,512]{1,0:T(8,128)(2,1)S(1)}, bf16[256,512]{1,0:T(8,128)(2,1)S(1)}, u32[]{:S(2)}, u32[]{:S(2)}) collective-permute-start(bf16[256,512]{1,0:T(8,128)(2,1)S(1)} %get-tuple-element.43), channel_id=1, source_target_pairs={{0,32},{1,97},{2,34},{3,99},{4,36},{5,101},{6,38},{7,103},{8,40},{... | collective-permute-start | bytes 786440 | tf_op jit(solution)/shard_map/ppermute | solution.py:31
  134.2 8.0 %collective-permute-start.26 = (bf16[256,512]{1,0:T(8,128)(2,1)S(1)}, bf16[256,512]{1,0:T(8,128)(2,1)S(1)}, u32[]{:S(2)}, u32[]{:S(2)}) collective-permute-start(bf16[256,512]{1,0:T(8,128)(2,1)S(1)} %get-tuple-element.42), channel_id=1, source_target_pairs={{0,48},{1,113},{2,50},{3,115},{4,52},{5,117},{6,54},{7,119},{8,56}... | collective-permute-start | bytes 786440 | tf_op jit(solution)/shard_map/ppermute | solution.py:31
  142.3 2.7 %collective-permute-start.27 = (bf16[4,256,512]{2,1,0:T(8,128)(2,1)S(1)}, bf16[4,256,512]{2,1,0:T(8,128)(2,1)S(1)}, u32[]{:S(2)}, u32[]{:S(2)}) collective-permute-start(bf16[4,256,512]{2,1,0:T(8,128)(2,1)S(1)} %pad_maximum_fusion.3.own), channel_id=1, source_target_pairs={{0,1},{1,0},{2,3},{3,2},{4,5},{5,4},{6,7},{7,6},{8,9},{9,8},{10,11... | collective-permute-start | bytes 3145736 | tf_op jit(solution)/shard_map/ppermute | solution.py:31
  145.8 10.1 %collective-permute-start.28 = (bf16[256,512]{1,0:T(8,128)(2,1)S(1)}, bf16[256,512]{1,0:T(8,128)(2,1)S(1)}, u32[]{:S(2)}, u32[]{:S(2)}) collective-permute-start(bf16[256,512]{1,0:T(8,128)(2,1)S(1)} %get-tuple-element.37), channel_id=1, source_target_pairs={{0,0},{1,8},{2,2},{3,10},{4,4},{5,12},{6,6},{7,14},{8,9},{9,1},{10... | collective-permute-start | bytes 786440 | tf_op jit(solution)/shard_map/ppermute | solution.py:31
  149.4 12.8 %collective-permute-start.29 = (bf16[256,512]{1,0:T(8,128)(2,1)S(1)}, bf16[256,512]{1,0:T(8,128)(2,1)S(1)}, u32[]{:S(2)}, u32[]{:S(2)}) collective-permute-start(bf16[256,512]{1,0:T(8,128)(2,1)S(1)} %get-tuple-element.38), channel_id=1, source_target_pairs={{0,2},{1,10},{2,4},{3,12},{4,6},{5,14},{6,0},{7,8},{8,11},{9,3},{1... | collective-permute-start | bytes 786440 | tf_op jit(solution)/shard_map/ppermute | solution.py:31
  150.3 15.2 %collective-permute-start.30 = (bf16[256,512]{1,0:T(8,128)(2,1)S(1)}, bf16[256,512]{1,0:T(8,128)(2,1)S(1)}, u32[]{:S(2)}, u32[]{:S(2)}) collective-permute-start(bf16[256,512]{1,0:T(8,128)(2,1)S(1)} %get-tuple-element.39), channel_id=1, source_target_pairs={{0,4},{1,12},{2,6},{3,14},{4,0},{5,8},{6,2},{7,10},{8,13},{9,5},{1... | collective-permute-start | bytes 786440 | tf_op jit(solution)/shard_map/ppermute | solution.py:31
  152.5 13.0 %collective-permute-start.31 = (bf16[256,512]{1,0:T(8,128)(2,1)S(1)}, bf16[256,512]{1,0:T(8,128)(2,1)S(1)}, u32[]{:S(2)}, u32[]{:S(2)}) collective-permute-start(bf16[256,512]{1,0:T(8,128)(2,1)S(1)} %get-tuple-element.40), channel_id=1, source_target_pairs={{0,6},{1,14},{2,0},{3,8},{4,2},{5,10},{6,4},{7,12},{8,15},{9,7},{1... | collective-permute-start | bytes 786440 | tf_op jit(solution)/shard_map/ppermute | solution.py:31

commit v6 on v5

--- a/solution.py
+++ b/solution.py
@@ -45,20 +45,43 @@
     return permute(value, move)
 
 
+def join_kernel(*refs):
+    pairs, outs = refs[:6], refs[6:]
+    for i, out in enumerate(outs):
+        left, right = pairs[2 * i], pairs[2 * i + 1]
+        n = left.shape[0]
+        out[:n] = left[...]
+        out[n:] = right[...]
+
+
+def join(pairs):
+    vmem = pl.BlockSpec(memory_space=pltpu.VMEM)
+    shapes = [(2 * left.shape[0], *left.shape[1:]) for left, _ in pairs]
+    size = sum(left.size for left, _ in pairs)
+    return pl.pallas_call(
+        join_kernel,
+        in_specs=[vmem] * 6,
+        out_specs=[vmem] * 3,
+        out_shape=[jax.ShapeDtypeStruct(shape, jnp.bfloat16) for shape in shapes],
+        compiler_params=pltpu.CompilerParams(vmem_limit_bytes=16 * MIB),
+        cost_estimate=pl.CostEstimate(flops=0, bytes_accessed=8 * size, transcendentals=0),
+    )(*[v for pair in pairs for v in pair])
+
+
 def gather_planes(blocks):
     for level in range(2):
         for which in (1, 2):
-            blocks = {
-                part: jnp.concatenate([block, exchange(block, ORDER[part][level], which)], axis=0)
-                for part, block in blocks.items()
-            }
-            blocks = lax.optimization_barrier(blocks)
+            pairs = {part: (block, exchange(block, ORDER[part][level], which)) for part, block in blocks.items()}
+            if level == 0:
+                blocks = lax.optimization_barrier({part: jnp.concatenate(pair) for part, pair in pairs.items()})
+            else:
+                blocks = dict(zip(pairs, join(list(pairs.values()))))
     return blocks
 
 
 def gather_last(block, axis):
     first = exchange(block, axis, 1)
-    if axis == "z":
+    if axis != "y":
         first, block = lax.optimization_barrier((first, block))
     second = exchange(block, axis, 2)
     relayed = exchange(first, axis, 2)
@@ -111,7 +134,7 @@
         out_specs=pl.BlockSpec(memory_space=pltpu.VMEM),
         out_shape=jax.ShapeDtypeStruct((8 * SHARE, COLS), jnp.bfloat16),
         scratch_shapes=[pltpu.VMEM((8, SHARE, COLS), jnp.float32), pltpu.SemaphoreType.DMA((8,))],
-        compiler_params=pltpu.CompilerParams(vmem_limit_bytes=48 * MIB),
+        compiler_params=pltpu.CompilerParams(vmem_limit_bytes=44 * MIB),
         cost_estimate=pl.CostEstimate(flops=size * 6, bytes_accessed=size * 6, transcendentals=0),
     )(table, master)
 
@@ -243,7 +266,7 @@
         out_specs=vmem,
         out_shape=out,
         scratch_shapes=held,
-        compiler_params=pltpu.CompilerParams(vmem_limit_bytes=32 * MIB),
+        compiler_params=pltpu.CompilerParams(vmem_limit_bytes=20 * MIB),
         cost_estimate=pl.CostEstimate(
             flops=work * 512 * 4096 * 256, bytes_accessed=(6 + work) * MIB, transcendentals=0
         ),

time: 168 us -> 164 us (0.976)
  waiting for transfers between devices: 76.6 us -> 69.4 us
  other arithmetic: 5.7 us -> 0.65 us
  starting transfers between devices: 58.5 us -> 62.9 us
  Pallas kernels: 23.4 us -> 25.9 us
    ppermute x32, waiting for transfers between devices: 76.6 us -> 69.4 us  [permute(): lax.ppermute(value, AXES, [(i, move(*coords(i))) for i in range(N_DEV)])]
    concatenate x12 -> x6, other arithmetic: 5.2 us -> 0.15 us  [gather_planes(): jnp.concatenate(pair)]
    ppermute x32, starting transfers between devices: 58.5 us -> 62.9 us  [permute(): lax.ppermute(value, AXES, [(i, move(*coords(i))) for i in range(N_DEV)])]
    pallas_call x0 -> x2, Pallas kernels: none -> 1.69 us  [join(): pl.pallas_call(join_kernel, in_specs=[vmem] * 6, out_specs=[vmem] * 3, ou...]
  transfers between devices with their start and end apart: 32 -> 32, of which waited for: 19 -> 16; matrix products, arithmetic and copies ran while one was open for 3% -> 1% of each run, Pallas kernels for 10% -> 11%
where the time goes in v6:
time: 164 us; the launch traced here: 163 us
  waiting for transfers between devices  69.4 us (42%)
  starting transfers between devices  62.9 us (38%)
  Pallas kernels  25.9 us (16%)
  local copies, waits for them, and re-layouts  3.7 us (2%)
    ppermute x32, waiting for transfers between devices, permute(): lax.ppermute(value, AXES, [(i, move(*coords(i))) for i in range(N_DEV)])  69.4 us
    ppermute x32, starting transfers between devices, permute(): lax.ppermute(value, AXES, [(i, move(*coords(i))) for i in range(N_DEV)])  62.9 us
    pallas_call x3, Pallas kernels, product(): pl.pallas_call(kernel, in_specs=[pl.BlockSpec(memory_space=pltpu.SMEM)] +...  15.4 us
    pallas_call x2, Pallas kernels, refit(): pl.pallas_call(functools.partial(refit_kernel, first), in_specs=[pl.Block...  6.55 us
  transfers between devices with their start and end apart: 32, of which 16 were waited for; matrix products, arithmetic and copies ran while one was open for 1% of the time, Pallas kernels for 11%

profile of v6, /device:TPU:3, one launch (start us, length us, event | category | flops | bytes accessed | tf_op | source)
XLA Modules:
  0.0 163.0 jit_solution(8992583462198405588)
XLA Ops:
  0.0 0.9 slice_bitcast_fusion.5
  0.9 2.8 %collective-permute-start.1 = (bf16[1,80,512]{2,1,0:T(8,128)(2,1)S(1)}, bf16[1,80,512]{2,1,0:T(8,128)(2,1)S(1)}, u32[]{:S(2)}, u32[]{:S(2)}) collective-permute-start(bf16[1,80,512]{2,1,0:T(8,128)(2,1)S(1)} %get-tuple-element.50), channel_id=1, source_target_pairs={{0,16},{1,49},{2,18},{3,51},{4,20},{5,53},{6,22},{7,55},{8,24},{9,... | collective-permute-start | bytes 245768 | tf_op jit(solution)/shard_map/ppermute | solution.py:31
  3.8 3.8 %collective-permute-start.2 = (bf16[1,80,512]{2,1,0:T(8,128)(2,1)S(1)}, bf16[1,80,512]{2,1,0:T(8,128)(2,1)S(1)}, u32[]{:S(2)}, u32[]{:S(2)}) collective-permute-start(bf16[1,80,512]{2,1,0:T(8,128)(2,1)S(1)} %get-tuple-element.49), channel_id=1, source_target_pairs={{0,2},{1,7},{2,0},{3,5},{4,6},{5,3},{6,4},{7,1},{8,10},{9,15},{10,... | collective-permute-start | bytes 245768 | tf_op jit(solution)/shard_map/ppermute | solution.py:31
  7.5 0.9 slice_bitcast_fusion.4
  8.4 1.2 collective-permute-start.3
  9.7 2.2 %collective-permute-done.3 = bf16[1,96,512]{2,1,0:T(8,128)(2,1)S(1)} collective-permute-done((bf16[1,96,512]{2,1,0:T(8,128)(2,1)S(1)}, bf16[1,96,512]{2,1,0:T(8,128)(2,1)S(1)}, u32[]{:S(2)}, u32[]{:S(2)}) %collective-permute-start.3) | collective-permute-done | bytes 98336 | tf_op jit(solution)/shard_map/ppermute | solution.py:31
  11.9 0.1 collective-permute-start.4
  12.0 0.1 collective-permute-start.5
  12.1 1.5 collective-permute-start.6
  13.6 2.8 %collective-permute-done.4 = bf16[2,80,512]{2,1,0:T(8,128)(2,1)S(1)} collective-permute-done((bf16[2,80,512]{2,1,0:T(8,128)(2,1)S(1)}, bf16[2,80,512]{2,1,0:T(8,128)(2,1)S(1)}, u32[]{:S(2)}, u32[]{:S(2)}) %collective-permute-start.4) | collective-permute-done | bytes 163872 | tf_op jit(solution)/shard_map/ppermute | solution.py:31
  16.5 0.1 collective-permute-done.5
  16.6 0.4 collective-permute-done.6
  17.0 0.9 collective-permute-start.9
  17.9 1.6 collective-permute-start.8
  19.4 5.6 %collective-permute-done.7.refs_1_ = bf16[4,80,512]{2,1,0:T(8,128)(2,1)S(1)} collective-permute-done((bf16[4,80,512]{2,1,0:T(8,128)(2,1)S(1)}, bf16[4,80,512]{2,1,0:T(8,128)(2,1)S(1)}, u32[]{:S(2)}, u32[]{:S(2)}) %collective-permute-start.7) | collective-permute-done | bytes 327712 | tf_op jit(solution)/shard_map/ppermute | solution.py:31
  25.0 0.1 shard_map.48
  25.1 0.0 copy-start
  25.1 0.7 collective-permute-start.12
  25.9 1.0 collective-permute-start.10
  26.9 1.7 %collective-permute-start.11 = (bf16[8,80,512]{2,1,0:T(8,128)(2,1)S(1)}, bf16[8,80,512]{2,1,0:T(8,128)(2,1)}, u32[]{:S(2)}, u32[]{:S(2)}) collective-permute-start(bf16[8,80,512]{2,1,0:T(8,128)(2,1)S(1)} %get-tuple-element.32.refs_2_), channel_id=1, source_target_pairs={{0,72},{1,9},{2,74},{3,11},{4,76},{5,13},{6,78},{7,15},{8,64},{9,1... | collective-permute-start | bytes 1966088 | tf_op jit(solution)/shard_map/ppermute | solution.py:31
  28.6 0.7 dynamic-slice_bitcast_fusion.table
  29.3 3.3 %shard_map.47 = bf16[4096,256]{1,0:T(8,128)(2,1)S(1)} custom-call(s32[28]{0:T(128)S(1)} %dynamic-slice_bitcast_fusion.table, f32[8192,256]{1,0:T(8,128)} %master.3), custom_call_target="tpu_custom_call" | custom-call | flops 6291456 | bytes 6291456 | tf_op jit(solution)/shard_map/pallas_call | solution.py:131
  32.6 5.1 %collective-permute-start = (bf16[4096,256]{1,0:T(8,128)(2,1)S(1)}, bf16[4096,256]{1,0:T(8,128)(2,1)S(1)}, u32[]{:S(2)}, u32[]{:S(2)}) collective-permute-start(bf16[4096,256]{1,0:T(8,128)(2,1)S(1)} %shard_map.47), channel_id=1, source_target_pairs={{0,1},{1,0},{2,3},{3,2},{4,5},{5,4},{6,7},{7,6},{8,9},{9,8},{10,11... | collective-permute-start | bytes 6291464 | tf_op jit(solution)/shard_map/ppermute | solution.py:31
  37.7 0.0 copy-start.1
  37.7 1.1 copy-done.1
  38.8 1.6 shard_map.49
  40.3 2.3 %collective-permute-start.13 = (bf16[16,96,512]{2,1,0:T(8,128)(2,1)S(1)}, bf16[16,96,512]{2,1,0:T(8,128)(2,1)S(1)}, u32[]{:S(2)}, u32[]{:S(2)}) collective-permute-start(bf16[16,96,512]{2,1,0:T(8,128)(2,1)S(1)} %get-tuple-element.35), channel_id=1, source_target_pairs={{0,2},{1,7},{2,0},{3,5},{4,6},{5,3},{6,4},{7,1},{8,10},{9,15},{10,... | collective-permute-start | bytes 4718600 | tf_op jit(solution)/shard_map/ppermute | solution.py:31
  42.7 0.9 collective-permute-start.19
  43.5 2.0 %collective-permute-start.17 = (bf16[16,80,512]{2,1,0:T(8,128)(2,1)S(1)}, bf16[16,80,512]{2,1,0:T(8,128)(2,1)}, u32[]{:S(2)}, u32[]{:S(2)}) collective-permute-start(bf16[16,80,512]{2,1,0:T(8,128)(2,1)S(1)} %get-tuple-element.37), channel_id=1, source_target_pairs={{0,16},{1,49},{2,18},{3,51},{4,20},{5,53},{6,22},{7,55},{8,24},{9,... | collective-permute-start | bytes 3932168 | tf_op jit(solution)/shard_map/ppermute | solution.py:31
  45.5 0.1 collective-permute-start.16
  45.6 15.6 %collective-permute-done.13 = bf16[16,96,512]{2,1,0:T(8,128)(2,1)S(1)} collective-permute-done((bf16[16,96,512]{2,1,0:T(8,128)(2,1)S(1)}, bf16[16,96,512]{2,1,0:T(8,128)(2,1)S(1)}, u32[]{:S(2)}, u32[]{:S(2)}) %collective-permute-start.13) | collective-permute-done | bytes 1572896 | tf_op jit(solution)/shard_map/ppermute | solution.py:31
  61.2 1.5 collective-permute-start.15
  62.6 2.3 %collective-permute-start.20 = (bf16[16,80,512]{2,1,0:T(8,128)(2,1)S(1)}, bf16[16,80,512]{2,1,0:T(8,128)(2,1)S(1)}, u32[]{:S(2)}, u32[]{:S(2)}) collective-permute-start(bf16[16,80,512]{2,1,0:T(8,128)(2,1)S(1)} %get-tuple-element.39), channel_id=1, source_target_pairs={{0,72},{1,9},{2,74},{3,11},{4,76},{5,13},{6,78},{7,15},{8,64},{9,1... | collective-permute-start | bytes 3932168 | tf_op jit(solution)/shard_map/ppermute | solution.py:31
  65.0 3.7 %collective-permute-done.17 = bf16[16,80,512]{2,1,0:T(8,128)(2,1)} collective-permute-done((bf16[16,80,512]{2,1,0:T(8,128)(2,1)S(1)}, bf16[16,80,512]{2,1,0:T(8,128)(2,1)}, u32[]{:S(2)}, u32[]{:S(2)}) %collective-permute-start.17) | collective-permute-done | bytes 1310752 | tf_op jit(solution)/shard_map/ppermute | solution.py:31
  68.7 4.2 %collective-permute-start.21 = (bf16[16,80,512]{2,1,0:T(8,128)(2,1)S(1)}, bf16[16,80,512]{2,1,0:T(8,128)(2,1)S(1)}, u32[]{:S(2)}, u32[]{:S(2)}) collective-permute-start(bf16[16,80,512]{2,1,0:T(8,128)(2,1)S(1)} %collective-permute-done.19), channel_id=1, source_target_pairs={{0,72},{1,9},{2,74},{3,11},{4,76},{5,13},{6,78},{7,15},{8,64},{9,1... | collective-permute-start | bytes 3932168 | tf_op jit(solution)/shard_map/ppermute | solution.py:31
  72.9 3.3 %shard_map.46.mine = bf16[4096,256]{1,0:T(8,128)(2,1)S(1)} custom-call(s32[28]{0:T(128)S(1)} %dynamic-slice_bitcast_fusion.table, f32[8192,256]{1,0:T(8,128)} %master.3), custom_call_target="tpu_custom_call" | custom-call | flops 6291456 | bytes 6291456 | tf_op jit(solution)/shard_map/pallas_call | solution.py:131
  76.2 6.2 %shard_map.50.early = f32[2,4,256,512]{3,2,1,0:T(8,128)S(1)} custom-call(s32[28]{0:T(128)S(1)} %dynamic-slice_bitcast_fusion.table, bf16[4096,256]{1,0:T(8,128)(2,1)S(1)} %shard_map.46.mine, bf16[4096,256]{1,0:T(8,128)(2,1)S(1)} %collective-permute-done.theirs, bf16[4,4,96,512]{3,2,1,0:T(8,128)(2,1)S(1)} %bitcast.44, bf16[4,4,96,512]{3,2,1,0:T(8,128)(2,1)S(1)} %bitcast.45, ...), custom_call_target="tpu_custom_call" | custom-call | flops 4294967296 | bytes 14680064 | tf_op jit(solution)/shard_map/pallas_call | solution.py:263
  82.4 11.9 %collective-permute-done.21 = bf16[16,80,512]{2,1,0:T(8,128)(2,1)S(1)} collective-permute-done((bf16[16,80,512]{2,1,0:T(8,128)(2,1)S(1)}, bf16[16,80,512]{2,1,0:T(8,128)(2,1)S(1)}, u32[]{:S(2)}, u32[]{:S(2)}) %collective-permute-start.21) | collective-permute-done | bytes 1310752 | tf_op jit(solution)/shard_map/ppermute | solution.py:31
  94.3 5.6 %collective-permute-done.15 = bf16[16,96,512]{2,1,0:T(8,128)(2,1)S(1)} collective-permute-done((bf16[16,96,512]{2,1,0:T(8,128)(2,1)S(1)}, bf16[16,96,512]{2,1,0:T(8,128)(2,1)S(1)}, u32[]{:S(2)}, u32[]{:S(2)}) %collective-permute-start.15) | collective-permute-done | bytes 1572896 | tf_op jit(solution)/shard_map/ppermute | solution.py:31
  100.0 4.9 %shard_map.52 = bf16[4,256,512]{2,1,0:T(8,128)(2,1)S(1)} custom-call(s32[28]{0:T(128)S(1)} %dynamic-slice_bitcast_fusion.table, bf16[4096,256]{1,0:T(8,128)(2,1)S(1)} %shard_map.46.mine, bf16[4096,256]{1,0:T(8,128)(2,1)S(1)} %collective-permute-done.theirs, bf16[4,4,96,512]{3,2,1,0:T(8,128)(2,1)S(1)} %bitcast.32, bf16[4,4,96,512]{3,2,1,0:T(8,128)(2,1)S(1)} %bitcast.34, ...), custom_call_target="tpu_custom_call" | custom-call | flops 4294967296 | bytes 14680064 | tf_op jit(solution)/shard_map/pallas_call | solution.py:263
  104.9 8.6 %collective-permute-start.22 = (bf16[4,256,512]{2,1,0:T(8,128)(2,1)S(1)}, bf16[4,256,512]{2,1,0:T(8,128)(2,1)S(1)}, u32[]{:S(2)}, u32[]{:S(2)}) collective-permute-start(bf16[4,256,512]{2,1,0:T(8,128)(2,1)S(1)} %shard_map.52), channel_id=1, source_target_pairs={{0,1},{1,0},{2,3},{3,2},{4,5},{5,4},{6,7},{7,6},{8,9},{9,8},{10,11... | collective-permute-start | bytes 3145736 | tf_op jit(solution)/shard_map/ppermute | solution.py:31
  113.4 4.4 %shard_map.51 = f32[4,256,512]{2,1,0:T(8,128)S(1)} custom-call(s32[28]{0:T(128)S(1)} %dynamic-slice_bitcast_fusion.table, bf16[4096,256]{1,0:T(8,128)(2,1)S(1)} %shard_map.46.mine, bf16[4096,256]{1,0:T(8,128)(2,1)S(1)} %collective-permute-done.theirs, bf16[4,4,96,512]{3,2,1,0:T(8,128)(2,1)S(1)} %bitcast.33, bf16[4,4,96,512]{3,2,1,0:T(8,128)(2,1)S(1)} %bitcast.35, ...), custom_call_target="tpu_custom_call" | custom-call | flops 4294967296 | bytes 14680064 | tf_op jit(solution)/shard_map/pallas_call | solution.py:263
  117.8 0.4 add_convert_fusion
  118.2 0.1 slice_bitcast_fusion.3
  118.3 0.0 copy-start.2
  118.3 5.6 %collective-permute-start.23 = (bf16[256,512]{1,0:T(8,128)(2,1)S(1)}, bf16[256,512]{1,0:T(8,128)(2,1)S(1)}, u32[]{:S(2)}, u32[]{:S(2)}) collective-permute-start(bf16[256,512]{1,0:T(8,128)(2,1)S(1)} %get-tuple-element.45), channel_id=1, source_target_pairs={{0,0},{1,65},{2,2},{3,67},{4,4},{5,69},{6,6},{7,71},{8,8},{9,73},{... | collective-permute-start | bytes 786440 | tf_op jit(solution)/shard_map/ppermute | solution.py:31
  123.9 0.9 collective-permute-start.24
  124.8 5.5 %collective-permute-start.25 = (bf16[256,512]{1,0:T(8,128)(2,1)S(1)}, bf16[256,512]{1,0:T(8,128)(2,1)S(1)}, u32[]{:S(2)}, u32[]{:S(2)}) collective-permute-start(bf16[256,512]{1,0:T(8,128)(2,1)S(1)} %get-tuple-element.47), channel_id=1, source_target_pairs={{0,32},{1,97},{2,34},{3,99},{4,36},{5,101},{6,38},{7,103},{8,40},{... | collective-permute-start | bytes 786440 | tf_op jit(solution)/shard_map/ppermute | solution.py:31
  130.3 0.9 collective-permute-start.26
  131.2 1.7 %collective-permute-done.24 = bf16[256,512]{1,0:T(8,128)(2,1)S(1)} collective-permute-done((bf16[256,512]{1,0:T(8,128)(2,1)S(1)}, bf16[256,512]{1,0:T(8,128)(2,1)S(1)}, u32[]{:S(2)}, u32[]{:S(2)}) %collective-permute-start.24) | collective-permute-done | bytes 262176 | tf_op jit(solution)/shard_map/ppermute | solution.py:31
  132.9 3.9 %collective-permute-done.25 = bf16[256,512]{1,0:T(8,128)(2,1)S(1)} collective-permute-done((bf16[256,512]{1,0:T(8,128)(2,1)S(1)}, bf16[256,512]{1,0:T(8,128)(2,1)S(1)}, u32[]{:S(2)}, u32[]{:S(2)}) %collective-permute-start.25) | collective-permute-done | bytes 262176 | tf_op jit(solution)/shard_map/ppermute | solution.py:31
  136.8 1.6 collective-permute-done.26
  138.4 0.1 pad_maximum_fusion.own
  138.6 0.1 collective-permute-start.27
  138.7 2.6 %collective-permute-done.27.other = bf16[4,256,512]{2,1,0:T(8,128)(2,1)S(1)} collective-permute-done((bf16[4,256,512]{2,1,0:T(8,128)(2,1)S(1)}, bf16[4,256,512]{2,1,0:T(8,128)(2,1)S(1)}, u32[]{:S(2)}, u32[]{:S(2)}) %collective-permute-start.27) | collective-permute-done | bytes 1048608 | tf_op jit(solution)/shard_map/ppermute | solution.py:31
  141.3 0.7 shard_map.53
  142.0 1.9 %collective-permute-start.28 = (bf16[256,512]{1,0:T(8,128)(2,1)S(1)}, bf16[256,512]{1,0:T(8,128)(2,1)S(1)}, u32[]{:S(2)}, u32[]{:S(2)}) collective-permute-start(bf16[256,512]{1,0:T(8,128)(2,1)S(1)} %get-tuple-element.41), channel_id=1, source_target_pairs={{0,0},{1,8},{2,2},{3,10},{4,4},{5,12},{6,6},{7,14},{8,9},{9,1},{10... | collective-permute-start | bytes 786440 | tf_op jit(solution)/shard_map/ppermute | solution.py:31
  143.9 1.5 collective-permute-start.29
  145.5 4.0 %collective-permute-start.30 = (bf16[256,512]{1,0:T(8,128)(2,1)S(1)}, bf16[256,512]{1,0:T(8,128)(2,1)S(1)}, u32[]{:S(2)}, u32[]{:S(2)}) collective-permute-start(bf16[256,512]{1,0:T(8,128)(2,1)S(1)} %get-tuple-element.43), channel_id=1, source_target_pairs={{0,4},{1,12},{2,6},{3,14},{4,0},{5,8},{6,2},{7,10},{8,13},{9,5},{1... | collective-permute-start | bytes 786440 | tf_op jit(solution)/shard_map/ppermute | solution.py:31
  149.4 0.2 collective-permute-start.31
  149.6 1.8 %collective-permute-done.29.refs_1_ = bf16[256,512]{1,0:T(8,128)(2,1)S(1)} collective-permute-done((bf16[256,512]{1,0:T(8,128)(2,1)S(1)}, bf16[256,512]{1,0:T(8,128)(2,1)S(1)}, u32[]{:S(2)}, u32[]{:S(2)}) %collective-permute-start.29) | collective-permute-done | bytes 262176 | tf_op jit(solution)/shard_map/ppermute | solution.py:31
  151.4 9.5 %collective-permute-done.30.refs_2_ = bf16[256,512]{1,0:T(8,128)(2,1)S(1)} collective-permute-done((bf16[256,512]{1,0:T(8,128)(2,1)S(1)}, bf16[256,512]{1,0:T(8,128)(2,1)S(1)}, u32[]{:S(2)}, u32[]{:S(2)}) %collective-permute-start.30) | collective-permute-done | bytes 262176 | tf_op jit(solution)/shard_map/ppermute | solution.py:31
  160.9 0.4 collective-permute-done.31.refs_3_
  161.3 1.5 shard_map.54
  (27 shorter events, 0.2 us)
Async XLA Ops:
  0.9 8.7 %collective-permute-start.1 = (bf16[1,80,512]{2,1,0:T(8,128)(2,1)S(1)}, bf16[1,80,512]{2,1,0:T(8,128)(2,1)S(1)}, u32[]{:S(2)}, u32[]{:S(2)}) collective-permute-start(bf16[1,80,512]{2,1,0:T(8,128)(2,1)S(1)} %get-tuple-element.50), channel_id=1, source_target_pairs={{0,16},{1,49},{2,18},{3,51},{4,20},{5,53},{6,22},{7,55},{8,24},{9,... | collective-permute-start | bytes 245768 | tf_op jit(solution)/shard_map/ppermute | solution.py:31
  3.8 5.9 %collective-permute-start.2 = (bf16[1,80,512]{2,1,0:T(8,128)(2,1)S(1)}, bf16[1,80,512]{2,1,0:T(8,128)(2,1)S(1)}, u32[]{:S(2)}, u32[]{:S(2)}) collective-permute-start(bf16[1,80,512]{2,1,0:T(8,128)(2,1)S(1)} %get-tuple-element.49), channel_id=1, source_target_pairs={{0,2},{1,7},{2,0},{3,5},{4,6},{5,3},{6,4},{7,1},{8,10},{9,15},{10,... | collective-permute-start | bytes 245768 | tf_op jit(solution)/shard_map/ppermute | solution.py:31
  8.4 3.5 %collective-permute-start.3 = (bf16[1,96,512]{2,1,0:T(8,128)(2,1)S(1)}, bf16[1,96,512]{2,1,0:T(8,128)(2,1)S(1)}, u32[]{:S(2)}, u32[]{:S(2)}) collective-permute-start(bf16[1,96,512]{2,1,0:T(8,128)(2,1)S(1)} %slice_bitcast_fusion.4), channel_id=1, source_target_pairs={{0,8},{1,73},{2,10},{3,75},{4,12},{5,77},{6,14},{7,79},{8,0},{9,65... | collective-permute-start | bytes 294920 | tf_op jit(solution)/shard_map/ppermute | solution.py:31
  11.9 4.5 %collective-permute-start.4 = (bf16[2,80,512]{2,1,0:T(8,128)(2,1)S(1)}, bf16[2,80,512]{2,1,0:T(8,128)(2,1)S(1)}, u32[]{:S(2)}, u32[]{:S(2)}) collective-permute-start(bf16[2,80,512]{2,1,0:T(8,128)(2,1)S(1)} %pad_maximum_fusion.5), channel_id=1, source_target_pairs={{0,48},{1,17},{2,50},{3,19},{4,52},{5,21},{6,54},{7,23},{8,56},{9,... | collective-permute-start | bytes 491528 | tf_op jit(solution)/shard_map/ppermute | solution.py:31
  12.0 4.5 %collective-permute-start.5 = (bf16[2,80,512]{2,1,0:T(8,128)(2,1)S(1)}, bf16[2,80,512]{2,1,0:T(8,128)(2,1)S(1)}, u32[]{:S(2)}, u32[]{:S(2)}) collective-permute-start(bf16[2,80,512]{2,1,0:T(8,128)(2,1)S(1)} %pad_maximum_fusion.6), channel_id=1, source_target_pairs={{0,6},{1,3},{2,4},{3,1},{4,2},{5,7},{6,0},{7,5},{8,14},{9,11},{10,... | collective-permute-start | bytes 491528 | tf_op jit(solution)/shard_map/ppermute | solution.py:31
  12.1 4.9 %collective-permute-start.6 = (bf16[2,96,512]{2,1,0:T(8,128)(2,1)S(1)}, bf16[2,96,512]{2,1,0:T(8,128)(2,1)S(1)}, u32[]{:S(2)}, u32[]{:S(2)}) collective-permute-start(bf16[2,96,512]{2,1,0:T(8,128)(2,1)S(1)} %pad_maximum_fusion.4), channel_id=1, source_target_pairs={{0,72},{1,9},{2,74},{3,11},{4,76},{5,13},{6,78},{7,15},{8,64},{9,1... | collective-permute-start | bytes 589832 | tf_op jit(solution)/shard_map/ppermute | solution.py:31
  17.0 8.0 %collective-permute-start.9 = (bf16[4,96,512]{2,1,0:T(8,128)(2,1)S(1)}, bf16[4,96,512]{2,1,0:T(8,128)(2,1)S(1)}, u32[]{:S(2)}, u32[]{:S(2)}) collective-permute-start(bf16[4,96,512]{2,1,0:T(8,128)(2,1)S(1)} %pad_maximum_fusion.1.refs_4_), channel_id=1, source_target_pairs={{0,16},{1,49},{2,18},{3,51},{4,20},{5,53},{6,22},{7,55},{8,24},{9,... | collective-permute-start | bytes 1179656 | tf_op jit(solution)/shard_map/ppermute | solution.py:31
  17.9 7.1 %collective-permute-start.7 = (bf16[4,80,512]{2,1,0:T(8,128)(2,1)S(1)}, bf16[4,80,512]{2,1,0:T(8,128)(2,1)S(1)}, u32[]{:S(2)}, u32[]{:S(2)}) collective-permute-start(bf16[4,80,512]{2,1,0:T(8,128)(2,1)S(1)} %pad_maximum_fusion.2.refs_0_), channel_id=1, source_target_pairs={{0,2},{1,7},{2,0},{3,5},{4,6},{5,3},{6,4},{7,1},{8,10},{9,15},{10,... | collective-permute-start | bytes 983048 | tf_op jit(solution)/shard_map/ppermute | solution.py:31
  17.9 7.1 %collective-permute-start.8 = (bf16[4,80,512]{2,1,0:T(8,128)(2,1)S(1)}, bf16[4,80,512]{2,1,0:T(8,128)(2,1)S(1)}, u32[]{:S(2)}, u32[]{:S(2)}) collective-permute-start(bf16[4,80,512]{2,1,0:T(8,128)(2,1)S(1)} %pad_maximum_fusion.3.refs_2_), channel_id=1, source_target_pairs={{0,8},{1,73},{2,10},{3,75},{4,12},{5,77},{6,14},{7,79},{8,0},{9,65... | collective-permute-start | bytes 983048 | tf_op jit(solution)/shard_map/ppermute | solution.py:31
  25.1 7.4 %copy-start = (bf16[8,80,512]{2,1,0:T(8,128)(2,1)}, bf16[8,80,512]{2,1,0:T(8,128)(2,1)S(1)}, u32[]{:S(2)}) copy-start(bf16[8,80,512]{2,1,0:T(8,128)(2,1)S(1)} %get-tuple-element.32.refs_2_) | copy-start | bytes 1966084
  25.1 12.5 %collective-permute-start.12 = (bf16[8,96,512]{2,1,0:T(8,128)(2,1)S(1)}, bf16[8,96,512]{2,1,0:T(8,128)(2,1)S(1)}, u32[]{:S(2)}, u32[]{:S(2)}) collective-permute-start(bf16[8,96,512]{2,1,0:T(8,128)(2,1)S(1)} %get-tuple-element.33.refs_4_), channel_id=1, source_target_pairs={{0,48},{1,17},{2,50},{3,19},{4,52},{5,21},{6,54},{7,23},{8,56},{9,... | collective-permute-start | bytes 2359304 | tf_op jit(solution)/shard_map/ppermute | solution.py:31
  25.9 11.8 %collective-permute-start.10 = (bf16[8,80,512]{2,1,0:T(8,128)(2,1)S(1)}, bf16[8,80,512]{2,1,0:T(8,128)(2,1)}, u32[]{:S(2)}, u32[]{:S(2)}) collective-permute-start(bf16[8,80,512]{2,1,0:T(8,128)(2,1)S(1)} %get-tuple-element.31.refs_0_), channel_id=1, source_target_pairs={{0,6},{1,3},{2,4},{3,1},{4,2},{5,7},{6,0},{7,5},{8,14},{9,11},{10,... | collective-permute-start | bytes 1966088 | tf_op jit(solution)/shard_map/ppermute | solution.py:31
  26.9 10.7 %collective-permute-start.11 = (bf16[8,80,512]{2,1,0:T(8,128)(2,1)S(1)}, bf16[8,80,512]{2,1,0:T(8,128)(2,1)}, u32[]{:S(2)}, u32[]{:S(2)}) collective-permute-start(bf16[8,80,512]{2,1,0:T(8,128)(2,1)S(1)} %get-tuple-element.32.refs_2_), channel_id=1, source_target_pairs={{0,72},{1,9},{2,74},{3,11},{4,76},{5,13},{6,78},{7,15},{8,64},{9,1... | collective-permute-start | bytes 1966088 | tf_op jit(solution)/shard_map/ppermute | solution.py:31
  32.6 30.1 %collective-permute-start = (bf16[4096,256]{1,0:T(8,128)(2,1)S(1)}, bf16[4096,256]{1,0:T(8,128)(2,1)S(1)}, u32[]{:S(2)}, u32[]{:S(2)}) collective-permute-start(bf16[4096,256]{1,0:T(8,128)(2,1)S(1)} %shard_map.47), channel_id=1, source_target_pairs={{0,1},{1,0},{2,3},{3,2},{4,5},{5,4},{6,7},{7,6},{8,9},{9,8},{10,11... | collective-permute-start | bytes 6291464 | tf_op jit(solution)/shard_map/ppermute | solution.py:31
  37.7 1.1 copy-start.1
  40.3 20.9 %collective-permute-start.13 = (bf16[16,96,512]{2,1,0:T(8,128)(2,1)S(1)}, bf16[16,96,512]{2,1,0:T(8,128)(2,1)S(1)}, u32[]{:S(2)}, u32[]{:S(2)}) collective-permute-start(bf16[16,96,512]{2,1,0:T(8,128)(2,1)S(1)} %get-tuple-element.35), channel_id=1, source_target_pairs={{0,2},{1,7},{2,0},{3,5},{4,6},{5,3},{6,4},{7,1},{8,10},{9,15},{10,... | collective-permute-start | bytes 4718600 | tf_op jit(solution)/shard_map/ppermute | solution.py:31
  42.7 18.5 %collective-permute-start.19 = (bf16[16,80,512]{2,1,0:T(8,128)(2,1)S(1)}, bf16[16,80,512]{2,1,0:T(8,128)(2,1)S(1)}, u32[]{:S(2)}, u32[]{:S(2)}) collective-permute-start(bf16[16,80,512]{2,1,0:T(8,128)(2,1)S(1)} %get-tuple-element.39), channel_id=1, source_target_pairs={{0,8},{1,73},{2,10},{3,75},{4,12},{5,77},{6,14},{7,79},{8,0},{9,65... | collective-permute-start | bytes 3932168 | tf_op jit(solution)/shard_map/ppermute | solution.py:31
  43.5 25.2 %collective-permute-start.17 = (bf16[16,80,512]{2,1,0:T(8,128)(2,1)S(1)}, bf16[16,80,512]{2,1,0:T(8,128)(2,1)}, u32[]{:S(2)}, u32[]{:S(2)}) collective-permute-start(bf16[16,80,512]{2,1,0:T(8,128)(2,1)S(1)} %get-tuple-element.37), channel_id=1, source_target_pairs={{0,16},{1,49},{2,18},{3,51},{4,20},{5,53},{6,22},{7,55},{8,24},{9,... | collective-permute-start | bytes 3932168 | tf_op jit(solution)/shard_map/ppermute | solution.py:31
  45.5 27.4 %collective-permute-start.16 = (bf16[16,80,512]{2,1,0:T(8,128)(2,1)S(1)}, bf16[16,80,512]{2,1,0:T(8,128)(2,1)S(1)}, u32[]{:S(2)}, u32[]{:S(2)}) collective-permute-start(bf16[16,80,512]{2,1,0:T(8,128)(2,1)S(1)} %get-tuple-element.37), channel_id=1, source_target_pairs={{0,48},{1,17},{2,50},{3,19},{4,52},{5,21},{6,54},{7,23},{8,56},{9,... | collective-permute-start | bytes 3932168 | tf_op jit(solution)/shard_map/ppermute | solution.py:31
  61.2 33.2 %collective-permute-start.14 = (bf16[16,96,512]{2,1,0:T(8,128)(2,1)S(1)}, bf16[16,96,512]{2,1,0:T(8,128)(2,1)S(1)}, u32[]{:S(2)}, u32[]{:S(2)}) collective-permute-start(bf16[16,96,512]{2,1,0:T(8,128)(2,1)S(1)} %get-tuple-element.35), channel_id=1, source_target_pairs={{0,6},{1,3},{2,4},{3,1},{4,2},{5,7},{6,0},{7,5},{8,14},{9,11},{10,... | collective-permute-start | bytes 4718600 | tf_op jit(solution)/shard_map/ppermute | solution.py:31
  61.2 38.8 %collective-permute-start.15 = (bf16[16,96,512]{2,1,0:T(8,128)(2,1)S(1)}, bf16[16,96,512]{2,1,0:T(8,128)(2,1)S(1)}, u32[]{:S(2)}, u32[]{:S(2)}) collective-permute-start(bf16[16,96,512]{2,1,0:T(8,128)(2,1)S(1)} %collective-permute-done.13), channel_id=1, source_target_pairs={{0,6},{1,3},{2,4},{3,1},{4,2},{5,7},{6,0},{7,5},{8,14},{9,11},{10,... | collective-permute-start | bytes 4718600 | tf_op jit(solution)/shard_map/ppermute | solution.py:31
  62.6 19.7 %collective-permute-start.20 = (bf16[16,80,512]{2,1,0:T(8,128)(2,1)S(1)}, bf16[16,80,512]{2,1,0:T(8,128)(2,1)S(1)}, u32[]{:S(2)}, u32[]{:S(2)}) collective-permute-start(bf16[16,80,512]{2,1,0:T(8,128)(2,1)S(1)} %get-tuple-element.39), channel_id=1, source_target_pairs={{0,72},{1,9},{2,74},{3,11},{4,76},{5,13},{6,78},{7,15},{8,64},{9,1... | collective-permute-start | bytes 3932168 | tf_op jit(solution)/shard_map/ppermute | solution.py:31
  68.7 25.6 %collective-permute-start.21 = (bf16[16,80,512]{2,1,0:T(8,128)(2,1)S(1)}, bf16[16,80,512]{2,1,0:T(8,128)(2,1)S(1)}, u32[]{:S(2)}, u32[]{:S(2)}) collective-permute-start(bf16[16,80,512]{2,1,0:T(8,128)(2,1)S(1)} %collective-permute-done.19), channel_id=1, source_target_pairs={{0,72},{1,9},{2,74},{3,11},{4,76},{5,13},{6,78},{7,15},{8,64},{9,1... | collective-permute-start | bytes 3932168 | tf_op jit(solution)/shard_map/ppermute | solution.py:31
  72.9 21.4 %collective-permute-start.18 = (bf16[16,80,512]{2,1,0:T(8,128)(2,1)}, bf16[16,80,512]{2,1,0:T(8,128)(2,1)S(1)}, u32[]{:S(2)}, u32[]{:S(2)}) collective-permute-start(bf16[16,80,512]{2,1,0:T(8,128)(2,1)} %collective-permute-done.17), channel_id=1, source_target_pairs={{0,48},{1,17},{2,50},{3,19},{4,52},{5,21},{6,54},{7,23},{8,56},{9,... | collective-permute-start | bytes 3932168 | tf_op jit(solution)/shard_map/ppermute | solution.py:31
  104.9 12.9 %collective-permute-start.22 = (bf16[4,256,512]{2,1,0:T(8,128)(2,1)S(1)}, bf16[4,256,512]{2,1,0:T(8,128)(2,1)S(1)}, u32[]{:S(2)}, u32[]{:S(2)}) collective-permute-start(bf16[4,256,512]{2,1,0:T(8,128)(2,1)S(1)} %shard_map.52), channel_id=1, source_target_pairs={{0,1},{1,0},{2,3},{3,2},{4,5},{5,4},{6,7},{7,6},{8,9},{9,8},{10,11... | collective-permute-start | bytes 3145736 | tf_op jit(solution)/shard_map/ppermute | solution.py:31
  118.3 23.0 %copy-start.2 = (s32[8]{0:T(128)S(1)}, s32[8]{0:T(128)}, u32[]{:S(2)}) copy-start(s32[8]{0:T(128)} %owner.1) | copy-start | bytes 100
  118.3 12.9 %collective-permute-start.23 = (bf16[256,512]{1,0:T(8,128)(2,1)S(1)}, bf16[256,512]{1,0:T(8,128)(2,1)S(1)}, u32[]{:S(2)}, u32[]{:S(2)}) collective-permute-start(bf16[256,512]{1,0:T(8,128)(2,1)S(1)} %get-tuple-element.45), channel_id=1, source_target_pairs={{0,0},{1,65},{2,2},{3,67},{4,4},{5,69},{6,6},{7,71},{8,8},{9,73},{... | collective-permute-start | bytes 786440 | tf_op jit(solution)/shard_map/ppermute | solution.py:31
  123.9 9.0 %collective-permute-start.24 = (bf16[256,512]{1,0:T(8,128)(2,1)S(1)}, bf16[256,512]{1,0:T(8,128)(2,1)S(1)}, u32[]{:S(2)}, u32[]{:S(2)}) collective-permute-start(bf16[256,512]{1,0:T(8,128)(2,1)S(1)} %get-tuple-element.48), channel_id=1, source_target_pairs={{0,16},{1,81},{2,18},{3,83},{4,20},{5,85},{6,22},{7,87},{8,24},{9,... | collective-permute-start | bytes 786440 | tf_op jit(solution)/shard_map/ppermute | solution.py:31
  124.8 12.0 %collective-permute-start.25 = (bf16[256,512]{1,0:T(8,128)(2,1)S(1)}, bf16[256,512]{1,0:T(8,128)(2,1)S(1)}, u32[]{:S(2)}, u32[]{:S(2)}) collective-permute-start(bf16[256,512]{1,0:T(8,128)(2,1)S(1)} %get-tuple-element.47), channel_id=1, source_target_pairs={{0,32},{1,97},{2,34},{3,99},{4,36},{5,101},{6,38},{7,103},{8,40},{... | collective-permute-start | bytes 786440 | tf_op jit(solution)/shard_map/ppermute | solution.py:31
  130.3 8.2 %collective-permute-start.26 = (bf16[256,512]{1,0:T(8,128)(2,1)S(1)}, bf16[256,512]{1,0:T(8,128)(2,1)S(1)}, u32[]{:S(2)}, u32[]{:S(2)}) collective-permute-start(bf16[256,512]{1,0:T(8,128)(2,1)S(1)} %get-tuple-element.46), channel_id=1, source_target_pairs={{0,48},{1,113},{2,50},{3,115},{4,52},{5,117},{6,54},{7,119},{8,56}... | collective-permute-start | bytes 786440 | tf_op jit(solution)/shard_map/ppermute | solution.py:31
  138.6 2.7 %collective-permute-start.27 = (bf16[4,256,512]{2,1,0:T(8,128)(2,1)S(1)}, bf16[4,256,512]{2,1,0:T(8,128)(2,1)S(1)}, u32[]{:S(2)}, u32[]{:S(2)}) collective-permute-start(bf16[4,256,512]{2,1,0:T(8,128)(2,1)S(1)} %pad_maximum_fusion.own), channel_id=1, source_target_pairs={{0,1},{1,0},{2,3},{3,2},{4,5},{5,4},{6,7},{7,6},{8,9},{9,8},{10,11... | collective-permute-start | bytes 3145736 | tf_op jit(solution)/shard_map/ppermute | solution.py:31
  142.0 7.6 %collective-permute-start.28 = (bf16[256,512]{1,0:T(8,128)(2,1)S(1)}, bf16[256,512]{1,0:T(8,128)(2,1)S(1)}, u32[]{:S(2)}, u32[]{:S(2)}) collective-permute-start(bf16[256,512]{1,0:T(8,128)(2,1)S(1)} %get-tuple-element.41), channel_id=1, source_target_pairs={{0,0},{1,8},{2,2},{3,10},{4,4},{5,12},{6,6},{7,14},{8,9},{9,1},{10... | collective-permute-start | bytes 786440 | tf_op jit(solution)/shard_map/ppermute | solution.py:31
  143.9 7.5 %collective-permute-start.29 = (bf16[256,512]{1,0:T(8,128)(2,1)S(1)}, bf16[256,512]{1,0:T(8,128)(2,1)S(1)}, u32[]{:S(2)}, u32[]{:S(2)}) collective-permute-start(bf16[256,512]{1,0:T(8,128)(2,1)S(1)} %get-tuple-element.42), channel_id=1, source_target_pairs={{0,2},{1,10},{2,4},{3,12},{4,6},{5,14},{6,0},{7,8},{8,11},{9,3},{1... | collective-permute-start | bytes 786440 | tf_op jit(solution)/shard_map/ppermute | solution.py:31
  145.5 15.4 %collective-permute-start.30 = (bf16[256,512]{1,0:T(8,128)(2,1)S(1)}, bf16[256,512]{1,0:T(8,128)(2,1)S(1)}, u32[]{:S(2)}, u32[]{:S(2)}) collective-permute-start(bf16[256,512]{1,0:T(8,128)(2,1)S(1)} %get-tuple-element.43), channel_id=1, source_target_pairs={{0,4},{1,12},{2,6},{3,14},{4,0},{5,8},{6,2},{7,10},{8,13},{9,5},{1... | collective-permute-start | bytes 786440 | tf_op jit(solution)/shard_map/ppermute | solution.py:31
  149.4 11.8 %collective-permute-start.31 = (bf16[256,512]{1,0:T(8,128)(2,1)S(1)}, bf16[256,512]{1,0:T(8,128)(2,1)S(1)}, u32[]{:S(2)}, u32[]{:S(2)}) collective-permute-start(bf16[256,512]{1,0:T(8,128)(2,1)S(1)} %get-tuple-element.44), channel_id=1, source_target_pairs={{0,6},{1,14},{2,0},{3,8},{4,2},{5,10},{6,4},{7,12},{8,15},{9,7},{1... | collective-permute-start | bytes 786440 | tf_op jit(solution)/shard_map/ppermute | solution.py:31

commit v7 on v6

--- a/solution.py
+++ b/solution.py
@@ -13,7 +13,9 @@
 N_DEV = 128
 SHARE = 512
 COLS = 256
-PARTS = {"z": (0, 96), "y": (96, 80), "x": (176, 80)}
+PARTS = {"z": (0, 64), "y": (64, 64), "x": (128, 64)}
+RING_ROWS = 192
+REST = 256 - RING_ROWS
 ORDER = {"z": "xyz", "y": "zxy", "x": "yzx"}
 MIB = 1024 * 1024
 
@@ -197,7 +199,22 @@
                 out[eh, :, x_rows, cols] += got
 
 
-def late_kernel(keep, table, mine, theirs, z2, z3, y2, y3, x2, x3, early, out, z_held, y_held, x_held, total, sems):
+def rest_kernel(table, mine, theirs, gathered, out, held, sems):
+    core = table[CORE]
+    for eh in range(2):
+        for ys in range(4):
+            group = (table[XH] ^ eh) * 4 + ((table[Y] + table[SLOT_OFFSET + ys]) & 3)
+            for n in range(8):
+                source = gathered.at[group * 8 + (table[MINE + n] >> 1)]
+                pltpu.make_async_copy(source, held.at[eh, ys, :, pl.ds(n * SHARE, SHARE)], sems.at[eh]).start()
+    for eh in range(2):
+        pltpu.make_async_copy(held.at[eh], held.at[eh], sems.at[eh]).wait()
+        acts = held[eh].reshape(4 * REST, 8 * SHARE)
+        for weight, cols in zip((mine, theirs), column_slices(core)):
+            out[eh, :, :, cols] = dot(acts, weight[...]).reshape(4, REST, COLS)
+
+
+def late_kernel(keep, table, mine, theirs, z2, z3, y2, y3, x2, x3, early, rest, out, z_held, y_held, x_held, total, sems):
     core = table[CORE]
     half = core if keep else 1 - core
     near = jnp.where(half == 0, 0, 3)
@@ -213,7 +230,8 @@
     for i, part in enumerate((z2, z3)):
         for sx, el in sources:
             start(part.at[:, sx], z_held.at[i, :, :, pl.ds(el * SHARE, SHARE)], 0)
-    start(early.at[half], total, 1)
+    start(early.at[half], total.at[:, pl.ds(0, RING_ROWS)], 1)
+    start(rest.at[half], total.at[:, pl.ds(RING_ROWS, REST)], 4)
     for i, part in enumerate((y2, y3)):
         for sx, el in sources:
             for zs in range(4):
@@ -225,7 +243,7 @@
     z_rows, y_rows, x_rows = rows_of("z"), rows_of("y"), rows_of("x")
     weights = list(zip((mine, theirs), column_slices(core)))
     ready(z_held, 0)
-    ready(total, 1)
+    ready(total.at[:, pl.ds(0, RING_ROWS)], 1)
     for weight, cols in weights:
         got = None
         for i in range(2):
@@ -252,21 +270,22 @@
         def _():
             add(1, 0)
 
+    ready(total.at[:, pl.ds(RING_ROWS, REST)], 4)
     for ys in range(4):
         out[table[SLOT_OFFSET + ys]] = total[ys].astype(out.dtype)
 
 
-def product(kernel, table, weights, blocks, slots, held, out, more=()):
+def product(kernel, table, weights, blocks, slots, held, out, more=(), vmem_mib=20):
     vmem, anywhere = pl.BlockSpec(memory_space=pltpu.VMEM), pl.BlockSpec(memory_space=pl.ANY)
     parts = [blocks[axis][s] for axis in "zyx" for s in slots] + list(more)
-    work = 2 * out.shape[0] * (2 if out.ndim == 4 else 1)
+    work = 4 if out.ndim == 4 else 2
     return pl.pallas_call(
         kernel,
         in_specs=[pl.BlockSpec(memory_space=pltpu.SMEM)] + [vmem] * 2 + [anywhere] * len(parts),
         out_specs=vmem,
         out_shape=out,
         scratch_shapes=held,
-        compiler_params=pltpu.CompilerParams(vmem_limit_bytes=20 * MIB),
+        compiler_params=pltpu.CompilerParams(vmem_limit_bytes=vmem_mib * MIB),
         cost_estimate=pl.CostEstimate(
             flops=work * 512 * 4096 * 256, bytes_accessed=(6 + work) * MIB, transcendentals=0
         ),
@@ -323,6 +342,9 @@
     me = lax.axis_index("group") * 16 + lax.axis_index("tp")
     table = lax.dynamic_index_in_dim(rows, me, 0, keepdims=False)
 
+    same_core = [[i for i in range(N_DEV) if i % 2 == c] for c in range(2)]
+    gathered = lax.all_gather(activations[RING_ROWS:], AXES, axis=0, tiled=True, axis_index_groups=same_core)
+    gathered = gathered.reshape(N_DEV // 2, REST, SHARE)
     planes = gather_planes({part: activations[None, at : at + n] for part, (at, n) in PARTS.items()})
     blocks = {axis: gather_last(planes[axis], axis) for axis in "zyx"}
 
@@ -343,14 +365,25 @@
             pltpu.VMEM((2, 4, xn, 4 * SHARE), bf16),
             pltpu.SemaphoreType.DMA((2, 3)),
         ],
-        jax.ShapeDtypeStruct((2, 4, 256, 2 * COLS), f32),
+        jax.ShapeDtypeStruct((2, 4, RING_ROWS, 2 * COLS), f32),
+    )
+    rest = product(
+        rest_kernel,
+        table,
+        weights,
+        blocks,
+        (),
+        [pltpu.VMEM((2, 4, REST, 8 * SHARE), bf16), pltpu.SemaphoreType.DMA((2,))],
+        jax.ShapeDtypeStruct((2, 4, REST, 2 * COLS), f32),
+        (gathered,),
+        44,
     )
     late = [
         pltpu.VMEM((2, 4, zn, 2 * SHARE), bf16),
         pltpu.VMEM((2, yn, 8 * SHARE), bf16),
         pltpu.VMEM((2, 4, xn, 4 * SHARE), bf16),
         pltpu.VMEM((4, 256, 2 * COLS), f32),
-        pltpu.SemaphoreType.DMA((4,)),
+        pltpu.SemaphoreType.DMA((5,)),
     ]
     passed, kept = (
         product(
@@ -361,7 +394,7 @@
             (2, 3),
             late,
             jax.ShapeDtypeStruct((4, 256, 2 * COLS), f32 if keep else bf16),
-            (early,),
+            (early, rest),
         )
         for keep in (False, True)
     )

time: 164 us -> 416 us (2.54)
  waiting for transfers between devices: 69.4 us -> 273 us
  starting transfers between devices: 62.9 us -> 88.8 us
  between operations: 0.41 us -> 13.7 us
    all_gather x0 -> x1, waiting for transfers between devices: none -> 206 us  [shards(): lax.all_gather(activations[RING_ROWS:], AXES, axis=0, tiled=True, axis_in...]
    ppermute x32, starting transfers between devices: 62.9 us -> 88.8 us  [permute(): lax.ppermute(value, AXES, [(i, move(*coords(i))) for i in range(N_DEV)])]
    unnamed x6 -> x12, local copies, waits for them, and re-layouts: 1.1 us -> 5.42 us
    pallas_call x3 -> x4, Pallas kernels: 15.4 us -> 19.2 us  [product(): pl.pallas_call(kernel, in_specs=[pl.BlockSpec(memory_space=pltpu.SMEM)] +...]
  transfers between devices with their start and end apart: 32 -> 33, of which waited for: 16 -> 19; matrix products, arithmetic and copies ran while one was open for 1% -> 0% of each run, Pallas kernels for 11% -> 5%
where the time goes in v7:
time: 416 us; the launch traced here: 414 us
  waiting for transfers between devices  273 us (66%)
  starting transfers between devices  88.8 us (21%)
  Pallas kernels  29.6 us (7%)
  between operations  13.7 us (3%)
  local copies, waits for them, and re-layouts  7.76 us (2%)
    all_gather x1, waiting for transfers between devices, shards(): lax.all_gather(activations[RING_ROWS:], AXES, axis=0, tiled=True, axis_in...  206 us
    ppermute x32, starting transfers between devices, permute(): lax.ppermute(value, AXES, [(i, move(*coords(i))) for i in range(N_DEV)])  88.8 us
    ppermute x32, waiting for transfers between devices, permute(): lax.ppermute(value, AXES, [(i, move(*coords(i))) for i in range(N_DEV)])  67 us
    pallas_call x4, Pallas kernels, product(): pl.pallas_call(kernel, in_specs=[pl.BlockSpec(memory_space=pltpu.SMEM)] +...  19.2 us
  transfers between devices with their start and end apart: 33, of which 19 were waited for; matrix products, arithmetic and copies ran while one was open for 0% of the time, Pallas kernels for 5%

profile of v7, /device:TPU:3, one launch (start us, length us, event | category | flops | bytes accessed | tf_op | source)
XLA Modules:
  0.0 413.5 jit_solution(14646981689051250736)
XLA Ops:
  6.5 1.6 fusion
  8.1 0.0 all-gather.2.cloned.1.call-update
  8.1 2.8 collective-permute-start.1
  10.9 3.8 collective-permute-start.2
  14.7 1.2 collective-permute-start.3
  15.9 0.4 collective-permute-done.2
  16.4 1.4 collective-permute-done.3
  17.8 0.1 collective-permute-start.4
  17.9 0.1 collective-permute-start.5
  18.0 0.7 dynamic-slice_bitcast_fusion.table
  18.7 3.3 shard_map.47
  22.0 3.5 collective-permute-start
  25.5 0.3 collective-permute-start.6
  25.8 3.8 collective-permute-done.6
  29.6 0.7 collective-permute-start.7
  30.4 1.2 collective-permute-start.8
  31.6 0.7 collective-permute-start.9
  32.3 4.1 collective-permute-done.7.refs_1_
  36.4 1.6 collective-permute-done.9.refs_5_
  38.0 0.1 shard_map.48
  38.1 0.4 collective-permute-start.10
  38.5 1.7 collective-permute-start.11
  40.2 7.5 %collective-permute-done.10.refs_1_ = bf16[8,64,512]{2,1,0:T(8,128)(2,1)S(1)} collective-permute-done((bf16[8,64,512]{2,1,0:T(8,128)(2,1)S(1)}, bf16[8,64,512]{2,1,0:T(8,128)(2,1)S(1)}, u32[]{:S(2)}, u32[]{:S(2)}) %collective-permute-start.10) | collective-permute-done | bytes 524320 | tf_op jit(solution)/shard_map/ppermute | solution.py:33
  47.8 1.7 collective-permute-done.12.refs_5_
  49.5 1.5 shard_map.49
  51.0 2.3 collective-permute-start.13
  53.4 1.2 collective-permute-start.17
  54.6 13.1 %collective-permute-done.19 = bf16[16,64,512]{2,1,0:T(8,128)(2,1)} collective-permute-done((bf16[16,64,512]{2,1,0:T(8,128)(2,1)}, bf16[16,64,512]{2,1,0:T(8,128)(2,1)}, u32[]{:S(2)}, u32[]{:S(2)}) %collective-permute-start.19) | collective-permute-done | bytes 1048608 | tf_op jit(solution)/shard_map/ppermute | solution.py:33
  67.7 0.9 collective-permute-done.13
  68.6 1.6 collective-permute-start.20
  70.2 0.0 collective-permute-start.21
  70.2 8.5 %collective-permute-done.17 = bf16[16,64,512]{2,1,0:T(8,128)(2,1)} collective-permute-done((bf16[16,64,512]{2,1,0:T(8,128)(2,1)S(1)}, bf16[16,64,512]{2,1,0:T(8,128)(2,1)}, u32[]{:S(2)}, u32[]{:S(2)}) %collective-permute-start.17) | collective-permute-done | bytes 1048608 | tf_op jit(solution)/shard_map/ppermute | solution.py:33
  78.8 3.4 collective-permute-done.16
  82.2 0.3 collective-permute-start.18
  82.5 3.3 shard_map.46.mine
  85.8 5.9 %shard_map.50.early = f32[2,4,192,512]{3,2,1,0:T(8,128)S(1)} custom-call(s32[28]{0:T(128)S(1)} %dynamic-slice_bitcast_fusion.table, bf16[4096,256]{1,0:T(8,128)(2,1)S(1)} %shard_map.46.mine, bf16[4096,256]{1,0:T(8,128)(2,1)S(1)} %collective-permute-done.theirs, bf16[4,4,64,512]{3,2,1,0:T(8,128)(2,1)} %bitcast.10.z0, bf16[4,4,64,512]{3,2,1,0:T(8,128)(2,1)} %bitcast.11.z1, ...), custom_call_target="tpu_custom_call" | custom-call | flops 2147483648 | bytes 10485760 | tf_op jit(solution)/shard_map/pallas_call | solution.py:282
  91.7 1.6 copy-done.2
  93.3 206.1 %all-gather.2.cloned.1.call-done = bf16[4096,512]{1,0:T(8,128)(2,1)} async-done(((bf16[64,512]{1,0:T(8,128)(2,1)}), bf16[4096,512]{1,0:T(8,128)(2,1)}) %all-gather.2.cloned.1.call-update) | async-done | bytes 4194320 | tf_op jit(solution)/shard_map/all_gather | solution.py:346
  299.4 1.6 copy-done.1
  301.0 2.2 copy-done.4
  303.2 4.2 %shard_map.51.rest = f32[2,4,64,512]{3,2,1,0:T(8,128)S(1)} custom-call(s32[28]{0:T(128)S(1)} %dynamic-slice_bitcast_fusion.table, bf16[4096,256]{1,0:T(8,128)(2,1)S(1)} %shard_map.46.mine, bf16[4096,256]{1,0:T(8,128)(2,1)S(1)} %copy-done.1, bf16[64,64,512]{2,1,0:T(8,128)(2,1)S(1)} %bitcast.35), custom_call_target="tpu_custom_call" | custom-call | flops 2147483648 | bytes 10485760 | tf_op jit(solution)/shard_map/pallas_call | solution.py:282
  307.4 4.8 %shard_map.53 = bf16[4,256,512]{2,1,0:T(8,128)(2,1)S(1)} custom-call(s32[28]{0:T(128)S(1)} %dynamic-slice_bitcast_fusion.table, bf16[4096,256]{1,0:T(8,128)(2,1)S(1)} %shard_map.46.mine, bf16[4096,256]{1,0:T(8,128)(2,1)S(1)} %copy-done.1, bf16[4,4,64,512]{3,2,1,0:T(8,128)(2,1)} %bitcast.4.z2, bf16[4,4,64,512]{3,2,1,0:T(8,128)(2,1)} %bitcast.5.z3, ...), custom_call_target="tpu_custom_call" | custom-call | flops 1073741824 | bytes 8388608 | tf_op jit(solution)/shard_map/pallas_call | solution.py:282
  312.2 44.9 %collective-permute-start.22 = (bf16[4,256,512]{2,1,0:T(8,128)(2,1)S(1)}, bf16[4,256,512]{2,1,0:T(8,128)(2,1)S(1)}, u32[]{:S(2)}, u32[]{:S(2)}) collective-permute-start(bf16[4,256,512]{2,1,0:T(8,128)(2,1)S(1)} %shard_map.53), channel_id=1, source_target_pairs={{0,1},{1,0},{2,3},{3,2},{4,5},{5,4},{6,7},{7,6},{8,9},{9,8},{10,11... | collective-permute-start | bytes 3145736 | tf_op jit(solution)/shard_map/ppermute | solution.py:33
  357.1 4.4 %shard_map.52 = f32[4,256,512]{2,1,0:T(8,128)S(1)} custom-call(s32[28]{0:T(128)S(1)} %dynamic-slice_bitcast_fusion.table, bf16[4096,256]{1,0:T(8,128)(2,1)S(1)} %shard_map.46.mine, bf16[4096,256]{1,0:T(8,128)(2,1)S(1)} %copy-done.1, bf16[4,4,64,512]{3,2,1,0:T(8,128)(2,1)} %bitcast.4.z2, bf16[4,4,64,512]{3,2,1,0:T(8,128)(2,1)} %bitcast.5.z3, ...), custom_call_target="tpu_custom_call" | custom-call | flops 1073741824 | bytes 8388608 | tf_op jit(solution)/shard_map/pallas_call | solution.py:282
  361.5 0.4 add_convert_fusion
  361.9 0.1 slice_bitcast_fusion.3
  362.0 1.9 collective-permute-start.23
  363.9 0.1 collective-permute-start.24
  364.0 7.7 %collective-permute-start.25 = (bf16[256,512]{1,0:T(8,128)(2,1)S(1)}, bf16[256,512]{1,0:T(8,128)(2,1)S(1)}, u32[]{:S(2)}, u32[]{:S(2)}) collective-permute-start(bf16[256,512]{1,0:T(8,128)(2,1)S(1)} %get-tuple-element.47), channel_id=1, source_target_pairs={{0,32},{1,97},{2,34},{3,99},{4,36},{5,101},{6,38},{7,103},{8,40},{... | collective-permute-start | bytes 786440 | tf_op jit(solution)/shard_map/ppermute | solution.py:33
  371.7 2.7 collective-permute-done.24
  374.4 3.8 collective-permute-done.25
  378.3 1.1 collective-permute-done.26
  379.3 0.1 pad_maximum_fusion.own
  379.5 0.1 collective-permute-start.27
  379.6 2.6 collective-permute-done.27.other
  382.2 0.7 shard_map.54
  382.9 6.3 %collective-permute-start.28 = (bf16[256,512]{1,0:T(8,128)(2,1)S(1)}, bf16[256,512]{1,0:T(8,128)(2,1)S(1)}, u32[]{:S(2)}, u32[]{:S(2)}) collective-permute-start(bf16[256,512]{1,0:T(8,128)(2,1)S(1)} %get-tuple-element.41), channel_id=1, source_target_pairs={{0,0},{1,8},{2,2},{3,10},{4,4},{5,12},{6,6},{7,14},{8,9},{9,1},{10... | collective-permute-start | bytes 786440 | tf_op jit(solution)/shard_map/ppermute | solution.py:33
  389.3 0.1 collective-permute-start.29
  389.3 4.0 collective-permute-start.30
  393.3 1.7 collective-permute-start.31
  395.0 4.8 %collective-permute-done.29.refs_1_ = bf16[256,512]{1,0:T(8,128)(2,1)S(1)} collective-permute-done((bf16[256,512]{1,0:T(8,128)(2,1)S(1)}, bf16[256,512]{1,0:T(8,128)(2,1)S(1)}, u32[]{:S(2)}, u32[]{:S(2)}) %collective-permute-start.29) | collective-permute-done | bytes 262176 | tf_op jit(solution)/shard_map/ppermute | solution.py:33
  399.8 5.0 %collective-permute-done.30.refs_2_ = bf16[256,512]{1,0:T(8,128)(2,1)S(1)} collective-permute-done((bf16[256,512]{1,0:T(8,128)(2,1)S(1)}, bf16[256,512]{1,0:T(8,128)(2,1)S(1)}, u32[]{:S(2)}, u32[]{:S(2)}) %collective-permute-start.30) | collective-permute-done | bytes 262176 | tf_op jit(solution)/shard_map/ppermute | solution.py:33
  404.8 0.3 collective-permute-done.31.refs_3_
  405.1 1.5 shard_map.55
  (36 shorter events, 0.2 us)
Async XLA Ops:
  6.5 292.8 %all-gather.2.cloned.1.call-start = ((), (), s32[]{:S(2)}) async-start(), calls=%async_computation | async-start | bytes 4259840 | tf_op jit(solution)/shard_map/all_gather | solution.py:346
  8.1 7.8 %collective-permute-start.1 = (bf16[1,64,512]{2,1,0:T(8,128)(2,1)S(1)}, bf16[1,64,512]{2,1,0:T(8,128)(2,1)S(1)}, u32[]{:S(2)}, u32[]{:S(2)}) collective-permute-start(bf16[1,64,512]{2,1,0:T(8,128)(2,1)S(1)} %get-tuple-element.51), channel_id=1, source_target_pairs={{0,16},{1,49},{2,18},{3,51},{4,20},{5,53},{6,22},{7,55},{8,24},{9,... | collective-permute-start | bytes 196616 | tf_op jit(solution)/shard_map/ppermute | solution.py:33
  10.9 5.4 %collective-permute-start.2 = (bf16[1,64,512]{2,1,0:T(8,128)(2,1)S(1)}, bf16[1,64,512]{2,1,0:T(8,128)(2,1)S(1)}, u32[]{:S(2)}, u32[]{:S(2)}) collective-permute-start(bf16[1,64,512]{2,1,0:T(8,128)(2,1)S(1)} %get-tuple-element.50), channel_id=1, source_target_pairs={{0,2},{1,7},{2,0},{3,5},{4,6},{5,3},{6,4},{7,1},{8,10},{9,15},{10,... | collective-permute-start | bytes 196616 | tf_op jit(solution)/shard_map/ppermute | solution.py:33
  14.7 3.1 collective-permute-start.3
  17.8 7.9 %collective-permute-start.4 = (bf16[2,64,512]{2,1,0:T(8,128)(2,1)S(1)}, bf16[2,64,512]{2,1,0:T(8,128)(2,1)S(1)}, u32[]{:S(2)}, u32[]{:S(2)}) collective-permute-start(bf16[2,64,512]{2,1,0:T(8,128)(2,1)S(1)} %pad_maximum_fusion.4), channel_id=1, source_target_pairs={{0,48},{1,17},{2,50},{3,19},{4,52},{5,21},{6,54},{7,23},{8,56},{9,... | collective-permute-start | bytes 393224 | tf_op jit(solution)/shard_map/ppermute | solution.py:33
  17.9 7.9 %collective-permute-start.5 = (bf16[2,64,512]{2,1,0:T(8,128)(2,1)S(1)}, bf16[2,64,512]{2,1,0:T(8,128)(2,1)S(1)}, u32[]{:S(2)}, u32[]{:S(2)}) collective-permute-start(bf16[2,64,512]{2,1,0:T(8,128)(2,1)S(1)} %pad_maximum_fusion.5), channel_id=1, source_target_pairs={{0,6},{1,3},{2,4},{3,1},{4,2},{5,7},{6,0},{7,5},{8,14},{9,11},{10,... | collective-permute-start | bytes 393224 | tf_op jit(solution)/shard_map/ppermute | solution.py:33
  22.0 60.2 %collective-permute-start = (bf16[4096,256]{1,0:T(8,128)(2,1)S(1)}, bf16[4096,256]{1,0:T(8,128)(2,1)S(1)}, u32[]{:S(2)}, u32[]{:S(2)}) collective-permute-start(bf16[4096,256]{1,0:T(8,128)(2,1)S(1)} %shard_map.47), channel_id=1, source_target_pairs={{0,1},{1,0},{2,3},{3,2},{4,5},{5,4},{6,7},{7,6},{8,9},{9,8},{10,11... | collective-permute-start | bytes 6291464 | tf_op jit(solution)/shard_map/ppermute | solution.py:33
  25.5 4.1 collective-permute-start.6
  29.6 6.8 %collective-permute-start.7 = (bf16[4,64,512]{2,1,0:T(8,128)(2,1)S(1)}, bf16[4,64,512]{2,1,0:T(8,128)(2,1)S(1)}, u32[]{:S(2)}, u32[]{:S(2)}) collective-permute-start(bf16[4,64,512]{2,1,0:T(8,128)(2,1)S(1)} %pad_maximum_fusion.1.refs_0_), channel_id=1, source_target_pairs={{0,2},{1,7},{2,0},{3,5},{4,6},{5,3},{6,4},{7,1},{8,10},{9,15},{10,... | collective-permute-start | bytes 786440 | tf_op jit(solution)/shard_map/ppermute | solution.py:33
  30.4 6.1 %collective-permute-start.8 = (bf16[4,64,512]{2,1,0:T(8,128)(2,1)S(1)}, bf16[4,64,512]{2,1,0:T(8,128)(2,1)S(1)}, u32[]{:S(2)}, u32[]{:S(2)}) collective-permute-start(bf16[4,64,512]{2,1,0:T(8,128)(2,1)S(1)} %pad_maximum_fusion.2.refs_2_), channel_id=1, source_target_pairs={{0,8},{1,73},{2,10},{3,75},{4,12},{5,77},{6,14},{7,79},{8,0},{9,65... | collective-permute-start | bytes 786440 | tf_op jit(solution)/shard_map/ppermute | solution.py:33
  31.6 6.4 %collective-permute-start.9 = (bf16[4,64,512]{2,1,0:T(8,128)(2,1)S(1)}, bf16[4,64,512]{2,1,0:T(8,128)(2,1)S(1)}, u32[]{:S(2)}, u32[]{:S(2)}) collective-permute-start(bf16[4,64,512]{2,1,0:T(8,128)(2,1)S(1)} %pad_maximum_fusion.3.refs_4_), channel_id=1, source_target_pairs={{0,16},{1,49},{2,18},{3,51},{4,20},{5,53},{6,22},{7,55},{8,24},{9,... | collective-permute-start | bytes 786440 | tf_op jit(solution)/shard_map/ppermute | solution.py:33
  38.1 9.6 %collective-permute-start.10 = (bf16[8,64,512]{2,1,0:T(8,128)(2,1)S(1)}, bf16[8,64,512]{2,1,0:T(8,128)(2,1)S(1)}, u32[]{:S(2)}, u32[]{:S(2)}) collective-permute-start(bf16[8,64,512]{2,1,0:T(8,128)(2,1)S(1)} %get-tuple-element.31.refs_0_), channel_id=1, source_target_pairs={{0,6},{1,3},{2,4},{3,1},{4,2},{5,7},{6,0},{7,5},{8,14},{9,11},{10,... | collective-permute-start | bytes 1572872 | tf_op jit(solution)/shard_map/ppermute | solution.py:33
  38.5 9.3 %collective-permute-start.11 = (bf16[8,64,512]{2,1,0:T(8,128)(2,1)S(1)}, bf16[8,64,512]{2,1,0:T(8,128)(2,1)S(1)}, u32[]{:S(2)}, u32[]{:S(2)}) collective-permute-start(bf16[8,64,512]{2,1,0:T(8,128)(2,1)S(1)} %get-tuple-element.32.refs_2_), channel_id=1, source_target_pairs={{0,72},{1,9},{2,74},{3,11},{4,76},{5,13},{6,78},{7,15},{8,64},{9,1... | collective-permute-start | bytes 1572872 | tf_op jit(solution)/shard_map/ppermute | solution.py:33
  40.2 9.3 %collective-permute-start.12 = (bf16[8,64,512]{2,1,0:T(8,128)(2,1)S(1)}, bf16[8,64,512]{2,1,0:T(8,128)(2,1)S(1)}, u32[]{:S(2)}, u32[]{:S(2)}) collective-permute-start(bf16[8,64,512]{2,1,0:T(8,128)(2,1)S(1)} %get-tuple-element.33.refs_4_), channel_id=1, source_target_pairs={{0,48},{1,17},{2,50},{3,19},{4,52},{5,21},{6,54},{7,23},{8,56},{9,... | collective-permute-start | bytes 1572872 | tf_op jit(solution)/shard_map/ppermute | solution.py:33
  51.0 16.6 %collective-permute-start.19 = (bf16[16,64,512]{2,1,0:T(8,128)(2,1)}, bf16[16,64,512]{2,1,0:T(8,128)(2,1)}, u32[]{:S(2)}, u32[]{:S(2)}) collective-permute-start(bf16[16,64,512]{2,1,0:T(8,128)(2,1)} %get-tuple-element.39), channel_id=1, source_target_pairs={{0,8},{1,73},{2,10},{3,75},{4,12},{5,77},{6,14},{7,79},{8,0},{9,65... | collective-permute-start | bytes 3145736 | tf_op jit(solution)/shard_map/ppermute | solution.py:33
  51.0 17.6 %collective-permute-start.13 = (bf16[16,64,512]{2,1,0:T(8,128)(2,1)}, bf16[16,64,512]{2,1,0:T(8,128)(2,1)}, u32[]{:S(2)}, u32[]{:S(2)}) collective-permute-start(bf16[16,64,512]{2,1,0:T(8,128)(2,1)} %get-tuple-element.35), channel_id=1, source_target_pairs={{0,2},{1,7},{2,0},{3,5},{4,6},{5,3},{6,4},{7,1},{8,10},{9,15},{10,... | collective-permute-start | bytes 3145736 | tf_op jit(solution)/shard_map/ppermute | solution.py:33
  53.4 25.4 %collective-permute-start.17 = (bf16[16,64,512]{2,1,0:T(8,128)(2,1)S(1)}, bf16[16,64,512]{2,1,0:T(8,128)(2,1)}, u32[]{:S(2)}, u32[]{:S(2)}) collective-permute-start(bf16[16,64,512]{2,1,0:T(8,128)(2,1)S(1)} %get-tuple-element.37), channel_id=1, source_target_pairs={{0,16},{1,49},{2,18},{3,51},{4,20},{5,53},{6,22},{7,55},{8,24},{9,... | collective-permute-start | bytes 3145736 | tf_op jit(solution)/shard_map/ppermute | solution.py:33
  54.6 27.6 %collective-permute-start.16 = (bf16[16,64,512]{2,1,0:T(8,128)(2,1)S(1)}, bf16[16,64,512]{2,1,0:T(8,128)(2,1)S(1)}, u32[]{:S(2)}, u32[]{:S(2)}) collective-permute-start(bf16[16,64,512]{2,1,0:T(8,128)(2,1)S(1)} %get-tuple-element.37), channel_id=1, source_target_pairs={{0,48},{1,17},{2,50},{3,19},{4,52},{5,21},{6,54},{7,23},{8,56},{9,... | collective-permute-start | bytes 3145736 | tf_op jit(solution)/shard_map/ppermute | solution.py:33
  68.6 238.7 %collective-permute-start.20 = (bf16[16,64,512]{2,1,0:T(8,128)(2,1)}, bf16[16,64,512]{2,1,0:T(8,128)(2,1)}, u32[]{:S(2)}, u32[]{:S(2)}) collective-permute-start(bf16[16,64,512]{2,1,0:T(8,128)(2,1)} %get-tuple-element.39), channel_id=1, source_target_pairs={{0,72},{1,9},{2,74},{3,11},{4,76},{5,13},{6,78},{7,15},{8,64},{9,1... | collective-permute-start | bytes 3145736 | tf_op jit(solution)/shard_map/ppermute | solution.py:33
  70.2 237.1 %collective-permute-start.21 = (bf16[16,64,512]{2,1,0:T(8,128)(2,1)}, bf16[16,64,512]{2,1,0:T(8,128)(2,1)}, u32[]{:S(2)}, u32[]{:S(2)}) collective-permute-start(bf16[16,64,512]{2,1,0:T(8,128)(2,1)} %collective-permute-done.19), channel_id=1, source_target_pairs={{0,72},{1,9},{2,74},{3,11},{4,76},{5,13},{6,78},{7,15},{8,64},{9,1... | collective-permute-start | bytes 3145736 | tf_op jit(solution)/shard_map/ppermute | solution.py:33
  78.8 228.5 %collective-permute-start.14 = (bf16[16,64,512]{2,1,0:T(8,128)(2,1)}, bf16[16,64,512]{2,1,0:T(8,128)(2,1)}, u32[]{:S(2)}, u32[]{:S(2)}) collective-permute-start(bf16[16,64,512]{2,1,0:T(8,128)(2,1)} %get-tuple-element.35), channel_id=1, source_target_pairs={{0,6},{1,3},{2,4},{3,1},{4,2},{5,7},{6,0},{7,5},{8,14},{9,11},{10,... | collective-permute-start | bytes 3145736 | tf_op jit(solution)/shard_map/ppermute | solution.py:33
  82.2 225.2 %collective-permute-start.15 = (bf16[16,64,512]{2,1,0:T(8,128)(2,1)}, bf16[16,64,512]{2,1,0:T(8,128)(2,1)}, u32[]{:S(2)}, u32[]{:S(2)}) collective-permute-start(bf16[16,64,512]{2,1,0:T(8,128)(2,1)} %collective-permute-done.13), channel_id=1, source_target_pairs={{0,6},{1,3},{2,4},{3,1},{4,2},{5,7},{6,0},{7,5},{8,14},{9,11},{10,... | collective-permute-start | bytes 3145736 | tf_op jit(solution)/shard_map/ppermute | solution.py:33
  82.2 3.6 copy-start
  82.2 225.2 %collective-permute-start.18 = (bf16[16,64,512]{2,1,0:T(8,128)(2,1)}, bf16[16,64,512]{2,1,0:T(8,128)(2,1)}, u32[]{:S(2)}, u32[]{:S(2)}) collective-permute-start(bf16[16,64,512]{2,1,0:T(8,128)(2,1)} %collective-permute-done.17), channel_id=1, source_target_pairs={{0,48},{1,17},{2,50},{3,19},{4,52},{5,21},{6,54},{7,23},{8,56},{9,... | collective-permute-start | bytes 3145736 | tf_op jit(solution)/shard_map/ppermute | solution.py:33
  91.7 1.6 copy-start.2
  299.4 1.6 copy-start.1
  301.0 2.2 copy-start.4
  303.2 4.2 %copy-start.3 = (f32[2,4,192,512]{3,2,1,0:T(8,128)S(1)}, f32[2,4,192,512]{3,2,1,0:T(8,128)}, u32[]{:S(2)}) copy-start(f32[2,4,192,512]{3,2,1,0:T(8,128)} %copy-done.2) | copy-start | bytes 9437188
  312.2 49.3 %collective-permute-start.22 = (bf16[4,256,512]{2,1,0:T(8,128)(2,1)S(1)}, bf16[4,256,512]{2,1,0:T(8,128)(2,1)S(1)}, u32[]{:S(2)}, u32[]{:S(2)}) collective-permute-start(bf16[4,256,512]{2,1,0:T(8,128)(2,1)S(1)} %shard_map.53), channel_id=1, source_target_pairs={{0,1},{1,0},{2,3},{3,2},{4,5},{5,4},{6,7},{7,6},{8,9},{9,8},{10,11... | collective-permute-start | bytes 3145736 | tf_op jit(solution)/shard_map/ppermute | solution.py:33
  361.9 20.4 %copy-start.5 = (s32[8]{0:T(128)S(1)}, s32[8]{0:T(128)}, u32[]{:S(2)}) copy-start(s32[8]{0:T(128)} %owner.1) | copy-start | bytes 100
  362.0 9.8 %collective-permute-start.23 = (bf16[256,512]{1,0:T(8,128)(2,1)S(1)}, bf16[256,512]{1,0:T(8,128)(2,1)S(1)}, u32[]{:S(2)}, u32[]{:S(2)}) collective-permute-start(bf16[256,512]{1,0:T(8,128)(2,1)S(1)} %get-tuple-element.45), channel_id=1, source_target_pairs={{0,0},{1,65},{2,2},{3,67},{4,4},{5,69},{6,6},{7,71},{8,8},{9,73},{... | collective-permute-start | bytes 786440 | tf_op jit(solution)/shard_map/ppermute | solution.py:33
  363.9 10.6 %collective-permute-start.24 = (bf16[256,512]{1,0:T(8,128)(2,1)S(1)}, bf16[256,512]{1,0:T(8,128)(2,1)S(1)}, u32[]{:S(2)}, u32[]{:S(2)}) collective-permute-start(bf16[256,512]{1,0:T(8,128)(2,1)S(1)} %get-tuple-element.48), channel_id=1, source_target_pairs={{0,16},{1,81},{2,18},{3,83},{4,20},{5,85},{6,22},{7,87},{8,24},{9,... | collective-permute-start | bytes 786440 | tf_op jit(solution)/shard_map/ppermute | solution.py:33
  364.0 14.3 %collective-permute-start.25 = (bf16[256,512]{1,0:T(8,128)(2,1)S(1)}, bf16[256,512]{1,0:T(8,128)(2,1)S(1)}, u32[]{:S(2)}, u32[]{:S(2)}) collective-permute-start(bf16[256,512]{1,0:T(8,128)(2,1)S(1)} %get-tuple-element.47), channel_id=1, source_target_pairs={{0,32},{1,97},{2,34},{3,99},{4,36},{5,101},{6,38},{7,103},{8,40},{... | collective-permute-start | bytes 786440 | tf_op jit(solution)/shard_map/ppermute | solution.py:33
  371.7 7.6 %collective-permute-start.26 = (bf16[256,512]{1,0:T(8,128)(2,1)S(1)}, bf16[256,512]{1,0:T(8,128)(2,1)S(1)}, u32[]{:S(2)}, u32[]{:S(2)}) collective-permute-start(bf16[256,512]{1,0:T(8,128)(2,1)S(1)} %get-tuple-element.46), channel_id=1, source_target_pairs={{0,48},{1,113},{2,50},{3,115},{4,52},{5,117},{6,54},{7,119},{8,56}... | collective-permute-start | bytes 786440 | tf_op jit(solution)/shard_map/ppermute | solution.py:33
  379.5 2.7 collective-permute-start.27
  382.9 12.1 %collective-permute-start.28 = (bf16[256,512]{1,0:T(8,128)(2,1)S(1)}, bf16[256,512]{1,0:T(8,128)(2,1)S(1)}, u32[]{:S(2)}, u32[]{:S(2)}) collective-permute-start(bf16[256,512]{1,0:T(8,128)(2,1)S(1)} %get-tuple-element.41), channel_id=1, source_target_pairs={{0,0},{1,8},{2,2},{3,10},{4,4},{5,12},{6,6},{7,14},{8,9},{9,1},{10... | collective-permute-start | bytes 786440 | tf_op jit(solution)/shard_map/ppermute | solution.py:33
  389.3 10.5 %collective-permute-start.29 = (bf16[256,512]{1,0:T(8,128)(2,1)S(1)}, bf16[256,512]{1,0:T(8,128)(2,1)S(1)}, u32[]{:S(2)}, u32[]{:S(2)}) collective-permute-start(bf16[256,512]{1,0:T(8,128)(2,1)S(1)} %get-tuple-element.42), channel_id=1, source_target_pairs={{0,2},{1,10},{2,4},{3,12},{4,6},{5,14},{6,0},{7,8},{8,11},{9,3},{1... | collective-permute-start | bytes 786440 | tf_op jit(solution)/shard_map/ppermute | solution.py:33
  389.3 15.5 %collective-permute-start.30 = (bf16[256,512]{1,0:T(8,128)(2,1)S(1)}, bf16[256,512]{1,0:T(8,128)(2,1)S(1)}, u32[]{:S(2)}, u32[]{:S(2)}) collective-permute-start(bf16[256,512]{1,0:T(8,128)(2,1)S(1)} %get-tuple-element.43), channel_id=1, source_target_pairs={{0,4},{1,12},{2,6},{3,14},{4,0},{5,8},{6,2},{7,10},{8,13},{9,5},{1... | collective-permute-start | bytes 786440 | tf_op jit(solution)/shard_map/ppermute | solution.py:33
  393.3 11.8 %collective-permute-start.31 = (bf16[256,512]{1,0:T(8,128)(2,1)S(1)}, bf16[256,512]{1,0:T(8,128)(2,1)S(1)}, u32[]{:S(2)}, u32[]{:S(2)}) collective-permute-start(bf16[256,512]{1,0:T(8,128)(2,1)S(1)} %get-tuple-element.44), channel_id=1, source_target_pairs={{0,6},{1,14},{2,0},{3,8},{4,2},{5,10},{6,4},{7,12},{8,15},{9,7},{1... | collective-permute-start | bytes 786440 | tf_op jit(solution)/shard_map/ppermute | solution.py:33
Sparse Core Ops, SparseCore 0:
  9.0 290.3 all-gather.1

commit v8 on v5

v8 whole, which is shorter than its diff:
```python
import functools

import jax
import jax.numpy as jnp
import numpy as np
from jax import lax
from jax.experimental import pallas as pl
from jax.experimental.pallas import tpu as pltpu
from jax.sharding import PartitionSpec as P

BLOCK = 128
AXES = ("group", "tp")
N_DEV = 128
SHARE = 512
COLS = 256
HALF = 128
MIB = 1024 * 1024


def coords(i):
    return i // 64 * 2 + i // 8 % 2, i // 16 % 4, i // 2 % 4, i % 2


def linear(x, y, z, core):
    x, y, z = x % 4, y % 4, z % 4
    return x // 2 * 64 + y * 16 + x % 2 * 8 + z * 2 + core


def permute(value, move):
    return lax.ppermute(value, AXES, [(i, move(*coords(i))) for i in range(N_DEV)])


def offset(slot, at, core):
    step = -1 if (at + core) % 2 else 1
    return (0, step, -step, 2)[slot] % 4


def exchange(value, axis, which):
    def move(x, y, z, core):
        at = {"x": x, "y": y, "z": z}
        at[axis] += offset(which, at[axis], core)
        return linear(at["x"], at["y"], at["z"], core)

    return permute(value, move)


def pair_exchange(value, axis, which):
    def move(x, y, z, core):
        at = {"x": x, "y": y, "z": z}
        at[axis] += offset(which, at[axis], 0)
        return linear(at["x"], at["y"], at["z"], core)

    return permute(value, move)


def other_core(x, y, z, core):
    return linear(x, y, z, 1 - core)


def other_chip(x, y, z, core):
    return linear(x ^ 1, y, z, core)


def after(value, *others):
    return lax.optimization_barrier((value, *others))[0]


def gather(activations, core, first_job, second_job):
    came = permute(activations, lambda x, y, z, c: linear(x + 2, y, z, c))
    block = jnp.stack([activations, after(came, first_job)])
    blocks = {"z": block[None, :, :HALF], "y": block[None, :, HALF:]}
    blocks = lax.optimization_barrier(blocks)
    for which in (1, 2):
        blocks = {
            part: jnp.concatenate([v, exchange(v, "y" if part == "z" else "z", which)]) for part, v in blocks.items()
        }
        blocks = lax.optimization_barrier(blocks)
    blocks, second_job = lax.optimization_barrier((blocks, second_job))
    slots, relays = {}, []
    for part, v in blocks.items():
        first = pair_exchange(v, part, 1)
        second = pair_exchange(v, part, 2)
        relays.append(jnp.where(core == 0, first, second))
        slots[part] = [v, first, second, exchange(relays[-1], part, 2)]
    return slots, relays


AWAY, HERE, CORE, Y_SLOT, Z_SLOT, Y_LAST, Z_LAST, XH, Y, Z, DEST, WIDTH = 0, 8, 16, 17, 21, 25, 29, 33, 34, 35, 36, 40


def device_row(i):
    x, y, z, core = coords(i)
    xh, xl = x // 2, x % 2

    def chunks(l, c):
        return [l * 8 + (z + dz) % 4 * 2 + c for dz in range(4)]

    row = chunks(1 - xl, core) + chunks(1 - xl, 1 - core) + chunks(xl, 1 - core) + chunks(xl, core) + [core]
    row += [offset(s, y, core) for s in range(4)] + [offset(s, z, core) for s in range(4)]
    row += [offset(s, y, 0) for s in range(4)] + [offset(s, z, 0) for s in range(4)]
    row += [xh, y, z] + [(xl ^ core) * 4 + (z + dz) % 4 for dz in range(4)]
    assert len(row) == WIDTH
    return row


def refit_kernel(first, table, master, *refs):
    outs, (held, sems) = refs[:-2], refs[-2:]
    copies = []
    for n in range(8):
        at = pl.multiple_of(table[first + n] * SHARE, SHARE)
        copies.append(pltpu.make_async_copy(master.at[pl.ds(at, SHARE)], held.at[n], sems.at[n]))
        copies[-1].start()
    tiles = SHARE // BLOCK
    for n in range(8):
        out = outs[n * len(outs) // 8]
        start = n * SHARE % out.shape[0]
        copies[n].wait()
        amax = jnp.max(jnp.abs(held[n]).reshape(tiles, BLOCK, COLS), axis=1)
        for c in range(COLS // BLOCK):
            cols = slice(c * BLOCK, (c + 1) * BLOCK)
            top = jnp.max(amax[:, cols], axis=1, keepdims=True)
            scales = ((top + 1e-6) / 448.0).astype(jnp.bfloat16).astype(jnp.float32)
            inverses = 1.0 / scales
            for r in range(tiles):
                tile = held[n, r * BLOCK : (r + 1) * BLOCK, cols]
                coded = (tile * inverses[r : r + 1]).astype(jnp.bfloat16)
                value = (coded.astype(jnp.float32) * scales[r : r + 1]).astype(jnp.bfloat16)
                out[start + r * BLOCK : start + (r + 1) * BLOCK, cols] = value


def refit(table, master, first, n_outs):
    size = 8 * SHARE * COLS
    return pl.pallas_call(
        functools.partial(refit_kernel, first),
        in_specs=[pl.BlockSpec(memory_space=pltpu.SMEM), pl.BlockSpec(memory_space=pltpu.HBM)],
        out_specs=[pl.BlockSpec(memory_space=pltpu.VMEM)] * n_outs,
        out_shape=[jax.ShapeDtypeStruct((8 * SHARE // n_outs, COLS), jnp.bfloat16)] * n_outs,
        scratch_shapes=[pltpu.VMEM((8, SHARE, COLS), jnp.float32), pltpu.SemaphoreType.DMA((8,))],
        compiler_params=pltpu.CompilerParams(vmem_limit_bytes=44 * MIB),
        cost_estimate=pl.CostEstimate(flops=size * 6, bytes_accessed=size * 6, transcendentals=0),
    )(table, master)


def dot(a, b):
    return jnp.dot(a, b, preferred_element_type=jnp.float32)


def pieces(core, mine, near, far, cross):
    def cols(at, c):
        return pl.ds(pl.multiple_of(at + c * COLS, COLS), COLS)

    return [(mine, cols(0, core)), (near, cols(0, 1 - core)), (far, cols(2 * COLS, core)), (cross, cols(2 * COLS, 1 - core))]


def chunk(distance):
    if isinstance(distance, int):
        return pl.ds(distance * SHARE, SHARE)
    return pl.ds(pl.multiple_of(distance * SHARE, SHARE), SHARE)


def whole_kernel(table, mine, near, far, cross, y0, y1, y2, kept, passed, held, sems):
    core = table[CORE]
    for i, part in enumerate((y0, y1, y2)):
        for zs in range(4):
            to = held.at[i, :, :, chunk(table[Z_SLOT + zs])]
            pltpu.make_async_copy(part.at[zs], to, sems.at[i]).start()
    for i in range(3):
        pltpu.make_async_copy(held.at[i], held.at[i], sems.at[i]).wait()
        to = (table[Y_LAST + i] + 1) >> 1
        for half, out in ((1 - core, passed), (core, kept)):
            acts = held[i, half]
            for weight, cols in pieces(core, mine, near, far, cross):
                out[to, :, cols] = dot(acts, weight[: 4 * SHARE, :]).astype(out.dtype)


def early_kernel(table, mine, near, far, cross, z0, z1, z2, out, held, sems):
    core = table[CORE]
    for i, part in enumerate((z0, z1, z2)):
        pltpu.make_async_copy(part, held.at[i], sems.at[i]).start()
    for i in range(3):
        pltpu.make_async_copy(held.at[i], held.at[i], sems.at[i]).wait()
    for ys in range(4):
        for weight, cols in pieces(core, mine, near, far, cross):
            got = None
            for i in range(3):
                acts = held[i, ys].reshape(2 * HALF, SHARE)
                term = dot(acts, weight[chunk(table[Z_LAST + i]), :])
                got = term if got is None else got + term
            out[:, table[Y_SLOT + ys], :, cols] = got.reshape(2, HALF, COLS)


def late_kernel(keep, table, mine, near, far, cross, z3, y3, early, out, z_held, y_held, total, sems):
    core = table[CORE]
    half = core if keep else 1 - core

    def start(src, dst, which):
        pltpu.make_async_copy(src, dst, sems.at[which]).start()

    def ready(held, which):
        pltpu.make_async_copy(held, held, sems.at[which]).wait()

    for zs in range(4):
        start(y3.at[zs, half], y_held.at[:, chunk(table[Z_SLOT + zs])], 0)
    start(z3.at[:, half], z_held, 1)
    start(early.at[half], total, 2)
    weights = pieces(core, mine, near, far, cross)
    ready(y_held, 0)
    for weight, cols in weights:
        out[4, :, cols] = dot(y_held[...], weight[: 4 * SHARE, :]).astype(out.dtype)
    ready(z_held, 1)
    ready(total, 2)
    acts = z_held[...].reshape(4 * HALF, SHARE)
    for weight, cols in weights:
        got = dot(acts, weight[chunk(2), :]).reshape(4, HALF, COLS)
        for ys in range(4):
            to = table[Y_SLOT + ys]
            out[to, :, cols] = (total[to, :, cols] + got[ys]).astype(out.dtype)


def product(kernel, table, weights, parts, outs, held, work):
    vmem, anywhere = pl.BlockSpec(memory_space=pltpu.VMEM), pl.BlockSpec(memory_space=pl.ANY)
    return pl.pallas_call(
        kernel,
        in_specs=[pl.BlockSpec(memory_space=pltpu.SMEM)] + [vmem] * 4 + [anywhere] * len(parts),
        out_specs=[vmem] * len(outs),
        out_shape=[jax.ShapeDtypeStruct(shape, t) for shape, t in outs],
        scratch_shapes=held,
        compiler_params=pltpu.CompilerParams(vmem_limit_bytes=20 * MIB),
        cost_estimate=pl.CostEstimate(
            flops=work * 2 * 128 * 2048 * 1024, bytes_accessed=work * MIB, transcendentals=0
        ),
    )(table, *weights, *parts)


def spread_kernel(table, owner, own, other, *outs):
    for k, out in enumerate(outs):
        section = owner[table[DEST + k]]
        half = jnp.where(section >= 4, 1, 0)
        far = jnp.where(half == table[XH], 0, 1)
        at = (table[Y] + 8 - section) & 3

        @pl.when(far == table[CORE])
        def _():
            out[...] = own[at]

        @pl.when(far != table[CORE])
        def _():
            out[...] = other[at]


def arrange_kernel(table, *refs):
    parts, out, sems = refs[:4], refs[4], refs[5]
    copies = []
    for dz, part in enumerate(parts):
        at = pl.multiple_of(((table[Z] + 4 - dz) & 3) * (2 * COLS), 2 * COLS)
        copies.append(pltpu.make_async_copy(part, out.at[:, pl.ds(at, 2 * COLS)], sems.at[dz]))
        copies[-1].start()
    for copy in copies:
        copy.wait()


def small_call(kernel, scalars, parts, shapes, out_space, scratch=()):
    smem, vmem = pl.BlockSpec(memory_space=pltpu.SMEM), pl.BlockSpec(memory_space=pltpu.VMEM)
    return pl.pallas_call(
        kernel,
        in_specs=[smem] * len(scalars) + [vmem] * len(parts),
        out_specs=[pl.BlockSpec(memory_space=out_space)] * len(shapes),
        out_shape=[jax.ShapeDtypeStruct(shape, jnp.bfloat16) for shape in shapes],
        scratch_shapes=scratch,
        compiler_params=pltpu.CompilerParams(vmem_limit_bytes=16 * MIB),
        cost_estimate=pl.CostEstimate(flops=0, bytes_accessed=2 * MIB, transcendentals=0),
    )(*scalars, *parts)


def shards(master, activations, owner):
    f32, bf16 = jnp.float32, jnp.bfloat16
    rows = jnp.asarray(np.array([device_row(i) for i in range(N_DEV)], np.int32))
    me = lax.axis_index("group") * 16 + lax.axis_index("tp")
    table = lax.dynamic_index_in_dim(rows, me, 0, keepdims=False)

    same, swapped = refit(table, master, AWAY, 2)
    swapped = permute(swapped, other_chip)
    slots, relays = gather(activations, lax.axis_index("tp") % 2, same, swapped)
    far = after(permute(after(same, swapped), other_chip), *relays)
    sent, mine = refit(table, master, HERE, 2)
    near = permute(sent, other_core)
    cross = permute(swapped, other_core)
    weights = [mine, near, far, cross]

    wide = 4 * COLS
    kept, passed = product(
        whole_kernel,
        table,
        weights,
        slots["y"][:3],
        [((3, HALF, wide), f32), ((3, HALF, wide), bf16)],
        [pltpu.VMEM((3, 2, HALF, 4 * SHARE), bf16), pltpu.SemaphoreType.DMA((3,))],
        6,
    )
    (early,) = product(
        early_kernel,
        after(table, passed),
        weights,
        slots["z"][:3],
        [((2, 4, HALF, wide), f32)],
        [pltpu.VMEM((3, 4, 2, HALF, SHARE), bf16), pltpu.SemaphoreType.DMA((3,))],
        6,
    )

    def cores_sum(kept, passed):
        both = kept + permute(passed, other_core).astype(f32)
        return both[..., : 2 * COLS], both[..., 2 * COLS :].astype(bf16)

    def chips_sum(own, sent):
        return (own + permute(sent, other_chip).astype(f32)).astype(bf16)

    own, sent = cores_sum(kept, passed)
    late_table = after(table, sent)
    whole = chips_sum(own, sent)
    passed, kept = (
        product(
            functools.partial(late_kernel, keep),
            late_table,
            weights,
            [slots["z"][3], slots["y"][3], early],
            [((5, HALF, wide), f32 if keep else bf16)],
            [
                pltpu.VMEM((4, HALF, SHARE), bf16),
                pltpu.VMEM((HALF, 4 * SHARE), bf16),
                pltpu.VMEM((4, HALF, wide), f32),
                pltpu.SemaphoreType.DMA((3,)),
            ],
            2,
        )[0]
        for keep in (False, True)
    )
    rest = chips_sum(*cores_sum(kept, passed))
    y_rows = (whole[0], whole[1], rest[4], whole[2])
    total = [jnp.concatenate([rest[dy], y_rows[dy]]) for dy in range(4)]

    got = {}
    for dy in (2, 1, 3, 0):
        got[dy] = permute(total[dy], lambda x, y, z, c: linear(x + 2 * c, y + dy, z, c))
    own = jnp.stack([got[dy] for dy in range(4)])
    other = permute(own, other_core)

    picked = small_call(spread_kernel, [table, owner], [own, other], [(256, 2 * COLS)] * 4, pltpu.VMEM)
    got = {}
    for dz in (2, 1, 3, 0):
        got[dz] = permute(picked[dz], lambda x, y, z, c: linear(x ^ c, y, z + dz, x % 2))
    got = [got[dz] for dz in range(4)]
    return small_call(arrange_kernel, [table], got, [(256, 8 * COLS)], pltpu.HBM, [pltpu.SemaphoreType.DMA((4,))])[0]


def solution(mesh):
    in_specs = (P(None, ("group", "tp")), P("group", "tp"), P())
    out_specs = P("group", "tp")
    return jax.shard_map(shards, mesh=mesh, in_specs=in_specs, out_specs=out_specs, check_vma=False)
```

time: 168 us -> 165 us (0.982)
  starting transfers between devices: 58.5 us -> 35.9 us
  waiting for transfers between devices: 76.6 us -> 91.1 us
  Pallas kernels: 23.4 us -> 28.3 us
    ppermute x32 -> x28, starting transfers between devices: 58.5 us -> 35.9 us  [permute(): lax.ppermute(value, AXES, [(i, move(*coords(i))) for i in range(N_DEV)])]
    ppermute x32 -> x28, waiting for transfers between devices: 76.6 us -> 91.1 us  [permute(): lax.ppermute(value, AXES, [(i, move(*coords(i))) for i in range(N_DEV)])]
    concatenate x12 -> x8, other arithmetic: 5.2 us -> 1.46 us  [the longest x4 1.39 us: gather(): jnp.concatenate([v, exchange(v, 'y' if part == 'z' else 'z', which)])]
    pallas_call x3 -> x4, Pallas kernels: 14.6 us -> 18 us  [product(): pl.pallas_call(kernel, in_specs=[pl.BlockSpec(memory_space=pltpu.SMEM)] +...]
    select_n x0 -> x2, other arithmetic: none -> 2.84 us  [gather(): relays.append(jnp.where(core == 0, first, second))]
    unnamed x10 -> x16, local copies, waits for them, and re-layouts: 0.02 us -> 2.2 us
    broadcast_in_dim x2 -> x0, local copies, waits for them, and re-layouts: 1.84 us -> none  [shards(): activations[None, at:at + n]]
  transfers between devices with their start and end apart: 32 -> 28, of which waited for: 19 -> 17; matrix products, arithmetic and copies ran while one was open for 3% -> 4% of each run, Pallas kernels for 10% -> 11%
where the time goes in v8:
time: 165 us; the launch traced here: 164 us
  waiting for transfers between devices  91.1 us (55%)
  starting transfers between devices  35.9 us (22%)
  Pallas kernels  28.3 us (17%)
  other arithmetic  5.52 us (3%)
  local copies, waits for them, and re-layouts  3.12 us (2%)
    ppermute x28, waiting for transfers between devices, permute(): lax.ppermute(value, AXES, [(i, move(*coords(i))) for i in range(N_DEV)])  91.1 us
    ppermute x28, starting transfers between devices, permute(): lax.ppermute(value, AXES, [(i, move(*coords(i))) for i in range(N_DEV)])  35.9 us
    pallas_call x4, Pallas kernels, product(): pl.pallas_call(kernel, in_specs=[pl.BlockSpec(memory_space=pltpu.SMEM)] +...  18 us
    pallas_call x2, Pallas kernels, refit(): pl.pallas_call(functools.partial(refit_kernel, first), in_specs=[pl.Block...  8.11 us
  transfers between devices with their start and end apart: 28, of which 17 were waited for; matrix products, arithmetic and copies ran while one was open for 4% of the time, Pallas kernels for 11%

profile of v8, /device:TPU:3, one launch (start us, length us, event | category | flops | bytes accessed | tf_op | source)
XLA Modules:
  0.0 164.5 jit_solution(11032966380832924161)
XLA Ops:
  0.0 1.8 %collective-permute-start.3 = (bf16[256,512]{1,0:T(8,128)(2,1)}, bf16[256,512]{1,0:T(8,128)(2,1)S(1)}, u32[]{:S(2)}, u32[]{:S(2)}) collective-permute-start(bf16[256,512]{1,0:T(8,128)(2,1)} %param.5), channel_id=1, source_target_pairs={{0,64},{1,65},{2,66},{3,67},{4,68},{5,69},{6,70},{7,71},{8,72},{9,... | collective-permute-start | bytes 786440 | tf_op jit(solution)/shard_map/ppermute | solution.py:30
  1.8 0.7 dynamic-slice_bitcast_fusion.table
  2.5 4.1 %shard_map.47 = (bf16[2048,256]{1,0:T(8,128)(2,1)}, bf16[2048,256]{1,0:T(8,128)(2,1)S(1)}) custom-call(s32[40]{0:T(128)S(1)} %dynamic-slice_bitcast_fusion.table, f32[8192,256]{1,0:T(8,128)} %master.3), custom_call_target="tpu_custom_call" | custom-call | flops 6291456 | bytes 6291456 | tf_op jit(solution)/shard_map/pallas_call | solution.py:133
  6.6 2.3 %collective-permute-done.3 = bf16[256,512]{1,0:T(8,128)(2,1)S(1)} collective-permute-done((bf16[256,512]{1,0:T(8,128)(2,1)}, bf16[256,512]{1,0:T(8,128)(2,1)S(1)}, u32[]{:S(2)}, u32[]{:S(2)}) %collective-permute-start.3) | collective-permute-done | bytes 262176 | tf_op jit(solution)/shard_map/ppermute | solution.py:30
  8.9 3.8 %collective-permute-start.4 = (bf16[1,2,128,512]{3,2,1,0:T(8,128)(2,1)S(1)}, bf16[1,2,128,512]{3,2,1,0:T(8,128)(2,1)S(1)}, u32[]{:S(2)}, u32[]{:S(2)}) collective-permute-start(bf16[1,2,128,512]{3,2,1,0:T(8,128)(2,1)S(1)} %get-tuple-element.34), channel_id=1, source_target_pairs={{0,2},{1,7},{2,0},{3,5},{4,6},{5,3},{6,4},{7,1},{8,10},{9,15},{10,... | collective-permute-start | bytes 786440 | tf_op jit(solution)/shard_map/ppermute | solution.py:30
  12.8 2.7 %collective-permute-start.5 = (bf16[1,2,128,512]{3,2,1,0:T(8,128)(2,1)S(1)}, bf16[1,2,128,512]{3,2,1,0:T(8,128)(2,1)S(1)}, u32[]{:S(2)}, u32[]{:S(2)}) collective-permute-start(bf16[1,2,128,512]{3,2,1,0:T(8,128)(2,1)S(1)} %get-tuple-element.35), channel_id=1, source_target_pairs={{0,16},{1,49},{2,18},{3,51},{4,20},{5,53},{6,22},{7,55},{8,24},{9,... | collective-permute-start | bytes 786440 | tf_op jit(solution)/shard_map/ppermute | solution.py:30
  15.5 0.3 collective-permute-start.1
  15.8 0.8 collective-permute-done.4
  16.6 2.7 %collective-permute-done.5 = bf16[1,2,128,512]{3,2,1,0:T(8,128)(2,1)S(1)} collective-permute-done((bf16[1,2,128,512]{3,2,1,0:T(8,128)(2,1)S(1)}, bf16[1,2,128,512]{3,2,1,0:T(8,128)(2,1)S(1)}, u32[]{:S(2)}, u32[]{:S(2)}) %collective-permute-start.5) | collective-permute-done | bytes 262176 | tf_op jit(solution)/shard_map/ppermute | solution.py:30
  19.3 0.1 collective-permute-start.6
  19.4 0.5 collective-permute-start.7
  19.9 7.9 %collective-permute-done.6 = bf16[2,2,128,512]{3,2,1,0:T(8,128)(2,1)S(1)} collective-permute-done((bf16[2,2,128,512]{3,2,1,0:T(8,128)(2,1)S(1)}, bf16[2,2,128,512]{3,2,1,0:T(8,128)(2,1)S(1)}, u32[]{:S(2)}, u32[]{:S(2)}) %collective-permute-start.6) | collective-permute-done | bytes 524320 | tf_op jit(solution)/shard_map/ppermute | solution.py:30
  27.8 0.1 pad_maximum_fusion.y0
  27.9 1.2 pad_maximum_fusion.1.z0
  29.1 10.4 %collective-permute-done.1 = bf16[2048,256]{1,0:T(8,128)(2,1)} collective-permute-done((bf16[2048,256]{1,0:T(8,128)(2,1)S(1)}, bf16[2048,256]{1,0:T(8,128)(2,1)}, u32[]{:S(2)}, u32[]{:S(2)}) %collective-permute-start.1) | collective-permute-done | bytes 1048608 | tf_op jit(solution)/shard_map/ppermute | solution.py:30
  39.5 0.4 collective-permute-start.9
  39.9 4.0 %shard_map.46 = (bf16[2048,256]{1,0:T(8,128)(2,1)}, bf16[2048,256]{1,0:T(8,128)(2,1)S(1)}) custom-call(s32[40]{0:T(128)S(1)} %dynamic-slice_bitcast_fusion.table, f32[8192,256]{1,0:T(8,128)} %master.3), custom_call_target="tpu_custom_call" | custom-call | flops 6291456 | bytes 6291456 | tf_op jit(solution)/shard_map/pallas_call | solution.py:133
  44.0 0.3 collective-permute-start.2
  44.3 21.5 %collective-permute-done.9.y2 = bf16[4,2,128,512]{3,2,1,0:T(8,128)(2,1)S(1)} collective-permute-done((bf16[4,2,128,512]{3,2,1,0:T(8,128)(2,1)S(1)}, bf16[4,2,128,512]{3,2,1,0:T(8,128)(2,1)S(1)}, u32[]{:S(2)}, u32[]{:S(2)}) %collective-permute-start.9) | collective-permute-done | bytes 1048608 | tf_op jit(solution)/shard_map/ppermute | solution.py:30
  65.8 0.5 collective-permute-start
  66.3 0.5 copy-done.2
  66.8 1.1 copy-done.4
  67.9 0.5 collective-permute-start.12
  68.4 1.3 broadcast_select_fusion.1
  69.7 1.5 broadcast_select_fusion
  71.3 0.3 copy-done.3
  71.5 0.3 copy-done.5
  71.9 5.4 %shard_map.48 = (f32[3,128,1024]{2,1,0:T(8,128)S(1)}, bf16[3,128,1024]{2,1,0:T(8,128)(2,1)S(1)}) custom-call(s32[40]{0:T(128)S(1)} %dynamic-slice_bitcast_fusion.table, bf16[2048,256]{1,0:T(8,128)(2,1)S(1)} %get-tuple-element.28.mine, bf16[2048,256]{1,0:T(8,128)(2,1)S(1)} %collective-permute-done.near, bf16[2048,256]{1,0:T(8,128)(2,1)S(1)} %collective-permute-done.2.far, ...), custom_call_target="tpu_custom_call" | custom-call | flops 3221225472 | bytes 6291456 | tf_op jit(solution)/shard_map/pallas_call | solution.py:222
  77.2 0.1 collective-permute-start.13
  77.4 0.8 collective-permute-start.14
  78.2 6.6 %shard_map.49.early = f32[2,4,128,1024]{3,2,1,0:T(8,128)S(1)} custom-call(s32[40]{0:T(128)S(1)} %dynamic-slice_bitcast_fusion.table, bf16[2048,256]{1,0:T(8,128)(2,1)S(1)} %get-tuple-element.28.mine, bf16[2048,256]{1,0:T(8,128)(2,1)S(1)} %collective-permute-done.near, bf16[2048,256]{1,0:T(8,128)(2,1)S(1)} %collective-permute-done.2.far, ...), custom_call_target="tpu_custom_call" | custom-call | flops 3221225472 | bytes 6291456 | tf_op jit(solution)/shard_map/pallas_call | solution.py:222
  84.8 0.3 convert_add_fusion.1
  85.2 6.1 %collective-permute-done.15.y3 = bf16[4,2,128,512]{3,2,1,0:T(8,128)(2,1)S(1)} collective-permute-done((bf16[4,2,128,512]{3,2,1,0:T(8,128)(2,1)S(1)}, bf16[4,2,128,512]{3,2,1,0:T(8,128)(2,1)S(1)}, u32[]{:S(2)}, u32[]{:S(2)}) %collective-permute-start.15) | collective-permute-done | bytes 1048608 | tf_op jit(solution)/shard_map/ppermute | solution.py:30
  91.4 0.3 collective-permute-done.14.z3
  91.6 3.0 %shard_map.51 = bf16[5,128,1024]{2,1,0:T(8,128)(2,1)S(1)} custom-call(s32[40]{0:T(128)S(1)} %dynamic-slice_bitcast_fusion.table, bf16[2048,256]{1,0:T(8,128)(2,1)S(1)} %get-tuple-element.28.mine, bf16[2048,256]{1,0:T(8,128)(2,1)S(1)} %collective-permute-done.near, bf16[2048,256]{1,0:T(8,128)(2,1)S(1)} %collective-permute-done.2.far, ...), custom_call_target="tpu_custom_call" | custom-call | flops 1073741824 | bytes 2097152 | tf_op jit(solution)/shard_map/pallas_call | solution.py:222
  94.7 3.1 %collective-permute-start.16 = (bf16[5,128,1024]{2,1,0:T(8,128)(2,1)S(1)}, bf16[5,128,1024]{2,1,0:T(8,128)(2,1)S(1)}, u32[]{:S(2)}, u32[]{:S(2)}) collective-permute-start(bf16[5,128,1024]{2,1,0:T(8,128)(2,1)S(1)} %shard_map.51), channel_id=1, source_target_pairs={{0,1},{1,0},{2,3},{3,2},{4,5},{5,4},{6,7},{7,6},{8,9},{9,8},{10,11... | collective-permute-start | bytes 3932168 | tf_op jit(solution)/shard_map/ppermute | solution.py:30
  97.7 0.3 collective-permute-start.18
  98.0 3.0 %shard_map.50 = f32[5,128,1024]{2,1,0:T(8,128)S(1)} custom-call(s32[40]{0:T(128)S(1)} %dynamic-slice_bitcast_fusion.table, bf16[2048,256]{1,0:T(8,128)(2,1)S(1)} %get-tuple-element.28.mine, bf16[2048,256]{1,0:T(8,128)(2,1)S(1)} %collective-permute-done.near, bf16[2048,256]{1,0:T(8,128)(2,1)S(1)} %collective-permute-done.2.far, ...), custom_call_target="tpu_custom_call" | custom-call | flops 1073741824 | bytes 2097152 | tf_op jit(solution)/shard_map/pallas_call | solution.py:222
  101.1 0.4 convert_add_fusion
  101.5 0.1 slice.96
  101.6 1.3 collective-permute-start.17
  102.9 5.5 %collective-permute-done.18 = bf16[3,128,512]{2,1,0:T(8,128)(2,1)S(1)} collective-permute-done((bf16[3,128,512]{2,1,0:T(8,128)(2,1)S(1)}, bf16[3,128,512]{2,1,0:T(8,128)(2,1)S(1)}, u32[]{:S(2)}, u32[]{:S(2)}) %collective-permute-start.18) | collective-permute-done | bytes 393248 | tf_op jit(solution)/shard_map/ppermute | solution.py:30
  108.4 0.1 fusion.1
  108.6 13.9 %collective-permute-done.17 = bf16[5,128,512]{2,1,0:T(8,128)(2,1)S(1)} collective-permute-done((bf16[5,128,512]{2,1,0:T(8,128)(2,1)S(1)}, bf16[5,128,512]{2,1,0:T(8,128)(2,1)S(1)}, u32[]{:S(2)}, u32[]{:S(2)}) %collective-permute-start.17) | collective-permute-done | bytes 655392 | tf_op jit(solution)/shard_map/ppermute | solution.py:30
  122.4 0.2 fusion
  122.8 2.4 %collective-permute-start.21 = (bf16[256,512]{1,0:T(8,128)(2,1)S(1)}, bf16[256,512]{1,0:T(8,128)(2,1)S(1)}, u32[]{:S(2)}, u32[]{:S(2)}) collective-permute-start(bf16[256,512]{1,0:T(8,128)(2,1)S(1)} %pad_maximum_fusion.8), channel_id=1, source_target_pairs={{0,32},{1,97},{2,34},{3,99},{4,36},{5,101},{6,38},{7,103},{8,40},{... | collective-permute-start | bytes 786440 | tf_op jit(solution)/shard_map/ppermute | solution.py:30
  125.2 2.9 %collective-permute-start.20 = (bf16[256,512]{1,0:T(8,128)(2,1)S(1)}, bf16[256,512]{1,0:T(8,128)(2,1)S(1)}, u32[]{:S(2)}, u32[]{:S(2)}) collective-permute-start(bf16[256,512]{1,0:T(8,128)(2,1)S(1)} %pad_maximum_fusion.7), channel_id=1, source_target_pairs={{0,16},{1,81},{2,18},{3,83},{4,20},{5,85},{6,22},{7,87},{8,24},{9,... | collective-permute-start | bytes 786440 | tf_op jit(solution)/shard_map/ppermute | solution.py:30
  128.1 2.3 %collective-permute-start.22 = (bf16[256,512]{1,0:T(8,128)(2,1)S(1)}, bf16[256,512]{1,0:T(8,128)(2,1)S(1)}, u32[]{:S(2)}, u32[]{:S(2)}) collective-permute-start(bf16[256,512]{1,0:T(8,128)(2,1)S(1)} %pad_maximum_fusion.9), channel_id=1, source_target_pairs={{0,48},{1,113},{2,50},{3,115},{4,52},{5,117},{6,54},{7,119},{8,56}... | collective-permute-start | bytes 786440 | tf_op jit(solution)/shard_map/ppermute | solution.py:30
  130.4 3.0 %collective-permute-start.19 = (bf16[256,512]{1,0:T(8,128)(2,1)S(1)}, bf16[256,512]{1,0:T(8,128)(2,1)S(1)}, u32[]{:S(2)}, u32[]{:S(2)}) collective-permute-start(bf16[256,512]{1,0:T(8,128)(2,1)S(1)} %pad_maximum_fusion.6), channel_id=1, source_target_pairs={{0,0},{1,65},{2,2},{3,67},{4,4},{5,69},{6,6},{7,71},{8,8},{9,73},{... | collective-permute-start | bytes 786440 | tf_op jit(solution)/shard_map/ppermute | solution.py:30
  133.5 1.5 collective-permute-done.20
  135.0 2.6 %collective-permute-done.22 = bf16[256,512]{1,0:T(8,128)(2,1)S(1)} collective-permute-done((bf16[256,512]{1,0:T(8,128)(2,1)S(1)}, bf16[256,512]{1,0:T(8,128)(2,1)S(1)}, u32[]{:S(2)}, u32[]{:S(2)}) %collective-permute-start.22) | collective-permute-done | bytes 262176 | tf_op jit(solution)/shard_map/ppermute | solution.py:30
  137.6 2.0 %collective-permute-done.19 = bf16[256,512]{1,0:T(8,128)(2,1)S(1)} collective-permute-done((bf16[256,512]{1,0:T(8,128)(2,1)S(1)}, bf16[256,512]{1,0:T(8,128)(2,1)S(1)}, u32[]{:S(2)}, u32[]{:S(2)}) %collective-permute-start.19) | collective-permute-done | bytes 262176 | tf_op jit(solution)/shard_map/ppermute | solution.py:30
  139.6 0.1 pad_maximum_fusion.2.own
  139.8 0.5 collective-permute-start.23
  140.2 2.3 %collective-permute-done.23.other = bf16[4,256,512]{2,1,0:T(8,128)(2,1)S(1)} collective-permute-done((bf16[4,256,512]{2,1,0:T(8,128)(2,1)S(1)}, bf16[4,256,512]{2,1,0:T(8,128)(2,1)S(1)}, u32[]{:S(2)}, u32[]{:S(2)}) %collective-permute-start.23) | collective-permute-done | bytes 1048608 | tf_op jit(solution)/shard_map/ppermute | solution.py:30
  142.5 0.7 shard_map.52
  143.2 2.8 %collective-permute-start.24 = (bf16[256,512]{1,0:T(8,128)(2,1)S(1)}, bf16[256,512]{1,0:T(8,128)(2,1)S(1)}, u32[]{:S(2)}, u32[]{:S(2)}) collective-permute-start(bf16[256,512]{1,0:T(8,128)(2,1)S(1)} %get-tuple-element.47), channel_id=1, source_target_pairs={{0,0},{1,8},{2,2},{3,10},{4,4},{5,12},{6,6},{7,14},{8,9},{9,1},{10... | collective-permute-start | bytes 786440 | tf_op jit(solution)/shard_map/ppermute | solution.py:30
  146.0 0.6 collective-permute-start.25
  146.6 3.1 %collective-permute-start.26 = (bf16[256,512]{1,0:T(8,128)(2,1)S(1)}, bf16[256,512]{1,0:T(8,128)(2,1)S(1)}, u32[]{:S(2)}, u32[]{:S(2)}) collective-permute-start(bf16[256,512]{1,0:T(8,128)(2,1)S(1)} %get-tuple-element.49), channel_id=1, source_target_pairs={{0,4},{1,12},{2,6},{3,14},{4,0},{5,8},{6,2},{7,10},{8,13},{9,5},{1... | collective-permute-start | bytes 786440 | tf_op jit(solution)/shard_map/ppermute | solution.py:30
  149.8 1.7 %collective-permute-start.27 = (bf16[256,512]{1,0:T(8,128)(2,1)S(1)}, bf16[256,512]{1,0:T(8,128)(2,1)S(1)}, u32[]{:S(2)}, u32[]{:S(2)}) collective-permute-start(bf16[256,512]{1,0:T(8,128)(2,1)S(1)} %get-tuple-element.50), channel_id=1, source_target_pairs={{0,6},{1,14},{2,0},{3,8},{4,2},{5,10},{6,4},{7,12},{8,15},{9,7},{1... | collective-permute-start | bytes 786440 | tf_op jit(solution)/shard_map/ppermute | solution.py:30
  151.5 7.4 %collective-permute-done.25.refs_1_ = bf16[256,512]{1,0:T(8,128)(2,1)S(1)} collective-permute-done((bf16[256,512]{1,0:T(8,128)(2,1)S(1)}, bf16[256,512]{1,0:T(8,128)(2,1)S(1)}, u32[]{:S(2)}, u32[]{:S(2)}) %collective-permute-start.25) | collective-permute-done | bytes 262176 | tf_op jit(solution)/shard_map/ppermute | solution.py:30
  158.9 3.3 %collective-permute-done.26.refs_2_ = bf16[256,512]{1,0:T(8,128)(2,1)S(1)} collective-permute-done((bf16[256,512]{1,0:T(8,128)(2,1)S(1)}, bf16[256,512]{1,0:T(8,128)(2,1)S(1)}, u32[]{:S(2)}, u32[]{:S(2)}) %collective-permute-start.26) | collective-permute-done | bytes 262176 | tf_op jit(solution)/shard_map/ppermute | solution.py:30
  162.2 0.6 collective-permute-done.27.refs_3_
  162.8 1.5 shard_map.53
  (37 shorter events, 0.4 us)
Async XLA Ops:
  0.0 8.9 %collective-permute-start.3 = (bf16[256,512]{1,0:T(8,128)(2,1)}, bf16[256,512]{1,0:T(8,128)(2,1)S(1)}, u32[]{:S(2)}, u32[]{:S(2)}) collective-permute-start(bf16[256,512]{1,0:T(8,128)(2,1)} %param.5), channel_id=1, source_target_pairs={{0,64},{1,65},{2,66},{3,67},{4,68},{5,69},{6,70},{7,71},{8,72},{9,... | collective-permute-start | bytes 786440 | tf_op jit(solution)/shard_map/ppermute | solution.py:30
  2.5 6.4 %copy-start.7 = (bf16[256,512]{1,0:T(8,128)(2,1)S(1)}, bf16[256,512]{1,0:T(8,128)(2,1)}, u32[]{:S(2)}) copy-start(bf16[256,512]{1,0:T(8,128)(2,1)} %param.5) | copy-start | bytes 786436
  8.9 7.6 %collective-permute-start.4 = (bf16[1,2,128,512]{3,2,1,0:T(8,128)(2,1)S(1)}, bf16[1,2,128,512]{3,2,1,0:T(8,128)(2,1)S(1)}, u32[]{:S(2)}, u32[]{:S(2)}) collective-permute-start(bf16[1,2,128,512]{3,2,1,0:T(8,128)(2,1)S(1)} %get-tuple-element.34), channel_id=1, source_target_pairs={{0,2},{1,7},{2,0},{3,5},{4,6},{5,3},{6,4},{7,1},{8,10},{9,15},{10,... | collective-permute-start | bytes 786440 | tf_op jit(solution)/shard_map/ppermute | solution.py:30
  12.8 6.5 %collective-permute-start.5 = (bf16[1,2,128,512]{3,2,1,0:T(8,128)(2,1)S(1)}, bf16[1,2,128,512]{3,2,1,0:T(8,128)(2,1)S(1)}, u32[]{:S(2)}, u32[]{:S(2)}) collective-permute-start(bf16[1,2,128,512]{3,2,1,0:T(8,128)(2,1)S(1)} %get-tuple-element.35), channel_id=1, source_target_pairs={{0,16},{1,49},{2,18},{3,51},{4,20},{5,53},{6,22},{7,55},{8,24},{9,... | collective-permute-start | bytes 786440 | tf_op jit(solution)/shard_map/ppermute | solution.py:30
  15.5 24.0 %collective-permute-start.1 = (bf16[2048,256]{1,0:T(8,128)(2,1)S(1)}, bf16[2048,256]{1,0:T(8,128)(2,1)}, u32[]{:S(2)}, u32[]{:S(2)}) collective-permute-start(bf16[2048,256]{1,0:T(8,128)(2,1)S(1)} %get-tuple-element.31), channel_id=1, source_target_pairs={{0,8},{1,9},{2,10},{3,11},{4,12},{5,13},{6,14},{7,15},{8,0},{9,1},... | collective-permute-start | bytes 3145736 | tf_op jit(solution)/shard_map/ppermute | solution.py:30
  19.3 8.5 %collective-permute-start.6 = (bf16[2,2,128,512]{3,2,1,0:T(8,128)(2,1)S(1)}, bf16[2,2,128,512]{3,2,1,0:T(8,128)(2,1)S(1)}, u32[]{:S(2)}, u32[]{:S(2)}) collective-permute-start(bf16[2,2,128,512]{3,2,1,0:T(8,128)(2,1)S(1)} %pad_maximum_fusion.3), channel_id=1, source_target_pairs={{0,6},{1,3},{2,4},{3,1},{4,2},{5,7},{6,0},{7,5},{8,14},{9,11},{10,... | collective-permute-start | bytes 1572872 | tf_op jit(solution)/shard_map/ppermute | solution.py:30
  19.4 8.5 %collective-permute-start.7 = (bf16[2,2,128,512]{3,2,1,0:T(8,128)(2,1)S(1)}, bf16[2,2,128,512]{3,2,1,0:T(8,128)(2,1)S(1)}, u32[]{:S(2)}, u32[]{:S(2)}) collective-permute-start(bf16[2,2,128,512]{3,2,1,0:T(8,128)(2,1)S(1)} %pad_maximum_fusion.4), channel_id=1, source_target_pairs={{0,48},{1,17},{2,50},{3,19},{4,52},{5,21},{6,54},{7,23},{8,56},{9,... | collective-permute-start | bytes 1572872 | tf_op jit(solution)/shard_map/ppermute | solution.py:30
  27.9 16.0 %copy-start = (bf16[4,2,128,512]{3,2,1,0:T(8,128)(2,1)}, bf16[4,2,128,512]{3,2,1,0:T(8,128)(2,1)S(1)}, u32[]{:S(2)}) copy-start(bf16[4,2,128,512]{3,2,1,0:T(8,128)(2,1)S(1)} %pad_maximum_fusion.y0) | copy-start | bytes 3145732
  39.5 26.3 %collective-permute-start.9 = (bf16[4,2,128,512]{3,2,1,0:T(8,128)(2,1)S(1)}, bf16[4,2,128,512]{3,2,1,0:T(8,128)(2,1)S(1)}, u32[]{:S(2)}, u32[]{:S(2)}) collective-permute-start(bf16[4,2,128,512]{3,2,1,0:T(8,128)(2,1)S(1)} %pad_maximum_fusion.y0), channel_id=1, source_target_pairs={{0,48},{1,49},{2,50},{3,51},{4,52},{5,53},{6,54},{7,55},{8,56},{9,... | collective-permute-start | bytes 3145736 | tf_op jit(solution)/shard_map/ppermute | solution.py:30
  39.9 26.4 %collective-permute-start.8 = (bf16[4,2,128,512]{3,2,1,0:T(8,128)(2,1)S(1)}, bf16[4,2,128,512]{3,2,1,0:T(8,128)(2,1)S(1)}, u32[]{:S(2)}, u32[]{:S(2)}) collective-permute-start(bf16[4,2,128,512]{3,2,1,0:T(8,128)(2,1)S(1)} %pad_maximum_fusion.y0), channel_id=1, source_target_pairs={{0,16},{1,17},{2,18},{3,19},{4,20},{5,21},{6,22},{7,23},{8,24},{9,... | collective-permute-start | bytes 3145736 | tf_op jit(solution)/shard_map/ppermute | solution.py:30
  39.9 29.8 %collective-permute-start.11 = (bf16[4,2,128,512]{3,2,1,0:T(8,128)(2,1)}, bf16[4,2,128,512]{3,2,1,0:T(8,128)(2,1)}, u32[]{:S(2)}, u32[]{:S(2)}) collective-permute-start(bf16[4,2,128,512]{3,2,1,0:T(8,128)(2,1)} %pad_maximum_fusion.1.z0), channel_id=1, source_target_pairs={{0,6},{1,7},{2,4},{3,5},{4,2},{5,3},{6,0},{7,1},{8,14},{9,15},{10,... | collective-permute-start | bytes 3145736 | tf_op jit(solution)/shard_map/ppermute | solution.py:30
  39.9 29.8 %collective-permute-start.10 = (bf16[4,2,128,512]{3,2,1,0:T(8,128)(2,1)}, bf16[4,2,128,512]{3,2,1,0:T(8,128)(2,1)}, u32[]{:S(2)}, u32[]{:S(2)}) collective-permute-start(bf16[4,2,128,512]{3,2,1,0:T(8,128)(2,1)} %pad_maximum_fusion.1.z0), channel_id=1, source_target_pairs={{0,2},{1,3},{2,0},{3,1},{4,6},{5,7},{6,4},{7,5},{8,10},{9,11},{10,... | collective-permute-start | bytes 3145736 | tf_op jit(solution)/shard_map/ppermute | solution.py:30
  44.0 27.3 %collective-permute-start.2 = (bf16[2048,256]{1,0:T(8,128)(2,1)}, bf16[2048,256]{1,0:T(8,128)(2,1)S(1)}, u32[]{:S(2)}, u32[]{:S(2)}) collective-permute-start(bf16[2048,256]{1,0:T(8,128)(2,1)} %get-tuple-element.32), channel_id=1, source_target_pairs={{0,8},{1,9},{2,10},{3,11},{4,12},{5,13},{6,14},{7,15},{8,0},{9,1},... | collective-permute-start | bytes 3145736 | tf_op jit(solution)/shard_map/ppermute | solution.py:30
  65.8 1.0 copy-start.2
  65.8 5.4 %collective-permute-start = (bf16[2048,256]{1,0:T(8,128)(2,1)}, bf16[2048,256]{1,0:T(8,128)(2,1)S(1)}, u32[]{:S(2)}, u32[]{:S(2)}) collective-permute-start(bf16[2048,256]{1,0:T(8,128)(2,1)} %get-tuple-element.29), channel_id=1, source_target_pairs={{0,1},{1,0},{2,3},{3,2},{4,5},{5,4},{6,7},{7,6},{8,9},{9,8},{10,11... | collective-permute-start | bytes 3145736 | tf_op jit(solution)/shard_map/ppermute | solution.py:30
  66.8 1.1 copy-start.4
  67.9 3.4 %collective-permute-start.12 = (bf16[2048,256]{1,0:T(8,128)(2,1)}, bf16[2048,256]{1,0:T(8,128)(2,1)}, u32[]{:S(2)}, u32[]{:S(2)}) collective-permute-start(bf16[2048,256]{1,0:T(8,128)(2,1)} %collective-permute-done.1), channel_id=1, source_target_pairs={{0,1},{1,0},{2,3},{3,2},{4,5},{5,4},{6,7},{7,6},{8,9},{9,8},{10,11... | collective-permute-start | bytes 3145736 | tf_op jit(solution)/shard_map/ppermute | solution.py:30
  69.7 1.6 copy-start.1
  69.7 1.8 %copy-start.3 = (bf16[4,2,128,512]{3,2,1,0:T(8,128)(2,1)S(1)}, bf16[4,2,128,512]{3,2,1,0:T(8,128)(2,1)}, u32[]{:S(2)}) copy-start(bf16[4,2,128,512]{3,2,1,0:T(8,128)(2,1)} %copy-done.2) | copy-start | bytes 3145732
  69.7 2.2 %copy-start.5 = (bf16[4,2,128,512]{3,2,1,0:T(8,128)(2,1)S(1)}, bf16[4,2,128,512]{3,2,1,0:T(8,128)(2,1)}, u32[]{:S(2)}) copy-start(bf16[4,2,128,512]{3,2,1,0:T(8,128)(2,1)} %copy-done.4) | copy-start | bytes 3145732
  77.2 7.6 %collective-permute-start.13 = (bf16[3,128,1024]{2,1,0:T(8,128)(2,1)S(1)}, bf16[3,128,1024]{2,1,0:T(8,128)(2,1)S(1)}, u32[]{:S(2)}, u32[]{:S(2)}) collective-permute-start(bf16[3,128,1024]{2,1,0:T(8,128)(2,1)S(1)} %get-tuple-element.44), channel_id=1, source_target_pairs={{0,1},{1,0},{2,3},{3,2},{4,5},{5,4},{6,7},{7,6},{8,9},{9,8},{10,11... | collective-permute-start | bytes 2359304 | tf_op jit(solution)/shard_map/ppermute | solution.py:30
  77.4 14.0 %collective-permute-start.15 = (bf16[4,2,128,512]{3,2,1,0:T(8,128)(2,1)S(1)}, bf16[4,2,128,512]{3,2,1,0:T(8,128)(2,1)S(1)}, u32[]{:S(2)}, u32[]{:S(2)}) collective-permute-start(bf16[4,2,128,512]{3,2,1,0:T(8,128)(2,1)S(1)} %broadcast_select_fusion.1), channel_id=1, source_target_pairs={{0,48},{1,17},{2,50},{3,19},{4,52},{5,21},{6,54},{7,23},{8,56},{9,... | collective-permute-start | bytes 3145736 | tf_op jit(solution)/shard_map/ppermute | solution.py:30
  77.4 14.2 %collective-permute-start.14 = (bf16[4,2,128,512]{3,2,1,0:T(8,128)(2,1)S(1)}, bf16[4,2,128,512]{3,2,1,0:T(8,128)(2,1)S(1)}, u32[]{:S(2)}, u32[]{:S(2)}) collective-permute-start(bf16[4,2,128,512]{3,2,1,0:T(8,128)(2,1)S(1)} %broadcast_select_fusion), channel_id=1, source_target_pairs={{0,6},{1,3},{2,4},{3,1},{4,2},{5,7},{6,0},{7,5},{8,14},{9,11},{10,... | collective-permute-start | bytes 3145736 | tf_op jit(solution)/shard_map/ppermute | solution.py:30
  94.7 6.4 %collective-permute-start.16 = (bf16[5,128,1024]{2,1,0:T(8,128)(2,1)S(1)}, bf16[5,128,1024]{2,1,0:T(8,128)(2,1)S(1)}, u32[]{:S(2)}, u32[]{:S(2)}) collective-permute-start(bf16[5,128,1024]{2,1,0:T(8,128)(2,1)S(1)} %shard_map.51), channel_id=1, source_target_pairs={{0,1},{1,0},{2,3},{3,2},{4,5},{5,4},{6,7},{7,6},{8,9},{9,8},{10,11... | collective-permute-start | bytes 3932168 | tf_op jit(solution)/shard_map/ppermute | solution.py:30
  97.7 10.7 %collective-permute-start.18 = (bf16[3,128,512]{2,1,0:T(8,128)(2,1)S(1)}, bf16[3,128,512]{2,1,0:T(8,128)(2,1)S(1)}, u32[]{:S(2)}, u32[]{:S(2)}) collective-permute-start(bf16[3,128,512]{2,1,0:T(8,128)(2,1)S(1)} %slice.97), channel_id=1, source_target_pairs={{0,8},{1,9},{2,10},{3,11},{4,12},{5,13},{6,14},{7,15},{8,0},{9,1},... | collective-permute-start | bytes 1179656 | tf_op jit(solution)/shard_map/ppermute | solution.py:30
  101.6 20.9 %collective-permute-start.17 = (bf16[5,128,512]{2,1,0:T(8,128)(2,1)S(1)}, bf16[5,128,512]{2,1,0:T(8,128)(2,1)S(1)}, u32[]{:S(2)}, u32[]{:S(2)}) collective-permute-start(bf16[5,128,512]{2,1,0:T(8,128)(2,1)S(1)} %slice.96), channel_id=1, source_target_pairs={{0,8},{1,9},{2,10},{3,11},{4,12},{5,13},{6,14},{7,15},{8,0},{9,1},... | collective-permute-start | bytes 1966088 | tf_op jit(solution)/shard_map/ppermute | solution.py:30
  122.8 10.7 %collective-permute-start.21 = (bf16[256,512]{1,0:T(8,128)(2,1)S(1)}, bf16[256,512]{1,0:T(8,128)(2,1)S(1)}, u32[]{:S(2)}, u32[]{:S(2)}) collective-permute-start(bf16[256,512]{1,0:T(8,128)(2,1)S(1)} %pad_maximum_fusion.8), channel_id=1, source_target_pairs={{0,32},{1,97},{2,34},{3,99},{4,36},{5,101},{6,38},{7,103},{8,40},{... | collective-permute-start | bytes 786440 | tf_op jit(solution)/shard_map/ppermute | solution.py:30
  125.2 9.8 %collective-permute-start.20 = (bf16[256,512]{1,0:T(8,128)(2,1)S(1)}, bf16[256,512]{1,0:T(8,128)(2,1)S(1)}, u32[]{:S(2)}, u32[]{:S(2)}) collective-permute-start(bf16[256,512]{1,0:T(8,128)(2,1)S(1)} %pad_maximum_fusion.7), channel_id=1, source_target_pairs={{0,16},{1,81},{2,18},{3,83},{4,20},{5,85},{6,22},{7,87},{8,24},{9,... | collective-permute-start | bytes 786440 | tf_op jit(solution)/shard_map/ppermute | solution.py:30
  128.1 14.4 %copy-start.6 = (s32[8]{0:T(128)S(1)}, s32[8]{0:T(128)}, u32[]{:S(2)}) copy-start(s32[8]{0:T(128)} %owner.1) | copy-start | bytes 100
  128.1 9.5 %collective-permute-start.22 = (bf16[256,512]{1,0:T(8,128)(2,1)S(1)}, bf16[256,512]{1,0:T(8,128)(2,1)S(1)}, u32[]{:S(2)}, u32[]{:S(2)}) collective-permute-start(bf16[256,512]{1,0:T(8,128)(2,1)S(1)} %pad_maximum_fusion.9), channel_id=1, source_target_pairs={{0,48},{1,113},{2,50},{3,115},{4,52},{5,117},{6,54},{7,119},{8,56}... | collective-permute-start | bytes 786440 | tf_op jit(solution)/shard_map/ppermute | solution.py:30
  130.4 9.2 %collective-permute-start.19 = (bf16[256,512]{1,0:T(8,128)(2,1)S(1)}, bf16[256,512]{1,0:T(8,128)(2,1)S(1)}, u32[]{:S(2)}, u32[]{:S(2)}) collective-permute-start(bf16[256,512]{1,0:T(8,128)(2,1)S(1)} %pad_maximum_fusion.6), channel_id=1, source_target_pairs={{0,0},{1,65},{2,2},{3,67},{4,4},{5,69},{6,6},{7,71},{8,8},{9,73},{... | collective-permute-start | bytes 786440 | tf_op jit(solution)/shard_map/ppermute | solution.py:30
  139.8 2.8 %collective-permute-start.23 = (bf16[4,256,512]{2,1,0:T(8,128)(2,1)S(1)}, bf16[4,256,512]{2,1,0:T(8,128)(2,1)S(1)}, u32[]{:S(2)}, u32[]{:S(2)}) collective-permute-start(bf16[4,256,512]{2,1,0:T(8,128)(2,1)S(1)} %pad_maximum_fusion.2.own), channel_id=1, source_target_pairs={{0,1},{1,0},{2,3},{3,2},{4,5},{5,4},{6,7},{7,6},{8,9},{9,8},{10,11... | collective-permute-start | bytes 3145736 | tf_op jit(solution)/shard_map/ppermute | solution.py:30
  143.2 8.3 %collective-permute-start.24 = (bf16[256,512]{1,0:T(8,128)(2,1)S(1)}, bf16[256,512]{1,0:T(8,128)(2,1)S(1)}, u32[]{:S(2)}, u32[]{:S(2)}) collective-permute-start(bf16[256,512]{1,0:T(8,128)(2,1)S(1)} %get-tuple-element.47), channel_id=1, source_target_pairs={{0,0},{1,8},{2,2},{3,10},{4,4},{5,12},{6,6},{7,14},{8,9},{9,1},{10... | collective-permute-start | bytes 786440 | tf_op jit(solution)/shard_map/ppermute | solution.py:30
  146.0 12.8 %collective-permute-start.25 = (bf16[256,512]{1,0:T(8,128)(2,1)S(1)}, bf16[256,512]{1,0:T(8,128)(2,1)S(1)}, u32[]{:S(2)}, u32[]{:S(2)}) collective-permute-start(bf16[256,512]{1,0:T(8,128)(2,1)S(1)} %get-tuple-element.48), channel_id=1, source_target_pairs={{0,2},{1,10},{2,4},{3,12},{4,6},{5,14},{6,0},{7,8},{8,11},{9,3},{1... | collective-permute-start | bytes 786440 | tf_op jit(solution)/shard_map/ppermute | solution.py:30
  146.6 15.6 %collective-permute-start.26 = (bf16[256,512]{1,0:T(8,128)(2,1)S(1)}, bf16[256,512]{1,0:T(8,128)(2,1)S(1)}, u32[]{:S(2)}, u32[]{:S(2)}) collective-permute-start(bf16[256,512]{1,0:T(8,128)(2,1)S(1)} %get-tuple-element.49), channel_id=1, source_target_pairs={{0,4},{1,12},{2,6},{3,14},{4,0},{5,8},{6,2},{7,10},{8,13},{9,5},{1... | collective-permute-start | bytes 786440 | tf_op jit(solution)/shard_map/ppermute | solution.py:30
  149.8 13.0 %collective-permute-start.27 = (bf16[256,512]{1,0:T(8,128)(2,1)S(1)}, bf16[256,512]{1,0:T(8,128)(2,1)S(1)}, u32[]{:S(2)}, u32[]{:S(2)}) collective-permute-start(bf16[256,512]{1,0:T(8,128)(2,1)S(1)} %get-tuple-element.50), channel_id=1, source_target_pairs={{0,6},{1,14},{2,0},{3,8},{4,2},{5,10},{6,4},{7,12},{8,15},{9,7},{1... | collective-permute-start | bytes 786440 | tf_op jit(solution)/shard_map/ppermute | solution.py:30

commit v9 on v8

--- a/solution.py
+++ b/solution.py
@@ -75,12 +75,11 @@
             part: jnp.concatenate([v, exchange(v, "y" if part == "z" else "z", which)]) for part, v in blocks.items()
         }
         blocks = lax.optimization_barrier(blocks)
-    blocks, second_job = lax.optimization_barrier((blocks, second_job))
     slots, relays = {}, []
     for part, v in blocks.items():
         first = pair_exchange(v, part, 1)
         second = pair_exchange(v, part, 2)
-        relays.append(jnp.where(core == 0, first, second))
+        relays.append(after(jnp.where(core == 0, first, second), second_job))
         slots[part] = [v, first, second, exchange(relays[-1], part, 2)]
     return slots, relays
 
@@ -158,32 +157,29 @@
     return pl.ds(pl.multiple_of(distance * SHARE, SHARE), SHARE)
 
 
-def whole_kernel(table, mine, near, far, cross, y0, y1, y2, kept, passed, held, sems):
+def early_kernel(table, mine, near, far, cross, y0, y1, y2, z0, z1, z2, kept, passed, out, y_held, z_held, sems):
     core = table[CORE]
     for i, part in enumerate((y0, y1, y2)):
         for zs in range(4):
-            to = held.at[i, :, :, chunk(table[Z_SLOT + zs])]
+            to = y_held.at[i, :, :, chunk(table[Z_SLOT + zs])]
             pltpu.make_async_copy(part.at[zs], to, sems.at[i]).start()
+    for i, part in enumerate((z0, z1, z2)):
+        pltpu.make_async_copy(part, z_held.at[i], sems.at[3 + i]).start()
+    weights = pieces(core, mine, near, far, cross)
     for i in range(3):
-        pltpu.make_async_copy(held.at[i], held.at[i], sems.at[i]).wait()
+        pltpu.make_async_copy(y_held.at[i], y_held.at[i], sems.at[i]).wait()
         to = (table[Y_LAST + i] + 1) >> 1
-        for half, out in ((1 - core, passed), (core, kept)):
-            acts = held[i, half]
-            for weight, cols in pieces(core, mine, near, far, cross):
-                out[to, :, cols] = dot(acts, weight[: 4 * SHARE, :]).astype(out.dtype)
-
-
-def early_kernel(table, mine, near, far, cross, z0, z1, z2, out, held, sems):
-    core = table[CORE]
-    for i, part in enumerate((z0, z1, z2)):
-        pltpu.make_async_copy(part, held.at[i], sems.at[i]).start()
+        for half, result in ((1 - core, passed), (core, kept)):
+            acts = y_held[i, half]
+            for weight, cols in weights:
+                result[to, :, cols] = dot(acts, weight[: 4 * SHARE, :]).astype(result.dtype)
     for i in range(3):
-        pltpu.make_async_copy(held.at[i], held.at[i], sems.at[i]).wait()
+        pltpu.make_async_copy(z_held.at[i], z_held.at[i], sems.at[3 + i]).wait()
     for ys in range(4):
-        for weight, cols in pieces(core, mine, near, far, cross):
+        for weight, cols in weights:
             got = None
             for i in range(3):
-                acts = held[i, ys].reshape(2 * HALF, SHARE)
+                acts = z_held[i, ys].reshape(2 * HALF, SHARE)
                 term = dot(acts, weight[chunk(table[Z_LAST + i]), :])
                 got = term if got is None else got + term
             out[:, table[Y_SLOT + ys], :, cols] = got.reshape(2, HALF, COLS)
@@ -288,23 +284,18 @@
     weights = [mine, near, far, cross]
 
     wide = 4 * COLS
-    kept, passed = product(
-        whole_kernel,
+    kept, passed, early = product(
+        early_kernel,
         table,
         weights,
-        slots["y"][:3],
-        [((3, HALF, wide), f32), ((3, HALF, wide), bf16)],
-        [pltpu.VMEM((3, 2, HALF, 4 * SHARE), bf16), pltpu.SemaphoreType.DMA((3,))],
-        6,
-    )
-    (early,) = product(
-        early_kernel,
-        after(table, passed),
-        weights,
-        slots["z"][:3],
-        [((2, 4, HALF, wide), f32)],
-        [pltpu.VMEM((3, 4, 2, HALF, SHARE), bf16), pltpu.SemaphoreType.DMA((3,))],
-        6,
+        slots["y"][:3] + slots["z"][:3],
+        [((3, HALF, wide), f32), ((3, HALF, wide), bf16), ((2, 4, HALF, wide), f32)],
+        [
+            pltpu.VMEM((3, 2, HALF, 4 * SHARE), bf16),
+            pltpu.VMEM((3, 4, 2, HALF, SHARE), bf16),
+            pltpu.SemaphoreType.DMA((6,)),
+        ],
+        12,
     )
 
     def cores_sum(kept, passed):
@@ -335,12 +326,15 @@
         for keep in (False, True)
     )
     rest = chips_sum(*cores_sum(kept, passed))
-    y_rows = (whole[0], whole[1], rest[4], whole[2])
-    total = [jnp.concatenate([rest[dy], y_rows[dy]]) for dy in range(4)]
-
-    got = {}
-    for dy in (2, 1, 3, 0):
-        got[dy] = permute(total[dy], lambda x, y, z, c: linear(x + 2 * c, y + dy, z, c))
+
+    def back(rows, dy):
+        return permute(rows, lambda x, y, z, c: linear(x + 2 * c, y + dy, z, c))
+
+    first = {dy: back(whole[i], dy) for i, dy in ((1, 1), (2, 3), (0, 0))}
+    rest = after(rest, *first.values())
+    got = {2: back(jnp.concatenate([rest[2], rest[4]]), 2)}
+    for dy in (1, 3, 0):
+        got[dy] = jnp.concatenate([back(rest[dy], dy), first[dy]])
     own = jnp.stack([got[dy] for dy in range(4)])
     other = permute(own, other_core)
 

time: 165 us -> 171 us (1.036)
  starting transfers between devices: 35.9 us -> 60.8 us
  waiting for transfers between devices: 91.1 us -> 77.4 us
  Pallas kernels: 28.3 us -> 25.2 us
    ppermute x28 -> x31, starting transfers between devices: 35.9 us -> 60.8 us  [permute(): lax.ppermute(value, AXES, [(i, move(*coords(i))) for i in range(N_DEV)])]
    ppermute x28 -> x31, waiting for transfers between devices: 91.1 us -> 77.4 us  [permute(): lax.ppermute(value, AXES, [(i, move(*coords(i))) for i in range(N_DEV)])]
    pallas_call x4 -> x3, Pallas kernels: 18 us -> 14.8 us  [product(): pl.pallas_call(kernel, in_specs=[pl.BlockSpec(memory_space=pltpu.SMEM)] +...]
  transfers between devices with their start and end apart: 28 -> 31, of which waited for: 17 -> 19; matrix products, arithmetic and copies ran while one was open for 4% -> 3% of each run, Pallas kernels for 11% -> 7%
where the time goes in v9:
time: 171 us; the launch traced here: 170 us
  waiting for transfers between devices  77.4 us (45%)
  starting transfers between devices  60.8 us (36%)
  Pallas kernels  25.2 us (15%)
  other arithmetic  4.6 us (3%)
  local copies, waits for them, and re-layouts  1.91 us (1%)
    ppermute x31, waiting for transfers between devices, permute(): lax.ppermute(value, AXES, [(i, move(*coords(i))) for i in range(N_DEV)])  77.4 us
    ppermute x31, starting transfers between devices, permute(): lax.ppermute(value, AXES, [(i, move(*coords(i))) for i in range(N_DEV)])  60.8 us
    pallas_call x3, Pallas kernels, product(): pl.pallas_call(kernel, in_specs=[pl.BlockSpec(memory_space=pltpu.SMEM)] +...  14.8 us
    pallas_call x2, Pallas kernels, refit(): pl.pallas_call(functools.partial(refit_kernel, first), in_specs=[pl.Block...  8.11 us
  transfers between devices with their start and end apart: 31, of which 19 were waited for; matrix products, arithmetic and copies ran while one was open for 3% of the time, Pallas kernels for 7%

profile of v9, /device:TPU:3, one launch (start us, length us, event | category | flops | bytes accessed | tf_op | source)
XLA Modules:
  0.0 170.4 jit_solution(6666554571007773677)
XLA Ops:
  0.0 1.8 %collective-permute-start.3 = (bf16[256,512]{1,0:T(8,128)(2,1)}, bf16[256,512]{1,0:T(8,128)(2,1)S(1)}, u32[]{:S(2)}, u32[]{:S(2)}) collective-permute-start(bf16[256,512]{1,0:T(8,128)(2,1)} %param.5), channel_id=1, source_target_pairs={{0,64},{1,65},{2,66},{3,67},{4,68},{5,69},{6,70},{7,71},{8,72},{9,... | collective-permute-start | bytes 786440 | tf_op jit(solution)/shard_map/ppermute | solution.py:30
  1.8 0.7 dynamic-slice_bitcast_fusion.table
  2.5 4.1 %shard_map.47 = (bf16[2048,256]{1,0:T(8,128)(2,1)}, bf16[2048,256]{1,0:T(8,128)(2,1)S(1)}) custom-call(s32[40]{0:T(128)S(1)} %dynamic-slice_bitcast_fusion.table, f32[8192,256]{1,0:T(8,128)} %master.3), custom_call_target="tpu_custom_call" | custom-call | flops 6291456 | bytes 6291456 | tf_op jit(solution)/shard_map/pallas_call | solution.py:132
  6.6 2.3 %collective-permute-done.3 = bf16[256,512]{1,0:T(8,128)(2,1)S(1)} collective-permute-done((bf16[256,512]{1,0:T(8,128)(2,1)}, bf16[256,512]{1,0:T(8,128)(2,1)S(1)}, u32[]{:S(2)}, u32[]{:S(2)}) %collective-permute-start.3) | collective-permute-done | bytes 262176 | tf_op jit(solution)/shard_map/ppermute | solution.py:30
  8.9 3.8 %collective-permute-start.4 = (bf16[1,2,128,512]{3,2,1,0:T(8,128)(2,1)S(1)}, bf16[1,2,128,512]{3,2,1,0:T(8,128)(2,1)S(1)}, u32[]{:S(2)}, u32[]{:S(2)}) collective-permute-start(bf16[1,2,128,512]{3,2,1,0:T(8,128)(2,1)S(1)} %get-tuple-element.35), channel_id=1, source_target_pairs={{0,2},{1,7},{2,0},{3,5},{4,6},{5,3},{6,4},{7,1},{8,10},{9,15},{10,... | collective-permute-start | bytes 786440 | tf_op jit(solution)/shard_map/ppermute | solution.py:30
  12.8 2.7 %collective-permute-start.5 = (bf16[1,2,128,512]{3,2,1,0:T(8,128)(2,1)S(1)}, bf16[1,2,128,512]{3,2,1,0:T(8,128)(2,1)S(1)}, u32[]{:S(2)}, u32[]{:S(2)}) collective-permute-start(bf16[1,2,128,512]{3,2,1,0:T(8,128)(2,1)S(1)} %get-tuple-element.36), channel_id=1, source_target_pairs={{0,16},{1,49},{2,18},{3,51},{4,20},{5,53},{6,22},{7,55},{8,24},{9,... | collective-permute-start | bytes 786440 | tf_op jit(solution)/shard_map/ppermute | solution.py:30
  15.5 1.0 collective-permute-done.4
  16.6 2.7 %collective-permute-done.5 = bf16[1,2,128,512]{3,2,1,0:T(8,128)(2,1)S(1)} collective-permute-done((bf16[1,2,128,512]{3,2,1,0:T(8,128)(2,1)S(1)}, bf16[1,2,128,512]{3,2,1,0:T(8,128)(2,1)S(1)}, u32[]{:S(2)}, u32[]{:S(2)}) %collective-permute-start.5) | collective-permute-done | bytes 262176 | tf_op jit(solution)/shard_map/ppermute | solution.py:30
  19.4 0.4 collective-permute-start.7
  19.8 0.3 collective-permute-start.1
  20.1 7.7 %collective-permute-done.6 = bf16[2,2,128,512]{3,2,1,0:T(8,128)(2,1)S(1)} collective-permute-done((bf16[2,2,128,512]{3,2,1,0:T(8,128)(2,1)S(1)}, bf16[2,2,128,512]{3,2,1,0:T(8,128)(2,1)S(1)}, u32[]{:S(2)}, u32[]{:S(2)}) %collective-permute-start.6) | collective-permute-done | bytes 524320 | tf_op jit(solution)/shard_map/ppermute | solution.py:30
  27.7 0.1 pad_maximum_fusion.y0
  27.8 0.1 collective-permute-done.7
  27.9 1.2 pad_maximum_fusion.1.z0
  29.1 2.7 %collective-permute-start.9 = (bf16[4,2,128,512]{3,2,1,0:T(8,128)(2,1)S(1)}, bf16[4,2,128,512]{3,2,1,0:T(8,128)(2,1)S(1)}, u32[]{:S(2)}, u32[]{:S(2)}) collective-permute-start(bf16[4,2,128,512]{3,2,1,0:T(8,128)(2,1)S(1)} %pad_maximum_fusion.y0), channel_id=1, source_target_pairs={{0,48},{1,49},{2,50},{3,51},{4,52},{5,53},{6,54},{7,55},{8,56},{9,... | collective-permute-start | bytes 3145736 | tf_op jit(solution)/shard_map/ppermute | solution.py:30
  31.9 1.1 collective-permute-start.10
  33.1 6.8 %collective-permute-done.1 = bf16[2048,256]{1,0:T(8,128)(2,1)} collective-permute-done((bf16[2048,256]{1,0:T(8,128)(2,1)S(1)}, bf16[2048,256]{1,0:T(8,128)(2,1)}, u32[]{:S(2)}, u32[]{:S(2)}) %collective-permute-start.1) | collective-permute-done | bytes 1048608 | tf_op jit(solution)/shard_map/ppermute | solution.py:30
  39.9 0.3 collective-permute-start.2
  40.1 4.0 %shard_map.46 = (bf16[2048,256]{1,0:T(8,128)(2,1)}, bf16[2048,256]{1,0:T(8,128)(2,1)S(1)}) custom-call(s32[40]{0:T(128)S(1)} %dynamic-slice_bitcast_fusion.table, f32[8192,256]{1,0:T(8,128)} %master.3), custom_call_target="tpu_custom_call" | custom-call | flops 6291456 | bytes 6291456 | tf_op jit(solution)/shard_map/pallas_call | solution.py:132
  44.2 7.1 %collective-permute-done.9.y2 = bf16[4,2,128,512]{3,2,1,0:T(8,128)(2,1)S(1)} collective-permute-done((bf16[4,2,128,512]{3,2,1,0:T(8,128)(2,1)S(1)}, bf16[4,2,128,512]{3,2,1,0:T(8,128)(2,1)S(1)}, u32[]{:S(2)}, u32[]{:S(2)}) %collective-permute-start.9) | collective-permute-done | bytes 1048608 | tf_op jit(solution)/shard_map/ppermute | solution.py:30
  51.3 1.0 copy-done
  52.3 4.6 %collective-permute-start = (bf16[2048,256]{1,0:T(8,128)(2,1)}, bf16[2048,256]{1,0:T(8,128)(2,1)S(1)}, u32[]{:S(2)}, u32[]{:S(2)}) collective-permute-start(bf16[2048,256]{1,0:T(8,128)(2,1)} %get-tuple-element.30), channel_id=1, source_target_pairs={{0,1},{1,0},{2,3},{3,2},{4,5},{5,4},{6,7},{7,6},{8,9},{9,8},{10,11... | collective-permute-start | bytes 3145736 | tf_op jit(solution)/shard_map/ppermute | solution.py:30
  56.9 0.6 collective-permute-start.12
  57.5 1.9 %broadcast_select_fusion = (bf16[4,2,128,512]{3,2,1,0:T(8,128)(2,1)S(1)}, bf16[4,2,128,512]{3,2,1,0:T(8,128)(2,1)S(1)}) fusion(bf16[4,2,128,512]{3,2,1,0:T(8,128)(2,1)} %collective-permute-done.10.z1, bf16[4,2,128,512]{3,2,1,0:T(8,128)(2,1)} %collective-permute-done.11.z2, pred[]{:T(512)S(6)} %eq.6, bf16[4,2,128,512]{3,2,1,0:T(8,128)(2,1)} %collective-permute-done.8.y1, ...), kind=kLoop, calls=%fused_computation.8 | loop fusion | flops 1048576 | bytes 6291457 | tf_op jit(solution)/shard_map/jit(_where)/select_n | solution.py:82
  59.4 1.9 %collective-permute-done.2.far = bf16[2048,256]{1,0:T(8,128)(2,1)S(1)} collective-permute-done((bf16[2048,256]{1,0:T(8,128)(2,1)}, bf16[2048,256]{1,0:T(8,128)(2,1)S(1)}, u32[]{:S(2)}, u32[]{:S(2)}) %collective-permute-start.2) | collective-permute-done | bytes 1048608 | tf_op jit(solution)/shard_map/ppermute | solution.py:30
  61.4 8.8 %shard_map.48 = (f32[3,128,1024]{2,1,0:T(8,128)S(1)}, bf16[3,128,1024]{2,1,0:T(8,128)(2,1)S(1)}, f32[2,4,128,1024]{3,2,1,0:T(8,128)S(1)}) custom-call(s32[40]{0:T(128)S(1)} %dynamic-slice_bitcast_fusion.table, bf16[2048,256]{1,0:T(8,128)(2,1)S(1)} %get-tuple-element.29.mine, bf16[2048,256]{1,0:T(8,128)(2,1)S(1)} %collective-permute-done.near, ...), custom_call_target="tpu_custom_call" | custom-call | flops 6442450944 | bytes 12582912 | tf_op jit(solution)/shard_map/pallas_call | solution.py:218
  70.2 6.6 %collective-permute-start.13 = (bf16[3,128,1024]{2,1,0:T(8,128)(2,1)S(1)}, bf16[3,128,1024]{2,1,0:T(8,128)(2,1)S(1)}, u32[]{:S(2)}, u32[]{:S(2)}) collective-permute-start(bf16[3,128,1024]{2,1,0:T(8,128)(2,1)S(1)} %get-tuple-element.45), channel_id=1, source_target_pairs={{0,1},{1,0},{2,3},{3,2},{4,5},{5,4},{6,7},{7,6},{8,9},{9,8},{10,11... | collective-permute-start | bytes 2359304 | tf_op jit(solution)/shard_map/ppermute | solution.py:30
  76.7 1.1 collective-permute-start.15
  77.9 1.4 collective-permute-start.14
  79.3 0.3 convert_add_fusion.1
  79.6 11.0 %collective-permute-done.15.y3 = bf16[4,2,128,512]{3,2,1,0:T(8,128)(2,1)S(1)} collective-permute-done((bf16[4,2,128,512]{3,2,1,0:T(8,128)(2,1)S(1)}, bf16[4,2,128,512]{3,2,1,0:T(8,128)(2,1)S(1)}, u32[]{:S(2)}, u32[]{:S(2)}) %collective-permute-start.15) | collective-permute-done | bytes 1048608 | tf_op jit(solution)/shard_map/ppermute | solution.py:30
  90.7 1.1 collective-permute-done.14.z3
  91.8 3.0 %shard_map.50 = bf16[5,128,1024]{2,1,0:T(8,128)(2,1)S(1)} custom-call(s32[40]{0:T(128)S(1)} %dynamic-slice_bitcast_fusion.table, bf16[2048,256]{1,0:T(8,128)(2,1)S(1)} %get-tuple-element.29.mine, bf16[2048,256]{1,0:T(8,128)(2,1)S(1)} %collective-permute-done.near, bf16[2048,256]{1,0:T(8,128)(2,1)S(1)} %collective-permute-done.2.far, ...), custom_call_target="tpu_custom_call" | custom-call | flops 1073741824 | bytes 2097152 | tf_op jit(solution)/shard_map/pallas_call | solution.py:218
  94.9 4.1 %collective-permute-start.16 = (bf16[5,128,1024]{2,1,0:T(8,128)(2,1)S(1)}, bf16[5,128,1024]{2,1,0:T(8,128)(2,1)S(1)}, u32[]{:S(2)}, u32[]{:S(2)}) collective-permute-start(bf16[5,128,1024]{2,1,0:T(8,128)(2,1)S(1)} %shard_map.50), channel_id=1, source_target_pairs={{0,1},{1,0},{2,3},{3,2},{4,5},{5,4},{6,7},{7,6},{8,9},{9,8},{10,11... | collective-permute-start | bytes 3932168 | tf_op jit(solution)/shard_map/ppermute | solution.py:30
  99.0 0.3 collective-permute-start.18
  99.3 3.0 %shard_map.49 = f32[5,128,1024]{2,1,0:T(8,128)S(1)} custom-call(s32[40]{0:T(128)S(1)} %dynamic-slice_bitcast_fusion.table, bf16[2048,256]{1,0:T(8,128)(2,1)S(1)} %get-tuple-element.29.mine, bf16[2048,256]{1,0:T(8,128)(2,1)S(1)} %collective-permute-done.near, bf16[2048,256]{1,0:T(8,128)(2,1)S(1)} %collective-permute-done.2.far, ...), custom_call_target="tpu_custom_call" | custom-call | flops 1073741824 | bytes 2097152 | tf_op jit(solution)/shard_map/pallas_call | solution.py:218
  102.3 0.4 convert_add_fusion
  102.7 0.1 slice.91
  102.8 1.3 collective-permute-start.17
  104.1 5.5 %collective-permute-done.18 = bf16[3,128,512]{2,1,0:T(8,128)(2,1)S(1)} collective-permute-done((bf16[3,128,512]{2,1,0:T(8,128)(2,1)S(1)}, bf16[3,128,512]{2,1,0:T(8,128)(2,1)S(1)}, u32[]{:S(2)}, u32[]{:S(2)}) %collective-permute-start.18) | collective-permute-done | bytes 393248 | tf_op jit(solution)/shard_map/ppermute | solution.py:30
  109.7 0.1 fusion.1
  109.8 3.8 %collective-permute-start.21 = (bf16[128,512]{1,0:T(8,128)(2,1)S(1)}, bf16[128,512]{1,0:T(8,128)(2,1)S(1)}, u32[]{:S(2)}, u32[]{:S(2)}) collective-permute-start(bf16[128,512]{1,0:T(8,128)(2,1)S(1)} %get-tuple-element.60), channel_id=1, source_target_pairs={{0,0},{1,65},{2,2},{3,67},{4,4},{5,69},{6,6},{7,71},{8,8},{9,73},{... | collective-permute-start | bytes 393224 | tf_op jit(solution)/shard_map/ppermute | solution.py:30
  113.6 0.7 collective-permute-start.20
  114.3 3.4 %collective-permute-start.19 = (bf16[128,512]{1,0:T(8,128)(2,1)S(1)}, bf16[128,512]{1,0:T(8,128)(2,1)S(1)}, u32[]{:S(2)}, u32[]{:S(2)}) collective-permute-start(bf16[128,512]{1,0:T(8,128)(2,1)S(1)} %get-tuple-element.62), channel_id=1, source_target_pairs={{0,16},{1,81},{2,18},{3,83},{4,20},{5,85},{6,22},{7,87},{8,24},{9,... | collective-permute-start | bytes 393224 | tf_op jit(solution)/shard_map/ppermute | solution.py:30
  117.7 6.0 %collective-permute-done.17 = bf16[5,128,512]{2,1,0:T(8,128)(2,1)S(1)} collective-permute-done((bf16[5,128,512]{2,1,0:T(8,128)(2,1)S(1)}, bf16[5,128,512]{2,1,0:T(8,128)(2,1)S(1)}, u32[]{:S(2)}, u32[]{:S(2)}) %collective-permute-start.17) | collective-permute-done | bytes 655392 | tf_op jit(solution)/shard_map/ppermute | solution.py:30
  123.7 0.2 fusion
  123.9 2.3 %collective-permute-done.21 = bf16[128,512]{1,0:T(8,128)(2,1)S(1)} collective-permute-done((bf16[128,512]{1,0:T(8,128)(2,1)S(1)}, bf16[128,512]{1,0:T(8,128)(2,1)S(1)}, u32[]{:S(2)}, u32[]{:S(2)}) %collective-permute-start.21) | collective-permute-done | bytes 131104 | tf_op jit(solution)/shard_map/ppermute | solution.py:30
  126.2 2.6 %collective-permute-done.20 = bf16[128,512]{1,0:T(8,128)(2,1)S(1)} collective-permute-done((bf16[128,512]{1,0:T(8,128)(2,1)S(1)}, bf16[128,512]{1,0:T(8,128)(2,1)S(1)}, u32[]{:S(2)}, u32[]{:S(2)}) %collective-permute-start.20) | collective-permute-done | bytes 131104 | tf_op jit(solution)/shard_map/ppermute | solution.py:30
  128.8 2.7 %collective-permute-start.22 = (bf16[128,512]{1,0:T(8,128)(2,1)S(1)}, bf16[128,512]{1,0:T(8,128)(2,1)S(1)}, u32[]{:S(2)}, u32[]{:S(2)}) collective-permute-start(bf16[128,512]{1,0:T(8,128)(2,1)S(1)} %get-tuple-element.53), channel_id=1, source_target_pairs={{0,0},{1,65},{2,2},{3,67},{4,4},{5,69},{6,6},{7,71},{8,8},{9,73},{... | collective-permute-start | bytes 393224 | tf_op jit(solution)/shard_map/ppermute | solution.py:30
  131.6 3.7 %collective-permute-start.25 = (bf16[128,512]{1,0:T(8,128)(2,1)S(1)}, bf16[128,512]{1,0:T(8,128)(2,1)S(1)}, u32[]{:S(2)}, u32[]{:S(2)}) collective-permute-start(bf16[128,512]{1,0:T(8,128)(2,1)S(1)} %get-tuple-element.54), channel_id=1, source_target_pairs={{0,48},{1,113},{2,50},{3,115},{4,52},{5,117},{6,54},{7,119},{8,56}... | collective-permute-start | bytes 393224 | tf_op jit(solution)/shard_map/ppermute | solution.py:30
  135.3 0.2 collective-permute-start.23
  135.5 5.1 %collective-permute-start.24 = (bf16[256,512]{1,0:T(8,128)(2,1)S(1)}, bf16[256,512]{1,0:T(8,128)(2,1)S(1)}, u32[]{:S(2)}, u32[]{:S(2)}) collective-permute-start(bf16[256,512]{1,0:T(8,128)(2,1)S(1)} %pad_maximum_fusion.6), channel_id=1, source_target_pairs={{0,32},{1,97},{2,34},{3,99},{4,36},{5,101},{6,38},{7,103},{8,40},{... | collective-permute-start | bytes 786440 | tf_op jit(solution)/shard_map/ppermute | solution.py:30
  140.7 2.0 %collective-permute-done.23 = bf16[128,512]{1,0:T(8,128)(2,1)S(1)} collective-permute-done((bf16[128,512]{1,0:T(8,128)(2,1)S(1)}, bf16[128,512]{1,0:T(8,128)(2,1)S(1)}, u32[]{:S(2)}, u32[]{:S(2)}) %collective-permute-start.23) | collective-permute-done | bytes 131104 | tf_op jit(solution)/shard_map/ppermute | solution.py:30
  142.8 2.9 %collective-permute-done.24 = bf16[256,512]{1,0:T(8,128)(2,1)S(1)} collective-permute-done((bf16[256,512]{1,0:T(8,128)(2,1)S(1)}, bf16[256,512]{1,0:T(8,128)(2,1)S(1)}, u32[]{:S(2)}, u32[]{:S(2)}) %collective-permute-start.24) | collective-permute-done | bytes 262176 | tf_op jit(solution)/shard_map/ppermute | solution.py:30
  145.7 0.1 pad_maximum_fusion.2.own
  146.0 2.6 %collective-permute-done.26.other = bf16[4,256,512]{2,1,0:T(8,128)(2,1)S(1)} collective-permute-done((bf16[4,256,512]{2,1,0:T(8,128)(2,1)S(1)}, bf16[4,256,512]{2,1,0:T(8,128)(2,1)S(1)}, u32[]{:S(2)}, u32[]{:S(2)}) %collective-permute-start.26) | collective-permute-done | bytes 1048608 | tf_op jit(solution)/shard_map/ppermute | solution.py:30
  148.6 0.7 shard_map.51
  149.3 3.5 %collective-permute-start.27 = (bf16[256,512]{1,0:T(8,128)(2,1)S(1)}, bf16[256,512]{1,0:T(8,128)(2,1)S(1)}, u32[]{:S(2)}, u32[]{:S(2)}) collective-permute-start(bf16[256,512]{1,0:T(8,128)(2,1)S(1)} %get-tuple-element.49), channel_id=1, source_target_pairs={{0,0},{1,8},{2,2},{3,10},{4,4},{5,12},{6,6},{7,14},{8,9},{9,1},{10... | collective-permute-start | bytes 786440 | tf_op jit(solution)/shard_map/ppermute | solution.py:30
  152.8 0.6 collective-permute-start.28
  153.5 0.2 collective-permute-start.29
  153.7 3.3 %collective-permute-start.30 = (bf16[256,512]{1,0:T(8,128)(2,1)S(1)}, bf16[256,512]{1,0:T(8,128)(2,1)S(1)}, u32[]{:S(2)}, u32[]{:S(2)}) collective-permute-start(bf16[256,512]{1,0:T(8,128)(2,1)S(1)} %get-tuple-element.52), channel_id=1, source_target_pairs={{0,6},{1,14},{2,0},{3,8},{4,2},{5,10},{6,4},{7,12},{8,15},{9,7},{1... | collective-permute-start | bytes 786440 | tf_op jit(solution)/shard_map/ppermute | solution.py:30
  157.0 10.4 %collective-permute-done.28.refs_1_ = bf16[256,512]{1,0:T(8,128)(2,1)S(1)} collective-permute-done((bf16[256,512]{1,0:T(8,128)(2,1)S(1)}, bf16[256,512]{1,0:T(8,128)(2,1)S(1)}, u32[]{:S(2)}, u32[]{:S(2)}) %collective-permute-start.28) | collective-permute-done | bytes 262176 | tf_op jit(solution)/shard_map/ppermute | solution.py:30
  167.5 1.2 collective-permute-done.30.refs_3_
  168.7 1.5 shard_map.52
  (37 shorter events, 0.7 us)
Async XLA Ops:
  0.0 8.9 %collective-permute-start.3 = (bf16[256,512]{1,0:T(8,128)(2,1)}, bf16[256,512]{1,0:T(8,128)(2,1)S(1)}, u32[]{:S(2)}, u32[]{:S(2)}) collective-permute-start(bf16[256,512]{1,0:T(8,128)(2,1)} %param.5), channel_id=1, source_target_pairs={{0,64},{1,65},{2,66},{3,67},{4,68},{5,69},{6,70},{7,71},{8,72},{9,... | collective-permute-start | bytes 786440 | tf_op jit(solution)/shard_map/ppermute | solution.py:30
  2.5 6.4 %copy-start.5 = (bf16[256,512]{1,0:T(8,128)(2,1)S(1)}, bf16[256,512]{1,0:T(8,128)(2,1)}, u32[]{:S(2)}) copy-start(bf16[256,512]{1,0:T(8,128)(2,1)} %param.5) | copy-start | bytes 786436
  8.9 7.6 %collective-permute-start.4 = (bf16[1,2,128,512]{3,2,1,0:T(8,128)(2,1)S(1)}, bf16[1,2,128,512]{3,2,1,0:T(8,128)(2,1)S(1)}, u32[]{:S(2)}, u32[]{:S(2)}) collective-permute-start(bf16[1,2,128,512]{3,2,1,0:T(8,128)(2,1)S(1)} %get-tuple-element.35), channel_id=1, source_target_pairs={{0,2},{1,7},{2,0},{3,5},{4,6},{5,3},{6,4},{7,1},{8,10},{9,15},{10,... | collective-permute-start | bytes 786440 | tf_op jit(solution)/shard_map/ppermute | solution.py:30
  12.8 6.5 %collective-permute-start.5 = (bf16[1,2,128,512]{3,2,1,0:T(8,128)(2,1)S(1)}, bf16[1,2,128,512]{3,2,1,0:T(8,128)(2,1)S(1)}, u32[]{:S(2)}, u32[]{:S(2)}) collective-permute-start(bf16[1,2,128,512]{3,2,1,0:T(8,128)(2,1)S(1)} %get-tuple-element.36), channel_id=1, source_target_pairs={{0,16},{1,49},{2,18},{3,51},{4,20},{5,53},{6,22},{7,55},{8,24},{9,... | collective-permute-start | bytes 786440 | tf_op jit(solution)/shard_map/ppermute | solution.py:30
  19.3 8.4 %collective-permute-start.6 = (bf16[2,2,128,512]{3,2,1,0:T(8,128)(2,1)S(1)}, bf16[2,2,128,512]{3,2,1,0:T(8,128)(2,1)S(1)}, u32[]{:S(2)}, u32[]{:S(2)}) collective-permute-start(bf16[2,2,128,512]{3,2,1,0:T(8,128)(2,1)S(1)} %pad_maximum_fusion.3), channel_id=1, source_target_pairs={{0,6},{1,3},{2,4},{3,1},{4,2},{5,7},{6,0},{7,5},{8,14},{9,11},{10,... | collective-permute-start | bytes 1572872 | tf_op jit(solution)/shard_map/ppermute | solution.py:30
  19.4 8.5 %collective-permute-start.7 = (bf16[2,2,128,512]{3,2,1,0:T(8,128)(2,1)S(1)}, bf16[2,2,128,512]{3,2,1,0:T(8,128)(2,1)S(1)}, u32[]{:S(2)}, u32[]{:S(2)}) collective-permute-start(bf16[2,2,128,512]{3,2,1,0:T(8,128)(2,1)S(1)} %pad_maximum_fusion.4), channel_id=1, source_target_pairs={{0,48},{1,17},{2,50},{3,19},{4,52},{5,21},{6,54},{7,23},{8,56},{9,... | collective-permute-start | bytes 1572872 | tf_op jit(solution)/shard_map/ppermute | solution.py:30
  19.8 20.0 %collective-permute-start.1 = (bf16[2048,256]{1,0:T(8,128)(2,1)S(1)}, bf16[2048,256]{1,0:T(8,128)(2,1)}, u32[]{:S(2)}, u32[]{:S(2)}) collective-permute-start(bf16[2048,256]{1,0:T(8,128)(2,1)S(1)} %get-tuple-element.32), channel_id=1, source_target_pairs={{0,8},{1,9},{2,10},{3,11},{4,12},{5,13},{6,14},{7,15},{8,0},{9,1},... | collective-permute-start | bytes 3145736 | tf_op jit(solution)/shard_map/ppermute | solution.py:30
  27.8 16.3 %copy-start.2 = (bf16[4,2,128,512]{3,2,1,0:T(8,128)(2,1)}, bf16[4,2,128,512]{3,2,1,0:T(8,128)(2,1)S(1)}, u32[]{:S(2)}) copy-start(bf16[4,2,128,512]{3,2,1,0:T(8,128)(2,1)S(1)} %pad_maximum_fusion.y0) | copy-start | bytes 3145732
  29.1 22.2 %collective-permute-start.9 = (bf16[4,2,128,512]{3,2,1,0:T(8,128)(2,1)S(1)}, bf16[4,2,128,512]{3,2,1,0:T(8,128)(2,1)S(1)}, u32[]{:S(2)}, u32[]{:S(2)}) collective-permute-start(bf16[4,2,128,512]{3,2,1,0:T(8,128)(2,1)S(1)} %pad_maximum_fusion.y0), channel_id=1, source_target_pairs={{0,48},{1,49},{2,50},{3,51},{4,52},{5,53},{6,54},{7,55},{8,56},{9,... | collective-permute-start | bytes 3145736 | tf_op jit(solution)/shard_map/ppermute | solution.py:30
  31.8 25.1 %collective-permute-start.8 = (bf16[4,2,128,512]{3,2,1,0:T(8,128)(2,1)S(1)}, bf16[4,2,128,512]{3,2,1,0:T(8,128)(2,1)}, u32[]{:S(2)}, u32[]{:S(2)}) collective-permute-start(bf16[4,2,128,512]{3,2,1,0:T(8,128)(2,1)S(1)} %pad_maximum_fusion.y0), channel_id=1, source_target_pairs={{0,16},{1,17},{2,18},{3,19},{4,20},{5,21},{6,22},{7,23},{8,24},{9,... | collective-permute-start | bytes 3145736 | tf_op jit(solution)/shard_map/ppermute | solution.py:30
  31.8 25.7 %collective-permute-start.11 = (bf16[4,2,128,512]{3,2,1,0:T(8,128)(2,1)}, bf16[4,2,128,512]{3,2,1,0:T(8,128)(2,1)}, u32[]{:S(2)}, u32[]{:S(2)}) collective-permute-start(bf16[4,2,128,512]{3,2,1,0:T(8,128)(2,1)} %pad_maximum_fusion.1.z0), channel_id=1, source_target_pairs={{0,6},{1,7},{2,4},{3,5},{4,2},{5,3},{6,0},{7,1},{8,14},{9,15},{10,... | collective-permute-start | bytes 3145736 | tf_op jit(solution)/shard_map/ppermute | solution.py:30
  31.9 25.6 %collective-permute-start.10 = (bf16[4,2,128,512]{3,2,1,0:T(8,128)(2,1)}, bf16[4,2,128,512]{3,2,1,0:T(8,128)(2,1)}, u32[]{:S(2)}, u32[]{:S(2)}) collective-permute-start(bf16[4,2,128,512]{3,2,1,0:T(8,128)(2,1)} %pad_maximum_fusion.1.z0), channel_id=1, source_target_pairs={{0,2},{1,3},{2,0},{3,1},{4,6},{5,7},{6,4},{7,5},{8,10},{9,11},{10,... | collective-permute-start | bytes 3145736 | tf_op jit(solution)/shard_map/ppermute | solution.py:30
  39.9 21.5 %collective-permute-start.2 = (bf16[2048,256]{1,0:T(8,128)(2,1)}, bf16[2048,256]{1,0:T(8,128)(2,1)S(1)}, u32[]{:S(2)}, u32[]{:S(2)}) collective-permute-start(bf16[2048,256]{1,0:T(8,128)(2,1)} %get-tuple-element.33), channel_id=1, source_target_pairs={{0,8},{1,9},{2,10},{3,11},{4,12},{5,13},{6,14},{7,15},{8,0},{9,1},... | collective-permute-start | bytes 3145736 | tf_op jit(solution)/shard_map/ppermute | solution.py:30
  51.3 1.0 copy-start
  52.3 9.1 %collective-permute-start = (bf16[2048,256]{1,0:T(8,128)(2,1)}, bf16[2048,256]{1,0:T(8,128)(2,1)S(1)}, u32[]{:S(2)}, u32[]{:S(2)}) collective-permute-start(bf16[2048,256]{1,0:T(8,128)(2,1)} %get-tuple-element.30), channel_id=1, source_target_pairs={{0,1},{1,0},{2,3},{3,2},{4,5},{5,4},{6,7},{7,6},{8,9},{9,8},{10,11... | collective-permute-start | bytes 3145736 | tf_op jit(solution)/shard_map/ppermute | solution.py:30
  56.9 4.5 %collective-permute-start.12 = (bf16[2048,256]{1,0:T(8,128)(2,1)}, bf16[2048,256]{1,0:T(8,128)(2,1)}, u32[]{:S(2)}, u32[]{:S(2)}) collective-permute-start(bf16[2048,256]{1,0:T(8,128)(2,1)} %collective-permute-done.1), channel_id=1, source_target_pairs={{0,1},{1,0},{2,3},{3,2},{4,5},{5,4},{6,7},{7,6},{8,9},{9,8},{10,11... | collective-permute-start | bytes 3145736 | tf_op jit(solution)/shard_map/ppermute | solution.py:30
  57.5 3.9 %copy-start.1 = (bf16[4,2,128,512]{3,2,1,0:T(8,128)(2,1)S(1)}, bf16[4,2,128,512]{3,2,1,0:T(8,128)(2,1)}, u32[]{:S(2)}) copy-start(bf16[4,2,128,512]{3,2,1,0:T(8,128)(2,1)} %copy-done) | copy-start | bytes 3145732
  57.5 3.9 %copy-start.3 = (bf16[4,2,128,512]{3,2,1,0:T(8,128)(2,1)S(1)}, bf16[4,2,128,512]{3,2,1,0:T(8,128)(2,1)}, u32[]{:S(2)}) copy-start(bf16[4,2,128,512]{3,2,1,0:T(8,128)(2,1)} %copy-done.2) | copy-start | bytes 3145732
  70.2 9.1 %collective-permute-start.13 = (bf16[3,128,1024]{2,1,0:T(8,128)(2,1)S(1)}, bf16[3,128,1024]{2,1,0:T(8,128)(2,1)S(1)}, u32[]{:S(2)}, u32[]{:S(2)}) collective-permute-start(bf16[3,128,1024]{2,1,0:T(8,128)(2,1)S(1)} %get-tuple-element.45), channel_id=1, source_target_pairs={{0,1},{1,0},{2,3},{3,2},{4,5},{5,4},{6,7},{7,6},{8,9},{9,8},{10,11... | collective-permute-start | bytes 2359304 | tf_op jit(solution)/shard_map/ppermute | solution.py:30
  76.7 13.9 %collective-permute-start.15 = (bf16[4,2,128,512]{3,2,1,0:T(8,128)(2,1)S(1)}, bf16[4,2,128,512]{3,2,1,0:T(8,128)(2,1)S(1)}, u32[]{:S(2)}, u32[]{:S(2)}) collective-permute-start(bf16[4,2,128,512]{3,2,1,0:T(8,128)(2,1)S(1)} %get-tuple-element.40), channel_id=1, source_target_pairs={{0,48},{1,17},{2,50},{3,19},{4,52},{5,21},{6,54},{7,23},{8,56},{9,... | collective-permute-start | bytes 3145736 | tf_op jit(solution)/shard_map/ppermute | solution.py:30
  77.9 13.9 %collective-permute-start.14 = (bf16[4,2,128,512]{3,2,1,0:T(8,128)(2,1)S(1)}, bf16[4,2,128,512]{3,2,1,0:T(8,128)(2,1)S(1)}, u32[]{:S(2)}, u32[]{:S(2)}) collective-permute-start(bf16[4,2,128,512]{3,2,1,0:T(8,128)(2,1)S(1)} %get-tuple-element.42), channel_id=1, source_target_pairs={{0,6},{1,3},{2,4},{3,1},{4,2},{5,7},{6,0},{7,5},{8,14},{9,11},{10,... | collective-permute-start | bytes 3145736 | tf_op jit(solution)/shard_map/ppermute | solution.py:30
  94.9 7.4 %collective-permute-start.16 = (bf16[5,128,1024]{2,1,0:T(8,128)(2,1)S(1)}, bf16[5,128,1024]{2,1,0:T(8,128)(2,1)S(1)}, u32[]{:S(2)}, u32[]{:S(2)}) collective-permute-start(bf16[5,128,1024]{2,1,0:T(8,128)(2,1)S(1)} %shard_map.50), channel_id=1, source_target_pairs={{0,1},{1,0},{2,3},{3,2},{4,5},{5,4},{6,7},{7,6},{8,9},{9,8},{10,11... | collective-permute-start | bytes 3932168 | tf_op jit(solution)/shard_map/ppermute | solution.py:30
  99.0 10.7 %collective-permute-start.18 = (bf16[3,128,512]{2,1,0:T(8,128)(2,1)S(1)}, bf16[3,128,512]{2,1,0:T(8,128)(2,1)S(1)}, u32[]{:S(2)}, u32[]{:S(2)}) collective-permute-start(bf16[3,128,512]{2,1,0:T(8,128)(2,1)S(1)} %slice.92), channel_id=1, source_target_pairs={{0,8},{1,9},{2,10},{3,11},{4,12},{5,13},{6,14},{7,15},{8,0},{9,1},... | collective-permute-start | bytes 1179656 | tf_op jit(solution)/shard_map/ppermute | solution.py:30
  102.8 20.9 %collective-permute-start.17 = (bf16[5,128,512]{2,1,0:T(8,128)(2,1)S(1)}, bf16[5,128,512]{2,1,0:T(8,128)(2,1)S(1)}, u32[]{:S(2)}, u32[]{:S(2)}) collective-permute-start(bf16[5,128,512]{2,1,0:T(8,128)(2,1)S(1)} %slice.91), channel_id=1, source_target_pairs={{0,8},{1,9},{2,10},{3,11},{4,12},{5,13},{6,14},{7,15},{8,0},{9,1},... | collective-permute-start | bytes 1966088 | tf_op jit(solution)/shard_map/ppermute | solution.py:30
  109.8 16.4 %collective-permute-start.21 = (bf16[128,512]{1,0:T(8,128)(2,1)S(1)}, bf16[128,512]{1,0:T(8,128)(2,1)S(1)}, u32[]{:S(2)}, u32[]{:S(2)}) collective-permute-start(bf16[128,512]{1,0:T(8,128)(2,1)S(1)} %get-tuple-element.60), channel_id=1, source_target_pairs={{0,0},{1,65},{2,2},{3,67},{4,4},{5,69},{6,6},{7,71},{8,8},{9,73},{... | collective-permute-start | bytes 393224 | tf_op jit(solution)/shard_map/ppermute | solution.py:30
  113.6 15.2 %collective-permute-start.20 = (bf16[128,512]{1,0:T(8,128)(2,1)S(1)}, bf16[128,512]{1,0:T(8,128)(2,1)S(1)}, u32[]{:S(2)}, u32[]{:S(2)}) collective-permute-start(bf16[128,512]{1,0:T(8,128)(2,1)S(1)} %get-tuple-element.61), channel_id=1, source_target_pairs={{0,48},{1,113},{2,50},{3,115},{4,52},{5,117},{6,54},{7,119},{8,56}... | collective-permute-start | bytes 393224 | tf_op jit(solution)/shard_map/ppermute | solution.py:30
  114.3 14.5 %collective-permute-start.19 = (bf16[128,512]{1,0:T(8,128)(2,1)S(1)}, bf16[128,512]{1,0:T(8,128)(2,1)S(1)}, u32[]{:S(2)}, u32[]{:S(2)}) collective-permute-start(bf16[128,512]{1,0:T(8,128)(2,1)S(1)} %get-tuple-element.62), channel_id=1, source_target_pairs={{0,16},{1,81},{2,18},{3,83},{4,20},{5,85},{6,22},{7,87},{8,24},{9,... | collective-permute-start | bytes 393224 | tf_op jit(solution)/shard_map/ppermute | solution.py:30
  128.8 11.8 %collective-permute-start.22 = (bf16[128,512]{1,0:T(8,128)(2,1)S(1)}, bf16[128,512]{1,0:T(8,128)(2,1)S(1)}, u32[]{:S(2)}, u32[]{:S(2)}) collective-permute-start(bf16[128,512]{1,0:T(8,128)(2,1)S(1)} %get-tuple-element.53), channel_id=1, source_target_pairs={{0,0},{1,65},{2,2},{3,67},{4,4},{5,69},{6,6},{7,71},{8,8},{9,73},{... | collective-permute-start | bytes 393224 | tf_op jit(solution)/shard_map/ppermute | solution.py:30
  131.6 9.1 %collective-permute-start.25 = (bf16[128,512]{1,0:T(8,128)(2,1)S(1)}, bf16[128,512]{1,0:T(8,128)(2,1)S(1)}, u32[]{:S(2)}, u32[]{:S(2)}) collective-permute-start(bf16[128,512]{1,0:T(8,128)(2,1)S(1)} %get-tuple-element.54), channel_id=1, source_target_pairs={{0,48},{1,113},{2,50},{3,115},{4,52},{5,117},{6,54},{7,119},{8,56}... | collective-permute-start | bytes 393224 | tf_op jit(solution)/shard_map/ppermute | solution.py:30
  135.3 7.4 %collective-permute-start.23 = (bf16[128,512]{1,0:T(8,128)(2,1)S(1)}, bf16[128,512]{1,0:T(8,128)(2,1)S(1)}, u32[]{:S(2)}, u32[]{:S(2)}) collective-permute-start(bf16[128,512]{1,0:T(8,128)(2,1)S(1)} %get-tuple-element.57), channel_id=1, source_target_pairs={{0,16},{1,81},{2,18},{3,83},{4,20},{5,85},{6,22},{7,87},{8,24},{9,... | collective-permute-start | bytes 393224 | tf_op jit(solution)/shard_map/ppermute | solution.py:30
  135.5 10.2 %collective-permute-start.24 = (bf16[256,512]{1,0:T(8,128)(2,1)S(1)}, bf16[256,512]{1,0:T(8,128)(2,1)S(1)}, u32[]{:S(2)}, u32[]{:S(2)}) collective-permute-start(bf16[256,512]{1,0:T(8,128)(2,1)S(1)} %pad_maximum_fusion.6), channel_id=1, source_target_pairs={{0,32},{1,97},{2,34},{3,99},{4,36},{5,101},{6,38},{7,103},{8,40},{... | collective-permute-start | bytes 786440 | tf_op jit(solution)/shard_map/ppermute | solution.py:30
  140.7 7.9 %copy-start.4 = (s32[8]{0:T(128)S(1)}, s32[8]{0:T(128)}, u32[]{:S(2)}) copy-start(s32[8]{0:T(128)} %owner.1) | copy-start | bytes 100
  145.9 2.7 %collective-permute-start.26 = (bf16[4,256,512]{2,1,0:T(8,128)(2,1)S(1)}, bf16[4,256,512]{2,1,0:T(8,128)(2,1)S(1)}, u32[]{:S(2)}, u32[]{:S(2)}) collective-permute-start(bf16[4,256,512]{2,1,0:T(8,128)(2,1)S(1)} %pad_maximum_fusion.2.own), channel_id=1, source_target_pairs={{0,1},{1,0},{2,3},{3,2},{4,5},{5,4},{6,7},{7,6},{8,9},{9,8},{10,11... | collective-permute-start | bytes 3145736 | tf_op jit(solution)/shard_map/ppermute | solution.py:30
  149.3 7.7 %collective-permute-start.27 = (bf16[256,512]{1,0:T(8,128)(2,1)S(1)}, bf16[256,512]{1,0:T(8,128)(2,1)S(1)}, u32[]{:S(2)}, u32[]{:S(2)}) collective-permute-start(bf16[256,512]{1,0:T(8,128)(2,1)S(1)} %get-tuple-element.49), channel_id=1, source_target_pairs={{0,0},{1,8},{2,2},{3,10},{4,4},{5,12},{6,6},{7,14},{8,9},{9,1},{10... | collective-permute-start | bytes 786440 | tf_op jit(solution)/shard_map/ppermute | solution.py:30
  152.8 14.6 %collective-permute-start.28 = (bf16[256,512]{1,0:T(8,128)(2,1)S(1)}, bf16[256,512]{1,0:T(8,128)(2,1)S(1)}, u32[]{:S(2)}, u32[]{:S(2)}) collective-permute-start(bf16[256,512]{1,0:T(8,128)(2,1)S(1)} %get-tuple-element.50), channel_id=1, source_target_pairs={{0,2},{1,10},{2,4},{3,12},{4,6},{5,14},{6,0},{7,8},{8,11},{9,3},{1... | collective-permute-start | bytes 786440 | tf_op jit(solution)/shard_map/ppermute | solution.py:30
  153.5 14.0 %collective-permute-start.29 = (bf16[256,512]{1,0:T(8,128)(2,1)S(1)}, bf16[256,512]{1,0:T(8,128)(2,1)S(1)}, u32[]{:S(2)}, u32[]{:S(2)}) collective-permute-start(bf16[256,512]{1,0:T(8,128)(2,1)S(1)} %get-tuple-element.51), channel_id=1, source_target_pairs={{0,4},{1,12},{2,6},{3,14},{4,0},{5,8},{6,2},{7,10},{8,13},{9,5},{1... | collective-permute-start | bytes 786440 | tf_op jit(solution)/shard_map/ppermute | solution.py:30
  153.7 15.0 %collective-permute-start.30 = (bf16[256,512]{1,0:T(8,128)(2,1)S(1)}, bf16[256,512]{1,0:T(8,128)(2,1)S(1)}, u32[]{:S(2)}, u32[]{:S(2)}) collective-permute-start(bf16[256,512]{1,0:T(8,128)(2,1)S(1)} %get-tuple-element.52), channel_id=1, source_target_pairs={{0,6},{1,14},{2,0},{3,8},{4,2},{5,10},{6,4},{7,12},{8,15},{9,7},{1... | collective-permute-start | bytes 786440 | tf_op jit(solution)/shard_map/ppermute | solution.py:30

commit v10 on v9

v10 whole, which is shorter than its diff:
```python
import functools

import jax
import jax.numpy as jnp
import numpy as np
from jax import lax
from jax.experimental import pallas as pl
from jax.experimental.pallas import tpu as pltpu
from jax.sharding import PartitionSpec as P

BLOCK = 128
AXES = ("group", "tp")
N_DEV = 128
SHARE = 512
COLS = 256
HALF = 128
MIB = 1024 * 1024


def coords(i):
    return i // 64 * 2 + i // 8 % 2, i // 16 % 4, i // 2 % 4, i % 2


def linear(x, y, z, core):
    x, y, z = x % 4, y % 4, z % 4
    return x // 2 * 64 + y * 16 + x % 2 * 8 + z * 2 + core


def permute(value, move):
    return lax.ppermute(value, AXES, [(i, move(*coords(i))) for i in range(N_DEV)])


def offset(slot, at, core):
    step = -1 if (at + core) % 2 else 1
    return (0, step, -step, 2)[slot] % 4


def exchange(value, axis, which):
    def move(x, y, z, core):
        at = {"x": x, "y": y, "z": z}
        at[axis] += offset(which, at[axis], core)
        return linear(at["x"], at["y"], at["z"], core)

    return permute(value, move)


def other_core(x, y, z, core):
    return linear(x, y, z, 1 - core)


def other_chip(x, y, z, core):
    return linear(x ^ 1, y, z, core)


def after(value, *others):
    return lax.optimization_barrier((value, *others))[0]


def gather(activations, first_job, second_job, third_job):
    came = permute(activations, lambda x, y, z, c: linear(x + 2, y, z, c))
    block = jnp.stack([activations, after(came, first_job)])
    blocks = {"z": block[None, :, :HALF], "y": block[None, :, HALF:]}
    blocks = lax.optimization_barrier(blocks)
    for which in (1, 2):
        blocks = {
            part: jnp.concatenate([v, exchange(v, "y" if part == "z" else "z", which)]) for part, v in blocks.items()
        }
        blocks = lax.optimization_barrier(blocks)
    blocks, second_job = lax.optimization_barrier((blocks, second_job))
    slots = {}
    for part, v in blocks.items():
        first = exchange(v, part, 1)
        second = exchange(v, part, 2)
        slots[part] = [v, first, second, exchange(after(first, third_job), part, 2)]
    return slots


AWAY, HERE, CORE, Y_SLOT, Z_SLOT, XH, Y, Z, DEST, WIDTH = 0, 8, 16, 17, 21, 25, 26, 27, 28, 32


def device_row(i):
    x, y, z, core = coords(i)
    xh, xl = x // 2, x % 2

    def chunks(l, c):
        return [l * 8 + (z + dz) % 4 * 2 + c for dz in range(4)]

    row = chunks(1 - xl, core) + chunks(1 - xl, 1 - core) + chunks(xl, 1 - core) + chunks(xl, core) + [core]
    row += [offset(s, y, core) for s in range(4)] + [offset(s, z, core) for s in range(4)]
    row += [xh, y, z] + [(xl ^ core) * 4 + (z + dz) % 4 for dz in range(4)]
    assert len(row) == WIDTH
    return row


def refit_kernel(first, table, master, *refs):
    outs, (held, sems) = refs[:-2], refs[-2:]
    copies = []
    for n in range(8):
        at = pl.multiple_of(table[first + n] * SHARE, SHARE)
        copies.append(pltpu.make_async_copy(master.at[pl.ds(at, SHARE)], held.at[n], sems.at[n]))
        copies[-1].start()
    tiles = SHARE // BLOCK
    for n in range(8):
        out = outs[n * len(outs) // 8]
        start = n * SHARE % out.shape[0]
        copies[n].wait()
        amax = jnp.max(jnp.abs(held[n]).reshape(tiles, BLOCK, COLS), axis=1)
        for c in range(COLS // BLOCK):
            cols = slice(c * BLOCK, (c + 1) * BLOCK)
            top = jnp.max(amax[:, cols], axis=1, keepdims=True)
            scales = ((top + 1e-6) / 448.0).astype(jnp.bfloat16).astype(jnp.float32)
            inverses = 1.0 / scales
            for r in range(tiles):
                tile = held[n, r * BLOCK : (r + 1) * BLOCK, cols]
                coded = (tile * inverses[r : r + 1]).astype(jnp.bfloat16)
                value = (coded.astype(jnp.float32) * scales[r : r + 1]).astype(jnp.bfloat16)
                out[start + r * BLOCK : start + (r + 1) * BLOCK, cols] = value


def refit(table, master, first, n_outs):
    size = 8 * SHARE * COLS
    return pl.pallas_call(
        functools.partial(refit_kernel, first),
        in_specs=[pl.BlockSpec(memory_space=pltpu.SMEM), pl.BlockSpec(memory_space=pltpu.HBM)],
        out_specs=[pl.BlockSpec(memory_space=pltpu.VMEM)] * n_outs,
        out_shape=[jax.ShapeDtypeStruct((8 * SHARE // n_outs, COLS), jnp.bfloat16)] * n_outs,
        scratch_shapes=[pltpu.VMEM((8, SHARE, COLS), jnp.float32), pltpu.SemaphoreType.DMA((8,))],
        compiler_params=pltpu.CompilerParams(vmem_limit_bytes=44 * MIB),
        cost_estimate=pl.CostEstimate(flops=size * 6, bytes_accessed=size * 6, transcendentals=0),
    )(table, master)


def dot(a, b):
    return jnp.dot(a, b, preferred_element_type=jnp.float32)


def pieces(core, mine, near, far, cross):
    def cols(at, c):
        return pl.ds(pl.multiple_of(at + c * COLS, COLS), COLS)

    return [(mine, cols(0, core)), (near, cols(0, 1 - core)), (far, cols(2 * COLS, core)), (cross, cols(2 * COLS, 1 - core))]


def product_kernel(part, half_of, table, mine, near, far, cross, *refs):
    slots, (out, held, sems) = refs[:4], refs[4:]
    core = table[CORE]
    half = half_of(core)
    for i, slot in enumerate(slots):
        for k in range(4):
            zs = k if part == "y" else i
            depth = pl.ds(pl.multiple_of(table[Z_SLOT + zs] * SHARE, SHARE), SHARE)
            to = held.at[i if part == "y" else k, :, depth]
            pltpu.make_async_copy(slot.at[k, half], to, sems.at[i]).start()
    for i in range(4):
        pltpu.make_async_copy(held.at[i], held.at[i], sems.at[i]).wait()
    acts = held[...].reshape(4 * HALF, 4 * SHARE)
    for weight, cols in pieces(core, mine, near, far, cross):
        got = jnp.dot(acts, weight[...], preferred_element_type=jnp.float32).reshape(4, HALF, COLS)
        for ys in range(4):
            out[table[Y_SLOT + ys], :, cols] = got[ys].astype(out.dtype)


def product(part, keep, table, weights, slots):
    vmem, anywhere = pl.BlockSpec(memory_space=pltpu.VMEM), pl.BlockSpec(memory_space=pl.ANY)
    return pl.pallas_call(
        functools.partial(product_kernel, part, (lambda core: core) if keep else (lambda core: 1 - core)),
        in_specs=[pl.BlockSpec(memory_space=pltpu.SMEM)] + [vmem] * 4 + [anywhere] * 4,
        out_specs=vmem,
        out_shape=jax.ShapeDtypeStruct((4, HALF, 4 * COLS), jnp.float32 if keep else jnp.bfloat16),
        scratch_shapes=[pltpu.VMEM((4, HALF, 4 * SHARE), jnp.bfloat16), pltpu.SemaphoreType.DMA((4,))],
        compiler_params=pltpu.CompilerParams(vmem_limit_bytes=20 * MIB),
        cost_estimate=pl.CostEstimate(flops=2 * 512 * 2048 * 1024, bytes_accessed=8 * MIB, transcendentals=0),
    )(table, *weights, *slots)


def spread_kernel(table, owner, own, other, *outs):
    for k, out in enumerate(outs):
        section = owner[table[DEST + k]]
        half = jnp.where(section >= 4, 1, 0)
        far = jnp.where(half == table[XH], 0, 1)
        at = (table[Y] + 8 - section) & 3

        @pl.when(far == table[CORE])
        def _():
            out[...] = own[at]

        @pl.when(far != table[CORE])
        def _():
            out[...] = other[at]


def arrange_kernel(table, *refs):
    parts, out, sems = refs[:8], refs[8], refs[9]
    copies = []
    for i, part in enumerate(parts):
        rows, dz = i // 4, i % 4
        at = pl.multiple_of(((table[Z] + 4 - dz) & 3) * (2 * COLS), 2 * COLS)
        to = out.at[pl.ds(rows * HALF, HALF), pl.ds(at, 2 * COLS)]
        copies.append(pltpu.make_async_copy(part, to, sems.at[i]))
        copies[-1].start()
    for copy in copies:
        copy.wait()


def small_call(kernel, scalars, parts, shapes, out_space, scratch=()):
    smem, vmem = pl.BlockSpec(memory_space=pltpu.SMEM), pl.BlockSpec(memory_space=pltpu.VMEM)
    return pl.pallas_call(
        kernel,
        in_specs=[smem] * len(scalars) + [vmem] * len(parts),
        out_specs=[pl.BlockSpec(memory_space=out_space)] * len(shapes),
        out_shape=[jax.ShapeDtypeStruct(shape, jnp.bfloat16) for shape in shapes],
        scratch_shapes=scratch,
        compiler_params=pltpu.CompilerParams(vmem_limit_bytes=16 * MIB),
        cost_estimate=pl.CostEstimate(flops=0, bytes_accessed=2 * MIB, transcendentals=0),
    )(*scalars, *parts)


def shards(master, activations, owner):
    f32, bf16 = jnp.float32, jnp.bfloat16
    rows = jnp.asarray(np.array([device_row(i) for i in range(N_DEV)], np.int32))
    me = lax.axis_index("group") * 16 + lax.axis_index("tp")
    table = lax.dynamic_index_in_dim(rows, me, 0, keepdims=False)

    same, swapped = refit(table, master, AWAY, 2)
    sent, mine = refit(table, master, HERE, 2)
    near = permute(sent, other_core)
    swapped = permute(swapped, other_chip)
    cross = permute(swapped, other_core)
    slots = gather(activations, same, near, cross)
    far = permute(after(same, swapped), other_chip)
    weights = [mine, near, far, cross]
    ready = after(table, slots["z"][3], slots["y"][3])

    def chain(part):
        passed = product(part, False, ready, weights, slots[part])
        kept = product(part, True, ready, weights, slots[part])
        both = kept + permute(passed, other_core).astype(f32)
        came = permute(both[..., 2 * COLS :].astype(bf16), other_chip)
        total = (both[..., : 2 * COLS] + came.astype(f32)).astype(bf16)
        got = {}
        for dy in (2, 1, 3, 0):
            got[dy] = permute(total[dy], lambda x, y, z, c: linear(x + 2 * c, y + dy, z, c))
        own = jnp.stack([got[dy] for dy in range(4)])
        other = permute(own, other_core)
        picked = small_call(spread_kernel, [table, owner], [own, other], [(HALF, 2 * COLS)] * 4, pltpu.VMEM)
        got = {}
        for dz in (2, 1, 3, 0):
            got[dz] = permute(picked[dz], lambda x, y, z, c: linear(x ^ c, y, z + dz, x % 2))
        return [got[dz] for dz in range(4)]

    blocks = chain("y")
    blocks = chain("z") + blocks
    return small_call(
        arrange_kernel, [table], blocks, [(256, 8 * COLS)], pltpu.HBM, [pltpu.SemaphoreType.DMA((8,))]
    )[0]


def solution(mesh):
    in_specs = (P(None, ("group", "tp")), P("group", "tp"), P())
    out_specs = P("group", "tp")
    return jax.shard_map(shards, mesh=mesh, in_specs=in_specs, out_specs=out_specs, check_vma=False)
```

time: 171 us -> 163 us (0.953)
  starting transfers between devices: 60.8 us -> 54.1 us
  waiting for transfers between devices: 77.4 us -> 83 us
  other arithmetic: 4.6 us -> 1.57 us
  Pallas kernels: 25.2 us -> 22.6 us
    ppermute x31 -> x37, starting transfers between devices: 60.8 us -> 54.1 us  [permute(): lax.ppermute(value, AXES, [(i, move(*coords(i))) for i in range(N_DEV)])]
    ppermute x31 -> x37, waiting for transfers between devices: 77.4 us -> 83 us  [permute(): lax.ppermute(value, AXES, [(i, move(*coords(i))) for i in range(N_DEV)])]
    select_n x1 -> x0, other arithmetic: 1.9 us -> none  [gather(): relays.append(after(jnp.where(core == 0, first, second), second_job))]
    pallas_call x3 -> x4, Pallas kernels: 14.8 us -> 13.1 us  [product(): pl.pallas_call(functools.partial(product_kernel, part, (lambda core: core...]
  transfers between devices with their start and end apart: 31 -> 37, of which waited for: 19 -> 15; matrix products, arithmetic and copies ran while one was open for 3% -> 2% of each run, Pallas kernels for 7% -> 13%
where the time goes in v10:
time: 163 us
  waiting for transfers between devices  83 us (51%)
  starting transfers between devices  54.1 us (33%)
  Pallas kernels  22.6 us (14%)
    ppermute x37, waiting for transfers between devices, permute(): lax.ppermute(value, AXES, [(i, move(*coords(i))) for i in range(N_DEV)])  83 us
    ppermute x37, starting transfers between devices, permute(): lax.ppermute(value, AXES, [(i, move(*coords(i))) for i in range(N_DEV)])  54.1 us
    pallas_call x4, Pallas kernels, product(): pl.pallas_call(functools.partial(product_kernel, part, (lambda core: core...  13.1 us
    pallas_call x2, Pallas kernels, refit(): pl.pallas_call(functools.partial(refit_kernel, first), in_specs=[pl.Block...  6.55 us
  transfers between devices with their start and end apart: 37, of which 15 were waited for; matrix products, arithmetic and copies ran while one was open for 2% of the time, Pallas kernels for 13%

profile of v10, /device:TPU:3, one launch (start us, length us, event | category | flops | bytes accessed | tf_op | source)
XLA Modules:
  0.0 162.7 jit_solution(8781155822766294480)
XLA Ops:
  0.0 1.8 %collective-permute-start = (bf16[256,512]{1,0:T(8,128)(2,1)}, bf16[256,512]{1,0:T(8,128)(2,1)S(1)}, u32[]{:S(2)}, u32[]{:S(2)}) collective-permute-start(bf16[256,512]{1,0:T(8,128)(2,1)} %param.5), channel_id=1, source_target_pairs={{0,64},{1,65},{2,66},{3,67},{4,68},{5,69},{6,70},{7,71},{8,72},{9,... | collective-permute-start | bytes 786440 | tf_op jit(solution)/shard_map/ppermute | solution.py:30
  1.8 0.7 dynamic-slice_bitcast_fusion.table
  2.5 3.3 %shard_map.46 = (bf16[2048,256]{1,0:T(8,128)(2,1)S(1)}, bf16[2048,256]{1,0:T(8,128)(2,1)S(1)}) custom-call(s32[32]{0:T(128)S(1)} %dynamic-slice_bitcast_fusion.table, f32[8192,256]{1,0:T(8,128)} %master.3), custom_call_target="tpu_custom_call" | custom-call | flops 6291456 | bytes 6291456 | tf_op jit(solution)/shard_map/pallas_call | solution.py:122
  5.8 3.1 %collective-permute-done = bf16[256,512]{1,0:T(8,128)(2,1)S(1)} collective-permute-done((bf16[256,512]{1,0:T(8,128)(2,1)}, bf16[256,512]{1,0:T(8,128)(2,1)S(1)}, u32[]{:S(2)}, u32[]{:S(2)}) %collective-permute-start) | collective-permute-done | bytes 262176 | tf_op jit(solution)/shard_map/ppermute | solution.py:30
  8.9 2.8 %collective-permute-start.2 = (bf16[1,2,128,512]{3,2,1,0:T(8,128)(2,1)S(1)}, bf16[1,2,128,512]{3,2,1,0:T(8,128)(2,1)S(1)}, u32[]{:S(2)}, u32[]{:S(2)}) collective-permute-start(bf16[1,2,128,512]{3,2,1,0:T(8,128)(2,1)S(1)} %get-tuple-element.33), channel_id=1, source_target_pairs={{0,16},{1,49},{2,18},{3,51},{4,20},{5,53},{6,22},{7,55},{8,24},{9,... | collective-permute-start | bytes 786440 | tf_op jit(solution)/shard_map/ppermute | solution.py:30
  11.8 3.8 %collective-permute-start.1 = (bf16[1,2,128,512]{3,2,1,0:T(8,128)(2,1)S(1)}, bf16[1,2,128,512]{3,2,1,0:T(8,128)(2,1)S(1)}, u32[]{:S(2)}, u32[]{:S(2)}) collective-permute-start(bf16[1,2,128,512]{3,2,1,0:T(8,128)(2,1)S(1)} %get-tuple-element.32), channel_id=1, source_target_pairs={{0,2},{1,7},{2,0},{3,5},{4,6},{5,3},{6,4},{7,1},{8,10},{9,15},{10,... | collective-permute-start | bytes 786440 | tf_op jit(solution)/shard_map/ppermute | solution.py:30
  15.5 3.3 %shard_map.47 = (bf16[2048,256]{1,0:T(8,128)(2,1)S(1)}, bf16[2048,256]{1,0:T(8,128)(2,1)S(1)}) custom-call(s32[32]{0:T(128)S(1)} %dynamic-slice_bitcast_fusion.table, f32[8192,256]{1,0:T(8,128)} %master.3), custom_call_target="tpu_custom_call" | custom-call | flops 6291456 | bytes 6291456 | tf_op jit(solution)/shard_map/pallas_call | solution.py:122
  18.8 0.1 collective-permute-start.5
  18.9 0.3 collective-permute-start.7
  19.3 0.1 collective-permute-start.4
  19.4 0.1 collective-permute-start.3
  19.5 8.2 %collective-permute-done.4 = bf16[2,2,128,512]{3,2,1,0:T(8,128)(2,1)S(1)} collective-permute-done((bf16[2,2,128,512]{3,2,1,0:T(8,128)(2,1)S(1)}, bf16[2,2,128,512]{3,2,1,0:T(8,128)(2,1)S(1)}, u32[]{:S(2)}, u32[]{:S(2)}) %collective-permute-start.4) | collective-permute-done | bytes 524320 | tf_op jit(solution)/shard_map/ppermute | solution.py:30
  27.8 0.1 pad_maximum_fusion.1.refs_0_
  27.9 0.1 pad_maximum_fusion.refs_0_
  28.0 1.3 collective-permute-start.10
  29.3 14.0 %collective-permute-done.7 = bf16[2048,256]{1,0:T(8,128)(2,1)S(1)} collective-permute-done((bf16[2048,256]{1,0:T(8,128)(2,1)S(1)}, bf16[2048,256]{1,0:T(8,128)(2,1)S(1)}, u32[]{:S(2)}, u32[]{:S(2)}) %collective-permute-start.7) | collective-permute-done | bytes 1048608 | tf_op jit(solution)/shard_map/ppermute | solution.py:30
  43.3 1.3 collective-permute-start.8
  44.5 0.7 collective-permute-start.6
  45.3 0.2 collective-permute-start.25
  45.4 1.4 collective-permute-done.8.cross
  46.8 12.9 %collective-permute-done.6.refs_1_ = bf16[4,2,128,512]{3,2,1,0:T(8,128)(2,1)S(1)} collective-permute-done((bf16[4,2,128,512]{3,2,1,0:T(8,128)(2,1)S(1)}, bf16[4,2,128,512]{3,2,1,0:T(8,128)(2,1)S(1)}, u32[]{:S(2)}, u32[]{:S(2)}) %collective-permute-start.6) | collective-permute-done | bytes 1048608 | tf_op jit(solution)/shard_map/ppermute | solution.py:30
  59.7 0.3 collective-permute-start.12
  60.0 1.5 collective-permute-start.13
  61.4 9.0 %collective-permute-done.11.refs_3_ = bf16[4,2,128,512]{3,2,1,0:T(8,128)(2,1)S(1)} collective-permute-done((bf16[4,2,128,512]{3,2,1,0:T(8,128)(2,1)S(1)}, bf16[4,2,128,512]{3,2,1,0:T(8,128)(2,1)S(1)}, u32[]{:S(2)}, u32[]{:S(2)}) %collective-permute-start.11) | collective-permute-done | bytes 1048608 | tf_op jit(solution)/shard_map/ppermute | solution.py:30
  70.4 3.2 %collective-permute-done.9.refs_3_ = bf16[4,2,128,512]{3,2,1,0:T(8,128)(2,1)S(1)} collective-permute-done((bf16[4,2,128,512]{3,2,1,0:T(8,128)(2,1)S(1)}, bf16[4,2,128,512]{3,2,1,0:T(8,128)(2,1)S(1)}, u32[]{:S(2)}, u32[]{:S(2)}) %collective-permute-start.9) | collective-permute-done | bytes 1048608 | tf_op jit(solution)/shard_map/ppermute | solution.py:30
  73.6 10.1 %collective-permute-done.12.far = bf16[2048,256]{1,0:T(8,128)(2,1)S(1)} collective-permute-done((bf16[2048,256]{1,0:T(8,128)(2,1)S(1)}, bf16[2048,256]{1,0:T(8,128)(2,1)S(1)}, u32[]{:S(2)}, u32[]{:S(2)}) %collective-permute-start.12) | collective-permute-done | bytes 1048608 | tf_op jit(solution)/shard_map/ppermute | solution.py:30
  83.8 3.3 %shard_map.52 = bf16[4,128,1024]{2,1,0:T(8,128)(2,1)S(1)} custom-call(s32[32]{0:T(128)S(1)} %dynamic-slice_bitcast_fusion.table, bf16[2048,256]{1,0:T(8,128)(2,1)S(1)} %get-tuple-element.45.mine, bf16[2048,256]{1,0:T(8,128)(2,1)S(1)} %collective-permute-done.5.near, bf16[2048,256]{1,0:T(8,128)(2,1)S(1)} %collective-permute-done.12.far, ...), custom_call_target="tpu_custom_call" | custom-call | flops 2147483648 | bytes 8388608 | tf_op jit(solution)/shard_map/pallas_call | solution.py:165
  87.1 1.6 collective-permute-start.26
  88.6 3.3 %shard_map.49 = bf16[4,128,1024]{2,1,0:T(8,128)(2,1)S(1)} custom-call(s32[32]{0:T(128)S(1)} %dynamic-slice_bitcast_fusion.table, bf16[2048,256]{1,0:T(8,128)(2,1)S(1)} %get-tuple-element.45.mine, bf16[2048,256]{1,0:T(8,128)(2,1)S(1)} %collective-permute-done.5.near, bf16[2048,256]{1,0:T(8,128)(2,1)S(1)} %collective-permute-done.12.far, ...), custom_call_target="tpu_custom_call" | custom-call | flops 2147483648 | bytes 8388608 | tf_op jit(solution)/shard_map/pallas_call | solution.py:165
  91.9 0.3 collective-permute-start.14
  92.2 3.3 %shard_map.51 = f32[4,128,1024]{2,1,0:T(8,128)S(1)} custom-call(s32[32]{0:T(128)S(1)} %dynamic-slice_bitcast_fusion.table, bf16[2048,256]{1,0:T(8,128)(2,1)S(1)} %get-tuple-element.45.mine, bf16[2048,256]{1,0:T(8,128)(2,1)S(1)} %collective-permute-done.5.near, bf16[2048,256]{1,0:T(8,128)(2,1)S(1)} %collective-permute-done.12.far, ...), custom_call_target="tpu_custom_call" | custom-call | flops 2147483648 | bytes 8388608 | tf_op jit(solution)/shard_map/pallas_call | solution.py:165
  95.5 0.4 convert_add_fusion
  96.0 0.3 collective-permute-start.27
  96.4 3.3 %shard_map.48 = f32[4,128,1024]{2,1,0:T(8,128)S(1)} custom-call(s32[32]{0:T(128)S(1)} %dynamic-slice_bitcast_fusion.table, bf16[2048,256]{1,0:T(8,128)(2,1)S(1)} %get-tuple-element.45.mine, bf16[2048,256]{1,0:T(8,128)(2,1)S(1)} %collective-permute-done.5.near, bf16[2048,256]{1,0:T(8,128)(2,1)S(1)} %collective-permute-done.12.far, ...), custom_call_target="tpu_custom_call" | custom-call | flops 2147483648 | bytes 8388608 | tf_op jit(solution)/shard_map/pallas_call | solution.py:165
  99.7 0.3 convert_add_fusion.1
  100.0 1.3 collective-permute-start.15
  101.3 7.8 %collective-permute-done.27 = bf16[4,128,512]{2,1,0:T(8,128)(2,1)S(1)} collective-permute-done((bf16[4,128,512]{2,1,0:T(8,128)(2,1)S(1)}, bf16[4,128,512]{2,1,0:T(8,128)(2,1)S(1)}, u32[]{:S(2)}, u32[]{:S(2)}) %collective-permute-start.27) | collective-permute-done | bytes 524320 | tf_op jit(solution)/shard_map/ppermute | solution.py:30
  109.1 0.2 fusion
  109.3 3.8 %collective-permute-start.28 = (bf16[128,512]{1,0:T(8,128)(2,1)S(1)}, bf16[128,512]{1,0:T(8,128)(2,1)S(1)}, u32[]{:S(2)}, u32[]{:S(2)}) collective-permute-start(bf16[128,512]{1,0:T(8,128)(2,1)S(1)} %get-tuple-element.55), channel_id=1, source_target_pairs={{0,0},{1,65},{2,2},{3,67},{4,4},{5,69},{6,6},{7,71},{8,8},{9,73},{... | collective-permute-start | bytes 393224 | tf_op jit(solution)/shard_map/ppermute | solution.py:30
  113.1 0.5 collective-permute-start.29
  113.6 3.9 %collective-permute-start.30 = (bf16[128,512]{1,0:T(8,128)(2,1)S(1)}, bf16[128,512]{1,0:T(8,128)(2,1)S(1)}, u32[]{:S(2)}, u32[]{:S(2)}) collective-permute-start(bf16[128,512]{1,0:T(8,128)(2,1)S(1)} %get-tuple-element.57), channel_id=1, source_target_pairs={{0,32},{1,97},{2,34},{3,99},{4,36},{5,101},{6,38},{7,103},{8,40},{... | collective-permute-start | bytes 393224 | tf_op jit(solution)/shard_map/ppermute | solution.py:30
  117.4 2.5 %collective-permute-start.31 = (bf16[128,512]{1,0:T(8,128)(2,1)S(1)}, bf16[128,512]{1,0:T(8,128)(2,1)S(1)}, u32[]{:S(2)}, u32[]{:S(2)}) collective-permute-start(bf16[128,512]{1,0:T(8,128)(2,1)S(1)} %get-tuple-element.56), channel_id=1, source_target_pairs={{0,48},{1,113},{2,50},{3,115},{4,52},{5,117},{6,54},{7,119},{8,56}... | collective-permute-start | bytes 393224 | tf_op jit(solution)/shard_map/ppermute | solution.py:30
  119.9 0.5 collective-permute-done.15
  120.4 0.2 fusion.1
  120.6 3.0 %collective-permute-start.18 = (bf16[128,512]{1,0:T(8,128)(2,1)S(1)}, bf16[128,512]{1,0:T(8,128)(2,1)S(1)}, u32[]{:S(2)}, u32[]{:S(2)}) collective-permute-start(bf16[128,512]{1,0:T(8,128)(2,1)S(1)} %get-tuple-element.61), channel_id=1, source_target_pairs={{0,32},{1,97},{2,34},{3,99},{4,36},{5,101},{6,38},{7,103},{8,40},{... | collective-permute-start | bytes 393224 | tf_op jit(solution)/shard_map/ppermute | solution.py:30
  123.7 1.4 collective-permute-start.19
  125.1 3.7 %collective-permute-start.16 = (bf16[128,512]{1,0:T(8,128)(2,1)S(1)}, bf16[128,512]{1,0:T(8,128)(2,1)S(1)}, u32[]{:S(2)}, u32[]{:S(2)}) collective-permute-start(bf16[128,512]{1,0:T(8,128)(2,1)S(1)} %get-tuple-element.59), channel_id=1, source_target_pairs={{0,0},{1,65},{2,2},{3,67},{4,4},{5,69},{6,6},{7,71},{8,8},{9,73},{... | collective-permute-start | bytes 393224 | tf_op jit(solution)/shard_map/ppermute | solution.py:30
  128.8 1.8 %collective-permute-start.17 = (bf16[128,512]{1,0:T(8,128)(2,1)S(1)}, bf16[128,512]{1,0:T(8,128)(2,1)S(1)}, u32[]{:S(2)}, u32[]{:S(2)}) collective-permute-start(bf16[128,512]{1,0:T(8,128)(2,1)S(1)} %get-tuple-element.62), channel_id=1, source_target_pairs={{0,16},{1,81},{2,18},{3,83},{4,20},{5,85},{6,22},{7,87},{8,24},{9,... | collective-permute-start | bytes 393224 | tf_op jit(solution)/shard_map/ppermute | solution.py:30
  130.7 0.1 collective-permute-start.32
  130.8 1.5 collective-permute-done.16
  132.3 4.0 %collective-permute-done.17 = bf16[128,512]{1,0:T(8,128)(2,1)S(1)} collective-permute-done((bf16[128,512]{1,0:T(8,128)(2,1)S(1)}, bf16[128,512]{1,0:T(8,128)(2,1)S(1)}, u32[]{:S(2)}, u32[]{:S(2)}) %collective-permute-start.17) | collective-permute-done | bytes 131104 | tf_op jit(solution)/shard_map/ppermute | solution.py:30
  136.4 0.1 collective-permute-start.20
  136.5 0.7 shard_map.53
  137.2 3.2 %collective-permute-start.33 = (bf16[128,512]{1,0:T(8,128)(2,1)S(1)}, bf16[128,512]{1,0:T(8,128)(2,1)S(1)}, u32[]{:S(2)}, u32[]{:S(2)}) collective-permute-start(bf16[128,512]{1,0:T(8,128)(2,1)S(1)} %get-tuple-element.51), channel_id=1, source_target_pairs={{0,0},{1,8},{2,2},{3,10},{4,4},{5,12},{6,6},{7,14},{8,9},{9,1},{10... | collective-permute-start | bytes 393224 | tf_op jit(solution)/shard_map/ppermute | solution.py:30
  140.4 1.8 %collective-permute-start.34 = (bf16[128,512]{1,0:T(8,128)(2,1)S(1)}, bf16[128,512]{1,0:T(8,128)(2,1)S(1)}, u32[]{:S(2)}, u32[]{:S(2)}) collective-permute-start(bf16[128,512]{1,0:T(8,128)(2,1)S(1)} %get-tuple-element.52), channel_id=1, source_target_pairs={{0,2},{1,10},{2,4},{3,12},{4,6},{5,14},{6,0},{7,8},{8,11},{9,3},{1... | collective-permute-start | bytes 393224 | tf_op jit(solution)/shard_map/ppermute | solution.py:30
  142.2 1.8 %collective-permute-start.35 = (bf16[128,512]{1,0:T(8,128)(2,1)S(1)}, bf16[128,512]{1,0:T(8,128)(2,1)S(1)}, u32[]{:S(2)}, u32[]{:S(2)}) collective-permute-start(bf16[128,512]{1,0:T(8,128)(2,1)S(1)} %get-tuple-element.53), channel_id=1, source_target_pairs={{0,4},{1,12},{2,6},{3,14},{4,0},{5,8},{6,2},{7,10},{8,13},{9,5},{1... | collective-permute-start | bytes 393224 | tf_op jit(solution)/shard_map/ppermute | solution.py:30
  144.0 3.0 %collective-permute-start.36 = (bf16[128,512]{1,0:T(8,128)(2,1)S(1)}, bf16[128,512]{1,0:T(8,128)(2,1)S(1)}, u32[]{:S(2)}, u32[]{:S(2)}) collective-permute-start(bf16[128,512]{1,0:T(8,128)(2,1)S(1)} %get-tuple-element.54), channel_id=1, source_target_pairs={{0,6},{1,14},{2,0},{3,8},{4,2},{5,10},{6,4},{7,12},{8,15},{9,7},{1... | collective-permute-start | bytes 393224 | tf_op jit(solution)/shard_map/ppermute | solution.py:30
  146.9 0.7 shard_map.50
  147.6 2.4 %collective-permute-start.21 = (bf16[128,512]{1,0:T(8,128)(2,1)S(1)}, bf16[128,512]{1,0:T(8,128)(2,1)S(1)}, u32[]{:S(2)}, u32[]{:S(2)}) collective-permute-start(bf16[128,512]{1,0:T(8,128)(2,1)S(1)} %get-tuple-element.47), channel_id=1, source_target_pairs={{0,0},{1,8},{2,2},{3,10},{4,4},{5,12},{6,6},{7,14},{8,9},{9,1},{10... | collective-permute-start | bytes 393224 | tf_op jit(solution)/shard_map/ppermute | solution.py:30
  150.1 1.3 collective-permute-start.23
  151.4 2.3 %collective-permute-start.24 = (bf16[128,512]{1,0:T(8,128)(2,1)S(1)}, bf16[128,512]{1,0:T(8,128)(2,1)S(1)}, u32[]{:S(2)}, u32[]{:S(2)}) collective-permute-start(bf16[128,512]{1,0:T(8,128)(2,1)S(1)} %get-tuple-element.50), channel_id=1, source_target_pairs={{0,6},{1,14},{2,0},{3,8},{4,2},{5,10},{6,4},{7,12},{8,15},{9,7},{1... | collective-permute-start | bytes 393224 | tf_op jit(solution)/shard_map/ppermute | solution.py:30
  153.7 6.2 %collective-permute-done.22.refs_1_ = bf16[128,512]{1,0:T(8,128)(2,1)S(1)} collective-permute-done((bf16[128,512]{1,0:T(8,128)(2,1)S(1)}, bf16[128,512]{1,0:T(8,128)(2,1)S(1)}, u32[]{:S(2)}, u32[]{:S(2)}) %collective-permute-start.22) | collective-permute-done | bytes 131104 | tf_op jit(solution)/shard_map/ppermute | solution.py:30
  159.9 1.1 collective-permute-done.24.refs_3_
  161.0 1.6 shard_map.54
  (39 shorter events, 0.7 us)
Async XLA Ops:
  0.0 8.9 %collective-permute-start = (bf16[256,512]{1,0:T(8,128)(2,1)}, bf16[256,512]{1,0:T(8,128)(2,1)S(1)}, u32[]{:S(2)}, u32[]{:S(2)}) collective-permute-start(bf16[256,512]{1,0:T(8,128)(2,1)} %param.5), channel_id=1, source_target_pairs={{0,64},{1,65},{2,66},{3,67},{4,68},{5,69},{6,70},{7,71},{8,72},{9,... | collective-permute-start | bytes 786440 | tf_op jit(solution)/shard_map/ppermute | solution.py:30
  2.5 6.4 %copy-start.1 = (bf16[256,512]{1,0:T(8,128)(2,1)S(1)}, bf16[256,512]{1,0:T(8,128)(2,1)}, u32[]{:S(2)}) copy-start(bf16[256,512]{1,0:T(8,128)(2,1)} %param.5) | copy-start | bytes 786436
  8.9 10.3 %collective-permute-start.2 = (bf16[1,2,128,512]{3,2,1,0:T(8,128)(2,1)S(1)}, bf16[1,2,128,512]{3,2,1,0:T(8,128)(2,1)S(1)}, u32[]{:S(2)}, u32[]{:S(2)}) collective-permute-start(bf16[1,2,128,512]{3,2,1,0:T(8,128)(2,1)S(1)} %get-tuple-element.33), channel_id=1, source_target_pairs={{0,16},{1,49},{2,18},{3,51},{4,20},{5,53},{6,22},{7,55},{8,24},{9,... | collective-permute-start | bytes 786440 | tf_op jit(solution)/shard_map/ppermute | solution.py:30
  11.8 7.5 %collective-permute-start.1 = (bf16[1,2,128,512]{3,2,1,0:T(8,128)(2,1)S(1)}, bf16[1,2,128,512]{3,2,1,0:T(8,128)(2,1)S(1)}, u32[]{:S(2)}, u32[]{:S(2)}) collective-permute-start(bf16[1,2,128,512]{3,2,1,0:T(8,128)(2,1)S(1)} %get-tuple-element.32), channel_id=1, source_target_pairs={{0,2},{1,7},{2,0},{3,5},{4,6},{5,3},{6,4},{7,1},{8,10},{9,15},{10,... | collective-permute-start | bytes 786440 | tf_op jit(solution)/shard_map/ppermute | solution.py:30
  18.8 9.2 %collective-permute-start.5 = (bf16[2048,256]{1,0:T(8,128)(2,1)S(1)}, bf16[2048,256]{1,0:T(8,128)(2,1)S(1)}, u32[]{:S(2)}, u32[]{:S(2)}) collective-permute-start(bf16[2048,256]{1,0:T(8,128)(2,1)S(1)} %get-tuple-element.38), channel_id=1, source_target_pairs={{0,1},{1,0},{2,3},{3,2},{4,5},{5,4},{6,7},{7,6},{8,9},{9,8},{10,11... | collective-permute-start | bytes 3145736 | tf_op jit(solution)/shard_map/ppermute | solution.py:30
  18.9 24.4 %collective-permute-start.7 = (bf16[2048,256]{1,0:T(8,128)(2,1)S(1)}, bf16[2048,256]{1,0:T(8,128)(2,1)S(1)}, u32[]{:S(2)}, u32[]{:S(2)}) collective-permute-start(bf16[2048,256]{1,0:T(8,128)(2,1)S(1)} %get-tuple-element.40), channel_id=1, source_target_pairs={{0,8},{1,9},{2,10},{3,11},{4,12},{5,13},{6,14},{7,15},{8,0},{9,1},... | collective-permute-start | bytes 3145736 | tf_op jit(solution)/shard_map/ppermute | solution.py:30
  19.3 8.4 %collective-permute-start.4 = (bf16[2,2,128,512]{3,2,1,0:T(8,128)(2,1)S(1)}, bf16[2,2,128,512]{3,2,1,0:T(8,128)(2,1)S(1)}, u32[]{:S(2)}, u32[]{:S(2)}) collective-permute-start(bf16[2,2,128,512]{3,2,1,0:T(8,128)(2,1)S(1)} %pad_maximum_fusion.3), channel_id=1, source_target_pairs={{0,48},{1,17},{2,50},{3,19},{4,52},{5,21},{6,54},{7,23},{8,56},{9,... | collective-permute-start | bytes 1572872 | tf_op jit(solution)/shard_map/ppermute | solution.py:30
  19.4 8.4 %collective-permute-start.3 = (bf16[2,2,128,512]{3,2,1,0:T(8,128)(2,1)S(1)}, bf16[2,2,128,512]{3,2,1,0:T(8,128)(2,1)S(1)}, u32[]{:S(2)}, u32[]{:S(2)}) collective-permute-start(bf16[2,2,128,512]{3,2,1,0:T(8,128)(2,1)S(1)} %pad_maximum_fusion.2), channel_id=1, source_target_pairs={{0,6},{1,3},{2,4},{3,1},{4,2},{5,7},{6,0},{7,5},{8,14},{9,11},{10,... | collective-permute-start | bytes 1572872 | tf_op jit(solution)/shard_map/ppermute | solution.py:30
  28.0 17.5 %collective-permute-start.10 = (bf16[4,2,128,512]{3,2,1,0:T(8,128)(2,1)S(1)}, bf16[4,2,128,512]{3,2,1,0:T(8,128)(2,1)S(1)}, u32[]{:S(2)}, u32[]{:S(2)}) collective-permute-start(bf16[4,2,128,512]{3,2,1,0:T(8,128)(2,1)S(1)} %pad_maximum_fusion.refs_0_), channel_id=1, source_target_pairs={{0,16},{1,49},{2,18},{3,51},{4,20},{5,53},{6,22},{7,55},{8,24},{9,... | collective-permute-start | bytes 3145736 | tf_op jit(solution)/shard_map/ppermute | solution.py:30
  43.3 3.5 %collective-permute-start.8 = (bf16[2048,256]{1,0:T(8,128)(2,1)S(1)}, bf16[2048,256]{1,0:T(8,128)(2,1)S(1)}, u32[]{:S(2)}, u32[]{:S(2)}) collective-permute-start(bf16[2048,256]{1,0:T(8,128)(2,1)S(1)} %collective-permute-done.7), channel_id=1, source_target_pairs={{0,1},{1,0},{2,3},{3,2},{4,5},{5,4},{6,7},{7,6},{8,9},{9,8},{10,11... | collective-permute-start | bytes 3145736 | tf_op jit(solution)/shard_map/ppermute | solution.py:30
  44.5 15.2 %collective-permute-start.6 = (bf16[4,2,128,512]{3,2,1,0:T(8,128)(2,1)S(1)}, bf16[4,2,128,512]{3,2,1,0:T(8,128)(2,1)S(1)}, u32[]{:S(2)}, u32[]{:S(2)}) collective-permute-start(bf16[4,2,128,512]{3,2,1,0:T(8,128)(2,1)S(1)} %pad_maximum_fusion.1.refs_0_), channel_id=1, source_target_pairs={{0,2},{1,7},{2,0},{3,5},{4,6},{5,3},{6,4},{7,1},{8,10},{9,15},{10,... | collective-permute-start | bytes 3145736 | tf_op jit(solution)/shard_map/ppermute | solution.py:30
  45.3 28.4 %collective-permute-start.25 = (bf16[4,2,128,512]{3,2,1,0:T(8,128)(2,1)S(1)}, bf16[4,2,128,512]{3,2,1,0:T(8,128)(2,1)S(1)}, u32[]{:S(2)}, u32[]{:S(2)}) collective-permute-start(bf16[4,2,128,512]{3,2,1,0:T(8,128)(2,1)S(1)} %pad_maximum_fusion.refs_0_), channel_id=1, source_target_pairs={{0,48},{1,17},{2,50},{3,19},{4,52},{5,21},{6,54},{7,23},{8,56},{9,... | collective-permute-start | bytes 3145736 | tf_op jit(solution)/shard_map/ppermute | solution.py:30
  46.8 23.6 %collective-permute-start.11 = (bf16[4,2,128,512]{3,2,1,0:T(8,128)(2,1)S(1)}, bf16[4,2,128,512]{3,2,1,0:T(8,128)(2,1)S(1)}, u32[]{:S(2)}, u32[]{:S(2)}) collective-permute-start(bf16[4,2,128,512]{3,2,1,0:T(8,128)(2,1)S(1)} %collective-permute-done.10.refs_1_), channel_id=1, source_target_pairs={{0,48},{1,17},{2,50},{3,19},{4,52},{5,21},{6,54},{7,23},{8,56},{9,... | collective-permute-start | bytes 3145736 | tf_op jit(solution)/shard_map/ppermute | solution.py:30
  59.7 13.9 %collective-permute-start.9 = (bf16[4,2,128,512]{3,2,1,0:T(8,128)(2,1)S(1)}, bf16[4,2,128,512]{3,2,1,0:T(8,128)(2,1)S(1)}, u32[]{:S(2)}, u32[]{:S(2)}) collective-permute-start(bf16[4,2,128,512]{3,2,1,0:T(8,128)(2,1)S(1)} %collective-permute-done.6.refs_1_), channel_id=1, source_target_pairs={{0,6},{1,3},{2,4},{3,1},{4,2},{5,7},{6,0},{7,5},{8,14},{9,11},{10,... | collective-permute-start | bytes 3145736 | tf_op jit(solution)/shard_map/ppermute | solution.py:30
  59.7 24.1 %collective-permute-start.12 = (bf16[2048,256]{1,0:T(8,128)(2,1)S(1)}, bf16[2048,256]{1,0:T(8,128)(2,1)S(1)}, u32[]{:S(2)}, u32[]{:S(2)}) collective-permute-start(bf16[2048,256]{1,0:T(8,128)(2,1)S(1)} %get-tuple-element.46), channel_id=1, source_target_pairs={{0,8},{1,9},{2,10},{3,11},{4,12},{5,13},{6,14},{7,15},{8,0},{9,1},... | collective-permute-start | bytes 3145736 | tf_op jit(solution)/shard_map/ppermute | solution.py:30
  60.0 28.7 %collective-permute-start.13 = (bf16[4,2,128,512]{3,2,1,0:T(8,128)(2,1)S(1)}, bf16[4,2,128,512]{3,2,1,0:T(8,128)(2,1)S(1)}, u32[]{:S(2)}, u32[]{:S(2)}) collective-permute-start(bf16[4,2,128,512]{3,2,1,0:T(8,128)(2,1)S(1)} %pad_maximum_fusion.1.refs_0_), channel_id=1, source_target_pairs={{0,6},{1,3},{2,4},{3,1},{4,2},{5,7},{6,0},{7,5},{8,14},{9,11},{10,... | collective-permute-start | bytes 3145736 | tf_op jit(solution)/shard_map/ppermute | solution.py:30
  87.1 8.4 %collective-permute-start.26 = (bf16[4,128,1024]{2,1,0:T(8,128)(2,1)S(1)}, bf16[4,128,1024]{2,1,0:T(8,128)(2,1)S(1)}, u32[]{:S(2)}, u32[]{:S(2)}) collective-permute-start(bf16[4,128,1024]{2,1,0:T(8,128)(2,1)S(1)} %shard_map.52), channel_id=1, source_target_pairs={{0,1},{1,0},{2,3},{3,2},{4,5},{5,4},{6,7},{7,6},{8,9},{9,8},{10,11... | collective-permute-start | bytes 3145736 | tf_op jit(solution)/shard_map/ppermute | solution.py:30
  91.9 7.7 %collective-permute-start.14 = (bf16[4,128,1024]{2,1,0:T(8,128)(2,1)S(1)}, bf16[4,128,1024]{2,1,0:T(8,128)(2,1)S(1)}, u32[]{:S(2)}, u32[]{:S(2)}) collective-permute-start(bf16[4,128,1024]{2,1,0:T(8,128)(2,1)S(1)} %shard_map.49), channel_id=1, source_target_pairs={{0,1},{1,0},{2,3},{3,2},{4,5},{5,4},{6,7},{7,6},{8,9},{9,8},{10,11... | collective-permute-start | bytes 3145736 | tf_op jit(solution)/shard_map/ppermute | solution.py:30
  96.0 13.1 %collective-permute-start.27 = (bf16[4,128,512]{2,1,0:T(8,128)(2,1)S(1)}, bf16[4,128,512]{2,1,0:T(8,128)(2,1)S(1)}, u32[]{:S(2)}, u32[]{:S(2)}) collective-permute-start(bf16[4,128,512]{2,1,0:T(8,128)(2,1)S(1)} %slice.96), channel_id=1, source_target_pairs={{0,8},{1,9},{2,10},{3,11},{4,12},{5,13},{6,14},{7,15},{8,0},{9,1},... | collective-permute-start | bytes 1572872 | tf_op jit(solution)/shard_map/ppermute | solution.py:30
  100.0 20.3 %collective-permute-start.15 = (bf16[4,128,512]{2,1,0:T(8,128)(2,1)S(1)}, bf16[4,128,512]{2,1,0:T(8,128)(2,1)S(1)}, u32[]{:S(2)}, u32[]{:S(2)}) collective-permute-start(bf16[4,128,512]{2,1,0:T(8,128)(2,1)S(1)} %slice.97), channel_id=1, source_target_pairs={{0,8},{1,9},{2,10},{3,11},{4,12},{5,13},{6,14},{7,15},{8,0},{9,1},... | collective-permute-start | bytes 1572872 | tf_op jit(solution)/shard_map/ppermute | solution.py:30
  109.3 14.3 %collective-permute-start.28 = (bf16[128,512]{1,0:T(8,128)(2,1)S(1)}, bf16[128,512]{1,0:T(8,128)(2,1)S(1)}, u32[]{:S(2)}, u32[]{:S(2)}) collective-permute-start(bf16[128,512]{1,0:T(8,128)(2,1)S(1)} %get-tuple-element.55), channel_id=1, source_target_pairs={{0,0},{1,65},{2,2},{3,67},{4,4},{5,69},{6,6},{7,71},{8,8},{9,73},{... | collective-permute-start | bytes 393224 | tf_op jit(solution)/shard_map/ppermute | solution.py:30
  113.1 12.0 %collective-permute-start.29 = (bf16[128,512]{1,0:T(8,128)(2,1)S(1)}, bf16[128,512]{1,0:T(8,128)(2,1)S(1)}, u32[]{:S(2)}, u32[]{:S(2)}) collective-permute-start(bf16[128,512]{1,0:T(8,128)(2,1)S(1)} %get-tuple-element.58), channel_id=1, source_target_pairs={{0,16},{1,81},{2,18},{3,83},{4,20},{5,85},{6,22},{7,87},{8,24},{9,... | collective-permute-start | bytes 393224 | tf_op jit(solution)/shard_map/ppermute | solution.py:30
  113.6 15.2 %collective-permute-start.30 = (bf16[128,512]{1,0:T(8,128)(2,1)S(1)}, bf16[128,512]{1,0:T(8,128)(2,1)S(1)}, u32[]{:S(2)}, u32[]{:S(2)}) collective-permute-start(bf16[128,512]{1,0:T(8,128)(2,1)S(1)} %get-tuple-element.57), channel_id=1, source_target_pairs={{0,32},{1,97},{2,34},{3,99},{4,36},{5,101},{6,38},{7,103},{8,40},{... | collective-permute-start | bytes 393224 | tf_op jit(solution)/shard_map/ppermute | solution.py:30
  117.4 13.2 %collective-permute-start.31 = (bf16[128,512]{1,0:T(8,128)(2,1)S(1)}, bf16[128,512]{1,0:T(8,128)(2,1)S(1)}, u32[]{:S(2)}, u32[]{:S(2)}) collective-permute-start(bf16[128,512]{1,0:T(8,128)(2,1)S(1)} %get-tuple-element.56), channel_id=1, source_target_pairs={{0,48},{1,113},{2,50},{3,115},{4,52},{5,117},{6,54},{7,119},{8,56}... | collective-permute-start | bytes 393224 | tf_op jit(solution)/shard_map/ppermute | solution.py:30
  120.6 15.9 %copy-start = (s32[8]{0:T(128)S(1)}, s32[8]{0:T(128)}, u32[]{:S(2)}) copy-start(s32[8]{0:T(128)} %owner.3) | copy-start | bytes 100
  120.6 10.2 %collective-permute-start.18 = (bf16[128,512]{1,0:T(8,128)(2,1)S(1)}, bf16[128,512]{1,0:T(8,128)(2,1)S(1)}, u32[]{:S(2)}, u32[]{:S(2)}) collective-permute-start(bf16[128,512]{1,0:T(8,128)(2,1)S(1)} %get-tuple-element.61), channel_id=1, source_target_pairs={{0,32},{1,97},{2,34},{3,99},{4,36},{5,101},{6,38},{7,103},{8,40},{... | collective-permute-start | bytes 393224 | tf_op jit(solution)/shard_map/ppermute | solution.py:30
  123.7 7.2 %collective-permute-start.19 = (bf16[128,512]{1,0:T(8,128)(2,1)S(1)}, bf16[128,512]{1,0:T(8,128)(2,1)S(1)}, u32[]{:S(2)}, u32[]{:S(2)}) collective-permute-start(bf16[128,512]{1,0:T(8,128)(2,1)S(1)} %get-tuple-element.60), channel_id=1, source_target_pairs={{0,48},{1,113},{2,50},{3,115},{4,52},{5,117},{6,54},{7,119},{8,56}... | collective-permute-start | bytes 393224 | tf_op jit(solution)/shard_map/ppermute | solution.py:30
  125.1 7.2 %collective-permute-start.16 = (bf16[128,512]{1,0:T(8,128)(2,1)S(1)}, bf16[128,512]{1,0:T(8,128)(2,1)S(1)}, u32[]{:S(2)}, u32[]{:S(2)}) collective-permute-start(bf16[128,512]{1,0:T(8,128)(2,1)S(1)} %get-tuple-element.59), channel_id=1, source_target_pairs={{0,0},{1,65},{2,2},{3,67},{4,4},{5,69},{6,6},{7,71},{8,8},{9,73},{... | collective-permute-start | bytes 393224 | tf_op jit(solution)/shard_map/ppermute | solution.py:30
  128.8 7.5 %collective-permute-start.17 = (bf16[128,512]{1,0:T(8,128)(2,1)S(1)}, bf16[128,512]{1,0:T(8,128)(2,1)S(1)}, u32[]{:S(2)}, u32[]{:S(2)}) collective-permute-start(bf16[128,512]{1,0:T(8,128)(2,1)S(1)} %get-tuple-element.62), channel_id=1, source_target_pairs={{0,16},{1,81},{2,18},{3,83},{4,20},{5,85},{6,22},{7,87},{8,24},{9,... | collective-permute-start | bytes 393224 | tf_op jit(solution)/shard_map/ppermute | solution.py:30
  130.7 5.8 %collective-permute-start.32 = (bf16[4,128,512]{2,1,0:T(8,128)(2,1)S(1)}, bf16[4,128,512]{2,1,0:T(8,128)(2,1)S(1)}, u32[]{:S(2)}, u32[]{:S(2)}) collective-permute-start(bf16[4,128,512]{2,1,0:T(8,128)(2,1)S(1)} %pad_maximum_fusion.5.own), channel_id=1, source_target_pairs={{0,1},{1,0},{2,3},{3,2},{4,5},{5,4},{6,7},{7,6},{8,9},{9,8},{10,11... | collective-permute-start | bytes 1572872 | tf_op jit(solution)/shard_map/ppermute | solution.py:30
  136.4 10.5 %collective-permute-start.20 = (bf16[4,128,512]{2,1,0:T(8,128)(2,1)S(1)}, bf16[4,128,512]{2,1,0:T(8,128)(2,1)S(1)}, u32[]{:S(2)}, u32[]{:S(2)}) collective-permute-start(bf16[4,128,512]{2,1,0:T(8,128)(2,1)S(1)} %pad_maximum_fusion.4.own), channel_id=1, source_target_pairs={{0,1},{1,0},{2,3},{3,2},{4,5},{5,4},{6,7},{7,6},{8,9},{9,8},{10,11... | collective-permute-start | bytes 1572872 | tf_op jit(solution)/shard_map/ppermute | solution.py:30
  137.2 12.8 %collective-permute-start.33 = (bf16[128,512]{1,0:T(8,128)(2,1)S(1)}, bf16[128,512]{1,0:T(8,128)(2,1)S(1)}, u32[]{:S(2)}, u32[]{:S(2)}) collective-permute-start(bf16[128,512]{1,0:T(8,128)(2,1)S(1)} %get-tuple-element.51), channel_id=1, source_target_pairs={{0,0},{1,8},{2,2},{3,10},{4,4},{5,12},{6,6},{7,14},{8,9},{9,1},{10... | collective-permute-start | bytes 393224 | tf_op jit(solution)/shard_map/ppermute | solution.py:30
  140.4 9.7 %collective-permute-start.34 = (bf16[128,512]{1,0:T(8,128)(2,1)S(1)}, bf16[128,512]{1,0:T(8,128)(2,1)S(1)}, u32[]{:S(2)}, u32[]{:S(2)}) collective-permute-start(bf16[128,512]{1,0:T(8,128)(2,1)S(1)} %get-tuple-element.52), channel_id=1, source_target_pairs={{0,2},{1,10},{2,4},{3,12},{4,6},{5,14},{6,0},{7,8},{8,11},{9,3},{1... | collective-permute-start | bytes 393224 | tf_op jit(solution)/shard_map/ppermute | solution.py:30
  142.2 9.2 %collective-permute-start.35 = (bf16[128,512]{1,0:T(8,128)(2,1)S(1)}, bf16[128,512]{1,0:T(8,128)(2,1)S(1)}, u32[]{:S(2)}, u32[]{:S(2)}) collective-permute-start(bf16[128,512]{1,0:T(8,128)(2,1)S(1)} %get-tuple-element.53), channel_id=1, source_target_pairs={{0,4},{1,12},{2,6},{3,14},{4,0},{5,8},{6,2},{7,10},{8,13},{9,5},{1... | collective-permute-start | bytes 393224 | tf_op jit(solution)/shard_map/ppermute | solution.py:30
  144.0 9.7 %collective-permute-start.36 = (bf16[128,512]{1,0:T(8,128)(2,1)S(1)}, bf16[128,512]{1,0:T(8,128)(2,1)S(1)}, u32[]{:S(2)}, u32[]{:S(2)}) collective-permute-start(bf16[128,512]{1,0:T(8,128)(2,1)S(1)} %get-tuple-element.54), channel_id=1, source_target_pairs={{0,6},{1,14},{2,0},{3,8},{4,2},{5,10},{6,4},{7,12},{8,15},{9,7},{1... | collective-permute-start | bytes 393224 | tf_op jit(solution)/shard_map/ppermute | solution.py:30
  147.6 6.1 %collective-permute-start.21 = (bf16[128,512]{1,0:T(8,128)(2,1)S(1)}, bf16[128,512]{1,0:T(8,128)(2,1)S(1)}, u32[]{:S(2)}, u32[]{:S(2)}) collective-permute-start(bf16[128,512]{1,0:T(8,128)(2,1)S(1)} %get-tuple-element.47), channel_id=1, source_target_pairs={{0,0},{1,8},{2,2},{3,10},{4,4},{5,12},{6,6},{7,14},{8,9},{9,1},{10... | collective-permute-start | bytes 393224 | tf_op jit(solution)/shard_map/ppermute | solution.py:30
  150.0 9.9 %collective-permute-start.22 = (bf16[128,512]{1,0:T(8,128)(2,1)S(1)}, bf16[128,512]{1,0:T(8,128)(2,1)S(1)}, u32[]{:S(2)}, u32[]{:S(2)}) collective-permute-start(bf16[128,512]{1,0:T(8,128)(2,1)S(1)} %get-tuple-element.48), channel_id=1, source_target_pairs={{0,2},{1,10},{2,4},{3,12},{4,6},{5,14},{6,0},{7,8},{8,11},{9,3},{1... | collective-permute-start | bytes 393224 | tf_op jit(solution)/shard_map/ppermute | solution.py:30
  150.1 9.8 %collective-permute-start.23 = (bf16[128,512]{1,0:T(8,128)(2,1)S(1)}, bf16[128,512]{1,0:T(8,128)(2,1)S(1)}, u32[]{:S(2)}, u32[]{:S(2)}) collective-permute-start(bf16[128,512]{1,0:T(8,128)(2,1)S(1)} %get-tuple-element.49), channel_id=1, source_target_pairs={{0,4},{1,12},{2,6},{3,14},{4,0},{5,8},{6,2},{7,10},{8,13},{9,5},{1... | collective-permute-start | bytes 393224 | tf_op jit(solution)/shard_map/ppermute | solution.py:30
  151.4 9.6 %collective-permute-start.24 = (bf16[128,512]{1,0:T(8,128)(2,1)S(1)}, bf16[128,512]{1,0:T(8,128)(2,1)S(1)}, u32[]{:S(2)}, u32[]{:S(2)}) collective-permute-start(bf16[128,512]{1,0:T(8,128)(2,1)S(1)} %get-tuple-element.50), channel_id=1, source_target_pairs={{0,6},{1,14},{2,0},{3,8},{4,2},{5,10},{6,4},{7,12},{8,15},{9,7},{1... | collective-permute-start | bytes 393224 | tf_op jit(solution)/shard_map/ppermute | solution.py:30

commit v11 on v10

--- a/solution.py
+++ b/solution.py
@@ -70,7 +70,7 @@
     slots = {}
     for part, v in blocks.items():
         first = exchange(v, part, 1)
-        second = exchange(v, part, 2)
+        second = exchange(after(v, third_job), part, 2)
         slots[part] = [v, first, second, exchange(after(first, third_job), part, 2)]
     return slots
 
@@ -224,10 +224,10 @@
     same, swapped = refit(table, master, AWAY, 2)
     sent, mine = refit(table, master, HERE, 2)
     near = permute(sent, other_core)
-    swapped = permute(swapped, other_chip)
-    cross = permute(swapped, other_core)
-    slots = gather(activations, same, near, cross)
-    far = permute(after(same, swapped), other_chip)
+    far = permute(same, other_chip)
+    swapped = permute(swapped, other_core)
+    slots = gather(activations, same, (near, swapped), far)
+    cross = permute(after(swapped, far), other_chip)
     weights = [mine, near, far, cross]
     ready = after(table, slots["z"][3], slots["y"][3])
 

time: 163 us -> 152 us (0.933)
  waiting for transfers between devices: 83 us -> 68.3 us
  starting transfers between devices: 54.1 us -> 58.1 us
    ppermute x37, waiting for transfers between devices: 83 us -> 68.3 us  [permute(): lax.ppermute(value, AXES, [(i, move(*coords(i))) for i in range(N_DEV)])]
    ppermute x37, starting transfers between devices: 54.1 us -> 58.1 us  [permute(): lax.ppermute(value, AXES, [(i, move(*coords(i))) for i in range(N_DEV)])]
  transfers between devices with their start and end apart: 37 -> 37, of which waited for: 15 -> 17; matrix products, arithmetic and copies ran while one was open for 2% -> 2% of each run, Pallas kernels for 13% -> 14%
where the time goes in v11:
time: 152 us
  waiting for transfers between devices  68.3 us (45%)
  starting transfers between devices  58.1 us (38%)
  Pallas kernels  22.6 us (15%)
  other arithmetic  1.53 us (1%)
    ppermute x37, waiting for transfers between devices, permute(): lax.ppermute(value, AXES, [(i, move(*coords(i))) for i in range(N_DEV)])  68.3 us
    ppermute x37, starting transfers between devices, permute(): lax.ppermute(value, AXES, [(i, move(*coords(i))) for i in range(N_DEV)])  58.1 us
    pallas_call x4, Pallas kernels, product(): pl.pallas_call(functools.partial(product_kernel, part, (lambda core: core...  13.1 us
    pallas_call x2, Pallas kernels, refit(): pl.pallas_call(functools.partial(refit_kernel, first), in_specs=[pl.Block...  6.55 us
  transfers between devices with their start and end apart: 37, of which 17 were waited for; matrix products, arithmetic and copies ran while one was open for 2% of the time, Pallas kernels for 14%

profile of v11, /device:TPU:3, one launch (start us, length us, event | category | flops | bytes accessed | tf_op | source)
XLA Modules:
  0.0 151.9 jit_solution(3651308372218044951)
XLA Ops:
  0.0 1.8 %collective-permute-start = (bf16[256,512]{1,0:T(8,128)(2,1)}, bf16[256,512]{1,0:T(8,128)(2,1)S(1)}, u32[]{:S(2)}, u32[]{:S(2)}) collective-permute-start(bf16[256,512]{1,0:T(8,128)(2,1)} %param.5), channel_id=1, source_target_pairs={{0,64},{1,65},{2,66},{3,67},{4,68},{5,69},{6,70},{7,71},{8,72},{9,... | collective-permute-start | bytes 786440 | tf_op jit(solution)/shard_map/ppermute | solution.py:30
  1.8 0.7 dynamic-slice_bitcast_fusion.table
  2.5 3.3 %shard_map.46 = (bf16[2048,256]{1,0:T(8,128)(2,1)S(1)}, bf16[2048,256]{1,0:T(8,128)(2,1)S(1)}) custom-call(s32[32]{0:T(128)S(1)} %dynamic-slice_bitcast_fusion.table, f32[8192,256]{1,0:T(8,128)} %master.3), custom_call_target="tpu_custom_call" | custom-call | flops 6291456 | bytes 6291456 | tf_op jit(solution)/shard_map/pallas_call | solution.py:122
  5.8 3.1 %collective-permute-done = bf16[256,512]{1,0:T(8,128)(2,1)S(1)} collective-permute-done((bf16[256,512]{1,0:T(8,128)(2,1)}, bf16[256,512]{1,0:T(8,128)(2,1)S(1)}, u32[]{:S(2)}, u32[]{:S(2)}) %collective-permute-start) | collective-permute-done | bytes 262176 | tf_op jit(solution)/shard_map/ppermute | solution.py:30
  8.9 3.8 %collective-permute-start.1 = (bf16[1,2,128,512]{3,2,1,0:T(8,128)(2,1)S(1)}, bf16[1,2,128,512]{3,2,1,0:T(8,128)(2,1)S(1)}, u32[]{:S(2)}, u32[]{:S(2)}) collective-permute-start(bf16[1,2,128,512]{3,2,1,0:T(8,128)(2,1)S(1)} %get-tuple-element.34), channel_id=1, source_target_pairs={{0,2},{1,7},{2,0},{3,5},{4,6},{5,3},{6,4},{7,1},{8,10},{9,15},{10,... | collective-permute-start | bytes 786440 | tf_op jit(solution)/shard_map/ppermute | solution.py:30
  12.8 2.7 %collective-permute-start.2 = (bf16[1,2,128,512]{3,2,1,0:T(8,128)(2,1)S(1)}, bf16[1,2,128,512]{3,2,1,0:T(8,128)(2,1)S(1)}, u32[]{:S(2)}, u32[]{:S(2)}) collective-permute-start(bf16[1,2,128,512]{3,2,1,0:T(8,128)(2,1)S(1)} %get-tuple-element.35), channel_id=1, source_target_pairs={{0,16},{1,49},{2,18},{3,51},{4,20},{5,53},{6,22},{7,55},{8,24},{9,... | collective-permute-start | bytes 786440 | tf_op jit(solution)/shard_map/ppermute | solution.py:30
  15.5 3.3 %shard_map.47 = (bf16[2048,256]{1,0:T(8,128)(2,1)S(1)}, bf16[2048,256]{1,0:T(8,128)(2,1)S(1)}) custom-call(s32[32]{0:T(128)S(1)} %dynamic-slice_bitcast_fusion.table, f32[8192,256]{1,0:T(8,128)} %master.3), custom_call_target="tpu_custom_call" | custom-call | flops 6291456 | bytes 6291456 | tf_op jit(solution)/shard_map/pallas_call | solution.py:122
  18.9 0.5 collective-permute-start.6
  19.5 0.1 collective-permute-start.3
  19.6 0.2 collective-permute-start.4
  19.8 0.3 collective-permute-start.8
  20.1 7.8 %collective-permute-done.3 = bf16[2,2,128,512]{3,2,1,0:T(8,128)(2,1)S(1)} collective-permute-done((bf16[2,2,128,512]{3,2,1,0:T(8,128)(2,1)S(1)}, bf16[2,2,128,512]{3,2,1,0:T(8,128)(2,1)S(1)}, u32[]{:S(2)}, u32[]{:S(2)}) %collective-permute-start.3) | collective-permute-done | bytes 524320 | tf_op jit(solution)/shard_map/ppermute | solution.py:30
  27.9 0.1 pad_maximum_fusion.refs_0_
  28.0 0.1 pad_maximum_fusion.1.refs_0_
  28.1 2.6 %collective-permute-start.10 = (bf16[4,2,128,512]{3,2,1,0:T(8,128)(2,1)S(1)}, bf16[4,2,128,512]{3,2,1,0:T(8,128)(2,1)S(1)}, u32[]{:S(2)}, u32[]{:S(2)}) collective-permute-start(bf16[4,2,128,512]{3,2,1,0:T(8,128)(2,1)S(1)} %pad_maximum_fusion.refs_0_), channel_id=1, source_target_pairs={{0,16},{1,49},{2,18},{3,51},{4,20},{5,53},{6,22},{7,55},{8,24},{9,... | collective-permute-start | bytes 3145736 | tf_op jit(solution)/shard_map/ppermute | solution.py:30
  30.7 1.0 collective-permute-start.7
  31.7 8.0 %collective-permute-done.8.far = bf16[2048,256]{1,0:T(8,128)(2,1)S(1)} collective-permute-done((bf16[2048,256]{1,0:T(8,128)(2,1)S(1)}, bf16[2048,256]{1,0:T(8,128)(2,1)S(1)}, u32[]{:S(2)}, u32[]{:S(2)}) %collective-permute-start.8) | collective-permute-done | bytes 1048608 | tf_op jit(solution)/shard_map/ppermute | solution.py:30
  39.8 3.3 %collective-permute-done.10.refs_1_ = bf16[4,2,128,512]{3,2,1,0:T(8,128)(2,1)S(1)} collective-permute-done((bf16[4,2,128,512]{3,2,1,0:T(8,128)(2,1)S(1)}, bf16[4,2,128,512]{3,2,1,0:T(8,128)(2,1)S(1)}, u32[]{:S(2)}, u32[]{:S(2)}) %collective-permute-start.10) | collective-permute-done | bytes 1048608 | tf_op jit(solution)/shard_map/ppermute | solution.py:30
  43.1 2.5 %collective-permute-done.7.refs_1_ = bf16[4,2,128,512]{3,2,1,0:T(8,128)(2,1)S(1)} collective-permute-done((bf16[4,2,128,512]{3,2,1,0:T(8,128)(2,1)S(1)}, bf16[4,2,128,512]{3,2,1,0:T(8,128)(2,1)S(1)}, u32[]{:S(2)}, u32[]{:S(2)}) %collective-permute-start.7) | collective-permute-done | bytes 1048608 | tf_op jit(solution)/shard_map/ppermute | solution.py:30
  45.6 0.4 collective-permute-start.9
  46.0 0.3 collective-permute-start.12
  46.3 1.0 collective-permute-start.13
  47.3 1.5 collective-permute-start.25
  48.8 10.8 %collective-permute-done.9.refs_3_ = bf16[4,2,128,512]{3,2,1,0:T(8,128)(2,1)S(1)} collective-permute-done((bf16[4,2,128,512]{3,2,1,0:T(8,128)(2,1)S(1)}, bf16[4,2,128,512]{3,2,1,0:T(8,128)(2,1)S(1)}, u32[]{:S(2)}, u32[]{:S(2)}) %collective-permute-start.9) | collective-permute-done | bytes 1048608 | tf_op jit(solution)/shard_map/ppermute | solution.py:30
  59.5 0.4 collective-permute-done.11.refs_3_
  60.0 5.9 %collective-permute-done.12.cross = bf16[2048,256]{1,0:T(8,128)(2,1)S(1)} collective-permute-done((bf16[2048,256]{1,0:T(8,128)(2,1)S(1)}, bf16[2048,256]{1,0:T(8,128)(2,1)S(1)}, u32[]{:S(2)}, u32[]{:S(2)}) %collective-permute-start.12) | collective-permute-done | bytes 1048608 | tf_op jit(solution)/shard_map/ppermute | solution.py:30
  65.9 4.9 %collective-permute-done.13.refs_2_ = bf16[4,2,128,512]{3,2,1,0:T(8,128)(2,1)S(1)} collective-permute-done((bf16[4,2,128,512]{3,2,1,0:T(8,128)(2,1)S(1)}, bf16[4,2,128,512]{3,2,1,0:T(8,128)(2,1)S(1)}, u32[]{:S(2)}, u32[]{:S(2)}) %collective-permute-start.13) | collective-permute-done | bytes 1048608 | tf_op jit(solution)/shard_map/ppermute | solution.py:30
  70.8 3.3 %shard_map.49 = bf16[4,128,1024]{2,1,0:T(8,128)(2,1)S(1)} custom-call(s32[32]{0:T(128)S(1)} %dynamic-slice_bitcast_fusion.table, bf16[2048,256]{1,0:T(8,128)(2,1)S(1)} %get-tuple-element.47.mine, bf16[2048,256]{1,0:T(8,128)(2,1)S(1)} %collective-permute-done.5.near, bf16[2048,256]{1,0:T(8,128)(2,1)S(1)} %collective-permute-done.8.far, ...), custom_call_target="tpu_custom_call" | custom-call | flops 2147483648 | bytes 8388608 | tf_op jit(solution)/shard_map/pallas_call | solution.py:165
  74.0 4.0 %collective-permute-start.14 = (bf16[4,128,1024]{2,1,0:T(8,128)(2,1)S(1)}, bf16[4,128,1024]{2,1,0:T(8,128)(2,1)S(1)}, u32[]{:S(2)}, u32[]{:S(2)}) collective-permute-start(bf16[4,128,1024]{2,1,0:T(8,128)(2,1)S(1)} %shard_map.49), channel_id=1, source_target_pairs={{0,1},{1,0},{2,3},{3,2},{4,5},{5,4},{6,7},{7,6},{8,9},{9,8},{10,11... | collective-permute-start | bytes 3145736 | tf_op jit(solution)/shard_map/ppermute | solution.py:30
  78.1 3.3 %shard_map.52 = bf16[4,128,1024]{2,1,0:T(8,128)(2,1)S(1)} custom-call(s32[32]{0:T(128)S(1)} %dynamic-slice_bitcast_fusion.table, bf16[2048,256]{1,0:T(8,128)(2,1)S(1)} %get-tuple-element.47.mine, bf16[2048,256]{1,0:T(8,128)(2,1)S(1)} %collective-permute-done.5.near, bf16[2048,256]{1,0:T(8,128)(2,1)S(1)} %collective-permute-done.8.far, ...), custom_call_target="tpu_custom_call" | custom-call | flops 2147483648 | bytes 8388608 | tf_op jit(solution)/shard_map/pallas_call | solution.py:165
  81.4 0.3 collective-permute-start.26
  81.6 3.3 %shard_map.48 = f32[4,128,1024]{2,1,0:T(8,128)S(1)} custom-call(s32[32]{0:T(128)S(1)} %dynamic-slice_bitcast_fusion.table, bf16[2048,256]{1,0:T(8,128)(2,1)S(1)} %get-tuple-element.47.mine, bf16[2048,256]{1,0:T(8,128)(2,1)S(1)} %collective-permute-done.5.near, bf16[2048,256]{1,0:T(8,128)(2,1)S(1)} %collective-permute-done.8.far, ...), custom_call_target="tpu_custom_call" | custom-call | flops 2147483648 | bytes 8388608 | tf_op jit(solution)/shard_map/pallas_call | solution.py:165
  84.9 0.4 convert_add_fusion.1
  85.5 0.3 collective-permute-start.15
  85.8 3.3 %shard_map.51 = f32[4,128,1024]{2,1,0:T(8,128)S(1)} custom-call(s32[32]{0:T(128)S(1)} %dynamic-slice_bitcast_fusion.table, bf16[2048,256]{1,0:T(8,128)(2,1)S(1)} %get-tuple-element.47.mine, bf16[2048,256]{1,0:T(8,128)(2,1)S(1)} %collective-permute-done.5.near, bf16[2048,256]{1,0:T(8,128)(2,1)S(1)} %collective-permute-done.8.far, ...), custom_call_target="tpu_custom_call" | custom-call | flops 2147483648 | bytes 8388608 | tf_op jit(solution)/shard_map/pallas_call | solution.py:165
  89.1 0.3 convert_add_fusion
  89.5 1.3 collective-permute-start.27
  90.8 7.8 %collective-permute-done.15 = bf16[4,128,512]{2,1,0:T(8,128)(2,1)S(1)} collective-permute-done((bf16[4,128,512]{2,1,0:T(8,128)(2,1)S(1)}, bf16[4,128,512]{2,1,0:T(8,128)(2,1)S(1)}, u32[]{:S(2)}, u32[]{:S(2)}) %collective-permute-start.15) | collective-permute-done | bytes 524320 | tf_op jit(solution)/shard_map/ppermute | solution.py:30
  98.5 0.2 fusion.1
  98.8 3.8 %collective-permute-start.16 = (bf16[128,512]{1,0:T(8,128)(2,1)S(1)}, bf16[128,512]{1,0:T(8,128)(2,1)S(1)}, u32[]{:S(2)}, u32[]{:S(2)}) collective-permute-start(bf16[128,512]{1,0:T(8,128)(2,1)S(1)} %get-tuple-element.63), channel_id=1, source_target_pairs={{0,0},{1,65},{2,2},{3,67},{4,4},{5,69},{6,6},{7,71},{8,8},{9,73},{... | collective-permute-start | bytes 393224 | tf_op jit(solution)/shard_map/ppermute | solution.py:30
  102.5 4.0 %collective-permute-start.19 = (bf16[128,512]{1,0:T(8,128)(2,1)S(1)}, bf16[128,512]{1,0:T(8,128)(2,1)S(1)}, u32[]{:S(2)}, u32[]{:S(2)}) collective-permute-start(bf16[128,512]{1,0:T(8,128)(2,1)S(1)} %get-tuple-element.64), channel_id=1, source_target_pairs={{0,48},{1,113},{2,50},{3,115},{4,52},{5,117},{6,54},{7,119},{8,56}... | collective-permute-start | bytes 393224 | tf_op jit(solution)/shard_map/ppermute | solution.py:30
  106.5 2.0 %collective-permute-start.18 = (bf16[128,512]{1,0:T(8,128)(2,1)S(1)}, bf16[128,512]{1,0:T(8,128)(2,1)S(1)}, u32[]{:S(2)}, u32[]{:S(2)}) collective-permute-start(bf16[128,512]{1,0:T(8,128)(2,1)S(1)} %get-tuple-element.65), channel_id=1, source_target_pairs={{0,32},{1,97},{2,34},{3,99},{4,36},{5,101},{6,38},{7,103},{8,40},{... | collective-permute-start | bytes 393224 | tf_op jit(solution)/shard_map/ppermute | solution.py:30
  108.5 2.7 %collective-permute-start.17 = (bf16[128,512]{1,0:T(8,128)(2,1)S(1)}, bf16[128,512]{1,0:T(8,128)(2,1)S(1)}, u32[]{:S(2)}, u32[]{:S(2)}) collective-permute-start(bf16[128,512]{1,0:T(8,128)(2,1)S(1)} %get-tuple-element.66), channel_id=1, source_target_pairs={{0,16},{1,81},{2,18},{3,83},{4,20},{5,85},{6,22},{7,87},{8,24},{9,... | collective-permute-start | bytes 393224 | tf_op jit(solution)/shard_map/ppermute | solution.py:30
  111.2 0.2 fusion
  111.4 3.8 %collective-permute-start.28 = (bf16[128,512]{1,0:T(8,128)(2,1)S(1)}, bf16[128,512]{1,0:T(8,128)(2,1)S(1)}, u32[]{:S(2)}, u32[]{:S(2)}) collective-permute-start(bf16[128,512]{1,0:T(8,128)(2,1)S(1)} %get-tuple-element.59), channel_id=1, source_target_pairs={{0,0},{1,65},{2,2},{3,67},{4,4},{5,69},{6,6},{7,71},{8,8},{9,73},{... | collective-permute-start | bytes 393224 | tf_op jit(solution)/shard_map/ppermute | solution.py:30
  115.2 2.5 %collective-permute-start.31 = (bf16[128,512]{1,0:T(8,128)(2,1)S(1)}, bf16[128,512]{1,0:T(8,128)(2,1)S(1)}, u32[]{:S(2)}, u32[]{:S(2)}) collective-permute-start(bf16[128,512]{1,0:T(8,128)(2,1)S(1)} %get-tuple-element.60), channel_id=1, source_target_pairs={{0,48},{1,113},{2,50},{3,115},{4,52},{5,117},{6,54},{7,119},{8,56}... | collective-permute-start | bytes 393224 | tf_op jit(solution)/shard_map/ppermute | solution.py:30
  117.8 2.1 %collective-permute-start.30 = (bf16[128,512]{1,0:T(8,128)(2,1)S(1)}, bf16[128,512]{1,0:T(8,128)(2,1)S(1)}, u32[]{:S(2)}, u32[]{:S(2)}) collective-permute-start(bf16[128,512]{1,0:T(8,128)(2,1)S(1)} %get-tuple-element.61), channel_id=1, source_target_pairs={{0,32},{1,97},{2,34},{3,99},{4,36},{5,101},{6,38},{7,103},{8,40},{... | collective-permute-start | bytes 393224 | tf_op jit(solution)/shard_map/ppermute | solution.py:30
  119.8 1.3 collective-permute-done.18
  121.2 1.3 collective-permute-start.29
  122.7 3.1 %collective-permute-done.30 = bf16[128,512]{1,0:T(8,128)(2,1)S(1)} collective-permute-done((bf16[128,512]{1,0:T(8,128)(2,1)S(1)}, bf16[128,512]{1,0:T(8,128)(2,1)S(1)}, u32[]{:S(2)}, u32[]{:S(2)}) %collective-permute-start.30) | collective-permute-done | bytes 131104 | tf_op jit(solution)/shard_map/ppermute | solution.py:30
  125.8 2.8 %collective-permute-done.29 = bf16[128,512]{1,0:T(8,128)(2,1)S(1)} collective-permute-done((bf16[128,512]{1,0:T(8,128)(2,1)S(1)}, bf16[128,512]{1,0:T(8,128)(2,1)S(1)}, u32[]{:S(2)}, u32[]{:S(2)}) %collective-permute-start.29) | collective-permute-done | bytes 131104 | tf_op jit(solution)/shard_map/ppermute | solution.py:30
  128.8 0.7 shard_map.50
  129.4 3.5 %collective-permute-start.21 = (bf16[128,512]{1,0:T(8,128)(2,1)S(1)}, bf16[128,512]{1,0:T(8,128)(2,1)S(1)}, u32[]{:S(2)}, u32[]{:S(2)}) collective-permute-start(bf16[128,512]{1,0:T(8,128)(2,1)S(1)} %get-tuple-element.50), channel_id=1, source_target_pairs={{0,0},{1,8},{2,2},{3,10},{4,4},{5,12},{6,6},{7,14},{8,9},{9,1},{10... | collective-permute-start | bytes 393224 | tf_op jit(solution)/shard_map/ppermute | solution.py:30
  133.1 0.6 collective-permute-start.23
  133.6 1.8 %collective-permute-start.24 = (bf16[128,512]{1,0:T(8,128)(2,1)S(1)}, bf16[128,512]{1,0:T(8,128)(2,1)S(1)}, u32[]{:S(2)}, u32[]{:S(2)}) collective-permute-start(bf16[128,512]{1,0:T(8,128)(2,1)S(1)} %get-tuple-element.53), channel_id=1, source_target_pairs={{0,6},{1,14},{2,0},{3,8},{4,2},{5,10},{6,4},{7,12},{8,15},{9,7},{1... | collective-permute-start | bytes 393224 | tf_op jit(solution)/shard_map/ppermute | solution.py:30
  135.4 0.7 shard_map.53
  136.1 3.7 %collective-permute-start.33 = (bf16[128,512]{1,0:T(8,128)(2,1)S(1)}, bf16[128,512]{1,0:T(8,128)(2,1)S(1)}, u32[]{:S(2)}, u32[]{:S(2)}) collective-permute-start(bf16[128,512]{1,0:T(8,128)(2,1)S(1)} %get-tuple-element.55), channel_id=1, source_target_pairs={{0,0},{1,8},{2,2},{3,10},{4,4},{5,12},{6,6},{7,14},{8,9},{9,1},{10... | collective-permute-start | bytes 393224 | tf_op jit(solution)/shard_map/ppermute | solution.py:30
  139.8 0.6 collective-permute-start.34
  140.4 1.7 %collective-permute-done.22.refs_1_ = bf16[128,512]{1,0:T(8,128)(2,1)S(1)} collective-permute-done((bf16[128,512]{1,0:T(8,128)(2,1)S(1)}, bf16[128,512]{1,0:T(8,128)(2,1)S(1)}, u32[]{:S(2)}, u32[]{:S(2)}) %collective-permute-start.22) | collective-permute-done | bytes 131104 | tf_op jit(solution)/shard_map/ppermute | solution.py:30
  142.1 3.3 %collective-permute-start.36 = (bf16[128,512]{1,0:T(8,128)(2,1)S(1)}, bf16[128,512]{1,0:T(8,128)(2,1)S(1)}, u32[]{:S(2)}, u32[]{:S(2)}) collective-permute-start(bf16[128,512]{1,0:T(8,128)(2,1)S(1)} %get-tuple-element.58), channel_id=1, source_target_pairs={{0,6},{1,14},{2,0},{3,8},{4,2},{5,10},{6,4},{7,12},{8,15},{9,7},{1... | collective-permute-start | bytes 393224 | tf_op jit(solution)/shard_map/ppermute | solution.py:30
  145.4 2.1 %collective-permute-done.34.refs_5_ = bf16[128,512]{1,0:T(8,128)(2,1)S(1)} collective-permute-done((bf16[128,512]{1,0:T(8,128)(2,1)S(1)}, bf16[128,512]{1,0:T(8,128)(2,1)S(1)}, u32[]{:S(2)}, u32[]{:S(2)}) %collective-permute-start.34) | collective-permute-done | bytes 131104 | tf_op jit(solution)/shard_map/ppermute | solution.py:30
  147.5 1.7 %collective-permute-done.35.refs_6_ = bf16[128,512]{1,0:T(8,128)(2,1)S(1)} collective-permute-done((bf16[128,512]{1,0:T(8,128)(2,1)S(1)}, bf16[128,512]{1,0:T(8,128)(2,1)S(1)}, u32[]{:S(2)}, u32[]{:S(2)}) %collective-permute-start.35) | collective-permute-done | bytes 131104 | tf_op jit(solution)/shard_map/ppermute | solution.py:30
  149.2 1.0 collective-permute-done.36.refs_7_
  150.2 1.6 %shard_map.54 = bf16[256,2048]{1,0:T(8,128)(2,1)} custom-call(s32[32]{0:T(128)S(1)} %dynamic-slice_bitcast_fusion.table, bf16[128,512]{1,0:T(8,128)(2,1)S(1)} %collective-permute-done.21.refs_0_, bf16[128,512]{1,0:T(8,128)(2,1)S(1)} %collective-permute-done.22.refs_1_, bf16[128,512]{1,0:T(8,128)(2,1)S(1)} %collective-permute-done.23.refs_2_, ...), custom_call_target="tpu_custom_call" | custom-call | bytes 2097152 | tf_op jit(solution)/shard_map/pallas_call | solution.py:207
  (39 shorter events, 0.9 us)
Async XLA Ops:
  0.0 8.9 %collective-permute-start = (bf16[256,512]{1,0:T(8,128)(2,1)}, bf16[256,512]{1,0:T(8,128)(2,1)S(1)}, u32[]{:S(2)}, u32[]{:S(2)}) collective-permute-start(bf16[256,512]{1,0:T(8,128)(2,1)} %param.5), channel_id=1, source_target_pairs={{0,64},{1,65},{2,66},{3,67},{4,68},{5,69},{6,70},{7,71},{8,72},{9,... | collective-permute-start | bytes 786440 | tf_op jit(solution)/shard_map/ppermute | solution.py:30
  2.5 6.4 %copy-start.1 = (bf16[256,512]{1,0:T(8,128)(2,1)S(1)}, bf16[256,512]{1,0:T(8,128)(2,1)}, u32[]{:S(2)}) copy-start(bf16[256,512]{1,0:T(8,128)(2,1)} %param.5) | copy-start | bytes 786436
  8.9 10.4 %collective-permute-start.1 = (bf16[1,2,128,512]{3,2,1,0:T(8,128)(2,1)S(1)}, bf16[1,2,128,512]{3,2,1,0:T(8,128)(2,1)S(1)}, u32[]{:S(2)}, u32[]{:S(2)}) collective-permute-start(bf16[1,2,128,512]{3,2,1,0:T(8,128)(2,1)S(1)} %get-tuple-element.34), channel_id=1, source_target_pairs={{0,2},{1,7},{2,0},{3,5},{4,6},{5,3},{6,4},{7,1},{8,10},{9,15},{10,... | collective-permute-start | bytes 786440 | tf_op jit(solution)/shard_map/ppermute | solution.py:30
  12.8 6.7 %collective-permute-start.2 = (bf16[1,2,128,512]{3,2,1,0:T(8,128)(2,1)S(1)}, bf16[1,2,128,512]{3,2,1,0:T(8,128)(2,1)S(1)}, u32[]{:S(2)}, u32[]{:S(2)}) collective-permute-start(bf16[1,2,128,512]{3,2,1,0:T(8,128)(2,1)S(1)} %get-tuple-element.35), channel_id=1, source_target_pairs={{0,16},{1,49},{2,18},{3,51},{4,20},{5,53},{6,22},{7,55},{8,24},{9,... | collective-permute-start | bytes 786440 | tf_op jit(solution)/shard_map/ppermute | solution.py:30
  18.8 9.3 %collective-permute-start.5 = (bf16[2048,256]{1,0:T(8,128)(2,1)S(1)}, bf16[2048,256]{1,0:T(8,128)(2,1)S(1)}, u32[]{:S(2)}, u32[]{:S(2)}) collective-permute-start(bf16[2048,256]{1,0:T(8,128)(2,1)S(1)} %get-tuple-element.40), channel_id=1, source_target_pairs={{0,1},{1,0},{2,3},{3,2},{4,5},{5,4},{6,7},{7,6},{8,9},{9,8},{10,11... | collective-permute-start | bytes 3145736 | tf_op jit(solution)/shard_map/ppermute | solution.py:30
  18.9 9.3 %collective-permute-start.6 = (bf16[2048,256]{1,0:T(8,128)(2,1)S(1)}, bf16[2048,256]{1,0:T(8,128)(2,1)S(1)}, u32[]{:S(2)}, u32[]{:S(2)}) collective-permute-start(bf16[2048,256]{1,0:T(8,128)(2,1)S(1)} %get-tuple-element.41), channel_id=1, source_target_pairs={{0,1},{1,0},{2,3},{3,2},{4,5},{5,4},{6,7},{7,6},{8,9},{9,8},{10,11... | collective-permute-start | bytes 3145736 | tf_op jit(solution)/shard_map/ppermute | solution.py:30
  19.5 8.4 %collective-permute-start.3 = (bf16[2,2,128,512]{3,2,1,0:T(8,128)(2,1)S(1)}, bf16[2,2,128,512]{3,2,1,0:T(8,128)(2,1)S(1)}, u32[]{:S(2)}, u32[]{:S(2)}) collective-permute-start(bf16[2,2,128,512]{3,2,1,0:T(8,128)(2,1)S(1)} %pad_maximum_fusion.2), channel_id=1, source_target_pairs={{0,6},{1,3},{2,4},{3,1},{4,2},{5,7},{6,0},{7,5},{8,14},{9,11},{10,... | collective-permute-start | bytes 1572872 | tf_op jit(solution)/shard_map/ppermute | solution.py:30
  19.6 8.4 %collective-permute-start.4 = (bf16[2,2,128,512]{3,2,1,0:T(8,128)(2,1)S(1)}, bf16[2,2,128,512]{3,2,1,0:T(8,128)(2,1)S(1)}, u32[]{:S(2)}, u32[]{:S(2)}) collective-permute-start(bf16[2,2,128,512]{3,2,1,0:T(8,128)(2,1)S(1)} %pad_maximum_fusion.3), channel_id=1, source_target_pairs={{0,48},{1,17},{2,50},{3,19},{4,52},{5,21},{6,54},{7,23},{8,56},{9,... | collective-permute-start | bytes 1572872 | tf_op jit(solution)/shard_map/ppermute | solution.py:30
  19.8 19.9 %collective-permute-start.8 = (bf16[2048,256]{1,0:T(8,128)(2,1)S(1)}, bf16[2048,256]{1,0:T(8,128)(2,1)S(1)}, u32[]{:S(2)}, u32[]{:S(2)}) collective-permute-start(bf16[2048,256]{1,0:T(8,128)(2,1)S(1)} %get-tuple-element.32), channel_id=1, source_target_pairs={{0,8},{1,9},{2,10},{3,11},{4,12},{5,13},{6,14},{7,15},{8,0},{9,1},... | collective-permute-start | bytes 3145736 | tf_op jit(solution)/shard_map/ppermute | solution.py:30
  28.1 14.9 %collective-permute-start.10 = (bf16[4,2,128,512]{3,2,1,0:T(8,128)(2,1)S(1)}, bf16[4,2,128,512]{3,2,1,0:T(8,128)(2,1)S(1)}, u32[]{:S(2)}, u32[]{:S(2)}) collective-permute-start(bf16[4,2,128,512]{3,2,1,0:T(8,128)(2,1)S(1)} %pad_maximum_fusion.refs_0_), channel_id=1, source_target_pairs={{0,16},{1,49},{2,18},{3,51},{4,20},{5,53},{6,22},{7,55},{8,24},{9,... | collective-permute-start | bytes 3145736 | tf_op jit(solution)/shard_map/ppermute | solution.py:30
  30.7 14.9 %collective-permute-start.7 = (bf16[4,2,128,512]{3,2,1,0:T(8,128)(2,1)S(1)}, bf16[4,2,128,512]{3,2,1,0:T(8,128)(2,1)S(1)}, u32[]{:S(2)}, u32[]{:S(2)}) collective-permute-start(bf16[4,2,128,512]{3,2,1,0:T(8,128)(2,1)S(1)} %pad_maximum_fusion.1.refs_0_), channel_id=1, source_target_pairs={{0,2},{1,7},{2,0},{3,5},{4,6},{5,3},{6,4},{7,1},{8,10},{9,15},{10,... | collective-permute-start | bytes 3145736 | tf_op jit(solution)/shard_map/ppermute | solution.py:30
  45.6 13.9 %collective-permute-start.9 = (bf16[4,2,128,512]{3,2,1,0:T(8,128)(2,1)S(1)}, bf16[4,2,128,512]{3,2,1,0:T(8,128)(2,1)S(1)}, u32[]{:S(2)}, u32[]{:S(2)}) collective-permute-start(bf16[4,2,128,512]{3,2,1,0:T(8,128)(2,1)S(1)} %collective-permute-done.7.refs_1_), channel_id=1, source_target_pairs={{0,6},{1,3},{2,4},{3,1},{4,2},{5,7},{6,0},{7,5},{8,14},{9,11},{10,... | collective-permute-start | bytes 3145736 | tf_op jit(solution)/shard_map/ppermute | solution.py:30
  46.0 13.9 %collective-permute-start.11 = (bf16[4,2,128,512]{3,2,1,0:T(8,128)(2,1)S(1)}, bf16[4,2,128,512]{3,2,1,0:T(8,128)(2,1)S(1)}, u32[]{:S(2)}, u32[]{:S(2)}) collective-permute-start(bf16[4,2,128,512]{3,2,1,0:T(8,128)(2,1)S(1)} %collective-permute-done.10.refs_1_), channel_id=1, source_target_pairs={{0,48},{1,17},{2,50},{3,19},{4,52},{5,21},{6,54},{7,23},{8,56},{9,... | collective-permute-start | bytes 3145736 | tf_op jit(solution)/shard_map/ppermute | solution.py:30
  46.0 19.9 %collective-permute-start.12 = (bf16[2048,256]{1,0:T(8,128)(2,1)S(1)}, bf16[2048,256]{1,0:T(8,128)(2,1)S(1)}, u32[]{:S(2)}, u32[]{:S(2)}) collective-permute-start(bf16[2048,256]{1,0:T(8,128)(2,1)S(1)} %collective-permute-done.6), channel_id=1, source_target_pairs={{0,8},{1,9},{2,10},{3,11},{4,12},{5,13},{6,14},{7,15},{8,0},{9,1},... | collective-permute-start | bytes 3145736 | tf_op jit(solution)/shard_map/ppermute | solution.py:30
  46.3 24.5 %collective-permute-start.13 = (bf16[4,2,128,512]{3,2,1,0:T(8,128)(2,1)S(1)}, bf16[4,2,128,512]{3,2,1,0:T(8,128)(2,1)S(1)}, u32[]{:S(2)}, u32[]{:S(2)}) collective-permute-start(bf16[4,2,128,512]{3,2,1,0:T(8,128)(2,1)S(1)} %pad_maximum_fusion.1.refs_0_), channel_id=1, source_target_pairs={{0,6},{1,3},{2,4},{3,1},{4,2},{5,7},{6,0},{7,5},{8,14},{9,11},{10,... | collective-permute-start | bytes 3145736 | tf_op jit(solution)/shard_map/ppermute | solution.py:30
  47.3 30.8 %collective-permute-start.25 = (bf16[4,2,128,512]{3,2,1,0:T(8,128)(2,1)S(1)}, bf16[4,2,128,512]{3,2,1,0:T(8,128)(2,1)S(1)}, u32[]{:S(2)}, u32[]{:S(2)}) collective-permute-start(bf16[4,2,128,512]{3,2,1,0:T(8,128)(2,1)S(1)} %pad_maximum_fusion.refs_0_), channel_id=1, source_target_pairs={{0,48},{1,17},{2,50},{3,19},{4,52},{5,21},{6,54},{7,23},{8,56},{9,... | collective-permute-start | bytes 3145736 | tf_op jit(solution)/shard_map/ppermute | solution.py:30
  74.0 10.9 %collective-permute-start.14 = (bf16[4,128,1024]{2,1,0:T(8,128)(2,1)S(1)}, bf16[4,128,1024]{2,1,0:T(8,128)(2,1)S(1)}, u32[]{:S(2)}, u32[]{:S(2)}) collective-permute-start(bf16[4,128,1024]{2,1,0:T(8,128)(2,1)S(1)} %shard_map.49), channel_id=1, source_target_pairs={{0,1},{1,0},{2,3},{3,2},{4,5},{5,4},{6,7},{7,6},{8,9},{9,8},{10,11... | collective-permute-start | bytes 3145736 | tf_op jit(solution)/shard_map/ppermute | solution.py:30
  81.4 7.7 %collective-permute-start.26 = (bf16[4,128,1024]{2,1,0:T(8,128)(2,1)S(1)}, bf16[4,128,1024]{2,1,0:T(8,128)(2,1)S(1)}, u32[]{:S(2)}, u32[]{:S(2)}) collective-permute-start(bf16[4,128,1024]{2,1,0:T(8,128)(2,1)S(1)} %shard_map.52), channel_id=1, source_target_pairs={{0,1},{1,0},{2,3},{3,2},{4,5},{5,4},{6,7},{7,6},{8,9},{9,8},{10,11... | collective-permute-start | bytes 3145736 | tf_op jit(solution)/shard_map/ppermute | solution.py:30
  85.5 13.1 %collective-permute-start.15 = (bf16[4,128,512]{2,1,0:T(8,128)(2,1)S(1)}, bf16[4,128,512]{2,1,0:T(8,128)(2,1)S(1)}, u32[]{:S(2)}, u32[]{:S(2)}) collective-permute-start(bf16[4,128,512]{2,1,0:T(8,128)(2,1)S(1)} %slice.97), channel_id=1, source_target_pairs={{0,8},{1,9},{2,10},{3,11},{4,12},{5,13},{6,14},{7,15},{8,0},{9,1},... | collective-permute-start | bytes 1572872 | tf_op jit(solution)/shard_map/ppermute | solution.py:30
  89.5 21.8 %collective-permute-start.27 = (bf16[4,128,512]{2,1,0:T(8,128)(2,1)S(1)}, bf16[4,128,512]{2,1,0:T(8,128)(2,1)S(1)}, u32[]{:S(2)}, u32[]{:S(2)}) collective-permute-start(bf16[4,128,512]{2,1,0:T(8,128)(2,1)S(1)} %slice.96), channel_id=1, source_target_pairs={{0,8},{1,9},{2,10},{3,11},{4,12},{5,13},{6,14},{7,15},{8,0},{9,1},... | collective-permute-start | bytes 1572872 | tf_op jit(solution)/shard_map/ppermute | solution.py:30
  98.8 16.5 %collective-permute-start.16 = (bf16[128,512]{1,0:T(8,128)(2,1)S(1)}, bf16[128,512]{1,0:T(8,128)(2,1)S(1)}, u32[]{:S(2)}, u32[]{:S(2)}) collective-permute-start(bf16[128,512]{1,0:T(8,128)(2,1)S(1)} %get-tuple-element.63), channel_id=1, source_target_pairs={{0,0},{1,65},{2,2},{3,67},{4,4},{5,69},{6,6},{7,71},{8,8},{9,73},{... | collective-permute-start | bytes 393224 | tf_op jit(solution)/shard_map/ppermute | solution.py:30
  102.5 15.2 %collective-permute-start.19 = (bf16[128,512]{1,0:T(8,128)(2,1)S(1)}, bf16[128,512]{1,0:T(8,128)(2,1)S(1)}, u32[]{:S(2)}, u32[]{:S(2)}) collective-permute-start(bf16[128,512]{1,0:T(8,128)(2,1)S(1)} %get-tuple-element.64), channel_id=1, source_target_pairs={{0,48},{1,113},{2,50},{3,115},{4,52},{5,117},{6,54},{7,119},{8,56}... | collective-permute-start | bytes 393224 | tf_op jit(solution)/shard_map/ppermute | solution.py:30
  106.5 14.7 %collective-permute-start.18 = (bf16[128,512]{1,0:T(8,128)(2,1)S(1)}, bf16[128,512]{1,0:T(8,128)(2,1)S(1)}, u32[]{:S(2)}, u32[]{:S(2)}) collective-permute-start(bf16[128,512]{1,0:T(8,128)(2,1)S(1)} %get-tuple-element.65), channel_id=1, source_target_pairs={{0,32},{1,97},{2,34},{3,99},{4,36},{5,101},{6,38},{7,103},{8,40},{... | collective-permute-start | bytes 393224 | tf_op jit(solution)/shard_map/ppermute | solution.py:30
  108.5 14.0 %collective-permute-start.17 = (bf16[128,512]{1,0:T(8,128)(2,1)S(1)}, bf16[128,512]{1,0:T(8,128)(2,1)S(1)}, u32[]{:S(2)}, u32[]{:S(2)}) collective-permute-start(bf16[128,512]{1,0:T(8,128)(2,1)S(1)} %get-tuple-element.66), channel_id=1, source_target_pairs={{0,16},{1,81},{2,18},{3,83},{4,20},{5,85},{6,22},{7,87},{8,24},{9,... | collective-permute-start | bytes 393224 | tf_op jit(solution)/shard_map/ppermute | solution.py:30
  111.4 17.4 %copy-start = (s32[8]{0:T(128)S(1)}, s32[8]{0:T(128)}, u32[]{:S(2)}) copy-start(s32[8]{0:T(128)} %owner.3) | copy-start | bytes 100
  111.4 11.2 %collective-permute-start.28 = (bf16[128,512]{1,0:T(8,128)(2,1)S(1)}, bf16[128,512]{1,0:T(8,128)(2,1)S(1)}, u32[]{:S(2)}, u32[]{:S(2)}) collective-permute-start(bf16[128,512]{1,0:T(8,128)(2,1)S(1)} %get-tuple-element.59), channel_id=1, source_target_pairs={{0,0},{1,65},{2,2},{3,67},{4,4},{5,69},{6,6},{7,71},{8,8},{9,73},{... | collective-permute-start | bytes 393224 | tf_op jit(solution)/shard_map/ppermute | solution.py:30
  115.2 7.4 %collective-permute-start.31 = (bf16[128,512]{1,0:T(8,128)(2,1)S(1)}, bf16[128,512]{1,0:T(8,128)(2,1)S(1)}, u32[]{:S(2)}, u32[]{:S(2)}) collective-permute-start(bf16[128,512]{1,0:T(8,128)(2,1)S(1)} %get-tuple-element.60), channel_id=1, source_target_pairs={{0,48},{1,113},{2,50},{3,115},{4,52},{5,117},{6,54},{7,119},{8,56}... | collective-permute-start | bytes 393224 | tf_op jit(solution)/shard_map/ppermute | solution.py:30
  117.8 8.0 %collective-permute-start.30 = (bf16[128,512]{1,0:T(8,128)(2,1)S(1)}, bf16[128,512]{1,0:T(8,128)(2,1)S(1)}, u32[]{:S(2)}, u32[]{:S(2)}) collective-permute-start(bf16[128,512]{1,0:T(8,128)(2,1)S(1)} %get-tuple-element.61), channel_id=1, source_target_pairs={{0,32},{1,97},{2,34},{3,99},{4,36},{5,101},{6,38},{7,103},{8,40},{... | collective-permute-start | bytes 393224 | tf_op jit(solution)/shard_map/ppermute | solution.py:30
  121.2 7.4 %collective-permute-start.29 = (bf16[128,512]{1,0:T(8,128)(2,1)S(1)}, bf16[128,512]{1,0:T(8,128)(2,1)S(1)}, u32[]{:S(2)}, u32[]{:S(2)}) collective-permute-start(bf16[128,512]{1,0:T(8,128)(2,1)S(1)} %get-tuple-element.62), channel_id=1, source_target_pairs={{0,16},{1,81},{2,18},{3,83},{4,20},{5,85},{6,22},{7,87},{8,24},{9,... | collective-permute-start | bytes 393224 | tf_op jit(solution)/shard_map/ppermute | solution.py:30
  122.5 6.2 %collective-permute-start.20 = (bf16[4,128,512]{2,1,0:T(8,128)(2,1)S(1)}, bf16[4,128,512]{2,1,0:T(8,128)(2,1)S(1)}, u32[]{:S(2)}, u32[]{:S(2)}) collective-permute-start(bf16[4,128,512]{2,1,0:T(8,128)(2,1)S(1)} %pad_maximum_fusion.4.own), channel_id=1, source_target_pairs={{0,1},{1,0},{2,3},{3,2},{4,5},{5,4},{6,7},{7,6},{8,9},{9,8},{10,11... | collective-permute-start | bytes 1572872 | tf_op jit(solution)/shard_map/ppermute | solution.py:30
  128.7 6.8 %collective-permute-start.32 = (bf16[4,128,512]{2,1,0:T(8,128)(2,1)S(1)}, bf16[4,128,512]{2,1,0:T(8,128)(2,1)S(1)}, u32[]{:S(2)}, u32[]{:S(2)}) collective-permute-start(bf16[4,128,512]{2,1,0:T(8,128)(2,1)S(1)} %pad_maximum_fusion.5.own), channel_id=1, source_target_pairs={{0,1},{1,0},{2,3},{3,2},{4,5},{5,4},{6,7},{7,6},{8,9},{9,8},{10,11... | collective-permute-start | bytes 1572872 | tf_op jit(solution)/shard_map/ppermute | solution.py:30
  129.4 10.3 %collective-permute-start.21 = (bf16[128,512]{1,0:T(8,128)(2,1)S(1)}, bf16[128,512]{1,0:T(8,128)(2,1)S(1)}, u32[]{:S(2)}, u32[]{:S(2)}) collective-permute-start(bf16[128,512]{1,0:T(8,128)(2,1)S(1)} %get-tuple-element.50), channel_id=1, source_target_pairs={{0,0},{1,8},{2,2},{3,10},{4,4},{5,12},{6,6},{7,14},{8,9},{9,1},{10... | collective-permute-start | bytes 393224 | tf_op jit(solution)/shard_map/ppermute | solution.py:30
  133.0 9.1 %collective-permute-start.22 = (bf16[128,512]{1,0:T(8,128)(2,1)S(1)}, bf16[128,512]{1,0:T(8,128)(2,1)S(1)}, u32[]{:S(2)}, u32[]{:S(2)}) collective-permute-start(bf16[128,512]{1,0:T(8,128)(2,1)S(1)} %get-tuple-element.51), channel_id=1, source_target_pairs={{0,2},{1,10},{2,4},{3,12},{4,6},{5,14},{6,0},{7,8},{8,11},{9,3},{1... | collective-permute-start | bytes 393224 | tf_op jit(solution)/shard_map/ppermute | solution.py:30
  133.1 9.1 %collective-permute-start.23 = (bf16[128,512]{1,0:T(8,128)(2,1)S(1)}, bf16[128,512]{1,0:T(8,128)(2,1)S(1)}, u32[]{:S(2)}, u32[]{:S(2)}) collective-permute-start(bf16[128,512]{1,0:T(8,128)(2,1)S(1)} %get-tuple-element.52), channel_id=1, source_target_pairs={{0,4},{1,12},{2,6},{3,14},{4,0},{5,8},{6,2},{7,10},{8,13},{9,5},{1... | collective-permute-start | bytes 393224 | tf_op jit(solution)/shard_map/ppermute | solution.py:30
  133.6 11.8 %collective-permute-start.24 = (bf16[128,512]{1,0:T(8,128)(2,1)S(1)}, bf16[128,512]{1,0:T(8,128)(2,1)S(1)}, u32[]{:S(2)}, u32[]{:S(2)}) collective-permute-start(bf16[128,512]{1,0:T(8,128)(2,1)S(1)} %get-tuple-element.53), channel_id=1, source_target_pairs={{0,6},{1,14},{2,0},{3,8},{4,2},{5,10},{6,4},{7,12},{8,15},{9,7},{1... | collective-permute-start | bytes 393224 | tf_op jit(solution)/shard_map/ppermute | solution.py:30
  136.1 9.3 %collective-permute-start.33 = (bf16[128,512]{1,0:T(8,128)(2,1)S(1)}, bf16[128,512]{1,0:T(8,128)(2,1)S(1)}, u32[]{:S(2)}, u32[]{:S(2)}) collective-permute-start(bf16[128,512]{1,0:T(8,128)(2,1)S(1)} %get-tuple-element.55), channel_id=1, source_target_pairs={{0,0},{1,8},{2,2},{3,10},{4,4},{5,12},{6,6},{7,14},{8,9},{9,1},{10... | collective-permute-start | bytes 393224 | tf_op jit(solution)/shard_map/ppermute | solution.py:30
  139.8 7.7 %collective-permute-start.34 = (bf16[128,512]{1,0:T(8,128)(2,1)S(1)}, bf16[128,512]{1,0:T(8,128)(2,1)S(1)}, u32[]{:S(2)}, u32[]{:S(2)}) collective-permute-start(bf16[128,512]{1,0:T(8,128)(2,1)S(1)} %get-tuple-element.56), channel_id=1, source_target_pairs={{0,2},{1,10},{2,4},{3,12},{4,6},{5,14},{6,0},{7,8},{8,11},{9,3},{1... | collective-permute-start | bytes 393224 | tf_op jit(solution)/shard_map/ppermute | solution.py:30
  142.1 7.1 %collective-permute-start.35 = (bf16[128,512]{1,0:T(8,128)(2,1)S(1)}, bf16[128,512]{1,0:T(8,128)(2,1)S(1)}, u32[]{:S(2)}, u32[]{:S(2)}) collective-permute-start(bf16[128,512]{1,0:T(8,128)(2,1)S(1)} %get-tuple-element.57), channel_id=1, source_target_pairs={{0,4},{1,12},{2,6},{3,14},{4,0},{5,8},{6,2},{7,10},{8,13},{9,5},{1... | collective-permute-start | bytes 393224 | tf_op jit(solution)/shard_map/ppermute | solution.py:30
  142.1 8.1 %collective-permute-start.36 = (bf16[128,512]{1,0:T(8,128)(2,1)S(1)}, bf16[128,512]{1,0:T(8,128)(2,1)S(1)}, u32[]{:S(2)}, u32[]{:S(2)}) collective-permute-start(bf16[128,512]{1,0:T(8,128)(2,1)S(1)} %get-tuple-element.58), channel_id=1, source_target_pairs={{0,6},{1,14},{2,0},{3,8},{4,2},{5,10},{6,4},{7,12},{8,15},{9,7},{1... | collective-permute-start | bytes 393224 | tf_op jit(solution)/shard_map/ppermute | solution.py:30

commit v12 on v11

--- a/solution.py
+++ b/solution.py
@@ -141,35 +141,38 @@
     return [(mine, cols(0, core)), (near, cols(0, 1 - core)), (far, cols(2 * COLS, core)), (cross, cols(2 * COLS, 1 - core))]
 
 
-def product_kernel(part, half_of, table, mine, near, far, cross, *refs):
-    slots, (out, held, sems) = refs[:4], refs[4:]
+def product_kernel(part, keeps, table, mine, near, far, cross, *refs):
+    slots, outs, (held, sems) = refs[:4], refs[4:-2], refs[-2:]
     core = table[CORE]
-    half = half_of(core)
-    for i, slot in enumerate(slots):
-        for k in range(4):
-            zs = k if part == "y" else i
-            depth = pl.ds(pl.multiple_of(table[Z_SLOT + zs] * SHARE, SHARE), SHARE)
-            to = held.at[i if part == "y" else k, :, depth]
-            pltpu.make_async_copy(slot.at[k, half], to, sems.at[i]).start()
-    for i in range(4):
-        pltpu.make_async_copy(held.at[i], held.at[i], sems.at[i]).wait()
-    acts = held[...].reshape(4 * HALF, 4 * SHARE)
-    for weight, cols in pieces(core, mine, near, far, cross):
-        got = jnp.dot(acts, weight[...], preferred_element_type=jnp.float32).reshape(4, HALF, COLS)
-        for ys in range(4):
-            out[table[Y_SLOT + ys], :, cols] = got[ys].astype(out.dtype)
-
-
-def product(part, keep, table, weights, slots):
+    for n, keep in enumerate(keeps):
+        half = core if keep else 1 - core
+        for i, slot in enumerate(slots):
+            for k in range(4):
+                zs = k if part == "y" else i
+                depth = pl.ds(pl.multiple_of(table[Z_SLOT + zs] * SHARE, SHARE), SHARE)
+                to = held.at[n, i if part == "y" else k, :, depth]
+                pltpu.make_async_copy(slot.at[k, half], to, sems.at[n]).start()
+    for n, out in enumerate(outs):
+        pltpu.make_async_copy(held.at[n], held.at[n], sems.at[n]).wait()
+        acts = held[n].reshape(4 * HALF, 4 * SHARE)
+        for weight, cols in pieces(core, mine, near, far, cross):
+            got = jnp.dot(acts, weight[...], preferred_element_type=jnp.float32).reshape(4, HALF, COLS)
+            for ys in range(4):
+                out[table[Y_SLOT + ys], :, cols] = got[ys].astype(out.dtype)
+
+
+def product(part, keeps, table, weights, slots):
     vmem, anywhere = pl.BlockSpec(memory_space=pltpu.VMEM), pl.BlockSpec(memory_space=pl.ANY)
+    n = len(keeps)
+    types = [jnp.float32 if keep else jnp.bfloat16 for keep in keeps]
     return pl.pallas_call(
-        functools.partial(product_kernel, part, (lambda core: core) if keep else (lambda core: 1 - core)),
+        functools.partial(product_kernel, part, keeps),
         in_specs=[pl.BlockSpec(memory_space=pltpu.SMEM)] + [vmem] * 4 + [anywhere] * 4,
-        out_specs=vmem,
-        out_shape=jax.ShapeDtypeStruct((4, HALF, 4 * COLS), jnp.float32 if keep else jnp.bfloat16),
-        scratch_shapes=[pltpu.VMEM((4, HALF, 4 * SHARE), jnp.bfloat16), pltpu.SemaphoreType.DMA((4,))],
+        out_specs=[vmem] * n,
+        out_shape=[jax.ShapeDtypeStruct((4, HALF, 4 * COLS), t) for t in types],
+        scratch_shapes=[pltpu.VMEM((n, 4, HALF, 4 * SHARE), jnp.bfloat16), pltpu.SemaphoreType.DMA((n,))],
         compiler_params=pltpu.CompilerParams(vmem_limit_bytes=20 * MIB),
-        cost_estimate=pl.CostEstimate(flops=2 * 512 * 2048 * 1024, bytes_accessed=8 * MIB, transcendentals=0),
+        cost_estimate=pl.CostEstimate(flops=n * 2 * 512 * 2048 * 1024, bytes_accessed=n * 8 * MIB, transcendentals=0),
     )(table, *weights, *slots)
 
 
@@ -190,13 +193,11 @@
 
 
 def arrange_kernel(table, *refs):
-    parts, out, sems = refs[:8], refs[8], refs[9]
+    parts, out, sems = refs[:4], refs[4], refs[5]
     copies = []
-    for i, part in enumerate(parts):
-        rows, dz = i // 4, i % 4
+    for dz, part in enumerate(parts):
         at = pl.multiple_of(((table[Z] + 4 - dz) & 3) * (2 * COLS), 2 * COLS)
-        to = out.at[pl.ds(rows * HALF, HALF), pl.ds(at, 2 * COLS)]
-        copies.append(pltpu.make_async_copy(part, to, sems.at[i]))
+        copies.append(pltpu.make_async_copy(part, out.at[:, pl.ds(at, 2 * COLS)], sems.at[dz]))
         copies[-1].start()
     for copy in copies:
         copy.wait()
@@ -229,30 +230,37 @@
     slots = gather(activations, same, (near, swapped), far)
     cross = permute(after(swapped, far), other_chip)
     weights = [mine, near, far, cross]
-    ready = after(table, slots["z"][3], slots["y"][3])
-
-    def chain(part):
-        passed = product(part, False, ready, weights, slots[part])
-        kept = product(part, True, ready, weights, slots[part])
+    ready = after(table, *slots["z"][2:], *slots["y"][2:])
+
+    def summed(passed, kept):
         both = kept + permute(passed, other_core).astype(f32)
-        came = permute(both[..., 2 * COLS :].astype(bf16), other_chip)
-        total = (both[..., : 2 * COLS] + came.astype(f32)).astype(bf16)
+        return both[..., : 2 * COLS], both[..., 2 * COLS :].astype(bf16)
+
+    def returned(own, came):
+        total = (own + came.astype(f32)).astype(bf16)
         got = {}
         for dy in (2, 1, 3, 0):
             got[dy] = permute(total[dy], lambda x, y, z, c: linear(x + 2 * c, y + dy, z, c))
-        own = jnp.stack([got[dy] for dy in range(4)])
-        other = permute(own, other_core)
-        picked = small_call(spread_kernel, [table, owner], [own, other], [(HALF, 2 * COLS)] * 4, pltpu.VMEM)
-        got = {}
-        for dz in (2, 1, 3, 0):
-            got[dz] = permute(picked[dz], lambda x, y, z, c: linear(x ^ c, y, z + dz, x % 2))
-        return [got[dz] for dz in range(4)]
-
-    blocks = chain("y")
-    blocks = chain("z") + blocks
-    return small_call(
-        arrange_kernel, [table], blocks, [(256, 8 * COLS)], pltpu.HBM, [pltpu.SemaphoreType.DMA((8,))]
-    )[0]
+        return jnp.stack([got[dy] for dy in range(4)])
+
+    (passed,) = product("z", [False], ready, weights, slots["z"])
+    (kept,) = product("z", [True], ready, weights, slots["z"])
+    first = summed(passed, kept)
+    ready = after(ready, first[1])
+    (passed,) = product("y", [False], ready, weights, slots["y"])
+    (kept,) = product("y", [True], ready, weights, slots["y"])
+    second = summed(passed, kept)
+    came = permute(first[1], other_chip)
+    came_last = permute(after(second[1], came), other_chip)
+    own = jnp.concatenate([returned(first[0], came), returned(second[0], came_last)], axis=1)
+    other = permute(own, other_core)
+
+    picked = small_call(spread_kernel, [table, owner], [own, other], [(256, 2 * COLS)] * 4, pltpu.VMEM)
+    got = {}
+    for dz in (2, 1, 3, 0):
+        got[dz] = permute(picked[dz], lambda x, y, z, c: linear(x ^ c, y, z + dz, x % 2))
+    got = [got[dz] for dz in range(4)]
+    return small_call(arrange_kernel, [table], got, [(256, 8 * COLS)], pltpu.HBM, [pltpu.SemaphoreType.DMA((4,))])[0]
 
 
 def solution(mesh):

time: 152 us -> 154 us (1.013)
  waiting for transfers between devices: 68.3 us -> 75.5 us
  starting transfers between devices: 58.1 us -> 53.3 us
    ppermute x37 -> x32, waiting for transfers between devices: 68.3 us -> 75.5 us  [permute(): lax.ppermute(value, AXES, [(i, move(*coords(i))) for i in range(N_DEV)])]
    ppermute x37 -> x32, starting transfers between devices: 58.1 us -> 53.3 us  [permute(): lax.ppermute(value, AXES, [(i, move(*coords(i))) for i in range(N_DEV)])]
  transfers between devices with their start and end apart: 37 -> 32, of which waited for: 17 -> 14; matrix products, arithmetic and copies ran while one was open for 2% -> 1% of each run, Pallas kernels for 14% -> 9%
where the time goes in v12:
time: 154 us; the launch traced here: 153 us
  waiting for transfers between devices  75.5 us (49%)
  starting transfers between devices  53.3 us (35%)
  Pallas kernels  21.8 us (14%)
    ppermute x32, waiting for transfers between devices, permute(): lax.ppermute(value, AXES, [(i, move(*coords(i))) for i in range(N_DEV)])  75.5 us
    ppermute x32, starting transfers between devices, permute(): lax.ppermute(value, AXES, [(i, move(*coords(i))) for i in range(N_DEV)])  53.3 us
    pallas_call x4, Pallas kernels, product(): pl.pallas_call(functools.partial(product_kernel, part, keeps), in_specs=[...  13 us
    pallas_call x2, Pallas kernels, refit(): pl.pallas_call(functools.partial(refit_kernel, first), in_specs=[pl.Block...  6.55 us
  transfers between devices with their start and end apart: 32, of which 14 were waited for; matrix products, arithmetic and copies ran while one was open for 1% of the time, Pallas kernels for 9%

profile of v12, /device:TPU:3, one launch (start us, length us, event | category | flops | bytes accessed | tf_op | source)
XLA Modules:
  0.0 153.3 jit_solution(1139392306170310657)
XLA Ops:
  0.0 1.8 %collective-permute-start = (bf16[256,512]{1,0:T(8,128)(2,1)}, bf16[256,512]{1,0:T(8,128)(2,1)S(1)}, u32[]{:S(2)}, u32[]{:S(2)}) collective-permute-start(bf16[256,512]{1,0:T(8,128)(2,1)} %param.5), channel_id=1, source_target_pairs={{0,64},{1,65},{2,66},{3,67},{4,68},{5,69},{6,70},{7,71},{8,72},{9,... | collective-permute-start | bytes 786440 | tf_op jit(solution)/shard_map/ppermute | solution.py:30
  1.8 0.7 dynamic-slice_bitcast_fusion.table
  2.5 3.3 %shard_map.46 = (bf16[2048,256]{1,0:T(8,128)(2,1)S(1)}, bf16[2048,256]{1,0:T(8,128)(2,1)S(1)}) custom-call(s32[32]{0:T(128)S(1)} %dynamic-slice_bitcast_fusion.table, f32[8192,256]{1,0:T(8,128)} %master.3), custom_call_target="tpu_custom_call" | custom-call | flops 6291456 | bytes 6291456 | tf_op jit(solution)/shard_map/pallas_call | solution.py:122
  5.8 3.1 %collective-permute-done = bf16[256,512]{1,0:T(8,128)(2,1)S(1)} collective-permute-done((bf16[256,512]{1,0:T(8,128)(2,1)}, bf16[256,512]{1,0:T(8,128)(2,1)S(1)}, u32[]{:S(2)}, u32[]{:S(2)}) %collective-permute-start) | collective-permute-done | bytes 262176 | tf_op jit(solution)/shard_map/ppermute | solution.py:30
  8.9 3.8 %collective-permute-start.1 = (bf16[1,2,128,512]{3,2,1,0:T(8,128)(2,1)S(1)}, bf16[1,2,128,512]{3,2,1,0:T(8,128)(2,1)S(1)}, u32[]{:S(2)}, u32[]{:S(2)}) collective-permute-start(bf16[1,2,128,512]{3,2,1,0:T(8,128)(2,1)S(1)} %get-tuple-element.32), channel_id=1, source_target_pairs={{0,2},{1,7},{2,0},{3,5},{4,6},{5,3},{6,4},{7,1},{8,10},{9,15},{10,... | collective-permute-start | bytes 786440 | tf_op jit(solution)/shard_map/ppermute | solution.py:30
  12.8 2.7 %collective-permute-start.2 = (bf16[1,2,128,512]{3,2,1,0:T(8,128)(2,1)S(1)}, bf16[1,2,128,512]{3,2,1,0:T(8,128)(2,1)S(1)}, u32[]{:S(2)}, u32[]{:S(2)}) collective-permute-start(bf16[1,2,128,512]{3,2,1,0:T(8,128)(2,1)S(1)} %get-tuple-element.33), channel_id=1, source_target_pairs={{0,16},{1,49},{2,18},{3,51},{4,20},{5,53},{6,22},{7,55},{8,24},{9,... | collective-permute-start | bytes 786440 | tf_op jit(solution)/shard_map/ppermute | solution.py:30
  15.5 3.3 %shard_map.47 = (bf16[2048,256]{1,0:T(8,128)(2,1)S(1)}, bf16[2048,256]{1,0:T(8,128)(2,1)S(1)}) custom-call(s32[32]{0:T(128)S(1)} %dynamic-slice_bitcast_fusion.table, f32[8192,256]{1,0:T(8,128)} %master.3), custom_call_target="tpu_custom_call" | custom-call | flops 6291456 | bytes 6291456 | tf_op jit(solution)/shard_map/pallas_call | solution.py:122
  18.8 0.1 collective-permute-start.5
  18.9 0.5 collective-permute-start.6
  19.4 0.1 pad_maximum_fusion.3
  19.5 0.1 collective-permute-start.3
  19.6 0.2 collective-permute-start.4
  19.8 0.3 collective-permute-start.7
  20.1 7.8 %collective-permute-done.3 = bf16[2,2,128,512]{3,2,1,0:T(8,128)(2,1)S(1)} collective-permute-done((bf16[2,2,128,512]{3,2,1,0:T(8,128)(2,1)S(1)}, bf16[2,2,128,512]{3,2,1,0:T(8,128)(2,1)S(1)}, u32[]{:S(2)}, u32[]{:S(2)}) %collective-permute-start.3) | collective-permute-done | bytes 524320 | tf_op jit(solution)/shard_map/ppermute | solution.py:30
  27.9 0.1 pad_maximum_fusion.refs_0_
  28.0 0.1 pad_maximum_fusion.1.refs_0_
  28.1 2.6 %collective-permute-start.12 = (bf16[4,2,128,512]{3,2,1,0:T(8,128)(2,1)S(1)}, bf16[4,2,128,512]{3,2,1,0:T(8,128)(2,1)S(1)}, u32[]{:S(2)}, u32[]{:S(2)}) collective-permute-start(bf16[4,2,128,512]{3,2,1,0:T(8,128)(2,1)S(1)} %pad_maximum_fusion.refs_0_), channel_id=1, source_target_pairs={{0,16},{1,49},{2,18},{3,51},{4,20},{5,53},{6,22},{7,55},{8,24},{9,... | collective-permute-start | bytes 3145736 | tf_op jit(solution)/shard_map/ppermute | solution.py:30
  30.7 1.0 collective-permute-start.9
  31.7 8.0 %collective-permute-done.7.far = bf16[2048,256]{1,0:T(8,128)(2,1)S(1)} collective-permute-done((bf16[2048,256]{1,0:T(8,128)(2,1)S(1)}, bf16[2048,256]{1,0:T(8,128)(2,1)S(1)}, u32[]{:S(2)}, u32[]{:S(2)}) %collective-permute-start.7) | collective-permute-done | bytes 1048608 | tf_op jit(solution)/shard_map/ppermute | solution.py:30
  39.8 2.0 %collective-permute-start.8 = (bf16[4,2,128,512]{3,2,1,0:T(8,128)(2,1)S(1)}, bf16[4,2,128,512]{3,2,1,0:T(8,128)(2,1)S(1)}, u32[]{:S(2)}, u32[]{:S(2)}) collective-permute-start(bf16[4,2,128,512]{3,2,1,0:T(8,128)(2,1)S(1)} %pad_maximum_fusion.1.refs_0_), channel_id=1, source_target_pairs={{0,6},{1,3},{2,4},{3,1},{4,2},{5,7},{6,0},{7,5},{8,14},{9,11},{10,... | collective-permute-start | bytes 3145736 | tf_op jit(solution)/shard_map/ppermute | solution.py:30
  41.8 2.8 %collective-permute-start.11 = (bf16[4,2,128,512]{3,2,1,0:T(8,128)(2,1)S(1)}, bf16[4,2,128,512]{3,2,1,0:T(8,128)(2,1)S(1)}, u32[]{:S(2)}, u32[]{:S(2)}) collective-permute-start(bf16[4,2,128,512]{3,2,1,0:T(8,128)(2,1)S(1)} %pad_maximum_fusion.refs_0_), channel_id=1, source_target_pairs={{0,48},{1,17},{2,50},{3,19},{4,52},{5,21},{6,54},{7,23},{8,56},{9,... | collective-permute-start | bytes 3145736 | tf_op jit(solution)/shard_map/ppermute | solution.py:30
  44.6 1.0 collective-permute-done.9.refs_1_
  45.6 0.4 collective-permute-start.10
  46.0 0.3 collective-permute-start.14
  46.3 12.0 %collective-permute-done.8.refs_2_ = bf16[4,2,128,512]{3,2,1,0:T(8,128)(2,1)S(1)} collective-permute-done((bf16[4,2,128,512]{3,2,1,0:T(8,128)(2,1)S(1)}, bf16[4,2,128,512]{3,2,1,0:T(8,128)(2,1)S(1)}, u32[]{:S(2)}, u32[]{:S(2)}) %collective-permute-start.8) | collective-permute-done | bytes 1048608 | tf_op jit(solution)/shard_map/ppermute | solution.py:30
  58.3 11.2 %collective-permute-done.10.refs_3_ = bf16[4,2,128,512]{3,2,1,0:T(8,128)(2,1)S(1)} collective-permute-done((bf16[4,2,128,512]{3,2,1,0:T(8,128)(2,1)S(1)}, bf16[4,2,128,512]{3,2,1,0:T(8,128)(2,1)S(1)}, u32[]{:S(2)}, u32[]{:S(2)}) %collective-permute-start.10) | collective-permute-done | bytes 1048608 | tf_op jit(solution)/shard_map/ppermute | solution.py:30
  69.5 3.3 %shard_map.49 = bf16[4,128,1024]{2,1,0:T(8,128)(2,1)S(1)} custom-call(s32[32]{0:T(128)S(1)} %dynamic-slice_bitcast_fusion.table, bf16[2048,256]{1,0:T(8,128)(2,1)S(1)} %get-tuple-element.47.mine, bf16[2048,256]{1,0:T(8,128)(2,1)S(1)} %collective-permute-done.5.near, bf16[2048,256]{1,0:T(8,128)(2,1)S(1)} %collective-permute-done.7.far, ...), custom_call_target="tpu_custom_call" | custom-call | flops 2147483648 | bytes 8388608 | tf_op jit(solution)/shard_map/pallas_call | solution.py:168
  72.8 5.3 %collective-permute-start.15 = (bf16[4,128,1024]{2,1,0:T(8,128)(2,1)S(1)}, bf16[4,128,1024]{2,1,0:T(8,128)(2,1)S(1)}, u32[]{:S(2)}, u32[]{:S(2)}) collective-permute-start(bf16[4,128,1024]{2,1,0:T(8,128)(2,1)S(1)} %shard_map.49), channel_id=1, source_target_pairs={{0,1},{1,0},{2,3},{3,2},{4,5},{5,4},{6,7},{7,6},{8,9},{9,8},{10,11... | collective-permute-start | bytes 3145736 | tf_op jit(solution)/shard_map/ppermute | solution.py:30
  78.1 3.2 %shard_map.48 = f32[4,128,1024]{2,1,0:T(8,128)S(1)} custom-call(s32[32]{0:T(128)S(1)} %dynamic-slice_bitcast_fusion.table, bf16[2048,256]{1,0:T(8,128)(2,1)S(1)} %get-tuple-element.47.mine, bf16[2048,256]{1,0:T(8,128)(2,1)S(1)} %collective-permute-done.5.near, bf16[2048,256]{1,0:T(8,128)(2,1)S(1)} %collective-permute-done.7.far, ...), custom_call_target="tpu_custom_call" | custom-call | flops 2147483648 | bytes 8388608 | tf_op jit(solution)/shard_map/pallas_call | solution.py:168
  81.4 0.4 convert_add_fusion.1
  81.8 0.1 slice.97
  81.9 3.3 %shard_map.51 = bf16[4,128,1024]{2,1,0:T(8,128)(2,1)S(1)} custom-call(s32[32]{0:T(128)S(1)} %dynamic-slice_bitcast_fusion.table, bf16[2048,256]{1,0:T(8,128)(2,1)S(1)} %get-tuple-element.47.mine, bf16[2048,256]{1,0:T(8,128)(2,1)S(1)} %collective-permute-done.5.near, bf16[2048,256]{1,0:T(8,128)(2,1)S(1)} %collective-permute-done.7.far, ...), custom_call_target="tpu_custom_call" | custom-call | flops 2147483648 | bytes 8388608 | tf_op jit(solution)/shard_map/pallas_call | solution.py:168
  85.2 0.1 collective-permute-start.21
  85.2 0.3 collective-permute-start.16
  85.6 3.2 %shard_map.50 = f32[4,128,1024]{2,1,0:T(8,128)S(1)} custom-call(s32[32]{0:T(128)S(1)} %dynamic-slice_bitcast_fusion.table, bf16[2048,256]{1,0:T(8,128)(2,1)S(1)} %get-tuple-element.47.mine, bf16[2048,256]{1,0:T(8,128)(2,1)S(1)} %collective-permute-done.5.near, bf16[2048,256]{1,0:T(8,128)(2,1)S(1)} %collective-permute-done.7.far, ...), custom_call_target="tpu_custom_call" | custom-call | flops 2147483648 | bytes 8388608 | tf_op jit(solution)/shard_map/pallas_call | solution.py:168
  88.8 0.3 convert_add_fusion
  89.1 0.1 slice.96
  89.2 9.2 %collective-permute-done.16 = bf16[4,128,512]{2,1,0:T(8,128)(2,1)S(1)} collective-permute-done((bf16[4,128,512]{2,1,0:T(8,128)(2,1)S(1)}, bf16[4,128,512]{2,1,0:T(8,128)(2,1)S(1)}, u32[]{:S(2)}, u32[]{:S(2)}) %collective-permute-start.16) | collective-permute-done | bytes 524320 | tf_op jit(solution)/shard_map/ppermute | solution.py:30
  98.4 0.3 collective-permute-start.22
  98.7 0.2 fusion.1
  98.9 4.0 %collective-permute-start.17 = (bf16[128,512]{1,0:T(8,128)(2,1)S(1)}, bf16[128,512]{1,0:T(8,128)(2,1)S(1)}, u32[]{:S(2)}, u32[]{:S(2)}) collective-permute-start(bf16[128,512]{1,0:T(8,128)(2,1)S(1)} %get-tuple-element.55), channel_id=1, source_target_pairs={{0,0},{1,65},{2,2},{3,67},{4,4},{5,69},{6,6},{7,71},{8,8},{9,73},{... | collective-permute-start | bytes 393224 | tf_op jit(solution)/shard_map/ppermute | solution.py:30
  102.9 3.4 %collective-permute-start.20 = (bf16[128,512]{1,0:T(8,128)(2,1)S(1)}, bf16[128,512]{1,0:T(8,128)(2,1)S(1)}, u32[]{:S(2)}, u32[]{:S(2)}) collective-permute-start(bf16[128,512]{1,0:T(8,128)(2,1)S(1)} %get-tuple-element.56), channel_id=1, source_target_pairs={{0,48},{1,113},{2,50},{3,115},{4,52},{5,117},{6,54},{7,119},{8,56}... | collective-permute-start | bytes 393224 | tf_op jit(solution)/shard_map/ppermute | solution.py:30
  106.3 1.0 collective-permute-start.19
  107.3 1.5 %collective-permute-start.18 = (bf16[128,512]{1,0:T(8,128)(2,1)S(1)}, bf16[128,512]{1,0:T(8,128)(2,1)S(1)}, u32[]{:S(2)}, u32[]{:S(2)}) collective-permute-start(bf16[128,512]{1,0:T(8,128)(2,1)S(1)} %get-tuple-element.58), channel_id=1, source_target_pairs={{0,16},{1,81},{2,18},{3,83},{4,20},{5,85},{6,22},{7,87},{8,24},{9,... | collective-permute-start | bytes 393224 | tf_op jit(solution)/shard_map/ppermute | solution.py:30
  108.8 1.8 %collective-permute-done.22 = bf16[4,128,512]{2,1,0:T(8,128)(2,1)S(1)} collective-permute-done((bf16[4,128,512]{2,1,0:T(8,128)(2,1)S(1)}, bf16[4,128,512]{2,1,0:T(8,128)(2,1)S(1)}, u32[]{:S(2)}, u32[]{:S(2)}) %collective-permute-start.22) | collective-permute-done | bytes 524320 | tf_op jit(solution)/shard_map/ppermute | solution.py:30
  110.6 0.2 fusion
  110.8 3.8 %collective-permute-start.23 = (bf16[128,512]{1,0:T(8,128)(2,1)S(1)}, bf16[128,512]{1,0:T(8,128)(2,1)S(1)}, u32[]{:S(2)}, u32[]{:S(2)}) collective-permute-start(bf16[128,512]{1,0:T(8,128)(2,1)S(1)} %get-tuple-element.59), channel_id=1, source_target_pairs={{0,0},{1,65},{2,2},{3,67},{4,4},{5,69},{6,6},{7,71},{8,8},{9,73},{... | collective-permute-start | bytes 393224 | tf_op jit(solution)/shard_map/ppermute | solution.py:30
  114.6 3.6 %collective-permute-start.26 = (bf16[128,512]{1,0:T(8,128)(2,1)S(1)}, bf16[128,512]{1,0:T(8,128)(2,1)S(1)}, u32[]{:S(2)}, u32[]{:S(2)}) collective-permute-start(bf16[128,512]{1,0:T(8,128)(2,1)S(1)} %get-tuple-element.60), channel_id=1, source_target_pairs={{0,48},{1,113},{2,50},{3,115},{4,52},{5,117},{6,54},{7,119},{8,56}... | collective-permute-start | bytes 393224 | tf_op jit(solution)/shard_map/ppermute | solution.py:30
  118.2 1.8 %collective-permute-start.25 = (bf16[128,512]{1,0:T(8,128)(2,1)S(1)}, bf16[128,512]{1,0:T(8,128)(2,1)S(1)}, u32[]{:S(2)}, u32[]{:S(2)}) collective-permute-start(bf16[128,512]{1,0:T(8,128)(2,1)S(1)} %get-tuple-element.61), channel_id=1, source_target_pairs={{0,32},{1,97},{2,34},{3,99},{4,36},{5,101},{6,38},{7,103},{8,40},{... | collective-permute-start | bytes 393224 | tf_op jit(solution)/shard_map/ppermute | solution.py:30
  120.0 1.4 collective-permute-start.24
  121.4 0.3 collective-permute-done.26
  121.7 4.4 %collective-permute-done.25 = bf16[128,512]{1,0:T(8,128)(2,1)S(1)} collective-permute-done((bf16[128,512]{1,0:T(8,128)(2,1)S(1)}, bf16[128,512]{1,0:T(8,128)(2,1)S(1)}, u32[]{:S(2)}, u32[]{:S(2)}) %collective-permute-start.25) | collective-permute-done | bytes 131104 | tf_op jit(solution)/shard_map/ppermute | solution.py:30
  126.1 1.4 collective-permute-done.24
  127.5 0.1 maximum_maximum_fusion.own
  127.6 1.6 %collective-permute-start.27 = (bf16[4,256,512]{2,1,0:T(8,128)(2,1)S(1)}, bf16[4,256,512]{2,1,0:T(8,128)(2,1)S(1)}, u32[]{:S(2)}, u32[]{:S(2)}) collective-permute-start(bf16[4,256,512]{2,1,0:T(8,128)(2,1)S(1)} %maximum_maximum_fusion.own), channel_id=1, source_target_pairs={{0,1},{1,0},{2,3},{3,2},{4,5},{5,4},{6,7},{7,6},{8,9},{9,8},{10,11... | collective-permute-start | bytes 3145736 | tf_op jit(solution)/shard_map/ppermute | solution.py:30
  129.1 2.3 %collective-permute-done.27.other = bf16[4,256,512]{2,1,0:T(8,128)(2,1)S(1)} collective-permute-done((bf16[4,256,512]{2,1,0:T(8,128)(2,1)S(1)}, bf16[4,256,512]{2,1,0:T(8,128)(2,1)S(1)}, u32[]{:S(2)}, u32[]{:S(2)}) %collective-permute-start.27) | collective-permute-done | bytes 1048608 | tf_op jit(solution)/shard_map/ppermute | solution.py:30
  131.4 0.7 shard_map.52
  132.1 2.2 %collective-permute-start.28 = (bf16[256,512]{1,0:T(8,128)(2,1)S(1)}, bf16[256,512]{1,0:T(8,128)(2,1)S(1)}, u32[]{:S(2)}, u32[]{:S(2)}) collective-permute-start(bf16[256,512]{1,0:T(8,128)(2,1)S(1)} %get-tuple-element.51), channel_id=1, source_target_pairs={{0,0},{1,8},{2,2},{3,10},{4,4},{5,12},{6,6},{7,14},{8,9},{9,1},{10... | collective-permute-start | bytes 786440 | tf_op jit(solution)/shard_map/ppermute | solution.py:30
  134.3 1.0 collective-permute-start.29
  135.3 2.0 %collective-permute-start.30 = (bf16[256,512]{1,0:T(8,128)(2,1)S(1)}, bf16[256,512]{1,0:T(8,128)(2,1)S(1)}, u32[]{:S(2)}, u32[]{:S(2)}) collective-permute-start(bf16[256,512]{1,0:T(8,128)(2,1)S(1)} %get-tuple-element.53), channel_id=1, source_target_pairs={{0,4},{1,12},{2,6},{3,14},{4,0},{5,8},{6,2},{7,10},{8,13},{9,5},{1... | collective-permute-start | bytes 786440 | tf_op jit(solution)/shard_map/ppermute | solution.py:30
  137.3 1.4 collective-permute-start.31
  138.8 11.1 %collective-permute-done.29.refs_1_ = bf16[256,512]{1,0:T(8,128)(2,1)S(1)} collective-permute-done((bf16[256,512]{1,0:T(8,128)(2,1)S(1)}, bf16[256,512]{1,0:T(8,128)(2,1)S(1)}, u32[]{:S(2)}, u32[]{:S(2)}) %collective-permute-start.29) | collective-permute-done | bytes 262176 | tf_op jit(solution)/shard_map/ppermute | solution.py:30
  149.8 1.8 %collective-permute-done.31.refs_3_ = bf16[256,512]{1,0:T(8,128)(2,1)S(1)} collective-permute-done((bf16[256,512]{1,0:T(8,128)(2,1)S(1)}, bf16[256,512]{1,0:T(8,128)(2,1)S(1)}, u32[]{:S(2)}, u32[]{:S(2)}) %collective-permute-start.31) | collective-permute-done | bytes 262176 | tf_op jit(solution)/shard_map/ppermute | solution.py:30
  151.6 1.5 %shard_map.53 = bf16[256,2048]{1,0:T(8,128)(2,1)} custom-call(s32[32]{0:T(128)S(1)} %dynamic-slice_bitcast_fusion.table, bf16[256,512]{1,0:T(8,128)(2,1)S(1)} %collective-permute-done.28.refs_0_, bf16[256,512]{1,0:T(8,128)(2,1)S(1)} %collective-permute-done.29.refs_1_, bf16[256,512]{1,0:T(8,128)(2,1)S(1)} %collective-permute-done.30.refs_2_, ...), custom_call_target="tpu_custom_call" | custom-call | bytes 2097152 | tf_op jit(solution)/shard_map/pallas_call | solution.py:208
  (27 shorter events, 0.2 us)
Async XLA Ops:
  0.0 8.9 %collective-permute-start = (bf16[256,512]{1,0:T(8,128)(2,1)}, bf16[256,512]{1,0:T(8,128)(2,1)S(1)}, u32[]{:S(2)}, u32[]{:S(2)}) collective-permute-start(bf16[256,512]{1,0:T(8,128)(2,1)} %param.5), channel_id=1, source_target_pairs={{0,64},{1,65},{2,66},{3,67},{4,68},{5,69},{6,70},{7,71},{8,72},{9,... | collective-permute-start | bytes 786440 | tf_op jit(solution)/shard_map/ppermute | solution.py:30
  2.5 6.4 %copy-start.1 = (bf16[256,512]{1,0:T(8,128)(2,1)S(1)}, bf16[256,512]{1,0:T(8,128)(2,1)}, u32[]{:S(2)}) copy-start(bf16[256,512]{1,0:T(8,128)(2,1)} %param.5) | copy-start | bytes 786436
  8.9 10.4 %collective-permute-start.1 = (bf16[1,2,128,512]{3,2,1,0:T(8,128)(2,1)S(1)}, bf16[1,2,128,512]{3,2,1,0:T(8,128)(2,1)S(1)}, u32[]{:S(2)}, u32[]{:S(2)}) collective-permute-start(bf16[1,2,128,512]{3,2,1,0:T(8,128)(2,1)S(1)} %get-tuple-element.32), channel_id=1, source_target_pairs={{0,2},{1,7},{2,0},{3,5},{4,6},{5,3},{6,4},{7,1},{8,10},{9,15},{10,... | collective-permute-start | bytes 786440 | tf_op jit(solution)/shard_map/ppermute | solution.py:30
  12.8 6.7 %collective-permute-start.2 = (bf16[1,2,128,512]{3,2,1,0:T(8,128)(2,1)S(1)}, bf16[1,2,128,512]{3,2,1,0:T(8,128)(2,1)S(1)}, u32[]{:S(2)}, u32[]{:S(2)}) collective-permute-start(bf16[1,2,128,512]{3,2,1,0:T(8,128)(2,1)S(1)} %get-tuple-element.33), channel_id=1, source_target_pairs={{0,16},{1,49},{2,18},{3,51},{4,20},{5,53},{6,22},{7,55},{8,24},{9,... | collective-permute-start | bytes 786440 | tf_op jit(solution)/shard_map/ppermute | solution.py:30
  18.8 9.3 %collective-permute-start.5 = (bf16[2048,256]{1,0:T(8,128)(2,1)S(1)}, bf16[2048,256]{1,0:T(8,128)(2,1)S(1)}, u32[]{:S(2)}, u32[]{:S(2)}) collective-permute-start(bf16[2048,256]{1,0:T(8,128)(2,1)S(1)} %get-tuple-element.38), channel_id=1, source_target_pairs={{0,1},{1,0},{2,3},{3,2},{4,5},{5,4},{6,7},{7,6},{8,9},{9,8},{10,11... | collective-permute-start | bytes 3145736 | tf_op jit(solution)/shard_map/ppermute | solution.py:30
  18.9 9.3 %collective-permute-start.6 = (bf16[2048,256]{1,0:T(8,128)(2,1)S(1)}, bf16[2048,256]{1,0:T(8,128)(2,1)S(1)}, u32[]{:S(2)}, u32[]{:S(2)}) collective-permute-start(bf16[2048,256]{1,0:T(8,128)(2,1)S(1)} %get-tuple-element.39), channel_id=1, source_target_pairs={{0,1},{1,0},{2,3},{3,2},{4,5},{5,4},{6,7},{7,6},{8,9},{9,8},{10,11... | collective-permute-start | bytes 3145736 | tf_op jit(solution)/shard_map/ppermute | solution.py:30
  19.5 8.4 %collective-permute-start.3 = (bf16[2,2,128,512]{3,2,1,0:T(8,128)(2,1)S(1)}, bf16[2,2,128,512]{3,2,1,0:T(8,128)(2,1)S(1)}, u32[]{:S(2)}, u32[]{:S(2)}) collective-permute-start(bf16[2,2,128,512]{3,2,1,0:T(8,128)(2,1)S(1)} %pad_maximum_fusion.2), channel_id=1, source_target_pairs={{0,6},{1,3},{2,4},{3,1},{4,2},{5,7},{6,0},{7,5},{8,14},{9,11},{10,... | collective-permute-start | bytes 1572872 | tf_op jit(solution)/shard_map/ppermute | solution.py:30
  19.6 8.4 %collective-permute-start.4 = (bf16[2,2,128,512]{3,2,1,0:T(8,128)(2,1)S(1)}, bf16[2,2,128,512]{3,2,1,0:T(8,128)(2,1)S(1)}, u32[]{:S(2)}, u32[]{:S(2)}) collective-permute-start(bf16[2,2,128,512]{3,2,1,0:T(8,128)(2,1)S(1)} %pad_maximum_fusion.3), channel_id=1, source_target_pairs={{0,48},{1,17},{2,50},{3,19},{4,52},{5,21},{6,54},{7,23},{8,56},{9,... | collective-permute-start | bytes 1572872 | tf_op jit(solution)/shard_map/ppermute | solution.py:30
  19.8 19.9 %collective-permute-start.7 = (bf16[2048,256]{1,0:T(8,128)(2,1)S(1)}, bf16[2048,256]{1,0:T(8,128)(2,1)S(1)}, u32[]{:S(2)}, u32[]{:S(2)}) collective-permute-start(bf16[2048,256]{1,0:T(8,128)(2,1)S(1)} %get-tuple-element.30), channel_id=1, source_target_pairs={{0,8},{1,9},{2,10},{3,11},{4,12},{5,13},{6,14},{7,15},{8,0},{9,1},... | collective-permute-start | bytes 3145736 | tf_op jit(solution)/shard_map/ppermute | solution.py:30
  28.1 16.4 %collective-permute-start.12 = (bf16[4,2,128,512]{3,2,1,0:T(8,128)(2,1)S(1)}, bf16[4,2,128,512]{3,2,1,0:T(8,128)(2,1)S(1)}, u32[]{:S(2)}, u32[]{:S(2)}) collective-permute-start(bf16[4,2,128,512]{3,2,1,0:T(8,128)(2,1)S(1)} %pad_maximum_fusion.refs_0_), channel_id=1, source_target_pairs={{0,16},{1,49},{2,18},{3,51},{4,20},{5,53},{6,22},{7,55},{8,24},{9,... | collective-permute-start | bytes 3145736 | tf_op jit(solution)/shard_map/ppermute | solution.py:30
  30.7 14.9 %collective-permute-start.9 = (bf16[4,2,128,512]{3,2,1,0:T(8,128)(2,1)S(1)}, bf16[4,2,128,512]{3,2,1,0:T(8,128)(2,1)S(1)}, u32[]{:S(2)}, u32[]{:S(2)}) collective-permute-start(bf16[4,2,128,512]{3,2,1,0:T(8,128)(2,1)S(1)} %pad_maximum_fusion.1.refs_0_), channel_id=1, source_target_pairs={{0,2},{1,7},{2,0},{3,5},{4,6},{5,3},{6,4},{7,1},{8,10},{9,15},{10,... | collective-permute-start | bytes 3145736 | tf_op jit(solution)/shard_map/ppermute | solution.py:30
  39.8 18.5 %collective-permute-start.8 = (bf16[4,2,128,512]{3,2,1,0:T(8,128)(2,1)S(1)}, bf16[4,2,128,512]{3,2,1,0:T(8,128)(2,1)S(1)}, u32[]{:S(2)}, u32[]{:S(2)}) collective-permute-start(bf16[4,2,128,512]{3,2,1,0:T(8,128)(2,1)S(1)} %pad_maximum_fusion.1.refs_0_), channel_id=1, source_target_pairs={{0,6},{1,3},{2,4},{3,1},{4,2},{5,7},{6,0},{7,5},{8,14},{9,11},{10,... | collective-permute-start | bytes 3145736 | tf_op jit(solution)/shard_map/ppermute | solution.py:30
  41.8 16.5 %collective-permute-start.11 = (bf16[4,2,128,512]{3,2,1,0:T(8,128)(2,1)S(1)}, bf16[4,2,128,512]{3,2,1,0:T(8,128)(2,1)S(1)}, u32[]{:S(2)}, u32[]{:S(2)}) collective-permute-start(bf16[4,2,128,512]{3,2,1,0:T(8,128)(2,1)S(1)} %pad_maximum_fusion.refs_0_), channel_id=1, source_target_pairs={{0,48},{1,17},{2,50},{3,19},{4,52},{5,21},{6,54},{7,23},{8,56},{9,... | collective-permute-start | bytes 3145736 | tf_op jit(solution)/shard_map/ppermute | solution.py:30
  45.6 23.9 %collective-permute-start.10 = (bf16[4,2,128,512]{3,2,1,0:T(8,128)(2,1)S(1)}, bf16[4,2,128,512]{3,2,1,0:T(8,128)(2,1)S(1)}, u32[]{:S(2)}, u32[]{:S(2)}) collective-permute-start(bf16[4,2,128,512]{3,2,1,0:T(8,128)(2,1)S(1)} %collective-permute-done.9.refs_1_), channel_id=1, source_target_pairs={{0,6},{1,3},{2,4},{3,1},{4,2},{5,7},{6,0},{7,5},{8,14},{9,11},{10,... | collective-permute-start | bytes 3145736 | tf_op jit(solution)/shard_map/ppermute | solution.py:30
  46.0 23.5 %collective-permute-start.13 = (bf16[4,2,128,512]{3,2,1,0:T(8,128)(2,1)S(1)}, bf16[4,2,128,512]{3,2,1,0:T(8,128)(2,1)S(1)}, u32[]{:S(2)}, u32[]{:S(2)}) collective-permute-start(bf16[4,2,128,512]{3,2,1,0:T(8,128)(2,1)S(1)} %collective-permute-done.12.refs_1_), channel_id=1, source_target_pairs={{0,48},{1,17},{2,50},{3,19},{4,52},{5,21},{6,54},{7,23},{8,56},{9,... | collective-permute-start | bytes 3145736 | tf_op jit(solution)/shard_map/ppermute | solution.py:30
  46.0 23.5 %collective-permute-start.14 = (bf16[2048,256]{1,0:T(8,128)(2,1)S(1)}, bf16[2048,256]{1,0:T(8,128)(2,1)S(1)}, u32[]{:S(2)}, u32[]{:S(2)}) collective-permute-start(bf16[2048,256]{1,0:T(8,128)(2,1)S(1)} %collective-permute-done.6), channel_id=1, source_target_pairs={{0,8},{1,9},{2,10},{3,11},{4,12},{5,13},{6,14},{7,15},{8,0},{9,1},... | collective-permute-start | bytes 3145736 | tf_op jit(solution)/shard_map/ppermute | solution.py:30
  72.8 8.6 %collective-permute-start.15 = (bf16[4,128,1024]{2,1,0:T(8,128)(2,1)S(1)}, bf16[4,128,1024]{2,1,0:T(8,128)(2,1)S(1)}, u32[]{:S(2)}, u32[]{:S(2)}) collective-permute-start(bf16[4,128,1024]{2,1,0:T(8,128)(2,1)S(1)} %shard_map.49), channel_id=1, source_target_pairs={{0,1},{1,0},{2,3},{3,2},{4,5},{5,4},{6,7},{7,6},{8,9},{9,8},{10,11... | collective-permute-start | bytes 3145736 | tf_op jit(solution)/shard_map/ppermute | solution.py:30
  85.2 3.7 %collective-permute-start.21 = (bf16[4,128,1024]{2,1,0:T(8,128)(2,1)S(1)}, bf16[4,128,1024]{2,1,0:T(8,128)(2,1)S(1)}, u32[]{:S(2)}, u32[]{:S(2)}) collective-permute-start(bf16[4,128,1024]{2,1,0:T(8,128)(2,1)S(1)} %shard_map.51), channel_id=1, source_target_pairs={{0,1},{1,0},{2,3},{3,2},{4,5},{5,4},{6,7},{7,6},{8,9},{9,8},{10,11... | collective-permute-start | bytes 3145736 | tf_op jit(solution)/shard_map/ppermute | solution.py:30
  85.2 13.2 %collective-permute-start.16 = (bf16[4,128,512]{2,1,0:T(8,128)(2,1)S(1)}, bf16[4,128,512]{2,1,0:T(8,128)(2,1)S(1)}, u32[]{:S(2)}, u32[]{:S(2)}) collective-permute-start(bf16[4,128,512]{2,1,0:T(8,128)(2,1)S(1)} %slice.97), channel_id=1, source_target_pairs={{0,8},{1,9},{2,10},{3,11},{4,12},{5,13},{6,14},{7,15},{8,0},{9,1},... | collective-permute-start | bytes 1572872 | tf_op jit(solution)/shard_map/ppermute | solution.py:30
  98.4 12.2 %collective-permute-start.22 = (bf16[4,128,512]{2,1,0:T(8,128)(2,1)S(1)}, bf16[4,128,512]{2,1,0:T(8,128)(2,1)S(1)}, u32[]{:S(2)}, u32[]{:S(2)}) collective-permute-start(bf16[4,128,512]{2,1,0:T(8,128)(2,1)S(1)} %slice.96), channel_id=1, source_target_pairs={{0,8},{1,9},{2,10},{3,11},{4,12},{5,13},{6,14},{7,15},{8,0},{9,1},... | collective-permute-start | bytes 1572872 | tf_op jit(solution)/shard_map/ppermute | solution.py:30
  98.9 15.7 %collective-permute-start.17 = (bf16[128,512]{1,0:T(8,128)(2,1)S(1)}, bf16[128,512]{1,0:T(8,128)(2,1)S(1)}, u32[]{:S(2)}, u32[]{:S(2)}) collective-permute-start(bf16[128,512]{1,0:T(8,128)(2,1)S(1)} %get-tuple-element.55), channel_id=1, source_target_pairs={{0,0},{1,65},{2,2},{3,67},{4,4},{5,69},{6,6},{7,71},{8,8},{9,73},{... | collective-permute-start | bytes 393224 | tf_op jit(solution)/shard_map/ppermute | solution.py:30
  102.9 15.3 %collective-permute-start.20 = (bf16[128,512]{1,0:T(8,128)(2,1)S(1)}, bf16[128,512]{1,0:T(8,128)(2,1)S(1)}, u32[]{:S(2)}, u32[]{:S(2)}) collective-permute-start(bf16[128,512]{1,0:T(8,128)(2,1)S(1)} %get-tuple-element.56), channel_id=1, source_target_pairs={{0,48},{1,113},{2,50},{3,115},{4,52},{5,117},{6,54},{7,119},{8,56}... | collective-permute-start | bytes 393224 | tf_op jit(solution)/shard_map/ppermute | solution.py:30
  106.3 13.7 %collective-permute-start.19 = (bf16[128,512]{1,0:T(8,128)(2,1)S(1)}, bf16[128,512]{1,0:T(8,128)(2,1)S(1)}, u32[]{:S(2)}, u32[]{:S(2)}) collective-permute-start(bf16[128,512]{1,0:T(8,128)(2,1)S(1)} %get-tuple-element.57), channel_id=1, source_target_pairs={{0,32},{1,97},{2,34},{3,99},{4,36},{5,101},{6,38},{7,103},{8,40},{... | collective-permute-start | bytes 393224 | tf_op jit(solution)/shard_map/ppermute | solution.py:30
  107.3 14.1 %collective-permute-start.18 = (bf16[128,512]{1,0:T(8,128)(2,1)S(1)}, bf16[128,512]{1,0:T(8,128)(2,1)S(1)}, u32[]{:S(2)}, u32[]{:S(2)}) collective-permute-start(bf16[128,512]{1,0:T(8,128)(2,1)S(1)} %get-tuple-element.58), channel_id=1, source_target_pairs={{0,16},{1,81},{2,18},{3,83},{4,20},{5,85},{6,22},{7,87},{8,24},{9,... | collective-permute-start | bytes 393224 | tf_op jit(solution)/shard_map/ppermute | solution.py:30
  110.8 20.7 %copy-start = (s32[8]{0:T(128)S(1)}, s32[8]{0:T(128)}, u32[]{:S(2)}) copy-start(s32[8]{0:T(128)} %owner.1) | copy-start | bytes 100
  110.8 10.6 %collective-permute-start.23 = (bf16[128,512]{1,0:T(8,128)(2,1)S(1)}, bf16[128,512]{1,0:T(8,128)(2,1)S(1)}, u32[]{:S(2)}, u32[]{:S(2)}) collective-permute-start(bf16[128,512]{1,0:T(8,128)(2,1)S(1)} %get-tuple-element.59), channel_id=1, source_target_pairs={{0,0},{1,65},{2,2},{3,67},{4,4},{5,69},{6,6},{7,71},{8,8},{9,73},{... | collective-permute-start | bytes 393224 | tf_op jit(solution)/shard_map/ppermute | solution.py:30
  114.6 7.1 %collective-permute-start.26 = (bf16[128,512]{1,0:T(8,128)(2,1)S(1)}, bf16[128,512]{1,0:T(8,128)(2,1)S(1)}, u32[]{:S(2)}, u32[]{:S(2)}) collective-permute-start(bf16[128,512]{1,0:T(8,128)(2,1)S(1)} %get-tuple-element.60), channel_id=1, source_target_pairs={{0,48},{1,113},{2,50},{3,115},{4,52},{5,117},{6,54},{7,119},{8,56}... | collective-permute-start | bytes 393224 | tf_op jit(solution)/shard_map/ppermute | solution.py:30
  118.2 7.9 %collective-permute-start.25 = (bf16[128,512]{1,0:T(8,128)(2,1)S(1)}, bf16[128,512]{1,0:T(8,128)(2,1)S(1)}, u32[]{:S(2)}, u32[]{:S(2)}) collective-permute-start(bf16[128,512]{1,0:T(8,128)(2,1)S(1)} %get-tuple-element.61), channel_id=1, source_target_pairs={{0,32},{1,97},{2,34},{3,99},{4,36},{5,101},{6,38},{7,103},{8,40},{... | collective-permute-start | bytes 393224 | tf_op jit(solution)/shard_map/ppermute | solution.py:30
  120.0 7.5 %collective-permute-start.24 = (bf16[128,512]{1,0:T(8,128)(2,1)S(1)}, bf16[128,512]{1,0:T(8,128)(2,1)S(1)}, u32[]{:S(2)}, u32[]{:S(2)}) collective-permute-start(bf16[128,512]{1,0:T(8,128)(2,1)S(1)} %get-tuple-element.62), channel_id=1, source_target_pairs={{0,16},{1,81},{2,18},{3,83},{4,20},{5,85},{6,22},{7,87},{8,24},{9,... | collective-permute-start | bytes 393224 | tf_op jit(solution)/shard_map/ppermute | solution.py:30
  127.6 3.8 %collective-permute-start.27 = (bf16[4,256,512]{2,1,0:T(8,128)(2,1)S(1)}, bf16[4,256,512]{2,1,0:T(8,128)(2,1)S(1)}, u32[]{:S(2)}, u32[]{:S(2)}) collective-permute-start(bf16[4,256,512]{2,1,0:T(8,128)(2,1)S(1)} %maximum_maximum_fusion.own), channel_id=1, source_target_pairs={{0,1},{1,0},{2,3},{3,2},{4,5},{5,4},{6,7},{7,6},{8,9},{9,8},{10,11... | collective-permute-start | bytes 3145736 | tf_op jit(solution)/shard_map/ppermute | solution.py:30
  132.1 6.6 %collective-permute-start.28 = (bf16[256,512]{1,0:T(8,128)(2,1)S(1)}, bf16[256,512]{1,0:T(8,128)(2,1)S(1)}, u32[]{:S(2)}, u32[]{:S(2)}) collective-permute-start(bf16[256,512]{1,0:T(8,128)(2,1)S(1)} %get-tuple-element.51), channel_id=1, source_target_pairs={{0,0},{1,8},{2,2},{3,10},{4,4},{5,12},{6,6},{7,14},{8,9},{9,1},{10... | collective-permute-start | bytes 786440 | tf_op jit(solution)/shard_map/ppermute | solution.py:30
  134.3 15.5 %collective-permute-start.29 = (bf16[256,512]{1,0:T(8,128)(2,1)S(1)}, bf16[256,512]{1,0:T(8,128)(2,1)S(1)}, u32[]{:S(2)}, u32[]{:S(2)}) collective-permute-start(bf16[256,512]{1,0:T(8,128)(2,1)S(1)} %get-tuple-element.52), channel_id=1, source_target_pairs={{0,2},{1,10},{2,4},{3,12},{4,6},{5,14},{6,0},{7,8},{8,11},{9,3},{1... | collective-permute-start | bytes 786440 | tf_op jit(solution)/shard_map/ppermute | solution.py:30
  135.3 14.5 %collective-permute-start.30 = (bf16[256,512]{1,0:T(8,128)(2,1)S(1)}, bf16[256,512]{1,0:T(8,128)(2,1)S(1)}, u32[]{:S(2)}, u32[]{:S(2)}) collective-permute-start(bf16[256,512]{1,0:T(8,128)(2,1)S(1)} %get-tuple-element.53), channel_id=1, source_target_pairs={{0,4},{1,12},{2,6},{3,14},{4,0},{5,8},{6,2},{7,10},{8,13},{9,5},{1... | collective-permute-start | bytes 786440 | tf_op jit(solution)/shard_map/ppermute | solution.py:30
  137.3 14.3 %collective-permute-start.31 = (bf16[256,512]{1,0:T(8,128)(2,1)S(1)}, bf16[256,512]{1,0:T(8,128)(2,1)S(1)}, u32[]{:S(2)}, u32[]{:S(2)}) collective-permute-start(bf16[256,512]{1,0:T(8,128)(2,1)S(1)} %get-tuple-element.54), channel_id=1, source_target_pairs={{0,6},{1,14},{2,0},{3,8},{4,2},{5,10},{6,4},{7,12},{8,15},{9,7},{1... | collective-permute-start | bytes 786440 | tf_op jit(solution)/shard_map/ppermute | solution.py:30

commit v13 on v12

--- a/solution.py
+++ b/solution.py
@@ -13,7 +13,7 @@
 N_DEV = 128
 SHARE = 512
 COLS = 256
-HALF = 128
+ROWS = {"z": 112, "y": 144}
 MIB = 1024 * 1024
 
 
@@ -56,22 +56,21 @@
     return lax.optimization_barrier((value, *others))[0]
 
 
-def gather(activations, first_job, second_job, third_job):
+def gather(activations, jobs):
     came = permute(activations, lambda x, y, z, c: linear(x + 2, y, z, c))
-    block = jnp.stack([activations, after(came, first_job)])
-    blocks = {"z": block[None, :, :HALF], "y": block[None, :, HALF:]}
+    block = jnp.stack([activations, after(came, *jobs[0])])[None]
+    blocks = {"z": block[:, :, : ROWS["z"]], "y": block[:, :, ROWS["z"] :]}
     blocks = lax.optimization_barrier(blocks)
     for which in (1, 2):
         blocks = {
             part: jnp.concatenate([v, exchange(v, "y" if part == "z" else "z", which)]) for part, v in blocks.items()
         }
-        blocks = lax.optimization_barrier(blocks)
-    blocks, second_job = lax.optimization_barrier((blocks, second_job))
+        blocks = after(blocks, *jobs[which])
     slots = {}
     for part, v in blocks.items():
         first = exchange(v, part, 1)
-        second = exchange(after(v, third_job), part, 2)
-        slots[part] = [v, first, second, exchange(after(first, third_job), part, 2)]
+        second = exchange(v, part, 2)
+        slots[part] = [v, first, second, exchange(first, part, 2)]
     return slots
 
 
@@ -100,9 +99,8 @@
         copies.append(pltpu.make_async_copy(master.at[pl.ds(at, SHARE)], held.at[n], sems.at[n]))
         copies[-1].start()
     tiles = SHARE // BLOCK
-    for n in range(8):
-        out = outs[n * len(outs) // 8]
-        start = n * SHARE % out.shape[0]
+    places = [(out, at) for out in outs for at in range(0, out.shape[0], SHARE)]
+    for n, (out, start) in enumerate(places):
         copies[n].wait()
         amax = jnp.max(jnp.abs(held[n]).reshape(tiles, BLOCK, COLS), axis=1)
         for c in range(COLS // BLOCK):
@@ -117,13 +115,13 @@
                 out[start + r * BLOCK : start + (r + 1) * BLOCK, cols] = value
 
 
-def refit(table, master, first, n_outs):
+def refit(table, master, first, counts):
     size = 8 * SHARE * COLS
     return pl.pallas_call(
         functools.partial(refit_kernel, first),
         in_specs=[pl.BlockSpec(memory_space=pltpu.SMEM), pl.BlockSpec(memory_space=pltpu.HBM)],
-        out_specs=[pl.BlockSpec(memory_space=pltpu.VMEM)] * n_outs,
-        out_shape=[jax.ShapeDtypeStruct((8 * SHARE // n_outs, COLS), jnp.bfloat16)] * n_outs,
+        out_specs=[pl.BlockSpec(memory_space=pltpu.VMEM)] * len(counts),
+        out_shape=[jax.ShapeDtypeStruct((n * SHARE, COLS), jnp.bfloat16) for n in counts],
         scratch_shapes=[pltpu.VMEM((8, SHARE, COLS), jnp.float32), pltpu.SemaphoreType.DMA((8,))],
         compiler_params=pltpu.CompilerParams(vmem_limit_bytes=44 * MIB),
         cost_estimate=pl.CostEstimate(flops=size * 6, bytes_accessed=size * 6, transcendentals=0),
@@ -134,45 +132,52 @@
     return jnp.dot(a, b, preferred_element_type=jnp.float32)
 
 
-def pieces(core, mine, near, far, cross):
+def pieces(core, mine, near, far, more, cross):
     def cols(at, c):
         return pl.ds(pl.multiple_of(at + c * COLS, COLS), COLS)
 
-    return [(mine, cols(0, core)), (near, cols(0, 1 - core)), (far, cols(2 * COLS, core)), (cross, cols(2 * COLS, 1 - core))]
-
-
-def product_kernel(part, keeps, table, mine, near, far, cross, *refs):
-    slots, outs, (held, sems) = refs[:4], refs[4:-2], refs[-2:]
+    return [
+        ((mine,), cols(0, core)),
+        ((near,), cols(0, 1 - core)),
+        ((far, more), cols(2 * COLS, core)),
+        ((cross,), cols(2 * COLS, 1 - core)),
+    ]
+
+
+def product_kernel(part, keep, table, mine, near, far, more, cross, *refs):
+    slots, (out, held, sem) = refs[:4], refs[4:]
     core = table[CORE]
-    for n, keep in enumerate(keeps):
-        half = core if keep else 1 - core
-        for i, slot in enumerate(slots):
-            for k in range(4):
-                zs = k if part == "y" else i
-                depth = pl.ds(pl.multiple_of(table[Z_SLOT + zs] * SHARE, SHARE), SHARE)
-                to = held.at[n, i if part == "y" else k, :, depth]
-                pltpu.make_async_copy(slot.at[k, half], to, sems.at[n]).start()
-    for n, out in enumerate(outs):
-        pltpu.make_async_copy(held.at[n], held.at[n], sems.at[n]).wait()
-        acts = held[n].reshape(4 * HALF, 4 * SHARE)
-        for weight, cols in pieces(core, mine, near, far, cross):
-            got = jnp.dot(acts, weight[...], preferred_element_type=jnp.float32).reshape(4, HALF, COLS)
-            for ys in range(4):
-                out[table[Y_SLOT + ys], :, cols] = got[ys].astype(out.dtype)
-
-
-def product(part, keeps, table, weights, slots):
+    half = core if keep else 1 - core
+    for i, slot in enumerate(slots):
+        for k in range(4):
+            zs = k if part == "y" else i
+            depth = pl.ds(pl.multiple_of(table[Z_SLOT + zs] * SHARE, SHARE), SHARE)
+            to = held.at[i if part == "y" else k, :, depth]
+            pltpu.make_async_copy(slot.at[k, half], to, sem).start()
+    pltpu.make_async_copy(held, held, sem).wait()
+    acts = held[...].reshape(4 * ROWS[part], 4 * SHARE)
+    for weights, cols in pieces(core, mine, near, far, more, cross):
+        got, at = None, 0
+        for weight in weights:
+            term = jnp.dot(
+                acts[:, at : at + weight.shape[0]], weight[...], preferred_element_type=jnp.float32
+            )
+            got, at = term if got is None else got + term, at + weight.shape[0]
+        got = got.reshape(4, ROWS[part], COLS)
+        for ys in range(4):
+            out[table[Y_SLOT + ys], :, cols] = got[ys].astype(out.dtype)
+
+
+def product(part, keep, table, weights, slots):
     vmem, anywhere = pl.BlockSpec(memory_space=pltpu.VMEM), pl.BlockSpec(memory_space=pl.ANY)
-    n = len(keeps)
-    types = [jnp.float32 if keep else jnp.bfloat16 for keep in keeps]
     return pl.pallas_call(
-        functools.partial(product_kernel, part, keeps),
-        in_specs=[pl.BlockSpec(memory_space=pltpu.SMEM)] + [vmem] * 4 + [anywhere] * 4,
-        out_specs=[vmem] * n,
-        out_shape=[jax.ShapeDtypeStruct((4, HALF, 4 * COLS), t) for t in types],
-        scratch_shapes=[pltpu.VMEM((n, 4, HALF, 4 * SHARE), jnp.bfloat16), pltpu.SemaphoreType.DMA((n,))],
+        functools.partial(product_kernel, part, keep),
+        in_specs=[pl.BlockSpec(memory_space=pltpu.SMEM)] + [vmem] * 5 + [anywhere] * 4,
+        out_specs=vmem,
+        out_shape=jax.ShapeDtypeStruct((4, ROWS[part], 4 * COLS), jnp.float32 if keep else jnp.bfloat16),
+        scratch_shapes=[pltpu.VMEM((4, ROWS[part], 4 * SHARE), jnp.bfloat16), pltpu.SemaphoreType.DMA],
         compiler_params=pltpu.CompilerParams(vmem_limit_bytes=20 * MIB),
-        cost_estimate=pl.CostEstimate(flops=n * 2 * 512 * 2048 * 1024, bytes_accessed=n * 8 * MIB, transcendentals=0),
+        cost_estimate=pl.CostEstimate(flops=2 * 512 * 2048 * 1024, bytes_accessed=8 * MIB, transcendentals=0),
     )(table, *weights, *slots)
 
 
@@ -222,15 +227,16 @@
     me = lax.axis_index("group") * 16 + lax.axis_index("tp")
     table = lax.dynamic_index_in_dim(rows, me, 0, keepdims=False)
 
-    same, swapped = refit(table, master, AWAY, 2)
-    sent, mine = refit(table, master, HERE, 2)
+    same, more, swapped = refit(table, master, AWAY, (2, 2, 4))
+    sent, mine = refit(table, master, HERE, (4, 4))
     near = permute(sent, other_core)
+    swapped = permute(swapped, other_core)
     far = permute(same, other_chip)
-    swapped = permute(swapped, other_core)
-    slots = gather(activations, same, (near, swapped), far)
-    cross = permute(after(swapped, far), other_chip)
-    weights = [mine, near, far, cross]
-    ready = after(table, *slots["z"][2:], *slots["y"][2:])
+    more = permute(after(more, far), other_chip)
+    cross = permute(after(swapped, more), other_chip)
+    weights = [mine, near, far, more, cross]
+    slots = gather(activations, [(same,), (far,), (near, swapped, more)])
+    ready = after(table, *slots["z"][2:], *slots["y"][1:3])
 
     def summed(passed, kept):
         both = kept + permute(passed, other_core).astype(f32)
@@ -243,16 +249,13 @@
             got[dy] = permute(total[dy], lambda x, y, z, c: linear(x + 2 * c, y + dy, z, c))
         return jnp.stack([got[dy] for dy in range(4)])
 
-    (passed,) = product("z", [False], ready, weights, slots["z"])
-    (kept,) = product("z", [True], ready, weights, slots["z"])
-    first = summed(passed, kept)
-    ready = after(ready, first[1])
-    (passed,) = product("y", [False], ready, weights, slots["y"])
-    (kept,) = product("y", [True], ready, weights, slots["y"])
-    second = summed(passed, kept)
+    first = summed(*(product("z", keep, ready, weights, slots["z"]) for keep in (False, True)))
     came = permute(first[1], other_chip)
-    came_last = permute(after(second[1], came), other_chip)
-    own = jnp.concatenate([returned(first[0], came), returned(second[0], came_last)], axis=1)
+    ready = after(ready, came)
+    second = summed(*(product("y", keep, ready, weights, slots["y"]) for keep in (False, True)))
+    came_last = permute(second[1], other_chip)
+    z_rows = returned(first[0], came)
+    own = jnp.concatenate([z_rows, returned(after(second[0], z_rows), came_last)], axis=1)
     other = permute(own, other_core)
 
     picked = small_call(spread_kernel, [table, owner], [own, other], [(256, 2 * COLS)] * 4, pltpu.VMEM)

time: 154 us -> 160 us (1.039)
  starting transfers between devices: 53.3 us -> 65.7 us
  waiting for transfers between devices: 75.5 us -> 69.2 us
    ppermute x32 -> x33, starting transfers between devices: 53.3 us -> 65.7 us  [permute(): lax.ppermute(value, AXES, [(i, move(*coords(i))) for i in range(N_DEV)])]
    ppermute x32 -> x33, waiting for transfers between devices: 75.5 us -> 69.2 us  [permute(): lax.ppermute(value, AXES, [(i, move(*coords(i))) for i in range(N_DEV)])]
  transfers between devices with their start and end apart: 32 -> 33, of which waited for: 14 -> 17; matrix products, arithmetic and copies ran while one was open for 1% -> 1% of each run, Pallas kernels for 9% -> 8%
where the time goes in v13:
time: 160 us
  waiting for transfers between devices  69.2 us (43%)
  starting transfers between devices  65.7 us (41%)
  Pallas kernels  21.8 us (14%)
    ppermute x33, waiting for transfers between devices, permute(): lax.ppermute(value, AXES, [(i, move(*coords(i))) for i in range(N_DEV)])  69.2 us
    ppermute x33, starting transfers between devices, permute(): lax.ppermute(value, AXES, [(i, move(*coords(i))) for i in range(N_DEV)])  65.7 us
    pallas_call x4, Pallas kernels, product(): pl.pallas_call(functools.partial(product_kernel, part, keep), in_specs=[p...  13 us
    pallas_call x2, Pallas kernels, refit(): pl.pallas_call(functools.partial(refit_kernel, first), in_specs=[pl.Block...  6.55 us
  transfers between devices with their start and end apart: 33, of which 17 were waited for; matrix products, arithmetic and copies ran while one was open for 1% of the time, Pallas kernels for 8%

profile of v13, /device:TPU:3, one launch (start us, length us, event | category | flops | bytes accessed | tf_op | source)
XLA Modules:
  0.0 159.7 jit_solution(14949715353769327221)
XLA Ops:
  0.0 1.8 %collective-permute-start = (bf16[256,512]{1,0:T(8,128)(2,1)}, bf16[256,512]{1,0:T(8,128)(2,1)S(1)}, u32[]{:S(2)}, u32[]{:S(2)}) collective-permute-start(bf16[256,512]{1,0:T(8,128)(2,1)} %param.5), channel_id=1, source_target_pairs={{0,64},{1,65},{2,66},{3,67},{4,68},{5,69},{6,70},{7,71},{8,72},{9,... | collective-permute-start | bytes 786440 | tf_op jit(solution)/shard_map/ppermute | solution.py:30
  1.8 0.7 dynamic-slice_bitcast_fusion.table
  2.5 3.3 %shard_map.46 = (bf16[1024,256]{1,0:T(8,128)(2,1)S(1)}, bf16[1024,256]{1,0:T(8,128)(2,1)S(1)}, bf16[2048,256]{1,0:T(8,128)(2,1)S(1)}) custom-call(s32[32]{0:T(128)S(1)} %dynamic-slice_bitcast_fusion.table, f32[8192,256]{1,0:T(8,128)} %master.3), custom_call_target="tpu_custom_call" | custom-call | flops 6291456 | bytes 6291456 | tf_op jit(solution)/shard_map/pallas_call | solution.py:120
  5.8 1.2 collective-permute-start.3
  7.1 1.8 %collective-permute-done = bf16[256,512]{1,0:T(8,128)(2,1)S(1)} collective-permute-done((bf16[256,512]{1,0:T(8,128)(2,1)}, bf16[256,512]{1,0:T(8,128)(2,1)S(1)}, u32[]{:S(2)}, u32[]{:S(2)}) %collective-permute-start) | collective-permute-done | bytes 262176 | tf_op jit(solution)/shard_map/ppermute | solution.py:30
  9.0 2.8 %collective-permute-start.2 = (bf16[1,2,112,512]{3,2,1,0:T(8,128)(2,1)S(1)}, bf16[1,2,112,512]{3,2,1,0:T(8,128)(2,1)S(1)}, u32[]{:S(2)}, u32[]{:S(2)}) collective-permute-start(bf16[1,2,112,512]{3,2,1,0:T(8,128)(2,1)S(1)} %slice.59), channel_id=1, source_target_pairs={{0,16},{1,49},{2,18},{3,51},{4,20},{5,53},{6,22},{7,55},{8,24},{9,... | collective-permute-start | bytes 688136 | tf_op jit(solution)/shard_map/ppermute | solution.py:30
  11.8 3.8 %collective-permute-start.1 = (bf16[1,2,144,512]{3,2,1,0:T(8,128)(2,1)S(1)}, bf16[1,2,144,512]{3,2,1,0:T(8,128)(2,1)S(1)}, u32[]{:S(2)}, u32[]{:S(2)}) collective-permute-start(bf16[1,2,144,512]{3,2,1,0:T(8,128)(2,1)S(1)} %slice.58), channel_id=1, source_target_pairs={{0,2},{1,7},{2,0},{3,5},{4,6},{5,3},{6,4},{7,1},{8,10},{9,15},{10,... | collective-permute-start | bytes 884744 | tf_op jit(solution)/shard_map/ppermute | solution.py:30
  15.6 3.3 %shard_map.47 = (bf16[2048,256]{1,0:T(8,128)(2,1)S(1)}, bf16[2048,256]{1,0:T(8,128)(2,1)S(1)}) custom-call(s32[32]{0:T(128)S(1)} %dynamic-slice_bitcast_fusion.table, f32[8192,256]{1,0:T(8,128)} %master.3), custom_call_target="tpu_custom_call" | custom-call | flops 6291456 | bytes 6291456 | tf_op jit(solution)/shard_map/pallas_call | solution.py:120
  18.9 0.6 collective-permute-start.6
  19.5 0.2 collective-permute-done.1
  19.7 0.4 collective-permute-done.3.far
  20.2 1.3 collective-permute-start.5
  21.5 1.6 %collective-permute-start.4 = (bf16[2,2,144,512]{3,2,1,0:T(8,128)(2,1)S(1)}, bf16[2,2,144,512]{3,2,1,0:T(8,128)(2,1)S(1)}, u32[]{:S(2)}, u32[]{:S(2)}) collective-permute-start(bf16[2,2,144,512]{3,2,1,0:T(8,128)(2,1)S(1)} %pad_maximum_fusion.2), channel_id=1, source_target_pairs={{0,6},{1,3},{2,4},{3,1},{4,2},{5,7},{6,0},{7,5},{8,14},{9,11},{10,... | collective-permute-start | bytes 1769480 | tf_op jit(solution)/shard_map/ppermute | solution.py:30
  23.1 0.6 collective-permute-start.8
  23.7 4.1 %collective-permute-done.5 = bf16[2,2,112,512]{3,2,1,0:T(8,128)(2,1)S(1)} collective-permute-done((bf16[2,2,112,512]{3,2,1,0:T(8,128)(2,1)S(1)}, bf16[2,2,112,512]{3,2,1,0:T(8,128)(2,1)S(1)}, u32[]{:S(2)}, u32[]{:S(2)}) %collective-permute-start.5) | collective-permute-done | bytes 458784 | tf_op jit(solution)/shard_map/ppermute | solution.py:30
  27.9 2.8 %collective-permute-done.4 = bf16[2,2,144,512]{3,2,1,0:T(8,128)(2,1)S(1)} collective-permute-done((bf16[2,2,144,512]{3,2,1,0:T(8,128)(2,1)S(1)}, bf16[2,2,144,512]{3,2,1,0:T(8,128)(2,1)S(1)}, u32[]{:S(2)}, u32[]{:S(2)}) %collective-permute-start.4) | collective-permute-done | bytes 589856 | tf_op jit(solution)/shard_map/ppermute | solution.py:30
  30.7 0.1 pad_maximum_fusion.refs_0_
  30.8 0.7 collective-permute-done.8.more
  31.4 4.2 %collective-permute-start.10 = (bf16[4,2,112,512]{3,2,1,0:T(8,128)(2,1)S(1)}, bf16[4,2,112,512]{3,2,1,0:T(8,128)(2,1)S(1)}, u32[]{:S(2)}, u32[]{:S(2)}) collective-permute-start(bf16[4,2,112,512]{3,2,1,0:T(8,128)(2,1)S(1)} %pad_maximum_fusion.1.refs_0_), channel_id=1, source_target_pairs={{0,2},{1,7},{2,0},{3,5},{4,6},{5,3},{6,4},{7,1},{8,10},{9,15},{10,... | collective-permute-start | bytes 2752520 | tf_op jit(solution)/shard_map/ppermute | solution.py:30
  35.6 0.5 collective-permute-start.13
  36.1 4.7 %collective-permute-start.12 = (bf16[4,2,144,512]{3,2,1,0:T(8,128)(2,1)S(1)}, bf16[4,2,144,512]{3,2,1,0:T(8,128)(2,1)S(1)}, u32[]{:S(2)}, u32[]{:S(2)}) collective-permute-start(bf16[4,2,144,512]{3,2,1,0:T(8,128)(2,1)S(1)} %pad_maximum_fusion.refs_0_), channel_id=1, source_target_pairs={{0,16},{1,49},{2,18},{3,51},{4,20},{5,53},{6,22},{7,55},{8,24},{9,... | collective-permute-start | bytes 3538952 | tf_op jit(solution)/shard_map/ppermute | solution.py:30
  40.8 0.9 collective-permute-start.14
  41.8 1.6 %collective-permute-start.9 = (bf16[4,2,112,512]{3,2,1,0:T(8,128)(2,1)S(1)}, bf16[4,2,112,512]{3,2,1,0:T(8,128)(2,1)S(1)}, u32[]{:S(2)}, u32[]{:S(2)}) collective-permute-start(bf16[4,2,112,512]{3,2,1,0:T(8,128)(2,1)S(1)} %pad_maximum_fusion.1.refs_0_), channel_id=1, source_target_pairs={{0,6},{1,3},{2,4},{3,1},{4,2},{5,7},{6,0},{7,5},{8,14},{9,11},{10,... | collective-permute-start | bytes 2752520 | tf_op jit(solution)/shard_map/ppermute | solution.py:30
  43.4 3.6 %collective-permute-done.10.refs_1_ = bf16[4,2,112,512]{3,2,1,0:T(8,128)(2,1)S(1)} collective-permute-done((bf16[4,2,112,512]{3,2,1,0:T(8,128)(2,1)S(1)}, bf16[4,2,112,512]{3,2,1,0:T(8,128)(2,1)S(1)}, u32[]{:S(2)}, u32[]{:S(2)}) %collective-permute-start.10) | collective-permute-done | bytes 917536 | tf_op jit(solution)/shard_map/ppermute | solution.py:30
  47.0 3.9 %collective-permute-start.11 = (bf16[4,2,112,512]{3,2,1,0:T(8,128)(2,1)S(1)}, bf16[4,2,112,512]{3,2,1,0:T(8,128)(2,1)S(1)}, u32[]{:S(2)}, u32[]{:S(2)}) collective-permute-start(bf16[4,2,112,512]{3,2,1,0:T(8,128)(2,1)S(1)} %collective-permute-done.10.refs_1_), channel_id=1, source_target_pairs={{0,6},{1,3},{2,4},{3,1},{4,2},{5,7},{6,0},{7,5},{8,14},{9,11},{10,... | collective-permute-start | bytes 2752520 | tf_op jit(solution)/shard_map/ppermute | solution.py:30
  50.9 9.9 %collective-permute-done.9.refs_2_ = bf16[4,2,112,512]{3,2,1,0:T(8,128)(2,1)S(1)} collective-permute-done((bf16[4,2,112,512]{3,2,1,0:T(8,128)(2,1)S(1)}, bf16[4,2,112,512]{3,2,1,0:T(8,128)(2,1)S(1)}, u32[]{:S(2)}, u32[]{:S(2)}) %collective-permute-start.9) | collective-permute-done | bytes 917536 | tf_op jit(solution)/shard_map/ppermute | solution.py:30
  60.8 6.3 %collective-permute-done.12.refs_1_ = bf16[4,2,144,512]{3,2,1,0:T(8,128)(2,1)S(1)} collective-permute-done((bf16[4,2,144,512]{3,2,1,0:T(8,128)(2,1)S(1)}, bf16[4,2,144,512]{3,2,1,0:T(8,128)(2,1)S(1)}, u32[]{:S(2)}, u32[]{:S(2)}) %collective-permute-start.12) | collective-permute-done | bytes 1179680 | tf_op jit(solution)/shard_map/ppermute | solution.py:30
  67.1 3.5 %collective-permute-done.11.refs_3_ = bf16[4,2,112,512]{3,2,1,0:T(8,128)(2,1)S(1)} collective-permute-done((bf16[4,2,112,512]{3,2,1,0:T(8,128)(2,1)S(1)}, bf16[4,2,112,512]{3,2,1,0:T(8,128)(2,1)S(1)}, u32[]{:S(2)}, u32[]{:S(2)}) %collective-permute-start.11) | collective-permute-done | bytes 917536 | tf_op jit(solution)/shard_map/ppermute | solution.py:30
  70.6 3.0 %shard_map.49 = bf16[4,112,1024]{2,1,0:T(8,128)(2,1)S(1)} custom-call(s32[32]{0:T(128)S(1)} %dynamic-slice_bitcast_fusion.table, bf16[2048,256]{1,0:T(8,128)(2,1)S(1)} %get-tuple-element.39.mine, bf16[2048,256]{1,0:T(8,128)(2,1)S(1)} %collective-permute-done.6.near, bf16[1024,256]{1,0:T(8,128)(2,1)S(1)} %collective-permute-done.3.far, ...), custom_call_target="tpu_custom_call" | custom-call | flops 2147483648 | bytes 8388608 | tf_op jit(solution)/shard_map/pallas_call | solution.py:173
  73.6 1.7 %collective-permute-start.15 = (bf16[4,112,1024]{2,1,0:T(8,128)(2,1)S(1)}, bf16[4,112,1024]{2,1,0:T(8,128)(2,1)S(1)}, u32[]{:S(2)}, u32[]{:S(2)}) collective-permute-start(bf16[4,112,1024]{2,1,0:T(8,128)(2,1)S(1)} %shard_map.49), channel_id=1, source_target_pairs={{0,1},{1,0},{2,3},{3,2},{4,5},{5,4},{6,7},{7,6},{8,9},{9,8},{10,11... | collective-permute-start | bytes 2752520 | tf_op jit(solution)/shard_map/ppermute | solution.py:30
  75.3 0.3 collective-permute-start.21
  75.6 3.0 %shard_map.48 = f32[4,112,1024]{2,1,0:T(8,128)S(1)} custom-call(s32[32]{0:T(128)S(1)} %dynamic-slice_bitcast_fusion.table, bf16[2048,256]{1,0:T(8,128)(2,1)S(1)} %get-tuple-element.39.mine, bf16[2048,256]{1,0:T(8,128)(2,1)S(1)} %collective-permute-done.6.near, bf16[1024,256]{1,0:T(8,128)(2,1)S(1)} %collective-permute-done.3.far, ...), custom_call_target="tpu_custom_call" | custom-call | flops 2147483648 | bytes 8388608 | tf_op jit(solution)/shard_map/pallas_call | solution.py:173
  78.6 0.4 convert_add_fusion.1
  79.1 0.9 collective-permute-start.16
  79.9 7.7 %collective-permute-done.16 = bf16[4,112,512]{2,1,0:T(8,128)(2,1)S(1)} collective-permute-done((bf16[4,112,512]{2,1,0:T(8,128)(2,1)S(1)}, bf16[4,112,512]{2,1,0:T(8,128)(2,1)S(1)}, u32[]{:S(2)}, u32[]{:S(2)}) %collective-permute-start.16) | collective-permute-done | bytes 458784 | tf_op jit(solution)/shard_map/ppermute | solution.py:30
  87.6 3.0 %collective-permute-done.21.refs_3_ = bf16[4,2,144,512]{3,2,1,0:T(8,128)(2,1)S(1)} collective-permute-done((bf16[4,2,144,512]{3,2,1,0:T(8,128)(2,1)S(1)}, bf16[4,2,144,512]{3,2,1,0:T(8,128)(2,1)S(1)}, u32[]{:S(2)}, u32[]{:S(2)}) %collective-permute-start.21) | collective-permute-done | bytes 1179680 | tf_op jit(solution)/shard_map/ppermute | solution.py:30
  90.6 3.5 %shard_map.51 = bf16[4,144,1024]{2,1,0:T(8,128)(2,1)S(1)} custom-call(s32[32]{0:T(128)S(1)} %dynamic-slice_bitcast_fusion.table, bf16[2048,256]{1,0:T(8,128)(2,1)S(1)} %get-tuple-element.39.mine, bf16[2048,256]{1,0:T(8,128)(2,1)S(1)} %collective-permute-done.6.near, bf16[1024,256]{1,0:T(8,128)(2,1)S(1)} %collective-permute-done.3.far, ...), custom_call_target="tpu_custom_call" | custom-call | flops 2147483648 | bytes 8388608 | tf_op jit(solution)/shard_map/pallas_call | solution.py:173
  94.2 3.0 %collective-permute-start.22 = (bf16[4,144,1024]{2,1,0:T(8,128)(2,1)S(1)}, bf16[4,144,1024]{2,1,0:T(8,128)(2,1)S(1)}, u32[]{:S(2)}, u32[]{:S(2)}) collective-permute-start(bf16[4,144,1024]{2,1,0:T(8,128)(2,1)S(1)} %shard_map.51), channel_id=1, source_target_pairs={{0,1},{1,0},{2,3},{3,2},{4,5},{5,4},{6,7},{7,6},{8,9},{9,8},{10,11... | collective-permute-start | bytes 3538952 | tf_op jit(solution)/shard_map/ppermute | solution.py:30
  97.2 3.5 %shard_map.50 = f32[4,144,1024]{2,1,0:T(8,128)S(1)} custom-call(s32[32]{0:T(128)S(1)} %dynamic-slice_bitcast_fusion.table, bf16[2048,256]{1,0:T(8,128)(2,1)S(1)} %get-tuple-element.39.mine, bf16[2048,256]{1,0:T(8,128)(2,1)S(1)} %collective-permute-done.6.near, bf16[1024,256]{1,0:T(8,128)(2,1)S(1)} %collective-permute-done.3.far, ...), custom_call_target="tpu_custom_call" | custom-call | flops 2147483648 | bytes 8388608 | tf_op jit(solution)/shard_map/pallas_call | solution.py:173
  100.8 0.4 convert_add_fusion
  101.1 0.1 slice.85
  101.2 0.5 collective-permute-start.23
  101.7 0.2 fusion
  101.9 3.4 %collective-permute-start.17 = (bf16[112,512]{1,0:T(8,128)(2,1)S(1)}, bf16[112,512]{1,0:T(8,128)(2,1)S(1)}, u32[]{:S(2)}, u32[]{:S(2)}) collective-permute-start(bf16[112,512]{1,0:T(8,128)(2,1)S(1)} %get-tuple-element.51), channel_id=1, source_target_pairs={{0,0},{1,65},{2,2},{3,67},{4,4},{5,69},{6,6},{7,71},{8,8},{9,73},{... | collective-permute-start | bytes 344072 | tf_op jit(solution)/shard_map/ppermute | solution.py:30
  105.4 4.2 %collective-permute-start.20 = (bf16[112,512]{1,0:T(8,128)(2,1)S(1)}, bf16[112,512]{1,0:T(8,128)(2,1)S(1)}, u32[]{:S(2)}, u32[]{:S(2)}) collective-permute-start(bf16[112,512]{1,0:T(8,128)(2,1)S(1)} %get-tuple-element.52), channel_id=1, source_target_pairs={{0,48},{1,113},{2,50},{3,115},{4,52},{5,117},{6,54},{7,119},{8,56}... | collective-permute-start | bytes 344072 | tf_op jit(solution)/shard_map/ppermute | solution.py:30
  109.5 0.7 collective-permute-start.19
  110.3 6.0 %collective-permute-done.23 = bf16[4,144,512]{2,1,0:T(8,128)(2,1)S(1)} collective-permute-done((bf16[4,144,512]{2,1,0:T(8,128)(2,1)S(1)}, bf16[4,144,512]{2,1,0:T(8,128)(2,1)S(1)}, u32[]{:S(2)}, u32[]{:S(2)}) %collective-permute-start.23) | collective-permute-done | bytes 589856 | tf_op jit(solution)/shard_map/ppermute | solution.py:30
  116.3 0.2 add_convert_fusion
  116.5 2.6 %collective-permute-start.24 = (bf16[144,512]{1,0:T(8,128)(2,1)S(1)}, bf16[144,512]{1,0:T(8,128)(2,1)S(1)}, u32[]{:S(2)}, u32[]{:S(2)}) collective-permute-start(bf16[144,512]{1,0:T(8,128)(2,1)S(1)} %get-tuple-element.47), channel_id=1, source_target_pairs={{0,0},{1,65},{2,2},{3,67},{4,4},{5,69},{6,6},{7,71},{8,8},{9,73},{... | collective-permute-start | bytes 442376 | tf_op jit(solution)/shard_map/ppermute | solution.py:30
  119.1 5.0 %collective-permute-start.27 = (bf16[144,512]{1,0:T(8,128)(2,1)S(1)}, bf16[144,512]{1,0:T(8,128)(2,1)S(1)}, u32[]{:S(2)}, u32[]{:S(2)}) collective-permute-start(bf16[144,512]{1,0:T(8,128)(2,1)S(1)} %get-tuple-element.48), channel_id=1, source_target_pairs={{0,48},{1,113},{2,50},{3,115},{4,52},{5,117},{6,54},{7,119},{8,56}... | collective-permute-start | bytes 442376 | tf_op jit(solution)/shard_map/ppermute | solution.py:30
  124.1 0.5 collective-permute-start.26
  124.6 3.2 %collective-permute-start.25 = (bf16[144,512]{1,0:T(8,128)(2,1)S(1)}, bf16[144,512]{1,0:T(8,128)(2,1)S(1)}, u32[]{:S(2)}, u32[]{:S(2)}) collective-permute-start(bf16[144,512]{1,0:T(8,128)(2,1)S(1)} %get-tuple-element.50), channel_id=1, source_target_pairs={{0,16},{1,81},{2,18},{3,83},{4,20},{5,85},{6,22},{7,87},{8,24},{9,... | collective-permute-start | bytes 442376 | tf_op jit(solution)/shard_map/ppermute | solution.py:30
  127.8 1.8 %collective-permute-start.18 = (bf16[112,512]{1,0:T(8,128)(2,1)S(1)}, bf16[112,512]{1,0:T(8,128)(2,1)S(1)}, u32[]{:S(2)}, u32[]{:S(2)}) collective-permute-start(bf16[112,512]{1,0:T(8,128)(2,1)S(1)} %get-tuple-element.54), channel_id=1, source_target_pairs={{0,16},{1,81},{2,18},{3,83},{4,20},{5,85},{6,22},{7,87},{8,24},{9,... | collective-permute-start | bytes 344072 | tf_op jit(solution)/shard_map/ppermute | solution.py:30
  129.6 5.5 %collective-permute-done.18 = bf16[112,512]{1,0:T(8,128)(2,1)S(1)} collective-permute-done((bf16[112,512]{1,0:T(8,128)(2,1)S(1)}, bf16[112,512]{1,0:T(8,128)(2,1)S(1)}, u32[]{:S(2)}, u32[]{:S(2)}) %collective-permute-start.18) | collective-permute-done | bytes 114720 | tf_op jit(solution)/shard_map/ppermute | solution.py:30
  135.1 0.1 collective-permute-start.28
  135.2 2.6 %collective-permute-done.28.other = bf16[4,256,512]{2,1,0:T(8,128)(2,1)S(1)} collective-permute-done((bf16[4,256,512]{2,1,0:T(8,128)(2,1)S(1)}, bf16[4,256,512]{2,1,0:T(8,128)(2,1)S(1)}, u32[]{:S(2)}, u32[]{:S(2)}) %collective-permute-start.28) | collective-permute-done | bytes 1048608 | tf_op jit(solution)/shard_map/ppermute | solution.py:30
  137.9 0.7 shard_map.52
  138.6 2.5 %collective-permute-start.29 = (bf16[256,512]{1,0:T(8,128)(2,1)S(1)}, bf16[256,512]{1,0:T(8,128)(2,1)S(1)}, u32[]{:S(2)}, u32[]{:S(2)}) collective-permute-start(bf16[256,512]{1,0:T(8,128)(2,1)S(1)} %get-tuple-element.43), channel_id=1, source_target_pairs={{0,0},{1,8},{2,2},{3,10},{4,4},{5,12},{6,6},{7,14},{8,9},{9,1},{10... | collective-permute-start | bytes 786440 | tf_op jit(solution)/shard_map/ppermute | solution.py:30
  141.1 1.3 collective-permute-start.30
  142.4 3.6 %collective-permute-start.31 = (bf16[256,512]{1,0:T(8,128)(2,1)S(1)}, bf16[256,512]{1,0:T(8,128)(2,1)S(1)}, u32[]{:S(2)}, u32[]{:S(2)}) collective-permute-start(bf16[256,512]{1,0:T(8,128)(2,1)S(1)} %get-tuple-element.45), channel_id=1, source_target_pairs={{0,4},{1,12},{2,6},{3,14},{4,0},{5,8},{6,2},{7,10},{8,13},{9,5},{1... | collective-permute-start | bytes 786440 | tf_op jit(solution)/shard_map/ppermute | solution.py:30
  146.0 0.8 collective-permute-start.32
  146.9 1.3 collective-permute-done.30.refs_1_
  148.2 9.8 %collective-permute-done.31.refs_2_ = bf16[256,512]{1,0:T(8,128)(2,1)S(1)} collective-permute-done((bf16[256,512]{1,0:T(8,128)(2,1)S(1)}, bf16[256,512]{1,0:T(8,128)(2,1)S(1)}, u32[]{:S(2)}, u32[]{:S(2)}) %collective-permute-start.31) | collective-permute-done | bytes 262176 | tf_op jit(solution)/shard_map/ppermute | solution.py:30
  158.0 1.5 shard_map.53
  (32 shorter events, 0.6 us)
Async XLA Ops:
  0.0 8.9 %collective-permute-start = (bf16[256,512]{1,0:T(8,128)(2,1)}, bf16[256,512]{1,0:T(8,128)(2,1)S(1)}, u32[]{:S(2)}, u32[]{:S(2)}) collective-permute-start(bf16[256,512]{1,0:T(8,128)(2,1)} %param.5), channel_id=1, source_target_pairs={{0,64},{1,65},{2,66},{3,67},{4,68},{5,69},{6,70},{7,71},{8,72},{9,... | collective-permute-start | bytes 786440 | tf_op jit(solution)/shard_map/ppermute | solution.py:30
  2.5 6.4 %copy-start.1 = (bf16[256,512]{1,0:T(8,128)(2,1)S(1)}, bf16[256,512]{1,0:T(8,128)(2,1)}, u32[]{:S(2)}) copy-start(bf16[256,512]{1,0:T(8,128)(2,1)} %param.5) | copy-start | bytes 786436
  5.8 14.3 %collective-permute-start.3 = (bf16[1024,256]{1,0:T(8,128)(2,1)S(1)}, bf16[1024,256]{1,0:T(8,128)(2,1)S(1)}, u32[]{:S(2)}, u32[]{:S(2)}) collective-permute-start(bf16[1024,256]{1,0:T(8,128)(2,1)S(1)} %get-tuple-element.26), channel_id=1, source_target_pairs={{0,8},{1,9},{2,10},{3,11},{4,12},{5,13},{6,14},{7,15},{8,0},{9,1},... | collective-permute-start | bytes 1572872 | tf_op jit(solution)/shard_map/ppermute | solution.py:30
  9.0 10.4 %collective-permute-start.2 = (bf16[1,2,112,512]{3,2,1,0:T(8,128)(2,1)S(1)}, bf16[1,2,112,512]{3,2,1,0:T(8,128)(2,1)S(1)}, u32[]{:S(2)}, u32[]{:S(2)}) collective-permute-start(bf16[1,2,112,512]{3,2,1,0:T(8,128)(2,1)S(1)} %slice.59), channel_id=1, source_target_pairs={{0,16},{1,49},{2,18},{3,51},{4,20},{5,53},{6,22},{7,55},{8,24},{9,... | collective-permute-start | bytes 688136 | tf_op jit(solution)/shard_map/ppermute | solution.py:30
  11.8 7.9 %collective-permute-start.1 = (bf16[1,2,144,512]{3,2,1,0:T(8,128)(2,1)S(1)}, bf16[1,2,144,512]{3,2,1,0:T(8,128)(2,1)S(1)}, u32[]{:S(2)}, u32[]{:S(2)}) collective-permute-start(bf16[1,2,144,512]{3,2,1,0:T(8,128)(2,1)S(1)} %slice.58), channel_id=1, source_target_pairs={{0,2},{1,7},{2,0},{3,5},{4,6},{5,3},{6,4},{7,1},{8,10},{9,15},{10,... | collective-permute-start | bytes 884744 | tf_op jit(solution)/shard_map/ppermute | solution.py:30
  15.6 15.8 %collective-permute-start.7 = (bf16[2048,256]{1,0:T(8,128)(2,1)S(1)}, bf16[2048,256]{1,0:T(8,128)(2,1)S(1)}, u32[]{:S(2)}, u32[]{:S(2)}) collective-permute-start(bf16[2048,256]{1,0:T(8,128)(2,1)S(1)} %get-tuple-element.33), channel_id=1, source_target_pairs={{0,1},{1,0},{2,3},{3,2},{4,5},{5,4},{6,7},{7,6},{8,9},{9,8},{10,11... | collective-permute-start | bytes 3145736 | tf_op jit(solution)/shard_map/ppermute | solution.py:30
  18.9 12.6 %collective-permute-start.6 = (bf16[2048,256]{1,0:T(8,128)(2,1)S(1)}, bf16[2048,256]{1,0:T(8,128)(2,1)S(1)}, u32[]{:S(2)}, u32[]{:S(2)}) collective-permute-start(bf16[2048,256]{1,0:T(8,128)(2,1)S(1)} %get-tuple-element.32), channel_id=1, source_target_pairs={{0,1},{1,0},{2,3},{3,2},{4,5},{5,4},{6,7},{7,6},{8,9},{9,8},{10,11... | collective-permute-start | bytes 3145736 | tf_op jit(solution)/shard_map/ppermute | solution.py:30
  20.2 7.6 %collective-permute-start.5 = (bf16[2,2,112,512]{3,2,1,0:T(8,128)(2,1)S(1)}, bf16[2,2,112,512]{3,2,1,0:T(8,128)(2,1)S(1)}, u32[]{:S(2)}, u32[]{:S(2)}) collective-permute-start(bf16[2,2,112,512]{3,2,1,0:T(8,128)(2,1)S(1)} %pad_maximum_fusion.3), channel_id=1, source_target_pairs={{0,48},{1,17},{2,50},{3,19},{4,52},{5,21},{6,54},{7,23},{8,56},{9,... | collective-permute-start | bytes 1376264 | tf_op jit(solution)/shard_map/ppermute | solution.py:30
  21.5 9.2 %collective-permute-start.4 = (bf16[2,2,144,512]{3,2,1,0:T(8,128)(2,1)S(1)}, bf16[2,2,144,512]{3,2,1,0:T(8,128)(2,1)S(1)}, u32[]{:S(2)}, u32[]{:S(2)}) collective-permute-start(bf16[2,2,144,512]{3,2,1,0:T(8,128)(2,1)S(1)} %pad_maximum_fusion.2), channel_id=1, source_target_pairs={{0,6},{1,3},{2,4},{3,1},{4,2},{5,7},{6,0},{7,5},{8,14},{9,11},{10,... | collective-permute-start | bytes 1769480 | tf_op jit(solution)/shard_map/ppermute | solution.py:30
  23.1 8.3 %collective-permute-start.8 = (bf16[1024,256]{1,0:T(8,128)(2,1)S(1)}, bf16[1024,256]{1,0:T(8,128)(2,1)S(1)}, u32[]{:S(2)}, u32[]{:S(2)}) collective-permute-start(bf16[1024,256]{1,0:T(8,128)(2,1)S(1)} %get-tuple-element.35), channel_id=1, source_target_pairs={{0,8},{1,9},{2,10},{3,11},{4,12},{5,13},{6,14},{7,15},{8,0},{9,1},... | collective-permute-start | bytes 1572872 | tf_op jit(solution)/shard_map/ppermute | solution.py:30
  31.4 15.6 %collective-permute-start.10 = (bf16[4,2,112,512]{3,2,1,0:T(8,128)(2,1)S(1)}, bf16[4,2,112,512]{3,2,1,0:T(8,128)(2,1)S(1)}, u32[]{:S(2)}, u32[]{:S(2)}) collective-permute-start(bf16[4,2,112,512]{3,2,1,0:T(8,128)(2,1)S(1)} %pad_maximum_fusion.1.refs_0_), channel_id=1, source_target_pairs={{0,2},{1,7},{2,0},{3,5},{4,6},{5,3},{6,4},{7,1},{8,10},{9,15},{10,... | collective-permute-start | bytes 2752520 | tf_op jit(solution)/shard_map/ppermute | solution.py:30
  35.6 25.2 %collective-permute-start.13 = (bf16[4,2,144,512]{3,2,1,0:T(8,128)(2,1)S(1)}, bf16[4,2,144,512]{3,2,1,0:T(8,128)(2,1)S(1)}, u32[]{:S(2)}, u32[]{:S(2)}) collective-permute-start(bf16[4,2,144,512]{3,2,1,0:T(8,128)(2,1)S(1)} %pad_maximum_fusion.refs_0_), channel_id=1, source_target_pairs={{0,48},{1,17},{2,50},{3,19},{4,52},{5,21},{6,54},{7,23},{8,56},{9,... | collective-permute-start | bytes 3538952 | tf_op jit(solution)/shard_map/ppermute | solution.py:30
  36.1 31.0 %collective-permute-start.12 = (bf16[4,2,144,512]{3,2,1,0:T(8,128)(2,1)S(1)}, bf16[4,2,144,512]{3,2,1,0:T(8,128)(2,1)S(1)}, u32[]{:S(2)}, u32[]{:S(2)}) collective-permute-start(bf16[4,2,144,512]{3,2,1,0:T(8,128)(2,1)S(1)} %pad_maximum_fusion.refs_0_), channel_id=1, source_target_pairs={{0,16},{1,49},{2,18},{3,51},{4,20},{5,53},{6,22},{7,55},{8,24},{9,... | collective-permute-start | bytes 3538952 | tf_op jit(solution)/shard_map/ppermute | solution.py:30
  40.8 29.8 %collective-permute-start.14 = (bf16[2048,256]{1,0:T(8,128)(2,1)S(1)}, bf16[2048,256]{1,0:T(8,128)(2,1)S(1)}, u32[]{:S(2)}, u32[]{:S(2)}) collective-permute-start(bf16[2048,256]{1,0:T(8,128)(2,1)S(1)} %collective-permute-done.7), channel_id=1, source_target_pairs={{0,8},{1,9},{2,10},{3,11},{4,12},{5,13},{6,14},{7,15},{8,0},{9,1},... | collective-permute-start | bytes 3145736 | tf_op jit(solution)/shard_map/ppermute | solution.py:30
  41.8 19.0 %collective-permute-start.9 = (bf16[4,2,112,512]{3,2,1,0:T(8,128)(2,1)S(1)}, bf16[4,2,112,512]{3,2,1,0:T(8,128)(2,1)S(1)}, u32[]{:S(2)}, u32[]{:S(2)}) collective-permute-start(bf16[4,2,112,512]{3,2,1,0:T(8,128)(2,1)S(1)} %pad_maximum_fusion.1.refs_0_), channel_id=1, source_target_pairs={{0,6},{1,3},{2,4},{3,1},{4,2},{5,7},{6,0},{7,5},{8,14},{9,11},{10,... | collective-permute-start | bytes 2752520 | tf_op jit(solution)/shard_map/ppermute | solution.py:30
  47.0 23.6 %collective-permute-start.11 = (bf16[4,2,112,512]{3,2,1,0:T(8,128)(2,1)S(1)}, bf16[4,2,112,512]{3,2,1,0:T(8,128)(2,1)S(1)}, u32[]{:S(2)}, u32[]{:S(2)}) collective-permute-start(bf16[4,2,112,512]{3,2,1,0:T(8,128)(2,1)S(1)} %collective-permute-done.10.refs_1_), channel_id=1, source_target_pairs={{0,6},{1,3},{2,4},{3,1},{4,2},{5,7},{6,0},{7,5},{8,14},{9,11},{10,... | collective-permute-start | bytes 2752520 | tf_op jit(solution)/shard_map/ppermute | solution.py:30
  73.6 5.0 %collective-permute-start.15 = (bf16[4,112,1024]{2,1,0:T(8,128)(2,1)S(1)}, bf16[4,112,1024]{2,1,0:T(8,128)(2,1)S(1)}, u32[]{:S(2)}, u32[]{:S(2)}) collective-permute-start(bf16[4,112,1024]{2,1,0:T(8,128)(2,1)S(1)} %shard_map.49), channel_id=1, source_target_pairs={{0,1},{1,0},{2,3},{3,2},{4,5},{5,4},{6,7},{7,6},{8,9},{9,8},{10,11... | collective-permute-start | bytes 2752520 | tf_op jit(solution)/shard_map/ppermute | solution.py:30
  75.3 15.3 %collective-permute-start.21 = (bf16[4,2,144,512]{3,2,1,0:T(8,128)(2,1)S(1)}, bf16[4,2,144,512]{3,2,1,0:T(8,128)(2,1)S(1)}, u32[]{:S(2)}, u32[]{:S(2)}) collective-permute-start(bf16[4,2,144,512]{3,2,1,0:T(8,128)(2,1)S(1)} %collective-permute-done.12.refs_1_), channel_id=1, source_target_pairs={{0,48},{1,17},{2,50},{3,19},{4,52},{5,21},{6,54},{7,23},{8,56},{9,... | collective-permute-start | bytes 3538952 | tf_op jit(solution)/shard_map/ppermute | solution.py:30
  79.1 8.5 %collective-permute-start.16 = (bf16[4,112,512]{2,1,0:T(8,128)(2,1)S(1)}, bf16[4,112,512]{2,1,0:T(8,128)(2,1)S(1)}, u32[]{:S(2)}, u32[]{:S(2)}) collective-permute-start(bf16[4,112,512]{2,1,0:T(8,128)(2,1)S(1)} %slice.86), channel_id=1, source_target_pairs={{0,8},{1,9},{2,10},{3,11},{4,12},{5,13},{6,14},{7,15},{8,0},{9,1},... | collective-permute-start | bytes 1376264 | tf_op jit(solution)/shard_map/ppermute | solution.py:30
  94.2 6.6 %collective-permute-start.22 = (bf16[4,144,1024]{2,1,0:T(8,128)(2,1)S(1)}, bf16[4,144,1024]{2,1,0:T(8,128)(2,1)S(1)}, u32[]{:S(2)}, u32[]{:S(2)}) collective-permute-start(bf16[4,144,1024]{2,1,0:T(8,128)(2,1)S(1)} %shard_map.51), channel_id=1, source_target_pairs={{0,1},{1,0},{2,3},{3,2},{4,5},{5,4},{6,7},{7,6},{8,9},{9,8},{10,11... | collective-permute-start | bytes 3538952 | tf_op jit(solution)/shard_map/ppermute | solution.py:30
  101.2 15.0 %collective-permute-start.23 = (bf16[4,144,512]{2,1,0:T(8,128)(2,1)S(1)}, bf16[4,144,512]{2,1,0:T(8,128)(2,1)S(1)}, u32[]{:S(2)}, u32[]{:S(2)}) collective-permute-start(bf16[4,144,512]{2,1,0:T(8,128)(2,1)S(1)} %slice.85), channel_id=1, source_target_pairs={{0,8},{1,9},{2,10},{3,11},{4,12},{5,13},{6,14},{7,15},{8,0},{9,1},... | collective-permute-start | bytes 1769480 | tf_op jit(solution)/shard_map/ppermute | solution.py:30
  101.9 22.2 %collective-permute-start.17 = (bf16[112,512]{1,0:T(8,128)(2,1)S(1)}, bf16[112,512]{1,0:T(8,128)(2,1)S(1)}, u32[]{:S(2)}, u32[]{:S(2)}) collective-permute-start(bf16[112,512]{1,0:T(8,128)(2,1)S(1)} %get-tuple-element.51), channel_id=1, source_target_pairs={{0,0},{1,65},{2,2},{3,67},{4,4},{5,69},{6,6},{7,71},{8,8},{9,73},{... | collective-permute-start | bytes 344072 | tf_op jit(solution)/shard_map/ppermute | solution.py:30
  105.4 19.3 %collective-permute-start.20 = (bf16[112,512]{1,0:T(8,128)(2,1)S(1)}, bf16[112,512]{1,0:T(8,128)(2,1)S(1)}, u32[]{:S(2)}, u32[]{:S(2)}) collective-permute-start(bf16[112,512]{1,0:T(8,128)(2,1)S(1)} %get-tuple-element.52), channel_id=1, source_target_pairs={{0,48},{1,113},{2,50},{3,115},{4,52},{5,117},{6,54},{7,119},{8,56}... | collective-permute-start | bytes 344072 | tf_op jit(solution)/shard_map/ppermute | solution.py:30
  109.5 18.3 %collective-permute-start.19 = (bf16[112,512]{1,0:T(8,128)(2,1)S(1)}, bf16[112,512]{1,0:T(8,128)(2,1)S(1)}, u32[]{:S(2)}, u32[]{:S(2)}) collective-permute-start(bf16[112,512]{1,0:T(8,128)(2,1)S(1)} %get-tuple-element.53), channel_id=1, source_target_pairs={{0,32},{1,97},{2,34},{3,99},{4,36},{5,101},{6,38},{7,103},{8,40},{... | collective-permute-start | bytes 344072 | tf_op jit(solution)/shard_map/ppermute | solution.py:30
  116.5 21.4 %copy-start = (s32[8]{0:T(128)S(1)}, s32[8]{0:T(128)}, u32[]{:S(2)}) copy-start(s32[8]{0:T(128)} %owner.1) | copy-start | bytes 100
  116.5 18.5 %collective-permute-start.24 = (bf16[144,512]{1,0:T(8,128)(2,1)S(1)}, bf16[144,512]{1,0:T(8,128)(2,1)S(1)}, u32[]{:S(2)}, u32[]{:S(2)}) collective-permute-start(bf16[144,512]{1,0:T(8,128)(2,1)S(1)} %get-tuple-element.47), channel_id=1, source_target_pairs={{0,0},{1,65},{2,2},{3,67},{4,4},{5,69},{6,6},{7,71},{8,8},{9,73},{... | collective-permute-start | bytes 442376 | tf_op jit(solution)/shard_map/ppermute | solution.py:30
  119.1 16.0 %collective-permute-start.27 = (bf16[144,512]{1,0:T(8,128)(2,1)S(1)}, bf16[144,512]{1,0:T(8,128)(2,1)S(1)}, u32[]{:S(2)}, u32[]{:S(2)}) collective-permute-start(bf16[144,512]{1,0:T(8,128)(2,1)S(1)} %get-tuple-element.48), channel_id=1, source_target_pairs={{0,48},{1,113},{2,50},{3,115},{4,52},{5,117},{6,54},{7,119},{8,56}... | collective-permute-start | bytes 442376 | tf_op jit(solution)/shard_map/ppermute | solution.py:30
  124.1 10.9 %collective-permute-start.26 = (bf16[144,512]{1,0:T(8,128)(2,1)S(1)}, bf16[144,512]{1,0:T(8,128)(2,1)S(1)}, u32[]{:S(2)}, u32[]{:S(2)}) collective-permute-start(bf16[144,512]{1,0:T(8,128)(2,1)S(1)} %get-tuple-element.49), channel_id=1, source_target_pairs={{0,32},{1,97},{2,34},{3,99},{4,36},{5,101},{6,38},{7,103},{8,40},{... | collective-permute-start | bytes 442376 | tf_op jit(solution)/shard_map/ppermute | solution.py:30
  124.6 10.4 %collective-permute-start.25 = (bf16[144,512]{1,0:T(8,128)(2,1)S(1)}, bf16[144,512]{1,0:T(8,128)(2,1)S(1)}, u32[]{:S(2)}, u32[]{:S(2)}) collective-permute-start(bf16[144,512]{1,0:T(8,128)(2,1)S(1)} %get-tuple-element.50), channel_id=1, source_target_pairs={{0,16},{1,81},{2,18},{3,83},{4,20},{5,85},{6,22},{7,87},{8,24},{9,... | collective-permute-start | bytes 442376 | tf_op jit(solution)/shard_map/ppermute | solution.py:30
  127.8 7.3 %collective-permute-start.18 = (bf16[112,512]{1,0:T(8,128)(2,1)S(1)}, bf16[112,512]{1,0:T(8,128)(2,1)S(1)}, u32[]{:S(2)}, u32[]{:S(2)}) collective-permute-start(bf16[112,512]{1,0:T(8,128)(2,1)S(1)} %get-tuple-element.54), channel_id=1, source_target_pairs={{0,16},{1,81},{2,18},{3,83},{4,20},{5,85},{6,22},{7,87},{8,24},{9,... | collective-permute-start | bytes 344072 | tf_op jit(solution)/shard_map/ppermute | solution.py:30
  135.1 2.7 %collective-permute-start.28 = (bf16[4,256,512]{2,1,0:T(8,128)(2,1)S(1)}, bf16[4,256,512]{2,1,0:T(8,128)(2,1)S(1)}, u32[]{:S(2)}, u32[]{:S(2)}) collective-permute-start(bf16[4,256,512]{2,1,0:T(8,128)(2,1)S(1)} %maximum_maximum_fusion.own), channel_id=1, source_target_pairs={{0,1},{1,0},{2,3},{3,2},{4,5},{5,4},{6,7},{7,6},{8,9},{9,8},{10,11... | collective-permute-start | bytes 3145736 | tf_op jit(solution)/shard_map/ppermute | solution.py:30
  138.6 8.3 %collective-permute-start.29 = (bf16[256,512]{1,0:T(8,128)(2,1)S(1)}, bf16[256,512]{1,0:T(8,128)(2,1)S(1)}, u32[]{:S(2)}, u32[]{:S(2)}) collective-permute-start(bf16[256,512]{1,0:T(8,128)(2,1)S(1)} %get-tuple-element.43), channel_id=1, source_target_pairs={{0,0},{1,8},{2,2},{3,10},{4,4},{5,12},{6,6},{7,14},{8,9},{9,1},{10... | collective-permute-start | bytes 786440 | tf_op jit(solution)/shard_map/ppermute | solution.py:30
  141.1 7.1 %collective-permute-start.30 = (bf16[256,512]{1,0:T(8,128)(2,1)S(1)}, bf16[256,512]{1,0:T(8,128)(2,1)S(1)}, u32[]{:S(2)}, u32[]{:S(2)}) collective-permute-start(bf16[256,512]{1,0:T(8,128)(2,1)S(1)} %get-tuple-element.44), channel_id=1, source_target_pairs={{0,2},{1,10},{2,4},{3,12},{4,6},{5,14},{6,0},{7,8},{8,11},{9,3},{1... | collective-permute-start | bytes 786440 | tf_op jit(solution)/shard_map/ppermute | solution.py:30
  142.4 15.6 %collective-permute-start.31 = (bf16[256,512]{1,0:T(8,128)(2,1)S(1)}, bf16[256,512]{1,0:T(8,128)(2,1)S(1)}, u32[]{:S(2)}, u32[]{:S(2)}) collective-permute-start(bf16[256,512]{1,0:T(8,128)(2,1)S(1)} %get-tuple-element.45), channel_id=1, source_target_pairs={{0,4},{1,12},{2,6},{3,14},{4,0},{5,8},{6,2},{7,10},{8,13},{9,5},{1... | collective-permute-start | bytes 786440 | tf_op jit(solution)/shard_map/ppermute | solution.py:30
  146.0 12.0 %collective-permute-start.32 = (bf16[256,512]{1,0:T(8,128)(2,1)S(1)}, bf16[256,512]{1,0:T(8,128)(2,1)S(1)}, u32[]{:S(2)}, u32[]{:S(2)}) collective-permute-start(bf16[256,512]{1,0:T(8,128)(2,1)S(1)} %get-tuple-element.46), channel_id=1, source_target_pairs={{0,6},{1,14},{2,0},{3,8},{4,2},{5,10},{6,4},{7,12},{8,15},{9,7},{1... | collective-permute-start | bytes 786440 | tf_op jit(solution)/shard_map/ppermute | solution.py:30

commit v14 on v11

--- a/solution.py
+++ b/solution.py
@@ -141,34 +141,36 @@
     return [(mine, cols(0, core)), (near, cols(0, 1 - core)), (far, cols(2 * COLS, core)), (cross, cols(2 * COLS, 1 - core))]
 
 
-def product_kernel(part, half_of, table, mine, near, far, cross, *refs):
-    slots, (out, held, sems) = refs[:4], refs[4:]
+def product_kernel(part, keep, table, mine, near, far, cross, *refs):
+    slots, out = refs[:4], refs[4]
     core = table[CORE]
-    half = half_of(core)
-    for i, slot in enumerate(slots):
-        for k in range(4):
-            zs = k if part == "y" else i
-            depth = pl.ds(pl.multiple_of(table[Z_SLOT + zs] * SHARE, SHARE), SHARE)
-            to = held.at[i if part == "y" else k, :, depth]
-            pltpu.make_async_copy(slot.at[k, half], to, sems.at[i]).start()
-    for i in range(4):
-        pltpu.make_async_copy(held.at[i], held.at[i], sems.at[i]).wait()
-    acts = held[...].reshape(4 * HALF, 4 * SHARE)
-    for weight, cols in pieces(core, mine, near, far, cross):
-        got = jnp.dot(acts, weight[...], preferred_element_type=jnp.float32).reshape(4, HALF, COLS)
+    half = core if keep else 1 - core
+    weights = pieces(core, mine, near, far, cross)
+    chunks = []
+    for n in range(4):
+        if part == "y":
+            rows = jnp.concatenate([slot[n, half] for slot in slots])
+        else:
+            rows = slots[n][:, half].reshape(4 * HALF, SHARE)
+        chunks.append((rows, pl.ds(pl.multiple_of(table[Z_SLOT + n] * SHARE, SHARE), SHARE)))
+    for weight, cols in weights:
+        got = None
+        for rows, depth in chunks:
+            term = jnp.dot(rows, weight[depth, :], preferred_element_type=jnp.float32)
+            got = term if got is None else got + term
+        got = got.reshape(4, HALF, COLS)
         for ys in range(4):
             out[table[Y_SLOT + ys], :, cols] = got[ys].astype(out.dtype)
 
 
 def product(part, keep, table, weights, slots):
-    vmem, anywhere = pl.BlockSpec(memory_space=pltpu.VMEM), pl.BlockSpec(memory_space=pl.ANY)
+    vmem = pl.BlockSpec(memory_space=pltpu.VMEM)
     return pl.pallas_call(
-        functools.partial(product_kernel, part, (lambda core: core) if keep else (lambda core: 1 - core)),
-        in_specs=[pl.BlockSpec(memory_space=pltpu.SMEM)] + [vmem] * 4 + [anywhere] * 4,
+        functools.partial(product_kernel, part, keep),
+        in_specs=[pl.BlockSpec(memory_space=pltpu.SMEM)] + [vmem] * 8,
         out_specs=vmem,
         out_shape=jax.ShapeDtypeStruct((4, HALF, 4 * COLS), jnp.float32 if keep else jnp.bfloat16),
-        scratch_shapes=[pltpu.VMEM((4, HALF, 4 * SHARE), jnp.bfloat16), pltpu.SemaphoreType.DMA((4,))],
-        compiler_params=pltpu.CompilerParams(vmem_limit_bytes=20 * MIB),
+        compiler_params=pltpu.CompilerParams(vmem_limit_bytes=24 * MIB),
         cost_estimate=pl.CostEstimate(flops=2 * 512 * 2048 * 1024, bytes_accessed=8 * MIB, transcendentals=0),
     )(table, *weights, *slots)
 

time: 152 us -> 151 us (level)
  transfers between devices with their start and end apart: 37 -> 37, of which waited for: 17 -> 17; matrix products, arithmetic and copies ran while one was open for 2% -> 2% of each run, Pallas kernels for 14% -> 13%
where the time goes in v14:
time: 151 us
  waiting for transfers between devices  68.5 us (45%)
  starting transfers between devices  58.1 us (38%)
  Pallas kernels  21.3 us (14%)
  other arithmetic  1.68 us (1%)
    ppermute x37, waiting for transfers between devices, permute(): lax.ppermute(value, AXES, [(i, move(*coords(i))) for i in range(N_DEV)])  68.5 us
    ppermute x37, starting transfers between devices, permute(): lax.ppermute(value, AXES, [(i, move(*coords(i))) for i in range(N_DEV)])  58.1 us
    pallas_call x4, Pallas kernels, product(): pl.pallas_call(functools.partial(product_kernel, part, keep), in_specs=[p...  11.8 us
    pallas_call x2, Pallas kernels, refit(): pl.pallas_call(functools.partial(refit_kernel, first), in_specs=[pl.Block...  6.55 us
  transfers between devices with their start and end apart: 37, of which 17 were waited for; matrix products, arithmetic and copies ran while one was open for 2% of the time, Pallas kernels for 13%

profile of v14, /device:TPU:3, one launch (start us, length us, event | category | flops | bytes accessed | tf_op | source)
XLA Modules:
  0.0 150.9 jit_solution(1664972982952198468)
XLA Ops:
  0.0 1.8 %collective-permute-start = (bf16[256,512]{1,0:T(8,128)(2,1)}, bf16[256,512]{1,0:T(8,128)(2,1)S(1)}, u32[]{:S(2)}, u32[]{:S(2)}) collective-permute-start(bf16[256,512]{1,0:T(8,128)(2,1)} %param.5), channel_id=1, source_target_pairs={{0,64},{1,65},{2,66},{3,67},{4,68},{5,69},{6,70},{7,71},{8,72},{9,... | collective-permute-start | bytes 786440 | tf_op jit(solution)/shard_map/ppermute | solution.py:30
  1.8 0.7 dynamic-slice_bitcast_fusion.table
  2.5 3.3 %shard_map.46 = (bf16[2048,256]{1,0:T(8,128)(2,1)S(1)}, bf16[2048,256]{1,0:T(8,128)(2,1)S(1)}) custom-call(s32[32]{0:T(128)S(1)} %dynamic-slice_bitcast_fusion.table, f32[8192,256]{1,0:T(8,128)} %master.3), custom_call_target="tpu_custom_call" | custom-call | flops 6291456 | bytes 6291456 | tf_op jit(solution)/shard_map/pallas_call | solution.py:122
  5.8 3.1 %collective-permute-done = bf16[256,512]{1,0:T(8,128)(2,1)S(1)} collective-permute-done((bf16[256,512]{1,0:T(8,128)(2,1)}, bf16[256,512]{1,0:T(8,128)(2,1)S(1)}, u32[]{:S(2)}, u32[]{:S(2)}) %collective-permute-start) | collective-permute-done | bytes 262176 | tf_op jit(solution)/shard_map/ppermute | solution.py:30
  8.9 3.8 %collective-permute-start.1 = (bf16[1,2,128,512]{3,2,1,0:T(8,128)(2,1)S(1)}, bf16[1,2,128,512]{3,2,1,0:T(8,128)(2,1)S(1)}, u32[]{:S(2)}, u32[]{:S(2)}) collective-permute-start(bf16[1,2,128,512]{3,2,1,0:T(8,128)(2,1)S(1)} %get-tuple-element.34), channel_id=1, source_target_pairs={{0,2},{1,7},{2,0},{3,5},{4,6},{5,3},{6,4},{7,1},{8,10},{9,15},{10,... | collective-permute-start | bytes 786440 | tf_op jit(solution)/shard_map/ppermute | solution.py:30
  12.8 2.7 %collective-permute-start.2 = (bf16[1,2,128,512]{3,2,1,0:T(8,128)(2,1)S(1)}, bf16[1,2,128,512]{3,2,1,0:T(8,128)(2,1)S(1)}, u32[]{:S(2)}, u32[]{:S(2)}) collective-permute-start(bf16[1,2,128,512]{3,2,1,0:T(8,128)(2,1)S(1)} %get-tuple-element.35), channel_id=1, source_target_pairs={{0,16},{1,49},{2,18},{3,51},{4,20},{5,53},{6,22},{7,55},{8,24},{9,... | collective-permute-start | bytes 786440 | tf_op jit(solution)/shard_map/ppermute | solution.py:30
  15.5 3.3 %shard_map.47 = (bf16[2048,256]{1,0:T(8,128)(2,1)S(1)}, bf16[2048,256]{1,0:T(8,128)(2,1)S(1)}) custom-call(s32[32]{0:T(128)S(1)} %dynamic-slice_bitcast_fusion.table, f32[8192,256]{1,0:T(8,128)} %master.3), custom_call_target="tpu_custom_call" | custom-call | flops 6291456 | bytes 6291456 | tf_op jit(solution)/shard_map/pallas_call | solution.py:122
  18.9 0.5 collective-permute-start.6
  19.5 0.1 collective-permute-start.3
  19.6 0.2 collective-permute-start.4
  19.8 0.3 collective-permute-start.8
  20.1 7.8 %collective-permute-done.3 = bf16[2,2,128,512]{3,2,1,0:T(8,128)(2,1)S(1)} collective-permute-done((bf16[2,2,128,512]{3,2,1,0:T(8,128)(2,1)S(1)}, bf16[2,2,128,512]{3,2,1,0:T(8,128)(2,1)S(1)}, u32[]{:S(2)}, u32[]{:S(2)}) %collective-permute-start.3) | collective-permute-done | bytes 524320 | tf_op jit(solution)/shard_map/ppermute | solution.py:30
  27.9 0.1 pad_maximum_fusion.refs_0_
  28.0 0.1 pad_maximum_fusion.1.refs_0_
  28.1 2.6 %collective-permute-start.10 = (bf16[4,2,128,512]{3,2,1,0:T(8,128)(2,1)S(1)}, bf16[4,2,128,512]{3,2,1,0:T(8,128)(2,1)S(1)}, u32[]{:S(2)}, u32[]{:S(2)}) collective-permute-start(bf16[4,2,128,512]{3,2,1,0:T(8,128)(2,1)S(1)} %pad_maximum_fusion.refs_0_), channel_id=1, source_target_pairs={{0,16},{1,49},{2,18},{3,51},{4,20},{5,53},{6,22},{7,55},{8,24},{9,... | collective-permute-start | bytes 3145736 | tf_op jit(solution)/shard_map/ppermute | solution.py:30
  30.7 1.0 collective-permute-start.7
  31.7 8.0 %collective-permute-done.8.far = bf16[2048,256]{1,0:T(8,128)(2,1)S(1)} collective-permute-done((bf16[2048,256]{1,0:T(8,128)(2,1)S(1)}, bf16[2048,256]{1,0:T(8,128)(2,1)S(1)}, u32[]{:S(2)}, u32[]{:S(2)}) %collective-permute-start.8) | collective-permute-done | bytes 1048608 | tf_op jit(solution)/shard_map/ppermute | solution.py:30
  39.8 3.3 %collective-permute-done.10.refs_1_ = bf16[4,2,128,512]{3,2,1,0:T(8,128)(2,1)S(1)} collective-permute-done((bf16[4,2,128,512]{3,2,1,0:T(8,128)(2,1)S(1)}, bf16[4,2,128,512]{3,2,1,0:T(8,128)(2,1)S(1)}, u32[]{:S(2)}, u32[]{:S(2)}) %collective-permute-start.10) | collective-permute-done | bytes 1048608 | tf_op jit(solution)/shard_map/ppermute | solution.py:30
  43.1 2.5 %collective-permute-done.7.refs_1_ = bf16[4,2,128,512]{3,2,1,0:T(8,128)(2,1)S(1)} collective-permute-done((bf16[4,2,128,512]{3,2,1,0:T(8,128)(2,1)S(1)}, bf16[4,2,128,512]{3,2,1,0:T(8,128)(2,1)S(1)}, u32[]{:S(2)}, u32[]{:S(2)}) %collective-permute-start.7) | collective-permute-done | bytes 1048608 | tf_op jit(solution)/shard_map/ppermute | solution.py:30
  45.6 0.4 collective-permute-start.9
  46.0 0.3 collective-permute-start.12
  46.3 1.0 collective-permute-start.13
  47.3 1.5 collective-permute-start.25
  48.8 10.8 %collective-permute-done.9.refs_3_ = bf16[4,2,128,512]{3,2,1,0:T(8,128)(2,1)S(1)} collective-permute-done((bf16[4,2,128,512]{3,2,1,0:T(8,128)(2,1)S(1)}, bf16[4,2,128,512]{3,2,1,0:T(8,128)(2,1)S(1)}, u32[]{:S(2)}, u32[]{:S(2)}) %collective-permute-start.9) | collective-permute-done | bytes 1048608 | tf_op jit(solution)/shard_map/ppermute | solution.py:30
  59.5 0.4 collective-permute-done.11.refs_3_
  60.0 5.9 %collective-permute-done.12.cross = bf16[2048,256]{1,0:T(8,128)(2,1)S(1)} collective-permute-done((bf16[2048,256]{1,0:T(8,128)(2,1)S(1)}, bf16[2048,256]{1,0:T(8,128)(2,1)S(1)}, u32[]{:S(2)}, u32[]{:S(2)}) %collective-permute-start.12) | collective-permute-done | bytes 1048608 | tf_op jit(solution)/shard_map/ppermute | solution.py:30
  65.9 4.9 %collective-permute-done.13.refs_2_ = bf16[4,2,128,512]{3,2,1,0:T(8,128)(2,1)S(1)} collective-permute-done((bf16[4,2,128,512]{3,2,1,0:T(8,128)(2,1)S(1)}, bf16[4,2,128,512]{3,2,1,0:T(8,128)(2,1)S(1)}, u32[]{:S(2)}, u32[]{:S(2)}) %collective-permute-start.13) | collective-permute-done | bytes 1048608 | tf_op jit(solution)/shard_map/ppermute | solution.py:30
  70.8 2.9 %shard_map.49 = bf16[4,128,1024]{2,1,0:T(8,128)(2,1)S(1)} custom-call(s32[32]{0:T(128)S(1)} %dynamic-slice_bitcast_fusion.table, bf16[2048,256]{1,0:T(8,128)(2,1)S(1)} %get-tuple-element.47.mine, bf16[2048,256]{1,0:T(8,128)(2,1)S(1)} %collective-permute-done.5.near, bf16[2048,256]{1,0:T(8,128)(2,1)S(1)} %collective-permute-done.8.far, ...), custom_call_target="tpu_custom_call" | custom-call | flops 2147483648 | bytes 8388608 | tf_op jit(solution)/shard_map/pallas_call | solution.py:168
  73.7 4.0 %collective-permute-start.14 = (bf16[4,128,1024]{2,1,0:T(8,128)(2,1)S(1)}, bf16[4,128,1024]{2,1,0:T(8,128)(2,1)S(1)}, u32[]{:S(2)}, u32[]{:S(2)}) collective-permute-start(bf16[4,128,1024]{2,1,0:T(8,128)(2,1)S(1)} %shard_map.49), channel_id=1, source_target_pairs={{0,1},{1,0},{2,3},{3,2},{4,5},{5,4},{6,7},{7,6},{8,9},{9,8},{10,11... | collective-permute-start | bytes 3145736 | tf_op jit(solution)/shard_map/ppermute | solution.py:30
  77.7 2.9 %shard_map.52 = bf16[4,128,1024]{2,1,0:T(8,128)(2,1)S(1)} custom-call(s32[32]{0:T(128)S(1)} %dynamic-slice_bitcast_fusion.table, bf16[2048,256]{1,0:T(8,128)(2,1)S(1)} %get-tuple-element.47.mine, bf16[2048,256]{1,0:T(8,128)(2,1)S(1)} %collective-permute-done.5.near, bf16[2048,256]{1,0:T(8,128)(2,1)S(1)} %collective-permute-done.8.far, ...), custom_call_target="tpu_custom_call" | custom-call | flops 2147483648 | bytes 8388608 | tf_op jit(solution)/shard_map/pallas_call | solution.py:168
  80.7 0.1 collective-permute-start.26
  80.8 3.0 %shard_map.48 = f32[4,128,1024]{2,1,0:T(8,128)S(1)} custom-call(s32[32]{0:T(128)S(1)} %dynamic-slice_bitcast_fusion.table, bf16[2048,256]{1,0:T(8,128)(2,1)S(1)} %get-tuple-element.47.mine, bf16[2048,256]{1,0:T(8,128)(2,1)S(1)} %collective-permute-done.5.near, bf16[2048,256]{1,0:T(8,128)(2,1)S(1)} %collective-permute-done.8.far, ...), custom_call_target="tpu_custom_call" | custom-call | flops 2147483648 | bytes 8388608 | tf_op jit(solution)/shard_map/pallas_call | solution.py:168
  83.8 0.4 convert_add_fusion.1
  84.3 0.5 collective-permute-start.15
  84.8 3.0 %shard_map.51 = f32[4,128,1024]{2,1,0:T(8,128)S(1)} custom-call(s32[32]{0:T(128)S(1)} %dynamic-slice_bitcast_fusion.table, bf16[2048,256]{1,0:T(8,128)(2,1)S(1)} %get-tuple-element.47.mine, bf16[2048,256]{1,0:T(8,128)(2,1)S(1)} %collective-permute-done.5.near, bf16[2048,256]{1,0:T(8,128)(2,1)S(1)} %collective-permute-done.8.far, ...), custom_call_target="tpu_custom_call" | custom-call | flops 2147483648 | bytes 8388608 | tf_op jit(solution)/shard_map/pallas_call | solution.py:168
  87.8 0.4 convert_add_fusion
  88.3 1.3 collective-permute-start.27
  89.6 8.0 %collective-permute-done.15 = bf16[4,128,512]{2,1,0:T(8,128)(2,1)S(1)} collective-permute-done((bf16[4,128,512]{2,1,0:T(8,128)(2,1)S(1)}, bf16[4,128,512]{2,1,0:T(8,128)(2,1)S(1)}, u32[]{:S(2)}, u32[]{:S(2)}) %collective-permute-start.15) | collective-permute-done | bytes 524320 | tf_op jit(solution)/shard_map/ppermute | solution.py:30
  97.6 0.2 fusion.1
  97.8 3.8 %collective-permute-start.16 = (bf16[128,512]{1,0:T(8,128)(2,1)S(1)}, bf16[128,512]{1,0:T(8,128)(2,1)S(1)}, u32[]{:S(2)}, u32[]{:S(2)}) collective-permute-start(bf16[128,512]{1,0:T(8,128)(2,1)S(1)} %get-tuple-element.63), channel_id=1, source_target_pairs={{0,0},{1,65},{2,2},{3,67},{4,4},{5,69},{6,6},{7,71},{8,8},{9,73},{... | collective-permute-start | bytes 393224 | tf_op jit(solution)/shard_map/ppermute | solution.py:30
  101.5 4.0 %collective-permute-start.19 = (bf16[128,512]{1,0:T(8,128)(2,1)S(1)}, bf16[128,512]{1,0:T(8,128)(2,1)S(1)}, u32[]{:S(2)}, u32[]{:S(2)}) collective-permute-start(bf16[128,512]{1,0:T(8,128)(2,1)S(1)} %get-tuple-element.64), channel_id=1, source_target_pairs={{0,48},{1,113},{2,50},{3,115},{4,52},{5,117},{6,54},{7,119},{8,56}... | collective-permute-start | bytes 393224 | tf_op jit(solution)/shard_map/ppermute | solution.py:30
  105.5 2.0 %collective-permute-start.18 = (bf16[128,512]{1,0:T(8,128)(2,1)S(1)}, bf16[128,512]{1,0:T(8,128)(2,1)S(1)}, u32[]{:S(2)}, u32[]{:S(2)}) collective-permute-start(bf16[128,512]{1,0:T(8,128)(2,1)S(1)} %get-tuple-element.65), channel_id=1, source_target_pairs={{0,32},{1,97},{2,34},{3,99},{4,36},{5,101},{6,38},{7,103},{8,40},{... | collective-permute-start | bytes 393224 | tf_op jit(solution)/shard_map/ppermute | solution.py:30
  107.5 2.7 %collective-permute-start.17 = (bf16[128,512]{1,0:T(8,128)(2,1)S(1)}, bf16[128,512]{1,0:T(8,128)(2,1)S(1)}, u32[]{:S(2)}, u32[]{:S(2)}) collective-permute-start(bf16[128,512]{1,0:T(8,128)(2,1)S(1)} %get-tuple-element.66), channel_id=1, source_target_pairs={{0,16},{1,81},{2,18},{3,83},{4,20},{5,85},{6,22},{7,87},{8,24},{9,... | collective-permute-start | bytes 393224 | tf_op jit(solution)/shard_map/ppermute | solution.py:30
  110.2 0.2 fusion
  110.5 3.7 %collective-permute-start.28 = (bf16[128,512]{1,0:T(8,128)(2,1)S(1)}, bf16[128,512]{1,0:T(8,128)(2,1)S(1)}, u32[]{:S(2)}, u32[]{:S(2)}) collective-permute-start(bf16[128,512]{1,0:T(8,128)(2,1)S(1)} %get-tuple-element.59), channel_id=1, source_target_pairs={{0,0},{1,65},{2,2},{3,67},{4,4},{5,69},{6,6},{7,71},{8,8},{9,73},{... | collective-permute-start | bytes 393224 | tf_op jit(solution)/shard_map/ppermute | solution.py:30
  114.2 2.5 %collective-permute-start.31 = (bf16[128,512]{1,0:T(8,128)(2,1)S(1)}, bf16[128,512]{1,0:T(8,128)(2,1)S(1)}, u32[]{:S(2)}, u32[]{:S(2)}) collective-permute-start(bf16[128,512]{1,0:T(8,128)(2,1)S(1)} %get-tuple-element.60), channel_id=1, source_target_pairs={{0,48},{1,113},{2,50},{3,115},{4,52},{5,117},{6,54},{7,119},{8,56}... | collective-permute-start | bytes 393224 | tf_op jit(solution)/shard_map/ppermute | solution.py:30
  116.8 2.0 %collective-permute-start.30 = (bf16[128,512]{1,0:T(8,128)(2,1)S(1)}, bf16[128,512]{1,0:T(8,128)(2,1)S(1)}, u32[]{:S(2)}, u32[]{:S(2)}) collective-permute-start(bf16[128,512]{1,0:T(8,128)(2,1)S(1)} %get-tuple-element.61), channel_id=1, source_target_pairs={{0,32},{1,97},{2,34},{3,99},{4,36},{5,101},{6,38},{7,103},{8,40},{... | collective-permute-start | bytes 393224 | tf_op jit(solution)/shard_map/ppermute | solution.py:30
  118.8 1.3 collective-permute-done.18
  120.2 1.3 collective-permute-start.29
  121.7 3.1 %collective-permute-done.30 = bf16[128,512]{1,0:T(8,128)(2,1)S(1)} collective-permute-done((bf16[128,512]{1,0:T(8,128)(2,1)S(1)}, bf16[128,512]{1,0:T(8,128)(2,1)S(1)}, u32[]{:S(2)}, u32[]{:S(2)}) %collective-permute-start.30) | collective-permute-done | bytes 131104 | tf_op jit(solution)/shard_map/ppermute | solution.py:30
  124.8 2.8 %collective-permute-done.29 = bf16[128,512]{1,0:T(8,128)(2,1)S(1)} collective-permute-done((bf16[128,512]{1,0:T(8,128)(2,1)S(1)}, bf16[128,512]{1,0:T(8,128)(2,1)S(1)}, u32[]{:S(2)}, u32[]{:S(2)}) %collective-permute-start.29) | collective-permute-done | bytes 131104 | tf_op jit(solution)/shard_map/ppermute | solution.py:30
  127.8 0.7 shard_map.50
  128.5 3.5 %collective-permute-start.21 = (bf16[128,512]{1,0:T(8,128)(2,1)S(1)}, bf16[128,512]{1,0:T(8,128)(2,1)S(1)}, u32[]{:S(2)}, u32[]{:S(2)}) collective-permute-start(bf16[128,512]{1,0:T(8,128)(2,1)S(1)} %get-tuple-element.50), channel_id=1, source_target_pairs={{0,0},{1,8},{2,2},{3,10},{4,4},{5,12},{6,6},{7,14},{8,9},{9,1},{10... | collective-permute-start | bytes 393224 | tf_op jit(solution)/shard_map/ppermute | solution.py:30
  132.1 0.6 collective-permute-start.23
  132.7 2.0 %collective-permute-start.24 = (bf16[128,512]{1,0:T(8,128)(2,1)S(1)}, bf16[128,512]{1,0:T(8,128)(2,1)S(1)}, u32[]{:S(2)}, u32[]{:S(2)}) collective-permute-start(bf16[128,512]{1,0:T(8,128)(2,1)S(1)} %get-tuple-element.53), channel_id=1, source_target_pairs={{0,6},{1,14},{2,0},{3,8},{4,2},{5,10},{6,4},{7,12},{8,15},{9,7},{1... | collective-permute-start | bytes 393224 | tf_op jit(solution)/shard_map/ppermute | solution.py:30
  134.6 0.7 shard_map.53
  135.3 3.5 %collective-permute-start.33 = (bf16[128,512]{1,0:T(8,128)(2,1)S(1)}, bf16[128,512]{1,0:T(8,128)(2,1)S(1)}, u32[]{:S(2)}, u32[]{:S(2)}) collective-permute-start(bf16[128,512]{1,0:T(8,128)(2,1)S(1)} %get-tuple-element.55), channel_id=1, source_target_pairs={{0,0},{1,8},{2,2},{3,10},{4,4},{5,12},{6,6},{7,14},{8,9},{9,1},{10... | collective-permute-start | bytes 393224 | tf_op jit(solution)/shard_map/ppermute | solution.py:30
  138.8 0.6 collective-permute-start.34
  139.4 1.7 %collective-permute-done.22.refs_1_ = bf16[128,512]{1,0:T(8,128)(2,1)S(1)} collective-permute-done((bf16[128,512]{1,0:T(8,128)(2,1)S(1)}, bf16[128,512]{1,0:T(8,128)(2,1)S(1)}, u32[]{:S(2)}, u32[]{:S(2)}) %collective-permute-start.22) | collective-permute-done | bytes 131104 | tf_op jit(solution)/shard_map/ppermute | solution.py:30
  141.1 3.3 %collective-permute-start.36 = (bf16[128,512]{1,0:T(8,128)(2,1)S(1)}, bf16[128,512]{1,0:T(8,128)(2,1)S(1)}, u32[]{:S(2)}, u32[]{:S(2)}) collective-permute-start(bf16[128,512]{1,0:T(8,128)(2,1)S(1)} %get-tuple-element.58), channel_id=1, source_target_pairs={{0,6},{1,14},{2,0},{3,8},{4,2},{5,10},{6,4},{7,12},{8,15},{9,7},{1... | collective-permute-start | bytes 393224 | tf_op jit(solution)/shard_map/ppermute | solution.py:30
  144.4 2.1 %collective-permute-done.34.refs_5_ = bf16[128,512]{1,0:T(8,128)(2,1)S(1)} collective-permute-done((bf16[128,512]{1,0:T(8,128)(2,1)S(1)}, bf16[128,512]{1,0:T(8,128)(2,1)S(1)}, u32[]{:S(2)}, u32[]{:S(2)}) %collective-permute-start.34) | collective-permute-done | bytes 131104 | tf_op jit(solution)/shard_map/ppermute | solution.py:30
  146.6 1.6 %collective-permute-done.35.refs_6_ = bf16[128,512]{1,0:T(8,128)(2,1)S(1)} collective-permute-done((bf16[128,512]{1,0:T(8,128)(2,1)S(1)}, bf16[128,512]{1,0:T(8,128)(2,1)S(1)}, u32[]{:S(2)}, u32[]{:S(2)}) %collective-permute-start.35) | collective-permute-done | bytes 131104 | tf_op jit(solution)/shard_map/ppermute | solution.py:30
  148.2 1.0 collective-permute-done.36.refs_7_
  149.2 1.6 %shard_map.54 = bf16[256,2048]{1,0:T(8,128)(2,1)} custom-call(s32[32]{0:T(128)S(1)} %dynamic-slice_bitcast_fusion.table, bf16[128,512]{1,0:T(8,128)(2,1)S(1)} %collective-permute-done.21.refs_0_, bf16[128,512]{1,0:T(8,128)(2,1)S(1)} %collective-permute-done.22.refs_1_, bf16[128,512]{1,0:T(8,128)(2,1)S(1)} %collective-permute-done.23.refs_2_, ...), custom_call_target="tpu_custom_call" | custom-call | bytes 2097152 | tf_op jit(solution)/shard_map/pallas_call | solution.py:209
  (39 shorter events, 0.9 us)
Async XLA Ops:
  0.0 8.9 %collective-permute-start = (bf16[256,512]{1,0:T(8,128)(2,1)}, bf16[256,512]{1,0:T(8,128)(2,1)S(1)}, u32[]{:S(2)}, u32[]{:S(2)}) collective-permute-start(bf16[256,512]{1,0:T(8,128)(2,1)} %param.5), channel_id=1, source_target_pairs={{0,64},{1,65},{2,66},{3,67},{4,68},{5,69},{6,70},{7,71},{8,72},{9,... | collective-permute-start | bytes 786440 | tf_op jit(solution)/shard_map/ppermute | solution.py:30
  2.5 6.4 %copy-start.1 = (bf16[256,512]{1,0:T(8,128)(2,1)S(1)}, bf16[256,512]{1,0:T(8,128)(2,1)}, u32[]{:S(2)}) copy-start(bf16[256,512]{1,0:T(8,128)(2,1)} %param.5) | copy-start | bytes 786436
  8.9 10.4 %collective-permute-start.1 = (bf16[1,2,128,512]{3,2,1,0:T(8,128)(2,1)S(1)}, bf16[1,2,128,512]{3,2,1,0:T(8,128)(2,1)S(1)}, u32[]{:S(2)}, u32[]{:S(2)}) collective-permute-start(bf16[1,2,128,512]{3,2,1,0:T(8,128)(2,1)S(1)} %get-tuple-element.34), channel_id=1, source_target_pairs={{0,2},{1,7},{2,0},{3,5},{4,6},{5,3},{6,4},{7,1},{8,10},{9,15},{10,... | collective-permute-start | bytes 786440 | tf_op jit(solution)/shard_map/ppermute | solution.py:30
  12.8 6.7 %collective-permute-start.2 = (bf16[1,2,128,512]{3,2,1,0:T(8,128)(2,1)S(1)}, bf16[1,2,128,512]{3,2,1,0:T(8,128)(2,1)S(1)}, u32[]{:S(2)}, u32[]{:S(2)}) collective-permute-start(bf16[1,2,128,512]{3,2,1,0:T(8,128)(2,1)S(1)} %get-tuple-element.35), channel_id=1, source_target_pairs={{0,16},{1,49},{2,18},{3,51},{4,20},{5,53},{6,22},{7,55},{8,24},{9,... | collective-permute-start | bytes 786440 | tf_op jit(solution)/shard_map/ppermute | solution.py:30
  18.8 9.3 %collective-permute-start.5 = (bf16[2048,256]{1,0:T(8,128)(2,1)S(1)}, bf16[2048,256]{1,0:T(8,128)(2,1)S(1)}, u32[]{:S(2)}, u32[]{:S(2)}) collective-permute-start(bf16[2048,256]{1,0:T(8,128)(2,1)S(1)} %get-tuple-element.40), channel_id=1, source_target_pairs={{0,1},{1,0},{2,3},{3,2},{4,5},{5,4},{6,7},{7,6},{8,9},{9,8},{10,11... | collective-permute-start | bytes 3145736 | tf_op jit(solution)/shard_map/ppermute | solution.py:30
  18.9 9.3 %collective-permute-start.6 = (bf16[2048,256]{1,0:T(8,128)(2,1)S(1)}, bf16[2048,256]{1,0:T(8,128)(2,1)S(1)}, u32[]{:S(2)}, u32[]{:S(2)}) collective-permute-start(bf16[2048,256]{1,0:T(8,128)(2,1)S(1)} %get-tuple-element.41), channel_id=1, source_target_pairs={{0,1},{1,0},{2,3},{3,2},{4,5},{5,4},{6,7},{7,6},{8,9},{9,8},{10,11... | collective-permute-start | bytes 3145736 | tf_op jit(solution)/shard_map/ppermute | solution.py:30
  19.5 8.4 %collective-permute-start.3 = (bf16[2,2,128,512]{3,2,1,0:T(8,128)(2,1)S(1)}, bf16[2,2,128,512]{3,2,1,0:T(8,128)(2,1)S(1)}, u32[]{:S(2)}, u32[]{:S(2)}) collective-permute-start(bf16[2,2,128,512]{3,2,1,0:T(8,128)(2,1)S(1)} %pad_maximum_fusion.2), channel_id=1, source_target_pairs={{0,6},{1,3},{2,4},{3,1},{4,2},{5,7},{6,0},{7,5},{8,14},{9,11},{10,... | collective-permute-start | bytes 1572872 | tf_op jit(solution)/shard_map/ppermute | solution.py:30
  19.6 8.4 %collective-permute-start.4 = (bf16[2,2,128,512]{3,2,1,0:T(8,128)(2,1)S(1)}, bf16[2,2,128,512]{3,2,1,0:T(8,128)(2,1)S(1)}, u32[]{:S(2)}, u32[]{:S(2)}) collective-permute-start(bf16[2,2,128,512]{3,2,1,0:T(8,128)(2,1)S(1)} %pad_maximum_fusion.3), channel_id=1, source_target_pairs={{0,48},{1,17},{2,50},{3,19},{4,52},{5,21},{6,54},{7,23},{8,56},{9,... | collective-permute-start | bytes 1572872 | tf_op jit(solution)/shard_map/ppermute | solution.py:30
  19.8 19.9 %collective-permute-start.8 = (bf16[2048,256]{1,0:T(8,128)(2,1)S(1)}, bf16[2048,256]{1,0:T(8,128)(2,1)S(1)}, u32[]{:S(2)}, u32[]{:S(2)}) collective-permute-start(bf16[2048,256]{1,0:T(8,128)(2,1)S(1)} %get-tuple-element.32), channel_id=1, source_target_pairs={{0,8},{1,9},{2,10},{3,11},{4,12},{5,13},{6,14},{7,15},{8,0},{9,1},... | collective-permute-start | bytes 3145736 | tf_op jit(solution)/shard_map/ppermute | solution.py:30
  28.1 14.9 %collective-permute-start.10 = (bf16[4,2,128,512]{3,2,1,0:T(8,128)(2,1)S(1)}, bf16[4,2,128,512]{3,2,1,0:T(8,128)(2,1)S(1)}, u32[]{:S(2)}, u32[]{:S(2)}) collective-permute-start(bf16[4,2,128,512]{3,2,1,0:T(8,128)(2,1)S(1)} %pad_maximum_fusion.refs_0_), channel_id=1, source_target_pairs={{0,16},{1,49},{2,18},{3,51},{4,20},{5,53},{6,22},{7,55},{8,24},{9,... | collective-permute-start | bytes 3145736 | tf_op jit(solution)/shard_map/ppermute | solution.py:30
  30.7 14.9 %collective-permute-start.7 = (bf16[4,2,128,512]{3,2,1,0:T(8,128)(2,1)S(1)}, bf16[4,2,128,512]{3,2,1,0:T(8,128)(2,1)S(1)}, u32[]{:S(2)}, u32[]{:S(2)}) collective-permute-start(bf16[4,2,128,512]{3,2,1,0:T(8,128)(2,1)S(1)} %pad_maximum_fusion.1.refs_0_), channel_id=1, source_target_pairs={{0,2},{1,7},{2,0},{3,5},{4,6},{5,3},{6,4},{7,1},{8,10},{9,15},{10,... | collective-permute-start | bytes 3145736 | tf_op jit(solution)/shard_map/ppermute | solution.py:30
  45.6 13.9 %collective-permute-start.9 = (bf16[4,2,128,512]{3,2,1,0:T(8,128)(2,1)S(1)}, bf16[4,2,128,512]{3,2,1,0:T(8,128)(2,1)S(1)}, u32[]{:S(2)}, u32[]{:S(2)}) collective-permute-start(bf16[4,2,128,512]{3,2,1,0:T(8,128)(2,1)S(1)} %collective-permute-done.7.refs_1_), channel_id=1, source_target_pairs={{0,6},{1,3},{2,4},{3,1},{4,2},{5,7},{6,0},{7,5},{8,14},{9,11},{10,... | collective-permute-start | bytes 3145736 | tf_op jit(solution)/shard_map/ppermute | solution.py:30
  46.0 13.9 %collective-permute-start.11 = (bf16[4,2,128,512]{3,2,1,0:T(8,128)(2,1)S(1)}, bf16[4,2,128,512]{3,2,1,0:T(8,128)(2,1)S(1)}, u32[]{:S(2)}, u32[]{:S(2)}) collective-permute-start(bf16[4,2,128,512]{3,2,1,0:T(8,128)(2,1)S(1)} %collective-permute-done.10.refs_1_), channel_id=1, source_target_pairs={{0,48},{1,17},{2,50},{3,19},{4,52},{5,21},{6,54},{7,23},{8,56},{9,... | collective-permute-start | bytes 3145736 | tf_op jit(solution)/shard_map/ppermute | solution.py:30
  46.0 19.9 %collective-permute-start.12 = (bf16[2048,256]{1,0:T(8,128)(2,1)S(1)}, bf16[2048,256]{1,0:T(8,128)(2,1)S(1)}, u32[]{:S(2)}, u32[]{:S(2)}) collective-permute-start(bf16[2048,256]{1,0:T(8,128)(2,1)S(1)} %collective-permute-done.6), channel_id=1, source_target_pairs={{0,8},{1,9},{2,10},{3,11},{4,12},{5,13},{6,14},{7,15},{8,0},{9,1},... | collective-permute-start | bytes 3145736 | tf_op jit(solution)/shard_map/ppermute | solution.py:30
  46.3 24.5 %collective-permute-start.13 = (bf16[4,2,128,512]{3,2,1,0:T(8,128)(2,1)S(1)}, bf16[4,2,128,512]{3,2,1,0:T(8,128)(2,1)S(1)}, u32[]{:S(2)}, u32[]{:S(2)}) collective-permute-start(bf16[4,2,128,512]{3,2,1,0:T(8,128)(2,1)S(1)} %pad_maximum_fusion.1.refs_0_), channel_id=1, source_target_pairs={{0,6},{1,3},{2,4},{3,1},{4,2},{5,7},{6,0},{7,5},{8,14},{9,11},{10,... | collective-permute-start | bytes 3145736 | tf_op jit(solution)/shard_map/ppermute | solution.py:30
  47.3 30.4 %collective-permute-start.25 = (bf16[4,2,128,512]{3,2,1,0:T(8,128)(2,1)S(1)}, bf16[4,2,128,512]{3,2,1,0:T(8,128)(2,1)S(1)}, u32[]{:S(2)}, u32[]{:S(2)}) collective-permute-start(bf16[4,2,128,512]{3,2,1,0:T(8,128)(2,1)S(1)} %pad_maximum_fusion.refs_0_), channel_id=1, source_target_pairs={{0,48},{1,17},{2,50},{3,19},{4,52},{5,21},{6,54},{7,23},{8,56},{9,... | collective-permute-start | bytes 3145736 | tf_op jit(solution)/shard_map/ppermute | solution.py:30
  73.7 10.1 %collective-permute-start.14 = (bf16[4,128,1024]{2,1,0:T(8,128)(2,1)S(1)}, bf16[4,128,1024]{2,1,0:T(8,128)(2,1)S(1)}, u32[]{:S(2)}, u32[]{:S(2)}) collective-permute-start(bf16[4,128,1024]{2,1,0:T(8,128)(2,1)S(1)} %shard_map.49), channel_id=1, source_target_pairs={{0,1},{1,0},{2,3},{3,2},{4,5},{5,4},{6,7},{7,6},{8,9},{9,8},{10,11... | collective-permute-start | bytes 3145736 | tf_op jit(solution)/shard_map/ppermute | solution.py:30
  80.7 7.1 %collective-permute-start.26 = (bf16[4,128,1024]{2,1,0:T(8,128)(2,1)S(1)}, bf16[4,128,1024]{2,1,0:T(8,128)(2,1)S(1)}, u32[]{:S(2)}, u32[]{:S(2)}) collective-permute-start(bf16[4,128,1024]{2,1,0:T(8,128)(2,1)S(1)} %shard_map.52), channel_id=1, source_target_pairs={{0,1},{1,0},{2,3},{3,2},{4,5},{5,4},{6,7},{7,6},{8,9},{9,8},{10,11... | collective-permute-start | bytes 3145736 | tf_op jit(solution)/shard_map/ppermute | solution.py:30
  84.3 13.3 %collective-permute-start.15 = (bf16[4,128,512]{2,1,0:T(8,128)(2,1)S(1)}, bf16[4,128,512]{2,1,0:T(8,128)(2,1)S(1)}, u32[]{:S(2)}, u32[]{:S(2)}) collective-permute-start(bf16[4,128,512]{2,1,0:T(8,128)(2,1)S(1)} %slice.97), channel_id=1, source_target_pairs={{0,8},{1,9},{2,10},{3,11},{4,12},{5,13},{6,14},{7,15},{8,0},{9,1},... | collective-permute-start | bytes 1572872 | tf_op jit(solution)/shard_map/ppermute | solution.py:30
  88.3 21.9 %collective-permute-start.27 = (bf16[4,128,512]{2,1,0:T(8,128)(2,1)S(1)}, bf16[4,128,512]{2,1,0:T(8,128)(2,1)S(1)}, u32[]{:S(2)}, u32[]{:S(2)}) collective-permute-start(bf16[4,128,512]{2,1,0:T(8,128)(2,1)S(1)} %slice.96), channel_id=1, source_target_pairs={{0,8},{1,9},{2,10},{3,11},{4,12},{5,13},{6,14},{7,15},{8,0},{9,1},... | collective-permute-start | bytes 1572872 | tf_op jit(solution)/shard_map/ppermute | solution.py:30
  97.8 16.5 %collective-permute-start.16 = (bf16[128,512]{1,0:T(8,128)(2,1)S(1)}, bf16[128,512]{1,0:T(8,128)(2,1)S(1)}, u32[]{:S(2)}, u32[]{:S(2)}) collective-permute-start(bf16[128,512]{1,0:T(8,128)(2,1)S(1)} %get-tuple-element.63), channel_id=1, source_target_pairs={{0,0},{1,65},{2,2},{3,67},{4,4},{5,69},{6,6},{7,71},{8,8},{9,73},{... | collective-permute-start | bytes 393224 | tf_op jit(solution)/shard_map/ppermute | solution.py:30
  101.5 15.2 %collective-permute-start.19 = (bf16[128,512]{1,0:T(8,128)(2,1)S(1)}, bf16[128,512]{1,0:T(8,128)(2,1)S(1)}, u32[]{:S(2)}, u32[]{:S(2)}) collective-permute-start(bf16[128,512]{1,0:T(8,128)(2,1)S(1)} %get-tuple-element.64), channel_id=1, source_target_pairs={{0,48},{1,113},{2,50},{3,115},{4,52},{5,117},{6,54},{7,119},{8,56}... | collective-permute-start | bytes 393224 | tf_op jit(solution)/shard_map/ppermute | solution.py:30
  105.5 14.6 %collective-permute-start.18 = (bf16[128,512]{1,0:T(8,128)(2,1)S(1)}, bf16[128,512]{1,0:T(8,128)(2,1)S(1)}, u32[]{:S(2)}, u32[]{:S(2)}) collective-permute-start(bf16[128,512]{1,0:T(8,128)(2,1)S(1)} %get-tuple-element.65), channel_id=1, source_target_pairs={{0,32},{1,97},{2,34},{3,99},{4,36},{5,101},{6,38},{7,103},{8,40},{... | collective-permute-start | bytes 393224 | tf_op jit(solution)/shard_map/ppermute | solution.py:30
  107.5 14.0 %collective-permute-start.17 = (bf16[128,512]{1,0:T(8,128)(2,1)S(1)}, bf16[128,512]{1,0:T(8,128)(2,1)S(1)}, u32[]{:S(2)}, u32[]{:S(2)}) collective-permute-start(bf16[128,512]{1,0:T(8,128)(2,1)S(1)} %get-tuple-element.66), channel_id=1, source_target_pairs={{0,16},{1,81},{2,18},{3,83},{4,20},{5,85},{6,22},{7,87},{8,24},{9,... | collective-permute-start | bytes 393224 | tf_op jit(solution)/shard_map/ppermute | solution.py:30
  110.4 17.4 %copy-start = (s32[8]{0:T(128)S(1)}, s32[8]{0:T(128)}, u32[]{:S(2)}) copy-start(s32[8]{0:T(128)} %owner.3) | copy-start | bytes 100
  110.5 11.2 %collective-permute-start.28 = (bf16[128,512]{1,0:T(8,128)(2,1)S(1)}, bf16[128,512]{1,0:T(8,128)(2,1)S(1)}, u32[]{:S(2)}, u32[]{:S(2)}) collective-permute-start(bf16[128,512]{1,0:T(8,128)(2,1)S(1)} %get-tuple-element.59), channel_id=1, source_target_pairs={{0,0},{1,65},{2,2},{3,67},{4,4},{5,69},{6,6},{7,71},{8,8},{9,73},{... | collective-permute-start | bytes 393224 | tf_op jit(solution)/shard_map/ppermute | solution.py:30
  114.2 7.4 %collective-permute-start.31 = (bf16[128,512]{1,0:T(8,128)(2,1)S(1)}, bf16[128,512]{1,0:T(8,128)(2,1)S(1)}, u32[]{:S(2)}, u32[]{:S(2)}) collective-permute-start(bf16[128,512]{1,0:T(8,128)(2,1)S(1)} %get-tuple-element.60), channel_id=1, source_target_pairs={{0,48},{1,113},{2,50},{3,115},{4,52},{5,117},{6,54},{7,119},{8,56}... | collective-permute-start | bytes 393224 | tf_op jit(solution)/shard_map/ppermute | solution.py:30
  116.8 8.0 %collective-permute-start.30 = (bf16[128,512]{1,0:T(8,128)(2,1)S(1)}, bf16[128,512]{1,0:T(8,128)(2,1)S(1)}, u32[]{:S(2)}, u32[]{:S(2)}) collective-permute-start(bf16[128,512]{1,0:T(8,128)(2,1)S(1)} %get-tuple-element.61), channel_id=1, source_target_pairs={{0,32},{1,97},{2,34},{3,99},{4,36},{5,101},{6,38},{7,103},{8,40},{... | collective-permute-start | bytes 393224 | tf_op jit(solution)/shard_map/ppermute | solution.py:30
  120.2 7.4 %collective-permute-start.29 = (bf16[128,512]{1,0:T(8,128)(2,1)S(1)}, bf16[128,512]{1,0:T(8,128)(2,1)S(1)}, u32[]{:S(2)}, u32[]{:S(2)}) collective-permute-start(bf16[128,512]{1,0:T(8,128)(2,1)S(1)} %get-tuple-element.62), channel_id=1, source_target_pairs={{0,16},{1,81},{2,18},{3,83},{4,20},{5,85},{6,22},{7,87},{8,24},{9,... | collective-permute-start | bytes 393224 | tf_op jit(solution)/shard_map/ppermute | solution.py:30
  121.6 6.2 %collective-permute-start.20 = (bf16[4,128,512]{2,1,0:T(8,128)(2,1)S(1)}, bf16[4,128,512]{2,1,0:T(8,128)(2,1)S(1)}, u32[]{:S(2)}, u32[]{:S(2)}) collective-permute-start(bf16[4,128,512]{2,1,0:T(8,128)(2,1)S(1)} %pad_maximum_fusion.4.own), channel_id=1, source_target_pairs={{0,1},{1,0},{2,3},{3,2},{4,5},{5,4},{6,7},{7,6},{8,9},{9,8},{10,11... | collective-permute-start | bytes 1572872 | tf_op jit(solution)/shard_map/ppermute | solution.py:30
  127.7 7.0 %collective-permute-start.32 = (bf16[4,128,512]{2,1,0:T(8,128)(2,1)S(1)}, bf16[4,128,512]{2,1,0:T(8,128)(2,1)S(1)}, u32[]{:S(2)}, u32[]{:S(2)}) collective-permute-start(bf16[4,128,512]{2,1,0:T(8,128)(2,1)S(1)} %pad_maximum_fusion.5.own), channel_id=1, source_target_pairs={{0,1},{1,0},{2,3},{3,2},{4,5},{5,4},{6,7},{7,6},{8,9},{9,8},{10,11... | collective-permute-start | bytes 1572872 | tf_op jit(solution)/shard_map/ppermute | solution.py:30
  128.5 10.3 %collective-permute-start.21 = (bf16[128,512]{1,0:T(8,128)(2,1)S(1)}, bf16[128,512]{1,0:T(8,128)(2,1)S(1)}, u32[]{:S(2)}, u32[]{:S(2)}) collective-permute-start(bf16[128,512]{1,0:T(8,128)(2,1)S(1)} %get-tuple-element.50), channel_id=1, source_target_pairs={{0,0},{1,8},{2,2},{3,10},{4,4},{5,12},{6,6},{7,14},{8,9},{9,1},{10... | collective-permute-start | bytes 393224 | tf_op jit(solution)/shard_map/ppermute | solution.py:30
  132.0 9.2 %collective-permute-start.22 = (bf16[128,512]{1,0:T(8,128)(2,1)S(1)}, bf16[128,512]{1,0:T(8,128)(2,1)S(1)}, u32[]{:S(2)}, u32[]{:S(2)}) collective-permute-start(bf16[128,512]{1,0:T(8,128)(2,1)S(1)} %get-tuple-element.51), channel_id=1, source_target_pairs={{0,2},{1,10},{2,4},{3,12},{4,6},{5,14},{6,0},{7,8},{8,11},{9,3},{1... | collective-permute-start | bytes 393224 | tf_op jit(solution)/shard_map/ppermute | solution.py:30
  132.1 9.1 %collective-permute-start.23 = (bf16[128,512]{1,0:T(8,128)(2,1)S(1)}, bf16[128,512]{1,0:T(8,128)(2,1)S(1)}, u32[]{:S(2)}, u32[]{:S(2)}) collective-permute-start(bf16[128,512]{1,0:T(8,128)(2,1)S(1)} %get-tuple-element.52), channel_id=1, source_target_pairs={{0,4},{1,12},{2,6},{3,14},{4,0},{5,8},{6,2},{7,10},{8,13},{9,5},{1... | collective-permute-start | bytes 393224 | tf_op jit(solution)/shard_map/ppermute | solution.py:30
  132.7 11.8 %collective-permute-start.24 = (bf16[128,512]{1,0:T(8,128)(2,1)S(1)}, bf16[128,512]{1,0:T(8,128)(2,1)S(1)}, u32[]{:S(2)}, u32[]{:S(2)}) collective-permute-start(bf16[128,512]{1,0:T(8,128)(2,1)S(1)} %get-tuple-element.53), channel_id=1, source_target_pairs={{0,6},{1,14},{2,0},{3,8},{4,2},{5,10},{6,4},{7,12},{8,15},{9,7},{1... | collective-permute-start | bytes 393224 | tf_op jit(solution)/shard_map/ppermute | solution.py:30
  135.3 9.1 %collective-permute-start.33 = (bf16[128,512]{1,0:T(8,128)(2,1)S(1)}, bf16[128,512]{1,0:T(8,128)(2,1)S(1)}, u32[]{:S(2)}, u32[]{:S(2)}) collective-permute-start(bf16[128,512]{1,0:T(8,128)(2,1)S(1)} %get-tuple-element.55), channel_id=1, source_target_pairs={{0,0},{1,8},{2,2},{3,10},{4,4},{5,12},{6,6},{7,14},{8,9},{9,1},{10... | collective-permute-start | bytes 393224 | tf_op jit(solution)/shard_map/ppermute | solution.py:30
  138.8 7.8 %collective-permute-start.34 = (bf16[128,512]{1,0:T(8,128)(2,1)S(1)}, bf16[128,512]{1,0:T(8,128)(2,1)S(1)}, u32[]{:S(2)}, u32[]{:S(2)}) collective-permute-start(bf16[128,512]{1,0:T(8,128)(2,1)S(1)} %get-tuple-element.56), channel_id=1, source_target_pairs={{0,2},{1,10},{2,4},{3,12},{4,6},{5,14},{6,0},{7,8},{8,11},{9,3},{1... | collective-permute-start | bytes 393224 | tf_op jit(solution)/shard_map/ppermute | solution.py:30
  141.1 7.1 %collective-permute-start.35 = (bf16[128,512]{1,0:T(8,128)(2,1)S(1)}, bf16[128,512]{1,0:T(8,128)(2,1)S(1)}, u32[]{:S(2)}, u32[]{:S(2)}) collective-permute-start(bf16[128,512]{1,0:T(8,128)(2,1)S(1)} %get-tuple-element.57), channel_id=1, source_target_pairs={{0,4},{1,12},{2,6},{3,14},{4,0},{5,8},{6,2},{7,10},{8,13},{9,5},{1... | collective-permute-start | bytes 393224 | tf_op jit(solution)/shard_map/ppermute | solution.py:30
  141.1 8.1 %collective-permute-start.36 = (bf16[128,512]{1,0:T(8,128)(2,1)S(1)}, bf16[128,512]{1,0:T(8,128)(2,1)S(1)}, u32[]{:S(2)}, u32[]{:S(2)}) collective-permute-start(bf16[128,512]{1,0:T(8,128)(2,1)S(1)} %get-tuple-element.58), channel_id=1, source_target_pairs={{0,6},{1,14},{2,0},{3,8},{4,2},{5,10},{6,4},{7,12},{8,15},{9,7},{1... | collective-permute-start | bytes 393224 | tf_op jit(solution)/shard_map/ppermute | solution.py:30

commit v15 on v14

--- a/solution.py
+++ b/solution.py
@@ -141,38 +141,86 @@
     return [(mine, cols(0, core)), (near, cols(0, 1 - core)), (far, cols(2 * COLS, core)), (cross, cols(2 * COLS, 1 - core))]
 
 
+def dot(a, b):
+    return jnp.dot(a, b, preferred_element_type=jnp.float32)
+
+
+def depth_of(table, n):
+    return pl.ds(pl.multiple_of(table[Z_SLOT + n] * SHARE, SHARE), SHARE)
+
+
+EARLY, LATE = (0, 1, 2), 3
+
+
+def early_kernel(table, mine, near, far, *refs):
+    z_slots, y_slots, (z_out, y_out) = refs[:3], refs[3:6], refs[6:]
+    for piece, weight in enumerate((mine, near, far)):
+        for half in range(2):
+            got = None
+            for n, slot in zip(EARLY, z_slots):
+                term = dot(slot[:, half].reshape(4 * HALF, SHARE), weight[depth_of(table, n), :])
+                got = term if got is None else got + term
+            z_out[piece, half] = got
+            got = None
+            for n in range(4):
+                term = dot(jnp.concatenate([slot[n, half] for slot in y_slots]), weight[depth_of(table, n), :])
+                got = term if got is None else got + term
+            y_out[piece, half] = got
+
+
+def early_product(table, weights, slots):
+    vmem = pl.BlockSpec(memory_space=pltpu.VMEM)
+    parts = [slots[part][n] for part in "zy" for n in EARLY]
+    shapes = [(3, 2, 4 * HALF, COLS), (3, 2, 3 * HALF, COLS)]
+    return pl.pallas_call(
+        early_kernel,
+        in_specs=[pl.BlockSpec(memory_space=pltpu.SMEM)] + [vmem] * 9,
+        out_specs=[vmem] * 2,
+        out_shape=[jax.ShapeDtypeStruct(shape, jnp.float32) for shape in shapes],
+        compiler_params=pltpu.CompilerParams(vmem_limit_bytes=24 * MIB),
+        cost_estimate=pl.CostEstimate(flops=5 * 2**30, bytes_accessed=16 * MIB, transcendentals=0),
+    )(table, *weights[:3], *parts)
+
+
 def product_kernel(part, keep, table, mine, near, far, cross, *refs):
-    slots, out = refs[:4], refs[4]
+    slots, early, out = refs[:4], refs[4], refs[5]
     core = table[CORE]
     half = core if keep else 1 - core
-    weights = pieces(core, mine, near, far, cross)
-    chunks = []
-    for n in range(4):
+
+    def rows(n, some):
         if part == "y":
-            rows = jnp.concatenate([slot[n, half] for slot in slots])
-        else:
-            rows = slots[n][:, half].reshape(4 * HALF, SHARE)
-        chunks.append((rows, pl.ds(pl.multiple_of(table[Z_SLOT + n] * SHARE, SHARE), SHARE)))
-    for weight, cols in weights:
+            return jnp.concatenate([slots[i][n, half] for i in some])
+        return slots[n][:, half].reshape(4 * HALF, SHARE)
+
+    for piece, (weight, cols) in enumerate(pieces(core, mine, near, far, cross)):
+        last = piece == 3
+        some = EARLY + (LATE,) if last else (LATE,)
         got = None
-        for rows, depth in chunks:
-            term = jnp.dot(rows, weight[depth, :], preferred_element_type=jnp.float32)
+        for n in range(4) if part == "y" else some:
+            term = dot(rows(n, some), weight[depth_of(table, n), :])
             got = term if got is None else got + term
-        got = got.reshape(4, HALF, COLS)
+        if not last and part == "z":
+            got += early[piece, half]
         for ys in range(4):
-            out[table[Y_SLOT + ys], :, cols] = got[ys].astype(out.dtype)
-
-
-def product(part, keep, table, weights, slots):
+            if last or part == "z":
+                value = got[ys * HALF : (ys + 1) * HALF]
+            elif ys == LATE:
+                value = got
+            else:
+                value = early[piece, half, pl.ds(EARLY.index(ys) * HALF, HALF)]
+            out[table[Y_SLOT + ys], :, cols] = value.astype(out.dtype)
+
+
+def product(part, keep, table, weights, slots, early):
     vmem = pl.BlockSpec(memory_space=pltpu.VMEM)
     return pl.pallas_call(
         functools.partial(product_kernel, part, keep),
-        in_specs=[pl.BlockSpec(memory_space=pltpu.SMEM)] + [vmem] * 8,
+        in_specs=[pl.BlockSpec(memory_space=pltpu.SMEM)] + [vmem] * 9,
         out_specs=vmem,
         out_shape=jax.ShapeDtypeStruct((4, HALF, 4 * COLS), jnp.float32 if keep else jnp.bfloat16),
         compiler_params=pltpu.CompilerParams(vmem_limit_bytes=24 * MIB),
-        cost_estimate=pl.CostEstimate(flops=2 * 512 * 2048 * 1024, bytes_accessed=8 * MIB, transcendentals=0),
-    )(table, *weights, *slots)
+        cost_estimate=pl.CostEstimate(flops=2**30, bytes_accessed=8 * MIB, transcendentals=0),
+    )(table, *weights, *slots, early)
 
 
 def spread_kernel(table, owner, own, other, *outs):
@@ -231,11 +279,12 @@
     slots = gather(activations, same, (near, swapped), far)
     cross = permute(after(swapped, far), other_chip)
     weights = [mine, near, far, cross]
-    ready = after(table, slots["z"][3], slots["y"][3])
+    early = dict(zip("zy", early_product(table, weights, slots)))
+    ready = after(table, slots["z"][LATE], slots["y"][LATE])
 
     def chain(part):
-        passed = product(part, False, ready, weights, slots[part])
-        kept = product(part, True, ready, weights, slots[part])
+        passed = product(part, False, ready, weights, slots[part], early[part])
+        kept = product(part, True, ready, weights, slots[part], early[part])
         both = kept + permute(passed, other_core).astype(f32)
         came = permute(both[..., 2 * COLS :].astype(bf16), other_chip)
         total = (both[..., : 2 * COLS] + came.astype(f32)).astype(bf16)

time: 151 us -> 146 us (0.967)
  waiting for transfers between devices: 68.5 us -> 62 us
    ppermute x37, waiting for transfers between devices: 68.5 us -> 62 us  [permute(): lax.ppermute(value, AXES, [(i, move(*coords(i))) for i in range(N_DEV)])]
    pallas_call x0 -> x1, Pallas kernels: none -> 5.58 us  [early_product(): pl.pallas_call(early_kernel, in_specs=[pl.BlockSpec(memory_space=pltpu.SM...]
    pallas_call x4, Pallas kernels: 11.8 us -> 6.84 us  [product(): pl.pallas_call(functools.partial(product_kernel, part, keep), in_specs=[p...]
  transfers between devices with their start and end apart: 37 -> 37, of which waited for: 17 -> 14; matrix products, arithmetic and copies ran while one was open for 2% -> 2% of each run, Pallas kernels for 13% -> 13%
where the time goes in v15:
time: 146 us
  waiting for transfers between devices  62 us (42%)
  starting transfers between devices  58.9 us (40%)
  Pallas kernels  21.9 us (15%)
  other arithmetic  1.57 us (1%)
    ppermute x37, waiting for transfers between devices, permute(): lax.ppermute(value, AXES, [(i, move(*coords(i))) for i in range(N_DEV)])  62 us
    ppermute x37, starting transfers between devices, permute(): lax.ppermute(value, AXES, [(i, move(*coords(i))) for i in range(N_DEV)])  58.9 us
    pallas_call x4, Pallas kernels, product(): pl.pallas_call(functools.partial(product_kernel, part, keep), in_specs=[p...  6.84 us
    pallas_call x2, Pallas kernels, refit(): pl.pallas_call(functools.partial(refit_kernel, first), in_specs=[pl.Block...  6.55 us
    pallas_call x1, Pallas kernels, early_product(): pl.pallas_call(early_kernel, in_specs=[pl.BlockSpec(memory_space=pltpu.SM...  5.58 us
  transfers between devices with their start and end apart: 37, of which 14 were waited for; matrix products, arithmetic and copies ran while one was open for 2% of the time, Pallas kernels for 13%

profile of v15, /device:TPU:3, one launch (start us, length us, event | category | flops | bytes accessed | tf_op | source)
XLA Modules:
  0.0 145.8 jit_solution(2176572099189586441)
XLA Ops:
  0.0 1.8 %collective-permute-start = (bf16[256,512]{1,0:T(8,128)(2,1)}, bf16[256,512]{1,0:T(8,128)(2,1)S(1)}, u32[]{:S(2)}, u32[]{:S(2)}) collective-permute-start(bf16[256,512]{1,0:T(8,128)(2,1)} %param.5), channel_id=1, source_target_pairs={{0,64},{1,65},{2,66},{3,67},{4,68},{5,69},{6,70},{7,71},{8,72},{9,... | collective-permute-start | bytes 786440 | tf_op jit(solution)/shard_map/ppermute | solution.py:30
  1.8 0.7 dynamic-slice_bitcast_fusion.table
  2.5 3.3 %shard_map.46 = (bf16[2048,256]{1,0:T(8,128)(2,1)S(1)}, bf16[2048,256]{1,0:T(8,128)(2,1)S(1)}) custom-call(s32[32]{0:T(128)S(1)} %dynamic-slice_bitcast_fusion.table, f32[8192,256]{1,0:T(8,128)} %master.3), custom_call_target="tpu_custom_call" | custom-call | flops 6291456 | bytes 6291456 | tf_op jit(solution)/shard_map/pallas_call | solution.py:122
  5.8 3.1 %collective-permute-done = bf16[256,512]{1,0:T(8,128)(2,1)S(1)} collective-permute-done((bf16[256,512]{1,0:T(8,128)(2,1)}, bf16[256,512]{1,0:T(8,128)(2,1)S(1)}, u32[]{:S(2)}, u32[]{:S(2)}) %collective-permute-start) | collective-permute-done | bytes 262176 | tf_op jit(solution)/shard_map/ppermute | solution.py:30
  8.9 3.8 %collective-permute-start.1 = (bf16[1,2,128,512]{3,2,1,0:T(8,128)(2,1)S(1)}, bf16[1,2,128,512]{3,2,1,0:T(8,128)(2,1)S(1)}, u32[]{:S(2)}, u32[]{:S(2)}) collective-permute-start(bf16[1,2,128,512]{3,2,1,0:T(8,128)(2,1)S(1)} %get-tuple-element.36), channel_id=1, source_target_pairs={{0,2},{1,7},{2,0},{3,5},{4,6},{5,3},{6,4},{7,1},{8,10},{9,15},{10,... | collective-permute-start | bytes 786440 | tf_op jit(solution)/shard_map/ppermute | solution.py:30
  12.8 2.7 %collective-permute-start.2 = (bf16[1,2,128,512]{3,2,1,0:T(8,128)(2,1)S(1)}, bf16[1,2,128,512]{3,2,1,0:T(8,128)(2,1)S(1)}, u32[]{:S(2)}, u32[]{:S(2)}) collective-permute-start(bf16[1,2,128,512]{3,2,1,0:T(8,128)(2,1)S(1)} %get-tuple-element.37), channel_id=1, source_target_pairs={{0,16},{1,49},{2,18},{3,51},{4,20},{5,53},{6,22},{7,55},{8,24},{9,... | collective-permute-start | bytes 786440 | tf_op jit(solution)/shard_map/ppermute | solution.py:30
  15.5 3.3 %shard_map.47 = (bf16[2048,256]{1,0:T(8,128)(2,1)S(1)}, bf16[2048,256]{1,0:T(8,128)(2,1)S(1)}) custom-call(s32[32]{0:T(128)S(1)} %dynamic-slice_bitcast_fusion.table, f32[8192,256]{1,0:T(8,128)} %master.3), custom_call_target="tpu_custom_call" | custom-call | flops 6291456 | bytes 6291456 | tf_op jit(solution)/shard_map/pallas_call | solution.py:122
  18.8 0.1 collective-permute-start.5
  18.9 0.5 collective-permute-start.6
  19.5 0.1 collective-permute-start.3
  19.6 0.2 collective-permute-start.4
  19.8 0.3 collective-permute-start.8
  20.1 7.8 %collective-permute-done.3 = bf16[2,2,128,512]{3,2,1,0:T(8,128)(2,1)S(1)} collective-permute-done((bf16[2,2,128,512]{3,2,1,0:T(8,128)(2,1)S(1)}, bf16[2,2,128,512]{3,2,1,0:T(8,128)(2,1)S(1)}, u32[]{:S(2)}, u32[]{:S(2)}) %collective-permute-start.3) | collective-permute-done | bytes 524320 | tf_op jit(solution)/shard_map/ppermute | solution.py:30
  27.9 0.1 pad_maximum_fusion.refs_3_.refs_0_
  28.0 0.1 pad_maximum_fusion.1.refs_0_
  28.1 2.6 %collective-permute-start.10 = (bf16[4,2,128,512]{3,2,1,0:T(8,128)(2,1)S(1)}, bf16[4,2,128,512]{3,2,1,0:T(8,128)(2,1)S(1)}, u32[]{:S(2)}, u32[]{:S(2)}) collective-permute-start(bf16[4,2,128,512]{3,2,1,0:T(8,128)(2,1)S(1)} %pad_maximum_fusion.refs_3_.refs_0_), channel_id=1, source_target_pairs={{0,16},{1,49},{2,18},{3,51},{4,20},{5,53},{6,22},{7,55},{8,24},{9,... | collective-permute-start | bytes 3145736 | tf_op jit(solution)/shard_map/ppermute | solution.py:30
  30.7 1.0 collective-permute-start.7
  31.7 8.0 %collective-permute-done.8.far = bf16[2048,256]{1,0:T(8,128)(2,1)S(1)} collective-permute-done((bf16[2048,256]{1,0:T(8,128)(2,1)S(1)}, bf16[2048,256]{1,0:T(8,128)(2,1)S(1)}, u32[]{:S(2)}, u32[]{:S(2)}) %collective-permute-start.8) | collective-permute-done | bytes 1048608 | tf_op jit(solution)/shard_map/ppermute | solution.py:30
  39.8 2.0 %collective-permute-start.13 = (bf16[4,2,128,512]{3,2,1,0:T(8,128)(2,1)S(1)}, bf16[4,2,128,512]{3,2,1,0:T(8,128)(2,1)S(1)}, u32[]{:S(2)}, u32[]{:S(2)}) collective-permute-start(bf16[4,2,128,512]{3,2,1,0:T(8,128)(2,1)S(1)} %pad_maximum_fusion.1.refs_0_), channel_id=1, source_target_pairs={{0,6},{1,3},{2,4},{3,1},{4,2},{5,7},{6,0},{7,5},{8,14},{9,11},{10,... | collective-permute-start | bytes 3145736 | tf_op jit(solution)/shard_map/ppermute | solution.py:30
  41.8 2.8 %collective-permute-start.14 = (bf16[4,2,128,512]{3,2,1,0:T(8,128)(2,1)S(1)}, bf16[4,2,128,512]{3,2,1,0:T(8,128)(2,1)S(1)}, u32[]{:S(2)}, u32[]{:S(2)}) collective-permute-start(bf16[4,2,128,512]{3,2,1,0:T(8,128)(2,1)S(1)} %pad_maximum_fusion.refs_3_.refs_0_), channel_id=1, source_target_pairs={{0,48},{1,17},{2,50},{3,19},{4,52},{5,21},{6,54},{7,23},{8,56},{9,... | collective-permute-start | bytes 3145736 | tf_op jit(solution)/shard_map/ppermute | solution.py:30
  44.6 1.0 collective-permute-done.7.refs_1_
  45.6 0.4 collective-permute-start.9
  46.0 0.3 collective-permute-start.12
  46.3 12.0 %collective-permute-done.13.refs_2_ = bf16[4,2,128,512]{3,2,1,0:T(8,128)(2,1)S(1)} collective-permute-done((bf16[4,2,128,512]{3,2,1,0:T(8,128)(2,1)S(1)}, bf16[4,2,128,512]{3,2,1,0:T(8,128)(2,1)S(1)}, u32[]{:S(2)}, u32[]{:S(2)}) %collective-permute-start.13) | collective-permute-done | bytes 1048608 | tf_op jit(solution)/shard_map/ppermute | solution.py:30
  58.3 5.6 %shard_map.48 = (f32[3,2,512,256]{3,2,1,0:T(8,128)S(1)}, f32[3,2,384,256]{3,2,1,0:T(8,128)S(1)}) custom-call(s32[32]{0:T(128)S(1)} %dynamic-slice_bitcast_fusion.table, bf16[2048,256]{1,0:T(8,128)(2,1)S(1)} %get-tuple-element.49.mine, bf16[2048,256]{1,0:T(8,128)(2,1)S(1)} %collective-permute-done.5.near, bf16[2048,256]{1,0:T(8,128)(2,1)S(1)} %collective-permute-done.8.far, ...), custom_call_target="tpu_custom_call" | custom-call | flops 5368709120 | bytes 16777216 | tf_op jit(solution)/shard_map/pallas_call | solution.py:175
  63.9 5.6 %collective-permute-done.9.refs_3_ = bf16[4,2,128,512]{3,2,1,0:T(8,128)(2,1)S(1)} collective-permute-done((bf16[4,2,128,512]{3,2,1,0:T(8,128)(2,1)S(1)}, bf16[4,2,128,512]{3,2,1,0:T(8,128)(2,1)S(1)}, u32[]{:S(2)}, u32[]{:S(2)}) %collective-permute-start.9) | collective-permute-done | bytes 1048608 | tf_op jit(solution)/shard_map/ppermute | solution.py:30
  69.5 1.8 %shard_map.53 = bf16[4,128,1024]{2,1,0:T(8,128)(2,1)S(1)} custom-call(s32[32]{0:T(128)S(1)} %dynamic-slice_bitcast_fusion.table, bf16[2048,256]{1,0:T(8,128)(2,1)S(1)} %get-tuple-element.49.mine, bf16[2048,256]{1,0:T(8,128)(2,1)S(1)} %collective-permute-done.5.near, bf16[2048,256]{1,0:T(8,128)(2,1)S(1)} %collective-permute-done.8.far, ...), custom_call_target="tpu_custom_call" | custom-call | flops 1073741824 | bytes 8388608 | tf_op jit(solution)/shard_map/pallas_call | solution.py:216
  71.3 5.3 %collective-permute-start.26 = (bf16[4,128,1024]{2,1,0:T(8,128)(2,1)S(1)}, bf16[4,128,1024]{2,1,0:T(8,128)(2,1)S(1)}, u32[]{:S(2)}, u32[]{:S(2)}) collective-permute-start(bf16[4,128,1024]{2,1,0:T(8,128)(2,1)S(1)} %shard_map.53), channel_id=1, source_target_pairs={{0,1},{1,0},{2,3},{3,2},{4,5},{5,4},{6,7},{7,6},{8,9},{9,8},{10,11... | collective-permute-start | bytes 3145736 | tf_op jit(solution)/shard_map/ppermute | solution.py:30
  76.6 1.7 %shard_map.50 = bf16[4,128,1024]{2,1,0:T(8,128)(2,1)S(1)} custom-call(s32[32]{0:T(128)S(1)} %dynamic-slice_bitcast_fusion.table, bf16[2048,256]{1,0:T(8,128)(2,1)S(1)} %get-tuple-element.49.mine, bf16[2048,256]{1,0:T(8,128)(2,1)S(1)} %collective-permute-done.5.near, bf16[2048,256]{1,0:T(8,128)(2,1)S(1)} %collective-permute-done.8.far, ...), custom_call_target="tpu_custom_call" | custom-call | flops 1073741824 | bytes 8388608 | tf_op jit(solution)/shard_map/pallas_call | solution.py:216
  78.3 0.1 collective-permute-start.15
  78.4 1.7 %shard_map.52 = f32[4,128,1024]{2,1,0:T(8,128)S(1)} custom-call(s32[32]{0:T(128)S(1)} %dynamic-slice_bitcast_fusion.table, bf16[2048,256]{1,0:T(8,128)(2,1)S(1)} %get-tuple-element.49.mine, bf16[2048,256]{1,0:T(8,128)(2,1)S(1)} %collective-permute-done.5.near, bf16[2048,256]{1,0:T(8,128)(2,1)S(1)} %collective-permute-done.8.far, ...), custom_call_target="tpu_custom_call" | custom-call | flops 1073741824 | bytes 8388608 | tf_op jit(solution)/shard_map/pallas_call | solution.py:216
  80.1 0.5 convert_add_fusion
  80.7 0.3 collective-permute-start.27
  81.0 1.7 %shard_map.49 = f32[4,128,1024]{2,1,0:T(8,128)S(1)} custom-call(s32[32]{0:T(128)S(1)} %dynamic-slice_bitcast_fusion.table, bf16[2048,256]{1,0:T(8,128)(2,1)S(1)} %get-tuple-element.49.mine, bf16[2048,256]{1,0:T(8,128)(2,1)S(1)} %collective-permute-done.5.near, bf16[2048,256]{1,0:T(8,128)(2,1)S(1)} %collective-permute-done.8.far, ...), custom_call_target="tpu_custom_call" | custom-call | flops 1073741824 | bytes 8388608 | tf_op jit(solution)/shard_map/pallas_call | solution.py:216
  82.7 0.3 convert_add_fusion.1
  83.1 1.3 collective-permute-start.16
  84.4 9.4 %collective-permute-done.27 = bf16[4,128,512]{2,1,0:T(8,128)(2,1)S(1)} collective-permute-done((bf16[4,128,512]{2,1,0:T(8,128)(2,1)S(1)}, bf16[4,128,512]{2,1,0:T(8,128)(2,1)S(1)}, u32[]{:S(2)}, u32[]{:S(2)}) %collective-permute-start.27) | collective-permute-done | bytes 524320 | tf_op jit(solution)/shard_map/ppermute | solution.py:30
  93.8 0.2 fusion
  94.0 3.8 %collective-permute-start.28 = (bf16[128,512]{1,0:T(8,128)(2,1)S(1)}, bf16[128,512]{1,0:T(8,128)(2,1)S(1)}, u32[]{:S(2)}, u32[]{:S(2)}) collective-permute-start(bf16[128,512]{1,0:T(8,128)(2,1)S(1)} %get-tuple-element.63), channel_id=1, source_target_pairs={{0,0},{1,65},{2,2},{3,67},{4,4},{5,69},{6,6},{7,71},{8,8},{9,73},{... | collective-permute-start | bytes 393224 | tf_op jit(solution)/shard_map/ppermute | solution.py:30
  97.7 3.6 %collective-permute-start.31 = (bf16[128,512]{1,0:T(8,128)(2,1)S(1)}, bf16[128,512]{1,0:T(8,128)(2,1)S(1)}, u32[]{:S(2)}, u32[]{:S(2)}) collective-permute-start(bf16[128,512]{1,0:T(8,128)(2,1)S(1)} %get-tuple-element.64), channel_id=1, source_target_pairs={{0,48},{1,113},{2,50},{3,115},{4,52},{5,117},{6,54},{7,119},{8,56}... | collective-permute-start | bytes 393224 | tf_op jit(solution)/shard_map/ppermute | solution.py:30
  101.4 0.7 collective-permute-start.30
  102.1 1.5 %collective-permute-start.29 = (bf16[128,512]{1,0:T(8,128)(2,1)S(1)}, bf16[128,512]{1,0:T(8,128)(2,1)S(1)}, u32[]{:S(2)}, u32[]{:S(2)}) collective-permute-start(bf16[128,512]{1,0:T(8,128)(2,1)S(1)} %get-tuple-element.66), channel_id=1, source_target_pairs={{0,16},{1,81},{2,18},{3,83},{4,20},{5,85},{6,22},{7,87},{8,24},{9,... | collective-permute-start | bytes 393224 | tf_op jit(solution)/shard_map/ppermute | solution.py:30
  103.6 1.4 collective-permute-done.16
  105.0 0.2 fusion.1
  105.2 3.8 %collective-permute-start.17 = (bf16[128,512]{1,0:T(8,128)(2,1)S(1)}, bf16[128,512]{1,0:T(8,128)(2,1)S(1)}, u32[]{:S(2)}, u32[]{:S(2)}) collective-permute-start(bf16[128,512]{1,0:T(8,128)(2,1)S(1)} %get-tuple-element.67), channel_id=1, source_target_pairs={{0,0},{1,65},{2,2},{3,67},{4,4},{5,69},{6,6},{7,71},{8,8},{9,73},{... | collective-permute-start | bytes 393224 | tf_op jit(solution)/shard_map/ppermute | solution.py:30
  109.0 3.6 %collective-permute-start.20 = (bf16[128,512]{1,0:T(8,128)(2,1)S(1)}, bf16[128,512]{1,0:T(8,128)(2,1)S(1)}, u32[]{:S(2)}, u32[]{:S(2)}) collective-permute-start(bf16[128,512]{1,0:T(8,128)(2,1)S(1)} %get-tuple-element.68), channel_id=1, source_target_pairs={{0,48},{1,113},{2,50},{3,115},{4,52},{5,117},{6,54},{7,119},{8,56}... | collective-permute-start | bytes 393224 | tf_op jit(solution)/shard_map/ppermute | solution.py:30
  112.6 2.1 %collective-permute-start.19 = (bf16[128,512]{1,0:T(8,128)(2,1)S(1)}, bf16[128,512]{1,0:T(8,128)(2,1)S(1)}, u32[]{:S(2)}, u32[]{:S(2)}) collective-permute-start(bf16[128,512]{1,0:T(8,128)(2,1)S(1)} %get-tuple-element.69), channel_id=1, source_target_pairs={{0,32},{1,97},{2,34},{3,99},{4,36},{5,101},{6,38},{7,103},{8,40},{... | collective-permute-start | bytes 393224 | tf_op jit(solution)/shard_map/ppermute | solution.py:30
  114.7 0.3 collective-permute-start.18
  115.0 0.1 collective-permute-start.32
  115.1 0.2 collective-permute-done.20
  115.4 5.0 %collective-permute-done.19 = bf16[128,512]{1,0:T(8,128)(2,1)S(1)} collective-permute-done((bf16[128,512]{1,0:T(8,128)(2,1)S(1)}, bf16[128,512]{1,0:T(8,128)(2,1)S(1)}, u32[]{:S(2)}, u32[]{:S(2)}) %collective-permute-start.19) | collective-permute-done | bytes 131104 | tf_op jit(solution)/shard_map/ppermute | solution.py:30
  120.4 1.8 %collective-permute-done.18 = bf16[128,512]{1,0:T(8,128)(2,1)S(1)} collective-permute-done((bf16[128,512]{1,0:T(8,128)(2,1)S(1)}, bf16[128,512]{1,0:T(8,128)(2,1)S(1)}, u32[]{:S(2)}, u32[]{:S(2)}) %collective-permute-start.18) | collective-permute-done | bytes 131104 | tf_op jit(solution)/shard_map/ppermute | solution.py:30
  122.3 0.7 shard_map.54
  123.0 3.1 %collective-permute-start.33 = (bf16[128,512]{1,0:T(8,128)(2,1)S(1)}, bf16[128,512]{1,0:T(8,128)(2,1)S(1)}, u32[]{:S(2)}, u32[]{:S(2)}) collective-permute-start(bf16[128,512]{1,0:T(8,128)(2,1)S(1)} %get-tuple-element.59), channel_id=1, source_target_pairs={{0,0},{1,8},{2,2},{3,10},{4,4},{5,12},{6,6},{7,14},{8,9},{9,1},{10... | collective-permute-start | bytes 393224 | tf_op jit(solution)/shard_map/ppermute | solution.py:30
  126.2 2.0 %collective-permute-start.35 = (bf16[128,512]{1,0:T(8,128)(2,1)S(1)}, bf16[128,512]{1,0:T(8,128)(2,1)S(1)}, u32[]{:S(2)}, u32[]{:S(2)}) collective-permute-start(bf16[128,512]{1,0:T(8,128)(2,1)S(1)} %get-tuple-element.61), channel_id=1, source_target_pairs={{0,4},{1,12},{2,6},{3,14},{4,0},{5,8},{6,2},{7,10},{8,13},{9,5},{1... | collective-permute-start | bytes 393224 | tf_op jit(solution)/shard_map/ppermute | solution.py:30
  128.2 2.3 %collective-permute-start.36 = (bf16[128,512]{1,0:T(8,128)(2,1)S(1)}, bf16[128,512]{1,0:T(8,128)(2,1)S(1)}, u32[]{:S(2)}, u32[]{:S(2)}) collective-permute-start(bf16[128,512]{1,0:T(8,128)(2,1)S(1)} %get-tuple-element.62), channel_id=1, source_target_pairs={{0,6},{1,14},{2,0},{3,8},{4,2},{5,10},{6,4},{7,12},{8,15},{9,7},{1... | collective-permute-start | bytes 393224 | tf_op jit(solution)/shard_map/ppermute | solution.py:30
  130.5 0.7 shard_map.51
  131.2 2.6 %collective-permute-start.22 = (bf16[128,512]{1,0:T(8,128)(2,1)S(1)}, bf16[128,512]{1,0:T(8,128)(2,1)S(1)}, u32[]{:S(2)}, u32[]{:S(2)}) collective-permute-start(bf16[128,512]{1,0:T(8,128)(2,1)S(1)} %get-tuple-element.54), channel_id=1, source_target_pairs={{0,0},{1,8},{2,2},{3,10},{4,4},{5,12},{6,6},{7,14},{8,9},{9,1},{10... | collective-permute-start | bytes 393224 | tf_op jit(solution)/shard_map/ppermute | solution.py:30
  133.8 0.1 collective-permute-start.23
  133.9 1.6 %collective-permute-done.34.refs_5_ = bf16[128,512]{1,0:T(8,128)(2,1)S(1)} collective-permute-done((bf16[128,512]{1,0:T(8,128)(2,1)S(1)}, bf16[128,512]{1,0:T(8,128)(2,1)S(1)}, u32[]{:S(2)}, u32[]{:S(2)}) %collective-permute-start.34) | collective-permute-done | bytes 131104 | tf_op jit(solution)/shard_map/ppermute | solution.py:30
  135.6 3.4 %collective-permute-start.25 = (bf16[128,512]{1,0:T(8,128)(2,1)S(1)}, bf16[128,512]{1,0:T(8,128)(2,1)S(1)}, u32[]{:S(2)}, u32[]{:S(2)}) collective-permute-start(bf16[128,512]{1,0:T(8,128)(2,1)S(1)} %get-tuple-element.57), channel_id=1, source_target_pairs={{0,6},{1,14},{2,0},{3,8},{4,2},{5,10},{6,4},{7,12},{8,15},{9,7},{1... | collective-permute-start | bytes 393224 | tf_op jit(solution)/shard_map/ppermute | solution.py:30
  139.0 4.7 %collective-permute-done.23.refs_1_ = bf16[128,512]{1,0:T(8,128)(2,1)S(1)} collective-permute-done((bf16[128,512]{1,0:T(8,128)(2,1)S(1)}, bf16[128,512]{1,0:T(8,128)(2,1)S(1)}, u32[]{:S(2)}, u32[]{:S(2)}) %collective-permute-start.23) | collective-permute-done | bytes 131104 | tf_op jit(solution)/shard_map/ppermute | solution.py:30
  143.7 0.3 collective-permute-done.25.refs_3_
  144.0 1.6 %shard_map.55 = bf16[256,2048]{1,0:T(8,128)(2,1)} custom-call(s32[32]{0:T(128)S(1)} %dynamic-slice_bitcast_fusion.table, bf16[128,512]{1,0:T(8,128)(2,1)S(1)} %collective-permute-done.22.refs_0_, bf16[128,512]{1,0:T(8,128)(2,1)S(1)} %collective-permute-done.23.refs_1_, bf16[128,512]{1,0:T(8,128)(2,1)S(1)} %collective-permute-done.24.refs_2_, ...), custom_call_target="tpu_custom_call" | custom-call | bytes 2097152 | tf_op jit(solution)/shard_map/pallas_call | solution.py:257
  (40 shorter events, 0.8 us)
Async XLA Ops:
  0.0 8.9 %collective-permute-start = (bf16[256,512]{1,0:T(8,128)(2,1)}, bf16[256,512]{1,0:T(8,128)(2,1)S(1)}, u32[]{:S(2)}, u32[]{:S(2)}) collective-permute-start(bf16[256,512]{1,0:T(8,128)(2,1)} %param.5), channel_id=1, source_target_pairs={{0,64},{1,65},{2,66},{3,67},{4,68},{5,69},{6,70},{7,71},{8,72},{9,... | collective-permute-start | bytes 786440 | tf_op jit(solution)/shard_map/ppermute | solution.py:30
  2.5 6.4 %copy-start.1 = (bf16[256,512]{1,0:T(8,128)(2,1)S(1)}, bf16[256,512]{1,0:T(8,128)(2,1)}, u32[]{:S(2)}) copy-start(bf16[256,512]{1,0:T(8,128)(2,1)} %param.5) | copy-start | bytes 786436
  8.9 10.4 %collective-permute-start.1 = (bf16[1,2,128,512]{3,2,1,0:T(8,128)(2,1)S(1)}, bf16[1,2,128,512]{3,2,1,0:T(8,128)(2,1)S(1)}, u32[]{:S(2)}, u32[]{:S(2)}) collective-permute-start(bf16[1,2,128,512]{3,2,1,0:T(8,128)(2,1)S(1)} %get-tuple-element.36), channel_id=1, source_target_pairs={{0,2},{1,7},{2,0},{3,5},{4,6},{5,3},{6,4},{7,1},{8,10},{9,15},{10,... | collective-permute-start | bytes 786440 | tf_op jit(solution)/shard_map/ppermute | solution.py:30
  12.8 6.7 %collective-permute-start.2 = (bf16[1,2,128,512]{3,2,1,0:T(8,128)(2,1)S(1)}, bf16[1,2,128,512]{3,2,1,0:T(8,128)(2,1)S(1)}, u32[]{:S(2)}, u32[]{:S(2)}) collective-permute-start(bf16[1,2,128,512]{3,2,1,0:T(8,128)(2,1)S(1)} %get-tuple-element.37), channel_id=1, source_target_pairs={{0,16},{1,49},{2,18},{3,51},{4,20},{5,53},{6,22},{7,55},{8,24},{9,... | collective-permute-start | bytes 786440 | tf_op jit(solution)/shard_map/ppermute | solution.py:30
  18.8 9.3 %collective-permute-start.5 = (bf16[2048,256]{1,0:T(8,128)(2,1)S(1)}, bf16[2048,256]{1,0:T(8,128)(2,1)S(1)}, u32[]{:S(2)}, u32[]{:S(2)}) collective-permute-start(bf16[2048,256]{1,0:T(8,128)(2,1)S(1)} %get-tuple-element.42), channel_id=1, source_target_pairs={{0,1},{1,0},{2,3},{3,2},{4,5},{5,4},{6,7},{7,6},{8,9},{9,8},{10,11... | collective-permute-start | bytes 3145736 | tf_op jit(solution)/shard_map/ppermute | solution.py:30
  18.9 9.3 %collective-permute-start.6 = (bf16[2048,256]{1,0:T(8,128)(2,1)S(1)}, bf16[2048,256]{1,0:T(8,128)(2,1)S(1)}, u32[]{:S(2)}, u32[]{:S(2)}) collective-permute-start(bf16[2048,256]{1,0:T(8,128)(2,1)S(1)} %get-tuple-element.43), channel_id=1, source_target_pairs={{0,1},{1,0},{2,3},{3,2},{4,5},{5,4},{6,7},{7,6},{8,9},{9,8},{10,11... | collective-permute-start | bytes 3145736 | tf_op jit(solution)/shard_map/ppermute | solution.py:30
  19.5 8.4 %collective-permute-start.3 = (bf16[2,2,128,512]{3,2,1,0:T(8,128)(2,1)S(1)}, bf16[2,2,128,512]{3,2,1,0:T(8,128)(2,1)S(1)}, u32[]{:S(2)}, u32[]{:S(2)}) collective-permute-start(bf16[2,2,128,512]{3,2,1,0:T(8,128)(2,1)S(1)} %pad_maximum_fusion.2), channel_id=1, source_target_pairs={{0,6},{1,3},{2,4},{3,1},{4,2},{5,7},{6,0},{7,5},{8,14},{9,11},{10,... | collective-permute-start | bytes 1572872 | tf_op jit(solution)/shard_map/ppermute | solution.py:30
  19.6 8.4 %collective-permute-start.4 = (bf16[2,2,128,512]{3,2,1,0:T(8,128)(2,1)S(1)}, bf16[2,2,128,512]{3,2,1,0:T(8,128)(2,1)S(1)}, u32[]{:S(2)}, u32[]{:S(2)}) collective-permute-start(bf16[2,2,128,512]{3,2,1,0:T(8,128)(2,1)S(1)} %pad_maximum_fusion.3), channel_id=1, source_target_pairs={{0,48},{1,17},{2,50},{3,19},{4,52},{5,21},{6,54},{7,23},{8,56},{9,... | collective-permute-start | bytes 1572872 | tf_op jit(solution)/shard_map/ppermute | solution.py:30
  19.8 19.9 %collective-permute-start.8 = (bf16[2048,256]{1,0:T(8,128)(2,1)S(1)}, bf16[2048,256]{1,0:T(8,128)(2,1)S(1)}, u32[]{:S(2)}, u32[]{:S(2)}) collective-permute-start(bf16[2048,256]{1,0:T(8,128)(2,1)S(1)} %get-tuple-element.34), channel_id=1, source_target_pairs={{0,8},{1,9},{2,10},{3,11},{4,12},{5,13},{6,14},{7,15},{8,0},{9,1},... | collective-permute-start | bytes 3145736 | tf_op jit(solution)/shard_map/ppermute | solution.py:30
  28.1 16.4 %collective-permute-start.10 = (bf16[4,2,128,512]{3,2,1,0:T(8,128)(2,1)S(1)}, bf16[4,2,128,512]{3,2,1,0:T(8,128)(2,1)S(1)}, u32[]{:S(2)}, u32[]{:S(2)}) collective-permute-start(bf16[4,2,128,512]{3,2,1,0:T(8,128)(2,1)S(1)} %pad_maximum_fusion.refs_3_.refs_0_), channel_id=1, source_target_pairs={{0,16},{1,49},{2,18},{3,51},{4,20},{5,53},{6,22},{7,55},{8,24},{9,... | collective-permute-start | bytes 3145736 | tf_op jit(solution)/shard_map/ppermute | solution.py:30
  30.7 14.9 %collective-permute-start.7 = (bf16[4,2,128,512]{3,2,1,0:T(8,128)(2,1)S(1)}, bf16[4,2,128,512]{3,2,1,0:T(8,128)(2,1)S(1)}, u32[]{:S(2)}, u32[]{:S(2)}) collective-permute-start(bf16[4,2,128,512]{3,2,1,0:T(8,128)(2,1)S(1)} %pad_maximum_fusion.1.refs_0_), channel_id=1, source_target_pairs={{0,2},{1,7},{2,0},{3,5},{4,6},{5,3},{6,4},{7,1},{8,10},{9,15},{10,... | collective-permute-start | bytes 3145736 | tf_op jit(solution)/shard_map/ppermute | solution.py:30
  39.8 18.5 %collective-permute-start.13 = (bf16[4,2,128,512]{3,2,1,0:T(8,128)(2,1)S(1)}, bf16[4,2,128,512]{3,2,1,0:T(8,128)(2,1)S(1)}, u32[]{:S(2)}, u32[]{:S(2)}) collective-permute-start(bf16[4,2,128,512]{3,2,1,0:T(8,128)(2,1)S(1)} %pad_maximum_fusion.1.refs_0_), channel_id=1, source_target_pairs={{0,6},{1,3},{2,4},{3,1},{4,2},{5,7},{6,0},{7,5},{8,14},{9,11},{10,... | collective-permute-start | bytes 3145736 | tf_op jit(solution)/shard_map/ppermute | solution.py:30
  41.8 16.5 %collective-permute-start.14 = (bf16[4,2,128,512]{3,2,1,0:T(8,128)(2,1)S(1)}, bf16[4,2,128,512]{3,2,1,0:T(8,128)(2,1)S(1)}, u32[]{:S(2)}, u32[]{:S(2)}) collective-permute-start(bf16[4,2,128,512]{3,2,1,0:T(8,128)(2,1)S(1)} %pad_maximum_fusion.refs_3_.refs_0_), channel_id=1, source_target_pairs={{0,48},{1,17},{2,50},{3,19},{4,52},{5,21},{6,54},{7,23},{8,56},{9,... | collective-permute-start | bytes 3145736 | tf_op jit(solution)/shard_map/ppermute | solution.py:30
  45.6 23.9 %collective-permute-start.9 = (bf16[4,2,128,512]{3,2,1,0:T(8,128)(2,1)S(1)}, bf16[4,2,128,512]{3,2,1,0:T(8,128)(2,1)S(1)}, u32[]{:S(2)}, u32[]{:S(2)}) collective-permute-start(bf16[4,2,128,512]{3,2,1,0:T(8,128)(2,1)S(1)} %collective-permute-done.7.refs_1_), channel_id=1, source_target_pairs={{0,6},{1,3},{2,4},{3,1},{4,2},{5,7},{6,0},{7,5},{8,14},{9,11},{10,... | collective-permute-start | bytes 3145736 | tf_op jit(solution)/shard_map/ppermute | solution.py:30
  46.0 23.5 %collective-permute-start.11 = (bf16[4,2,128,512]{3,2,1,0:T(8,128)(2,1)S(1)}, bf16[4,2,128,512]{3,2,1,0:T(8,128)(2,1)S(1)}, u32[]{:S(2)}, u32[]{:S(2)}) collective-permute-start(bf16[4,2,128,512]{3,2,1,0:T(8,128)(2,1)S(1)} %collective-permute-done.10.refs_4_.refs_1_), channel_id=1, source_target_pairs={{0,48},{1,17},{2,50},{3,19},{4,52},{5,21},{6,54},{7,23},{8,56},{9,... | collective-permute-start | bytes 3145736 | tf_op jit(solution)/shard_map/ppermute | solution.py:30
  46.0 23.5 %collective-permute-start.12 = (bf16[2048,256]{1,0:T(8,128)(2,1)S(1)}, bf16[2048,256]{1,0:T(8,128)(2,1)S(1)}, u32[]{:S(2)}, u32[]{:S(2)}) collective-permute-start(bf16[2048,256]{1,0:T(8,128)(2,1)S(1)} %collective-permute-done.6), channel_id=1, source_target_pairs={{0,8},{1,9},{2,10},{3,11},{4,12},{5,13},{6,14},{7,15},{8,0},{9,1},... | collective-permute-start | bytes 3145736 | tf_op jit(solution)/shard_map/ppermute | solution.py:30
  71.3 8.8 %collective-permute-start.26 = (bf16[4,128,1024]{2,1,0:T(8,128)(2,1)S(1)}, bf16[4,128,1024]{2,1,0:T(8,128)(2,1)S(1)}, u32[]{:S(2)}, u32[]{:S(2)}) collective-permute-start(bf16[4,128,1024]{2,1,0:T(8,128)(2,1)S(1)} %shard_map.53), channel_id=1, source_target_pairs={{0,1},{1,0},{2,3},{3,2},{4,5},{5,4},{6,7},{7,6},{8,9},{9,8},{10,11... | collective-permute-start | bytes 3145736 | tf_op jit(solution)/shard_map/ppermute | solution.py:30
  78.3 4.4 %collective-permute-start.15 = (bf16[4,128,1024]{2,1,0:T(8,128)(2,1)S(1)}, bf16[4,128,1024]{2,1,0:T(8,128)(2,1)S(1)}, u32[]{:S(2)}, u32[]{:S(2)}) collective-permute-start(bf16[4,128,1024]{2,1,0:T(8,128)(2,1)S(1)} %shard_map.50), channel_id=1, source_target_pairs={{0,1},{1,0},{2,3},{3,2},{4,5},{5,4},{6,7},{7,6},{8,9},{9,8},{10,11... | collective-permute-start | bytes 3145736 | tf_op jit(solution)/shard_map/ppermute | solution.py:30
  80.7 13.1 %collective-permute-start.27 = (bf16[4,128,512]{2,1,0:T(8,128)(2,1)S(1)}, bf16[4,128,512]{2,1,0:T(8,128)(2,1)S(1)}, u32[]{:S(2)}, u32[]{:S(2)}) collective-permute-start(bf16[4,128,512]{2,1,0:T(8,128)(2,1)S(1)} %slice.96), channel_id=1, source_target_pairs={{0,8},{1,9},{2,10},{3,11},{4,12},{5,13},{6,14},{7,15},{8,0},{9,1},... | collective-permute-start | bytes 1572872 | tf_op jit(solution)/shard_map/ppermute | solution.py:30
  83.1 21.9 %collective-permute-start.16 = (bf16[4,128,512]{2,1,0:T(8,128)(2,1)S(1)}, bf16[4,128,512]{2,1,0:T(8,128)(2,1)S(1)}, u32[]{:S(2)}, u32[]{:S(2)}) collective-permute-start(bf16[4,128,512]{2,1,0:T(8,128)(2,1)S(1)} %slice.97), channel_id=1, source_target_pairs={{0,8},{1,9},{2,10},{3,11},{4,12},{5,13},{6,14},{7,15},{8,0},{9,1},... | collective-permute-start | bytes 1572872 | tf_op jit(solution)/shard_map/ppermute | solution.py:30
  94.0 15.0 %collective-permute-start.28 = (bf16[128,512]{1,0:T(8,128)(2,1)S(1)}, bf16[128,512]{1,0:T(8,128)(2,1)S(1)}, u32[]{:S(2)}, u32[]{:S(2)}) collective-permute-start(bf16[128,512]{1,0:T(8,128)(2,1)S(1)} %get-tuple-element.63), channel_id=1, source_target_pairs={{0,0},{1,65},{2,2},{3,67},{4,4},{5,69},{6,6},{7,71},{8,8},{9,73},{... | collective-permute-start | bytes 393224 | tf_op jit(solution)/shard_map/ppermute | solution.py:30
  97.7 14.9 %collective-permute-start.31 = (bf16[128,512]{1,0:T(8,128)(2,1)S(1)}, bf16[128,512]{1,0:T(8,128)(2,1)S(1)}, u32[]{:S(2)}, u32[]{:S(2)}) collective-permute-start(bf16[128,512]{1,0:T(8,128)(2,1)S(1)} %get-tuple-element.64), channel_id=1, source_target_pairs={{0,48},{1,113},{2,50},{3,115},{4,52},{5,117},{6,54},{7,119},{8,56}... | collective-permute-start | bytes 393224 | tf_op jit(solution)/shard_map/ppermute | solution.py:30
  101.4 13.3 %collective-permute-start.30 = (bf16[128,512]{1,0:T(8,128)(2,1)S(1)}, bf16[128,512]{1,0:T(8,128)(2,1)S(1)}, u32[]{:S(2)}, u32[]{:S(2)}) collective-permute-start(bf16[128,512]{1,0:T(8,128)(2,1)S(1)} %get-tuple-element.65), channel_id=1, source_target_pairs={{0,32},{1,97},{2,34},{3,99},{4,36},{5,101},{6,38},{7,103},{8,40},{... | collective-permute-start | bytes 393224 | tf_op jit(solution)/shard_map/ppermute | solution.py:30
  102.1 12.9 %collective-permute-start.29 = (bf16[128,512]{1,0:T(8,128)(2,1)S(1)}, bf16[128,512]{1,0:T(8,128)(2,1)S(1)}, u32[]{:S(2)}, u32[]{:S(2)}) collective-permute-start(bf16[128,512]{1,0:T(8,128)(2,1)S(1)} %get-tuple-element.66), channel_id=1, source_target_pairs={{0,16},{1,81},{2,18},{3,83},{4,20},{5,85},{6,22},{7,87},{8,24},{9,... | collective-permute-start | bytes 393224 | tf_op jit(solution)/shard_map/ppermute | solution.py:30
  105.2 17.2 %copy-start = (s32[8]{0:T(128)S(1)}, s32[8]{0:T(128)}, u32[]{:S(2)}) copy-start(s32[8]{0:T(128)} %owner.3) | copy-start | bytes 100
  105.2 9.9 %collective-permute-start.17 = (bf16[128,512]{1,0:T(8,128)(2,1)S(1)}, bf16[128,512]{1,0:T(8,128)(2,1)S(1)}, u32[]{:S(2)}, u32[]{:S(2)}) collective-permute-start(bf16[128,512]{1,0:T(8,128)(2,1)S(1)} %get-tuple-element.67), channel_id=1, source_target_pairs={{0,0},{1,65},{2,2},{3,67},{4,4},{5,69},{6,6},{7,71},{8,8},{9,73},{... | collective-permute-start | bytes 393224 | tf_op jit(solution)/shard_map/ppermute | solution.py:30
  109.0 6.4 %collective-permute-start.20 = (bf16[128,512]{1,0:T(8,128)(2,1)S(1)}, bf16[128,512]{1,0:T(8,128)(2,1)S(1)}, u32[]{:S(2)}, u32[]{:S(2)}) collective-permute-start(bf16[128,512]{1,0:T(8,128)(2,1)S(1)} %get-tuple-element.68), channel_id=1, source_target_pairs={{0,48},{1,113},{2,50},{3,115},{4,52},{5,117},{6,54},{7,119},{8,56}... | collective-permute-start | bytes 393224 | tf_op jit(solution)/shard_map/ppermute | solution.py:30
  112.6 7.7 %collective-permute-start.19 = (bf16[128,512]{1,0:T(8,128)(2,1)S(1)}, bf16[128,512]{1,0:T(8,128)(2,1)S(1)}, u32[]{:S(2)}, u32[]{:S(2)}) collective-permute-start(bf16[128,512]{1,0:T(8,128)(2,1)S(1)} %get-tuple-element.69), channel_id=1, source_target_pairs={{0,32},{1,97},{2,34},{3,99},{4,36},{5,101},{6,38},{7,103},{8,40},{... | collective-permute-start | bytes 393224 | tf_op jit(solution)/shard_map/ppermute | solution.py:30
  114.7 7.4 %collective-permute-start.18 = (bf16[128,512]{1,0:T(8,128)(2,1)S(1)}, bf16[128,512]{1,0:T(8,128)(2,1)S(1)}, u32[]{:S(2)}, u32[]{:S(2)}) collective-permute-start(bf16[128,512]{1,0:T(8,128)(2,1)S(1)} %get-tuple-element.70), channel_id=1, source_target_pairs={{0,16},{1,81},{2,18},{3,83},{4,20},{5,85},{6,22},{7,87},{8,24},{9,... | collective-permute-start | bytes 393224 | tf_op jit(solution)/shard_map/ppermute | solution.py:30
  115.0 7.3 %collective-permute-start.32 = (bf16[4,128,512]{2,1,0:T(8,128)(2,1)S(1)}, bf16[4,128,512]{2,1,0:T(8,128)(2,1)S(1)}, u32[]{:S(2)}, u32[]{:S(2)}) collective-permute-start(bf16[4,128,512]{2,1,0:T(8,128)(2,1)S(1)} %pad_maximum_fusion.5.own), channel_id=1, source_target_pairs={{0,1},{1,0},{2,3},{3,2},{4,5},{5,4},{6,7},{7,6},{8,9},{9,8},{10,11... | collective-permute-start | bytes 1572872 | tf_op jit(solution)/shard_map/ppermute | solution.py:30
  122.2 8.3 %collective-permute-start.21 = (bf16[4,128,512]{2,1,0:T(8,128)(2,1)S(1)}, bf16[4,128,512]{2,1,0:T(8,128)(2,1)S(1)}, u32[]{:S(2)}, u32[]{:S(2)}) collective-permute-start(bf16[4,128,512]{2,1,0:T(8,128)(2,1)S(1)} %pad_maximum_fusion.4.own), channel_id=1, source_target_pairs={{0,1},{1,0},{2,3},{3,2},{4,5},{5,4},{6,7},{7,6},{8,9},{9,8},{10,11... | collective-permute-start | bytes 1572872 | tf_op jit(solution)/shard_map/ppermute | solution.py:30
  123.0 10.8 %collective-permute-start.33 = (bf16[128,512]{1,0:T(8,128)(2,1)S(1)}, bf16[128,512]{1,0:T(8,128)(2,1)S(1)}, u32[]{:S(2)}, u32[]{:S(2)}) collective-permute-start(bf16[128,512]{1,0:T(8,128)(2,1)S(1)} %get-tuple-element.59), channel_id=1, source_target_pairs={{0,0},{1,8},{2,2},{3,10},{4,4},{5,12},{6,6},{7,14},{8,9},{9,1},{10... | collective-permute-start | bytes 393224 | tf_op jit(solution)/shard_map/ppermute | solution.py:30
  126.1 9.5 %collective-permute-start.34 = (bf16[128,512]{1,0:T(8,128)(2,1)S(1)}, bf16[128,512]{1,0:T(8,128)(2,1)S(1)}, u32[]{:S(2)}, u32[]{:S(2)}) collective-permute-start(bf16[128,512]{1,0:T(8,128)(2,1)S(1)} %get-tuple-element.60), channel_id=1, source_target_pairs={{0,2},{1,10},{2,4},{3,12},{4,6},{5,14},{6,0},{7,8},{8,11},{9,3},{1... | collective-permute-start | bytes 393224 | tf_op jit(solution)/shard_map/ppermute | solution.py:30
  126.2 9.4 %collective-permute-start.35 = (bf16[128,512]{1,0:T(8,128)(2,1)S(1)}, bf16[128,512]{1,0:T(8,128)(2,1)S(1)}, u32[]{:S(2)}, u32[]{:S(2)}) collective-permute-start(bf16[128,512]{1,0:T(8,128)(2,1)S(1)} %get-tuple-element.61), channel_id=1, source_target_pairs={{0,4},{1,12},{2,6},{3,14},{4,0},{5,8},{6,2},{7,10},{8,13},{9,5},{1... | collective-permute-start | bytes 393224 | tf_op jit(solution)/shard_map/ppermute | solution.py:30
  128.2 10.8 %collective-permute-start.36 = (bf16[128,512]{1,0:T(8,128)(2,1)S(1)}, bf16[128,512]{1,0:T(8,128)(2,1)S(1)}, u32[]{:S(2)}, u32[]{:S(2)}) collective-permute-start(bf16[128,512]{1,0:T(8,128)(2,1)S(1)} %get-tuple-element.62), channel_id=1, source_target_pairs={{0,6},{1,14},{2,0},{3,8},{4,2},{5,10},{6,4},{7,12},{8,15},{9,7},{1... | collective-permute-start | bytes 393224 | tf_op jit(solution)/shard_map/ppermute | solution.py:30
  131.2 7.8 %collective-permute-start.22 = (bf16[128,512]{1,0:T(8,128)(2,1)S(1)}, bf16[128,512]{1,0:T(8,128)(2,1)S(1)}, u32[]{:S(2)}, u32[]{:S(2)}) collective-permute-start(bf16[128,512]{1,0:T(8,128)(2,1)S(1)} %get-tuple-element.54), channel_id=1, source_target_pairs={{0,0},{1,8},{2,2},{3,10},{4,4},{5,12},{6,6},{7,14},{8,9},{9,1},{10... | collective-permute-start | bytes 393224 | tf_op jit(solution)/shard_map/ppermute | solution.py:30
  133.8 9.9 %collective-permute-start.23 = (bf16[128,512]{1,0:T(8,128)(2,1)S(1)}, bf16[128,512]{1,0:T(8,128)(2,1)S(1)}, u32[]{:S(2)}, u32[]{:S(2)}) collective-permute-start(bf16[128,512]{1,0:T(8,128)(2,1)S(1)} %get-tuple-element.55), channel_id=1, source_target_pairs={{0,2},{1,10},{2,4},{3,12},{4,6},{5,14},{6,0},{7,8},{8,11},{9,3},{1... | collective-permute-start | bytes 393224 | tf_op jit(solution)/shard_map/ppermute | solution.py:30
  135.5 8.2 %collective-permute-start.24 = (bf16[128,512]{1,0:T(8,128)(2,1)S(1)}, bf16[128,512]{1,0:T(8,128)(2,1)S(1)}, u32[]{:S(2)}, u32[]{:S(2)}) collective-permute-start(bf16[128,512]{1,0:T(8,128)(2,1)S(1)} %get-tuple-element.56), channel_id=1, source_target_pairs={{0,4},{1,12},{2,6},{3,14},{4,0},{5,8},{6,2},{7,10},{8,13},{9,5},{1... | collective-permute-start | bytes 393224 | tf_op jit(solution)/shard_map/ppermute | solution.py:30
  135.6 8.5 %collective-permute-start.25 = (bf16[128,512]{1,0:T(8,128)(2,1)S(1)}, bf16[128,512]{1,0:T(8,128)(2,1)S(1)}, u32[]{:S(2)}, u32[]{:S(2)}) collective-permute-start(bf16[128,512]{1,0:T(8,128)(2,1)S(1)} %get-tuple-element.57), channel_id=1, source_target_pairs={{0,6},{1,14},{2,0},{3,8},{4,2},{5,10},{6,4},{7,12},{8,15},{9,7},{1... | collective-permute-start | bytes 393224 | tf_op jit(solution)/shard_map/ppermute | solution.py:30

commit v16 on v15

--- a/solution.py
+++ b/solution.py
@@ -152,9 +152,9 @@
 EARLY, LATE = (0, 1, 2), 3
 
 
-def early_kernel(table, mine, near, far, *refs):
-    z_slots, y_slots, (z_out, y_out) = refs[:3], refs[3:6], refs[6:]
-    for piece, weight in enumerate((mine, near, far)):
+def early_kernel(count, table, *refs):
+    weights, z_slots, y_slots, (z_out, y_out) = refs[:count], refs[count : count + 3], refs[count + 3 : -2], refs[-2:]
+    for piece, weight in enumerate(weights):
         for half in range(2):
             got = None
             for n, slot in zip(EARLY, z_slots):
@@ -171,56 +171,47 @@
 def early_product(table, weights, slots):
     vmem = pl.BlockSpec(memory_space=pltpu.VMEM)
     parts = [slots[part][n] for part in "zy" for n in EARLY]
-    shapes = [(3, 2, 4 * HALF, COLS), (3, 2, 3 * HALF, COLS)]
+    count = len(weights)
+    shapes = [(count, 2, 4 * HALF, COLS), (count, 2, 3 * HALF, COLS)]
     return pl.pallas_call(
-        early_kernel,
-        in_specs=[pl.BlockSpec(memory_space=pltpu.SMEM)] + [vmem] * 9,
+        functools.partial(early_kernel, count),
+        in_specs=[pl.BlockSpec(memory_space=pltpu.SMEM)] + [vmem] * (count + 6),
         out_specs=[vmem] * 2,
         out_shape=[jax.ShapeDtypeStruct(shape, jnp.float32) for shape in shapes],
         compiler_params=pltpu.CompilerParams(vmem_limit_bytes=24 * MIB),
-        cost_estimate=pl.CostEstimate(flops=5 * 2**30, bytes_accessed=16 * MIB, transcendentals=0),
-    )(table, *weights[:3], *parts)
+        cost_estimate=pl.CostEstimate(flops=count * 2**30, bytes_accessed=16 * MIB, transcendentals=0),
+    )(table, *weights, *parts)
 
 
 def product_kernel(part, keep, table, mine, near, far, cross, *refs):
-    slots, early, out = refs[:4], refs[4], refs[5]
+    slot, first, last, out = refs
     core = table[CORE]
     half = core if keep else 1 - core
-
-    def rows(n, some):
-        if part == "y":
-            return jnp.concatenate([slots[i][n, half] for i in some])
-        return slots[n][:, half].reshape(4 * HALF, SHARE)
-
     for piece, (weight, cols) in enumerate(pieces(core, mine, near, far, cross)):
-        last = piece == 3
-        some = EARLY + (LATE,) if last else (LATE,)
-        got = None
-        for n in range(4) if part == "y" else some:
-            term = dot(rows(n, some), weight[depth_of(table, n), :])
-            got = term if got is None else got + term
-        if not last and part == "z":
-            got += early[piece, half]
+        early = first.at[piece, half] if piece < 3 else last.at[0, half]
+        if part == "z":
+            got = early[...] + dot(slot[:, half].reshape(4 * HALF, SHARE), weight[depth_of(table, LATE), :])
+            values = [got[ys * HALF : (ys + 1) * HALF] for ys in range(4)]
+        else:
+            got = None
+            for n in range(4):
+                term = dot(slot[n, half], weight[depth_of(table, n), :])
+                got = term if got is None else got + term
+            values = [early[pl.ds(n * HALF, HALF)] for n in range(3)] + [got]
         for ys in range(4):
-            if last or part == "z":
-                value = got[ys * HALF : (ys + 1) * HALF]
-            elif ys == LATE:
-                value = got
-            else:
-                value = early[piece, half, pl.ds(EARLY.index(ys) * HALF, HALF)]
-            out[table[Y_SLOT + ys], :, cols] = value.astype(out.dtype)
-
-
-def product(part, keep, table, weights, slots, early):
+            out[table[Y_SLOT + ys], :, cols] = values[ys].astype(out.dtype)
+
+
+def product(part, keep, table, weights, slot, early):
     vmem = pl.BlockSpec(memory_space=pltpu.VMEM)
     return pl.pallas_call(
         functools.partial(product_kernel, part, keep),
-        in_specs=[pl.BlockSpec(memory_space=pltpu.SMEM)] + [vmem] * 9,
+        in_specs=[pl.BlockSpec(memory_space=pltpu.SMEM)] + [vmem] * 7,
         out_specs=vmem,
         out_shape=jax.ShapeDtypeStruct((4, HALF, 4 * COLS), jnp.float32 if keep else jnp.bfloat16),
         compiler_params=pltpu.CompilerParams(vmem_limit_bytes=24 * MIB),
-        cost_estimate=pl.CostEstimate(flops=2**30, bytes_accessed=8 * MIB, transcendentals=0),
-    )(table, *weights, *slots, early)
+        cost_estimate=pl.CostEstimate(flops=2**29, bytes_accessed=8 * MIB, transcendentals=0),
+    )(table, *weights, slot, *early)
 
 
 def spread_kernel(table, owner, own, other, *outs):
@@ -279,12 +270,13 @@
     slots = gather(activations, same, (near, swapped), far)
     cross = permute(after(swapped, far), other_chip)
     weights = [mine, near, far, cross]
-    early = dict(zip("zy", early_product(table, weights, slots)))
+    early = early_product(table, weights[:3], slots)
+    early = dict(zip("zy", zip(early, early_product(after(table, *early), weights[3:], slots))))
     ready = after(table, slots["z"][LATE], slots["y"][LATE])
 
     def chain(part):
-        passed = product(part, False, ready, weights, slots[part], early[part])
-        kept = product(part, True, ready, weights, slots[part], early[part])
+        passed = product(part, False, ready, weights, slots[part][LATE], early[part])
+        kept = product(part, True, ready, weights, slots[part][LATE], early[part])
         both = kept + permute(passed, other_core).astype(f32)
         came = permute(both[..., 2 * COLS :].astype(bf16), other_chip)
         total = (both[..., : 2 * COLS] + came.astype(f32)).astype(bf16)

time: 146 us -> 146 us (level)
  waiting for transfers between devices: 62 us -> 59.9 us
    pallas_call x1 -> x2, Pallas kernels: 5.58 us -> 7.91 us  [early_product(): pl.pallas_call(functools.partial(early_kernel, count), in_specs=[pl.Block...]
    ppermute x37, waiting for transfers between devices: 62 us -> 59.9 us  [permute(): lax.ppermute(value, AXES, [(i, move(*coords(i))) for i in range(N_DEV)])]
  transfers between devices with their start and end apart: 37 -> 37, of which waited for: 14 -> 14; matrix products, arithmetic and copies ran while one was open for 2% -> 2% of each run, Pallas kernels for 13% -> 14%
where the time goes in v16:
time: 146 us; the launch traced here: 145 us
  waiting for transfers between devices  59.9 us (41%)
  starting transfers between devices  59.3 us (41%)
  Pallas kernels  22.9 us (16%)
  other arithmetic  1.68 us (1%)
    ppermute x37, waiting for transfers between devices, permute(): lax.ppermute(value, AXES, [(i, move(*coords(i))) for i in range(N_DEV)])  59.9 us
    ppermute x37, starting transfers between devices, permute(): lax.ppermute(value, AXES, [(i, move(*coords(i))) for i in range(N_DEV)])  59.3 us
    pallas_call x2, Pallas kernels, early_product(): pl.pallas_call(functools.partial(early_kernel, count), in_specs=[pl.Block...  7.91 us
    pallas_call x2, Pallas kernels, refit(): pl.pallas_call(functools.partial(refit_kernel, first), in_specs=[pl.Block...  6.55 us
    pallas_call x4, Pallas kernels, product(): pl.pallas_call(functools.partial(product_kernel, part, keep), in_specs=[p...  5.52 us
  transfers between devices with their start and end apart: 37, of which 14 were waited for; matrix products, arithmetic and copies ran while one was open for 2% of the time, Pallas kernels for 14%

profile of v16, /device:TPU:3, one launch (start us, length us, event | category | flops | bytes accessed | tf_op | source)
XLA Modules:
  0.0 145.3 jit_solution(18086434431018863929)
XLA Ops:
  0.0 1.8 %collective-permute-start = (bf16[256,512]{1,0:T(8,128)(2,1)}, bf16[256,512]{1,0:T(8,128)(2,1)S(1)}, u32[]{:S(2)}, u32[]{:S(2)}) collective-permute-start(bf16[256,512]{1,0:T(8,128)(2,1)} %param.5), channel_id=1, source_target_pairs={{0,64},{1,65},{2,66},{3,67},{4,68},{5,69},{6,70},{7,71},{8,72},{9,... | collective-permute-start | bytes 786440 | tf_op jit(solution)/shard_map/ppermute | solution.py:30
  1.8 0.7 dynamic-slice_bitcast_fusion.table
  2.5 3.3 %shard_map.46 = (bf16[2048,256]{1,0:T(8,128)(2,1)S(1)}, bf16[2048,256]{1,0:T(8,128)(2,1)S(1)}) custom-call(s32[32]{0:T(128)S(1)} %dynamic-slice_bitcast_fusion.table, f32[8192,256]{1,0:T(8,128)} %master.3), custom_call_target="tpu_custom_call" | custom-call | flops 6291456 | bytes 6291456 | tf_op jit(solution)/shard_map/pallas_call | solution.py:122
  5.8 3.1 %collective-permute-done = bf16[256,512]{1,0:T(8,128)(2,1)S(1)} collective-permute-done((bf16[256,512]{1,0:T(8,128)(2,1)}, bf16[256,512]{1,0:T(8,128)(2,1)S(1)}, u32[]{:S(2)}, u32[]{:S(2)}) %collective-permute-start) | collective-permute-done | bytes 262176 | tf_op jit(solution)/shard_map/ppermute | solution.py:30
  8.9 2.8 %collective-permute-start.2 = (bf16[1,2,128,512]{3,2,1,0:T(8,128)(2,1)S(1)}, bf16[1,2,128,512]{3,2,1,0:T(8,128)(2,1)S(1)}, u32[]{:S(2)}, u32[]{:S(2)}) collective-permute-start(bf16[1,2,128,512]{3,2,1,0:T(8,128)(2,1)S(1)} %get-tuple-element.40), channel_id=1, source_target_pairs={{0,16},{1,49},{2,18},{3,51},{4,20},{5,53},{6,22},{7,55},{8,24},{9,... | collective-permute-start | bytes 786440 | tf_op jit(solution)/shard_map/ppermute | solution.py:30
  11.8 3.8 %collective-permute-start.1 = (bf16[1,2,128,512]{3,2,1,0:T(8,128)(2,1)S(1)}, bf16[1,2,128,512]{3,2,1,0:T(8,128)(2,1)S(1)}, u32[]{:S(2)}, u32[]{:S(2)}) collective-permute-start(bf16[1,2,128,512]{3,2,1,0:T(8,128)(2,1)S(1)} %get-tuple-element.39), channel_id=1, source_target_pairs={{0,2},{1,7},{2,0},{3,5},{4,6},{5,3},{6,4},{7,1},{8,10},{9,15},{10,... | collective-permute-start | bytes 786440 | tf_op jit(solution)/shard_map/ppermute | solution.py:30
  15.5 3.3 %shard_map.47 = (bf16[2048,256]{1,0:T(8,128)(2,1)S(1)}, bf16[2048,256]{1,0:T(8,128)(2,1)S(1)}) custom-call(s32[32]{0:T(128)S(1)} %dynamic-slice_bitcast_fusion.table, f32[8192,256]{1,0:T(8,128)} %master.3), custom_call_target="tpu_custom_call" | custom-call | flops 6291456 | bytes 6291456 | tf_op jit(solution)/shard_map/pallas_call | solution.py:122
  18.9 0.5 collective-permute-start.6
  19.7 0.3 collective-permute-start.8
  20.0 7.9 %collective-permute-done.4 = bf16[2,2,128,512]{3,2,1,0:T(8,128)(2,1)S(1)} collective-permute-done((bf16[2,2,128,512]{3,2,1,0:T(8,128)(2,1)S(1)}, bf16[2,2,128,512]{3,2,1,0:T(8,128)(2,1)S(1)}, u32[]{:S(2)}, u32[]{:S(2)}) %collective-permute-start.4) | collective-permute-done | bytes 524320 | tf_op jit(solution)/shard_map/ppermute | solution.py:30
  27.9 0.1 pad_maximum_fusion.1.refs_3_.refs_1_
  28.0 0.1 pad_maximum_fusion.refs_6_.refs_4_
  28.1 1.0 collective-permute-start.10
  29.1 2.2 %collective-permute-start.7 = (bf16[4,2,128,512]{3,2,1,0:T(8,128)(2,1)S(1)}, bf16[4,2,128,512]{3,2,1,0:T(8,128)(2,1)S(1)}, u32[]{:S(2)}, u32[]{:S(2)}) collective-permute-start(bf16[4,2,128,512]{3,2,1,0:T(8,128)(2,1)S(1)} %pad_maximum_fusion.1.refs_3_.refs_1_), channel_id=1, source_target_pairs={{0,2},{1,7},{2,0},{3,5},{4,6},{5,3},{6,4},{7,1},{8,10},{9,15},{10,... | collective-permute-start | bytes 3145736 | tf_op jit(solution)/shard_map/ppermute | solution.py:30
  31.4 7.9 %collective-permute-done.8.refs_2_.far = bf16[2048,256]{1,0:T(8,128)(2,1)S(1)} collective-permute-done((bf16[2048,256]{1,0:T(8,128)(2,1)S(1)}, bf16[2048,256]{1,0:T(8,128)(2,1)S(1)}, u32[]{:S(2)}, u32[]{:S(2)}) %collective-permute-start.8) | collective-permute-done | bytes 1048608 | tf_op jit(solution)/shard_map/ppermute | solution.py:30
  39.3 3.2 %collective-permute-start.13 = (bf16[4,2,128,512]{3,2,1,0:T(8,128)(2,1)S(1)}, bf16[4,2,128,512]{3,2,1,0:T(8,128)(2,1)S(1)}, u32[]{:S(2)}, u32[]{:S(2)}) collective-permute-start(bf16[4,2,128,512]{3,2,1,0:T(8,128)(2,1)S(1)} %pad_maximum_fusion.1.refs_3_.refs_1_), channel_id=1, source_target_pairs={{0,6},{1,3},{2,4},{3,1},{4,2},{5,7},{6,0},{7,5},{8,14},{9,11},{10,... | collective-permute-start | bytes 3145736 | tf_op jit(solution)/shard_map/ppermute | solution.py:30
  42.6 2.3 %collective-permute-start.14 = (bf16[4,2,128,512]{3,2,1,0:T(8,128)(2,1)S(1)}, bf16[4,2,128,512]{3,2,1,0:T(8,128)(2,1)S(1)}, u32[]{:S(2)}, u32[]{:S(2)}) collective-permute-start(bf16[4,2,128,512]{3,2,1,0:T(8,128)(2,1)S(1)} %pad_maximum_fusion.refs_6_.refs_4_), channel_id=1, source_target_pairs={{0,48},{1,17},{2,50},{3,19},{4,52},{5,21},{6,54},{7,23},{8,56},{9,... | collective-permute-start | bytes 3145736 | tf_op jit(solution)/shard_map/ppermute | solution.py:30
  44.9 0.3 collective-permute-start.12
  45.2 0.3 collective-permute-start.9
  45.5 13.1 %collective-permute-done.13.refs_5_.refs_3_ = bf16[4,2,128,512]{3,2,1,0:T(8,128)(2,1)S(1)} collective-permute-done((bf16[4,2,128,512]{3,2,1,0:T(8,128)(2,1)S(1)}, bf16[4,2,128,512]{3,2,1,0:T(8,128)(2,1)S(1)}, u32[]{:S(2)}, u32[]{:S(2)}) %collective-permute-start.13) | collective-permute-done | bytes 1048608 | tf_op jit(solution)/shard_map/ppermute | solution.py:30
  58.5 5.6 %shard_map.48 = (f32[3,2,512,256]{3,2,1,0:T(8,128)S(1)}, f32[3,2,384,256]{3,2,1,0:T(8,128)S(1)}) custom-call(s32[32]{0:T(128)S(1)} %dynamic-slice_bitcast_fusion.table, bf16[2048,256]{1,0:T(8,128)(2,1)S(1)} %get-tuple-element.52.refs_0_.mine, bf16[2048,256]{1,0:T(8,128)(2,1)S(1)} %collective-permute-done.5.refs_1_.near, ...), custom_call_target="tpu_custom_call" | custom-call | flops 3221225472 | bytes 16777216 | tf_op jit(solution)/shard_map/pallas_call | solution.py:176
  64.1 2.3 %shard_map.49 = (f32[1,2,512,256]{3,2,1,0:T(8,128)S(1)}, f32[1,2,384,256]{3,2,1,0:T(8,128)S(1)}) custom-call(s32[32]{0:T(128)S(1)} %dynamic-slice_bitcast_fusion.table, bf16[2048,256]{1,0:T(8,128)(2,1)S(1)} %collective-permute-done.12.refs_0_.cross, bf16[4,2,128,512]{3,2,1,0:T(8,128)(2,1)S(1)} %pad_maximum_fusion.1.refs_3_.refs_1_, ...), custom_call_target="tpu_custom_call" | custom-call | flops 1073741824 | bytes 16777216 | tf_op jit(solution)/shard_map/pallas_call | solution.py:176
  66.5 2.6 %collective-permute-done.11.refs_0_ = bf16[4,2,128,512]{3,2,1,0:T(8,128)(2,1)S(1)} collective-permute-done((bf16[4,2,128,512]{3,2,1,0:T(8,128)(2,1)S(1)}, bf16[4,2,128,512]{3,2,1,0:T(8,128)(2,1)S(1)}, u32[]{:S(2)}, u32[]{:S(2)}) %collective-permute-start.11) | collective-permute-done | bytes 1048608 | tf_op jit(solution)/shard_map/ppermute | solution.py:30
  69.1 0.7 collective-permute-done.9.refs_0_
  69.8 1.4 shard_map.54
  71.2 5.7 %collective-permute-start.26 = (bf16[4,128,1024]{2,1,0:T(8,128)(2,1)S(1)}, bf16[4,128,1024]{2,1,0:T(8,128)(2,1)S(1)}, u32[]{:S(2)}, u32[]{:S(2)}) collective-permute-start(bf16[4,128,1024]{2,1,0:T(8,128)(2,1)S(1)} %shard_map.54), channel_id=1, source_target_pairs={{0,1},{1,0},{2,3},{3,2},{4,5},{5,4},{6,7},{7,6},{8,9},{9,8},{10,11... | collective-permute-start | bytes 3145736 | tf_op jit(solution)/shard_map/ppermute | solution.py:30
  76.8 1.3 shard_map.51
  78.2 0.1 collective-permute-start.15
  78.3 1.4 shard_map.53
  79.7 0.4 convert_add_fusion
  80.2 0.3 collective-permute-start.27
  80.6 1.4 shard_map.50
  82.0 0.4 convert_add_fusion.1
  82.5 1.3 collective-permute-start.16
  83.8 9.5 %collective-permute-done.27 = bf16[4,128,512]{2,1,0:T(8,128)(2,1)S(1)} collective-permute-done((bf16[4,128,512]{2,1,0:T(8,128)(2,1)S(1)}, bf16[4,128,512]{2,1,0:T(8,128)(2,1)S(1)}, u32[]{:S(2)}, u32[]{:S(2)}) %collective-permute-start.27) | collective-permute-done | bytes 524320 | tf_op jit(solution)/shard_map/ppermute | solution.py:30
  93.3 0.2 fusion
  93.5 3.7 %collective-permute-start.28 = (bf16[128,512]{1,0:T(8,128)(2,1)S(1)}, bf16[128,512]{1,0:T(8,128)(2,1)S(1)}, u32[]{:S(2)}, u32[]{:S(2)}) collective-permute-start(bf16[128,512]{1,0:T(8,128)(2,1)S(1)} %get-tuple-element.69), channel_id=1, source_target_pairs={{0,0},{1,65},{2,2},{3,67},{4,4},{5,69},{6,6},{7,71},{8,8},{9,73},{... | collective-permute-start | bytes 393224 | tf_op jit(solution)/shard_map/ppermute | solution.py:30
  97.3 1.0 collective-permute-start.29
  98.3 4.6 %collective-permute-start.30 = (bf16[128,512]{1,0:T(8,128)(2,1)S(1)}, bf16[128,512]{1,0:T(8,128)(2,1)S(1)}, u32[]{:S(2)}, u32[]{:S(2)}) collective-permute-start(bf16[128,512]{1,0:T(8,128)(2,1)S(1)} %get-tuple-element.71), channel_id=1, source_target_pairs={{0,32},{1,97},{2,34},{3,99},{4,36},{5,101},{6,38},{7,103},{8,40},{... | collective-permute-start | bytes 393224 | tf_op jit(solution)/shard_map/ppermute | solution.py:30
  102.9 0.7 collective-permute-start.31
  103.6 1.0 collective-permute-done.16
  104.5 0.2 fusion.1
  104.8 2.7 %collective-permute-start.19 = (bf16[128,512]{1,0:T(8,128)(2,1)S(1)}, bf16[128,512]{1,0:T(8,128)(2,1)S(1)}, u32[]{:S(2)}, u32[]{:S(2)}) collective-permute-start(bf16[128,512]{1,0:T(8,128)(2,1)S(1)} %get-tuple-element.75), channel_id=1, source_target_pairs={{0,32},{1,97},{2,34},{3,99},{4,36},{5,101},{6,38},{7,103},{8,40},{... | collective-permute-start | bytes 393224 | tf_op jit(solution)/shard_map/ppermute | solution.py:30
  107.5 2.8 %collective-permute-start.20 = (bf16[128,512]{1,0:T(8,128)(2,1)S(1)}, bf16[128,512]{1,0:T(8,128)(2,1)S(1)}, u32[]{:S(2)}, u32[]{:S(2)}) collective-permute-start(bf16[128,512]{1,0:T(8,128)(2,1)S(1)} %get-tuple-element.74), channel_id=1, source_target_pairs={{0,48},{1,113},{2,50},{3,115},{4,52},{5,117},{6,54},{7,119},{8,56}... | collective-permute-start | bytes 393224 | tf_op jit(solution)/shard_map/ppermute | solution.py:30
  110.3 1.3 collective-permute-done.29
  111.6 2.7 %collective-permute-start.17 = (bf16[128,512]{1,0:T(8,128)(2,1)S(1)}, bf16[128,512]{1,0:T(8,128)(2,1)S(1)}, u32[]{:S(2)}, u32[]{:S(2)}) collective-permute-start(bf16[128,512]{1,0:T(8,128)(2,1)S(1)} %get-tuple-element.73), channel_id=1, source_target_pairs={{0,0},{1,65},{2,2},{3,67},{4,4},{5,69},{6,6},{7,71},{8,8},{9,73},{... | collective-permute-start | bytes 393224 | tf_op jit(solution)/shard_map/ppermute | solution.py:30
  114.4 0.4 collective-permute-start.18
  114.9 0.3 collective-permute-start.32
  115.2 3.6 %collective-permute-done.17 = bf16[128,512]{1,0:T(8,128)(2,1)S(1)} collective-permute-done((bf16[128,512]{1,0:T(8,128)(2,1)S(1)}, bf16[128,512]{1,0:T(8,128)(2,1)S(1)}, u32[]{:S(2)}, u32[]{:S(2)}) %collective-permute-start.17) | collective-permute-done | bytes 131104 | tf_op jit(solution)/shard_map/ppermute | solution.py:30
  118.8 3.0 %collective-permute-done.18 = bf16[128,512]{1,0:T(8,128)(2,1)S(1)} collective-permute-done((bf16[128,512]{1,0:T(8,128)(2,1)S(1)}, bf16[128,512]{1,0:T(8,128)(2,1)S(1)}, u32[]{:S(2)}, u32[]{:S(2)}) %collective-permute-start.18) | collective-permute-done | bytes 131104 | tf_op jit(solution)/shard_map/ppermute | solution.py:30
  122.0 0.7 shard_map.55
  122.7 3.2 %collective-permute-start.33 = (bf16[128,512]{1,0:T(8,128)(2,1)S(1)}, bf16[128,512]{1,0:T(8,128)(2,1)S(1)}, u32[]{:S(2)}, u32[]{:S(2)}) collective-permute-start(bf16[128,512]{1,0:T(8,128)(2,1)S(1)} %get-tuple-element.65), channel_id=1, source_target_pairs={{0,0},{1,8},{2,2},{3,10},{4,4},{5,12},{6,6},{7,14},{8,9},{9,1},{10... | collective-permute-start | bytes 393224 | tf_op jit(solution)/shard_map/ppermute | solution.py:30
  125.9 0.4 collective-permute-start.34
  126.2 2.1 %collective-permute-start.35 = (bf16[128,512]{1,0:T(8,128)(2,1)S(1)}, bf16[128,512]{1,0:T(8,128)(2,1)S(1)}, u32[]{:S(2)}, u32[]{:S(2)}) collective-permute-start(bf16[128,512]{1,0:T(8,128)(2,1)S(1)} %get-tuple-element.67), channel_id=1, source_target_pairs={{0,4},{1,12},{2,6},{3,14},{4,0},{5,8},{6,2},{7,10},{8,13},{9,5},{1... | collective-permute-start | bytes 393224 | tf_op jit(solution)/shard_map/ppermute | solution.py:30
  128.4 1.7 %collective-permute-start.36 = (bf16[128,512]{1,0:T(8,128)(2,1)S(1)}, bf16[128,512]{1,0:T(8,128)(2,1)S(1)}, u32[]{:S(2)}, u32[]{:S(2)}) collective-permute-start(bf16[128,512]{1,0:T(8,128)(2,1)S(1)} %get-tuple-element.68), channel_id=1, source_target_pairs={{0,6},{1,14},{2,0},{3,8},{4,2},{5,10},{6,4},{7,12},{8,15},{9,7},{1... | collective-permute-start | bytes 393224 | tf_op jit(solution)/shard_map/ppermute | solution.py:30
  130.0 0.7 shard_map.52
  130.7 2.6 %collective-permute-start.22 = (bf16[128,512]{1,0:T(8,128)(2,1)S(1)}, bf16[128,512]{1,0:T(8,128)(2,1)S(1)}, u32[]{:S(2)}, u32[]{:S(2)}) collective-permute-start(bf16[128,512]{1,0:T(8,128)(2,1)S(1)} %get-tuple-element.60), channel_id=1, source_target_pairs={{0,0},{1,8},{2,2},{3,10},{4,4},{5,12},{6,6},{7,14},{8,9},{9,1},{10... | collective-permute-start | bytes 393224 | tf_op jit(solution)/shard_map/ppermute | solution.py:30
  133.3 0.7 collective-permute-start.23
  134.0 1.3 collective-permute-done.34.refs_5_
  135.3 0.1 collective-permute-start.24
  135.4 3.3 %collective-permute-start.25 = (bf16[128,512]{1,0:T(8,128)(2,1)S(1)}, bf16[128,512]{1,0:T(8,128)(2,1)S(1)}, u32[]{:S(2)}, u32[]{:S(2)}) collective-permute-start(bf16[128,512]{1,0:T(8,128)(2,1)S(1)} %get-tuple-element.63), channel_id=1, source_target_pairs={{0,6},{1,14},{2,0},{3,8},{4,2},{5,10},{6,4},{7,12},{8,15},{9,7},{1... | collective-permute-start | bytes 393224 | tf_op jit(solution)/shard_map/ppermute | solution.py:30
  138.7 4.5 %collective-permute-done.23.refs_1_ = bf16[128,512]{1,0:T(8,128)(2,1)S(1)} collective-permute-done((bf16[128,512]{1,0:T(8,128)(2,1)S(1)}, bf16[128,512]{1,0:T(8,128)(2,1)S(1)}, u32[]{:S(2)}, u32[]{:S(2)}) %collective-permute-start.23) | collective-permute-done | bytes 131104 | tf_op jit(solution)/shard_map/ppermute | solution.py:30
  143.2 0.3 collective-permute-done.25.refs_3_
  143.5 1.6 %shard_map.56 = bf16[256,2048]{1,0:T(8,128)(2,1)} custom-call(s32[32]{0:T(128)S(1)} %dynamic-slice_bitcast_fusion.table, bf16[128,512]{1,0:T(8,128)(2,1)S(1)} %collective-permute-done.22.refs_0_, bf16[128,512]{1,0:T(8,128)(2,1)S(1)} %collective-permute-done.23.refs_1_, bf16[128,512]{1,0:T(8,128)(2,1)S(1)} %collective-permute-done.24.refs_2_, ...), custom_call_target="tpu_custom_call" | custom-call | bytes 2097152 | tf_op jit(solution)/shard_map/pallas_call | solution.py:248
  (41 shorter events, 0.9 us)
Async XLA Ops:
  0.0 8.9 %collective-permute-start = (bf16[256,512]{1,0:T(8,128)(2,1)}, bf16[256,512]{1,0:T(8,128)(2,1)S(1)}, u32[]{:S(2)}, u32[]{:S(2)}) collective-permute-start(bf16[256,512]{1,0:T(8,128)(2,1)} %param.5), channel_id=1, source_target_pairs={{0,64},{1,65},{2,66},{3,67},{4,68},{5,69},{6,70},{7,71},{8,72},{9,... | collective-permute-start | bytes 786440 | tf_op jit(solution)/shard_map/ppermute | solution.py:30
  2.5 6.4 %copy-start.1 = (bf16[256,512]{1,0:T(8,128)(2,1)S(1)}, bf16[256,512]{1,0:T(8,128)(2,1)}, u32[]{:S(2)}) copy-start(bf16[256,512]{1,0:T(8,128)(2,1)} %param.5) | copy-start | bytes 786436
  8.9 10.4 %collective-permute-start.2 = (bf16[1,2,128,512]{3,2,1,0:T(8,128)(2,1)S(1)}, bf16[1,2,128,512]{3,2,1,0:T(8,128)(2,1)S(1)}, u32[]{:S(2)}, u32[]{:S(2)}) collective-permute-start(bf16[1,2,128,512]{3,2,1,0:T(8,128)(2,1)S(1)} %get-tuple-element.40), channel_id=1, source_target_pairs={{0,16},{1,49},{2,18},{3,51},{4,20},{5,53},{6,22},{7,55},{8,24},{9,... | collective-permute-start | bytes 786440 | tf_op jit(solution)/shard_map/ppermute | solution.py:30
  11.8 7.7 %collective-permute-start.1 = (bf16[1,2,128,512]{3,2,1,0:T(8,128)(2,1)S(1)}, bf16[1,2,128,512]{3,2,1,0:T(8,128)(2,1)S(1)}, u32[]{:S(2)}, u32[]{:S(2)}) collective-permute-start(bf16[1,2,128,512]{3,2,1,0:T(8,128)(2,1)S(1)} %get-tuple-element.39), channel_id=1, source_target_pairs={{0,2},{1,7},{2,0},{3,5},{4,6},{5,3},{6,4},{7,1},{8,10},{9,15},{10,... | collective-permute-start | bytes 786440 | tf_op jit(solution)/shard_map/ppermute | solution.py:30
  18.8 9.3 %collective-permute-start.5 = (bf16[2048,256]{1,0:T(8,128)(2,1)S(1)}, bf16[2048,256]{1,0:T(8,128)(2,1)S(1)}, u32[]{:S(2)}, u32[]{:S(2)}) collective-permute-start(bf16[2048,256]{1,0:T(8,128)(2,1)S(1)} %get-tuple-element.45), channel_id=1, source_target_pairs={{0,1},{1,0},{2,3},{3,2},{4,5},{5,4},{6,7},{7,6},{8,9},{9,8},{10,11... | collective-permute-start | bytes 3145736 | tf_op jit(solution)/shard_map/ppermute | solution.py:30
  18.9 9.3 %collective-permute-start.6 = (bf16[2048,256]{1,0:T(8,128)(2,1)S(1)}, bf16[2048,256]{1,0:T(8,128)(2,1)S(1)}, u32[]{:S(2)}, u32[]{:S(2)}) collective-permute-start(bf16[2048,256]{1,0:T(8,128)(2,1)S(1)} %get-tuple-element.46), channel_id=1, source_target_pairs={{0,1},{1,0},{2,3},{3,2},{4,5},{5,4},{6,7},{7,6},{8,9},{9,8},{10,11... | collective-permute-start | bytes 3145736 | tf_op jit(solution)/shard_map/ppermute | solution.py:30
  19.5 8.4 %collective-permute-start.4 = (bf16[2,2,128,512]{3,2,1,0:T(8,128)(2,1)S(1)}, bf16[2,2,128,512]{3,2,1,0:T(8,128)(2,1)S(1)}, u32[]{:S(2)}, u32[]{:S(2)}) collective-permute-start(bf16[2,2,128,512]{3,2,1,0:T(8,128)(2,1)S(1)} %pad_maximum_fusion.3), channel_id=1, source_target_pairs={{0,48},{1,17},{2,50},{3,19},{4,52},{5,21},{6,54},{7,23},{8,56},{9,... | collective-permute-start | bytes 1572872 | tf_op jit(solution)/shard_map/ppermute | solution.py:30
  19.6 8.4 %collective-permute-start.3 = (bf16[2,2,128,512]{3,2,1,0:T(8,128)(2,1)S(1)}, bf16[2,2,128,512]{3,2,1,0:T(8,128)(2,1)S(1)}, u32[]{:S(2)}, u32[]{:S(2)}) collective-permute-start(bf16[2,2,128,512]{3,2,1,0:T(8,128)(2,1)S(1)} %pad_maximum_fusion.2), channel_id=1, source_target_pairs={{0,6},{1,3},{2,4},{3,1},{4,2},{5,7},{6,0},{7,5},{8,14},{9,11},{10,... | collective-permute-start | bytes 1572872 | tf_op jit(solution)/shard_map/ppermute | solution.py:30
  19.7 19.6 %collective-permute-start.8 = (bf16[2048,256]{1,0:T(8,128)(2,1)S(1)}, bf16[2048,256]{1,0:T(8,128)(2,1)S(1)}, u32[]{:S(2)}, u32[]{:S(2)}) collective-permute-start(bf16[2048,256]{1,0:T(8,128)(2,1)S(1)} %get-tuple-element.37), channel_id=1, source_target_pairs={{0,8},{1,9},{2,10},{3,11},{4,12},{5,13},{6,14},{7,15},{8,0},{9,1},... | collective-permute-start | bytes 3145736 | tf_op jit(solution)/shard_map/ppermute | solution.py:30
  28.1 17.0 %collective-permute-start.10 = (bf16[4,2,128,512]{3,2,1,0:T(8,128)(2,1)S(1)}, bf16[4,2,128,512]{3,2,1,0:T(8,128)(2,1)S(1)}, u32[]{:S(2)}, u32[]{:S(2)}) collective-permute-start(bf16[4,2,128,512]{3,2,1,0:T(8,128)(2,1)S(1)} %pad_maximum_fusion.refs_6_.refs_4_), channel_id=1, source_target_pairs={{0,16},{1,49},{2,18},{3,51},{4,20},{5,53},{6,22},{7,55},{8,24},{9,... | collective-permute-start | bytes 3145736 | tf_op jit(solution)/shard_map/ppermute | solution.py:30
  29.1 16.0 %collective-permute-start.7 = (bf16[4,2,128,512]{3,2,1,0:T(8,128)(2,1)S(1)}, bf16[4,2,128,512]{3,2,1,0:T(8,128)(2,1)S(1)}, u32[]{:S(2)}, u32[]{:S(2)}) collective-permute-start(bf16[4,2,128,512]{3,2,1,0:T(8,128)(2,1)S(1)} %pad_maximum_fusion.1.refs_3_.refs_1_), channel_id=1, source_target_pairs={{0,2},{1,7},{2,0},{3,5},{4,6},{5,3},{6,4},{7,1},{8,10},{9,15},{10,... | collective-permute-start | bytes 3145736 | tf_op jit(solution)/shard_map/ppermute | solution.py:30
  39.3 19.2 %collective-permute-start.13 = (bf16[4,2,128,512]{3,2,1,0:T(8,128)(2,1)S(1)}, bf16[4,2,128,512]{3,2,1,0:T(8,128)(2,1)S(1)}, u32[]{:S(2)}, u32[]{:S(2)}) collective-permute-start(bf16[4,2,128,512]{3,2,1,0:T(8,128)(2,1)S(1)} %pad_maximum_fusion.1.refs_3_.refs_1_), channel_id=1, source_target_pairs={{0,6},{1,3},{2,4},{3,1},{4,2},{5,7},{6,0},{7,5},{8,14},{9,11},{10,... | collective-permute-start | bytes 3145736 | tf_op jit(solution)/shard_map/ppermute | solution.py:30
  42.6 16.0 %collective-permute-start.14 = (bf16[4,2,128,512]{3,2,1,0:T(8,128)(2,1)S(1)}, bf16[4,2,128,512]{3,2,1,0:T(8,128)(2,1)S(1)}, u32[]{:S(2)}, u32[]{:S(2)}) collective-permute-start(bf16[4,2,128,512]{3,2,1,0:T(8,128)(2,1)S(1)} %pad_maximum_fusion.refs_6_.refs_4_), channel_id=1, source_target_pairs={{0,48},{1,17},{2,50},{3,19},{4,52},{5,21},{6,54},{7,23},{8,56},{9,... | collective-permute-start | bytes 3145736 | tf_op jit(solution)/shard_map/ppermute | solution.py:30
  44.9 19.2 %collective-permute-start.12 = (bf16[2048,256]{1,0:T(8,128)(2,1)S(1)}, bf16[2048,256]{1,0:T(8,128)(2,1)S(1)}, u32[]{:S(2)}, u32[]{:S(2)}) collective-permute-start(bf16[2048,256]{1,0:T(8,128)(2,1)S(1)} %collective-permute-done.6), channel_id=1, source_target_pairs={{0,8},{1,9},{2,10},{3,11},{4,12},{5,13},{6,14},{7,15},{8,0},{9,1},... | collective-permute-start | bytes 3145736 | tf_op jit(solution)/shard_map/ppermute | solution.py:30
  45.2 23.9 %collective-permute-start.11 = (bf16[4,2,128,512]{3,2,1,0:T(8,128)(2,1)S(1)}, bf16[4,2,128,512]{3,2,1,0:T(8,128)(2,1)S(1)}, u32[]{:S(2)}, u32[]{:S(2)}) collective-permute-start(bf16[4,2,128,512]{3,2,1,0:T(8,128)(2,1)S(1)} %collective-permute-done.10.refs_7_.refs_5_), channel_id=1, source_target_pairs={{0,48},{1,17},{2,50},{3,19},{4,52},{5,21},{6,54},{7,23},{8,56},{9,... | collective-permute-start | bytes 3145736 | tf_op jit(solution)/shard_map/ppermute | solution.py:30
  45.2 24.6 %collective-permute-start.9 = (bf16[4,2,128,512]{3,2,1,0:T(8,128)(2,1)S(1)}, bf16[4,2,128,512]{3,2,1,0:T(8,128)(2,1)S(1)}, u32[]{:S(2)}, u32[]{:S(2)}) collective-permute-start(bf16[4,2,128,512]{3,2,1,0:T(8,128)(2,1)S(1)} %collective-permute-done.7.refs_4_.refs_2_), channel_id=1, source_target_pairs={{0,6},{1,3},{2,4},{3,1},{4,2},{5,7},{6,0},{7,5},{8,14},{9,11},{10,... | collective-permute-start | bytes 3145736 | tf_op jit(solution)/shard_map/ppermute | solution.py:30
  71.2 8.5 %collective-permute-start.26 = (bf16[4,128,1024]{2,1,0:T(8,128)(2,1)S(1)}, bf16[4,128,1024]{2,1,0:T(8,128)(2,1)S(1)}, u32[]{:S(2)}, u32[]{:S(2)}) collective-permute-start(bf16[4,128,1024]{2,1,0:T(8,128)(2,1)S(1)} %shard_map.54), channel_id=1, source_target_pairs={{0,1},{1,0},{2,3},{3,2},{4,5},{5,4},{6,7},{7,6},{8,9},{9,8},{10,11... | collective-permute-start | bytes 3145736 | tf_op jit(solution)/shard_map/ppermute | solution.py:30
  78.2 3.8 %collective-permute-start.15 = (bf16[4,128,1024]{2,1,0:T(8,128)(2,1)S(1)}, bf16[4,128,1024]{2,1,0:T(8,128)(2,1)S(1)}, u32[]{:S(2)}, u32[]{:S(2)}) collective-permute-start(bf16[4,128,1024]{2,1,0:T(8,128)(2,1)S(1)} %shard_map.51), channel_id=1, source_target_pairs={{0,1},{1,0},{2,3},{3,2},{4,5},{5,4},{6,7},{7,6},{8,9},{9,8},{10,11... | collective-permute-start | bytes 3145736 | tf_op jit(solution)/shard_map/ppermute | solution.py:30
  80.2 13.1 %collective-permute-start.27 = (bf16[4,128,512]{2,1,0:T(8,128)(2,1)S(1)}, bf16[4,128,512]{2,1,0:T(8,128)(2,1)S(1)}, u32[]{:S(2)}, u32[]{:S(2)}) collective-permute-start(bf16[4,128,512]{2,1,0:T(8,128)(2,1)S(1)} %slice.96), channel_id=1, source_target_pairs={{0,8},{1,9},{2,10},{3,11},{4,12},{5,13},{6,14},{7,15},{8,0},{9,1},... | collective-permute-start | bytes 1572872 | tf_op jit(solution)/shard_map/ppermute | solution.py:30
  82.5 22.0 %collective-permute-start.16 = (bf16[4,128,512]{2,1,0:T(8,128)(2,1)S(1)}, bf16[4,128,512]{2,1,0:T(8,128)(2,1)S(1)}, u32[]{:S(2)}, u32[]{:S(2)}) collective-permute-start(bf16[4,128,512]{2,1,0:T(8,128)(2,1)S(1)} %slice.97), channel_id=1, source_target_pairs={{0,8},{1,9},{2,10},{3,11},{4,12},{5,13},{6,14},{7,15},{8,0},{9,1},... | collective-permute-start | bytes 1572872 | tf_op jit(solution)/shard_map/ppermute | solution.py:30
  93.5 14.0 %collective-permute-start.28 = (bf16[128,512]{1,0:T(8,128)(2,1)S(1)}, bf16[128,512]{1,0:T(8,128)(2,1)S(1)}, u32[]{:S(2)}, u32[]{:S(2)}) collective-permute-start(bf16[128,512]{1,0:T(8,128)(2,1)S(1)} %get-tuple-element.69), channel_id=1, source_target_pairs={{0,0},{1,65},{2,2},{3,67},{4,4},{5,69},{6,6},{7,71},{8,8},{9,73},{... | collective-permute-start | bytes 393224 | tf_op jit(solution)/shard_map/ppermute | solution.py:30
  97.3 14.3 %collective-permute-start.29 = (bf16[128,512]{1,0:T(8,128)(2,1)S(1)}, bf16[128,512]{1,0:T(8,128)(2,1)S(1)}, u32[]{:S(2)}, u32[]{:S(2)}) collective-permute-start(bf16[128,512]{1,0:T(8,128)(2,1)S(1)} %get-tuple-element.72), channel_id=1, source_target_pairs={{0,16},{1,81},{2,18},{3,83},{4,20},{5,85},{6,22},{7,87},{8,24},{9,... | collective-permute-start | bytes 393224 | tf_op jit(solution)/shard_map/ppermute | solution.py:30
  98.3 16.1 %collective-permute-start.30 = (bf16[128,512]{1,0:T(8,128)(2,1)S(1)}, bf16[128,512]{1,0:T(8,128)(2,1)S(1)}, u32[]{:S(2)}, u32[]{:S(2)}) collective-permute-start(bf16[128,512]{1,0:T(8,128)(2,1)S(1)} %get-tuple-element.71), channel_id=1, source_target_pairs={{0,32},{1,97},{2,34},{3,99},{4,36},{5,101},{6,38},{7,103},{8,40},{... | collective-permute-start | bytes 393224 | tf_op jit(solution)/shard_map/ppermute | solution.py:30
  102.9 11.9 %collective-permute-start.31 = (bf16[128,512]{1,0:T(8,128)(2,1)S(1)}, bf16[128,512]{1,0:T(8,128)(2,1)S(1)}, u32[]{:S(2)}, u32[]{:S(2)}) collective-permute-start(bf16[128,512]{1,0:T(8,128)(2,1)S(1)} %get-tuple-element.70), channel_id=1, source_target_pairs={{0,48},{1,113},{2,50},{3,115},{4,52},{5,117},{6,54},{7,119},{8,56}... | collective-permute-start | bytes 393224 | tf_op jit(solution)/shard_map/ppermute | solution.py:30
  104.7 17.3 %copy-start = (s32[8]{0:T(128)S(1)}, s32[8]{0:T(128)}, u32[]{:S(2)}) copy-start(s32[8]{0:T(128)} %owner.3) | copy-start | bytes 100
  104.8 10.4 %collective-permute-start.19 = (bf16[128,512]{1,0:T(8,128)(2,1)S(1)}, bf16[128,512]{1,0:T(8,128)(2,1)S(1)}, u32[]{:S(2)}, u32[]{:S(2)}) collective-permute-start(bf16[128,512]{1,0:T(8,128)(2,1)S(1)} %get-tuple-element.75), channel_id=1, source_target_pairs={{0,32},{1,97},{2,34},{3,99},{4,36},{5,101},{6,38},{7,103},{8,40},{... | collective-permute-start | bytes 393224 | tf_op jit(solution)/shard_map/ppermute | solution.py:30
  107.5 7.7 %collective-permute-start.20 = (bf16[128,512]{1,0:T(8,128)(2,1)S(1)}, bf16[128,512]{1,0:T(8,128)(2,1)S(1)}, u32[]{:S(2)}, u32[]{:S(2)}) collective-permute-start(bf16[128,512]{1,0:T(8,128)(2,1)S(1)} %get-tuple-element.74), channel_id=1, source_target_pairs={{0,48},{1,113},{2,50},{3,115},{4,52},{5,117},{6,54},{7,119},{8,56}... | collective-permute-start | bytes 393224 | tf_op jit(solution)/shard_map/ppermute | solution.py:30
  111.6 7.2 %collective-permute-start.17 = (bf16[128,512]{1,0:T(8,128)(2,1)S(1)}, bf16[128,512]{1,0:T(8,128)(2,1)S(1)}, u32[]{:S(2)}, u32[]{:S(2)}) collective-permute-start(bf16[128,512]{1,0:T(8,128)(2,1)S(1)} %get-tuple-element.73), channel_id=1, source_target_pairs={{0,0},{1,65},{2,2},{3,67},{4,4},{5,69},{6,6},{7,71},{8,8},{9,73},{... | collective-permute-start | bytes 393224 | tf_op jit(solution)/shard_map/ppermute | solution.py:30
  114.4 7.5 %collective-permute-start.18 = (bf16[128,512]{1,0:T(8,128)(2,1)S(1)}, bf16[128,512]{1,0:T(8,128)(2,1)S(1)}, u32[]{:S(2)}, u32[]{:S(2)}) collective-permute-start(bf16[128,512]{1,0:T(8,128)(2,1)S(1)} %get-tuple-element.76), channel_id=1, source_target_pairs={{0,16},{1,81},{2,18},{3,83},{4,20},{5,85},{6,22},{7,87},{8,24},{9,... | collective-permute-start | bytes 393224 | tf_op jit(solution)/shard_map/ppermute | solution.py:30
  114.9 7.2 %collective-permute-start.32 = (bf16[4,128,512]{2,1,0:T(8,128)(2,1)S(1)}, bf16[4,128,512]{2,1,0:T(8,128)(2,1)S(1)}, u32[]{:S(2)}, u32[]{:S(2)}) collective-permute-start(bf16[4,128,512]{2,1,0:T(8,128)(2,1)S(1)} %pad_maximum_fusion.5.own), channel_id=1, source_target_pairs={{0,1},{1,0},{2,3},{3,2},{4,5},{5,4},{6,7},{7,6},{8,9},{9,8},{10,11... | collective-permute-start | bytes 1572872 | tf_op jit(solution)/shard_map/ppermute | solution.py:30
  121.9 8.1 %collective-permute-start.21 = (bf16[4,128,512]{2,1,0:T(8,128)(2,1)S(1)}, bf16[4,128,512]{2,1,0:T(8,128)(2,1)S(1)}, u32[]{:S(2)}, u32[]{:S(2)}) collective-permute-start(bf16[4,128,512]{2,1,0:T(8,128)(2,1)S(1)} %pad_maximum_fusion.4.own), channel_id=1, source_target_pairs={{0,1},{1,0},{2,3},{3,2},{4,5},{5,4},{6,7},{7,6},{8,9},{9,8},{10,11... | collective-permute-start | bytes 1572872 | tf_op jit(solution)/shard_map/ppermute | solution.py:30
  122.7 10.6 %collective-permute-start.33 = (bf16[128,512]{1,0:T(8,128)(2,1)S(1)}, bf16[128,512]{1,0:T(8,128)(2,1)S(1)}, u32[]{:S(2)}, u32[]{:S(2)}) collective-permute-start(bf16[128,512]{1,0:T(8,128)(2,1)S(1)} %get-tuple-element.65), channel_id=1, source_target_pairs={{0,0},{1,8},{2,2},{3,10},{4,4},{5,12},{6,6},{7,14},{8,9},{9,1},{10... | collective-permute-start | bytes 393224 | tf_op jit(solution)/shard_map/ppermute | solution.py:30
  125.9 9.4 %collective-permute-start.34 = (bf16[128,512]{1,0:T(8,128)(2,1)S(1)}, bf16[128,512]{1,0:T(8,128)(2,1)S(1)}, u32[]{:S(2)}, u32[]{:S(2)}) collective-permute-start(bf16[128,512]{1,0:T(8,128)(2,1)S(1)} %get-tuple-element.66), channel_id=1, source_target_pairs={{0,2},{1,10},{2,4},{3,12},{4,6},{5,14},{6,0},{7,8},{8,11},{9,3},{1... | collective-permute-start | bytes 393224 | tf_op jit(solution)/shard_map/ppermute | solution.py:30
  126.2 9.2 %collective-permute-start.35 = (bf16[128,512]{1,0:T(8,128)(2,1)S(1)}, bf16[128,512]{1,0:T(8,128)(2,1)S(1)}, u32[]{:S(2)}, u32[]{:S(2)}) collective-permute-start(bf16[128,512]{1,0:T(8,128)(2,1)S(1)} %get-tuple-element.67), channel_id=1, source_target_pairs={{0,4},{1,12},{2,6},{3,14},{4,0},{5,8},{6,2},{7,10},{8,13},{9,5},{1... | collective-permute-start | bytes 393224 | tf_op jit(solution)/shard_map/ppermute | solution.py:30
  128.4 10.3 %collective-permute-start.36 = (bf16[128,512]{1,0:T(8,128)(2,1)S(1)}, bf16[128,512]{1,0:T(8,128)(2,1)S(1)}, u32[]{:S(2)}, u32[]{:S(2)}) collective-permute-start(bf16[128,512]{1,0:T(8,128)(2,1)S(1)} %get-tuple-element.68), channel_id=1, source_target_pairs={{0,6},{1,14},{2,0},{3,8},{4,2},{5,10},{6,4},{7,12},{8,15},{9,7},{1... | collective-permute-start | bytes 393224 | tf_op jit(solution)/shard_map/ppermute | solution.py:30
  130.7 8.0 %collective-permute-start.22 = (bf16[128,512]{1,0:T(8,128)(2,1)S(1)}, bf16[128,512]{1,0:T(8,128)(2,1)S(1)}, u32[]{:S(2)}, u32[]{:S(2)}) collective-permute-start(bf16[128,512]{1,0:T(8,128)(2,1)S(1)} %get-tuple-element.60), channel_id=1, source_target_pairs={{0,0},{1,8},{2,2},{3,10},{4,4},{5,12},{6,6},{7,14},{8,9},{9,1},{10... | collective-permute-start | bytes 393224 | tf_op jit(solution)/shard_map/ppermute | solution.py:30
  133.3 9.9 %collective-permute-start.23 = (bf16[128,512]{1,0:T(8,128)(2,1)S(1)}, bf16[128,512]{1,0:T(8,128)(2,1)S(1)}, u32[]{:S(2)}, u32[]{:S(2)}) collective-permute-start(bf16[128,512]{1,0:T(8,128)(2,1)S(1)} %get-tuple-element.61), channel_id=1, source_target_pairs={{0,2},{1,10},{2,4},{3,12},{4,6},{5,14},{6,0},{7,8},{8,11},{9,3},{1... | collective-permute-start | bytes 393224 | tf_op jit(solution)/shard_map/ppermute | solution.py:30
  135.3 7.9 %collective-permute-start.24 = (bf16[128,512]{1,0:T(8,128)(2,1)S(1)}, bf16[128,512]{1,0:T(8,128)(2,1)S(1)}, u32[]{:S(2)}, u32[]{:S(2)}) collective-permute-start(bf16[128,512]{1,0:T(8,128)(2,1)S(1)} %get-tuple-element.62), channel_id=1, source_target_pairs={{0,4},{1,12},{2,6},{3,14},{4,0},{5,8},{6,2},{7,10},{8,13},{9,5},{1... | collective-permute-start | bytes 393224 | tf_op jit(solution)/shard_map/ppermute | solution.py:30
  135.4 8.1 %collective-permute-start.25 = (bf16[128,512]{1,0:T(8,128)(2,1)S(1)}, bf16[128,512]{1,0:T(8,128)(2,1)S(1)}, u32[]{:S(2)}, u32[]{:S(2)}) collective-permute-start(bf16[128,512]{1,0:T(8,128)(2,1)S(1)} %get-tuple-element.63), channel_id=1, source_target_pairs={{0,6},{1,14},{2,0},{3,8},{4,2},{5,10},{6,4},{7,12},{8,15},{9,7},{1... | collective-permute-start | bytes 393224 | tf_op jit(solution)/shard_map/ppermute | solution.py:30

commit v17 on v16

--- a/solution.py
+++ b/solution.py
@@ -58,7 +58,7 @@
 
 def gather(activations, first_job, second_job, third_job):
     came = permute(activations, lambda x, y, z, c: linear(x + 2, y, z, c))
-    block = jnp.stack([activations, after(came, first_job)])
+    block = jnp.stack([activations, after(came, *first_job)])
     blocks = {"z": block[None, :, :HALF], "y": block[None, :, HALF:]}
     blocks = lax.optimization_barrier(blocks)
     for which in (1, 2):
@@ -267,7 +267,7 @@
     near = permute(sent, other_core)
     far = permute(same, other_chip)
     swapped = permute(swapped, other_core)
-    slots = gather(activations, same, (near, swapped), far)
+    slots = gather(activations, (same, mine), (near, swapped), far)
     cross = permute(after(swapped, far), other_chip)
     weights = [mine, near, far, cross]
     early = early_product(table, weights[:3], slots)

time: 146 us -> 146 us (level)
  starting transfers between devices: 59.3 us -> 63.8 us
  waiting for transfers between devices: 59.9 us -> 55.5 us
    ppermute x37, starting transfers between devices: 59.3 us -> 63.8 us  [permute(): lax.ppermute(value, AXES, [(i, move(*coords(i))) for i in range(N_DEV)])]
    ppermute x37, waiting for transfers between devices: 59.9 us -> 55.5 us  [permute(): lax.ppermute(value, AXES, [(i, move(*coords(i))) for i in range(N_DEV)])]
  transfers between devices with their start and end apart: 37 -> 37, of which waited for: 14 -> 13; matrix products, arithmetic and copies ran while one was open for 2% -> 2% of each run, Pallas kernels for 14% -> 14%
where the time goes in v17:
time: 146 us; the launch traced here: 145 us
  starting transfers between devices  63.8 us (44%)
  waiting for transfers between devices  55.5 us (38%)
  Pallas kernels  22.9 us (16%)
  other arithmetic  1.71 us (1%)
    ppermute x37, starting transfers between devices, permute(): lax.ppermute(value, AXES, [(i, move(*coords(i))) for i in range(N_DEV)])  63.8 us
    ppermute x37, waiting for transfers between devices, permute(): lax.ppermute(value, AXES, [(i, move(*coords(i))) for i in range(N_DEV)])  55.5 us
    pallas_call x2, Pallas kernels, early_product(): pl.pallas_call(functools.partial(early_kernel, count), in_specs=[pl.Block...  7.91 us
    pallas_call x2, Pallas kernels, refit(): pl.pallas_call(functools.partial(refit_kernel, first), in_specs=[pl.Block...  6.55 us
    pallas_call x4, Pallas kernels, product(): pl.pallas_call(functools.partial(product_kernel, part, keep), in_specs=[p...  5.53 us
  transfers between devices with their start and end apart: 37, of which 13 were waited for; matrix products, arithmetic and copies ran while one was open for 2% of the time, Pallas kernels for 14%

profile of v17, /device:TPU:3, one launch (start us, length us, event | category | flops | bytes accessed | tf_op | source)
XLA Modules:
  0.0 145.4 jit_solution(8408329027522695481)
XLA Ops:
  0.0 1.8 %collective-permute-start = (bf16[256,512]{1,0:T(8,128)(2,1)}, bf16[256,512]{1,0:T(8,128)(2,1)S(1)}, u32[]{:S(2)}, u32[]{:S(2)}) collective-permute-start(bf16[256,512]{1,0:T(8,128)(2,1)} %param.5), channel_id=1, source_target_pairs={{0,64},{1,65},{2,66},{3,67},{4,68},{5,69},{6,70},{7,71},{8,72},{9,... | collective-permute-start | bytes 786440 | tf_op jit(solution)/shard_map/ppermute | solution.py:30
  1.8 0.7 dynamic-slice_bitcast_fusion.table
  2.5 3.3 %shard_map.47 = (bf16[2048,256]{1,0:T(8,128)(2,1)S(1)}, bf16[2048,256]{1,0:T(8,128)(2,1)S(1)}) custom-call(s32[32]{0:T(128)S(1)} %dynamic-slice_bitcast_fusion.table, f32[8192,256]{1,0:T(8,128)} %master.3), custom_call_target="tpu_custom_call" | custom-call | flops 6291456 | bytes 6291456 | tf_op jit(solution)/shard_map/pallas_call | solution.py:122
  5.8 3.3 %shard_map.46 = (bf16[2048,256]{1,0:T(8,128)(2,1)S(1)}, bf16[2048,256]{1,0:T(8,128)(2,1)S(1)}) custom-call(s32[32]{0:T(128)S(1)} %dynamic-slice_bitcast_fusion.table, f32[8192,256]{1,0:T(8,128)} %master.3), custom_call_target="tpu_custom_call" | custom-call | flops 6291456 | bytes 6291456 | tf_op jit(solution)/shard_map/pallas_call | solution.py:122
  9.2 2.8 %collective-permute-start.2 = (bf16[1,2,128,512]{3,2,1,0:T(8,128)(2,1)S(1)}, bf16[1,2,128,512]{3,2,1,0:T(8,128)(2,1)S(1)}, u32[]{:S(2)}, u32[]{:S(2)}) collective-permute-start(bf16[1,2,128,512]{3,2,1,0:T(8,128)(2,1)S(1)} %get-tuple-element.41), channel_id=1, source_target_pairs={{0,16},{1,49},{2,18},{3,51},{4,20},{5,53},{6,22},{7,55},{8,24},{9,... | collective-permute-start | bytes 786440 | tf_op jit(solution)/shard_map/ppermute | solution.py:30
  12.0 3.8 %collective-permute-start.1 = (bf16[1,2,128,512]{3,2,1,0:T(8,128)(2,1)S(1)}, bf16[1,2,128,512]{3,2,1,0:T(8,128)(2,1)S(1)}, u32[]{:S(2)}, u32[]{:S(2)}) collective-permute-start(bf16[1,2,128,512]{3,2,1,0:T(8,128)(2,1)S(1)} %get-tuple-element.40), channel_id=1, source_target_pairs={{0,2},{1,7},{2,0},{3,5},{4,6},{5,3},{6,4},{7,1},{8,10},{9,15},{10,... | collective-permute-start | bytes 786440 | tf_op jit(solution)/shard_map/ppermute | solution.py:30
  15.8 0.5 collective-permute-start.6
  16.3 3.2 %collective-permute-done.1 = bf16[1,2,128,512]{3,2,1,0:T(8,128)(2,1)S(1)} collective-permute-done((bf16[1,2,128,512]{3,2,1,0:T(8,128)(2,1)S(1)}, bf16[1,2,128,512]{3,2,1,0:T(8,128)(2,1)S(1)}, u32[]{:S(2)}, u32[]{:S(2)}) %collective-permute-start.1) | collective-permute-done | bytes 262176 | tf_op jit(solution)/shard_map/ppermute | solution.py:30
  19.7 0.1 collective-permute-start.3
  19.8 1.2 collective-permute-start.8
  21.0 7.0 %collective-permute-done.4 = bf16[2,2,128,512]{3,2,1,0:T(8,128)(2,1)S(1)} collective-permute-done((bf16[2,2,128,512]{3,2,1,0:T(8,128)(2,1)S(1)}, bf16[2,2,128,512]{3,2,1,0:T(8,128)(2,1)S(1)}, u32[]{:S(2)}, u32[]{:S(2)}) %collective-permute-start.4) | collective-permute-done | bytes 524320 | tf_op jit(solution)/shard_map/ppermute | solution.py:30
  28.0 0.1 pad_maximum_fusion.1.refs_3_.refs_1_
  28.1 0.1 pad_maximum_fusion.refs_6_.refs_4_
  28.2 0.6 collective-permute-start.10
  28.8 2.7 %collective-permute-start.7 = (bf16[4,2,128,512]{3,2,1,0:T(8,128)(2,1)S(1)}, bf16[4,2,128,512]{3,2,1,0:T(8,128)(2,1)S(1)}, u32[]{:S(2)}, u32[]{:S(2)}) collective-permute-start(bf16[4,2,128,512]{3,2,1,0:T(8,128)(2,1)S(1)} %pad_maximum_fusion.1.refs_3_.refs_1_), channel_id=1, source_target_pairs={{0,2},{1,7},{2,0},{3,5},{4,6},{5,3},{6,4},{7,1},{8,10},{9,15},{10,... | collective-permute-start | bytes 3145736 | tf_op jit(solution)/shard_map/ppermute | solution.py:30
  31.5 8.0 %collective-permute-done.8.refs_2_.far = bf16[2048,256]{1,0:T(8,128)(2,1)S(1)} collective-permute-done((bf16[2048,256]{1,0:T(8,128)(2,1)S(1)}, bf16[2048,256]{1,0:T(8,128)(2,1)S(1)}, u32[]{:S(2)}, u32[]{:S(2)}) %collective-permute-start.8) | collective-permute-done | bytes 1048608 | tf_op jit(solution)/shard_map/ppermute | solution.py:30
  39.5 3.2 %collective-permute-start.13 = (bf16[4,2,128,512]{3,2,1,0:T(8,128)(2,1)S(1)}, bf16[4,2,128,512]{3,2,1,0:T(8,128)(2,1)S(1)}, u32[]{:S(2)}, u32[]{:S(2)}) collective-permute-start(bf16[4,2,128,512]{3,2,1,0:T(8,128)(2,1)S(1)} %pad_maximum_fusion.1.refs_3_.refs_1_), channel_id=1, source_target_pairs={{0,6},{1,3},{2,4},{3,1},{4,2},{5,7},{6,0},{7,5},{8,14},{9,11},{10,... | collective-permute-start | bytes 3145736 | tf_op jit(solution)/shard_map/ppermute | solution.py:30
  42.7 2.3 %collective-permute-start.14 = (bf16[4,2,128,512]{3,2,1,0:T(8,128)(2,1)S(1)}, bf16[4,2,128,512]{3,2,1,0:T(8,128)(2,1)S(1)}, u32[]{:S(2)}, u32[]{:S(2)}) collective-permute-start(bf16[4,2,128,512]{3,2,1,0:T(8,128)(2,1)S(1)} %pad_maximum_fusion.refs_6_.refs_4_), channel_id=1, source_target_pairs={{0,48},{1,17},{2,50},{3,19},{4,52},{5,21},{6,54},{7,23},{8,56},{9,... | collective-permute-start | bytes 3145736 | tf_op jit(solution)/shard_map/ppermute | solution.py:30
  45.0 1.5 %collective-permute-start.12 = (bf16[2048,256]{1,0:T(8,128)(2,1)S(1)}, bf16[2048,256]{1,0:T(8,128)(2,1)S(1)}, u32[]{:S(2)}, u32[]{:S(2)}) collective-permute-start(bf16[2048,256]{1,0:T(8,128)(2,1)S(1)} %collective-permute-done.6), channel_id=1, source_target_pairs={{0,8},{1,9},{2,10},{3,11},{4,12},{5,13},{6,14},{7,15},{8,0},{9,1},... | collective-permute-start | bytes 3145736 | tf_op jit(solution)/shard_map/ppermute | solution.py:30
  46.5 0.3 collective-permute-start.9
  46.8 11.7 %collective-permute-done.13.refs_5_.refs_3_ = bf16[4,2,128,512]{3,2,1,0:T(8,128)(2,1)S(1)} collective-permute-done((bf16[4,2,128,512]{3,2,1,0:T(8,128)(2,1)S(1)}, bf16[4,2,128,512]{3,2,1,0:T(8,128)(2,1)S(1)}, u32[]{:S(2)}, u32[]{:S(2)}) %collective-permute-start.13) | collective-permute-done | bytes 1048608 | tf_op jit(solution)/shard_map/ppermute | solution.py:30
  58.5 5.6 %shard_map.48 = (f32[3,2,512,256]{3,2,1,0:T(8,128)S(1)}, f32[3,2,384,256]{3,2,1,0:T(8,128)S(1)}) custom-call(s32[32]{0:T(128)S(1)} %dynamic-slice_bitcast_fusion.table, bf16[2048,256]{1,0:T(8,128)(2,1)S(1)} %get-tuple-element.38.refs_0_.mine, bf16[2048,256]{1,0:T(8,128)(2,1)S(1)} %collective-permute-done.5.refs_1_.near, ...), custom_call_target="tpu_custom_call" | custom-call | flops 3221225472 | bytes 16777216 | tf_op jit(solution)/shard_map/pallas_call | solution.py:176
  64.1 1.6 %collective-permute-done.12.refs_0_.cross = bf16[2048,256]{1,0:T(8,128)(2,1)S(1)} collective-permute-done((bf16[2048,256]{1,0:T(8,128)(2,1)S(1)}, bf16[2048,256]{1,0:T(8,128)(2,1)S(1)}, u32[]{:S(2)}, u32[]{:S(2)}) %collective-permute-start.12) | collective-permute-done | bytes 1048608 | tf_op jit(solution)/shard_map/ppermute | solution.py:30
  65.7 2.3 %shard_map.49 = (f32[1,2,512,256]{3,2,1,0:T(8,128)S(1)}, f32[1,2,384,256]{3,2,1,0:T(8,128)S(1)}) custom-call(s32[32]{0:T(128)S(1)} %dynamic-slice_bitcast_fusion.table, bf16[2048,256]{1,0:T(8,128)(2,1)S(1)} %collective-permute-done.12.refs_0_.cross, bf16[4,2,128,512]{3,2,1,0:T(8,128)(2,1)S(1)} %pad_maximum_fusion.1.refs_3_.refs_1_, ...), custom_call_target="tpu_custom_call" | custom-call | flops 1073741824 | bytes 16777216 | tf_op jit(solution)/shard_map/pallas_call | solution.py:176
  68.0 1.1 collective-permute-done.11.refs_0_
  69.1 0.7 collective-permute-done.9.refs_0_
  69.8 1.4 shard_map.54
  71.2 5.9 %collective-permute-start.26 = (bf16[4,128,1024]{2,1,0:T(8,128)(2,1)S(1)}, bf16[4,128,1024]{2,1,0:T(8,128)(2,1)S(1)}, u32[]{:S(2)}, u32[]{:S(2)}) collective-permute-start(bf16[4,128,1024]{2,1,0:T(8,128)(2,1)S(1)} %shard_map.54), channel_id=1, source_target_pairs={{0,1},{1,0},{2,3},{3,2},{4,5},{5,4},{6,7},{7,6},{8,9},{9,8},{10,11... | collective-permute-start | bytes 3145736 | tf_op jit(solution)/shard_map/ppermute | solution.py:30
  77.1 1.3 shard_map.51
  78.4 0.1 collective-permute-start.15
  78.5 1.4 shard_map.53
  79.9 0.4 convert_add_fusion
  80.5 1.2 collective-permute-start.27
  81.7 1.4 shard_map.50
  83.1 0.4 convert_add_fusion.1
  83.7 0.4 collective-permute-start.16
  84.0 9.5 %collective-permute-done.27 = bf16[4,128,512]{2,1,0:T(8,128)(2,1)S(1)} collective-permute-done((bf16[4,128,512]{2,1,0:T(8,128)(2,1)S(1)}, bf16[4,128,512]{2,1,0:T(8,128)(2,1)S(1)}, u32[]{:S(2)}, u32[]{:S(2)}) %collective-permute-start.27) | collective-permute-done | bytes 524320 | tf_op jit(solution)/shard_map/ppermute | solution.py:30
  93.5 0.2 fusion
  93.8 3.5 %collective-permute-start.28 = (bf16[128,512]{1,0:T(8,128)(2,1)S(1)}, bf16[128,512]{1,0:T(8,128)(2,1)S(1)}, u32[]{:S(2)}, u32[]{:S(2)}) collective-permute-start(bf16[128,512]{1,0:T(8,128)(2,1)S(1)} %get-tuple-element.69), channel_id=1, source_target_pairs={{0,0},{1,65},{2,2},{3,67},{4,4},{5,69},{6,6},{7,71},{8,8},{9,73},{... | collective-permute-start | bytes 393224 | tf_op jit(solution)/shard_map/ppermute | solution.py:30
  97.3 1.2 collective-permute-start.29
  98.5 2.9 %collective-permute-start.30 = (bf16[128,512]{1,0:T(8,128)(2,1)S(1)}, bf16[128,512]{1,0:T(8,128)(2,1)S(1)}, u32[]{:S(2)}, u32[]{:S(2)}) collective-permute-start(bf16[128,512]{1,0:T(8,128)(2,1)S(1)} %get-tuple-element.71), channel_id=1, source_target_pairs={{0,32},{1,97},{2,34},{3,99},{4,36},{5,101},{6,38},{7,103},{8,40},{... | collective-permute-start | bytes 393224 | tf_op jit(solution)/shard_map/ppermute | solution.py:30
  101.4 1.7 %collective-permute-start.31 = (bf16[128,512]{1,0:T(8,128)(2,1)S(1)}, bf16[128,512]{1,0:T(8,128)(2,1)S(1)}, u32[]{:S(2)}, u32[]{:S(2)}) collective-permute-start(bf16[128,512]{1,0:T(8,128)(2,1)S(1)} %get-tuple-element.70), channel_id=1, source_target_pairs={{0,48},{1,113},{2,50},{3,115},{4,52},{5,117},{6,54},{7,119},{8,56}... | collective-permute-start | bytes 393224 | tf_op jit(solution)/shard_map/ppermute | solution.py:30
  103.1 1.7 %collective-permute-done.16 = bf16[4,128,512]{2,1,0:T(8,128)(2,1)S(1)} collective-permute-done((bf16[4,128,512]{2,1,0:T(8,128)(2,1)S(1)}, bf16[4,128,512]{2,1,0:T(8,128)(2,1)S(1)}, u32[]{:S(2)}, u32[]{:S(2)}) %collective-permute-start.16) | collective-permute-done | bytes 524320 | tf_op jit(solution)/shard_map/ppermute | solution.py:30
  104.8 0.2 fusion.1
  105.0 2.5 %collective-permute-start.19 = (bf16[128,512]{1,0:T(8,128)(2,1)S(1)}, bf16[128,512]{1,0:T(8,128)(2,1)S(1)}, u32[]{:S(2)}, u32[]{:S(2)}) collective-permute-start(bf16[128,512]{1,0:T(8,128)(2,1)S(1)} %get-tuple-element.75), channel_id=1, source_target_pairs={{0,32},{1,97},{2,34},{3,99},{4,36},{5,101},{6,38},{7,103},{8,40},{... | collective-permute-start | bytes 393224 | tf_op jit(solution)/shard_map/ppermute | solution.py:30
  107.5 2.4 %collective-permute-start.20 = (bf16[128,512]{1,0:T(8,128)(2,1)S(1)}, bf16[128,512]{1,0:T(8,128)(2,1)S(1)}, u32[]{:S(2)}, u32[]{:S(2)}) collective-permute-start(bf16[128,512]{1,0:T(8,128)(2,1)S(1)} %get-tuple-element.74), channel_id=1, source_target_pairs={{0,48},{1,113},{2,50},{3,115},{4,52},{5,117},{6,54},{7,119},{8,56}... | collective-permute-start | bytes 393224 | tf_op jit(solution)/shard_map/ppermute | solution.py:30
  110.0 3.5 %collective-permute-start.17 = (bf16[128,512]{1,0:T(8,128)(2,1)S(1)}, bf16[128,512]{1,0:T(8,128)(2,1)S(1)}, u32[]{:S(2)}, u32[]{:S(2)}) collective-permute-start(bf16[128,512]{1,0:T(8,128)(2,1)S(1)} %get-tuple-element.73), channel_id=1, source_target_pairs={{0,0},{1,65},{2,2},{3,67},{4,4},{5,69},{6,6},{7,71},{8,8},{9,73},{... | collective-permute-start | bytes 393224 | tf_op jit(solution)/shard_map/ppermute | solution.py:30
  113.5 1.9 %collective-permute-start.18 = (bf16[128,512]{1,0:T(8,128)(2,1)S(1)}, bf16[128,512]{1,0:T(8,128)(2,1)S(1)}, u32[]{:S(2)}, u32[]{:S(2)}) collective-permute-start(bf16[128,512]{1,0:T(8,128)(2,1)S(1)} %get-tuple-element.76), channel_id=1, source_target_pairs={{0,16},{1,81},{2,18},{3,83},{4,20},{5,85},{6,22},{7,87},{8,24},{9,... | collective-permute-start | bytes 393224 | tf_op jit(solution)/shard_map/ppermute | solution.py:30
  115.4 0.3 collective-permute-start.32
  115.8 1.4 collective-permute-done.17
  117.2 3.8 %collective-permute-done.18 = bf16[128,512]{1,0:T(8,128)(2,1)S(1)} collective-permute-done((bf16[128,512]{1,0:T(8,128)(2,1)S(1)}, bf16[128,512]{1,0:T(8,128)(2,1)S(1)}, u32[]{:S(2)}, u32[]{:S(2)}) %collective-permute-start.18) | collective-permute-done | bytes 131104 | tf_op jit(solution)/shard_map/ppermute | solution.py:30
  121.2 0.7 shard_map.55
  121.8 3.1 %collective-permute-start.33 = (bf16[128,512]{1,0:T(8,128)(2,1)S(1)}, bf16[128,512]{1,0:T(8,128)(2,1)S(1)}, u32[]{:S(2)}, u32[]{:S(2)}) collective-permute-start(bf16[128,512]{1,0:T(8,128)(2,1)S(1)} %get-tuple-element.65), channel_id=1, source_target_pairs={{0,0},{1,8},{2,2},{3,10},{4,4},{5,12},{6,6},{7,14},{8,9},{9,1},{10... | collective-permute-start | bytes 393224 | tf_op jit(solution)/shard_map/ppermute | solution.py:30
  124.9 1.3 collective-permute-start.34
  126.2 2.1 %collective-permute-start.35 = (bf16[128,512]{1,0:T(8,128)(2,1)S(1)}, bf16[128,512]{1,0:T(8,128)(2,1)S(1)}, u32[]{:S(2)}, u32[]{:S(2)}) collective-permute-start(bf16[128,512]{1,0:T(8,128)(2,1)S(1)} %get-tuple-element.67), channel_id=1, source_target_pairs={{0,4},{1,12},{2,6},{3,14},{4,0},{5,8},{6,2},{7,10},{8,13},{9,5},{1... | collective-permute-start | bytes 393224 | tf_op jit(solution)/shard_map/ppermute | solution.py:30
  128.4 1.7 %collective-permute-start.36 = (bf16[128,512]{1,0:T(8,128)(2,1)S(1)}, bf16[128,512]{1,0:T(8,128)(2,1)S(1)}, u32[]{:S(2)}, u32[]{:S(2)}) collective-permute-start(bf16[128,512]{1,0:T(8,128)(2,1)S(1)} %get-tuple-element.68), channel_id=1, source_target_pairs={{0,6},{1,14},{2,0},{3,8},{4,2},{5,10},{6,4},{7,12},{8,15},{9,7},{1... | collective-permute-start | bytes 393224 | tf_op jit(solution)/shard_map/ppermute | solution.py:30
  130.0 0.7 shard_map.52
  130.7 2.6 %collective-permute-start.22 = (bf16[128,512]{1,0:T(8,128)(2,1)S(1)}, bf16[128,512]{1,0:T(8,128)(2,1)S(1)}, u32[]{:S(2)}, u32[]{:S(2)}) collective-permute-start(bf16[128,512]{1,0:T(8,128)(2,1)S(1)} %get-tuple-element.60), channel_id=1, source_target_pairs={{0,0},{1,8},{2,2},{3,10},{4,4},{5,12},{6,6},{7,14},{8,9},{9,1},{10... | collective-permute-start | bytes 393224 | tf_op jit(solution)/shard_map/ppermute | solution.py:30
  133.3 0.7 collective-permute-start.23
  134.0 1.5 collective-permute-start.24
  135.4 2.4 %collective-permute-start.25 = (bf16[128,512]{1,0:T(8,128)(2,1)S(1)}, bf16[128,512]{1,0:T(8,128)(2,1)S(1)}, u32[]{:S(2)}, u32[]{:S(2)}) collective-permute-start(bf16[128,512]{1,0:T(8,128)(2,1)S(1)} %get-tuple-element.63), channel_id=1, source_target_pairs={{0,6},{1,14},{2,0},{3,8},{4,2},{5,10},{6,4},{7,12},{8,15},{9,7},{1... | collective-permute-start | bytes 393224 | tf_op jit(solution)/shard_map/ppermute | solution.py:30
  137.8 5.4 %collective-permute-done.23.refs_1_ = bf16[128,512]{1,0:T(8,128)(2,1)S(1)} collective-permute-done((bf16[128,512]{1,0:T(8,128)(2,1)S(1)}, bf16[128,512]{1,0:T(8,128)(2,1)S(1)}, u32[]{:S(2)}, u32[]{:S(2)}) %collective-permute-start.23) | collective-permute-done | bytes 131104 | tf_op jit(solution)/shard_map/ppermute | solution.py:30
  143.2 0.4 collective-permute-done.25.refs_3_
  143.6 1.6 %shard_map.56 = bf16[256,2048]{1,0:T(8,128)(2,1)} custom-call(s32[32]{0:T(128)S(1)} %dynamic-slice_bitcast_fusion.table, bf16[128,512]{1,0:T(8,128)(2,1)S(1)} %collective-permute-done.22.refs_0_, bf16[128,512]{1,0:T(8,128)(2,1)S(1)} %collective-permute-done.23.refs_1_, bf16[128,512]{1,0:T(8,128)(2,1)S(1)} %collective-permute-done.24.refs_2_, ...), custom_call_target="tpu_custom_call" | custom-call | bytes 2097152 | tf_op jit(solution)/shard_map/pallas_call | solution.py:248
  (41 shorter events, 0.7 us)
Async XLA Ops:
  0.0 9.1 %collective-permute-start = (bf16[256,512]{1,0:T(8,128)(2,1)}, bf16[256,512]{1,0:T(8,128)(2,1)S(1)}, u32[]{:S(2)}, u32[]{:S(2)}) collective-permute-start(bf16[256,512]{1,0:T(8,128)(2,1)} %param.5), channel_id=1, source_target_pairs={{0,64},{1,65},{2,66},{3,67},{4,68},{5,69},{6,70},{7,71},{8,72},{9,... | collective-permute-start | bytes 786440 | tf_op jit(solution)/shard_map/ppermute | solution.py:30
  5.8 3.3 %copy-start.1 = (bf16[256,512]{1,0:T(8,128)(2,1)S(1)}, bf16[256,512]{1,0:T(8,128)(2,1)}, u32[]{:S(2)}) copy-start(bf16[256,512]{1,0:T(8,128)(2,1)} %param.5) | copy-start | bytes 786436
  9.2 7.1 %collective-permute-start.2 = (bf16[1,2,128,512]{3,2,1,0:T(8,128)(2,1)S(1)}, bf16[1,2,128,512]{3,2,1,0:T(8,128)(2,1)S(1)}, u32[]{:S(2)}, u32[]{:S(2)}) collective-permute-start(bf16[1,2,128,512]{3,2,1,0:T(8,128)(2,1)S(1)} %get-tuple-element.41), channel_id=1, source_target_pairs={{0,16},{1,49},{2,18},{3,51},{4,20},{5,53},{6,22},{7,55},{8,24},{9,... | collective-permute-start | bytes 786440 | tf_op jit(solution)/shard_map/ppermute | solution.py:30
  12.0 7.5 %collective-permute-start.1 = (bf16[1,2,128,512]{3,2,1,0:T(8,128)(2,1)S(1)}, bf16[1,2,128,512]{3,2,1,0:T(8,128)(2,1)S(1)}, u32[]{:S(2)}, u32[]{:S(2)}) collective-permute-start(bf16[1,2,128,512]{3,2,1,0:T(8,128)(2,1)S(1)} %get-tuple-element.40), channel_id=1, source_target_pairs={{0,2},{1,7},{2,0},{3,5},{4,6},{5,3},{6,4},{7,1},{8,10},{9,15},{10,... | collective-permute-start | bytes 786440 | tf_op jit(solution)/shard_map/ppermute | solution.py:30
  15.8 12.4 %collective-permute-start.5 = (bf16[2048,256]{1,0:T(8,128)(2,1)S(1)}, bf16[2048,256]{1,0:T(8,128)(2,1)S(1)}, u32[]{:S(2)}, u32[]{:S(2)}) collective-permute-start(bf16[2048,256]{1,0:T(8,128)(2,1)S(1)} %get-tuple-element.46), channel_id=1, source_target_pairs={{0,1},{1,0},{2,3},{3,2},{4,5},{5,4},{6,7},{7,6},{8,9},{9,8},{10,11... | collective-permute-start | bytes 3145736 | tf_op jit(solution)/shard_map/ppermute | solution.py:30
  15.8 12.4 %collective-permute-start.6 = (bf16[2048,256]{1,0:T(8,128)(2,1)S(1)}, bf16[2048,256]{1,0:T(8,128)(2,1)S(1)}, u32[]{:S(2)}, u32[]{:S(2)}) collective-permute-start(bf16[2048,256]{1,0:T(8,128)(2,1)S(1)} %get-tuple-element.47), channel_id=1, source_target_pairs={{0,1},{1,0},{2,3},{3,2},{4,5},{5,4},{6,7},{7,6},{8,9},{9,8},{10,11... | collective-permute-start | bytes 3145736 | tf_op jit(solution)/shard_map/ppermute | solution.py:30
  19.6 8.4 %collective-permute-start.4 = (bf16[2,2,128,512]{3,2,1,0:T(8,128)(2,1)S(1)}, bf16[2,2,128,512]{3,2,1,0:T(8,128)(2,1)S(1)}, u32[]{:S(2)}, u32[]{:S(2)}) collective-permute-start(bf16[2,2,128,512]{3,2,1,0:T(8,128)(2,1)S(1)} %pad_maximum_fusion.3), channel_id=1, source_target_pairs={{0,48},{1,17},{2,50},{3,19},{4,52},{5,21},{6,54},{7,23},{8,56},{9,... | collective-permute-start | bytes 1572872 | tf_op jit(solution)/shard_map/ppermute | solution.py:30
  19.7 8.4 %collective-permute-start.3 = (bf16[2,2,128,512]{3,2,1,0:T(8,128)(2,1)S(1)}, bf16[2,2,128,512]{3,2,1,0:T(8,128)(2,1)S(1)}, u32[]{:S(2)}, u32[]{:S(2)}) collective-permute-start(bf16[2,2,128,512]{3,2,1,0:T(8,128)(2,1)S(1)} %pad_maximum_fusion.2), channel_id=1, source_target_pairs={{0,6},{1,3},{2,4},{3,1},{4,2},{5,7},{6,0},{7,5},{8,14},{9,11},{10,... | collective-permute-start | bytes 1572872 | tf_op jit(solution)/shard_map/ppermute | solution.py:30
  19.8 19.7 %collective-permute-start.8 = (bf16[2048,256]{1,0:T(8,128)(2,1)S(1)}, bf16[2048,256]{1,0:T(8,128)(2,1)S(1)}, u32[]{:S(2)}, u32[]{:S(2)}) collective-permute-start(bf16[2048,256]{1,0:T(8,128)(2,1)S(1)} %get-tuple-element.37), channel_id=1, source_target_pairs={{0,8},{1,9},{2,10},{3,11},{4,12},{5,13},{6,14},{7,15},{8,0},{9,1},... | collective-permute-start | bytes 3145736 | tf_op jit(solution)/shard_map/ppermute | solution.py:30
  28.2 18.3 %collective-permute-start.10 = (bf16[4,2,128,512]{3,2,1,0:T(8,128)(2,1)S(1)}, bf16[4,2,128,512]{3,2,1,0:T(8,128)(2,1)S(1)}, u32[]{:S(2)}, u32[]{:S(2)}) collective-permute-start(bf16[4,2,128,512]{3,2,1,0:T(8,128)(2,1)S(1)} %pad_maximum_fusion.refs_6_.refs_4_), channel_id=1, source_target_pairs={{0,16},{1,49},{2,18},{3,51},{4,20},{5,53},{6,22},{7,55},{8,24},{9,... | collective-permute-start | bytes 3145736 | tf_op jit(solution)/shard_map/ppermute | solution.py:30
  28.8 17.7 %collective-permute-start.7 = (bf16[4,2,128,512]{3,2,1,0:T(8,128)(2,1)S(1)}, bf16[4,2,128,512]{3,2,1,0:T(8,128)(2,1)S(1)}, u32[]{:S(2)}, u32[]{:S(2)}) collective-permute-start(bf16[4,2,128,512]{3,2,1,0:T(8,128)(2,1)S(1)} %pad_maximum_fusion.1.refs_3_.refs_1_), channel_id=1, source_target_pairs={{0,2},{1,7},{2,0},{3,5},{4,6},{5,3},{6,4},{7,1},{8,10},{9,15},{10,... | collective-permute-start | bytes 3145736 | tf_op jit(solution)/shard_map/ppermute | solution.py:30
  39.5 19.1 %collective-permute-start.13 = (bf16[4,2,128,512]{3,2,1,0:T(8,128)(2,1)S(1)}, bf16[4,2,128,512]{3,2,1,0:T(8,128)(2,1)S(1)}, u32[]{:S(2)}, u32[]{:S(2)}) collective-permute-start(bf16[4,2,128,512]{3,2,1,0:T(8,128)(2,1)S(1)} %pad_maximum_fusion.1.refs_3_.refs_1_), channel_id=1, source_target_pairs={{0,6},{1,3},{2,4},{3,1},{4,2},{5,7},{6,0},{7,5},{8,14},{9,11},{10,... | collective-permute-start | bytes 3145736 | tf_op jit(solution)/shard_map/ppermute | solution.py:30
  42.7 15.8 %collective-permute-start.14 = (bf16[4,2,128,512]{3,2,1,0:T(8,128)(2,1)S(1)}, bf16[4,2,128,512]{3,2,1,0:T(8,128)(2,1)S(1)}, u32[]{:S(2)}, u32[]{:S(2)}) collective-permute-start(bf16[4,2,128,512]{3,2,1,0:T(8,128)(2,1)S(1)} %pad_maximum_fusion.refs_6_.refs_4_), channel_id=1, source_target_pairs={{0,48},{1,17},{2,50},{3,19},{4,52},{5,21},{6,54},{7,23},{8,56},{9,... | collective-permute-start | bytes 3145736 | tf_op jit(solution)/shard_map/ppermute | solution.py:30
  45.0 20.7 %collective-permute-start.12 = (bf16[2048,256]{1,0:T(8,128)(2,1)S(1)}, bf16[2048,256]{1,0:T(8,128)(2,1)S(1)}, u32[]{:S(2)}, u32[]{:S(2)}) collective-permute-start(bf16[2048,256]{1,0:T(8,128)(2,1)S(1)} %collective-permute-done.6), channel_id=1, source_target_pairs={{0,8},{1,9},{2,10},{3,11},{4,12},{5,13},{6,14},{7,15},{8,0},{9,1},... | collective-permute-start | bytes 3145736 | tf_op jit(solution)/shard_map/ppermute | solution.py:30
  46.5 22.6 %collective-permute-start.11 = (bf16[4,2,128,512]{3,2,1,0:T(8,128)(2,1)S(1)}, bf16[4,2,128,512]{3,2,1,0:T(8,128)(2,1)S(1)}, u32[]{:S(2)}, u32[]{:S(2)}) collective-permute-start(bf16[4,2,128,512]{3,2,1,0:T(8,128)(2,1)S(1)} %collective-permute-done.10.refs_7_.refs_5_), channel_id=1, source_target_pairs={{0,48},{1,17},{2,50},{3,19},{4,52},{5,21},{6,54},{7,23},{8,56},{9,... | collective-permute-start | bytes 3145736 | tf_op jit(solution)/shard_map/ppermute | solution.py:30
  46.5 23.2 %collective-permute-start.9 = (bf16[4,2,128,512]{3,2,1,0:T(8,128)(2,1)S(1)}, bf16[4,2,128,512]{3,2,1,0:T(8,128)(2,1)S(1)}, u32[]{:S(2)}, u32[]{:S(2)}) collective-permute-start(bf16[4,2,128,512]{3,2,1,0:T(8,128)(2,1)S(1)} %collective-permute-done.7.refs_4_.refs_2_), channel_id=1, source_target_pairs={{0,6},{1,3},{2,4},{3,1},{4,2},{5,7},{6,0},{7,5},{8,14},{9,11},{10,... | collective-permute-start | bytes 3145736 | tf_op jit(solution)/shard_map/ppermute | solution.py:30
  71.2 8.8 %collective-permute-start.26 = (bf16[4,128,1024]{2,1,0:T(8,128)(2,1)S(1)}, bf16[4,128,1024]{2,1,0:T(8,128)(2,1)S(1)}, u32[]{:S(2)}, u32[]{:S(2)}) collective-permute-start(bf16[4,128,1024]{2,1,0:T(8,128)(2,1)S(1)} %shard_map.54), channel_id=1, source_target_pairs={{0,1},{1,0},{2,3},{3,2},{4,5},{5,4},{6,7},{7,6},{8,9},{9,8},{10,11... | collective-permute-start | bytes 3145736 | tf_op jit(solution)/shard_map/ppermute | solution.py:30
  78.4 4.7 %collective-permute-start.15 = (bf16[4,128,1024]{2,1,0:T(8,128)(2,1)S(1)}, bf16[4,128,1024]{2,1,0:T(8,128)(2,1)S(1)}, u32[]{:S(2)}, u32[]{:S(2)}) collective-permute-start(bf16[4,128,1024]{2,1,0:T(8,128)(2,1)S(1)} %shard_map.51), channel_id=1, source_target_pairs={{0,1},{1,0},{2,3},{3,2},{4,5},{5,4},{6,7},{7,6},{8,9},{9,8},{10,11... | collective-permute-start | bytes 3145736 | tf_op jit(solution)/shard_map/ppermute | solution.py:30
  80.5 13.1 %collective-permute-start.27 = (bf16[4,128,512]{2,1,0:T(8,128)(2,1)S(1)}, bf16[4,128,512]{2,1,0:T(8,128)(2,1)S(1)}, u32[]{:S(2)}, u32[]{:S(2)}) collective-permute-start(bf16[4,128,512]{2,1,0:T(8,128)(2,1)S(1)} %slice.96), channel_id=1, source_target_pairs={{0,8},{1,9},{2,10},{3,11},{4,12},{5,13},{6,14},{7,15},{8,0},{9,1},... | collective-permute-start | bytes 1572872 | tf_op jit(solution)/shard_map/ppermute | solution.py:30
  83.7 21.1 %collective-permute-start.16 = (bf16[4,128,512]{2,1,0:T(8,128)(2,1)S(1)}, bf16[4,128,512]{2,1,0:T(8,128)(2,1)S(1)}, u32[]{:S(2)}, u32[]{:S(2)}) collective-permute-start(bf16[4,128,512]{2,1,0:T(8,128)(2,1)S(1)} %slice.97), channel_id=1, source_target_pairs={{0,8},{1,9},{2,10},{3,11},{4,12},{5,13},{6,14},{7,15},{8,0},{9,1},... | collective-permute-start | bytes 1572872 | tf_op jit(solution)/shard_map/ppermute | solution.py:30
  93.8 13.7 %collective-permute-start.28 = (bf16[128,512]{1,0:T(8,128)(2,1)S(1)}, bf16[128,512]{1,0:T(8,128)(2,1)S(1)}, u32[]{:S(2)}, u32[]{:S(2)}) collective-permute-start(bf16[128,512]{1,0:T(8,128)(2,1)S(1)} %get-tuple-element.69), channel_id=1, source_target_pairs={{0,0},{1,65},{2,2},{3,67},{4,4},{5,69},{6,6},{7,71},{8,8},{9,73},{... | collective-permute-start | bytes 393224 | tf_op jit(solution)/shard_map/ppermute | solution.py:30
  97.3 12.7 %collective-permute-start.29 = (bf16[128,512]{1,0:T(8,128)(2,1)S(1)}, bf16[128,512]{1,0:T(8,128)(2,1)S(1)}, u32[]{:S(2)}, u32[]{:S(2)}) collective-permute-start(bf16[128,512]{1,0:T(8,128)(2,1)S(1)} %get-tuple-element.72), channel_id=1, source_target_pairs={{0,16},{1,81},{2,18},{3,83},{4,20},{5,85},{6,22},{7,87},{8,24},{9,... | collective-permute-start | bytes 393224 | tf_op jit(solution)/shard_map/ppermute | solution.py:30
  98.5 14.9 %collective-permute-start.30 = (bf16[128,512]{1,0:T(8,128)(2,1)S(1)}, bf16[128,512]{1,0:T(8,128)(2,1)S(1)}, u32[]{:S(2)}, u32[]{:S(2)}) collective-permute-start(bf16[128,512]{1,0:T(8,128)(2,1)S(1)} %get-tuple-element.71), channel_id=1, source_target_pairs={{0,32},{1,97},{2,34},{3,99},{4,36},{5,101},{6,38},{7,103},{8,40},{... | collective-permute-start | bytes 393224 | tf_op jit(solution)/shard_map/ppermute | solution.py:30
  101.4 14.0 %collective-permute-start.31 = (bf16[128,512]{1,0:T(8,128)(2,1)S(1)}, bf16[128,512]{1,0:T(8,128)(2,1)S(1)}, u32[]{:S(2)}, u32[]{:S(2)}) collective-permute-start(bf16[128,512]{1,0:T(8,128)(2,1)S(1)} %get-tuple-element.70), channel_id=1, source_target_pairs={{0,48},{1,113},{2,50},{3,115},{4,52},{5,117},{6,54},{7,119},{8,56}... | collective-permute-start | bytes 393224 | tf_op jit(solution)/shard_map/ppermute | solution.py:30
  105.0 16.2 %copy-start = (s32[8]{0:T(128)S(1)}, s32[8]{0:T(128)}, u32[]{:S(2)}) copy-start(s32[8]{0:T(128)} %owner.3) | copy-start | bytes 100
  105.0 10.7 %collective-permute-start.19 = (bf16[128,512]{1,0:T(8,128)(2,1)S(1)}, bf16[128,512]{1,0:T(8,128)(2,1)S(1)}, u32[]{:S(2)}, u32[]{:S(2)}) collective-permute-start(bf16[128,512]{1,0:T(8,128)(2,1)S(1)} %get-tuple-element.75), channel_id=1, source_target_pairs={{0,32},{1,97},{2,34},{3,99},{4,36},{5,101},{6,38},{7,103},{8,40},{... | collective-permute-start | bytes 393224 | tf_op jit(solution)/shard_map/ppermute | solution.py:30
  107.5 8.2 %collective-permute-start.20 = (bf16[128,512]{1,0:T(8,128)(2,1)S(1)}, bf16[128,512]{1,0:T(8,128)(2,1)S(1)}, u32[]{:S(2)}, u32[]{:S(2)}) collective-permute-start(bf16[128,512]{1,0:T(8,128)(2,1)S(1)} %get-tuple-element.74), channel_id=1, source_target_pairs={{0,48},{1,113},{2,50},{3,115},{4,52},{5,117},{6,54},{7,119},{8,56}... | collective-permute-start | bytes 393224 | tf_op jit(solution)/shard_map/ppermute | solution.py:30
  110.0 7.2 %collective-permute-start.17 = (bf16[128,512]{1,0:T(8,128)(2,1)S(1)}, bf16[128,512]{1,0:T(8,128)(2,1)S(1)}, u32[]{:S(2)}, u32[]{:S(2)}) collective-permute-start(bf16[128,512]{1,0:T(8,128)(2,1)S(1)} %get-tuple-element.73), channel_id=1, source_target_pairs={{0,0},{1,65},{2,2},{3,67},{4,4},{5,69},{6,6},{7,71},{8,8},{9,73},{... | collective-permute-start | bytes 393224 | tf_op jit(solution)/shard_map/ppermute | solution.py:30
  113.5 7.5 %collective-permute-start.18 = (bf16[128,512]{1,0:T(8,128)(2,1)S(1)}, bf16[128,512]{1,0:T(8,128)(2,1)S(1)}, u32[]{:S(2)}, u32[]{:S(2)}) collective-permute-start(bf16[128,512]{1,0:T(8,128)(2,1)S(1)} %get-tuple-element.76), channel_id=1, source_target_pairs={{0,16},{1,81},{2,18},{3,83},{4,20},{5,85},{6,22},{7,87},{8,24},{9,... | collective-permute-start | bytes 393224 | tf_op jit(solution)/shard_map/ppermute | solution.py:30
  115.4 5.7 %collective-permute-start.32 = (bf16[4,128,512]{2,1,0:T(8,128)(2,1)S(1)}, bf16[4,128,512]{2,1,0:T(8,128)(2,1)S(1)}, u32[]{:S(2)}, u32[]{:S(2)}) collective-permute-start(bf16[4,128,512]{2,1,0:T(8,128)(2,1)S(1)} %pad_maximum_fusion.5.own), channel_id=1, source_target_pairs={{0,1},{1,0},{2,3},{3,2},{4,5},{5,4},{6,7},{7,6},{8,9},{9,8},{10,11... | collective-permute-start | bytes 1572872 | tf_op jit(solution)/shard_map/ppermute | solution.py:30
  121.1 9.0 %collective-permute-start.21 = (bf16[4,128,512]{2,1,0:T(8,128)(2,1)S(1)}, bf16[4,128,512]{2,1,0:T(8,128)(2,1)S(1)}, u32[]{:S(2)}, u32[]{:S(2)}) collective-permute-start(bf16[4,128,512]{2,1,0:T(8,128)(2,1)S(1)} %pad_maximum_fusion.4.own), channel_id=1, source_target_pairs={{0,1},{1,0},{2,3},{3,2},{4,5},{5,4},{6,7},{7,6},{8,9},{9,8},{10,11... | collective-permute-start | bytes 1572872 | tf_op jit(solution)/shard_map/ppermute | solution.py:30
  121.8 11.5 %collective-permute-start.33 = (bf16[128,512]{1,0:T(8,128)(2,1)S(1)}, bf16[128,512]{1,0:T(8,128)(2,1)S(1)}, u32[]{:S(2)}, u32[]{:S(2)}) collective-permute-start(bf16[128,512]{1,0:T(8,128)(2,1)S(1)} %get-tuple-element.65), channel_id=1, source_target_pairs={{0,0},{1,8},{2,2},{3,10},{4,4},{5,12},{6,6},{7,14},{8,9},{9,1},{10... | collective-permute-start | bytes 393224 | tf_op jit(solution)/shard_map/ppermute | solution.py:30
  124.9 9.1 %collective-permute-start.34 = (bf16[128,512]{1,0:T(8,128)(2,1)S(1)}, bf16[128,512]{1,0:T(8,128)(2,1)S(1)}, u32[]{:S(2)}, u32[]{:S(2)}) collective-permute-start(bf16[128,512]{1,0:T(8,128)(2,1)S(1)} %get-tuple-element.66), channel_id=1, source_target_pairs={{0,2},{1,10},{2,4},{3,12},{4,6},{5,14},{6,0},{7,8},{8,11},{9,3},{1... | collective-permute-start | bytes 393224 | tf_op jit(solution)/shard_map/ppermute | solution.py:30
  126.2 9.2 %collective-permute-start.35 = (bf16[128,512]{1,0:T(8,128)(2,1)S(1)}, bf16[128,512]{1,0:T(8,128)(2,1)S(1)}, u32[]{:S(2)}, u32[]{:S(2)}) collective-permute-start(bf16[128,512]{1,0:T(8,128)(2,1)S(1)} %get-tuple-element.67), channel_id=1, source_target_pairs={{0,4},{1,12},{2,6},{3,14},{4,0},{5,8},{6,2},{7,10},{8,13},{9,5},{1... | collective-permute-start | bytes 393224 | tf_op jit(solution)/shard_map/ppermute | solution.py:30
  128.4 9.5 %collective-permute-start.36 = (bf16[128,512]{1,0:T(8,128)(2,1)S(1)}, bf16[128,512]{1,0:T(8,128)(2,1)S(1)}, u32[]{:S(2)}, u32[]{:S(2)}) collective-permute-start(bf16[128,512]{1,0:T(8,128)(2,1)S(1)} %get-tuple-element.68), channel_id=1, source_target_pairs={{0,6},{1,14},{2,0},{3,8},{4,2},{5,10},{6,4},{7,12},{8,15},{9,7},{1... | collective-permute-start | bytes 393224 | tf_op jit(solution)/shard_map/ppermute | solution.py:30
  130.7 7.1 %collective-permute-start.22 = (bf16[128,512]{1,0:T(8,128)(2,1)S(1)}, bf16[128,512]{1,0:T(8,128)(2,1)S(1)}, u32[]{:S(2)}, u32[]{:S(2)}) collective-permute-start(bf16[128,512]{1,0:T(8,128)(2,1)S(1)} %get-tuple-element.60), channel_id=1, source_target_pairs={{0,0},{1,8},{2,2},{3,10},{4,4},{5,12},{6,6},{7,14},{8,9},{9,1},{10... | collective-permute-start | bytes 393224 | tf_op jit(solution)/shard_map/ppermute | solution.py:30
  133.3 9.9 %collective-permute-start.23 = (bf16[128,512]{1,0:T(8,128)(2,1)S(1)}, bf16[128,512]{1,0:T(8,128)(2,1)S(1)}, u32[]{:S(2)}, u32[]{:S(2)}) collective-permute-start(bf16[128,512]{1,0:T(8,128)(2,1)S(1)} %get-tuple-element.61), channel_id=1, source_target_pairs={{0,2},{1,10},{2,4},{3,12},{4,6},{5,14},{6,0},{7,8},{8,11},{9,3},{1... | collective-permute-start | bytes 393224 | tf_op jit(solution)/shard_map/ppermute | solution.py:30
  134.0 9.2 %collective-permute-start.24 = (bf16[128,512]{1,0:T(8,128)(2,1)S(1)}, bf16[128,512]{1,0:T(8,128)(2,1)S(1)}, u32[]{:S(2)}, u32[]{:S(2)}) collective-permute-start(bf16[128,512]{1,0:T(8,128)(2,1)S(1)} %get-tuple-element.62), channel_id=1, source_target_pairs={{0,4},{1,12},{2,6},{3,14},{4,0},{5,8},{6,2},{7,10},{8,13},{9,5},{1... | collective-permute-start | bytes 393224 | tf_op jit(solution)/shard_map/ppermute | solution.py:30
  135.4 8.2 %collective-permute-start.25 = (bf16[128,512]{1,0:T(8,128)(2,1)S(1)}, bf16[128,512]{1,0:T(8,128)(2,1)S(1)}, u32[]{:S(2)}, u32[]{:S(2)}) collective-permute-start(bf16[128,512]{1,0:T(8,128)(2,1)S(1)} %get-tuple-element.63), channel_id=1, source_target_pairs={{0,6},{1,14},{2,0},{3,8},{4,2},{5,10},{6,4},{7,12},{8,15},{9,7},{1... | collective-permute-start | bytes 393224 | tf_op jit(solution)/shard_map/ppermute | solution.py:30

commit v18 on v16

--- a/solution.py
+++ b/solution.py
@@ -231,13 +231,11 @@
 
 
 def arrange_kernel(table, *refs):
-    parts, out, sems = refs[:8], refs[8], refs[9]
+    parts, out, sems = refs[:4], refs[4], refs[5]
     copies = []
-    for i, part in enumerate(parts):
-        rows, dz = i // 4, i % 4
+    for dz, part in enumerate(parts):
         at = pl.multiple_of(((table[Z] + 4 - dz) & 3) * (2 * COLS), 2 * COLS)
-        to = out.at[pl.ds(rows * HALF, HALF), pl.ds(at, 2 * COLS)]
-        copies.append(pltpu.make_async_copy(part, to, sems.at[i]))
+        copies.append(pltpu.make_async_copy(part, out.at[:, pl.ds(at, 2 * COLS)], sems.at[dz]))
         copies[-1].start()
     for copy in copies:
         copy.wait()
@@ -284,18 +282,18 @@
         for dy in (2, 1, 3, 0):
             got[dy] = permute(total[dy], lambda x, y, z, c: linear(x + 2 * c, y + dy, z, c))
         own = jnp.stack([got[dy] for dy in range(4)])
-        other = permute(own, other_core)
-        picked = small_call(spread_kernel, [table, owner], [own, other], [(HALF, 2 * COLS)] * 4, pltpu.VMEM)
-        got = {}
-        for dz in (2, 1, 3, 0):
-            got[dz] = permute(picked[dz], lambda x, y, z, c: linear(x ^ c, y, z + dz, x % 2))
-        return [got[dz] for dz in range(4)]
-
-    blocks = chain("y")
-    blocks = chain("z") + blocks
-    return small_call(
-        arrange_kernel, [table], blocks, [(256, 8 * COLS)], pltpu.HBM, [pltpu.SemaphoreType.DMA((8,))]
-    )[0]
+        return own
+
+    own = chain("y")
+    own = jnp.concatenate([chain("z"), own], axis=1)
+    other = permute(own, other_core)
+
+    picked = small_call(spread_kernel, [table, owner], [own, other], [(256, 2 * COLS)] * 4, pltpu.VMEM)
+    got = {}
+    for dz in (2, 1, 3, 0):
+        got[dz] = permute(picked[dz], lambda x, y, z, c: linear(x ^ c, y, z + dz, x % 2))
+    got = [got[dz] for dz in range(4)]
+    return small_call(arrange_kernel, [table], got, [(256, 8 * COLS)], pltpu.HBM, [pltpu.SemaphoreType.DMA((4,))])[0]
 
 
 def solution(mesh):

time: 146 us -> 145 us (level)
  waiting for transfers between devices: 59.9 us -> 65.8 us
  starting transfers between devices: 59.3 us -> 54 us
    ppermute x37 -> x32, waiting for transfers between devices: 59.9 us -> 65.8 us  [permute(): lax.ppermute(value, AXES, [(i, move(*coords(i))) for i in range(N_DEV)])]
    ppermute x37 -> x32, starting transfers between devices: 59.3 us -> 54 us  [permute(): lax.ppermute(value, AXES, [(i, move(*coords(i))) for i in range(N_DEV)])]
  transfers between devices with their start and end apart: 37 -> 32, of which waited for: 14 -> 15; matrix products, arithmetic and copies ran while one was open for 2% -> 2% of each run, Pallas kernels for 14% -> 13%
where the time goes in v18:
time: 145 us
  waiting for transfers between devices  65.8 us (45%)
  starting transfers between devices  54 us (37%)
  Pallas kernels  22.2 us (15%)
  other arithmetic  1.46 us (1%)
    ppermute x32, waiting for transfers between devices, permute(): lax.ppermute(value, AXES, [(i, move(*coords(i))) for i in range(N_DEV)])  65.8 us
    ppermute x32, starting transfers between devices, permute(): lax.ppermute(value, AXES, [(i, move(*coords(i))) for i in range(N_DEV)])  54 us
    pallas_call x2, Pallas kernels, early_product(): pl.pallas_call(functools.partial(early_kernel, count), in_specs=[pl.Block...  7.91 us
    pallas_call x2, Pallas kernels, refit(): pl.pallas_call(functools.partial(refit_kernel, first), in_specs=[pl.Block...  6.55 us
    pallas_call x4, Pallas kernels, product(): pl.pallas_call(functools.partial(product_kernel, part, keep), in_specs=[p...  5.52 us
  transfers between devices with their start and end apart: 32, of which 15 were waited for; matrix products, arithmetic and copies ran while one was open for 2% of the time, Pallas kernels for 13%

profile of v18, /device:TPU:3, one launch (start us, length us, event | category | flops | bytes accessed | tf_op | source)
XLA Modules:
  0.0 144.8 jit_solution(7046036271817467923)
XLA Ops:
  0.0 1.8 %collective-permute-start = (bf16[256,512]{1,0:T(8,128)(2,1)}, bf16[256,512]{1,0:T(8,128)(2,1)S(1)}, u32[]{:S(2)}, u32[]{:S(2)}) collective-permute-start(bf16[256,512]{1,0:T(8,128)(2,1)} %param.5), channel_id=1, source_target_pairs={{0,64},{1,65},{2,66},{3,67},{4,68},{5,69},{6,70},{7,71},{8,72},{9,... | collective-permute-start | bytes 786440 | tf_op jit(solution)/shard_map/ppermute | solution.py:30
  1.8 0.7 dynamic-slice_bitcast_fusion.table
  2.5 3.3 %shard_map.46 = (bf16[2048,256]{1,0:T(8,128)(2,1)S(1)}, bf16[2048,256]{1,0:T(8,128)(2,1)S(1)}) custom-call(s32[32]{0:T(128)S(1)} %dynamic-slice_bitcast_fusion.table, f32[8192,256]{1,0:T(8,128)} %master.3), custom_call_target="tpu_custom_call" | custom-call | flops 6291456 | bytes 6291456 | tf_op jit(solution)/shard_map/pallas_call | solution.py:122
  5.8 3.1 %collective-permute-done = bf16[256,512]{1,0:T(8,128)(2,1)S(1)} collective-permute-done((bf16[256,512]{1,0:T(8,128)(2,1)}, bf16[256,512]{1,0:T(8,128)(2,1)S(1)}, u32[]{:S(2)}, u32[]{:S(2)}) %collective-permute-start) | collective-permute-done | bytes 262176 | tf_op jit(solution)/shard_map/ppermute | solution.py:30
  8.9 2.8 %collective-permute-start.2 = (bf16[1,2,128,512]{3,2,1,0:T(8,128)(2,1)S(1)}, bf16[1,2,128,512]{3,2,1,0:T(8,128)(2,1)S(1)}, u32[]{:S(2)}, u32[]{:S(2)}) collective-permute-start(bf16[1,2,128,512]{3,2,1,0:T(8,128)(2,1)S(1)} %get-tuple-element.36), channel_id=1, source_target_pairs={{0,16},{1,49},{2,18},{3,51},{4,20},{5,53},{6,22},{7,55},{8,24},{9,... | collective-permute-start | bytes 786440 | tf_op jit(solution)/shard_map/ppermute | solution.py:30
  11.8 3.8 %collective-permute-start.1 = (bf16[1,2,128,512]{3,2,1,0:T(8,128)(2,1)S(1)}, bf16[1,2,128,512]{3,2,1,0:T(8,128)(2,1)S(1)}, u32[]{:S(2)}, u32[]{:S(2)}) collective-permute-start(bf16[1,2,128,512]{3,2,1,0:T(8,128)(2,1)S(1)} %get-tuple-element.35), channel_id=1, source_target_pairs={{0,2},{1,7},{2,0},{3,5},{4,6},{5,3},{6,4},{7,1},{8,10},{9,15},{10,... | collective-permute-start | bytes 786440 | tf_op jit(solution)/shard_map/ppermute | solution.py:30
  15.5 3.3 %shard_map.47 = (bf16[2048,256]{1,0:T(8,128)(2,1)S(1)}, bf16[2048,256]{1,0:T(8,128)(2,1)S(1)}) custom-call(s32[32]{0:T(128)S(1)} %dynamic-slice_bitcast_fusion.table, f32[8192,256]{1,0:T(8,128)} %master.3), custom_call_target="tpu_custom_call" | custom-call | flops 6291456 | bytes 6291456 | tf_op jit(solution)/shard_map/pallas_call | solution.py:122
  18.8 0.1 collective-permute-start.5
  18.9 0.5 collective-permute-start.6
  19.5 0.1 collective-permute-start.4
  19.6 0.1 collective-permute-start.3
  19.7 0.3 collective-permute-start.8
  20.0 7.9 %collective-permute-done.4 = bf16[2,2,128,512]{3,2,1,0:T(8,128)(2,1)S(1)} collective-permute-done((bf16[2,2,128,512]{3,2,1,0:T(8,128)(2,1)S(1)}, bf16[2,2,128,512]{3,2,1,0:T(8,128)(2,1)S(1)}, u32[]{:S(2)}, u32[]{:S(2)}) %collective-permute-start.4) | collective-permute-done | bytes 524320 | tf_op jit(solution)/shard_map/ppermute | solution.py:30
  27.9 0.1 pad_maximum_fusion.1.refs_3_.refs_1_
  28.0 0.1 pad_maximum_fusion.refs_6_.refs_4_
  28.1 1.0 collective-permute-start.10
  29.1 2.2 %collective-permute-start.7 = (bf16[4,2,128,512]{3,2,1,0:T(8,128)(2,1)S(1)}, bf16[4,2,128,512]{3,2,1,0:T(8,128)(2,1)S(1)}, u32[]{:S(2)}, u32[]{:S(2)}) collective-permute-start(bf16[4,2,128,512]{3,2,1,0:T(8,128)(2,1)S(1)} %pad_maximum_fusion.1.refs_3_.refs_1_), channel_id=1, source_target_pairs={{0,2},{1,7},{2,0},{3,5},{4,6},{5,3},{6,4},{7,1},{8,10},{9,15},{10,... | collective-permute-start | bytes 3145736 | tf_op jit(solution)/shard_map/ppermute | solution.py:30
  31.4 7.9 %collective-permute-done.8.refs_2_.far = bf16[2048,256]{1,0:T(8,128)(2,1)S(1)} collective-permute-done((bf16[2048,256]{1,0:T(8,128)(2,1)S(1)}, bf16[2048,256]{1,0:T(8,128)(2,1)S(1)}, u32[]{:S(2)}, u32[]{:S(2)}) %collective-permute-start.8) | collective-permute-done | bytes 1048608 | tf_op jit(solution)/shard_map/ppermute | solution.py:30
  39.3 3.2 %collective-permute-start.13 = (bf16[4,2,128,512]{3,2,1,0:T(8,128)(2,1)S(1)}, bf16[4,2,128,512]{3,2,1,0:T(8,128)(2,1)S(1)}, u32[]{:S(2)}, u32[]{:S(2)}) collective-permute-start(bf16[4,2,128,512]{3,2,1,0:T(8,128)(2,1)S(1)} %pad_maximum_fusion.1.refs_3_.refs_1_), channel_id=1, source_target_pairs={{0,6},{1,3},{2,4},{3,1},{4,2},{5,7},{6,0},{7,5},{8,14},{9,11},{10,... | collective-permute-start | bytes 3145736 | tf_op jit(solution)/shard_map/ppermute | solution.py:30
  42.6 2.3 %collective-permute-start.14 = (bf16[4,2,128,512]{3,2,1,0:T(8,128)(2,1)S(1)}, bf16[4,2,128,512]{3,2,1,0:T(8,128)(2,1)S(1)}, u32[]{:S(2)}, u32[]{:S(2)}) collective-permute-start(bf16[4,2,128,512]{3,2,1,0:T(8,128)(2,1)S(1)} %pad_maximum_fusion.refs_6_.refs_4_), channel_id=1, source_target_pairs={{0,48},{1,17},{2,50},{3,19},{4,52},{5,21},{6,54},{7,23},{8,56},{9,... | collective-permute-start | bytes 3145736 | tf_op jit(solution)/shard_map/ppermute | solution.py:30
  44.9 0.3 collective-permute-start.12
  45.2 0.3 collective-permute-start.9
  45.5 13.1 %collective-permute-done.13.refs_5_.refs_3_ = bf16[4,2,128,512]{3,2,1,0:T(8,128)(2,1)S(1)} collective-permute-done((bf16[4,2,128,512]{3,2,1,0:T(8,128)(2,1)S(1)}, bf16[4,2,128,512]{3,2,1,0:T(8,128)(2,1)S(1)}, u32[]{:S(2)}, u32[]{:S(2)}) %collective-permute-start.13) | collective-permute-done | bytes 1048608 | tf_op jit(solution)/shard_map/ppermute | solution.py:30
  58.5 5.6 %shard_map.48 = (f32[3,2,512,256]{3,2,1,0:T(8,128)S(1)}, f32[3,2,384,256]{3,2,1,0:T(8,128)S(1)}) custom-call(s32[32]{0:T(128)S(1)} %dynamic-slice_bitcast_fusion.table, bf16[2048,256]{1,0:T(8,128)(2,1)S(1)} %get-tuple-element.48.refs_0_.mine, bf16[2048,256]{1,0:T(8,128)(2,1)S(1)} %collective-permute-done.5.refs_1_.near, ...), custom_call_target="tpu_custom_call" | custom-call | flops 3221225472 | bytes 16777216 | tf_op jit(solution)/shard_map/pallas_call | solution.py:176
  64.1 2.3 %shard_map.49 = (f32[1,2,512,256]{3,2,1,0:T(8,128)S(1)}, f32[1,2,384,256]{3,2,1,0:T(8,128)S(1)}) custom-call(s32[32]{0:T(128)S(1)} %dynamic-slice_bitcast_fusion.table, bf16[2048,256]{1,0:T(8,128)(2,1)S(1)} %collective-permute-done.12.refs_0_.cross, bf16[4,2,128,512]{3,2,1,0:T(8,128)(2,1)S(1)} %pad_maximum_fusion.1.refs_3_.refs_1_, ...), custom_call_target="tpu_custom_call" | custom-call | flops 1073741824 | bytes 16777216 | tf_op jit(solution)/shard_map/pallas_call | solution.py:176
  66.5 2.6 %collective-permute-done.11.refs_0_ = bf16[4,2,128,512]{3,2,1,0:T(8,128)(2,1)S(1)} collective-permute-done((bf16[4,2,128,512]{3,2,1,0:T(8,128)(2,1)S(1)}, bf16[4,2,128,512]{3,2,1,0:T(8,128)(2,1)S(1)}, u32[]{:S(2)}, u32[]{:S(2)}) %collective-permute-start.11) | collective-permute-done | bytes 1048608 | tf_op jit(solution)/shard_map/ppermute | solution.py:30
  69.1 0.7 collective-permute-done.9.refs_0_
  69.8 1.3 shard_map.51
  71.1 5.7 %collective-permute-start.15 = (bf16[4,128,1024]{2,1,0:T(8,128)(2,1)S(1)}, bf16[4,128,1024]{2,1,0:T(8,128)(2,1)S(1)}, u32[]{:S(2)}, u32[]{:S(2)}) collective-permute-start(bf16[4,128,1024]{2,1,0:T(8,128)(2,1)S(1)} %shard_map.51), channel_id=1, source_target_pairs={{0,1},{1,0},{2,3},{3,2},{4,5},{5,4},{6,7},{7,6},{8,9},{9,8},{10,11... | collective-permute-start | bytes 3145736 | tf_op jit(solution)/shard_map/ppermute | solution.py:30
  76.8 1.4 shard_map.53
  78.2 0.1 collective-permute-start.21
  78.3 1.4 shard_map.50
  79.7 0.4 convert_add_fusion.1
  80.2 0.3 collective-permute-start.16
  80.6 1.4 shard_map.52
  82.0 0.3 convert_add_fusion
  82.3 0.1 slice.96
  82.4 1.3 collective-permute-start.22
  83.7 9.6 %collective-permute-done.16 = bf16[4,128,512]{2,1,0:T(8,128)(2,1)S(1)} collective-permute-done((bf16[4,128,512]{2,1,0:T(8,128)(2,1)S(1)}, bf16[4,128,512]{2,1,0:T(8,128)(2,1)S(1)}, u32[]{:S(2)}, u32[]{:S(2)}) %collective-permute-start.16) | collective-permute-done | bytes 524320 | tf_op jit(solution)/shard_map/ppermute | solution.py:30
  93.3 0.2 fusion.1
  93.5 2.6 %collective-permute-start.19 = (bf16[128,512]{1,0:T(8,128)(2,1)S(1)}, bf16[128,512]{1,0:T(8,128)(2,1)S(1)}, u32[]{:S(2)}, u32[]{:S(2)}) collective-permute-start(bf16[128,512]{1,0:T(8,128)(2,1)S(1)} %get-tuple-element.63), channel_id=1, source_target_pairs={{0,32},{1,97},{2,34},{3,99},{4,36},{5,101},{6,38},{7,103},{8,40},{... | collective-permute-start | bytes 393224 | tf_op jit(solution)/shard_map/ppermute | solution.py:30
  96.1 2.4 %collective-permute-start.20 = (bf16[128,512]{1,0:T(8,128)(2,1)S(1)}, bf16[128,512]{1,0:T(8,128)(2,1)S(1)}, u32[]{:S(2)}, u32[]{:S(2)}) collective-permute-start(bf16[128,512]{1,0:T(8,128)(2,1)S(1)} %get-tuple-element.62), channel_id=1, source_target_pairs={{0,48},{1,113},{2,50},{3,115},{4,52},{5,117},{6,54},{7,119},{8,56}... | collective-permute-start | bytes 393224 | tf_op jit(solution)/shard_map/ppermute | solution.py:30
  98.5 3.7 %collective-permute-start.17 = (bf16[128,512]{1,0:T(8,128)(2,1)S(1)}, bf16[128,512]{1,0:T(8,128)(2,1)S(1)}, u32[]{:S(2)}, u32[]{:S(2)}) collective-permute-start(bf16[128,512]{1,0:T(8,128)(2,1)S(1)} %get-tuple-element.61), channel_id=1, source_target_pairs={{0,0},{1,65},{2,2},{3,67},{4,4},{5,69},{6,6},{7,71},{8,8},{9,73},{... | collective-permute-start | bytes 393224 | tf_op jit(solution)/shard_map/ppermute | solution.py:30
  102.2 0.8 collective-permute-start.18
  103.0 1.5 %collective-permute-done.22 = bf16[4,128,512]{2,1,0:T(8,128)(2,1)S(1)} collective-permute-done((bf16[4,128,512]{2,1,0:T(8,128)(2,1)S(1)}, bf16[4,128,512]{2,1,0:T(8,128)(2,1)S(1)}, u32[]{:S(2)}, u32[]{:S(2)}) %collective-permute-start.22) | collective-permute-done | bytes 524320 | tf_op jit(solution)/shard_map/ppermute | solution.py:30
  104.5 0.2 fusion
  104.8 3.8 %collective-permute-start.23 = (bf16[128,512]{1,0:T(8,128)(2,1)S(1)}, bf16[128,512]{1,0:T(8,128)(2,1)S(1)}, u32[]{:S(2)}, u32[]{:S(2)}) collective-permute-start(bf16[128,512]{1,0:T(8,128)(2,1)S(1)} %get-tuple-element.65), channel_id=1, source_target_pairs={{0,0},{1,65},{2,2},{3,67},{4,4},{5,69},{6,6},{7,71},{8,8},{9,73},{... | collective-permute-start | bytes 393224 | tf_op jit(solution)/shard_map/ppermute | solution.py:30
  108.5 2.4 %collective-permute-start.24 = (bf16[128,512]{1,0:T(8,128)(2,1)S(1)}, bf16[128,512]{1,0:T(8,128)(2,1)S(1)}, u32[]{:S(2)}, u32[]{:S(2)}) collective-permute-start(bf16[128,512]{1,0:T(8,128)(2,1)S(1)} %get-tuple-element.68), channel_id=1, source_target_pairs={{0,16},{1,81},{2,18},{3,83},{4,20},{5,85},{6,22},{7,87},{8,24},{9,... | collective-permute-start | bytes 393224 | tf_op jit(solution)/shard_map/ppermute | solution.py:30
  111.0 3.2 %collective-permute-start.25 = (bf16[128,512]{1,0:T(8,128)(2,1)S(1)}, bf16[128,512]{1,0:T(8,128)(2,1)S(1)}, u32[]{:S(2)}, u32[]{:S(2)}) collective-permute-start(bf16[128,512]{1,0:T(8,128)(2,1)S(1)} %get-tuple-element.67), channel_id=1, source_target_pairs={{0,32},{1,97},{2,34},{3,99},{4,36},{5,101},{6,38},{7,103},{8,40},{... | collective-permute-start | bytes 393224 | tf_op jit(solution)/shard_map/ppermute | solution.py:30
  114.1 1.1 collective-permute-start.26
  115.2 1.4 collective-permute-done.24
  116.6 2.1 %collective-permute-done.25 = bf16[128,512]{1,0:T(8,128)(2,1)S(1)} collective-permute-done((bf16[128,512]{1,0:T(8,128)(2,1)S(1)}, bf16[128,512]{1,0:T(8,128)(2,1)S(1)}, u32[]{:S(2)}, u32[]{:S(2)}) %collective-permute-start.25) | collective-permute-done | bytes 131104 | tf_op jit(solution)/shard_map/ppermute | solution.py:30
  118.8 1.6 %collective-permute-done.26 = bf16[128,512]{1,0:T(8,128)(2,1)S(1)} collective-permute-done((bf16[128,512]{1,0:T(8,128)(2,1)S(1)}, bf16[128,512]{1,0:T(8,128)(2,1)S(1)}, u32[]{:S(2)}, u32[]{:S(2)}) %collective-permute-start.26) | collective-permute-done | bytes 131104 | tf_op jit(solution)/shard_map/ppermute | solution.py:30
  120.4 0.1 collective-permute-start.27
  120.5 2.6 %collective-permute-done.27.other = bf16[4,256,512]{2,1,0:T(8,128)(2,1)S(1)} collective-permute-done((bf16[4,256,512]{2,1,0:T(8,128)(2,1)S(1)}, bf16[4,256,512]{2,1,0:T(8,128)(2,1)S(1)}, u32[]{:S(2)}, u32[]{:S(2)}) %collective-permute-start.27) | collective-permute-done | bytes 1048608 | tf_op jit(solution)/shard_map/ppermute | solution.py:30
  123.2 0.7 shard_map.54
  123.9 3.1 %collective-permute-start.28 = (bf16[256,512]{1,0:T(8,128)(2,1)S(1)}, bf16[256,512]{1,0:T(8,128)(2,1)S(1)}, u32[]{:S(2)}, u32[]{:S(2)}) collective-permute-start(bf16[256,512]{1,0:T(8,128)(2,1)S(1)} %get-tuple-element.57), channel_id=1, source_target_pairs={{0,0},{1,8},{2,2},{3,10},{4,4},{5,12},{6,6},{7,14},{8,9},{9,1},{10... | collective-permute-start | bytes 786440 | tf_op jit(solution)/shard_map/ppermute | solution.py:30
  126.9 0.3 collective-permute-start.29
  127.3 2.5 %collective-permute-start.30 = (bf16[256,512]{1,0:T(8,128)(2,1)S(1)}, bf16[256,512]{1,0:T(8,128)(2,1)S(1)}, u32[]{:S(2)}, u32[]{:S(2)}) collective-permute-start(bf16[256,512]{1,0:T(8,128)(2,1)S(1)} %get-tuple-element.59), channel_id=1, source_target_pairs={{0,4},{1,12},{2,6},{3,14},{4,0},{5,8},{6,2},{7,10},{8,13},{9,5},{1... | collective-permute-start | bytes 786440 | tf_op jit(solution)/shard_map/ppermute | solution.py:30
  129.7 1.8 %collective-permute-start.31 = (bf16[256,512]{1,0:T(8,128)(2,1)S(1)}, bf16[256,512]{1,0:T(8,128)(2,1)S(1)}, u32[]{:S(2)}, u32[]{:S(2)}) collective-permute-start(bf16[256,512]{1,0:T(8,128)(2,1)S(1)} %get-tuple-element.60), channel_id=1, source_target_pairs={{0,6},{1,14},{2,0},{3,8},{4,2},{5,10},{6,4},{7,12},{8,15},{9,7},{1... | collective-permute-start | bytes 786440 | tf_op jit(solution)/shard_map/ppermute | solution.py:30
  131.6 8.2 %collective-permute-done.29.refs_1_ = bf16[256,512]{1,0:T(8,128)(2,1)S(1)} collective-permute-done((bf16[256,512]{1,0:T(8,128)(2,1)S(1)}, bf16[256,512]{1,0:T(8,128)(2,1)S(1)}, u32[]{:S(2)}, u32[]{:S(2)}) %collective-permute-start.29) | collective-permute-done | bytes 262176 | tf_op jit(solution)/shard_map/ppermute | solution.py:30
  139.8 2.8 %collective-permute-done.30.refs_2_ = bf16[256,512]{1,0:T(8,128)(2,1)S(1)} collective-permute-done((bf16[256,512]{1,0:T(8,128)(2,1)S(1)}, bf16[256,512]{1,0:T(8,128)(2,1)S(1)}, u32[]{:S(2)}, u32[]{:S(2)}) %collective-permute-start.30) | collective-permute-done | bytes 262176 | tf_op jit(solution)/shard_map/ppermute | solution.py:30
  142.6 0.6 collective-permute-done.31.refs_3_
  143.1 1.5 %shard_map.55 = bf16[256,2048]{1,0:T(8,128)(2,1)} custom-call(s32[32]{0:T(128)S(1)} %dynamic-slice_bitcast_fusion.table, bf16[256,512]{1,0:T(8,128)(2,1)S(1)} %collective-permute-done.28.refs_0_, bf16[256,512]{1,0:T(8,128)(2,1)S(1)} %collective-permute-done.29.refs_1_, bf16[256,512]{1,0:T(8,128)(2,1)S(1)} %collective-permute-done.30.refs_2_, ...), custom_call_target="tpu_custom_call" | custom-call | bytes 2097152 | tf_op jit(solution)/shard_map/pallas_call | solution.py:246
  (29 shorter events, 0.4 us)
Async XLA Ops:
  0.0 8.9 %collective-permute-start = (bf16[256,512]{1,0:T(8,128)(2,1)}, bf16[256,512]{1,0:T(8,128)(2,1)S(1)}, u32[]{:S(2)}, u32[]{:S(2)}) collective-permute-start(bf16[256,512]{1,0:T(8,128)(2,1)} %param.5), channel_id=1, source_target_pairs={{0,64},{1,65},{2,66},{3,67},{4,68},{5,69},{6,70},{7,71},{8,72},{9,... | collective-permute-start | bytes 786440 | tf_op jit(solution)/shard_map/ppermute | solution.py:30
  2.5 6.4 %copy-start.1 = (bf16[256,512]{1,0:T(8,128)(2,1)S(1)}, bf16[256,512]{1,0:T(8,128)(2,1)}, u32[]{:S(2)}) copy-start(bf16[256,512]{1,0:T(8,128)(2,1)} %param.5) | copy-start | bytes 786436
  8.9 10.4 %collective-permute-start.2 = (bf16[1,2,128,512]{3,2,1,0:T(8,128)(2,1)S(1)}, bf16[1,2,128,512]{3,2,1,0:T(8,128)(2,1)S(1)}, u32[]{:S(2)}, u32[]{:S(2)}) collective-permute-start(bf16[1,2,128,512]{3,2,1,0:T(8,128)(2,1)S(1)} %get-tuple-element.36), channel_id=1, source_target_pairs={{0,16},{1,49},{2,18},{3,51},{4,20},{5,53},{6,22},{7,55},{8,24},{9,... | collective-permute-start | bytes 786440 | tf_op jit(solution)/shard_map/ppermute | solution.py:30
  11.8 7.7 %collective-permute-start.1 = (bf16[1,2,128,512]{3,2,1,0:T(8,128)(2,1)S(1)}, bf16[1,2,128,512]{3,2,1,0:T(8,128)(2,1)S(1)}, u32[]{:S(2)}, u32[]{:S(2)}) collective-permute-start(bf16[1,2,128,512]{3,2,1,0:T(8,128)(2,1)S(1)} %get-tuple-element.35), channel_id=1, source_target_pairs={{0,2},{1,7},{2,0},{3,5},{4,6},{5,3},{6,4},{7,1},{8,10},{9,15},{10,... | collective-permute-start | bytes 786440 | tf_op jit(solution)/shard_map/ppermute | solution.py:30
  18.8 9.3 %collective-permute-start.5 = (bf16[2048,256]{1,0:T(8,128)(2,1)S(1)}, bf16[2048,256]{1,0:T(8,128)(2,1)S(1)}, u32[]{:S(2)}, u32[]{:S(2)}) collective-permute-start(bf16[2048,256]{1,0:T(8,128)(2,1)S(1)} %get-tuple-element.41), channel_id=1, source_target_pairs={{0,1},{1,0},{2,3},{3,2},{4,5},{5,4},{6,7},{7,6},{8,9},{9,8},{10,11... | collective-permute-start | bytes 3145736 | tf_op jit(solution)/shard_map/ppermute | solution.py:30
  18.9 9.3 %collective-permute-start.6 = (bf16[2048,256]{1,0:T(8,128)(2,1)S(1)}, bf16[2048,256]{1,0:T(8,128)(2,1)S(1)}, u32[]{:S(2)}, u32[]{:S(2)}) collective-permute-start(bf16[2048,256]{1,0:T(8,128)(2,1)S(1)} %get-tuple-element.42), channel_id=1, source_target_pairs={{0,1},{1,0},{2,3},{3,2},{4,5},{5,4},{6,7},{7,6},{8,9},{9,8},{10,11... | collective-permute-start | bytes 3145736 | tf_op jit(solution)/shard_map/ppermute | solution.py:30
  19.5 8.4 %collective-permute-start.4 = (bf16[2,2,128,512]{3,2,1,0:T(8,128)(2,1)S(1)}, bf16[2,2,128,512]{3,2,1,0:T(8,128)(2,1)S(1)}, u32[]{:S(2)}, u32[]{:S(2)}) collective-permute-start(bf16[2,2,128,512]{3,2,1,0:T(8,128)(2,1)S(1)} %pad_maximum_fusion.3), channel_id=1, source_target_pairs={{0,48},{1,17},{2,50},{3,19},{4,52},{5,21},{6,54},{7,23},{8,56},{9,... | collective-permute-start | bytes 1572872 | tf_op jit(solution)/shard_map/ppermute | solution.py:30
  19.6 8.4 %collective-permute-start.3 = (bf16[2,2,128,512]{3,2,1,0:T(8,128)(2,1)S(1)}, bf16[2,2,128,512]{3,2,1,0:T(8,128)(2,1)S(1)}, u32[]{:S(2)}, u32[]{:S(2)}) collective-permute-start(bf16[2,2,128,512]{3,2,1,0:T(8,128)(2,1)S(1)} %pad_maximum_fusion.2), channel_id=1, source_target_pairs={{0,6},{1,3},{2,4},{3,1},{4,2},{5,7},{6,0},{7,5},{8,14},{9,11},{10,... | collective-permute-start | bytes 1572872 | tf_op jit(solution)/shard_map/ppermute | solution.py:30
  19.7 19.6 %collective-permute-start.8 = (bf16[2048,256]{1,0:T(8,128)(2,1)S(1)}, bf16[2048,256]{1,0:T(8,128)(2,1)S(1)}, u32[]{:S(2)}, u32[]{:S(2)}) collective-permute-start(bf16[2048,256]{1,0:T(8,128)(2,1)S(1)} %get-tuple-element.33), channel_id=1, source_target_pairs={{0,8},{1,9},{2,10},{3,11},{4,12},{5,13},{6,14},{7,15},{8,0},{9,1},... | collective-permute-start | bytes 3145736 | tf_op jit(solution)/shard_map/ppermute | solution.py:30
  28.1 17.0 %collective-permute-start.10 = (bf16[4,2,128,512]{3,2,1,0:T(8,128)(2,1)S(1)}, bf16[4,2,128,512]{3,2,1,0:T(8,128)(2,1)S(1)}, u32[]{:S(2)}, u32[]{:S(2)}) collective-permute-start(bf16[4,2,128,512]{3,2,1,0:T(8,128)(2,1)S(1)} %pad_maximum_fusion.refs_6_.refs_4_), channel_id=1, source_target_pairs={{0,16},{1,49},{2,18},{3,51},{4,20},{5,53},{6,22},{7,55},{8,24},{9,... | collective-permute-start | bytes 3145736 | tf_op jit(solution)/shard_map/ppermute | solution.py:30
  29.1 16.0 %collective-permute-start.7 = (bf16[4,2,128,512]{3,2,1,0:T(8,128)(2,1)S(1)}, bf16[4,2,128,512]{3,2,1,0:T(8,128)(2,1)S(1)}, u32[]{:S(2)}, u32[]{:S(2)}) collective-permute-start(bf16[4,2,128,512]{3,2,1,0:T(8,128)(2,1)S(1)} %pad_maximum_fusion.1.refs_3_.refs_1_), channel_id=1, source_target_pairs={{0,2},{1,7},{2,0},{3,5},{4,6},{5,3},{6,4},{7,1},{8,10},{9,15},{10,... | collective-permute-start | bytes 3145736 | tf_op jit(solution)/shard_map/ppermute | solution.py:30
  39.3 19.2 %collective-permute-start.13 = (bf16[4,2,128,512]{3,2,1,0:T(8,128)(2,1)S(1)}, bf16[4,2,128,512]{3,2,1,0:T(8,128)(2,1)S(1)}, u32[]{:S(2)}, u32[]{:S(2)}) collective-permute-start(bf16[4,2,128,512]{3,2,1,0:T(8,128)(2,1)S(1)} %pad_maximum_fusion.1.refs_3_.refs_1_), channel_id=1, source_target_pairs={{0,6},{1,3},{2,4},{3,1},{4,2},{5,7},{6,0},{7,5},{8,14},{9,11},{10,... | collective-permute-start | bytes 3145736 | tf_op jit(solution)/shard_map/ppermute | solution.py:30
  42.6 16.0 %collective-permute-start.14 = (bf16[4,2,128,512]{3,2,1,0:T(8,128)(2,1)S(1)}, bf16[4,2,128,512]{3,2,1,0:T(8,128)(2,1)S(1)}, u32[]{:S(2)}, u32[]{:S(2)}) collective-permute-start(bf16[4,2,128,512]{3,2,1,0:T(8,128)(2,1)S(1)} %pad_maximum_fusion.refs_6_.refs_4_), channel_id=1, source_target_pairs={{0,48},{1,17},{2,50},{3,19},{4,52},{5,21},{6,54},{7,23},{8,56},{9,... | collective-permute-start | bytes 3145736 | tf_op jit(solution)/shard_map/ppermute | solution.py:30
  44.9 19.2 %collective-permute-start.12 = (bf16[2048,256]{1,0:T(8,128)(2,1)S(1)}, bf16[2048,256]{1,0:T(8,128)(2,1)S(1)}, u32[]{:S(2)}, u32[]{:S(2)}) collective-permute-start(bf16[2048,256]{1,0:T(8,128)(2,1)S(1)} %collective-permute-done.6), channel_id=1, source_target_pairs={{0,8},{1,9},{2,10},{3,11},{4,12},{5,13},{6,14},{7,15},{8,0},{9,1},... | collective-permute-start | bytes 3145736 | tf_op jit(solution)/shard_map/ppermute | solution.py:30
  45.2 23.9 %collective-permute-start.11 = (bf16[4,2,128,512]{3,2,1,0:T(8,128)(2,1)S(1)}, bf16[4,2,128,512]{3,2,1,0:T(8,128)(2,1)S(1)}, u32[]{:S(2)}, u32[]{:S(2)}) collective-permute-start(bf16[4,2,128,512]{3,2,1,0:T(8,128)(2,1)S(1)} %collective-permute-done.10.refs_7_.refs_5_), channel_id=1, source_target_pairs={{0,48},{1,17},{2,50},{3,19},{4,52},{5,21},{6,54},{7,23},{8,56},{9,... | collective-permute-start | bytes 3145736 | tf_op jit(solution)/shard_map/ppermute | solution.py:30
  45.2 24.6 %collective-permute-start.9 = (bf16[4,2,128,512]{3,2,1,0:T(8,128)(2,1)S(1)}, bf16[4,2,128,512]{3,2,1,0:T(8,128)(2,1)S(1)}, u32[]{:S(2)}, u32[]{:S(2)}) collective-permute-start(bf16[4,2,128,512]{3,2,1,0:T(8,128)(2,1)S(1)} %collective-permute-done.7.refs_4_.refs_2_), channel_id=1, source_target_pairs={{0,6},{1,3},{2,4},{3,1},{4,2},{5,7},{6,0},{7,5},{8,14},{9,11},{10,... | collective-permute-start | bytes 3145736 | tf_op jit(solution)/shard_map/ppermute | solution.py:30
  71.1 8.6 %collective-permute-start.15 = (bf16[4,128,1024]{2,1,0:T(8,128)(2,1)S(1)}, bf16[4,128,1024]{2,1,0:T(8,128)(2,1)S(1)}, u32[]{:S(2)}, u32[]{:S(2)}) collective-permute-start(bf16[4,128,1024]{2,1,0:T(8,128)(2,1)S(1)} %shard_map.51), channel_id=1, source_target_pairs={{0,1},{1,0},{2,3},{3,2},{4,5},{5,4},{6,7},{7,6},{8,9},{9,8},{10,11... | collective-permute-start | bytes 3145736 | tf_op jit(solution)/shard_map/ppermute | solution.py:30
  78.2 3.8 %collective-permute-start.21 = (bf16[4,128,1024]{2,1,0:T(8,128)(2,1)S(1)}, bf16[4,128,1024]{2,1,0:T(8,128)(2,1)S(1)}, u32[]{:S(2)}, u32[]{:S(2)}) collective-permute-start(bf16[4,128,1024]{2,1,0:T(8,128)(2,1)S(1)} %shard_map.53), channel_id=1, source_target_pairs={{0,1},{1,0},{2,3},{3,2},{4,5},{5,4},{6,7},{7,6},{8,9},{9,8},{10,11... | collective-permute-start | bytes 3145736 | tf_op jit(solution)/shard_map/ppermute | solution.py:30
  80.2 13.1 %collective-permute-start.16 = (bf16[4,128,512]{2,1,0:T(8,128)(2,1)S(1)}, bf16[4,128,512]{2,1,0:T(8,128)(2,1)S(1)}, u32[]{:S(2)}, u32[]{:S(2)}) collective-permute-start(bf16[4,128,512]{2,1,0:T(8,128)(2,1)S(1)} %slice.97), channel_id=1, source_target_pairs={{0,8},{1,9},{2,10},{3,11},{4,12},{5,13},{6,14},{7,15},{8,0},{9,1},... | collective-permute-start | bytes 1572872 | tf_op jit(solution)/shard_map/ppermute | solution.py:30
  82.4 22.2 %collective-permute-start.22 = (bf16[4,128,512]{2,1,0:T(8,128)(2,1)S(1)}, bf16[4,128,512]{2,1,0:T(8,128)(2,1)S(1)}, u32[]{:S(2)}, u32[]{:S(2)}) collective-permute-start(bf16[4,128,512]{2,1,0:T(8,128)(2,1)S(1)} %slice.96), channel_id=1, source_target_pairs={{0,8},{1,9},{2,10},{3,11},{4,12},{5,13},{6,14},{7,15},{8,0},{9,1},... | collective-permute-start | bytes 1572872 | tf_op jit(solution)/shard_map/ppermute | solution.py:30
  93.5 15.0 %collective-permute-start.19 = (bf16[128,512]{1,0:T(8,128)(2,1)S(1)}, bf16[128,512]{1,0:T(8,128)(2,1)S(1)}, u32[]{:S(2)}, u32[]{:S(2)}) collective-permute-start(bf16[128,512]{1,0:T(8,128)(2,1)S(1)} %get-tuple-element.63), channel_id=1, source_target_pairs={{0,32},{1,97},{2,34},{3,99},{4,36},{5,101},{6,38},{7,103},{8,40},{... | collective-permute-start | bytes 393224 | tf_op jit(solution)/shard_map/ppermute | solution.py:30
  96.1 14.9 %collective-permute-start.20 = (bf16[128,512]{1,0:T(8,128)(2,1)S(1)}, bf16[128,512]{1,0:T(8,128)(2,1)S(1)}, u32[]{:S(2)}, u32[]{:S(2)}) collective-permute-start(bf16[128,512]{1,0:T(8,128)(2,1)S(1)} %get-tuple-element.62), channel_id=1, source_target_pairs={{0,48},{1,113},{2,50},{3,115},{4,52},{5,117},{6,54},{7,119},{8,56}... | collective-permute-start | bytes 393224 | tf_op jit(solution)/shard_map/ppermute | solution.py:30
  98.5 15.7 %collective-permute-start.17 = (bf16[128,512]{1,0:T(8,128)(2,1)S(1)}, bf16[128,512]{1,0:T(8,128)(2,1)S(1)}, u32[]{:S(2)}, u32[]{:S(2)}) collective-permute-start(bf16[128,512]{1,0:T(8,128)(2,1)S(1)} %get-tuple-element.61), channel_id=1, source_target_pairs={{0,0},{1,65},{2,2},{3,67},{4,4},{5,69},{6,6},{7,71},{8,8},{9,73},{... | collective-permute-start | bytes 393224 | tf_op jit(solution)/shard_map/ppermute | solution.py:30
  102.2 13.0 %collective-permute-start.18 = (bf16[128,512]{1,0:T(8,128)(2,1)S(1)}, bf16[128,512]{1,0:T(8,128)(2,1)S(1)}, u32[]{:S(2)}, u32[]{:S(2)}) collective-permute-start(bf16[128,512]{1,0:T(8,128)(2,1)S(1)} %get-tuple-element.64), channel_id=1, source_target_pairs={{0,16},{1,81},{2,18},{3,83},{4,20},{5,85},{6,22},{7,87},{8,24},{9,... | collective-permute-start | bytes 393224 | tf_op jit(solution)/shard_map/ppermute | solution.py:30
  104.7 18.5 %copy-start = (s32[8]{0:T(128)S(1)}, s32[8]{0:T(128)}, u32[]{:S(2)}) copy-start(s32[8]{0:T(128)} %owner.1) | copy-start | bytes 100
  104.8 10.5 %collective-permute-start.23 = (bf16[128,512]{1,0:T(8,128)(2,1)S(1)}, bf16[128,512]{1,0:T(8,128)(2,1)S(1)}, u32[]{:S(2)}, u32[]{:S(2)}) collective-permute-start(bf16[128,512]{1,0:T(8,128)(2,1)S(1)} %get-tuple-element.65), channel_id=1, source_target_pairs={{0,0},{1,65},{2,2},{3,67},{4,4},{5,69},{6,6},{7,71},{8,8},{9,73},{... | collective-permute-start | bytes 393224 | tf_op jit(solution)/shard_map/ppermute | solution.py:30
  108.5 8.1 %collective-permute-start.24 = (bf16[128,512]{1,0:T(8,128)(2,1)S(1)}, bf16[128,512]{1,0:T(8,128)(2,1)S(1)}, u32[]{:S(2)}, u32[]{:S(2)}) collective-permute-start(bf16[128,512]{1,0:T(8,128)(2,1)S(1)} %get-tuple-element.68), channel_id=1, source_target_pairs={{0,16},{1,81},{2,18},{3,83},{4,20},{5,85},{6,22},{7,87},{8,24},{9,... | collective-permute-start | bytes 393224 | tf_op jit(solution)/shard_map/ppermute | solution.py:30
  111.0 7.8 %collective-permute-start.25 = (bf16[128,512]{1,0:T(8,128)(2,1)S(1)}, bf16[128,512]{1,0:T(8,128)(2,1)S(1)}, u32[]{:S(2)}, u32[]{:S(2)}) collective-permute-start(bf16[128,512]{1,0:T(8,128)(2,1)S(1)} %get-tuple-element.67), channel_id=1, source_target_pairs={{0,32},{1,97},{2,34},{3,99},{4,36},{5,101},{6,38},{7,103},{8,40},{... | collective-permute-start | bytes 393224 | tf_op jit(solution)/shard_map/ppermute | solution.py:30
  114.1 6.2 %collective-permute-start.26 = (bf16[128,512]{1,0:T(8,128)(2,1)S(1)}, bf16[128,512]{1,0:T(8,128)(2,1)S(1)}, u32[]{:S(2)}, u32[]{:S(2)}) collective-permute-start(bf16[128,512]{1,0:T(8,128)(2,1)S(1)} %get-tuple-element.66), channel_id=1, source_target_pairs={{0,48},{1,113},{2,50},{3,115},{4,52},{5,117},{6,54},{7,119},{8,56}... | collective-permute-start | bytes 393224 | tf_op jit(solution)/shard_map/ppermute | solution.py:30
  120.4 2.7 %collective-permute-start.27 = (bf16[4,256,512]{2,1,0:T(8,128)(2,1)S(1)}, bf16[4,256,512]{2,1,0:T(8,128)(2,1)S(1)}, u32[]{:S(2)}, u32[]{:S(2)}) collective-permute-start(bf16[4,256,512]{2,1,0:T(8,128)(2,1)S(1)} %maximum_maximum_fusion.own), channel_id=1, source_target_pairs={{0,1},{1,0},{2,3},{3,2},{4,5},{5,4},{6,7},{7,6},{8,9},{9,8},{10,11... | collective-permute-start | bytes 3145736 | tf_op jit(solution)/shard_map/ppermute | solution.py:30
  123.9 7.7 %collective-permute-start.28 = (bf16[256,512]{1,0:T(8,128)(2,1)S(1)}, bf16[256,512]{1,0:T(8,128)(2,1)S(1)}, u32[]{:S(2)}, u32[]{:S(2)}) collective-permute-start(bf16[256,512]{1,0:T(8,128)(2,1)S(1)} %get-tuple-element.57), channel_id=1, source_target_pairs={{0,0},{1,8},{2,2},{3,10},{4,4},{5,12},{6,6},{7,14},{8,9},{9,1},{10... | collective-permute-start | bytes 786440 | tf_op jit(solution)/shard_map/ppermute | solution.py:30
  126.9 12.8 %collective-permute-start.29 = (bf16[256,512]{1,0:T(8,128)(2,1)S(1)}, bf16[256,512]{1,0:T(8,128)(2,1)S(1)}, u32[]{:S(2)}, u32[]{:S(2)}) collective-permute-start(bf16[256,512]{1,0:T(8,128)(2,1)S(1)} %get-tuple-element.58), channel_id=1, source_target_pairs={{0,2},{1,10},{2,4},{3,12},{4,6},{5,14},{6,0},{7,8},{8,11},{9,3},{1... | collective-permute-start | bytes 786440 | tf_op jit(solution)/shard_map/ppermute | solution.py:30
  127.3 15.3 %collective-permute-start.30 = (bf16[256,512]{1,0:T(8,128)(2,1)S(1)}, bf16[256,512]{1,0:T(8,128)(2,1)S(1)}, u32[]{:S(2)}, u32[]{:S(2)}) collective-permute-start(bf16[256,512]{1,0:T(8,128)(2,1)S(1)} %get-tuple-element.59), channel_id=1, source_target_pairs={{0,4},{1,12},{2,6},{3,14},{4,0},{5,8},{6,2},{7,10},{8,13},{9,5},{1... | collective-permute-start | bytes 786440 | tf_op jit(solution)/shard_map/ppermute | solution.py:30
  129.7 13.4 %collective-permute-start.31 = (bf16[256,512]{1,0:T(8,128)(2,1)S(1)}, bf16[256,512]{1,0:T(8,128)(2,1)S(1)}, u32[]{:S(2)}, u32[]{:S(2)}) collective-permute-start(bf16[256,512]{1,0:T(8,128)(2,1)S(1)} %get-tuple-element.60), channel_id=1, source_target_pairs={{0,6},{1,14},{2,0},{3,8},{4,2},{5,10},{6,4},{7,12},{8,15},{9,7},{1... | collective-permute-start | bytes 786440 | tf_op jit(solution)/shard_map/ppermute | solution.py:30
